TPU v7x, 32 devices: a whole 2x2x4 slice. The times are simulated.
32 devices in a mesh: group: 4 (over z), member: 8 (over y, x, core).
Axes of the slice: x: 2, y: 2, z: 4, core: 2. Of those that a mesh axis runs over, the one named last changes fastest.
Arguments:
- audio_vectors: bfloat16 [4096, 768], P(('group', 'member')), may hold values from -8 to 8
- sentence_vectors: bfloat16 [2048, 768], P(('group', 'member')), may hold values from -8 to 8
- matching_indices: int32 [4096], P(('group', 'member')), may hold values from 0 to 2047, as said below
- sharpness_array: float32 [1], replicated, may hold values from 8 to 16
- offset_term: float32 [1], replicated, may hold values from -4 to -2
Outputs:
- speech_grad: float32 [4096, 768], P(('group', 'member'))
- text_grad: float32 [2048, 768], P(('group', 'member'))
Inputs may be any that keep to these rules, and one draw needn't show every extreme that they name: `matching_indices`: each caption matches exactly two speech clips.
All inputs are finite; a program needn't handle non-finite values.
Results may differ from a plain program's by a relative error of at most 0.00072.
Values may be sent and summed in bfloat16 or wider, within the bound.
No kernel may reach another device: no remote copies, remote signals or barrier semaphores. Data moves between devices by JAX's collectives and lax.ppermute only.
A program may use at most 128 MiB of HBM per device.

v0:
```python
import jax
import jax.numpy as jnp
from jax import lax
from jax.sharding import PartitionSpec as P


def shifted(value, axis, by):
    size = lax.axis_size(axis)
    return lax.ppermute(value, axis, [(i, (i + by) % size) for i in range(size)])


def unit_rows(values):
    floats = values.astype(jnp.float32)
    norms = jnp.sqrt(jnp.sum(floats * floats, axis=-1, keepdims=True) + 1e-06)
    return (floats / norms, norms)


def project_gradient(back, direction, norms):
    along = jnp.sum(direction * back, axis=-1, keepdims=True)
    return (back - direction * along) / norms


def pair_coef(audio_entries, label_rows, text_rows, columns, sharpness_factor, shift):
    logits = (
        sharpness_factor * jnp.dot(audio_entries, text_rows.T, preferred_element_type=jnp.float32)
        + shift
    )
    match = (label_rows[:, None] == columns[None, :]).astype(jnp.float32)
    return (sharpness_factor * (jax.nn.sigmoid(logits) - match)).astype(jnp.bfloat16)


def column_product(pair_weight, visitor):
    return lax.dot_general(
        pair_weight, visitor, (((0,), (0,)), ((), ())), preferred_element_type=jnp.float32
    )


def shards(audio_vectors, sentence_vectors, matching_indices, sharpness_array, offset_term):
    audio_heading, speech_norm = unit_rows(audio_vectors)
    text_dir, text_norm = unit_rows(sentence_vectors)
    speech_unit = audio_heading.astype(jnp.bfloat16)
    text_normalized = text_dir.astype(jnp.bfloat16)
    sharpness_factor = sharpness_array[0]
    shift = offset_term[0]
    own_rows = audio_vectors.shape[0]
    rounds = lax.axis_size("group")
    group_now = lax.axis_index("group")
    text_rows = lax.all_gather(text_normalized, "member", axis=0, tiled=True)
    width = text_rows.shape[0]
    columns = group_now * width + jnp.arange(width, dtype=jnp.int32)
    label_all = lax.all_gather(matching_indices, "group", axis=0, tiled=True)
    weight_list = []
    visitor_list = []
    visiting = speech_unit
    carried = jnp.zeros((own_rows, audio_vectors.shape[1]), jnp.float32)
    for turn in range(rounds):
        source = jnp.mod(group_now - turn, rounds)
        label_rows = lax.dynamic_slice_in_dim(label_all, source * own_rows, own_rows, 0)
        pair_weight = pair_coef(visiting, label_rows, text_rows, columns, sharpness_factor, shift)
        carried = carried + jnp.dot(pair_weight, text_rows, preferred_element_type=jnp.float32)
        weight_list.append(pair_weight)
        visitor_list.append(visiting)
        carried = shifted(carried, "group", 1)
        if turn + 1 < rounds:
            visiting = shifted(visiting, "group", 1)
    text_part = column_product(weight_list[0], visitor_list[0])
    for shard_position in range(1, len(weight_list)):
        text_part = text_part + column_product(
            weight_list[shard_position], visitor_list[shard_position]
        )
    text_back = lax.psum_scatter(text_part, "member", scatter_dimension=0, tiled=True)
    speech_grad = project_gradient(carried, audio_heading, speech_norm)
    text_grad = project_gradient(text_back, text_dir, text_norm)
    return (speech_grad, text_grad)


def solution(mesh):
    in_specs = (
        P(("group", "member"), None),
        P(("group", "member"), None),
        P(("group", "member")),
        P(),
        P(),
    )
    out_specs = (P(("group", "member"), None), P(("group", "member"), None))
    return jax.shard_map(shards, mesh=mesh, in_specs=in_specs, out_specs=out_specs, check_vma=False)
```

profile of v0, /device:TPU:0, one launch (start us, length us, event | category | flops | bytes accessed | tf_op | source)
XLA Modules:
  0.0 109.0 jit_solution(14539950945226397365)
XLA Ops:
  7.2 1.0 fusion.32
  8.3 1.0 fusion.35
  9.3 3.1 %collective-permute-start.1 = (bf16[128,768]{1,0:T(8,128)(2,1)S(1)}, bf16[128,768]{1,0:T(8,128)(2,1)S(1)}, u32[]{:S(2)}, u32[]{:S(2)}) collective-permute-start(bf16[128,768]{1,0:T(8,128)(2,1)S(1)} %fusion.35), channel_id=1, source_target_pairs={{0,8},{8,16},{16,24},{24,0},{1,9},{9,17},{17,25},{25,1},{2,10},{10... | collective-permute-start | bytes 589832 | tf_op jit(solution)/shard_map/ppermute | solution.py:9
  13.7 1.0 fusion.33
  14.7 9.8 %all-gather = s32[4,1,128]{2,1,0:T(1,128)S(1)} all-gather(s32[1,1,128]{2,1,0:T(1,128)} %bitcast.37), channel_id=1, replica_groups=mesh['group'=4,'member'=8] {'group'}, dimensions={0}, use_global_device_ids=true | all-gather | bytes 2560 | tf_op jit(solution)/shard_map/all_gather | solution.py:51
  24.5 1.0 fusion.34
  25.5 10.5 %all_gather.6 = bf16[512,768]{1,0:T(8,128)(2,1)S(1)} all-gather(bf16[64,768]{1,0:T(8,128)(2,1)S(1)} %fusion.34), channel_id=1, replica_groups=mesh['group'=4,'member'=8] {'member'}, dimensions={0}, use_global_device_ids=true | all-gather | bytes 884736 | tf_op jit(solution)/shard_map/all_gather | solution.py:48
  36.0 0.1 fusion.36
  36.1 0.4 fusion.31
  36.6 0.4 fusion.40
  37.0 0.1 collective-permute-start.3
  37.0 0.4 fusion.30
  37.5 0.4 fusion.41
  37.9 8.1 %collective-permute-done.3 = bf16[128,768]{1,0:T(8,128)(2,1)S(1)} collective-permute-done((bf16[128,768]{1,0:T(8,128)(2,1)S(1)}, bf16[128,768]{1,0:T(8,128)(2,1)S(1)}, u32[]{:S(2)}, u32[]{:S(2)}) %collective-permute-start.3) | collective-permute-done | bytes 196640 | tf_op jit(solution)/shard_map/ppermute | solution.py:9
  46.0 0.4 fusion.29
  46.4 0.4 fusion.42
  46.8 7.3 %collective-permute-done.5 = bf16[128,768]{1,0:T(8,128)(2,1)S(1)} collective-permute-done((bf16[128,768]{1,0:T(8,128)(2,1)S(1)}, bf16[128,768]{1,0:T(8,128)(2,1)S(1)}, u32[]{:S(2)}, u32[]{:S(2)}) %collective-permute-start.5) | collective-permute-done | bytes 196640 | tf_op jit(solution)/shard_map/ppermute | solution.py:9
  54.1 0.4 fusion.28
  54.6 1.5 %add_add_fusion = f32[512,768]{1,0:T(8,128)} fusion(f32[512,768]{1,0:T(8,128)S(1)} %fusion.42, f32[512,768]{1,0:T(8,128)S(1)} %fusion.40, f32[512,768]{1,0:T(8,128)S(1)} %fusion.41, bf16[128,512]{1,0:T(8,128)(2,1)S(1)} %fusion.28, bf16[128,768]{1,0:T(8,128)(2,1)S(1)} %collective-permute-done.5), kind=kOutput, calls=%fused_computation | convolution fusion | flops 101842944 | bytes 6619136 | tf_op jit(solution)/shard_map/dot_general | solution.py:33
  56.1 0.3 fusion.37
  56.4 0.1 collective-permute-start
  56.5 11.4 %collective-permute-done = f32[128,768]{1,0:T(8,128)S(1)} collective-permute-done((f32[128,768]{1,0:T(8,128)S(1)}, f32[128,768]{1,0:T(8,128)S(1)}, u32[]{:S(2)}, u32[]{:S(2)}) %collective-permute-start) | collective-permute-done | bytes 393248 | tf_op jit(solution)/shard_map/ppermute | solution.py:9
  67.9 0.3 convolution_add_fusion
  68.3 0.3 fusion.38
  68.6 10.2 %collective-permute-done.2 = f32[128,768]{1,0:T(8,128)S(1)} collective-permute-done((f32[128,768]{1,0:T(8,128)S(1)}, f32[128,768]{1,0:T(8,128)S(1)}, u32[]{:S(2)}, u32[]{:S(2)}) %collective-permute-start.2) | collective-permute-done | bytes 393248 | tf_op jit(solution)/shard_map/ppermute | solution.py:9
  78.9 0.3 fusion.39
  79.2 9.3 %collective-permute-done.4 = f32[128,768]{1,0:T(8,128)S(1)} collective-permute-done((f32[128,768]{1,0:T(8,128)S(1)}, f32[128,768]{1,0:T(8,128)S(1)}, u32[]{:S(2)}, u32[]{:S(2)}) %collective-permute-start.4) | collective-permute-done | bytes 393248 | tf_op jit(solution)/shard_map/ppermute | solution.py:9
  88.6 9.6 %collective-permute-done.6 = f32[128,768]{1,0:T(8,128)S(1)} collective-permute-done((f32[128,768]{1,0:T(8,128)S(1)}, f32[128,768]{1,0:T(8,128)S(1)}, u32[]{:S(2)}, u32[]{:S(2)}) %collective-permute-start.6) | collective-permute-done | bytes 393248 | tf_op jit(solution)/shard_map/ppermute | solution.py:9
  98.2 0.2 multiply_reduce_fusion
  98.4 0.9 subtract_divide_fusion
  99.3 1.1 %multiply_reduce_fusion.1 = f32[64]{0:T(128)S(1)} fusion(f32[64,768]{1,0:T(8,128)} %reduce-scatter.2.cloned.1.call-done, f32[64]{0:T(128)S(1)} %add_sqrt_fusion, bf16[64,768]{1,0:T(8,128)(2,1)S(1)} %copy-done.1), kind=kLoop, calls=%fused_computation.47 | loop fusion | flops 196544 | bytes 295424 | tf_op jit(solution)/shard_map/reduce_sum | solution.py:19
  100.4 1.7 %subtract_divide_fusion.1 = f32[64,768]{1,0:T(8,128)} fusion(f32[64,768]{1,0:T(8,128)} %reduce-scatter.2.cloned.1.call-done, f32[64]{0:T(128)S(1)} %multiply_reduce_fusion.1, f32[64]{0:T(128)S(1)} %add_sqrt_fusion, bf16[64,768]{1,0:T(8,128)(2,1)S(1)} %copy-done.1), kind=kLoop, calls=%fused_computation.46 | loop fusion | flops 245760 | bytes 492032 | tf_op jit(solution)/shard_map/div | solution.py:20
  (17 shorter events, 0.4 us)
Async XLA Ops:
  7.2 92.1 %reduce-scatter.2.cloned.1.call-start = ((), (), s32[]{:S(2)}) async-start(), calls=%async_computation.1 | async-start | bytes 1769472 | tf_op jit(solution)/shard_map/reduce_scatter | solution.py:71
  9.3 27.6 %collective-permute-start.1 = (bf16[128,768]{1,0:T(8,128)(2,1)S(1)}, bf16[128,768]{1,0:T(8,128)(2,1)S(1)}, u32[]{:S(2)}, u32[]{:S(2)}) collective-permute-start(bf16[128,768]{1,0:T(8,128)(2,1)S(1)} %fusion.35), channel_id=1, source_target_pairs={{0,8},{8,16},{16,24},{24,0},{1,9},{9,17},{17,25},{25,1},{2,10},{10... | collective-permute-start | bytes 589832 | tf_op jit(solution)/shard_map/ppermute | solution.py:9
  37.0 9.0 %collective-permute-start.3 = (bf16[128,768]{1,0:T(8,128)(2,1)S(1)}, bf16[128,768]{1,0:T(8,128)(2,1)S(1)}, u32[]{:S(2)}, u32[]{:S(2)}) collective-permute-start(bf16[128,768]{1,0:T(8,128)(2,1)S(1)} %collective-permute-done.1), channel_id=1, source_target_pairs={{0,8},{8,16},{16,24},{24,0},{1,9},{9,17},{17,25},{25,1},{2,10},{10... | collective-permute-start | bytes 589832 | tf_op jit(solution)/shard_map/ppermute | solution.py:9
  46.0 8.1 %collective-permute-start.5 = (bf16[128,768]{1,0:T(8,128)(2,1)S(1)}, bf16[128,768]{1,0:T(8,128)(2,1)S(1)}, u32[]{:S(2)}, u32[]{:S(2)}) collective-permute-start(bf16[128,768]{1,0:T(8,128)(2,1)S(1)} %collective-permute-done.3), channel_id=1, source_target_pairs={{0,8},{8,16},{16,24},{24,0},{1,9},{9,17},{17,25},{25,1},{2,10},{10... | collective-permute-start | bytes 589832 | tf_op jit(solution)/shard_map/ppermute | solution.py:9
  56.4 11.5 %collective-permute-start = (f32[128,768]{1,0:T(8,128)S(1)}, f32[128,768]{1,0:T(8,128)S(1)}, u32[]{:S(2)}, u32[]{:S(2)}) collective-permute-start(f32[128,768]{1,0:T(8,128)S(1)} %fusion.37), channel_id=1, source_target_pairs={{0,8},{8,16},{16,24},{24,0},{1,9},{9,17},{17,25},{25,1},{2,10},{10... | collective-permute-start | bytes 1179656 | tf_op jit(solution)/shard_map/ppermute | solution.py:9
  68.2 10.6 %collective-permute-start.2 = (f32[128,768]{1,0:T(8,128)S(1)}, f32[128,768]{1,0:T(8,128)S(1)}, u32[]{:S(2)}, u32[]{:S(2)}) collective-permute-start(f32[128,768]{1,0:T(8,128)S(1)} %convolution_add_fusion), channel_id=1, source_target_pairs={{0,8},{8,16},{16,24},{24,0},{1,9},{9,17},{17,25},{25,1},{2,10},{10... | collective-permute-start | bytes 1179656 | tf_op jit(solution)/shard_map/ppermute | solution.py:9
  68.5 29.6 %copy-start = (bf16[128,768]{1,0:T(8,128)(2,1)S(1)}, bf16[128,768]{1,0:T(8,128)(2,1)}, u32[]{:S(2)}) copy-start(bf16[128,768]{1,0:T(8,128)(2,1)} %param.5) | copy-start | bytes 589828
  78.8 9.7 %collective-permute-start.4 = (f32[128,768]{1,0:T(8,128)S(1)}, f32[128,768]{1,0:T(8,128)S(1)}, u32[]{:S(2)}, u32[]{:S(2)}) collective-permute-start(f32[128,768]{1,0:T(8,128)S(1)} %add.130), channel_id=1, source_target_pairs={{0,8},{8,16},{16,24},{24,0},{1,9},{9,17},{17,25},{25,1},{2,10},{10... | collective-permute-start | bytes 1179656 | tf_op jit(solution)/shard_map/ppermute | solution.py:9
  79.2 20.1 %copy-start.1 = (bf16[64,768]{1,0:T(8,128)(2,1)S(1)}, bf16[64,768]{1,0:T(8,128)(2,1)}, u32[]{:S(2)}) copy-start(bf16[64,768]{1,0:T(8,128)(2,1)} %param.6) | copy-start | bytes 294916
  88.5 9.6 %collective-permute-start.6 = (f32[128,768]{1,0:T(8,128)S(1)}, f32[128,768]{1,0:T(8,128)S(1)}, u32[]{:S(2)}, u32[]{:S(2)}) collective-permute-start(f32[128,768]{1,0:T(8,128)S(1)} %add.135), channel_id=1, source_target_pairs={{0,8},{8,16},{16,24},{24,0},{1,9},{9,17},{17,25},{25,1},{2,10},{10... | collective-permute-start | bytes 1179656 | tf_op jit(solution)/shard_map/ppermute | solution.py:9
Sparse Core Ops, SparseCore 0:
  56.3 35.7 reduce-scatter.1
where the time goes:
time: 109 us
  waiting for transfers between devices  56 us (51%)
  blocking collectives  20.3 us (19%)
  between operations  15.5 us (14%)
  other arithmetic  8.13 us (7%)
  matrix products  5.54 us (5%)
  starting transfers between devices  3.41 us (3%)
    ppermute x7, waiting for transfers between devices, shifted(): lax.ppermute(value, axis, [(i, (i + by) % size) for i in range(size)])  55.9 us
    all_gather x1, blocking collectives, shards(): text_rows = lax.all_gather(text_normalized, 'member', axis=0, tiled=True)  10.5 us
    all_gather x1, blocking collectives, shards(): label_all = lax.all_gather(matching_indices, 'group', axis=0, tiled=True)  9.78 us
    ppermute x7, starting transfers between devices, shifted(): lax.ppermute(value, axis, [(i, (i + by) % size) for i in range(size)])  3.37 us
    dot_general x4, matrix products, column_product(): lax.dot_general(pair_weight, visitor, (((0,), (0,)), ((), ())), preferred...  2.68 us
    div x2, other arithmetic, project_gradient(): return (back - direction * along) / norms  2.62 us
  transfers between devices with their start and end apart: 8, of which 6 were waited for; matrix products, arithmetic and copies ran while one was open for 6% of the time, Pallas kernels for 0%

commit v1 on v0

v1 whole, which is shorter than its diff:
```python
import functools
import jax
import jax.numpy as jnp
from jax import lax
from jax.experimental import pallas as pl
from jax.experimental.pallas import tpu as pltpu
from jax.sharding import PartitionSpec as P

VMEM_LIMIT = 56 * 1024 * 1024
CHUNK = 512


def exchanged(value, axis, mask):
    size = lax.axis_size(axis)
    return lax.ppermute(value, axis, [(i, i ^ mask) for i in range(size)])


def call(body, out_shape, operands, flops=0, names="kernel"):
    moved = sum(v.size * v.dtype.itemsize for v in operands)
    specs = []
    for v in operands:
        smem = v.shape == (1,)
        specs.append(pl.BlockSpec(memory_space=pltpu.SMEM if smem else pltpu.VMEM))
    return pl.pallas_call(
        body,
        out_shape=out_shape,
        in_specs=specs,
        out_specs=jax.tree.map(lambda _: pl.BlockSpec(memory_space=pltpu.VMEM), out_shape),
        compiler_params=pltpu.CompilerParams(vmem_limit_bytes=VMEM_LIMIT),
        cost_estimate=pl.CostEstimate(flops=flops, bytes_accessed=moved, transcendentals=0),
        name=names,
    )(*operands)


def direction(values):
    floats = values.astype(jnp.float32)
    norms = jnp.sqrt(jnp.sum(floats * floats, axis=-1, keepdims=True) + 1e-06)
    return floats / norms, norms


def unit_body(*refs):
    out = refs[-1]
    rows = refs[0].shape[0]
    for k, ref in enumerate(refs[:-1]):
        out[k * rows : (k + 1) * rows, :] = direction(ref[...])[0].astype(jnp.bfloat16)


def unit_rows(blocks):
    rows, width = blocks[0].shape
    shape = jax.ShapeDtypeStruct((len(blocks) * rows, width), jnp.bfloat16)
    return call(unit_body, shape, blocks, names="unit_rows")


def text_coef(text, speech, labels, sharp, shift, own_text):
    groups = lax.axis_size("group")
    members = lax.axis_size("member")
    group = lax.axis_index("group")
    member = lax.axis_index("member")
    logits = sharp * lax.dot_general(
        text, speech, (((1,), (1,)), ((), ())), preferred_element_type=jnp.float32
    ) + shift
    probs = 1.0 / (1.0 + jnp.exp(-logits))
    pieces = []
    for k in range(groups):
        base = ((group ^ k) * members + member) * own_text
        ids = base + lax.broadcasted_iota(jnp.int32, (own_text, labels.shape[1]), 0)
        match = jnp.where(ids == labels, 1.0, 0.0)
        pieces.append(probs[k * own_text : (k + 1) * own_text, :] - match)
    return (sharp * jnp.concatenate(pieces, axis=0)).astype(jnp.bfloat16)


def text_part_body(count, own_text, has_start, *refs):
    sharp, shift = refs[0][0], refs[1][0]
    text, speech = refs[2], refs[3]
    labels = refs[4 : 4 + count]
    at = 4 + count
    start = None
    if has_start:
        start = refs[at]
        at += 1
    outs = refs[at:]
    rows = speech.shape[0] // count
    group = max(1, min(count, CHUNK // rows))
    total = start[...] if has_start else None
    for first in range(0, count, group):
        some = labels[first : first + group]
        mark = jnp.concatenate([ref[...] for ref in some], axis=1)
        block = speech[first * rows : (first + len(some)) * rows, :]
        coef = text_coef(text[...], block, mark, sharp, shift, own_text)
        part = jnp.dot(coef, block, preferred_element_type=jnp.float32)
        total = part if total is None else total + part
    if len(outs) == 1:
        outs[0][...] = total
    else:
        for k, out in enumerate(outs):
            out[...] = total[k * own_text : (k + 1) * own_text, :]


def speech_part_body(own_text, *refs):
    sharp, shift = refs[0][0], refs[1][0]
    label, speech = refs[2], refs[3]
    texts, out = refs[4:-1], refs[-1]
    groups = lax.axis_size("group")
    members = lax.axis_size("member")
    group = lax.axis_index("group")
    member = lax.axis_index("member")
    rows = label.shape[1]
    spread = jnp.broadcast_to(label[...], (rows, rows)).T[:, 0:1]
    block = speech[0:rows, :]
    total = None
    for j, text in enumerate(texts):
        other = member ^ (2 * j)
        logits = sharp * lax.dot_general(
            block, text[...], (((1,), (1,)), ((), ())), preferred_element_type=jnp.float32
        ) + shift
        probs = 1.0 / (1.0 + jnp.exp(-logits))
        lane = lax.broadcasted_iota(jnp.int32, (1, groups * own_text), 1)
        ids = ((group ^ (lane // own_text)) * members + other) * own_text + lane % own_text
        match = jnp.where(spread == ids, 1.0, 0.0)
        coef = (sharp * (probs - match)).astype(jnp.bfloat16)
        part = jnp.dot(coef, text[...], preferred_element_type=jnp.float32)
        total = part if total is None else total + part
    out[...] = total


def finish_body(*refs):
    values, parts, out = refs[0], refs[1:-1], refs[-1]
    heading, norms = direction(values[...])
    back = parts[0][...]
    for part in parts[1:]:
        back = back + part[...]
    along = jnp.sum(heading * back, axis=-1, keepdims=True)
    out[...] = (back - heading * along) / norms


def finish(values, parts):
    shape = jax.ShapeDtypeStruct(values.shape, jnp.float32)
    return call(finish_body, shape, [values, *parts], names="finish")


def shards(audio_vectors, sentence_vectors, matching_indices, sharpness_array, offset_term):
    members = lax.axis_size("member")
    groups = lax.axis_size("group")
    chips = members // 2
    own_speech, width = audio_vectors.shape
    own_text = sentence_vectors.shape[0]
    scalars = [sharpness_array, offset_term]
    label = matching_indices.reshape(1, own_speech)

    text_column = [sentence_vectors]
    for k in range(1, groups):
        text_column.append(exchanged(sentence_vectors, "group", k))
    speech_blocks = [audio_vectors]
    for k in range(1, chips):
        speech_blocks.append(exchanged(audio_vectors, "member", 2 * k))
    labels = [label]
    for k in range(1, members):
        labels.append(exchanged(label, "member", k))

    text = unit_rows(text_column)
    texts = [text]
    for k in range(1, chips):
        texts.append(exchanged(text, "member", 2 * k))
    speech = unit_rows(speech_blocks)
    other = exchanged(speech, "member", 1)

    work = 4 * text.shape[0] * speech.shape[0] * width
    column_shape = jax.ShapeDtypeStruct((groups * own_text, width), jnp.float32)
    half = call(
        functools.partial(text_part_body, chips, own_text, False),
        column_shape,
        scalars + [text, speech] + labels[0::2],
        work,
        "text_part",
    )
    parts = call(
        functools.partial(text_part_body, chips, own_text, True),
        [jax.ShapeDtypeStruct((own_text, width), jnp.float32)] * groups,
        scalars + [text, other] + labels[1::2] + [half],
        work,
        "text_part_sum",
    )
    text_back = [parts[0]]
    for k in range(1, groups):
        text_back.append(exchanged(parts[k], "group", k))

    work = 4 * own_speech * chips * text.shape[0] * width
    row_shape = jax.ShapeDtypeStruct((own_speech, width), jnp.float32)
    speech_part = functools.partial(speech_part_body, own_text)
    away = call(speech_part, row_shape, scalars + [labels[1], other] + texts, work, "speech_part")
    back = exchanged(away, "member", 1)
    home = call(speech_part, row_shape, scalars + [labels[0], speech] + texts, work, "speech_part")

    text_grad = finish(sentence_vectors, text_back)
    speech_grad = finish(audio_vectors, [home, back])
    return (speech_grad, text_grad)


def solution(mesh):
    in_specs = (
        P(("group", "member"), None),
        P(("group", "member"), None),
        P(("group", "member")),
        P(),
        P(),
    )
    out_specs = (P(("group", "member"), None), P(("group", "member"), None))
    return jax.shard_map(shards, mesh=mesh, in_specs=in_specs, out_specs=out_specs, check_vma=False)
```

time: 109 us -> 99.2 us (0.910)
  Pallas kernels: 0 us -> 22.4 us
  blocking collectives: 20.3 us -> 0 us
  starting transfers between devices: 3.41 us -> 23.4 us
  between operations: 15.5 us -> 2.04 us
  waiting for transfers between devices: 56 us -> 43.2 us
  other arithmetic: 8.13 us -> 0 us
  local copies, waits for them, and re-layouts: 0.09 us -> 7.39 us
  matrix products: 5.54 us -> 0 us
    pallas_call x0 -> x8, Pallas kernels: none -> 22.4 us  [call(): pl.pallas_call(body, out_shape=out_shape, in_specs=specs, out_specs=jax.t...]
    all_gather x2 -> x0, blocking collectives: 20.3 us -> none  [the longest x1 10.5 us: shards(): text_rows = lax.all_gather(text_normalized, 'member', axis=0, tiled=True)]
    ppermute x7 -> x21, starting transfers between devices: 3.37 us -> 23.4 us  [exchanged(): return lax.ppermute(value, axis, [(i, i ^ mask) for i in range(size)])]
    ppermute x7 -> x21, waiting for transfers between devices: 55.9 us -> 43.2 us  [exchanged(): return lax.ppermute(value, axis, [(i, i ^ mask) for i in range(size)])]
    unnamed x4 -> x46, local copies, waits for them, and re-layouts: 0.01 us -> 7.39 us
    dot_general x12 -> x0, matrix products: 5.54 us -> none  [the longest x4 2.68 us: column_product(): lax.dot_general(pair_weight, visitor, (((0,), (0,)), ((), ())), preferred...]
    reduce_sum x4 -> x0, other arithmetic: 3.39 us -> none  [the longest x2 2.06 us: unit_rows(): norms = jnp.sqrt(jnp.sum(floats * floats, axis=-1, keepdims=True) + 1e-06)]
    div x2 -> x0, other arithmetic: 2.62 us -> none  [project_gradient(): return (back - direction * along) / norms]
  transfers between devices with their start and end apart: 8 -> 21, of which waited for: 6 -> 10; matrix products, arithmetic and copies ran while one was open for 6% -> 0% of each run, Pallas kernels for 0% -> 14%
where the time goes in v1:
time: 99.2 us; the launch traced here: 98.4 us
  waiting for transfers between devices  43.2 us (44%)
  starting transfers between devices  23.4 us (24%)
  Pallas kernels  22.4 us (23%)
  local copies, waits for them, and re-layouts  7.39 us (7%)
  between operations  2.04 us (2%)
    ppermute x21, waiting for transfers between devices, exchanged(): return lax.ppermute(value, axis, [(i, i ^ mask) for i in range(size)])  43.2 us
    ppermute x21, starting transfers between devices, exchanged(): return lax.ppermute(value, axis, [(i, i ^ mask) for i in range(size)])  23.4 us
    pallas_call x8, Pallas kernels, call(): pl.pallas_call(body, out_shape=out_shape, in_specs=specs, out_specs=jax.t...  22.4 us
    unnamed x46, local copies, waits for them, and re-layouts  7.39 us
  transfers between devices with their start and end apart: 21, of which 10 were waited for; matrix products, arithmetic and copies ran while one was open for 0% of the time, Pallas kernels for 14%

profile of v1, /device:TPU:0, one launch (start us, length us, event | category | flops | bytes accessed | tf_op | source)
XLA Modules:
  0.0 98.4 jit_solution(17159849327823688116)
XLA Ops:
  0.6 3.0 %collective-permute-start = (bf16[128,768]{1,0:T(8,128)(2,1)}, bf16[128,768]{1,0:T(8,128)(2,1)S(1)}, u32[]{:S(2)}, u32[]{:S(2)}) collective-permute-start(bf16[128,768]{1,0:T(8,128)(2,1)} %refs_0_.10), channel_id=1, source_target_pairs={{0,2},{1,3},{2,0},{3,1},{4,6},{5,7},{6,4},{7,5},{8,10},{9,11},{10,... | collective-permute-start | bytes 589832 | tf_op jit(solution)/shard_map/ppermute | solution.py:15
  3.6 1.5 %collective-permute-start.1 = (bf16[128,768]{1,0:T(8,128)(2,1)}, bf16[128,768]{1,0:T(8,128)(2,1)S(1)}, u32[]{:S(2)}, u32[]{:S(2)}) collective-permute-start(bf16[128,768]{1,0:T(8,128)(2,1)} %refs_0_.10), channel_id=1, source_target_pairs={{0,4},{1,5},{2,6},{3,7},{4,0},{5,1},{6,2},{7,3},{8,12},{9,13},{10,... | collective-permute-start | bytes 589832 | tf_op jit(solution)/shard_map/ppermute | solution.py:15
  5.2 4.4 %collective-permute-done.refs_1_ = bf16[128,768]{1,0:T(8,128)(2,1)S(1)} collective-permute-done((bf16[128,768]{1,0:T(8,128)(2,1)}, bf16[128,768]{1,0:T(8,128)(2,1)S(1)}, u32[]{:S(2)}, u32[]{:S(2)}) %collective-permute-start) | collective-permute-done | bytes 196640 | tf_op jit(solution)/shard_map/ppermute | solution.py:15
  9.6 4.8 %collective-permute-done.1.refs_2_ = bf16[128,768]{1,0:T(8,128)(2,1)S(1)} collective-permute-done((bf16[128,768]{1,0:T(8,128)(2,1)}, bf16[128,768]{1,0:T(8,128)(2,1)S(1)}, u32[]{:S(2)}, u32[]{:S(2)}) %collective-permute-start.1) | collective-permute-done | bytes 196640 | tf_op jit(solution)/shard_map/ppermute | solution.py:15
  15.8 2.4 %unit_rows.2.refs_3_ = bf16[512,768]{1,0:T(8,128)(2,1)} custom-call(bf16[128,768]{1,0:T(8,128)(2,1)} %refs_0_.10, bf16[128,768]{1,0:T(8,128)(2,1)} %copy-done.6, bf16[128,768]{1,0:T(8,128)(2,1)} %copy-done.7, bf16[128,768]{1,0:T(8,128)(2,1)} %copy-done.8), custom_call_target="tpu_custom_call" | custom-call | bytes 786432 | tf_op jit(solution)/shard_map/unit_rows/pallas_call | solution.py:24
  18.2 1.6 %collective-permute-start.3 = (bf16[64,768]{1,0:T(8,128)(2,1)S(1)}, bf16[64,768]{1,0:T(8,128)(2,1)S(1)}, u32[]{:S(2)}, u32[]{:S(2)}) collective-permute-start(bf16[64,768]{1,0:T(8,128)(2,1)S(1)} %copy-done.4), channel_id=1, source_target_pairs={{0,8},{8,0},{16,24},{24,16},{1,9},{9,1},{17,25},{25,17},{2,10},{10... | collective-permute-start | bytes 294920 | tf_op jit(solution)/shard_map/ppermute | solution.py:15
  19.8 2.6 %collective-permute-start.4 = (bf16[64,768]{1,0:T(8,128)(2,1)S(1)}, bf16[64,768]{1,0:T(8,128)(2,1)S(1)}, u32[]{:S(2)}, u32[]{:S(2)}) collective-permute-start(bf16[64,768]{1,0:T(8,128)(2,1)S(1)} %copy-done.4), channel_id=1, source_target_pairs={{0,16},{8,24},{16,0},{24,8},{1,17},{9,25},{17,1},{25,9},{2,18},{10... | collective-permute-start | bytes 294920 | tf_op jit(solution)/shard_map/ppermute | solution.py:15
  22.6 0.8 collective-permute-done.3.refs_1_
  23.4 7.1 %collective-permute-done.4.refs_2_ = bf16[64,768]{1,0:T(8,128)(2,1)S(1)} collective-permute-done((bf16[64,768]{1,0:T(8,128)(2,1)S(1)}, bf16[64,768]{1,0:T(8,128)(2,1)S(1)}, u32[]{:S(2)}, u32[]{:S(2)}) %collective-permute-start.4) | collective-permute-done | bytes 98336 | tf_op jit(solution)/shard_map/ppermute | solution.py:15
  31.8 2.0 %unit_rows.3.refs_4_.refs_2_ = bf16[256,768]{1,0:T(8,128)(2,1)} custom-call(bf16[64,768]{1,0:T(8,128)(2,1)} %refs_0_.11, bf16[64,768]{1,0:T(8,128)(2,1)} %copy-done.12, bf16[64,768]{1,0:T(8,128)(2,1)} %copy-done.13, bf16[64,768]{1,0:T(8,128)(2,1)} %copy-done.14), custom_call_target="tpu_custom_call" | custom-call | bytes 393216 | tf_op jit(solution)/shard_map/unit_rows/pallas_call | solution.py:24
  34.3 1.5 %collective-permute-start.7 = (bf16[256,768]{1,0:T(8,128)(2,1)}, bf16[256,768]{1,0:T(8,128)(2,1)S(1)}, u32[]{:S(2)}, u32[]{:S(2)}) collective-permute-start(bf16[256,768]{1,0:T(8,128)(2,1)} %unit_rows.3.refs_4_.refs_2_), channel_id=1, source_target_pairs={{0,4},{1,5},{2,6},{3,7},{4,0},{5,1},{6,2},{7,3},{8,12},{9,13},{10,... | collective-permute-start | bytes 1179656 | tf_op jit(solution)/shard_map/ppermute | solution.py:15
  35.8 1.4 %collective-permute-start.8 = (bf16[256,768]{1,0:T(8,128)(2,1)}, bf16[256,768]{1,0:T(8,128)(2,1)S(1)}, u32[]{:S(2)}, u32[]{:S(2)}) collective-permute-start(bf16[256,768]{1,0:T(8,128)(2,1)} %unit_rows.3.refs_4_.refs_2_), channel_id=1, source_target_pairs={{0,6},{1,7},{2,4},{3,5},{4,2},{5,3},{6,0},{7,1},{8,14},{9,15},{10,... | collective-permute-start | bytes 1179656 | tf_op jit(solution)/shard_map/ppermute | solution.py:15
  38.6 7.4 %collective-permute-done.6.refs_5_ = bf16[256,768]{1,0:T(8,128)(2,1)S(1)} collective-permute-done((bf16[256,768]{1,0:T(8,128)(2,1)}, bf16[256,768]{1,0:T(8,128)(2,1)S(1)}, u32[]{:S(2)}, u32[]{:S(2)}) %collective-permute-start.6) | collective-permute-done | bytes 393248 | tf_op jit(solution)/shard_map/ppermute | solution.py:15
  46.0 5.1 %collective-permute-done.7.refs_6_ = bf16[256,768]{1,0:T(8,128)(2,1)S(1)} collective-permute-done((bf16[256,768]{1,0:T(8,128)(2,1)}, bf16[256,768]{1,0:T(8,128)(2,1)S(1)}, u32[]{:S(2)}, u32[]{:S(2)}) %collective-permute-start.7) | collective-permute-done | bytes 393248 | tf_op jit(solution)/shard_map/ppermute | solution.py:15
  51.1 1.5 %collective-permute-done.8.refs_7_ = bf16[256,768]{1,0:T(8,128)(2,1)S(1)} collective-permute-done((bf16[256,768]{1,0:T(8,128)(2,1)}, bf16[256,768]{1,0:T(8,128)(2,1)S(1)}, u32[]{:S(2)}, u32[]{:S(2)}) %collective-permute-start.8) | collective-permute-done | bytes 393248 | tf_op jit(solution)/shard_map/ppermute | solution.py:15
  53.4 0.9 copy-done
  54.3 3.8 %speech_part.3 = f32[128,768]{1,0:T(8,128)} custom-call(f32[1]{0:T(128)S(6)} %copy.7.refs_0_, f32[1]{0:T(128)S(6)} %copy.8.refs_1_, s32[1,128]{1,0:T(1,128)} %copy-done.16, bf16[512,768]{1,0:T(8,128)(2,1)} %copy-done, bf16[256,768]{1,0:T(8,128)(2,1)} %unit_rows.3.refs_4_.refs_2_, bf16[256,768]{1,0:T(8,128)(2,1)} %copy-done.1, bf16[256,768]{1,0:T(8,128)(2,1)} %copy-done.2, ...), custom_call_target="tpu_custom_call" | custom-call | flops 402653184 | bytes 2359816 | tf_op jit(solution)/shard_map/speech_part/pallas_call | solution.py:24
  58.1 0.9 collective-permute-start.15
  59.0 1.5 %collective-permute-start.16 = (s32[1,128]{1,0:T(1,128)S(1)}, s32[1,128]{1,0:T(1,128)S(1)}, u32[]{:S(2)}, u32[]{:S(2)}) collective-permute-start(s32[1,128]{1,0:T(1,128)S(1)} %bitcast.5), channel_id=1, source_target_pairs={{0,4},{1,5},{2,6},{3,7},{4,0},{5,1},{6,2},{7,3},{8,12},{9,13},{10,... | collective-permute-start | bytes 1544 | tf_op jit(solution)/shard_map/ppermute | solution.py:15
  60.5 1.0 %collective-permute-start.17 = (s32[1,128]{1,0:T(1,128)S(1)}, s32[1,128]{1,0:T(1,128)S(1)}, u32[]{:S(2)}, u32[]{:S(2)}) collective-permute-start(s32[1,128]{1,0:T(1,128)S(1)} %bitcast.6), channel_id=1, source_target_pairs={{0,6},{1,7},{2,4},{3,5},{4,2},{5,3},{6,0},{7,1},{8,14},{9,15},{10,... | collective-permute-start | bytes 1544 | tf_op jit(solution)/shard_map/ppermute | solution.py:15
  61.8 2.0 %collective-permute-start.13 = (s32[1,128]{1,0:T(1,128)S(1)}, s32[1,128]{1,0:T(1,128)S(1)}, u32[]{:S(2)}, u32[]{:S(2)}) collective-permute-start(s32[1,128]{1,0:T(1,128)S(1)} %bitcast.8), channel_id=1, source_target_pairs={{0,5},{1,4},{2,7},{3,6},{4,1},{5,0},{6,3},{7,2},{8,13},{9,12},{10,... | collective-permute-start | bytes 1544 | tf_op jit(solution)/shard_map/ppermute | solution.py:15
  64.1 0.9 collective-permute-done.17.refs_7_
  65.6 2.9 %text_part.1.refs_8_ = f32[256,768]{1,0:T(8,128)} custom-call(f32[1]{0:T(128)S(6)} %copy.7.refs_0_, f32[1]{0:T(128)S(6)} %copy.8.refs_1_, bf16[256,768]{1,0:T(8,128)(2,1)} %unit_rows.3.refs_4_.refs_2_, bf16[512,768]{1,0:T(8,128)(2,1)} %unit_rows.2.refs_3_, s32[1,128]{1,0:T(1,128)} %bitcast.1, s32[1,128]{1,0:T(1,128)} %copy-done.19, s32[1,128]{1,0:T(1,128)} %copy-done.20, ...), custom_call_target="tpu_custom_call" | custom-call | flops 402653184 | bytes 1181704 | tf_op jit(solution)/shard_map/text_part/pallas_call | solution.py:24
  69.6 3.1 %text_part_sum.1 = (f32[64,768]{1,0:T(8,128)}, f32[64,768]{1,0:T(8,128)}, f32[64,768]{1,0:T(8,128)}, f32[64,768]{1,0:T(8,128)}) custom-call(f32[1]{0:T(128)S(6)} %copy.7.refs_0_, f32[1]{0:T(128)S(6)} %copy.8.refs_1_, bf16[256,768]{1,0:T(8,128)(2,1)} %unit_rows.3.refs_4_.refs_2_, bf16[512,768]{1,0:T(8,128)(2,1)} %copy-done, s32[1,128]{1,0:T(1,128)} %copy-done.16, ...), custom_call_target="tpu_custom_call" | custom-call | flops 402653184 | bytes 1968136 | tf_op jit(solution)/shard_map/text_part_sum/pallas_call | solution.py:24
  72.7 2.5 %collective-permute-start.18 = (f32[64,768]{1,0:T(8,128)}, f32[64,768]{1,0:T(8,128)S(1)}, u32[]{:S(2)}, u32[]{:S(2)}) collective-permute-start(f32[64,768]{1,0:T(8,128)} %get-tuple-element.7), channel_id=1, source_target_pairs={{0,8},{8,0},{16,24},{24,16},{1,9},{9,1},{17,25},{25,17},{2,10},{10... | collective-permute-start | bytes 589832 | tf_op jit(solution)/shard_map/ppermute | solution.py:15
  75.2 1.1 %collective-permute-start.19 = (f32[64,768]{1,0:T(8,128)}, f32[64,768]{1,0:T(8,128)S(1)}, u32[]{:S(2)}, u32[]{:S(2)}) collective-permute-start(f32[64,768]{1,0:T(8,128)} %get-tuple-element.8), channel_id=1, source_target_pairs={{0,16},{8,24},{16,0},{24,8},{1,17},{9,25},{17,1},{25,9},{2,18},{10... | collective-permute-start | bytes 589832 | tf_op jit(solution)/shard_map/ppermute | solution.py:15
  76.3 1.5 %collective-permute-start.20 = (f32[64,768]{1,0:T(8,128)}, f32[64,768]{1,0:T(8,128)S(1)}, u32[]{:S(2)}, u32[]{:S(2)}) collective-permute-start(f32[64,768]{1,0:T(8,128)} %get-tuple-element.9), channel_id=1, source_target_pairs={{0,24},{8,16},{16,8},{24,0},{1,25},{9,17},{17,9},{25,1},{2,26},{10... | collective-permute-start | bytes 589832 | tf_op jit(solution)/shard_map/ppermute | solution.py:15
  77.7 3.8 %speech_part.2.refs_1_ = f32[128,768]{1,0:T(8,128)} custom-call(f32[1]{0:T(128)S(6)} %copy.7.refs_0_, f32[1]{0:T(128)S(6)} %copy.8.refs_1_, s32[1,128]{1,0:T(1,128)} %bitcast.2, bf16[512,768]{1,0:T(8,128)(2,1)} %unit_rows.2.refs_3_, bf16[256,768]{1,0:T(8,128)(2,1)} %unit_rows.3.refs_4_.refs_2_, bf16[256,768]{1,0:T(8,128)(2,1)} %copy-done.1, ...), custom_call_target="tpu_custom_call" | custom-call | flops 402653184 | bytes 2359816 | tf_op jit(solution)/shard_map/speech_part/pallas_call | solution.py:24
  81.5 2.4 %collective-permute-done.18.refs_2_ = f32[64,768]{1,0:T(8,128)S(1)} collective-permute-done((f32[64,768]{1,0:T(8,128)}, f32[64,768]{1,0:T(8,128)S(1)}, u32[]{:S(2)}, u32[]{:S(2)}) %collective-permute-start.18) | collective-permute-done | bytes 196640 | tf_op jit(solution)/shard_map/ppermute | solution.py:15
  84.0 8.6 %collective-permute-done.19.refs_3_ = f32[64,768]{1,0:T(8,128)S(1)} collective-permute-done((f32[64,768]{1,0:T(8,128)}, f32[64,768]{1,0:T(8,128)S(1)}, u32[]{:S(2)}, u32[]{:S(2)}) %collective-permute-start.19) | collective-permute-done | bytes 196640 | tf_op jit(solution)/shard_map/ppermute | solution.py:15
  93.3 2.1 %finish.3 = f32[64,768]{1,0:T(8,128)} custom-call(bf16[64,768]{1,0:T(8,128)(2,1)} %refs_0_.11, f32[64,768]{1,0:T(8,128)} %get-tuple-element.6.refs_1_, f32[64,768]{1,0:T(8,128)} %copy-done.9, f32[64,768]{1,0:T(8,128)} %copy-done.10, f32[64,768]{1,0:T(8,128)} %copy-done.11), custom_call_target="tpu_custom_call" | custom-call | bytes 884736 | tf_op jit(solution)/shard_map/finish/pallas_call | solution.py:24
  96.2 2.2 %finish.2 = f32[128,768]{1,0:T(8,128)} custom-call(bf16[128,768]{1,0:T(8,128)(2,1)} %refs_0_.10, f32[128,768]{1,0:T(8,128)} %speech_part.2.refs_1_, f32[128,768]{1,0:T(8,128)} %copy-done.5), custom_call_target="tpu_custom_call" | custom-call | bytes 983040 | tf_op jit(solution)/shard_map/finish/pallas_call | solution.py:24
  (64 shorter events, 7.9 us)
Async XLA Ops:
  0.6 17.6 %copy-start.4 = (bf16[64,768]{1,0:T(8,128)(2,1)S(1)}, bf16[64,768]{1,0:T(8,128)(2,1)}, u32[]{:S(2)}) copy-start(bf16[64,768]{1,0:T(8,128)(2,1)} %refs_0_.11) | copy-start | bytes 294916
  0.6 8.9 %collective-permute-start = (bf16[128,768]{1,0:T(8,128)(2,1)}, bf16[128,768]{1,0:T(8,128)(2,1)S(1)}, u32[]{:S(2)}, u32[]{:S(2)}) collective-permute-start(bf16[128,768]{1,0:T(8,128)(2,1)} %refs_0_.10), channel_id=1, source_target_pairs={{0,2},{1,3},{2,0},{3,1},{4,6},{5,7},{6,4},{7,5},{8,10},{9,11},{10,... | collective-permute-start | bytes 589832 | tf_op jit(solution)/shard_map/ppermute | solution.py:15
  3.6 10.8 %collective-permute-start.1 = (bf16[128,768]{1,0:T(8,128)(2,1)}, bf16[128,768]{1,0:T(8,128)(2,1)S(1)}, u32[]{:S(2)}, u32[]{:S(2)}) collective-permute-start(bf16[128,768]{1,0:T(8,128)(2,1)} %refs_0_.10), channel_id=1, source_target_pairs={{0,4},{1,5},{2,6},{3,7},{4,0},{5,1},{6,2},{7,3},{8,12},{9,13},{10,... | collective-permute-start | bytes 589832 | tf_op jit(solution)/shard_map/ppermute | solution.py:15
  5.2 9.3 %collective-permute-start.2 = (bf16[128,768]{1,0:T(8,128)(2,1)}, bf16[128,768]{1,0:T(8,128)(2,1)S(1)}, u32[]{:S(2)}, u32[]{:S(2)}) collective-permute-start(bf16[128,768]{1,0:T(8,128)(2,1)} %refs_0_.10), channel_id=1, source_target_pairs={{0,6},{1,7},{2,4},{3,5},{4,2},{5,3},{6,0},{7,1},{8,14},{9,15},{10,... | collective-permute-start | bytes 589832 | tf_op jit(solution)/shard_map/ppermute | solution.py:15
  9.6 4.9 %copy-start.6 = (bf16[128,768]{1,0:T(8,128)(2,1)}, bf16[128,768]{1,0:T(8,128)(2,1)S(1)}, u32[]{:S(2)}) copy-start(bf16[128,768]{1,0:T(8,128)(2,1)S(1)} %collective-permute-done.refs_1_) | copy-start | bytes 589828
  18.2 34.4 %collective-permute-start.10 = (bf16[512,768]{1,0:T(8,128)(2,1)}, bf16[512,768]{1,0:T(8,128)(2,1)S(1)}, u32[]{:S(2)}, u32[]{:S(2)}) collective-permute-start(bf16[512,768]{1,0:T(8,128)(2,1)} %unit_rows.2.refs_3_), channel_id=1, source_target_pairs={{0,1},{1,0},{2,3},{3,2},{4,5},{5,4},{6,7},{7,6},{8,9},{9,8},{10,11... | collective-permute-start | bytes 2359304 | tf_op jit(solution)/shard_map/ppermute | solution.py:15
  18.2 5.2 %collective-permute-start.3 = (bf16[64,768]{1,0:T(8,128)(2,1)S(1)}, bf16[64,768]{1,0:T(8,128)(2,1)S(1)}, u32[]{:S(2)}, u32[]{:S(2)}) collective-permute-start(bf16[64,768]{1,0:T(8,128)(2,1)S(1)} %copy-done.4), channel_id=1, source_target_pairs={{0,8},{8,0},{16,24},{24,16},{1,9},{9,1},{17,25},{25,17},{2,10},{10... | collective-permute-start | bytes 294920 | tf_op jit(solution)/shard_map/ppermute | solution.py:15
  19.8 10.7 %collective-permute-start.4 = (bf16[64,768]{1,0:T(8,128)(2,1)S(1)}, bf16[64,768]{1,0:T(8,128)(2,1)S(1)}, u32[]{:S(2)}, u32[]{:S(2)}) collective-permute-start(bf16[64,768]{1,0:T(8,128)(2,1)S(1)} %copy-done.4), channel_id=1, source_target_pairs={{0,16},{8,24},{16,0},{24,8},{1,17},{9,25},{17,1},{25,9},{2,18},{10... | collective-permute-start | bytes 294920 | tf_op jit(solution)/shard_map/ppermute | solution.py:15
  22.4 8.2 %collective-permute-start.5 = (bf16[64,768]{1,0:T(8,128)(2,1)S(1)}, bf16[64,768]{1,0:T(8,128)(2,1)S(1)}, u32[]{:S(2)}, u32[]{:S(2)}) collective-permute-start(bf16[64,768]{1,0:T(8,128)(2,1)S(1)} %copy-done.4), channel_id=1, source_target_pairs={{0,24},{8,16},{16,8},{24,0},{1,25},{9,17},{17,9},{25,1},{2,26},{10... | collective-permute-start | bytes 294920 | tf_op jit(solution)/shard_map/ppermute | solution.py:15
  23.4 7.1 %copy-start.12 = (bf16[64,768]{1,0:T(8,128)(2,1)}, bf16[64,768]{1,0:T(8,128)(2,1)S(1)}, u32[]{:S(2)}) copy-start(bf16[64,768]{1,0:T(8,128)(2,1)S(1)} %collective-permute-done.3.refs_1_) | copy-start | bytes 294916
  33.8 3.5 %copy-start.15 = (s32[128]{0:T(128)S(1)}, s32[128]{0:T(128)}, u32[]{:S(2)}) copy-start(s32[128]{0:T(128)} %param.7) | copy-start | bytes 1540
  33.8 12.3 %collective-permute-start.6 = (bf16[256,768]{1,0:T(8,128)(2,1)}, bf16[256,768]{1,0:T(8,128)(2,1)S(1)}, u32[]{:S(2)}, u32[]{:S(2)}) collective-permute-start(bf16[256,768]{1,0:T(8,128)(2,1)} %unit_rows.3.refs_4_.refs_2_), channel_id=1, source_target_pairs={{0,2},{1,3},{2,0},{3,1},{4,6},{5,7},{6,4},{7,5},{8,10},{9,11},{10,... | collective-permute-start | bytes 1179656 | tf_op jit(solution)/shard_map/ppermute | solution.py:15
  34.3 16.8 %collective-permute-start.7 = (bf16[256,768]{1,0:T(8,128)(2,1)}, bf16[256,768]{1,0:T(8,128)(2,1)S(1)}, u32[]{:S(2)}, u32[]{:S(2)}) collective-permute-start(bf16[256,768]{1,0:T(8,128)(2,1)} %unit_rows.3.refs_4_.refs_2_), channel_id=1, source_target_pairs={{0,4},{1,5},{2,6},{3,7},{4,0},{5,1},{6,2},{7,3},{8,12},{9,13},{10,... | collective-permute-start | bytes 1179656 | tf_op jit(solution)/shard_map/ppermute | solution.py:15
  35.8 16.8 %collective-permute-start.8 = (bf16[256,768]{1,0:T(8,128)(2,1)}, bf16[256,768]{1,0:T(8,128)(2,1)S(1)}, u32[]{:S(2)}, u32[]{:S(2)}) collective-permute-start(bf16[256,768]{1,0:T(8,128)(2,1)} %unit_rows.3.refs_4_.refs_2_), channel_id=1, source_target_pairs={{0,6},{1,7},{2,4},{3,5},{4,2},{5,3},{6,0},{7,1},{8,14},{9,15},{10,... | collective-permute-start | bytes 1179656 | tf_op jit(solution)/shard_map/ppermute | solution.py:15
  37.3 1.3 %collective-permute-start.9 = (s32[1,128]{1,0:T(1,128)S(1)}, s32[1,128]{1,0:T(1,128)S(1)}, u32[]{:S(2)}, u32[]{:S(2)}) collective-permute-start(s32[1,128]{1,0:T(1,128)S(1)} %bitcast.3), channel_id=1, source_target_pairs={{0,1},{1,0},{2,3},{3,2},{4,5},{5,4},{6,7},{7,6},{8,9},{9,8},{10,11... | collective-permute-start | bytes 1544 | tf_op jit(solution)/shard_map/ppermute | solution.py:15
  38.6 14.1 %copy-start.16 = (s32[1,128]{1,0:T(1,128)}, s32[1,128]{1,0:T(1,128)S(1)}, u32[]{:S(2)}) copy-start(s32[1,128]{1,0:T(1,128)S(1)} %collective-permute-done.9.refs_2_.refs_4_) | copy-start | bytes 1540
  46.0 6.6 %copy-start.1 = (bf16[256,768]{1,0:T(8,128)(2,1)}, bf16[256,768]{1,0:T(8,128)(2,1)S(1)}, u32[]{:S(2)}) copy-start(bf16[256,768]{1,0:T(8,128)(2,1)S(1)} %collective-permute-done.6.refs_5_) | copy-start | bytes 1179652
  51.1 1.5 %copy-start.2 = (bf16[256,768]{1,0:T(8,128)(2,1)}, bf16[256,768]{1,0:T(8,128)(2,1)S(1)}, u32[]{:S(2)}) copy-start(bf16[256,768]{1,0:T(8,128)(2,1)S(1)} %collective-permute-done.7.refs_6_) | copy-start | bytes 1179652
  53.4 0.9 copy-start
  58.1 37.4 %collective-permute-start.11 = (f32[128,768]{1,0:T(8,128)}, f32[128,768]{1,0:T(8,128)S(1)}, u32[]{:S(2)}, u32[]{:S(2)}) collective-permute-start(f32[128,768]{1,0:T(8,128)} %speech_part.3), channel_id=1, source_target_pairs={{0,1},{1,0},{2,3},{3,2},{4,5},{5,4},{6,7},{7,6},{8,9},{9,8},{10,11... | collective-permute-start | bytes 1179656 | tf_op jit(solution)/shard_map/ppermute | solution.py:15
  58.1 3.7 %collective-permute-start.15 = (s32[1,128]{1,0:T(1,128)S(1)}, s32[1,128]{1,0:T(1,128)S(1)}, u32[]{:S(2)}, u32[]{:S(2)}) collective-permute-start(s32[1,128]{1,0:T(1,128)S(1)} %bitcast.4), channel_id=1, source_target_pairs={{0,2},{1,3},{2,0},{3,1},{4,6},{5,7},{6,4},{7,5},{8,10},{9,11},{10,... | collective-permute-start | bytes 1544 | tf_op jit(solution)/shard_map/ppermute | solution.py:15
  59.0 4.7 %collective-permute-start.16 = (s32[1,128]{1,0:T(1,128)S(1)}, s32[1,128]{1,0:T(1,128)S(1)}, u32[]{:S(2)}, u32[]{:S(2)}) collective-permute-start(s32[1,128]{1,0:T(1,128)S(1)} %bitcast.5), channel_id=1, source_target_pairs={{0,4},{1,5},{2,6},{3,7},{4,0},{5,1},{6,2},{7,3},{8,12},{9,13},{10,... | collective-permute-start | bytes 1544 | tf_op jit(solution)/shard_map/ppermute | solution.py:15
  60.5 4.4 %collective-permute-start.17 = (s32[1,128]{1,0:T(1,128)S(1)}, s32[1,128]{1,0:T(1,128)S(1)}, u32[]{:S(2)}, u32[]{:S(2)}) collective-permute-start(s32[1,128]{1,0:T(1,128)S(1)} %bitcast.6), channel_id=1, source_target_pairs={{0,6},{1,7},{2,4},{3,5},{4,2},{5,3},{6,0},{7,1},{8,14},{9,15},{10,... | collective-permute-start | bytes 1544 | tf_op jit(solution)/shard_map/ppermute | solution.py:15
  61.6 6.9 %collective-permute-start.12 = (s32[1,128]{1,0:T(1,128)S(1)}, s32[1,128]{1,0:T(1,128)S(1)}, u32[]{:S(2)}, u32[]{:S(2)}) collective-permute-start(s32[1,128]{1,0:T(1,128)S(1)} %bitcast.7), channel_id=1, source_target_pairs={{0,3},{1,2},{2,1},{3,0},{4,7},{5,6},{6,5},{7,4},{8,11},{9,10},{10,... | collective-permute-start | bytes 1544 | tf_op jit(solution)/shard_map/ppermute | solution.py:15
  61.8 3.2 %copy-start.19 = (s32[1,128]{1,0:T(1,128)}, s32[1,128]{1,0:T(1,128)S(1)}, u32[]{:S(2)}) copy-start(s32[1,128]{1,0:T(1,128)S(1)} %collective-permute-done.15.refs_5_) | copy-start | bytes 1540
  61.8 6.7 %collective-permute-start.13 = (s32[1,128]{1,0:T(1,128)S(1)}, s32[1,128]{1,0:T(1,128)S(1)}, u32[]{:S(2)}, u32[]{:S(2)}) collective-permute-start(s32[1,128]{1,0:T(1,128)S(1)} %bitcast.8), channel_id=1, source_target_pairs={{0,5},{1,4},{2,7},{3,6},{4,1},{5,0},{6,3},{7,2},{8,13},{9,12},{10,... | collective-permute-start | bytes 1544 | tf_op jit(solution)/shard_map/ppermute | solution.py:15
  63.8 1.2 %copy-start.20 = (s32[1,128]{1,0:T(1,128)}, s32[1,128]{1,0:T(1,128)S(1)}, u32[]{:S(2)}) copy-start(s32[1,128]{1,0:T(1,128)S(1)} %collective-permute-done.16.refs_6_) | copy-start | bytes 1540
  63.8 4.7 %collective-permute-start.14 = (s32[1,128]{1,0:T(1,128)S(1)}, s32[1,128]{1,0:T(1,128)S(1)}, u32[]{:S(2)}, u32[]{:S(2)}) collective-permute-start(s32[1,128]{1,0:T(1,128)S(1)} %bitcast.9), channel_id=1, source_target_pairs={{0,7},{1,6},{2,5},{3,4},{4,3},{5,2},{6,1},{7,0},{8,15},{9,14},{10,... | collective-permute-start | bytes 1544 | tf_op jit(solution)/shard_map/ppermute | solution.py:15
  72.7 11.2 %collective-permute-start.18 = (f32[64,768]{1,0:T(8,128)}, f32[64,768]{1,0:T(8,128)S(1)}, u32[]{:S(2)}, u32[]{:S(2)}) collective-permute-start(f32[64,768]{1,0:T(8,128)} %get-tuple-element.7), channel_id=1, source_target_pairs={{0,8},{8,0},{16,24},{24,16},{1,9},{9,1},{17,25},{25,17},{2,10},{10... | collective-permute-start | bytes 589832 | tf_op jit(solution)/shard_map/ppermute | solution.py:15
  75.2 17.4 %collective-permute-start.19 = (f32[64,768]{1,0:T(8,128)}, f32[64,768]{1,0:T(8,128)S(1)}, u32[]{:S(2)}, u32[]{:S(2)}) collective-permute-start(f32[64,768]{1,0:T(8,128)} %get-tuple-element.8), channel_id=1, source_target_pairs={{0,16},{8,24},{16,0},{24,8},{1,17},{9,25},{17,1},{25,9},{2,18},{10... | collective-permute-start | bytes 589832 | tf_op jit(solution)/shard_map/ppermute | solution.py:15
  76.3 16.3 %collective-permute-start.20 = (f32[64,768]{1,0:T(8,128)}, f32[64,768]{1,0:T(8,128)S(1)}, u32[]{:S(2)}, u32[]{:S(2)}) collective-permute-start(f32[64,768]{1,0:T(8,128)} %get-tuple-element.9), channel_id=1, source_target_pairs={{0,24},{8,16},{16,8},{24,0},{1,25},{9,17},{17,9},{25,1},{2,26},{10... | collective-permute-start | bytes 589832 | tf_op jit(solution)/shard_map/ppermute | solution.py:15
  84.0 8.6 %copy-start.9 = (f32[64,768]{1,0:T(8,128)}, f32[64,768]{1,0:T(8,128)S(1)}, u32[]{:S(2)}) copy-start(f32[64,768]{1,0:T(8,128)S(1)} %collective-permute-done.18.refs_2_) | copy-start | bytes 589828
  (12 other events, 7.8 us)

commit v2 on v1

v2 whole, which is shorter than its diff:
```python
import functools
import jax
import jax.numpy as jnp
from jax import lax
from jax.experimental import pallas as pl
from jax.experimental.pallas import tpu as pltpu
from jax.sharding import PartitionSpec as P

MARK_ROWS = 16
RADIX = 256
CHUNK = 512


def exchanged(value, axis, mask):
    size = lax.axis_size(axis)
    return lax.ppermute(value, axis, [(i, i ^ mask) for i in range(size)])


def total_bytes(values):
    return sum(v.size * v.dtype.itemsize for v in jax.tree.leaves(values))


def call(body, out_shape, operands, after=(), flops=0, temporary=0, name="kernel"):
    specs = []
    for v in operands:
        scalar = v.shape == (1,)
        specs.append(pl.BlockSpec(memory_space=pltpu.SMEM if scalar else pltpu.VMEM))
    specs += [pl.BlockSpec(memory_space=pl.ANY) for _ in after]
    used = len(operands)

    def whole(*refs):
        body(*refs[:used], *refs[used + len(after) :])

    moved = total_bytes(operands) + total_bytes(out_shape)
    return pl.pallas_call(
        whole,
        out_shape=out_shape,
        in_specs=specs,
        out_specs=jax.tree.map(lambda _: pl.BlockSpec(memory_space=pltpu.VMEM), out_shape),
        compiler_params=pltpu.CompilerParams(vmem_limit_bytes=(4 << 20) + 2 * moved + temporary),
        cost_estimate=pl.CostEstimate(flops=flops, bytes_accessed=moved, transcendentals=0),
        name=name,
    )(*operands, *after)


def direction(values):
    floats = values.astype(jnp.float32)
    norms = jnp.sqrt(jnp.sum(floats * floats, axis=-1, keepdims=True) + 1e-06)
    return floats / norms, norms


def prepare_body(audio, sentence, label, speech, text):
    rows = audio.shape[0]
    speech[0:rows, :] = direction(audio[...])[0].astype(jnp.bfloat16)
    text[...] = direction(sentence[...])[0].astype(jnp.bfloat16)
    number = label[...]
    digits = jnp.concatenate([number % RADIX, number // RADIX], axis=1).astype(jnp.float32)
    wide = jnp.concatenate(
        [digits, jnp.zeros((1, speech.shape[1] - 2 * rows), jnp.float32)], axis=1
    )
    speech[rows : rows + MARK_ROWS, :] = jnp.broadcast_to(
        wide, (MARK_ROWS, speech.shape[1])
    ).astype(jnp.bfloat16)


def join_body(counts, *refs):
    outs = refs[sum(counts) :]
    at = 0
    for count, out in zip(counts, outs):
        rows = refs[at].shape[0]
        for k in range(count):
            out[k * rows : (k + 1) * rows, :] = refs[at + k][...]
        at += count


def marks_of(block, rows):
    digits = block[rows : rows + MARK_ROWS, 0 : 2 * rows][0:1, :].astype(jnp.float32)
    return digits[:, 0:rows] + RADIX * digits[:, rows : 2 * rows]


def coefficients(dots, match, sharp, shift):
    logits = sharp * dots + shift
    probs = 1.0 / (1.0 + jnp.exp(-logits))
    return (sharp * (probs - jnp.where(match, 1.0, 0.0))).astype(jnp.bfloat16)


def dot_rows(left, right):
    return lax.dot_general(left, right, (((1,), (1,)), ((), ())), preferred_element_type=jnp.float32)


def text_part_body(rows, own_text, *refs):
    sharp, shift = refs[0][0], refs[1][0]
    text = jnp.concatenate([refs[2][...], refs[3][...]], axis=0)
    speech = refs[4]
    start = refs[5] if len(refs) > 6 and refs[5].shape == text.shape else None
    outs = refs[5:] if start is None else refs[6:]
    groups = lax.axis_size("group")
    members = lax.axis_size("member")
    group = lax.axis_index("group")
    member = lax.axis_index("member")
    stride = rows + MARK_ROWS
    count = speech.shape[0] // stride
    step = max(1, min(count, CHUNK // rows))
    iota = lax.broadcasted_iota(jnp.int32, (own_text, step * rows), 0)
    ids = [((group ^ k) * members + member) * own_text + iota for k in range(groups)]
    ids = jnp.concatenate(ids, axis=0).astype(jnp.float32)
    total = None if start is None else start[...]
    for first in range(0, count, step):
        blocks = range(first, first + step)
        chunk = jnp.concatenate([speech[k * stride : k * stride + rows, :] for k in blocks], axis=0)
        marks = [marks_of(speech.at[k * stride : (k + 1) * stride, :], rows) for k in blocks]
        match = ids == jnp.concatenate(marks, axis=1)
        coef = coefficients(dot_rows(text, chunk), match, sharp, shift)
        part = jnp.dot(coef, chunk, preferred_element_type=jnp.float32)
        total = part if total is None else total + part
    size = outs[0].shape[0]
    for k, out in enumerate(outs):
        out[...] = total[k * size : (k + 1) * size, :]


def speech_part_body(rows, own_text, places, *refs):
    sharp, shift = refs[0][0], refs[1][0]
    speech, texts, out = refs[2], refs[3:-1], refs[-1]
    groups = lax.axis_size("group")
    members = lax.axis_size("member")
    group = lax.axis_index("group")
    member = lax.axis_index("member")
    marks = jnp.broadcast_to(marks_of(speech, rows), (rows, rows)).T[:, 0:1]
    block = speech[0:rows, :]
    many = groups
    lane = lax.broadcasted_iota(jnp.int32, (1, many * own_text), 1)
    total = None
    at = 0
    for ref in texts:
        for first in range(0, ref.shape[0], many * own_text):
            text = ref[first : first + many * own_text, :]
            ids = lane
            for i, (k, j) in enumerate(places[at : at + many]):
                base = ((group ^ k) * members + (member ^ (2 * j))) * own_text
                ids = jnp.where(lane // own_text == i, lane + (base - i * own_text), ids)
            at += many
            match = marks == ids.astype(jnp.float32)
            coef = coefficients(dot_rows(block, text), match, sharp, shift)
            part = jnp.dot(coef, text, preferred_element_type=jnp.float32)
            total = part if total is None else total + part
    out[...] = total


def finish_body(*refs):
    values, parts, out = refs[0], refs[1:-1], refs[-1]
    heading, norms = direction(values[...])
    back = parts[0][...]
    for part in parts[1:]:
        back = back + part[...]
    along = jnp.sum(heading * back, axis=-1, keepdims=True)
    out[...] = (back - heading * along) / norms


def shards(audio_vectors, sentence_vectors, matching_indices, sharpness_array, offset_term):
    members = lax.axis_size("member")
    groups = lax.axis_size("group")
    chips = members // 2
    rows, width = audio_vectors.shape
    own_text = sentence_vectors.shape[0]
    scalars = [sharpness_array, offset_term]
    label = matching_indices.reshape(1, rows)

    def bf16(*shape):
        return jax.ShapeDtypeStruct(shape, jnp.bfloat16)

    def f32(*shape):
        return jax.ShapeDtypeStruct(shape, jnp.float32)

    speech_own, text_own = call(
        prepare_body,
        [bf16(rows + MARK_ROWS, width), bf16(own_text, width)],
        [audio_vectors, sentence_vectors, label],
        name="unit_rows",
    )
    speech_blocks = [speech_own]
    for k in range(1, chips):
        speech_blocks.append(exchanged(speech_own, "member", 2 * k))
    text_blocks = [text_own]
    for k in range(1, groups):
        text_blocks.append(exchanged(text_own, "group", k))
    half_rows = groups * own_text // 2
    speech, upper, lower = call(
        functools.partial(join_body, (chips, groups // 2, groups // 2)),
        [bf16(chips * (rows + MARK_ROWS), width), bf16(half_rows, width), bf16(half_rows, width)],
        speech_blocks + text_blocks,
        name="join_rows",
    )
    other = exchanged(speech, "member", 1)

    column = groups * own_text
    text_part = functools.partial(text_part_body, rows, own_text)
    work = 4 * column * chips * rows * width
    temporary = 4 * column * (6 * CHUNK + 3 * width)
    half = call(
        text_part,
        [f32(column, width)],
        scalars + [upper, lower, speech],
        (),
        work,
        temporary,
        "text_part",
    )
    parts = call(
        text_part,
        [f32(own_text, width)] * groups,
        scalars + [upper, lower, other, half[0]],
        (),
        work,
        temporary,
        "text_part_sum",
    )
    text_back = [parts[0]]
    for k in range(1, groups):
        text_back.append(exchanged(parts[k], "group", k))

    bits = [1 << i for i in range(chips.bit_length() - 1)]
    orders = [bits, bits[1:] + bits[:1]]
    held = [upper, lower]
    places = [
        [(k, 0) for k in range(groups // 2)],
        [(k, 0) for k in range(groups // 2, groups)],
    ]
    came = []
    for step in range(len(bits)):
        masks = [order[step] for order in orders]
        came = [exchanged(v, "member", 2 * mask) for v, mask in zip(held, masks)]
        theirs = [[(k, j ^ mask) for k, j in own] for own, mask in zip(places, masks)]
        if step + 1 < len(bits):
            held = call(
                functools.partial(join_body, (2, 2)),
                [bf16(2 * v.shape[0], width) for v in held],
                [held[0], came[0], held[1], came[1]],
                (parts[0],) if step + 2 == len(bits) else (),
                name="join_texts",
            )
            places = [own + other for own, other in zip(places, theirs)]
    texts = [*held, *came]
    places = places[0] + places[1] + theirs[0] + theirs[1]

    speech_part = functools.partial(speech_part_body, rows, own_text, places)
    work = 4 * rows * chips * column * width
    stride = rows + MARK_ROWS
    away = call(
        speech_part,
        f32(rows, width),
        scalars + [other[0:stride]] + texts,
        (parts[0],),
        work,
        temporary,
        "speech_part",
    )
    back = exchanged(away, "member", 1)
    home = call(
        speech_part,
        f32(rows, width),
        scalars + [speech_own] + texts,
        (away,),
        work,
        temporary,
        "speech_part",
    )
    text_grad = call(
        finish_body, f32(own_text, width), [sentence_vectors, *text_back], (), 1 << 33, name="finish_text"
    )
    speech_grad = call(
        finish_body, f32(rows, width), [audio_vectors, home, back], name="finish_speech"
    )
    return (speech_grad, text_grad)


def solution(mesh):
    in_specs = (
        P(("group", "member"), None),
        P(("group", "member"), None),
        P(("group", "member")),
        P(),
        P(),
    )
    out_specs = (P(("group", "member"), None), P(("group", "member"), None))
    return jax.shard_map(shards, mesh=mesh, in_specs=in_specs, out_specs=out_specs, check_vma=False)
```

time: 99.2 us -> 52.5 us (0.53)
  waiting for transfers between devices: 43.2 us -> 18.6 us
  Pallas kernels: 22.4 us -> 6.61 us
  local copies, waits for them, and re-layouts: 7.39 us -> 2.49 us
    ppermute x21 -> x15, waiting for transfers between devices: 43.2 us -> 18.6 us  [exchanged(): return lax.ppermute(value, axis, [(i, i ^ mask) for i in range(size)])]
    pallas_call x8 -> x9, Pallas kernels: 22.4 us -> 6.61 us  [call(): pl.pallas_call(whole, out_shape=out_shape, in_specs=specs, out_specs=jax....]
    unnamed x46 -> x10, local copies, waits for them, and re-layouts: 7.39 us -> 2.48 us
    ppermute x21 -> x15, starting transfers between devices: 23.4 us -> 22.6 us  [exchanged(): return lax.ppermute(value, axis, [(i, i ^ mask) for i in range(size)])]
  transfers between devices with their start and end apart: 21 -> 15, of which waited for: 10 -> 8; matrix products, arithmetic and copies ran while one was open for 0% -> 0% of each run, Pallas kernels for 14% -> 10%
where the time goes in v2:
time: 52.5 us; the launch traced here: 52.3 us
  starting transfers between devices  22.6 us (43%)
  waiting for transfers between devices  18.6 us (35%)
  Pallas kernels  6.61 us (13%)
  local copies, waits for them, and re-layouts  2.49 us (5%)
  between operations  2.06 us (4%)
    ppermute x15, starting transfers between devices, exchanged(): return lax.ppermute(value, axis, [(i, i ^ mask) for i in range(size)])  22.6 us
    ppermute x15, waiting for transfers between devices, exchanged(): return lax.ppermute(value, axis, [(i, i ^ mask) for i in range(size)])  18.6 us
    pallas_call x9, Pallas kernels, call(): pl.pallas_call(whole, out_shape=out_shape, in_specs=specs, out_specs=jax....  6.61 us
    unnamed x10, local copies, waits for them, and re-layouts  2.48 us
  transfers between devices with their start and end apart: 15, of which 8 were waited for; matrix products, arithmetic and copies ran while one was open for 0% of the time, Pallas kernels for 10%

profile of v2, /device:TPU:0, one launch (start us, length us, event | category | flops | bytes accessed | tf_op | source)
XLA Modules:
  0.0 52.3 jit_solution(4894930419215996902)
XLA Ops:
  0.6 0.6 %copy-done.4 = s32[128]{0:T(128)S(1)} copy-done((s32[128]{0:T(128)S(1)}, s32[128]{0:T(128)}, u32[]{:S(2)}) %copy-start.4) | copy-done | bytes 536
  1.3 0.9 %copy-done = bf16[128,768]{1,0:T(8,128)(2,1)S(1)} copy-done((bf16[128,768]{1,0:T(8,128)(2,1)S(1)}, bf16[128,768]{1,0:T(8,128)(2,1)}, u32[]{:S(2)}) %copy-start) | copy-done | bytes 196632
  2.2 0.9 %copy-done.2 = bf16[64,768]{1,0:T(8,128)(2,1)S(1)} copy-done((bf16[64,768]{1,0:T(8,128)(2,1)S(1)}, bf16[64,768]{1,0:T(8,128)(2,1)}, u32[]{:S(2)}) %copy-start.2) | copy-done | bytes 98328
  3.1 0.2 unit_rows.1
  3.3 3.0 %collective-permute-start = (bf16[144,768]{1,0:T(8,128)(2,1)S(1)}, bf16[144,768]{1,0:T(8,128)(2,1)S(1)}, u32[]{:S(2)}, u32[]{:S(2)}) collective-permute-start(bf16[144,768]{1,0:T(8,128)(2,1)S(1)} %get-tuple-element.13.refs_0_.refs_2_), channel_id=1, source_target_pairs={{0,2},{1,3},{2,0},{3,1},{4,6},{5,7},{6,4},{7,5},{8,10},{9,11},{10,... | collective-permute-start | bytes 663560 | tf_op jit(solution)/shard_map/ppermute | solution.py:16
  6.3 1.5 %collective-permute-start.1 = (bf16[144,768]{1,0:T(8,128)(2,1)S(1)}, bf16[144,768]{1,0:T(8,128)(2,1)S(1)}, u32[]{:S(2)}, u32[]{:S(2)}) collective-permute-start(bf16[144,768]{1,0:T(8,128)(2,1)S(1)} %get-tuple-element.13.refs_0_.refs_2_), channel_id=1, source_target_pairs={{0,4},{1,5},{2,6},{3,7},{4,0},{5,1},{6,2},{7,3},{8,12},{9,13},{10,... | collective-permute-start | bytes 663560 | tf_op jit(solution)/shard_map/ppermute | solution.py:16
  7.8 2.0 %collective-permute-start.3 = (bf16[64,768]{1,0:T(8,128)(2,1)S(1)}, bf16[64,768]{1,0:T(8,128)(2,1)S(1)}, u32[]{:S(2)}, u32[]{:S(2)}) collective-permute-start(bf16[64,768]{1,0:T(8,128)(2,1)S(1)} %get-tuple-element.14.refs_4_), channel_id=1, source_target_pairs={{0,8},{8,0},{16,24},{24,16},{1,9},{9,1},{17,25},{25,17},{2,10},{10... | collective-permute-start | bytes 294920 | tf_op jit(solution)/shard_map/ppermute | solution.py:16
  9.8 2.6 %collective-permute-start.4 = (bf16[64,768]{1,0:T(8,128)(2,1)S(1)}, bf16[64,768]{1,0:T(8,128)(2,1)S(1)}, u32[]{:S(2)}, u32[]{:S(2)}) collective-permute-start(bf16[64,768]{1,0:T(8,128)(2,1)S(1)} %get-tuple-element.14.refs_4_), channel_id=1, source_target_pairs={{0,16},{8,24},{16,0},{24,8},{1,17},{9,25},{17,1},{25,9},{2,18},{10... | collective-permute-start | bytes 294920 | tf_op jit(solution)/shard_map/ppermute | solution.py:16
  12.4 1.0 %collective-permute-done.3.refs_5_ = bf16[64,768]{1,0:T(8,128)(2,1)S(1)} collective-permute-done((bf16[64,768]{1,0:T(8,128)(2,1)S(1)}, bf16[64,768]{1,0:T(8,128)(2,1)S(1)}, u32[]{:S(2)}, u32[]{:S(2)}) %collective-permute-start.3) | collective-permute-done | bytes 98336 | tf_op jit(solution)/shard_map/ppermute | solution.py:16
  13.4 3.2 %collective-permute-start.5 = (bf16[64,768]{1,0:T(8,128)(2,1)S(1)}, bf16[64,768]{1,0:T(8,128)(2,1)S(1)}, u32[]{:S(2)}, u32[]{:S(2)}) collective-permute-start(bf16[64,768]{1,0:T(8,128)(2,1)S(1)} %get-tuple-element.14.refs_4_), channel_id=1, source_target_pairs={{0,24},{8,16},{16,8},{24,0},{1,25},{9,17},{17,9},{25,1},{2,26},{10... | collective-permute-start | bytes 294920 | tf_op jit(solution)/shard_map/ppermute | solution.py:16
  16.6 1.6 %collective-permute-done.4.refs_6_ = bf16[64,768]{1,0:T(8,128)(2,1)S(1)} collective-permute-done((bf16[64,768]{1,0:T(8,128)(2,1)S(1)}, bf16[64,768]{1,0:T(8,128)(2,1)S(1)}, u32[]{:S(2)}, u32[]{:S(2)}) %collective-permute-start.4) | collective-permute-done | bytes 98336 | tf_op jit(solution)/shard_map/ppermute | solution.py:16
  18.2 1.7 %collective-permute-done.5.refs_7_ = bf16[64,768]{1,0:T(8,128)(2,1)S(1)} collective-permute-done((bf16[64,768]{1,0:T(8,128)(2,1)S(1)}, bf16[64,768]{1,0:T(8,128)(2,1)S(1)}, u32[]{:S(2)}, u32[]{:S(2)}) %collective-permute-start.5) | collective-permute-done | bytes 98336 | tf_op jit(solution)/shard_map/ppermute | solution.py:16
  20.0 0.1 join_rows.1
  20.0 0.1 collective-permute-start.8
  20.1 2.0 %collective-permute-start.6 = (bf16[128,768]{1,0:T(8,128)(2,1)S(1)}, bf16[128,768]{1,0:T(8,128)(2,1)S(1)}, u32[]{:S(2)}, u32[]{:S(2)}) collective-permute-start(bf16[128,768]{1,0:T(8,128)(2,1)S(1)} %get-tuple-element.15.refs_2_.refs_0_), channel_id=1, source_target_pairs={{0,2},{1,3},{2,0},{3,1},{4,6},{5,7},{6,4},{7,5},{8,10},{9,11},{10,... | collective-permute-start | bytes 589832 | tf_op jit(solution)/shard_map/ppermute | solution.py:16
  22.1 1.5 %collective-permute-start.7 = (bf16[128,768]{1,0:T(8,128)(2,1)S(1)}, bf16[128,768]{1,0:T(8,128)(2,1)S(1)}, u32[]{:S(2)}, u32[]{:S(2)}) collective-permute-start(bf16[128,768]{1,0:T(8,128)(2,1)S(1)} %get-tuple-element.16.refs_3_.refs_2_), channel_id=1, source_target_pairs={{0,4},{1,5},{2,6},{3,7},{4,0},{5,1},{6,2},{7,3},{8,12},{9,13},{10,... | collective-permute-start | bytes 589832 | tf_op jit(solution)/shard_map/ppermute | solution.py:16
  25.0 0.8 %text_part.1.refs_5_ = f32[256,768]{1,0:T(8,128)S(1)} custom-call(f32[1]{0:T(128)S(6)} %copy.7.refs_0_, f32[1]{0:T(128)S(6)} %copy.8.refs_1_, bf16[128,768]{1,0:T(8,128)(2,1)S(1)} %get-tuple-element.15.refs_2_.refs_0_, bf16[128,768]{1,0:T(8,128)(2,1)S(1)} %get-tuple-element.16.refs_3_.refs_2_, bf16[576,768]{1,0:T(8,128)(2,1)S(1)} %get-tuple-element.17.refs_4_), custom_call_target="tpu_custom_call" | custom-call | flops 402653184 | bytes 2064392 | tf_op jit(solution)/shard_map/text_part/pallas_call | solution.py:35
  25.7 0.8 %text_part_sum.1 = (f32[64,768]{1,0:T(8,128)S(1)}, f32[64,768]{1,0:T(8,128)S(1)}, f32[64,768]{1,0:T(8,128)S(1)}, f32[64,768]{1,0:T(8,128)S(1)}) custom-call(f32[1]{0:T(128)S(6)} %copy.7.refs_0_, f32[1]{0:T(128)S(6)} %copy.8.refs_1_, bf16[128,768]{1,0:T(8,128)(2,1)S(1)} %get-tuple-element.15.refs_2_.refs_0_, ...), custom_call_target="tpu_custom_call" | custom-call | flops 402653184 | bytes 2850824 | tf_op jit(solution)/shard_map/text_part_sum/pallas_call | solution.py:35
  26.5 1.1 %collective-permute-done.6.refs_1_ = bf16[128,768]{1,0:T(8,128)(2,1)S(1)} collective-permute-done((bf16[128,768]{1,0:T(8,128)(2,1)S(1)}, bf16[128,768]{1,0:T(8,128)(2,1)S(1)}, u32[]{:S(2)}, u32[]{:S(2)}) %collective-permute-start.6) | collective-permute-done | bytes 196640 | tf_op jit(solution)/shard_map/ppermute | solution.py:16
  27.6 1.5 %collective-permute-done.7.refs_3_ = bf16[128,768]{1,0:T(8,128)(2,1)S(1)} collective-permute-done((bf16[128,768]{1,0:T(8,128)(2,1)S(1)}, bf16[128,768]{1,0:T(8,128)(2,1)S(1)}, u32[]{:S(2)}, u32[]{:S(2)}) %collective-permute-start.7) | collective-permute-done | bytes 196640 | tf_op jit(solution)/shard_map/ppermute | solution.py:16
  29.2 0.4 collective-permute-start.10
  29.5 1.7 %collective-permute-start.9 = (bf16[256,768]{1,0:T(8,128)(2,1)S(1)}, bf16[256,768]{1,0:T(8,128)(2,1)S(1)}, u32[]{:S(2)}, u32[]{:S(2)}) collective-permute-start(bf16[256,768]{1,0:T(8,128)(2,1)S(1)} %get-tuple-element.19.refs_3_), channel_id=1, source_target_pairs={{0,4},{1,5},{2,6},{3,7},{4,0},{5,1},{6,2},{7,3},{8,12},{9,13},{10,... | collective-permute-start | bytes 1179656 | tf_op jit(solution)/shard_map/ppermute | solution.py:16
  31.3 0.8 %collective-permute-start.12 = (f32[64,768]{1,0:T(8,128)S(1)}, f32[64,768]{1,0:T(8,128)S(1)}, u32[]{:S(2)}, u32[]{:S(2)}) collective-permute-start(f32[64,768]{1,0:T(8,128)S(1)} %get-tuple-element.21), channel_id=1, source_target_pairs={{0,8},{8,0},{16,24},{24,16},{1,9},{9,1},{17,25},{25,17},{2,10},{10... | collective-permute-start | bytes 589832 | tf_op jit(solution)/shard_map/ppermute | solution.py:16
  32.1 2.5 %collective-permute-start.13 = (f32[64,768]{1,0:T(8,128)S(1)}, f32[64,768]{1,0:T(8,128)S(1)}, u32[]{:S(2)}, u32[]{:S(2)}) collective-permute-start(f32[64,768]{1,0:T(8,128)S(1)} %get-tuple-element.22), channel_id=1, source_target_pairs={{0,16},{8,24},{16,0},{24,8},{1,17},{9,25},{17,1},{25,9},{2,18},{10... | collective-permute-start | bytes 589832 | tf_op jit(solution)/shard_map/ppermute | solution.py:16
  34.6 1.1 %collective-permute-start.14 = (f32[64,768]{1,0:T(8,128)S(1)}, f32[64,768]{1,0:T(8,128)S(1)}, u32[]{:S(2)}, u32[]{:S(2)}) collective-permute-start(f32[64,768]{1,0:T(8,128)S(1)} %get-tuple-element.23), channel_id=1, source_target_pairs={{0,24},{8,16},{16,8},{24,0},{1,25},{9,17},{17,9},{25,1},{2,26},{10... | collective-permute-start | bytes 589832 | tf_op jit(solution)/shard_map/ppermute | solution.py:16
  35.7 3.9 %collective-permute-done.10.refs_6_ = bf16[256,768]{1,0:T(8,128)(2,1)S(1)} collective-permute-done((bf16[256,768]{1,0:T(8,128)(2,1)S(1)}, bf16[256,768]{1,0:T(8,128)(2,1)S(1)}, u32[]{:S(2)}, u32[]{:S(2)}) %collective-permute-start.10) | collective-permute-done | bytes 393248 | tf_op jit(solution)/shard_map/ppermute | solution.py:16
  39.6 0.3 collective-permute-done.9.refs_5_
  39.9 1.5 %speech_part.2.refs_7_ = f32[128,768]{1,0:T(8,128)S(1)} custom-call(f32[1]{0:T(128)S(6)} %copy.7.refs_0_, f32[1]{0:T(128)S(6)} %copy.8.refs_1_, bf16[144,768]{1,0:T(8,128)(2,1)S(1)} %slice.4.refs_2_, bf16[256,768]{1,0:T(8,128)(2,1)S(1)} %get-tuple-element.19.refs_3_, bf16[256,768]{1,0:T(8,128)(2,1)S(1)} %get-tuple-element.20.refs_4_, ...), custom_call_target="tpu_custom_call" | custom-call | flops 402653184 | bytes 2187272 | tf_op jit(solution)/shard_map/speech_part/pallas_call | solution.py:35
  41.5 7.5 %collective-permute-done.13.refs_3_ = f32[64,768]{1,0:T(8,128)S(1)} collective-permute-done((f32[64,768]{1,0:T(8,128)S(1)}, f32[64,768]{1,0:T(8,128)S(1)}, u32[]{:S(2)}, u32[]{:S(2)}) %collective-permute-start.13) | collective-permute-done | bytes 196640 | tf_op jit(solution)/shard_map/ppermute | solution.py:16
  48.9 0.9 %finish_text.1 = f32[64,768]{1,0:T(8,128)} custom-call(bf16[64,768]{1,0:T(8,128)(2,1)S(1)} %copy-done.3, f32[64,768]{1,0:T(8,128)S(1)} %get-tuple-element.18.refs_4_.refs_7_.refs_1_, f32[64,768]{1,0:T(8,128)S(1)} %collective-permute-done.12.refs_2_, f32[64,768]{1,0:T(8,128)S(1)} %collective-permute-done.13.refs_3_, f32[64,768]{1,0:T(8,128)S(1)} %collective-permute-done.14.refs_4_), custom_call_target="tpu_custom_call" | custom-call | flops 8589934592 | bytes 1081344 | tf_op jit(solution)/shard_map/finish_text/pallas_call | solution.py:35
  49.8 1.5 %speech_part.3.refs_1_ = f32[128,768]{1,0:T(8,128)S(1)} custom-call(f32[1]{0:T(128)S(6)} %copy.7.refs_0_, f32[1]{0:T(128)S(6)} %copy.8.refs_1_, bf16[144,768]{1,0:T(8,128)(2,1)S(1)} %get-tuple-element.13.refs_0_.refs_2_, bf16[256,768]{1,0:T(8,128)(2,1)S(1)} %get-tuple-element.19.refs_3_, bf16[256,768]{1,0:T(8,128)(2,1)S(1)} %get-tuple-element.20.refs_4_, ...), custom_call_target="tpu_custom_call" | custom-call | flops 402653184 | bytes 2187272 | tf_op jit(solution)/shard_map/speech_part/pallas_call | solution.py:35
  51.3 1.0 %finish_speech.1 = f32[128,768]{1,0:T(8,128)} custom-call(bf16[128,768]{1,0:T(8,128)(2,1)S(1)} %copy-done.1, f32[128,768]{1,0:T(8,128)S(1)} %speech_part.3.refs_1_, f32[128,768]{1,0:T(8,128)S(1)} %collective-permute-done.11.refs_2_), custom_call_target="tpu_custom_call" | custom-call | bytes 1376256 | tf_op jit(solution)/shard_map/finish_speech/pallas_call | solution.py:35
  (18 shorter events, 0.2 us)
Async XLA Ops:
  0.6 0.7 %copy-start.4 = (s32[128]{0:T(128)S(1)}, s32[128]{0:T(128)}, u32[]{:S(2)}) copy-start(s32[128]{0:T(128)} %param.7) | copy-start | bytes 1540
  1.3 0.9 %copy-start = (bf16[128,768]{1,0:T(8,128)(2,1)S(1)}, bf16[128,768]{1,0:T(8,128)(2,1)}, u32[]{:S(2)}) copy-start(bf16[128,768]{1,0:T(8,128)(2,1)} %refs_0_.8) | copy-start | bytes 589828
  2.2 0.9 %copy-start.2 = (bf16[64,768]{1,0:T(8,128)(2,1)S(1)}, bf16[64,768]{1,0:T(8,128)(2,1)}, u32[]{:S(2)}) copy-start(bf16[64,768]{1,0:T(8,128)(2,1)} %refs_0_.9) | copy-start | bytes 294916
  3.3 16.7 %collective-permute-start = (bf16[144,768]{1,0:T(8,128)(2,1)S(1)}, bf16[144,768]{1,0:T(8,128)(2,1)S(1)}, u32[]{:S(2)}, u32[]{:S(2)}) collective-permute-start(bf16[144,768]{1,0:T(8,128)(2,1)S(1)} %get-tuple-element.13.refs_0_.refs_2_), channel_id=1, source_target_pairs={{0,2},{1,3},{2,0},{3,1},{4,6},{5,7},{6,4},{7,5},{8,10},{9,11},{10,... | collective-permute-start | bytes 663560 | tf_op jit(solution)/shard_map/ppermute | solution.py:16
  6.3 13.7 %collective-permute-start.1 = (bf16[144,768]{1,0:T(8,128)(2,1)S(1)}, bf16[144,768]{1,0:T(8,128)(2,1)S(1)}, u32[]{:S(2)}, u32[]{:S(2)}) collective-permute-start(bf16[144,768]{1,0:T(8,128)(2,1)S(1)} %get-tuple-element.13.refs_0_.refs_2_), channel_id=1, source_target_pairs={{0,4},{1,5},{2,6},{3,7},{4,0},{5,1},{6,2},{7,3},{8,12},{9,13},{10,... | collective-permute-start | bytes 663560 | tf_op jit(solution)/shard_map/ppermute | solution.py:16
  7.8 12.2 %collective-permute-start.2 = (bf16[144,768]{1,0:T(8,128)(2,1)S(1)}, bf16[144,768]{1,0:T(8,128)(2,1)S(1)}, u32[]{:S(2)}, u32[]{:S(2)}) collective-permute-start(bf16[144,768]{1,0:T(8,128)(2,1)S(1)} %get-tuple-element.13.refs_0_.refs_2_), channel_id=1, source_target_pairs={{0,6},{1,7},{2,4},{3,5},{4,2},{5,3},{6,0},{7,1},{8,14},{9,15},{10,... | collective-permute-start | bytes 663560 | tf_op jit(solution)/shard_map/ppermute | solution.py:16
  7.8 5.6 %collective-permute-start.3 = (bf16[64,768]{1,0:T(8,128)(2,1)S(1)}, bf16[64,768]{1,0:T(8,128)(2,1)S(1)}, u32[]{:S(2)}, u32[]{:S(2)}) collective-permute-start(bf16[64,768]{1,0:T(8,128)(2,1)S(1)} %get-tuple-element.14.refs_4_), channel_id=1, source_target_pairs={{0,8},{8,0},{16,24},{24,16},{1,9},{9,1},{17,25},{25,17},{2,10},{10... | collective-permute-start | bytes 294920 | tf_op jit(solution)/shard_map/ppermute | solution.py:16
  9.8 8.3 %collective-permute-start.4 = (bf16[64,768]{1,0:T(8,128)(2,1)S(1)}, bf16[64,768]{1,0:T(8,128)(2,1)S(1)}, u32[]{:S(2)}, u32[]{:S(2)}) collective-permute-start(bf16[64,768]{1,0:T(8,128)(2,1)S(1)} %get-tuple-element.14.refs_4_), channel_id=1, source_target_pairs={{0,16},{8,24},{16,0},{24,8},{1,17},{9,25},{17,1},{25,9},{2,18},{10... | collective-permute-start | bytes 294920 | tf_op jit(solution)/shard_map/ppermute | solution.py:16
  13.4 6.5 %collective-permute-start.5 = (bf16[64,768]{1,0:T(8,128)(2,1)S(1)}, bf16[64,768]{1,0:T(8,128)(2,1)S(1)}, u32[]{:S(2)}, u32[]{:S(2)}) collective-permute-start(bf16[64,768]{1,0:T(8,128)(2,1)S(1)} %get-tuple-element.14.refs_4_), channel_id=1, source_target_pairs={{0,24},{8,16},{16,8},{24,0},{1,25},{9,17},{17,9},{25,1},{2,26},{10... | collective-permute-start | bytes 294920 | tf_op jit(solution)/shard_map/ppermute | solution.py:16
  20.0 5.7 %collective-permute-start.8 = (bf16[576,768]{1,0:T(8,128)(2,1)S(1)}, bf16[576,768]{1,0:T(8,128)(2,1)S(1)}, u32[]{:S(2)}, u32[]{:S(2)}) collective-permute-start(bf16[576,768]{1,0:T(8,128)(2,1)S(1)} %get-tuple-element.17.refs_4_), channel_id=1, source_target_pairs={{0,1},{1,0},{2,3},{3,2},{4,5},{5,4},{6,7},{7,6},{8,9},{9,8},{10,11... | collective-permute-start | bytes 2654216 | tf_op jit(solution)/shard_map/ppermute | solution.py:16
  20.1 7.5 %collective-permute-start.6 = (bf16[128,768]{1,0:T(8,128)(2,1)S(1)}, bf16[128,768]{1,0:T(8,128)(2,1)S(1)}, u32[]{:S(2)}, u32[]{:S(2)}) collective-permute-start(bf16[128,768]{1,0:T(8,128)(2,1)S(1)} %get-tuple-element.15.refs_2_.refs_0_), channel_id=1, source_target_pairs={{0,2},{1,3},{2,0},{3,1},{4,6},{5,7},{6,4},{7,5},{8,10},{9,11},{10,... | collective-permute-start | bytes 589832 | tf_op jit(solution)/shard_map/ppermute | solution.py:16
  22.1 7.0 %collective-permute-start.7 = (bf16[128,768]{1,0:T(8,128)(2,1)S(1)}, bf16[128,768]{1,0:T(8,128)(2,1)S(1)}, u32[]{:S(2)}, u32[]{:S(2)}) collective-permute-start(bf16[128,768]{1,0:T(8,128)(2,1)S(1)} %get-tuple-element.16.refs_3_.refs_2_), channel_id=1, source_target_pairs={{0,4},{1,5},{2,6},{3,7},{4,0},{5,1},{6,2},{7,3},{8,12},{9,13},{10,... | collective-permute-start | bytes 589832 | tf_op jit(solution)/shard_map/ppermute | solution.py:16
  29.2 10.4 %collective-permute-start.10 = (bf16[256,768]{1,0:T(8,128)(2,1)S(1)}, bf16[256,768]{1,0:T(8,128)(2,1)S(1)}, u32[]{:S(2)}, u32[]{:S(2)}) collective-permute-start(bf16[256,768]{1,0:T(8,128)(2,1)S(1)} %get-tuple-element.20.refs_4_), channel_id=1, source_target_pairs={{0,2},{1,3},{2,0},{3,1},{4,6},{5,7},{6,4},{7,5},{8,10},{9,11},{10,... | collective-permute-start | bytes 1179656 | tf_op jit(solution)/shard_map/ppermute | solution.py:16
  29.5 10.4 %collective-permute-start.9 = (bf16[256,768]{1,0:T(8,128)(2,1)S(1)}, bf16[256,768]{1,0:T(8,128)(2,1)S(1)}, u32[]{:S(2)}, u32[]{:S(2)}) collective-permute-start(bf16[256,768]{1,0:T(8,128)(2,1)S(1)} %get-tuple-element.19.refs_3_), channel_id=1, source_target_pairs={{0,4},{1,5},{2,6},{3,7},{4,0},{5,1},{6,2},{7,3},{8,12},{9,13},{10,... | collective-permute-start | bytes 1179656 | tf_op jit(solution)/shard_map/ppermute | solution.py:16
  31.3 10.2 %collective-permute-start.12 = (f32[64,768]{1,0:T(8,128)S(1)}, f32[64,768]{1,0:T(8,128)S(1)}, u32[]{:S(2)}, u32[]{:S(2)}) collective-permute-start(f32[64,768]{1,0:T(8,128)S(1)} %get-tuple-element.21), channel_id=1, source_target_pairs={{0,8},{8,0},{16,24},{24,16},{1,9},{9,1},{17,25},{25,17},{2,10},{10... | collective-permute-start | bytes 589832 | tf_op jit(solution)/shard_map/ppermute | solution.py:16
  32.1 16.9 %collective-permute-start.13 = (f32[64,768]{1,0:T(8,128)S(1)}, f32[64,768]{1,0:T(8,128)S(1)}, u32[]{:S(2)}, u32[]{:S(2)}) collective-permute-start(f32[64,768]{1,0:T(8,128)S(1)} %get-tuple-element.22), channel_id=1, source_target_pairs={{0,16},{8,24},{16,0},{24,8},{1,17},{9,25},{17,1},{25,9},{2,18},{10... | collective-permute-start | bytes 589832 | tf_op jit(solution)/shard_map/ppermute | solution.py:16
  34.6 14.3 %collective-permute-start.14 = (f32[64,768]{1,0:T(8,128)S(1)}, f32[64,768]{1,0:T(8,128)S(1)}, u32[]{:S(2)}, u32[]{:S(2)}) collective-permute-start(f32[64,768]{1,0:T(8,128)S(1)} %get-tuple-element.23), channel_id=1, source_target_pairs={{0,24},{8,16},{16,8},{24,0},{1,25},{9,17},{17,9},{25,1},{2,26},{10... | collective-permute-start | bytes 589832 | tf_op jit(solution)/shard_map/ppermute | solution.py:16
  35.7 13.3 %copy-start.3 = (bf16[64,768]{1,0:T(8,128)(2,1)S(1)}, bf16[64,768]{1,0:T(8,128)(2,1)}, u32[]{:S(2)}) copy-start(bf16[64,768]{1,0:T(8,128)(2,1)} %refs_0_.9) | copy-start | bytes 294916
  41.4 9.9 %collective-permute-start.11 = (f32[128,768]{1,0:T(8,128)S(1)}, f32[128,768]{1,0:T(8,128)S(1)}, u32[]{:S(2)}, u32[]{:S(2)}) collective-permute-start(f32[128,768]{1,0:T(8,128)S(1)} %speech_part.2.refs_7_), channel_id=1, source_target_pairs={{0,1},{1,0},{2,3},{3,2},{4,5},{5,4},{6,7},{7,6},{8,9},{9,8},{10,11... | collective-permute-start | bytes 1179656 | tf_op jit(solution)/shard_map/ppermute | solution.py:16
  49.8 1.5 %copy-start.1 = (bf16[128,768]{1,0:T(8,128)(2,1)S(1)}, bf16[128,768]{1,0:T(8,128)(2,1)}, u32[]{:S(2)}) copy-start(bf16[128,768]{1,0:T(8,128)(2,1)} %refs_0_.8) | copy-start | bytes 589828

commit v3 on v2

--- a/solution.py
+++ b/solution.py
@@ -49,7 +49,15 @@
     return floats / norms, norms
 
 
-def prepare_body(audio, sentence, label, speech, text):
+def prepare_body(audio_hbm, sentence_hbm, label_hbm, speech, text, audio, sentence, label, done):
+    pairs = [(audio_hbm, audio), (sentence_hbm, sentence), (label_hbm, label)]
+    copies = [
+        pltpu.make_async_copy(source, target, done.at[i]) for i, (source, target) in enumerate(pairs)
+    ]
+    for copy in copies:
+        copy.start()
+    for copy in copies:
+        copy.wait()
     rows = audio.shape[0]
     speech[0:rows, :] = direction(audio[...])[0].astype(jnp.bfloat16)
     text[...] = direction(sentence[...])[0].astype(jnp.bfloat16)
@@ -63,14 +71,23 @@
     ).astype(jnp.bfloat16)
 
 
-def join_body(counts, *refs):
-    outs = refs[sum(counts) :]
-    at = 0
-    for count, out in zip(counts, outs):
-        rows = refs[at].shape[0]
-        for k in range(count):
-            out[k * rows : (k + 1) * rows, :] = refs[at + k][...]
-        at += count
+def unit_body(values, out):
+    out[...] = direction(values[...])[0].astype(jnp.bfloat16)
+
+
+def join_body(chips, raw, *refs):
+    speech, text = refs[-2:]
+    rows = refs[0].shape[0]
+    for k in range(chips):
+        speech[k * rows : (k + 1) * rows, :] = refs[k][...]
+    rows = refs[chips].shape[0]
+    for k, is_raw in enumerate(raw):
+        block = refs[chips + k]
+        target = text.at[k * rows : (k + 1) * rows, :]
+        if is_raw:
+            unit_body(block, target)
+        else:
+            target[...] = block[...]
 
 
 def marks_of(block, rows):
@@ -90,10 +107,9 @@
 
 def text_part_body(rows, own_text, *refs):
     sharp, shift = refs[0][0], refs[1][0]
-    text = jnp.concatenate([refs[2][...], refs[3][...]], axis=0)
-    speech = refs[4]
-    start = refs[5] if len(refs) > 6 and refs[5].shape == text.shape else None
-    outs = refs[5:] if start is None else refs[6:]
+    text, speech = refs[2][...], refs[3]
+    start = refs[4] if len(refs) > 5 and refs[4].shape == text.shape else None
+    outs = refs[4:] if start is None else refs[5:]
     groups = lax.axis_size("group")
     members = lax.axis_size("member")
     group = lax.axis_index("group")
@@ -118,7 +134,7 @@
         out[...] = total[k * size : (k + 1) * size, :]
 
 
-def speech_part_body(rows, own_text, places, *refs):
+def speech_part_body(rows, own_text, *refs):
     sharp, shift = refs[0][0], refs[1][0]
     speech, texts, out = refs[2], refs[3:-1], refs[-1]
     groups = lax.axis_size("group")
@@ -127,33 +143,33 @@
     member = lax.axis_index("member")
     marks = jnp.broadcast_to(marks_of(speech, rows), (rows, rows)).T[:, 0:1]
     block = speech[0:rows, :]
-    many = groups
-    lane = lax.broadcasted_iota(jnp.int32, (1, many * own_text), 1)
+    lane = lax.broadcasted_iota(jnp.int32, (1, groups * own_text), 1)
+    base = (group ^ (lane // own_text)) * members * own_text + lane % own_text
     total = None
-    at = 0
-    for ref in texts:
-        for first in range(0, ref.shape[0], many * own_text):
-            text = ref[first : first + many * own_text, :]
-            ids = lane
-            for i, (k, j) in enumerate(places[at : at + many]):
-                base = ((group ^ k) * members + (member ^ (2 * j))) * own_text
-                ids = jnp.where(lane // own_text == i, lane + (base - i * own_text), ids)
-            at += many
-            match = marks == ids.astype(jnp.float32)
-            coef = coefficients(dot_rows(block, text), match, sharp, shift)
-            part = jnp.dot(coef, text, preferred_element_type=jnp.float32)
-            total = part if total is None else total + part
+    for j, text in enumerate(texts):
+        ids = (base + (member ^ (2 * j)) * own_text).astype(jnp.float32)
+        coef = coefficients(dot_rows(block, text[...]), marks == ids, sharp, shift)
+        part = jnp.dot(coef, text[...], preferred_element_type=jnp.float32)
+        total = part if total is None else total + part
     out[...] = total
 
 
-def finish_body(*refs):
-    values, parts, out = refs[0], refs[1:-1], refs[-1]
-    heading, norms = direction(values[...])
-    back = parts[0][...]
-    for part in parts[1:]:
-        back = back + part[...]
+def sum_body(*refs):
+    total = refs[0][...]
+    for ref in refs[1:-1]:
+        total = total + ref[...]
+    refs[-1][...] = total
+
+
+def project(values, back, out):
+    heading, norms = direction(values)
     along = jnp.sum(heading * back, axis=-1, keepdims=True)
     out[...] = (back - heading * along) / norms
+
+
+def finish_body(audio, home, back, sentence, text_back, speech_grad, text_grad):
+    project(sentence[...], text_back[...], text_grad)
+    project(audio[...], home[...] + back[...], speech_grad)
 
 
 def shards(audio_vectors, sentence_vectors, matching_indices, sharpness_array, offset_term):
@@ -171,78 +187,65 @@
     def f32(*shape):
         return jax.ShapeDtypeStruct(shape, jnp.float32)
 
-    speech_own, text_own = call(
+    speech_own, text_own = pl.pallas_call(
         prepare_body,
-        [bf16(rows + MARK_ROWS, width), bf16(own_text, width)],
-        [audio_vectors, sentence_vectors, label],
+        out_shape=[bf16(rows + MARK_ROWS, width), bf16(own_text, width)],
+        in_specs=[pl.BlockSpec(memory_space=pltpu.HBM)] * 3,
+        out_specs=[pl.BlockSpec(memory_space=pltpu.VMEM)] * 2,
+        scratch_shapes=[
+            pltpu.VMEM((rows, width), jnp.bfloat16),
+            pltpu.VMEM((own_text, width), jnp.bfloat16),
+            pltpu.VMEM((1, rows), jnp.int32),
+            pltpu.SemaphoreType.DMA((3,)),
+        ],
+        compiler_params=pltpu.CompilerParams(vmem_limit_bytes=8 << 20),
         name="unit_rows",
-    )
+    )(*[pltpu.with_memory_space_constraint(v, pltpu.HBM) for v in (audio_vectors, sentence_vectors, label)])
+    text_blocks = [text_own] + [None] * (groups - 1)
+    raw = [False] * groups
+    for k in [1 << i for i in reversed(range(groups.bit_length() - 1))]:
+        for j in range(0, groups, 2 * k):
+            came = exchanged(text_blocks[j] if j else sentence_vectors, "group", k)
+            raw[j + k] = not j
+            if not j and k > 1:
+                came = call(unit_body, bf16(own_text, width), [came], (), 1 << 33, name="unit_far")
+                raw[j + k] = False
+            text_blocks[j + k] = came
     speech_blocks = [speech_own]
     for k in range(1, chips):
         speech_blocks.append(exchanged(speech_own, "member", 2 * k))
-    text_blocks = [text_own]
-    for k in range(1, groups):
-        text_blocks.append(exchanged(text_own, "group", k))
-    half_rows = groups * own_text // 2
-    speech, upper, lower = call(
-        functools.partial(join_body, (chips, groups // 2, groups // 2)),
-        [bf16(chips * (rows + MARK_ROWS), width), bf16(half_rows, width), bf16(half_rows, width)],
+    column = groups * own_text
+    speech, text = call(
+        functools.partial(join_body, chips, raw),
+        [bf16(chips * (rows + MARK_ROWS), width), bf16(column, width)],
         speech_blocks + text_blocks,
         name="join_rows",
     )
     other = exchanged(speech, "member", 1)
-
-    column = groups * own_text
+    texts = [text]
+    for k in range(1, chips):
+        texts.append(exchanged(text, "member", 2 * k))
+
     text_part = functools.partial(text_part_body, rows, own_text)
     work = 4 * column * chips * rows * width
     temporary = 4 * column * (6 * CHUNK + 3 * width)
     half = call(
-        text_part,
-        [f32(column, width)],
-        scalars + [upper, lower, speech],
-        (),
-        work,
-        temporary,
-        "text_part",
+        text_part, [f32(column, width)], scalars + [text, speech], (), work, temporary, "text_part"
     )
     parts = call(
         text_part,
         [f32(own_text, width)] * groups,
-        scalars + [upper, lower, other, half[0]],
+        scalars + [text, other, half[0]],
         (),
         work,
         temporary,
         "text_part_sum",
     )
     text_back = [parts[0]]
-    for k in range(1, groups):
+    for k in reversed(range(1, groups)):
         text_back.append(exchanged(parts[k], "group", k))
 
-    bits = [1 << i for i in range(chips.bit_length() - 1)]
-    orders = [bits, bits[1:] + bits[:1]]
-    held = [upper, lower]
-    places = [
-        [(k, 0) for k in range(groups // 2)],
-        [(k, 0) for k in range(groups // 2, groups)],
-    ]
-    came = []
-    for step in range(len(bits)):
-        masks = [order[step] for order in orders]
-        came = [exchanged(v, "member", 2 * mask) for v, mask in zip(held, masks)]
-        theirs = [[(k, j ^ mask) for k, j in own] for own, mask in zip(places, masks)]
-        if step + 1 < len(bits):
-            held = call(
-                functools.partial(join_body, (2, 2)),
-                [bf16(2 * v.shape[0], width) for v in held],
-                [held[0], came[0], held[1], came[1]],
-                (parts[0],) if step + 2 == len(bits) else (),
-                name="join_texts",
-            )
-            places = [own + other for own, other in zip(places, theirs)]
-    texts = [*held, *came]
-    places = places[0] + places[1] + theirs[0] + theirs[1]
-
-    speech_part = functools.partial(speech_part_body, rows, own_text, places)
+    speech_part = functools.partial(speech_part_body, rows, own_text)
     work = 4 * rows * chips * column * width
     stride = rows + MARK_ROWS
     away = call(
@@ -264,11 +267,12 @@
         temporary,
         "speech_part",
     )
-    text_grad = call(
-        finish_body, f32(own_text, width), [sentence_vectors, *text_back], (), 1 << 33, name="finish_text"
-    )
-    speech_grad = call(
-        finish_body, f32(rows, width), [audio_vectors, home, back], name="finish_speech"
+    text_back = call(sum_body, f32(own_text, width), text_back, (), 1 << 33, name="text_sum")
+    speech_grad, text_grad = call(
+        finish_body,
+        [f32(rows, width), f32(own_text, width)],
+        [audio_vectors, home, back, sentence_vectors, text_back],
+        name="finish",
     )
     return (speech_grad, text_grad)
 

time: 52.5 us -> 46.9 us (0.89)
  starting transfers between devices: 22.6 us -> 18.1 us
  local copies, waits for them, and re-layouts: 2.49 us -> 0.03 us
  waiting for transfers between devices: 18.6 us -> 19.6 us
    ppermute x15 -> x14, starting transfers between devices: 22.6 us -> 18.1 us  [exchanged(): return lax.ppermute(value, axis, [(i, i ^ mask) for i in range(size)])]
    unnamed x10 -> x4, local copies, waits for them, and re-layouts: 2.48 us -> 0.01 us
    pallas_call x0 -> x1, Pallas kernels: none -> 1.21 us  [shards(): pl.pallas_call(prepare_body, out_shape=[bf16(rows + MARK_ROWS, width), bf...]
    ppermute x15 -> x14, waiting for transfers between devices: 18.6 us -> 19.6 us  [exchanged(): return lax.ppermute(value, axis, [(i, i ^ mask) for i in range(size)])]
    pallas_call x9 -> x8, Pallas kernels: 6.61 us -> 5.78 us  [call(): pl.pallas_call(whole, out_shape=out_shape, in_specs=specs, out_specs=jax....]
  transfers between devices with their start and end apart: 15 -> 14, of which waited for: 8 -> 7; matrix products, arithmetic and copies ran while one was open for 0% -> 0% of each run, Pallas kernels for 10% -> 12%
where the time goes in v3:
time: 46.9 us; the launch traced here: 46.7 us
  waiting for transfers between devices  19.6 us (42%)
  starting transfers between devices  18.1 us (39%)
  Pallas kernels  6.99 us (15%)
  between operations  2.05 us (4%)
    ppermute x14, waiting for transfers between devices, exchanged(): return lax.ppermute(value, axis, [(i, i ^ mask) for i in range(size)])  19.6 us
    ppermute x14, starting transfers between devices, exchanged(): return lax.ppermute(value, axis, [(i, i ^ mask) for i in range(size)])  18.1 us
    pallas_call x8, Pallas kernels, call(): pl.pallas_call(whole, out_shape=out_shape, in_specs=specs, out_specs=jax....  5.78 us
    pallas_call x1, Pallas kernels, shards(): pl.pallas_call(prepare_body, out_shape=[bf16(rows + MARK_ROWS, width), bf...  1.21 us
  transfers between devices with their start and end apart: 14, of which 7 were waited for; matrix products, arithmetic and copies ran while one was open for 0% of the time, Pallas kernels for 12%

profile of v3, /device:TPU:0, one launch (start us, length us, event | category | flops | bytes accessed | tf_op | source)
XLA Modules:
  0.0 46.7 jit_solution(8933488295386096327)
XLA Ops:
  0.6 4.1 %collective-permute-start.4 = (bf16[64,768]{1,0:T(8,128)(2,1)}, bf16[64,768]{1,0:T(8,128)(2,1)S(1)}, u32[]{:S(2)}, u32[]{:S(2)}) collective-permute-start(bf16[64,768]{1,0:T(8,128)(2,1)} %refs_3_.1), channel_id=1, source_target_pairs={{0,16},{8,24},{16,0},{24,8},{1,17},{9,25},{17,1},{25,9},{2,18},{10... | collective-permute-start | bytes 294920 | tf_op jit(solution)/shard_map/ppermute | solution.py:16
  4.7 1.2 %unit_rows.1 = (bf16[144,768]{1,0:T(8,128)(2,1)S(1)}, bf16[64,768]{1,0:T(8,128)(2,1)S(1)}) custom-call(bf16[128,768]{1,0:T(8,128)(2,1)} %refs_0_.5, bf16[64,768]{1,0:T(8,128)(2,1)} %refs_3_.1, s32[1,128]{1,0:T(1,128)} %bitcast.1), custom_call_target="tpu_custom_call" | custom-call | tf_op jit(solution)/shard_map/unit_rows/pallas_call | solution.py:190
  6.0 1.6 %collective-permute-start = (bf16[144,768]{1,0:T(8,128)(2,1)S(1)}, bf16[144,768]{1,0:T(8,128)(2,1)S(1)}, u32[]{:S(2)}, u32[]{:S(2)}) collective-permute-start(bf16[144,768]{1,0:T(8,128)(2,1)S(1)} %get-tuple-element.10.refs_0_.refs_2_), channel_id=1, source_target_pairs={{0,2},{1,3},{2,0},{3,1},{4,6},{5,7},{6,4},{7,5},{8,10},{9,11},{10,... | collective-permute-start | bytes 663560 | tf_op jit(solution)/shard_map/ppermute | solution.py:16
  7.5 1.5 %collective-permute-start.1 = (bf16[144,768]{1,0:T(8,128)(2,1)S(1)}, bf16[144,768]{1,0:T(8,128)(2,1)S(1)}, u32[]{:S(2)}, u32[]{:S(2)}) collective-permute-start(bf16[144,768]{1,0:T(8,128)(2,1)S(1)} %get-tuple-element.10.refs_0_.refs_2_), channel_id=1, source_target_pairs={{0,4},{1,5},{2,6},{3,7},{4,0},{5,1},{6,2},{7,3},{8,12},{9,13},{10,... | collective-permute-start | bytes 663560 | tf_op jit(solution)/shard_map/ppermute | solution.py:16
  9.0 0.5 %collective-permute-start.2 = (bf16[144,768]{1,0:T(8,128)(2,1)S(1)}, bf16[144,768]{1,0:T(8,128)(2,1)S(1)}, u32[]{:S(2)}, u32[]{:S(2)}) collective-permute-start(bf16[144,768]{1,0:T(8,128)(2,1)S(1)} %get-tuple-element.10.refs_0_.refs_2_), channel_id=1, source_target_pairs={{0,6},{1,7},{2,4},{3,5},{4,2},{5,3},{6,0},{7,1},{8,14},{9,15},{10,... | collective-permute-start | bytes 663560 | tf_op jit(solution)/shard_map/ppermute | solution.py:16
  9.5 1.6 %collective-permute-start.3 = (bf16[64,768]{1,0:T(8,128)(2,1)S(1)}, bf16[64,768]{1,0:T(8,128)(2,1)S(1)}, u32[]{:S(2)}, u32[]{:S(2)}) collective-permute-start(bf16[64,768]{1,0:T(8,128)(2,1)S(1)} %copy-done.1), channel_id=1, source_target_pairs={{0,8},{8,0},{16,24},{24,16},{1,9},{9,1},{17,25},{25,17},{2,10},{10... | collective-permute-start | bytes 294920 | tf_op jit(solution)/shard_map/ppermute | solution.py:16
  11.1 0.0 collective-permute-done.4.refs_0_
  11.1 0.1 unit_far.1.refs_6_
  11.2 0.5 %collective-permute-start.5 = (bf16[64,768]{1,0:T(8,128)(2,1)S(1)}, bf16[64,768]{1,0:T(8,128)(2,1)S(1)}, u32[]{:S(2)}, u32[]{:S(2)}) collective-permute-start(bf16[64,768]{1,0:T(8,128)(2,1)S(1)} %unit_far.1.refs_6_), channel_id=1, source_target_pairs={{0,8},{8,0},{16,24},{24,16},{1,9},{9,1},{17,25},{25,17},{2,10},{10... | collective-permute-start | bytes 294920 | tf_op jit(solution)/shard_map/ppermute | solution.py:16
  11.7 2.7 %collective-permute-done.3.refs_5_ = bf16[64,768]{1,0:T(8,128)(2,1)S(1)} collective-permute-done((bf16[64,768]{1,0:T(8,128)(2,1)S(1)}, bf16[64,768]{1,0:T(8,128)(2,1)S(1)}, u32[]{:S(2)}, u32[]{:S(2)}) %collective-permute-start.3) | collective-permute-done | bytes 98336 | tf_op jit(solution)/shard_map/ppermute | solution.py:16
  14.4 1.5 %collective-permute-done.5.refs_7_ = bf16[64,768]{1,0:T(8,128)(2,1)S(1)} collective-permute-done((bf16[64,768]{1,0:T(8,128)(2,1)S(1)}, bf16[64,768]{1,0:T(8,128)(2,1)S(1)}, u32[]{:S(2)}, u32[]{:S(2)}) %collective-permute-start.5) | collective-permute-done | bytes 98336 | tf_op jit(solution)/shard_map/ppermute | solution.py:16
  15.9 3.0 %collective-permute-done.1.refs_2_ = bf16[144,768]{1,0:T(8,128)(2,1)S(1)} collective-permute-done((bf16[144,768]{1,0:T(8,128)(2,1)S(1)}, bf16[144,768]{1,0:T(8,128)(2,1)S(1)}, u32[]{:S(2)}, u32[]{:S(2)}) %collective-permute-start.1) | collective-permute-done | bytes 221216 | tf_op jit(solution)/shard_map/ppermute | solution.py:16
  18.9 0.1 join_rows.1
  19.0 0.1 collective-permute-start.9
  19.1 1.3 %collective-permute-start.6 = (bf16[256,768]{1,0:T(8,128)(2,1)S(1)}, bf16[256,768]{1,0:T(8,128)(2,1)S(1)}, u32[]{:S(2)}, u32[]{:S(2)}) collective-permute-start(bf16[256,768]{1,0:T(8,128)(2,1)S(1)} %get-tuple-element.12.refs_2_.refs_3_), channel_id=1, source_target_pairs={{0,2},{1,3},{2,0},{3,1},{4,6},{5,7},{6,4},{7,5},{8,10},{9,11},{10,... | collective-permute-start | bytes 1179656 | tf_op jit(solution)/shard_map/ppermute | solution.py:16
  20.4 0.8 %collective-permute-start.7 = (bf16[256,768]{1,0:T(8,128)(2,1)S(1)}, bf16[256,768]{1,0:T(8,128)(2,1)S(1)}, u32[]{:S(2)}, u32[]{:S(2)}) collective-permute-start(bf16[256,768]{1,0:T(8,128)(2,1)S(1)} %get-tuple-element.12.refs_2_.refs_3_), channel_id=1, source_target_pairs={{0,4},{1,5},{2,6},{3,7},{4,0},{5,1},{6,2},{7,3},{8,12},{9,13},{10,... | collective-permute-start | bytes 1179656 | tf_op jit(solution)/shard_map/ppermute | solution.py:16
  21.2 1.4 %collective-permute-start.8 = (bf16[256,768]{1,0:T(8,128)(2,1)S(1)}, bf16[256,768]{1,0:T(8,128)(2,1)S(1)}, u32[]{:S(2)}, u32[]{:S(2)}) collective-permute-start(bf16[256,768]{1,0:T(8,128)(2,1)S(1)} %get-tuple-element.12.refs_2_.refs_3_), channel_id=1, source_target_pairs={{0,6},{1,7},{2,4},{3,5},{4,2},{5,3},{6,0},{7,1},{8,14},{9,15},{10,... | collective-permute-start | bytes 1179656 | tf_op jit(solution)/shard_map/ppermute | solution.py:16
  23.9 0.8 %text_part.1.refs_4_ = f32[256,768]{1,0:T(8,128)S(1)} custom-call(f32[1]{0:T(128)S(6)} %copy.7.refs_0_, f32[1]{0:T(128)S(6)} %copy.8.refs_1_, bf16[256,768]{1,0:T(8,128)(2,1)S(1)} %get-tuple-element.12.refs_2_.refs_3_, bf16[576,768]{1,0:T(8,128)(2,1)S(1)} %get-tuple-element.13.refs_3_), custom_call_target="tpu_custom_call" | custom-call | flops 402653184 | bytes 2064392 | tf_op jit(solution)/shard_map/text_part/pallas_call | solution.py:35
  24.7 0.0 collective-permute-done.9.refs_3_
  24.7 0.8 %text_part_sum.1 = (f32[64,768]{1,0:T(8,128)S(1)}, f32[64,768]{1,0:T(8,128)S(1)}, f32[64,768]{1,0:T(8,128)S(1)}, f32[64,768]{1,0:T(8,128)S(1)}) custom-call(f32[1]{0:T(128)S(6)} %copy.7.refs_0_, f32[1]{0:T(128)S(6)} %copy.8.refs_1_, bf16[256,768]{1,0:T(8,128)(2,1)S(1)} %get-tuple-element.12.refs_2_.refs_3_, ...), custom_call_target="tpu_custom_call" | custom-call | flops 402653184 | bytes 2850824 | tf_op jit(solution)/shard_map/text_part_sum/pallas_call | solution.py:35
  25.5 1.4 %collective-permute-start.11 = (f32[64,768]{1,0:T(8,128)S(1)}, f32[64,768]{1,0:T(8,128)S(1)}, u32[]{:S(2)}, u32[]{:S(2)}) collective-permute-start(f32[64,768]{1,0:T(8,128)S(1)} %get-tuple-element.15), channel_id=1, source_target_pairs={{0,24},{8,16},{16,8},{24,0},{1,25},{9,17},{17,9},{25,1},{2,26},{10... | collective-permute-start | bytes 589832 | tf_op jit(solution)/shard_map/ppermute | solution.py:16
  26.9 1.7 %collective-permute-start.12 = (f32[64,768]{1,0:T(8,128)S(1)}, f32[64,768]{1,0:T(8,128)S(1)}, u32[]{:S(2)}, u32[]{:S(2)}) collective-permute-start(f32[64,768]{1,0:T(8,128)S(1)} %get-tuple-element.16), channel_id=1, source_target_pairs={{0,16},{8,24},{16,0},{24,8},{1,17},{9,25},{17,1},{25,9},{2,18},{10... | collective-permute-start | bytes 589832 | tf_op jit(solution)/shard_map/ppermute | solution.py:16
  28.6 2.5 %collective-permute-done.6.refs_4_ = bf16[256,768]{1,0:T(8,128)(2,1)S(1)} collective-permute-done((bf16[256,768]{1,0:T(8,128)(2,1)S(1)}, bf16[256,768]{1,0:T(8,128)(2,1)S(1)}, u32[]{:S(2)}, u32[]{:S(2)}) %collective-permute-start.6) | collective-permute-done | bytes 393248 | tf_op jit(solution)/shard_map/ppermute | solution.py:16
  31.0 1.6 %collective-permute-start.13 = (f32[64,768]{1,0:T(8,128)S(1)}, f32[64,768]{1,0:T(8,128)S(1)}, u32[]{:S(2)}, u32[]{:S(2)}) collective-permute-start(f32[64,768]{1,0:T(8,128)S(1)} %get-tuple-element.17), channel_id=1, source_target_pairs={{0,8},{8,0},{16,24},{24,16},{1,9},{9,1},{17,25},{25,17},{2,10},{10... | collective-permute-start | bytes 589832 | tf_op jit(solution)/shard_map/ppermute | solution.py:16
  32.6 5.7 %collective-permute-done.7.refs_5_ = bf16[256,768]{1,0:T(8,128)(2,1)S(1)} collective-permute-done((bf16[256,768]{1,0:T(8,128)(2,1)S(1)}, bf16[256,768]{1,0:T(8,128)(2,1)S(1)}, u32[]{:S(2)}, u32[]{:S(2)}) %collective-permute-start.7) | collective-permute-done | bytes 393248 | tf_op jit(solution)/shard_map/ppermute | solution.py:16
  38.3 1.6 %collective-permute-done.8.refs_6_ = bf16[256,768]{1,0:T(8,128)(2,1)S(1)} collective-permute-done((bf16[256,768]{1,0:T(8,128)(2,1)S(1)}, bf16[256,768]{1,0:T(8,128)(2,1)S(1)}, u32[]{:S(2)}, u32[]{:S(2)}) %collective-permute-start.8) | collective-permute-done | bytes 393248 | tf_op jit(solution)/shard_map/ppermute | solution.py:16
  40.0 1.5 %speech_part.2.refs_7_ = f32[128,768]{1,0:T(8,128)S(1)} custom-call(f32[1]{0:T(128)S(6)} %copy.7.refs_0_, f32[1]{0:T(128)S(6)} %copy.8.refs_1_, bf16[144,768]{1,0:T(8,128)(2,1)S(1)} %slice.4.refs_2_, bf16[256,768]{1,0:T(8,128)(2,1)S(1)} %get-tuple-element.12.refs_2_.refs_3_, bf16[256,768]{1,0:T(8,128)(2,1)S(1)} %collective-permute-done.6.refs_4_, ...), custom_call_target="tpu_custom_call" | custom-call | flops 402653184 | bytes 2187272 | tf_op jit(solution)/shard_map/speech_part/pallas_call | solution.py:35
  41.4 0.1 collective-permute-start.10
  41.5 1.5 %speech_part.3.refs_1_ = f32[128,768]{1,0:T(8,128)S(1)} custom-call(f32[1]{0:T(128)S(6)} %copy.7.refs_0_, f32[1]{0:T(128)S(6)} %copy.8.refs_1_, bf16[144,768]{1,0:T(8,128)(2,1)S(1)} %get-tuple-element.10.refs_0_.refs_2_, bf16[256,768]{1,0:T(8,128)(2,1)S(1)} %get-tuple-element.12.refs_2_.refs_3_, bf16[256,768]{1,0:T(8,128)(2,1)S(1)} %collective-permute-done.6.refs_4_, ...), custom_call_target="tpu_custom_call" | custom-call | flops 402653184 | bytes 2187272 | tf_op jit(solution)/shard_map/speech_part/pallas_call | solution.py:35
  43.0 0.0 copy-start
  43.0 2.6 %collective-permute-done.12.refs_2_ = f32[64,768]{1,0:T(8,128)S(1)} collective-permute-done((f32[64,768]{1,0:T(8,128)S(1)}, f32[64,768]{1,0:T(8,128)S(1)}, u32[]{:S(2)}, u32[]{:S(2)}) %collective-permute-start.12) | collective-permute-done | bytes 196640 | tf_op jit(solution)/shard_map/ppermute | solution.py:16
  45.7 1.1 %finish.1 = (f32[128,768]{1,0:T(8,128)}, f32[64,768]{1,0:T(8,128)}) custom-call(bf16[128,768]{1,0:T(8,128)(2,1)S(1)} %copy-done, f32[128,768]{1,0:T(8,128)S(1)} %speech_part.3.refs_1_, f32[128,768]{1,0:T(8,128)S(1)} %collective-permute-done.10.refs_2_, bf16[64,768]{1,0:T(8,128)(2,1)S(1)} %copy-done.1, f32[64,768]{1,0:T(8,128)S(1)} %text_sum.1.refs_4_), custom_call_target="tpu_custom_call" | custom-call | bytes 1867776 | tf_op jit(solution)/shard_map/finish/pallas_call | solution.py:35
  (10 shorter events, 0.1 us)
Async XLA Ops:
  0.6 10.5 %collective-permute-start.4 = (bf16[64,768]{1,0:T(8,128)(2,1)}, bf16[64,768]{1,0:T(8,128)(2,1)S(1)}, u32[]{:S(2)}, u32[]{:S(2)}) collective-permute-start(bf16[64,768]{1,0:T(8,128)(2,1)} %refs_3_.1), channel_id=1, source_target_pairs={{0,16},{8,24},{16,0},{24,8},{1,17},{9,25},{17,1},{25,9},{2,18},{10... | collective-permute-start | bytes 294920 | tf_op jit(solution)/shard_map/ppermute | solution.py:16
  4.7 4.8 %copy-start.1 = (bf16[64,768]{1,0:T(8,128)(2,1)S(1)}, bf16[64,768]{1,0:T(8,128)(2,1)}, u32[]{:S(2)}) copy-start(bf16[64,768]{1,0:T(8,128)(2,1)} %refs_3_.1) | copy-start | bytes 294916
  6.0 9.9 %collective-permute-start = (bf16[144,768]{1,0:T(8,128)(2,1)S(1)}, bf16[144,768]{1,0:T(8,128)(2,1)S(1)}, u32[]{:S(2)}, u32[]{:S(2)}) collective-permute-start(bf16[144,768]{1,0:T(8,128)(2,1)S(1)} %get-tuple-element.10.refs_0_.refs_2_), channel_id=1, source_target_pairs={{0,2},{1,3},{2,0},{3,1},{4,6},{5,7},{6,4},{7,5},{8,10},{9,11},{10,... | collective-permute-start | bytes 663560 | tf_op jit(solution)/shard_map/ppermute | solution.py:16
  7.5 11.3 %collective-permute-start.1 = (bf16[144,768]{1,0:T(8,128)(2,1)S(1)}, bf16[144,768]{1,0:T(8,128)(2,1)S(1)}, u32[]{:S(2)}, u32[]{:S(2)}) collective-permute-start(bf16[144,768]{1,0:T(8,128)(2,1)S(1)} %get-tuple-element.10.refs_0_.refs_2_), channel_id=1, source_target_pairs={{0,4},{1,5},{2,6},{3,7},{4,0},{5,1},{6,2},{7,3},{8,12},{9,13},{10,... | collective-permute-start | bytes 663560 | tf_op jit(solution)/shard_map/ppermute | solution.py:16
  9.0 9.8 %collective-permute-start.2 = (bf16[144,768]{1,0:T(8,128)(2,1)S(1)}, bf16[144,768]{1,0:T(8,128)(2,1)S(1)}, u32[]{:S(2)}, u32[]{:S(2)}) collective-permute-start(bf16[144,768]{1,0:T(8,128)(2,1)S(1)} %get-tuple-element.10.refs_0_.refs_2_), channel_id=1, source_target_pairs={{0,6},{1,7},{2,4},{3,5},{4,2},{5,3},{6,0},{7,1},{8,14},{9,15},{10,... | collective-permute-start | bytes 663560 | tf_op jit(solution)/shard_map/ppermute | solution.py:16
  9.5 4.9 %collective-permute-start.3 = (bf16[64,768]{1,0:T(8,128)(2,1)S(1)}, bf16[64,768]{1,0:T(8,128)(2,1)S(1)}, u32[]{:S(2)}, u32[]{:S(2)}) collective-permute-start(bf16[64,768]{1,0:T(8,128)(2,1)S(1)} %copy-done.1), channel_id=1, source_target_pairs={{0,8},{8,0},{16,24},{24,16},{1,9},{9,1},{17,25},{25,17},{2,10},{10... | collective-permute-start | bytes 294920 | tf_op jit(solution)/shard_map/ppermute | solution.py:16
  11.2 4.7 %collective-permute-start.5 = (bf16[64,768]{1,0:T(8,128)(2,1)S(1)}, bf16[64,768]{1,0:T(8,128)(2,1)S(1)}, u32[]{:S(2)}, u32[]{:S(2)}) collective-permute-start(bf16[64,768]{1,0:T(8,128)(2,1)S(1)} %unit_far.1.refs_6_), channel_id=1, source_target_pairs={{0,8},{8,0},{16,24},{24,16},{1,9},{9,1},{17,25},{25,17},{2,10},{10... | collective-permute-start | bytes 294920 | tf_op jit(solution)/shard_map/ppermute | solution.py:16
  19.0 5.7 %collective-permute-start.9 = (bf16[576,768]{1,0:T(8,128)(2,1)S(1)}, bf16[576,768]{1,0:T(8,128)(2,1)S(1)}, u32[]{:S(2)}, u32[]{:S(2)}) collective-permute-start(bf16[576,768]{1,0:T(8,128)(2,1)S(1)} %get-tuple-element.13.refs_3_), channel_id=1, source_target_pairs={{0,1},{1,0},{2,3},{3,2},{4,5},{5,4},{6,7},{7,6},{8,9},{9,8},{10,11... | collective-permute-start | bytes 2654216 | tf_op jit(solution)/shard_map/ppermute | solution.py:16
  19.1 12.0 %collective-permute-start.6 = (bf16[256,768]{1,0:T(8,128)(2,1)S(1)}, bf16[256,768]{1,0:T(8,128)(2,1)S(1)}, u32[]{:S(2)}, u32[]{:S(2)}) collective-permute-start(bf16[256,768]{1,0:T(8,128)(2,1)S(1)} %get-tuple-element.12.refs_2_.refs_3_), channel_id=1, source_target_pairs={{0,2},{1,3},{2,0},{3,1},{4,6},{5,7},{6,4},{7,5},{8,10},{9,11},{10,... | collective-permute-start | bytes 1179656 | tf_op jit(solution)/shard_map/ppermute | solution.py:16
  20.4 18.0 %collective-permute-start.7 = (bf16[256,768]{1,0:T(8,128)(2,1)S(1)}, bf16[256,768]{1,0:T(8,128)(2,1)S(1)}, u32[]{:S(2)}, u32[]{:S(2)}) collective-permute-start(bf16[256,768]{1,0:T(8,128)(2,1)S(1)} %get-tuple-element.12.refs_2_.refs_3_), channel_id=1, source_target_pairs={{0,4},{1,5},{2,6},{3,7},{4,0},{5,1},{6,2},{7,3},{8,12},{9,13},{10,... | collective-permute-start | bytes 1179656 | tf_op jit(solution)/shard_map/ppermute | solution.py:16
  21.2 18.8 %collective-permute-start.8 = (bf16[256,768]{1,0:T(8,128)(2,1)S(1)}, bf16[256,768]{1,0:T(8,128)(2,1)S(1)}, u32[]{:S(2)}, u32[]{:S(2)}) collective-permute-start(bf16[256,768]{1,0:T(8,128)(2,1)S(1)} %get-tuple-element.12.refs_2_.refs_3_), channel_id=1, source_target_pairs={{0,6},{1,7},{2,4},{3,5},{4,2},{5,3},{6,0},{7,1},{8,14},{9,15},{10,... | collective-permute-start | bytes 1179656 | tf_op jit(solution)/shard_map/ppermute | solution.py:16
  25.5 17.5 %collective-permute-start.11 = (f32[64,768]{1,0:T(8,128)S(1)}, f32[64,768]{1,0:T(8,128)S(1)}, u32[]{:S(2)}, u32[]{:S(2)}) collective-permute-start(f32[64,768]{1,0:T(8,128)S(1)} %get-tuple-element.15), channel_id=1, source_target_pairs={{0,24},{8,16},{16,8},{24,0},{1,25},{9,17},{17,9},{25,1},{2,26},{10... | collective-permute-start | bytes 589832 | tf_op jit(solution)/shard_map/ppermute | solution.py:16
  26.9 18.7 %collective-permute-start.12 = (f32[64,768]{1,0:T(8,128)S(1)}, f32[64,768]{1,0:T(8,128)S(1)}, u32[]{:S(2)}, u32[]{:S(2)}) collective-permute-start(f32[64,768]{1,0:T(8,128)S(1)} %get-tuple-element.16), channel_id=1, source_target_pairs={{0,16},{8,24},{16,0},{24,8},{1,17},{9,25},{17,1},{25,9},{2,18},{10... | collective-permute-start | bytes 589832 | tf_op jit(solution)/shard_map/ppermute | solution.py:16
  31.0 14.6 %collective-permute-start.13 = (f32[64,768]{1,0:T(8,128)S(1)}, f32[64,768]{1,0:T(8,128)S(1)}, u32[]{:S(2)}, u32[]{:S(2)}) collective-permute-start(f32[64,768]{1,0:T(8,128)S(1)} %get-tuple-element.17), channel_id=1, source_target_pairs={{0,8},{8,0},{16,24},{24,16},{1,9},{9,1},{17,25},{25,17},{2,10},{10... | collective-permute-start | bytes 589832 | tf_op jit(solution)/shard_map/ppermute | solution.py:16
  41.4 4.2 %collective-permute-start.10 = (f32[128,768]{1,0:T(8,128)S(1)}, f32[128,768]{1,0:T(8,128)S(1)}, u32[]{:S(2)}, u32[]{:S(2)}) collective-permute-start(f32[128,768]{1,0:T(8,128)S(1)} %speech_part.2.refs_7_), channel_id=1, source_target_pairs={{0,1},{1,0},{2,3},{3,2},{4,5},{5,4},{6,7},{7,6},{8,9},{9,8},{10,11... | collective-permute-start | bytes 1179656 | tf_op jit(solution)/shard_map/ppermute | solution.py:16
  43.0 2.7 %copy-start = (bf16[128,768]{1,0:T(8,128)(2,1)S(1)}, bf16[128,768]{1,0:T(8,128)(2,1)}, u32[]{:S(2)}) copy-start(bf16[128,768]{1,0:T(8,128)(2,1)} %refs_0_.5) | copy-start | bytes 589828

commit v4 on v3

--- a/solution.py
+++ b/solution.py
@@ -9,6 +9,7 @@
 MARK_ROWS = 16
 RADIX = 256
 CHUNK = 512
+EARLY = 1 << 33
 
 
 def exchanged(value, axis, mask):
@@ -75,19 +76,27 @@
     out[...] = direction(values[...])[0].astype(jnp.bfloat16)
 
 
-def join_body(chips, raw, *refs):
-    speech, text = refs[-2:]
-    rows = refs[0].shape[0]
-    for k in range(chips):
-        speech[k * rows : (k + 1) * rows, :] = refs[k][...]
-    rows = refs[chips].shape[0]
-    for k, is_raw in enumerate(raw):
-        block = refs[chips + k]
-        target = text.at[k * rows : (k + 1) * rows, :]
+def join_body(raw, *refs):
+    out = refs[-1]
+    at = 0
+    for ref, is_raw in zip(refs[:-1], raw):
+        target = out.at[at : at + ref.shape[0], :]
+        at += ref.shape[0]
         if is_raw:
-            unit_body(block, target)
+            unit_body(ref, target)
         else:
-            target[...] = block[...]
+            target[...] = ref[...]
+
+
+def halves_body(upper, lower, upper_out, lower_out):
+    upper_out[...] = upper[: upper_out.shape[0], :]
+    lower_out[...] = lower[upper_out.shape[0] :, :]
+
+
+def joined(blocks, raw=None, after=(), name="join"):
+    shape = (sum(v.shape[0] for v in blocks), blocks[0].shape[1])
+    body = functools.partial(join_body, raw or [False] * len(blocks))
+    return call(body, jax.ShapeDtypeStruct(shape, jnp.bfloat16), blocks, after, name=name)
 
 
 def marks_of(block, rows):
@@ -105,51 +114,57 @@
     return lax.dot_general(left, right, (((1,), (1,)), ((), ())), preferred_element_type=jnp.float32)
 
 
-def text_part_body(rows, own_text, *refs):
-    sharp, shift = refs[0][0], refs[1][0]
-    text, speech = refs[2][...], refs[3]
-    start = refs[4] if len(refs) > 5 and refs[4].shape == text.shape else None
-    outs = refs[4:] if start is None else refs[5:]
+def text_part_body(rows, own_text, has_start, speeches, *refs):
+    sharp, shift, text = refs[0][0], refs[1][0], refs[2][...]
+    total = refs[3][...] if has_start else None
+    at = 4 if has_start else 3
+    blocks = refs[at : at + speeches]
+    outs = refs[at + speeches :]
     groups = lax.axis_size("group")
     members = lax.axis_size("member")
     group = lax.axis_index("group")
     member = lax.axis_index("member")
     stride = rows + MARK_ROWS
-    count = speech.shape[0] // stride
-    step = max(1, min(count, CHUNK // rows))
-    iota = lax.broadcasted_iota(jnp.int32, (own_text, step * rows), 0)
-    ids = [((group ^ k) * members + member) * own_text + iota for k in range(groups)]
-    ids = jnp.concatenate(ids, axis=0).astype(jnp.float32)
-    total = None if start is None else start[...]
-    for first in range(0, count, step):
-        blocks = range(first, first + step)
-        chunk = jnp.concatenate([speech[k * stride : k * stride + rows, :] for k in blocks], axis=0)
-        marks = [marks_of(speech.at[k * stride : (k + 1) * stride, :], rows) for k in blocks]
-        match = ids == jnp.concatenate(marks, axis=1)
-        coef = coefficients(dot_rows(text, chunk), match, sharp, shift)
-        part = jnp.dot(coef, chunk, preferred_element_type=jnp.float32)
-        total = part if total is None else total + part
+    for speech in blocks:
+        count = speech.shape[0] // stride
+        for first in range(0, count, CHUNK // rows):
+            some = range(first, min(count, first + CHUNK // rows))
+            chunk = [speech[k * stride : k * stride + rows, :] for k in some]
+            marks = [marks_of(speech.at[k * stride : (k + 1) * stride, :], rows) for k in some]
+            chunk = jnp.concatenate(chunk, axis=0)
+            marks = jnp.concatenate(marks, axis=1)
+            iota = lax.broadcasted_iota(jnp.int32, (own_text, marks.shape[1]), 0)
+            ids = [((group ^ k) * members + member) * own_text + iota for k in range(groups)]
+            match = jnp.concatenate(ids, axis=0).astype(jnp.float32) == marks
+            coef = coefficients(dot_rows(text, chunk), match, sharp, shift)
+            part = jnp.dot(coef, chunk, preferred_element_type=jnp.float32)
+            total = part if total is None else total + part
     size = outs[0].shape[0]
     for k, out in enumerate(outs):
         out[...] = total[k * size : (k + 1) * size, :]
 
 
-def speech_part_body(rows, own_text, *refs):
-    sharp, shift = refs[0][0], refs[1][0]
-    speech, texts, out = refs[2], refs[3:-1], refs[-1]
+def speech_part_body(rows, own_text, has_start, masks, *refs):
+    sharp, shift, speech = refs[0][0], refs[1][0], refs[2]
+    total = refs[3][...] if has_start else None
+    texts, out = list(refs[4 if has_start else 3 : -1]), refs[-1]
     groups = lax.axis_size("group")
     members = lax.axis_size("member")
     group = lax.axis_index("group")
     member = lax.axis_index("member")
     marks = jnp.broadcast_to(marks_of(speech, rows), (rows, rows)).T[:, 0:1]
     block = speech[0:rows, :]
-    lane = lax.broadcasted_iota(jnp.int32, (1, groups * own_text), 1)
+    column = groups * own_text
+    lane = lax.broadcasted_iota(jnp.int32, (1, column), 1)
     base = (group ^ (lane // own_text)) * members * own_text + lane % own_text
-    total = None
-    for j, text in enumerate(texts):
-        ids = (base + (member ^ (2 * j)) * own_text).astype(jnp.float32)
-        coef = coefficients(dot_rows(block, text[...]), marks == ids, sharp, shift)
-        part = jnp.dot(coef, text[...], preferred_element_type=jnp.float32)
+    for mask in masks:
+        pieces = [texts.pop(0)[...]]
+        while sum(v.shape[0] for v in pieces) < column:
+            pieces.append(texts.pop(0)[...])
+        text = jnp.concatenate(pieces, axis=0)
+        ids = (base + (member ^ (2 * mask)) * own_text).astype(jnp.float32)
+        coef = coefficients(dot_rows(block, text), marks == ids, sharp, shift)
+        part = jnp.dot(coef, text, preferred_element_type=jnp.float32)
         total = part if total is None else total + part
     out[...] = total
 
@@ -208,66 +223,67 @@
             came = exchanged(text_blocks[j] if j else sentence_vectors, "group", k)
             raw[j + k] = not j
             if not j and k > 1:
-                came = call(unit_body, bf16(own_text, width), [came], (), 1 << 33, name="unit_far")
+                came = call(unit_body, bf16(own_text, width), [came], (), EARLY, name="unit_far")
                 raw[j + k] = False
             text_blocks[j + k] = came
-    speech_blocks = [speech_own]
-    for k in range(1, chips):
-        speech_blocks.append(exchanged(speech_own, "member", 2 * k))
+    square = chips == 4
+    masks = [1, 2] if square else list(range(1, chips))
+
+    def far_halves(near, middle, after=()):
+        sizes = [middle, near[0].shape[0] - middle]
+        halves = call(
+            halves_body, [bf16(size, width) for size in sizes], near[::-1], after, name="halves"
+        )
+        return [exchanged(half, "member", 2 * k) for half, k in zip(halves, masks)]
+
+    speech_near = [exchanged(speech_own, "member", 2 * k) for k in masks]
+    speech = [joined([speech_own, *speech_near], name="join_speech")]
+    other = [exchanged(speech[0], "member", 1)]
+    if square:
+        speech.append(joined(far_halves(speech_near, rows // 2), name="join_far"))
+        other.append(exchanged(speech[1], "member", 1))
+    text = joined(text_blocks, raw, (speech[-1],), name="join_text")
+    text_near = [exchanged(text, "member", 2 * k) for k in masks]
+
     column = groups * own_text
-    speech, text = call(
-        functools.partial(join_body, chips, raw),
-        [bf16(chips * (rows + MARK_ROWS), width), bf16(column, width)],
-        speech_blocks + text_blocks,
-        name="join_rows",
-    )
-    other = exchanged(speech, "member", 1)
-    texts = [text]
-    for k in range(1, chips):
-        texts.append(exchanged(text, "member", 2 * k))
-
-    text_part = functools.partial(text_part_body, rows, own_text)
-    work = 4 * column * chips * rows * width
     temporary = 4 * column * (6 * CHUNK + 3 * width)
-    half = call(
-        text_part, [f32(column, width)], scalars + [text, speech], (), work, temporary, "text_part"
-    )
-    parts = call(
-        text_part,
-        [f32(own_text, width)] * groups,
-        scalars + [text, other, half[0]],
-        (),
-        work,
-        temporary,
-        "text_part_sum",
-    )
+
+    def text_part(outs, blocks, start):
+        count = sum(v.shape[0] for v in blocks) // (rows + MARK_ROWS)
+        body = functools.partial(text_part_body, rows, own_text, bool(start), len(blocks))
+        operands = [*scalars, text, *start, *blocks]
+        work = 4 * column * count * rows * width
+        return call(body, outs, operands, (), work, temporary, "text_part")
+
+    half = text_part([f32(column, width)], [*speech, *other[:-1]], [])
+    parts = list(text_part([f32(own_text, width)] * groups, other[-1:], half))
+
     text_back = [parts[0]]
-    for k in reversed(range(1, groups)):
-        text_back.append(exchanged(parts[k], "group", k))
-
-    speech_part = functools.partial(speech_part_body, rows, own_text)
-    work = 4 * rows * chips * column * width
-    stride = rows + MARK_ROWS
-    away = call(
-        speech_part,
-        f32(rows, width),
-        scalars + [other[0:stride]] + texts,
-        (parts[0],),
-        work,
-        temporary,
-        "speech_part",
-    )
+    for bit in [1 << i for i in range(groups.bit_length() - 1)]:
+        for k in reversed(range(bit, groups, 2 * bit)):
+            came = exchanged(parts[k], "group", bit)
+            if k == bit:
+                text_back.append(came)
+            else:
+                parts[k - bit] = call(
+                    sum_body, f32(own_text, width), [parts[k - bit], came], name="sum_near"
+                )
+
+    def speech_part(block, start, columns, texts, after=()):
+        body = functools.partial(speech_part_body, rows, own_text, bool(start), columns)
+        operands = [*scalars, block, *start, *texts]
+        work = 40 * rows * column * len(columns) * width
+        return call(body, f32(rows, width), operands, after, work, temporary, "speech_part")
+
+    near = [[0, *masks], [text, *text_near], (parts[groups // 2],)]
+    away = speech_part(other[0][0 : rows + MARK_ROWS], [], *near)
+    home = speech_part(speech_own, [], *near)
+    if square:
+        text_far = far_halves(text_near, column // 2, (parts[groups // 2],))
+        away = speech_part(other[0][0 : rows + MARK_ROWS], [away], [3], text_far)
+        home = speech_part(speech_own, [home], [3], text_far)
     back = exchanged(away, "member", 1)
-    home = call(
-        speech_part,
-        f32(rows, width),
-        scalars + [speech_own] + texts,
-        (away,),
-        work,
-        temporary,
-        "speech_part",
-    )
-    text_back = call(sum_body, f32(own_text, width), text_back, (), 1 << 33, name="text_sum")
+    text_back = call(sum_body, f32(own_text, width), text_back, (), EARLY, name="text_sum")
     speech_grad, text_grad = call(
         finish_body,
         [f32(rows, width), f32(own_text, width)],

time: 46.9 us -> 46.8 us (level)
  waiting for transfers between devices: 19.6 us -> 14.8 us
  starting transfers between devices: 18.1 us -> 21.5 us
  Pallas kernels: 6.99 us -> 8.25 us
    ppermute x14 -> x17, waiting for transfers between devices: 19.6 us -> 14.8 us  [exchanged(): return lax.ppermute(value, axis, [(i, i ^ mask) for i in range(size)])]
    ppermute x14 -> x17, starting transfers between devices: 18.1 us -> 21.5 us  [exchanged(): return lax.ppermute(value, axis, [(i, i ^ mask) for i in range(size)])]
    pallas_call x8 -> x15, Pallas kernels: 5.78 us -> 7.04 us  [call(): pl.pallas_call(whole, out_shape=out_shape, in_specs=specs, out_specs=jax....]
  transfers between devices with their start and end apart: 14 -> 17, of which waited for: 7 -> 7; matrix products, arithmetic and copies ran while one was open for 0% -> 0% of each run, Pallas kernels for 12% -> 13%
where the time goes in v4:
time: 46.8 us; the launch traced here: 46.7 us
  starting transfers between devices  21.5 us (46%)
  waiting for transfers between devices  14.8 us (32%)
  Pallas kernels  8.25 us (18%)
  between operations  2.11 us (5%)
    ppermute x17, starting transfers between devices, exchanged(): return lax.ppermute(value, axis, [(i, i ^ mask) for i in range(size)])  21.5 us
    ppermute x17, waiting for transfers between devices, exchanged(): return lax.ppermute(value, axis, [(i, i ^ mask) for i in range(size)])  14.8 us
    pallas_call x15, Pallas kernels, call(): pl.pallas_call(whole, out_shape=out_shape, in_specs=specs, out_specs=jax....  7.04 us
    pallas_call x1, Pallas kernels, shards(): pl.pallas_call(prepare_body, out_shape=[bf16(rows + MARK_ROWS, width), bf...  1.21 us
  transfers between devices with their start and end apart: 17, of which 7 were waited for; matrix products, arithmetic and copies ran while one was open for 0% of the time, Pallas kernels for 13%

profile of v4, /device:TPU:0, one launch (start us, length us, event | category | flops | bytes accessed | tf_op | source)
XLA Modules:
  0.0 46.7 jit_solution(17535269468248681439)
XLA Ops:
  0.6 1.2 %unit_rows.1 = (bf16[144,768]{1,0:T(8,128)(2,1)S(1)}, bf16[64,768]{1,0:T(8,128)(2,1)S(1)}) custom-call(bf16[128,768]{1,0:T(8,128)(2,1)} %refs_0_.7, bf16[64,768]{1,0:T(8,128)(2,1)} %refs_3_.1, s32[1,128]{1,0:T(1,128)} %bitcast.1), custom_call_target="tpu_custom_call" | custom-call | tf_op jit(solution)/shard_map/unit_rows/pallas_call | solution.py:205
  1.9 3.0 %collective-permute-start.3 = (bf16[144,768]{1,0:T(8,128)(2,1)S(1)}, bf16[144,768]{1,0:T(8,128)(2,1)S(1)}, u32[]{:S(2)}, u32[]{:S(2)}) collective-permute-start(bf16[144,768]{1,0:T(8,128)(2,1)S(1)} %get-tuple-element.12.refs_0_.refs_2_), channel_id=1, source_target_pairs={{0,4},{1,5},{2,6},{3,7},{4,0},{5,1},{6,2},{7,3},{8,12},{9,13},{10,... | collective-permute-start | bytes 663560 | tf_op jit(solution)/shard_map/ppermute | solution.py:17
  4.9 1.5 %collective-permute-start.4 = (bf16[144,768]{1,0:T(8,128)(2,1)S(1)}, bf16[144,768]{1,0:T(8,128)(2,1)S(1)}, u32[]{:S(2)}, u32[]{:S(2)}) collective-permute-start(bf16[144,768]{1,0:T(8,128)(2,1)S(1)} %get-tuple-element.12.refs_0_.refs_2_), channel_id=1, source_target_pairs={{0,2},{1,3},{2,0},{3,1},{4,6},{5,7},{6,4},{7,5},{8,10},{9,11},{10,... | collective-permute-start | bytes 663560 | tf_op jit(solution)/shard_map/ppermute | solution.py:17
  6.4 2.6 %collective-permute-start.1 = (bf16[64,768]{1,0:T(8,128)(2,1)S(1)}, bf16[64,768]{1,0:T(8,128)(2,1)S(1)}, u32[]{:S(2)}, u32[]{:S(2)}) collective-permute-start(bf16[64,768]{1,0:T(8,128)(2,1)S(1)} %copy-done.1), channel_id=1, source_target_pairs={{0,16},{8,24},{16,0},{24,8},{1,17},{9,25},{17,1},{25,9},{2,18},{10... | collective-permute-start | bytes 294920 | tf_op jit(solution)/shard_map/ppermute | solution.py:17
  9.0 1.6 %collective-permute-start = (bf16[64,768]{1,0:T(8,128)(2,1)S(1)}, bf16[64,768]{1,0:T(8,128)(2,1)S(1)}, u32[]{:S(2)}, u32[]{:S(2)}) collective-permute-start(bf16[64,768]{1,0:T(8,128)(2,1)S(1)} %copy-done.1), channel_id=1, source_target_pairs={{0,8},{8,0},{16,24},{24,16},{1,9},{9,1},{17,25},{25,17},{2,10},{10... | collective-permute-start | bytes 294920 | tf_op jit(solution)/shard_map/ppermute | solution.py:17
  10.6 1.2 %collective-permute-done.4.refs_1_ = bf16[144,768]{1,0:T(8,128)(2,1)S(1)} collective-permute-done((bf16[144,768]{1,0:T(8,128)(2,1)S(1)}, bf16[144,768]{1,0:T(8,128)(2,1)S(1)}, u32[]{:S(2)}, u32[]{:S(2)}) %collective-permute-start.4) | collective-permute-done | bytes 221216 | tf_op jit(solution)/shard_map/ppermute | solution.py:17
  11.8 0.4 collective-permute-start.6
  12.2 1.6 %collective-permute-start.5 = (bf16[64,768]{1,0:T(8,128)(2,1)S(1)}, bf16[64,768]{1,0:T(8,128)(2,1)S(1)}, u32[]{:S(2)}, u32[]{:S(2)}) collective-permute-start(bf16[64,768]{1,0:T(8,128)(2,1)S(1)} %get-tuple-element.14), channel_id=1, source_target_pairs={{0,2},{1,3},{2,0},{3,1},{4,6},{5,7},{6,4},{7,5},{8,10},{9,11},{10,... | collective-permute-start | bytes 294920 | tf_op jit(solution)/shard_map/ppermute | solution.py:17
  13.9 0.1 collective-permute-start.9
  14.0 0.1 unit_far.1.refs_2_
  14.1 1.6 %collective-permute-start.2 = (bf16[64,768]{1,0:T(8,128)(2,1)S(1)}, bf16[64,768]{1,0:T(8,128)(2,1)S(1)}, u32[]{:S(2)}, u32[]{:S(2)}) collective-permute-start(bf16[64,768]{1,0:T(8,128)(2,1)S(1)} %unit_far.1.refs_2_), channel_id=1, source_target_pairs={{0,8},{8,0},{16,24},{24,16},{1,9},{9,1},{17,25},{25,17},{2,10},{10... | collective-permute-start | bytes 294920 | tf_op jit(solution)/shard_map/ppermute | solution.py:17
  15.8 1.1 %collective-permute-done.5.refs_0_ = bf16[64,768]{1,0:T(8,128)(2,1)S(1)} collective-permute-done((bf16[64,768]{1,0:T(8,128)(2,1)S(1)}, bf16[64,768]{1,0:T(8,128)(2,1)S(1)}, u32[]{:S(2)}, u32[]{:S(2)}) %collective-permute-start.5) | collective-permute-done | bytes 98336 | tf_op jit(solution)/shard_map/ppermute | solution.py:17
  17.0 2.4 %collective-permute-done.2.refs_3_ = bf16[64,768]{1,0:T(8,128)(2,1)S(1)} collective-permute-done((bf16[64,768]{1,0:T(8,128)(2,1)S(1)}, bf16[64,768]{1,0:T(8,128)(2,1)S(1)}, u32[]{:S(2)}, u32[]{:S(2)}) %collective-permute-start.2) | collective-permute-done | bytes 98336 | tf_op jit(solution)/shard_map/ppermute | solution.py:17
  19.4 0.1 join_text.1.refs_2_.refs_3_
  19.5 0.5 collective-permute-start.7
  20.0 1.7 %collective-permute-start.8 = (bf16[256,768]{1,0:T(8,128)(2,1)S(1)}, bf16[256,768]{1,0:T(8,128)(2,1)S(1)}, u32[]{:S(2)}, u32[]{:S(2)}) collective-permute-start(bf16[256,768]{1,0:T(8,128)(2,1)S(1)} %join_text.1.refs_2_.refs_3_), channel_id=1, source_target_pairs={{0,4},{1,5},{2,6},{3,7},{4,0},{5,1},{6,2},{7,3},{8,12},{9,13},{10,... | collective-permute-start | bytes 1179656 | tf_op jit(solution)/shard_map/ppermute | solution.py:17
  22.9 1.9 %text_part.2.refs_3_ = f32[256,768]{1,0:T(8,128)S(1)} custom-call(f32[1]{0:T(128)S(6)} %copy.7.refs_0_, f32[1]{0:T(128)S(6)} %copy.8.refs_1_, bf16[256,768]{1,0:T(8,128)(2,1)S(1)} %join_text.1.refs_2_.refs_3_, bf16[432,768]{1,0:T(8,128)(2,1)S(1)} %join_speech.1.refs_3_, bf16[144,768]{1,0:T(8,128)(2,1)S(1)} %join_far.1.refs_4_, ...), custom_call_target="tpu_custom_call" | custom-call | flops 704643072 | bytes 2727944 | tf_op jit(solution)/shard_map/text_part/pallas_call | solution.py:36
  24.8 0.6 %text_part.3 = (f32[64,768]{1,0:T(8,128)S(1)}, f32[64,768]{1,0:T(8,128)S(1)}, f32[64,768]{1,0:T(8,128)S(1)}, f32[64,768]{1,0:T(8,128)S(1)}) custom-call(f32[1]{0:T(128)S(6)} %copy.7.refs_0_, f32[1]{0:T(128)S(6)} %copy.8.refs_1_, bf16[256,768]{1,0:T(8,128)(2,1)S(1)} %join_text.1.refs_2_.refs_3_, f32[256,768]{1,0:T(8,128)S(1)} %text_part.2.refs_3_, ...), custom_call_target="tpu_custom_call" | custom-call | flops 100663296 | bytes 2187272 | tf_op jit(solution)/shard_map/text_part/pallas_call | solution.py:36
  25.5 1.6 %collective-permute-start.11 = (f32[64,768]{1,0:T(8,128)S(1)}, f32[64,768]{1,0:T(8,128)S(1)}, u32[]{:S(2)}, u32[]{:S(2)}) collective-permute-start(f32[64,768]{1,0:T(8,128)S(1)} %get-tuple-element.17), channel_id=1, source_target_pairs={{0,8},{8,0},{16,24},{24,16},{1,9},{9,1},{17,25},{25,17},{2,10},{10... | collective-permute-start | bytes 589832 | tf_op jit(solution)/shard_map/ppermute | solution.py:17
  27.1 0.4 collective-permute-start.15
  27.6 5.8 %collective-permute-done.11.refs_1_ = f32[64,768]{1,0:T(8,128)S(1)} collective-permute-done((f32[64,768]{1,0:T(8,128)S(1)}, f32[64,768]{1,0:T(8,128)S(1)}, u32[]{:S(2)}, u32[]{:S(2)}) %collective-permute-start.11) | collective-permute-done | bytes 196640 | tf_op jit(solution)/shard_map/ppermute | solution.py:17
  33.4 2.6 %collective-permute-start.16 = (f32[64,768]{1,0:T(8,128)S(1)}, f32[64,768]{1,0:T(8,128)S(1)}, u32[]{:S(2)}, u32[]{:S(2)}) collective-permute-start(f32[64,768]{1,0:T(8,128)S(1)} %sum_near.1.refs_6_.refs_2_), channel_id=1, source_target_pairs={{0,16},{8,24},{16,0},{24,8},{1,17},{9,25},{17,1},{25,9},{2,18},{10... | collective-permute-start | bytes 589832 | tf_op jit(solution)/shard_map/ppermute | solution.py:17
  36.1 1.6 %collective-permute-start.12 = (bf16[128,768]{1,0:T(8,128)(2,1)S(1)}, bf16[128,768]{1,0:T(8,128)(2,1)S(1)}, u32[]{:S(2)}, u32[]{:S(2)}) collective-permute-start(bf16[128,768]{1,0:T(8,128)(2,1)S(1)} %get-tuple-element.18), channel_id=1, source_target_pairs={{0,2},{1,3},{2,0},{3,1},{4,6},{5,7},{6,4},{7,5},{8,10},{9,11},{10,... | collective-permute-start | bytes 589832 | tf_op jit(solution)/shard_map/ppermute | solution.py:17
  37.6 0.5 %collective-permute-start.13 = (bf16[128,768]{1,0:T(8,128)(2,1)S(1)}, bf16[128,768]{1,0:T(8,128)(2,1)S(1)}, u32[]{:S(2)}, u32[]{:S(2)}) collective-permute-start(bf16[128,768]{1,0:T(8,128)(2,1)S(1)} %get-tuple-element.19), channel_id=1, source_target_pairs={{0,4},{1,5},{2,6},{3,7},{4,0},{5,1},{6,2},{7,3},{8,12},{9,13},{10,... | collective-permute-start | bytes 589832 | tf_op jit(solution)/shard_map/ppermute | solution.py:17
  38.2 1.0 %speech_part.4.refs_3_ = f32[128,768]{1,0:T(8,128)S(1)} custom-call(f32[1]{0:T(128)S(6)} %copy.7.refs_0_, f32[1]{0:T(128)S(6)} %copy.8.refs_1_, bf16[144,768]{1,0:T(8,128)(2,1)S(1)} %get-tuple-element.12.refs_0_.refs_2_, bf16[256,768]{1,0:T(8,128)(2,1)S(1)} %join_text.1.refs_2_.refs_3_, bf16[256,768]{1,0:T(8,128)(2,1)S(1)} %collective-permute-done.7.refs_4_.refs_1_, ...), custom_call_target="tpu_custom_call" | custom-call | flops 3019898880 | bytes 1794056 | tf_op jit(solution)/shard_map/speech_part/pallas_call | solution.py:36
  39.2 1.0 %speech_part.6.refs_3_ = f32[128,768]{1,0:T(8,128)S(1)} custom-call(f32[1]{0:T(128)S(6)} %copy.7.refs_0_, f32[1]{0:T(128)S(6)} %copy.8.refs_1_, bf16[144,768]{1,0:T(8,128)(2,1)S(1)} %slice.5.refs_2_, bf16[256,768]{1,0:T(8,128)(2,1)S(1)} %join_text.1.refs_2_.refs_3_, bf16[256,768]{1,0:T(8,128)(2,1)S(1)} %collective-permute-done.7.refs_4_.refs_1_, ...), custom_call_target="tpu_custom_call" | custom-call | flops 3019898880 | bytes 1794056 | tf_op jit(solution)/shard_map/speech_part/pallas_call | solution.py:36
  40.2 1.6 %collective-permute-done.12.refs_4_ = bf16[128,768]{1,0:T(8,128)(2,1)S(1)} collective-permute-done((bf16[128,768]{1,0:T(8,128)(2,1)S(1)}, bf16[128,768]{1,0:T(8,128)(2,1)S(1)}, u32[]{:S(2)}, u32[]{:S(2)}) %collective-permute-start.12) | collective-permute-done | bytes 196640 | tf_op jit(solution)/shard_map/ppermute | solution.py:17
  41.8 1.5 %collective-permute-done.13.refs_5_ = bf16[128,768]{1,0:T(8,128)(2,1)S(1)} collective-permute-done((bf16[128,768]{1,0:T(8,128)(2,1)S(1)}, bf16[128,768]{1,0:T(8,128)(2,1)S(1)}, u32[]{:S(2)}, u32[]{:S(2)}) %collective-permute-start.13) | collective-permute-done | bytes 196640 | tf_op jit(solution)/shard_map/ppermute | solution.py:17
  43.3 0.5 %speech_part.7 = f32[128,768]{1,0:T(8,128)S(1)} custom-call(f32[1]{0:T(128)S(6)} %copy.7.refs_0_, f32[1]{0:T(128)S(6)} %copy.8.refs_1_, bf16[144,768]{1,0:T(8,128)(2,1)S(1)} %slice.5.refs_2_, f32[128,768]{1,0:T(8,128)S(1)} %speech_part.6.refs_3_, bf16[128,768]{1,0:T(8,128)(2,1)S(1)} %collective-permute-done.12.refs_4_, ...), custom_call_target="tpu_custom_call" | custom-call | flops 1006632960 | bytes 1400840 | tf_op jit(solution)/shard_map/speech_part/pallas_call | solution.py:36
  44.0 0.5 %speech_part.5.refs_1_ = f32[128,768]{1,0:T(8,128)S(1)} custom-call(f32[1]{0:T(128)S(6)} %copy.7.refs_0_, f32[1]{0:T(128)S(6)} %copy.8.refs_1_, bf16[144,768]{1,0:T(8,128)(2,1)S(1)} %get-tuple-element.12.refs_0_.refs_2_, f32[128,768]{1,0:T(8,128)S(1)} %speech_part.4.refs_3_, bf16[128,768]{1,0:T(8,128)(2,1)S(1)} %collective-permute-done.12.refs_4_, ...), custom_call_target="tpu_custom_call" | custom-call | flops 1006632960 | bytes 1400840 | tf_op jit(solution)/shard_map/speech_part/pallas_call | solution.py:36
  44.5 1.1 %collective-permute-done.14.refs_2_ = f32[128,768]{1,0:T(8,128)S(1)} collective-permute-done((f32[128,768]{1,0:T(8,128)S(1)}, f32[128,768]{1,0:T(8,128)S(1)}, u32[]{:S(2)}, u32[]{:S(2)}) %collective-permute-start.14) | collective-permute-done | bytes 393248 | tf_op jit(solution)/shard_map/ppermute | solution.py:17
  45.6 1.1 %finish.1 = (f32[128,768]{1,0:T(8,128)}, f32[64,768]{1,0:T(8,128)}) custom-call(bf16[128,768]{1,0:T(8,128)(2,1)S(1)} %copy-done, f32[128,768]{1,0:T(8,128)S(1)} %speech_part.5.refs_1_, f32[128,768]{1,0:T(8,128)S(1)} %collective-permute-done.14.refs_2_, bf16[64,768]{1,0:T(8,128)(2,1)S(1)} %copy-done.1, f32[64,768]{1,0:T(8,128)S(1)} %text_sum.1.refs_4_), custom_call_target="tpu_custom_call" | custom-call | bytes 1867776 | tf_op jit(solution)/shard_map/finish/pallas_call | solution.py:36
  (23 shorter events, 0.4 us)
Async XLA Ops:
  0.6 5.8 %copy-start.1 = (bf16[64,768]{1,0:T(8,128)(2,1)S(1)}, bf16[64,768]{1,0:T(8,128)(2,1)}, u32[]{:S(2)}) copy-start(bf16[64,768]{1,0:T(8,128)(2,1)} %refs_3_.1) | copy-start | bytes 294916
  1.9 8.7 %collective-permute-start.3 = (bf16[144,768]{1,0:T(8,128)(2,1)S(1)}, bf16[144,768]{1,0:T(8,128)(2,1)S(1)}, u32[]{:S(2)}, u32[]{:S(2)}) collective-permute-start(bf16[144,768]{1,0:T(8,128)(2,1)S(1)} %get-tuple-element.12.refs_0_.refs_2_), channel_id=1, source_target_pairs={{0,4},{1,5},{2,6},{3,7},{4,0},{5,1},{6,2},{7,3},{8,12},{9,13},{10,... | collective-permute-start | bytes 663560 | tf_op jit(solution)/shard_map/ppermute | solution.py:17
  4.9 6.9 %collective-permute-start.4 = (bf16[144,768]{1,0:T(8,128)(2,1)S(1)}, bf16[144,768]{1,0:T(8,128)(2,1)S(1)}, u32[]{:S(2)}, u32[]{:S(2)}) collective-permute-start(bf16[144,768]{1,0:T(8,128)(2,1)S(1)} %get-tuple-element.12.refs_0_.refs_2_), channel_id=1, source_target_pairs={{0,2},{1,3},{2,0},{3,1},{4,6},{5,7},{6,4},{7,5},{8,10},{9,11},{10,... | collective-permute-start | bytes 663560 | tf_op jit(solution)/shard_map/ppermute | solution.py:17
  6.4 7.6 %collective-permute-start.1 = (bf16[64,768]{1,0:T(8,128)(2,1)S(1)}, bf16[64,768]{1,0:T(8,128)(2,1)S(1)}, u32[]{:S(2)}, u32[]{:S(2)}) collective-permute-start(bf16[64,768]{1,0:T(8,128)(2,1)S(1)} %copy-done.1), channel_id=1, source_target_pairs={{0,16},{8,24},{16,0},{24,8},{1,17},{9,25},{17,1},{25,9},{2,18},{10... | collective-permute-start | bytes 294920 | tf_op jit(solution)/shard_map/ppermute | solution.py:17
  9.0 8.0 %collective-permute-start = (bf16[64,768]{1,0:T(8,128)(2,1)S(1)}, bf16[64,768]{1,0:T(8,128)(2,1)S(1)}, u32[]{:S(2)}, u32[]{:S(2)}) collective-permute-start(bf16[64,768]{1,0:T(8,128)(2,1)S(1)} %copy-done.1), channel_id=1, source_target_pairs={{0,8},{8,0},{16,24},{24,16},{1,9},{9,1},{17,25},{25,17},{2,10},{10... | collective-permute-start | bytes 294920 | tf_op jit(solution)/shard_map/ppermute | solution.py:17
  11.8 5.0 %collective-permute-start.6 = (bf16[80,768]{1,0:T(8,128)(2,1)S(1)}, bf16[80,768]{1,0:T(8,128)(2,1)S(1)}, u32[]{:S(2)}, u32[]{:S(2)}) collective-permute-start(bf16[80,768]{1,0:T(8,128)(2,1)S(1)} %get-tuple-element.15), channel_id=1, source_target_pairs={{0,4},{1,5},{2,6},{3,7},{4,0},{5,1},{6,2},{7,3},{8,12},{9,13},{10,... | collective-permute-start | bytes 368648 | tf_op jit(solution)/shard_map/ppermute | solution.py:17
  12.2 4.6 %collective-permute-start.5 = (bf16[64,768]{1,0:T(8,128)(2,1)S(1)}, bf16[64,768]{1,0:T(8,128)(2,1)S(1)}, u32[]{:S(2)}, u32[]{:S(2)}) collective-permute-start(bf16[64,768]{1,0:T(8,128)(2,1)S(1)} %get-tuple-element.14), channel_id=1, source_target_pairs={{0,2},{1,3},{2,0},{3,1},{4,6},{5,7},{6,4},{7,5},{8,10},{9,11},{10,... | collective-permute-start | bytes 294920 | tf_op jit(solution)/shard_map/ppermute | solution.py:17
  13.9 9.0 %collective-permute-start.9 = (bf16[432,768]{1,0:T(8,128)(2,1)S(1)}, bf16[432,768]{1,0:T(8,128)(2,1)S(1)}, u32[]{:S(2)}, u32[]{:S(2)}) collective-permute-start(bf16[432,768]{1,0:T(8,128)(2,1)S(1)} %join_speech.1.refs_3_), channel_id=1, source_target_pairs={{0,1},{1,0},{2,3},{3,2},{4,5},{5,4},{6,7},{7,6},{8,9},{9,8},{10,11... | collective-permute-start | bytes 1990664 | tf_op jit(solution)/shard_map/ppermute | solution.py:17
  14.1 5.3 %collective-permute-start.2 = (bf16[64,768]{1,0:T(8,128)(2,1)S(1)}, bf16[64,768]{1,0:T(8,128)(2,1)S(1)}, u32[]{:S(2)}, u32[]{:S(2)}) collective-permute-start(bf16[64,768]{1,0:T(8,128)(2,1)S(1)} %unit_far.1.refs_2_), channel_id=1, source_target_pairs={{0,8},{8,0},{16,24},{24,16},{1,9},{9,1},{17,25},{25,17},{2,10},{10... | collective-permute-start | bytes 294920 | tf_op jit(solution)/shard_map/ppermute | solution.py:17
  16.9 8.0 %collective-permute-start.10 = (bf16[144,768]{1,0:T(8,128)(2,1)S(1)}, bf16[144,768]{1,0:T(8,128)(2,1)S(1)}, u32[]{:S(2)}, u32[]{:S(2)}) collective-permute-start(bf16[144,768]{1,0:T(8,128)(2,1)S(1)} %join_far.1.refs_4_), channel_id=1, source_target_pairs={{0,1},{1,0},{2,3},{3,2},{4,5},{5,4},{6,7},{7,6},{8,9},{9,8},{10,11... | collective-permute-start | bytes 663560 | tf_op jit(solution)/shard_map/ppermute | solution.py:17
  19.5 16.6 %collective-permute-start.7 = (bf16[256,768]{1,0:T(8,128)(2,1)S(1)}, bf16[256,768]{1,0:T(8,128)(2,1)S(1)}, u32[]{:S(2)}, u32[]{:S(2)}) collective-permute-start(bf16[256,768]{1,0:T(8,128)(2,1)S(1)} %join_text.1.refs_2_.refs_3_), channel_id=1, source_target_pairs={{0,2},{1,3},{2,0},{3,1},{4,6},{5,7},{6,4},{7,5},{8,10},{9,11},{10,... | collective-permute-start | bytes 1179656 | tf_op jit(solution)/shard_map/ppermute | solution.py:17
  20.0 16.1 %collective-permute-start.8 = (bf16[256,768]{1,0:T(8,128)(2,1)S(1)}, bf16[256,768]{1,0:T(8,128)(2,1)S(1)}, u32[]{:S(2)}, u32[]{:S(2)}) collective-permute-start(bf16[256,768]{1,0:T(8,128)(2,1)S(1)} %join_text.1.refs_2_.refs_3_), channel_id=1, source_target_pairs={{0,4},{1,5},{2,6},{3,7},{4,0},{5,1},{6,2},{7,3},{8,12},{9,13},{10,... | collective-permute-start | bytes 1179656 | tf_op jit(solution)/shard_map/ppermute | solution.py:17
  25.5 7.9 %collective-permute-start.11 = (f32[64,768]{1,0:T(8,128)S(1)}, f32[64,768]{1,0:T(8,128)S(1)}, u32[]{:S(2)}, u32[]{:S(2)}) collective-permute-start(f32[64,768]{1,0:T(8,128)S(1)} %get-tuple-element.17), channel_id=1, source_target_pairs={{0,8},{8,0},{16,24},{24,16},{1,9},{9,1},{17,25},{25,17},{2,10},{10... | collective-permute-start | bytes 589832 | tf_op jit(solution)/shard_map/ppermute | solution.py:17
  27.1 16.8 %collective-permute-start.15 = (f32[64,768]{1,0:T(8,128)S(1)}, f32[64,768]{1,0:T(8,128)S(1)}, u32[]{:S(2)}, u32[]{:S(2)}) collective-permute-start(f32[64,768]{1,0:T(8,128)S(1)} %get-tuple-element.21), channel_id=1, source_target_pairs={{0,8},{8,0},{16,24},{24,16},{1,9},{9,1},{17,25},{25,17},{2,10},{10... | collective-permute-start | bytes 589832 | tf_op jit(solution)/shard_map/ppermute | solution.py:17
  33.4 10.5 %collective-permute-start.16 = (f32[64,768]{1,0:T(8,128)S(1)}, f32[64,768]{1,0:T(8,128)S(1)}, u32[]{:S(2)}, u32[]{:S(2)}) collective-permute-start(f32[64,768]{1,0:T(8,128)S(1)} %sum_near.1.refs_6_.refs_2_), channel_id=1, source_target_pairs={{0,16},{8,24},{16,0},{24,8},{1,17},{9,25},{17,1},{25,9},{2,18},{10... | collective-permute-start | bytes 589832 | tf_op jit(solution)/shard_map/ppermute | solution.py:17
  36.1 5.7 %collective-permute-start.12 = (bf16[128,768]{1,0:T(8,128)(2,1)S(1)}, bf16[128,768]{1,0:T(8,128)(2,1)S(1)}, u32[]{:S(2)}, u32[]{:S(2)}) collective-permute-start(bf16[128,768]{1,0:T(8,128)(2,1)S(1)} %get-tuple-element.18), channel_id=1, source_target_pairs={{0,2},{1,3},{2,0},{3,1},{4,6},{5,7},{6,4},{7,5},{8,10},{9,11},{10,... | collective-permute-start | bytes 589832 | tf_op jit(solution)/shard_map/ppermute | solution.py:17
  37.6 5.7 %collective-permute-start.13 = (bf16[128,768]{1,0:T(8,128)(2,1)S(1)}, bf16[128,768]{1,0:T(8,128)(2,1)S(1)}, u32[]{:S(2)}, u32[]{:S(2)}) collective-permute-start(bf16[128,768]{1,0:T(8,128)(2,1)S(1)} %get-tuple-element.19), channel_id=1, source_target_pairs={{0,4},{1,5},{2,6},{3,7},{4,0},{5,1},{6,2},{7,3},{8,12},{9,13},{10,... | collective-permute-start | bytes 589832 | tf_op jit(solution)/shard_map/ppermute | solution.py:17
  43.8 1.8 %collective-permute-start.14 = (f32[128,768]{1,0:T(8,128)S(1)}, f32[128,768]{1,0:T(8,128)S(1)}, u32[]{:S(2)}, u32[]{:S(2)}) collective-permute-start(f32[128,768]{1,0:T(8,128)S(1)} %speech_part.7), channel_id=1, source_target_pairs={{0,1},{1,0},{2,3},{3,2},{4,5},{5,4},{6,7},{7,6},{8,9},{9,8},{10,11... | collective-permute-start | bytes 1179656 | tf_op jit(solution)/shard_map/ppermute | solution.py:17
  44.0 1.6 %copy-start = (bf16[128,768]{1,0:T(8,128)(2,1)S(1)}, bf16[128,768]{1,0:T(8,128)(2,1)}, u32[]{:S(2)}) copy-start(bf16[128,768]{1,0:T(8,128)(2,1)} %refs_0_.7) | copy-start | bytes 589828

commit v5 on v4

--- a/solution.py
+++ b/solution.py
@@ -22,10 +22,7 @@
 
 
 def call(body, out_shape, operands, after=(), flops=0, temporary=0, name="kernel"):
-    specs = []
-    for v in operands:
-        scalar = v.shape == (1,)
-        specs.append(pl.BlockSpec(memory_space=pltpu.SMEM if scalar else pltpu.VMEM))
+    specs = [pl.BlockSpec(memory_space=pltpu.VMEM) for _ in operands]
     specs += [pl.BlockSpec(memory_space=pl.ANY) for _ in after]
     used = len(operands)
 
@@ -50,15 +47,15 @@
     return floats / norms, norms
 
 
-def prepare_body(audio_hbm, sentence_hbm, label_hbm, speech, text, audio, sentence, label, done):
-    pairs = [(audio_hbm, audio), (sentence_hbm, sentence), (label_hbm, label)]
-    copies = [
-        pltpu.make_async_copy(source, target, done.at[i]) for i, (source, target) in enumerate(pairs)
-    ]
+def prepare_body(*refs):
+    sources, (speech, text) = refs[:3], refs[3:5]
+    held, done = refs[5:8], refs[8]
+    copies = [pltpu.make_async_copy(sources[i], held[i], done.at[i]) for i in range(3)]
     for copy in copies:
         copy.start()
     for copy in copies:
         copy.wait()
+    audio, sentence, label = held
     rows = audio.shape[0]
     speech[0:rows, :] = direction(audio[...])[0].astype(jnp.bfloat16)
     text[...] = direction(sentence[...])[0].astype(jnp.bfloat16)
@@ -76,27 +73,24 @@
     out[...] = direction(values[...])[0].astype(jnp.bfloat16)
 
 
-def join_body(raw, *refs):
-    out = refs[-1]
-    at = 0
-    for ref, is_raw in zip(refs[:-1], raw):
-        target = out.at[at : at + ref.shape[0], :]
-        at += ref.shape[0]
+def join_body(chips, raw, *refs):
+    speech, text = refs[-2:]
+    rows = refs[0].shape[0]
+    for k in range(chips):
+        speech[k * rows : (k + 1) * rows, :] = refs[k][...]
+    rows = refs[chips].shape[0]
+    for k, is_raw in enumerate(raw):
+        block = refs[chips + k]
+        target = text.at[k * rows : (k + 1) * rows, :]
         if is_raw:
-            unit_body(ref, target)
+            unit_body(block, target)
         else:
-            target[...] = ref[...]
+            target[...] = block[...]
 
 
 def halves_body(upper, lower, upper_out, lower_out):
     upper_out[...] = upper[: upper_out.shape[0], :]
     lower_out[...] = lower[upper_out.shape[0] :, :]
-
-
-def joined(blocks, raw=None, after=(), name="join"):
-    shape = (sum(v.shape[0] for v in blocks), blocks[0].shape[1])
-    body = functools.partial(join_body, raw or [False] * len(blocks))
-    return call(body, jax.ShapeDtypeStruct(shape, jnp.bfloat16), blocks, after, name=name)
 
 
 def marks_of(block, rows):
@@ -115,9 +109,9 @@
 
 
 def text_part_body(rows, own_text, has_start, speeches, *refs):
-    sharp, shift, text = refs[0][0], refs[1][0], refs[2][...]
-    total = refs[3][...] if has_start else None
-    at = 4 if has_start else 3
+    sharp, shift, text = refs[0][0:1, 0:1], refs[0][1:2, 0:1], refs[1][...]
+    total = refs[2][...] if has_start else None
+    at = 3 if has_start else 2
     blocks = refs[at : at + speeches]
     outs = refs[at + speeches :]
     groups = lax.axis_size("group")
@@ -145,9 +139,9 @@
 
 
 def speech_part_body(rows, own_text, has_start, masks, *refs):
-    sharp, shift, speech = refs[0][0], refs[1][0], refs[2]
-    total = refs[3][...] if has_start else None
-    texts, out = list(refs[4 if has_start else 3 : -1]), refs[-1]
+    sharp, shift, speech = refs[0][0:1, 0:1], refs[0][1:2, 0:1], refs[1]
+    total = refs[2][...] if has_start else None
+    texts, out = list(refs[3 if has_start else 2 : -1]), refs[-1]
     groups = lax.axis_size("group")
     members = lax.axis_size("member")
     group = lax.axis_index("group")
@@ -169,6 +163,11 @@
     out[...] = total
 
 
+def sum_near_body(mine, came, kept, total, kept_out):
+    total[...] = mine[...] + came[...]
+    kept_out[...] = kept[...]
+
+
 def sum_body(*refs):
     total = refs[0][...]
     for ref in refs[1:-1]:
@@ -193,8 +192,10 @@
     chips = members // 2
     rows, width = audio_vectors.shape
     own_text = sentence_vectors.shape[0]
-    scalars = [sharpness_array, offset_term]
     label = matching_indices.reshape(1, rows)
+    scalars = jnp.concatenate(
+        [jnp.broadcast_to(v[:, None], (1, 128)) for v in (sharpness_array, offset_term)], axis=0
+    )
 
     def bf16(*shape):
         return jax.ShapeDtypeStruct(shape, jnp.bfloat16)
@@ -202,20 +203,19 @@
     def f32(*shape):
         return jax.ShapeDtypeStruct(shape, jnp.float32)
 
+    arguments = [audio_vectors, sentence_vectors, label]
     speech_own, text_own = pl.pallas_call(
         prepare_body,
         out_shape=[bf16(rows + MARK_ROWS, width), bf16(own_text, width)],
         in_specs=[pl.BlockSpec(memory_space=pltpu.HBM)] * 3,
         out_specs=[pl.BlockSpec(memory_space=pltpu.VMEM)] * 2,
         scratch_shapes=[
-            pltpu.VMEM((rows, width), jnp.bfloat16),
-            pltpu.VMEM((own_text, width), jnp.bfloat16),
-            pltpu.VMEM((1, rows), jnp.int32),
+            *[pltpu.VMEM(v.shape, v.dtype) for v in arguments],
             pltpu.SemaphoreType.DMA((3,)),
         ],
         compiler_params=pltpu.CompilerParams(vmem_limit_bytes=8 << 20),
         name="unit_rows",
-    )(*[pltpu.with_memory_space_constraint(v, pltpu.HBM) for v in (audio_vectors, sentence_vectors, label)])
+    )(*[pltpu.with_memory_space_constraint(v, pltpu.HBM) for v in arguments])
     text_blocks = [text_own] + [None] * (groups - 1)
     raw = [False] * groups
     for k in [1 << i for i in reversed(range(groups.bit_length() - 1))]:
@@ -223,7 +223,7 @@
             came = exchanged(text_blocks[j] if j else sentence_vectors, "group", k)
             raw[j + k] = not j
             if not j and k > 1:
-                came = call(unit_body, bf16(own_text, width), [came], (), EARLY, name="unit_far")
+                came = call(unit_body, bf16(own_text, width), [came], (scalars,), EARLY, name="unit_far")
                 raw[j + k] = False
             text_blocks[j + k] = came
     square = chips == 4
@@ -236,27 +236,28 @@
         )
         return [exchanged(half, "member", 2 * k) for half, k in zip(halves, masks)]
 
-    speech_near = [exchanged(speech_own, "member", 2 * k) for k in masks]
-    speech = [joined([speech_own, *speech_near], name="join_speech")]
-    other = [exchanged(speech[0], "member", 1)]
-    if square:
-        speech.append(joined(far_halves(speech_near, rows // 2), name="join_far"))
-        other.append(exchanged(speech[1], "member", 1))
-    text = joined(text_blocks, raw, (speech[-1],), name="join_text")
+    speech_blocks = [exchanged(speech_own, "member", 2 * k) for k in reversed(range(1, chips))]
+    column = groups * own_text
+    speech, text = call(
+        functools.partial(join_body, chips, raw),
+        [bf16(chips * (rows + MARK_ROWS), width), bf16(column, width)],
+        [speech_own, *speech_blocks, *text_blocks],
+        name="join_rows",
+    )
+    other = exchanged(speech, "member", 1)
     text_near = [exchanged(text, "member", 2 * k) for k in masks]
 
-    column = groups * own_text
     temporary = 4 * column * (6 * CHUNK + 3 * width)
 
     def text_part(outs, blocks, start):
         count = sum(v.shape[0] for v in blocks) // (rows + MARK_ROWS)
         body = functools.partial(text_part_body, rows, own_text, bool(start), len(blocks))
-        operands = [*scalars, text, *start, *blocks]
+        operands = [scalars, text, *start, *blocks]
         work = 4 * column * count * rows * width
         return call(body, outs, operands, (), work, temporary, "text_part")
 
-    half = text_part([f32(column, width)], [*speech, *other[:-1]], [])
-    parts = list(text_part([f32(own_text, width)] * groups, other[-1:], half))
+    half = text_part([f32(column, width)], [speech], [])
+    parts = list(text_part([f32(own_text, width)] * groups, [other], half))
 
     text_back = [parts[0]]
     for bit in [1 << i for i in range(groups.bit_length() - 1)]:
@@ -265,25 +266,28 @@
             if k == bit:
                 text_back.append(came)
             else:
-                parts[k - bit] = call(
-                    sum_body, f32(own_text, width), [parts[k - bit], came], name="sum_near"
+                parts[k - bit], parts[bit] = call(
+                    sum_near_body,
+                    [f32(own_text, width)] * 2,
+                    [parts[k - bit], came, parts[bit]],
+                    name="sum_near",
                 )
 
     def speech_part(block, start, columns, texts, after=()):
         body = functools.partial(speech_part_body, rows, own_text, bool(start), columns)
-        operands = [*scalars, block, *start, *texts]
+        operands = [scalars, block, *start, *texts]
         work = 40 * rows * column * len(columns) * width
         return call(body, f32(rows, width), operands, after, work, temporary, "speech_part")
 
     near = [[0, *masks], [text, *text_near], (parts[groups // 2],)]
-    away = speech_part(other[0][0 : rows + MARK_ROWS], [], *near)
+    away = speech_part(other[0 : rows + MARK_ROWS], [], *near)
     home = speech_part(speech_own, [], *near)
     if square:
         text_far = far_halves(text_near, column // 2, (parts[groups // 2],))
-        away = speech_part(other[0][0 : rows + MARK_ROWS], [away], [3], text_far)
+        away = speech_part(other[0 : rows + MARK_ROWS], [away], [3], text_far)
         home = speech_part(speech_own, [home], [3], text_far)
     back = exchanged(away, "member", 1)
-    text_back = call(sum_body, f32(own_text, width), text_back, (), EARLY, name="text_sum")
+    text_back = call(sum_body, f32(own_text, width), text_back[::-1], (), EARLY, name="text_sum")
     speech_grad, text_grad = call(
         finish_body,
         [f32(rows, width), f32(own_text, width)],

time: 46.8 us -> 42.7 us (0.912)
  starting transfers between devices: 21.5 us -> 17.8 us
  Pallas kernels: 8.25 us -> 7.2 us
    ppermute x17 -> x15, starting transfers between devices: 21.5 us -> 17.8 us  [exchanged(): return lax.ppermute(value, axis, [(i, i ^ mask) for i in range(size)])]
    pallas_call x15 -> x12, Pallas kernels: 7.04 us -> 5.99 us  [call(): pl.pallas_call(whole, out_shape=out_shape, in_specs=specs, out_specs=jax....]
    ppermute x17 -> x15, waiting for transfers between devices: 14.8 us -> 15 us  [exchanged(): return lax.ppermute(value, axis, [(i, i ^ mask) for i in range(size)])]
  transfers between devices with their start and end apart: 17 -> 15, of which waited for: 7 -> 9; matrix products, arithmetic and copies ran while one was open for 0% -> 0% of each run, Pallas kernels for 13% -> 14%
where the time goes in v5:
time: 42.7 us; the launch traced here: 42.6 us
  starting transfers between devices  17.8 us (42%)
  waiting for transfers between devices  15 us (35%)
  Pallas kernels  7.2 us (17%)
  between operations  2.07 us (5%)
  local copies, waits for them, and re-layouts  0.49 us (1%)
    ppermute x15, starting transfers between devices, exchanged(): return lax.ppermute(value, axis, [(i, i ^ mask) for i in range(size)])  17.8 us
    ppermute x15, waiting for transfers between devices, exchanged(): return lax.ppermute(value, axis, [(i, i ^ mask) for i in range(size)])  15 us
    pallas_call x12, Pallas kernels, call(): pl.pallas_call(whole, out_shape=out_shape, in_specs=specs, out_specs=jax....  5.99 us
    pallas_call x1, Pallas kernels, shards(): pl.pallas_call(prepare_body, out_shape=[bf16(rows + MARK_ROWS, width), bf...  1.21 us
  transfers between devices with their start and end apart: 15, of which 9 were waited for; matrix products, arithmetic and copies ran while one was open for 0% of the time, Pallas kernels for 14%

profile of v5, /device:TPU:0, one launch (start us, length us, event | category | flops | bytes accessed | tf_op | source)
XLA Modules:
  0.0 42.6 jit_solution(14183810378752614605)
XLA Ops:
  0.6 4.1 %collective-permute-start.4 = (bf16[64,768]{1,0:T(8,128)(2,1)}, bf16[64,768]{1,0:T(8,128)(2,1)S(1)}, u32[]{:S(2)}, u32[]{:S(2)}) collective-permute-start(bf16[64,768]{1,0:T(8,128)(2,1)} %refs_3_.1), channel_id=1, source_target_pairs={{0,16},{8,24},{16,0},{24,8},{1,17},{9,25},{17,1},{25,9},{2,18},{10... | collective-permute-start | bytes 294920 | tf_op jit(solution)/shard_map/ppermute | solution.py:17
  4.7 1.2 %unit_rows.1 = (bf16[144,768]{1,0:T(8,128)(2,1)S(1)}, bf16[64,768]{1,0:T(8,128)(2,1)S(1)}) custom-call(bf16[128,768]{1,0:T(8,128)(2,1)} %refs_0_.3, bf16[64,768]{1,0:T(8,128)(2,1)} %refs_3_.1, s32[1,128]{1,0:T(1,128)} %bitcast.3), custom_call_target="tpu_custom_call" | custom-call | tf_op jit(solution)/shard_map/unit_rows/pallas_call | solution.py:207
  6.0 2.5 %collective-permute-start = (bf16[144,768]{1,0:T(8,128)(2,1)S(1)}, bf16[144,768]{1,0:T(8,128)(2,1)S(1)}, u32[]{:S(2)}, u32[]{:S(2)}) collective-permute-start(bf16[144,768]{1,0:T(8,128)(2,1)S(1)} %get-tuple-element.14.refs_0_.refs_1_), channel_id=1, source_target_pairs={{0,6},{1,7},{2,4},{3,5},{4,2},{5,3},{6,0},{7,1},{8,14},{9,15},{10,... | collective-permute-start | bytes 663560 | tf_op jit(solution)/shard_map/ppermute | solution.py:17
  8.5 0.5 %collective-permute-start.1 = (bf16[144,768]{1,0:T(8,128)(2,1)S(1)}, bf16[144,768]{1,0:T(8,128)(2,1)S(1)}, u32[]{:S(2)}, u32[]{:S(2)}) collective-permute-start(bf16[144,768]{1,0:T(8,128)(2,1)S(1)} %get-tuple-element.14.refs_0_.refs_1_), channel_id=1, source_target_pairs={{0,4},{1,5},{2,6},{3,7},{4,0},{5,1},{6,2},{7,3},{8,12},{9,13},{10,... | collective-permute-start | bytes 663560 | tf_op jit(solution)/shard_map/ppermute | solution.py:17
  9.0 0.5 %collective-permute-start.2 = (bf16[144,768]{1,0:T(8,128)(2,1)S(1)}, bf16[144,768]{1,0:T(8,128)(2,1)S(1)}, u32[]{:S(2)}, u32[]{:S(2)}) collective-permute-start(bf16[144,768]{1,0:T(8,128)(2,1)S(1)} %get-tuple-element.14.refs_0_.refs_1_), channel_id=1, source_target_pairs={{0,2},{1,3},{2,0},{3,1},{4,6},{5,7},{6,4},{7,5},{8,10},{9,11},{10,... | collective-permute-start | bytes 663560 | tf_op jit(solution)/shard_map/ppermute | solution.py:17
  9.5 1.6 %collective-permute-start.3 = (bf16[64,768]{1,0:T(8,128)(2,1)S(1)}, bf16[64,768]{1,0:T(8,128)(2,1)S(1)}, u32[]{:S(2)}, u32[]{:S(2)}) collective-permute-start(bf16[64,768]{1,0:T(8,128)(2,1)S(1)} %copy-done.1), channel_id=1, source_target_pairs={{0,8},{8,0},{16,24},{24,16},{1,9},{9,1},{17,25},{25,17},{2,10},{10... | collective-permute-start | bytes 294920 | tf_op jit(solution)/shard_map/ppermute | solution.py:17
  12.5 0.1 unit_far.1.refs_6_
  12.6 0.5 %collective-permute-start.5 = (bf16[64,768]{1,0:T(8,128)(2,1)S(1)}, bf16[64,768]{1,0:T(8,128)(2,1)S(1)}, u32[]{:S(2)}, u32[]{:S(2)}) collective-permute-start(bf16[64,768]{1,0:T(8,128)(2,1)S(1)} %unit_far.1.refs_6_), channel_id=1, source_target_pairs={{0,8},{8,0},{16,24},{24,16},{1,9},{9,1},{17,25},{25,17},{2,10},{10... | collective-permute-start | bytes 294920 | tf_op jit(solution)/shard_map/ppermute | solution.py:17
  13.1 1.5 %collective-permute-done.3.refs_5_ = bf16[64,768]{1,0:T(8,128)(2,1)S(1)} collective-permute-done((bf16[64,768]{1,0:T(8,128)(2,1)S(1)}, bf16[64,768]{1,0:T(8,128)(2,1)S(1)}, u32[]{:S(2)}, u32[]{:S(2)}) %collective-permute-start.3) | collective-permute-done | bytes 98336 | tf_op jit(solution)/shard_map/ppermute | solution.py:17
  14.6 2.7 %collective-permute-done.5.refs_7_ = bf16[64,768]{1,0:T(8,128)(2,1)S(1)} collective-permute-done((bf16[64,768]{1,0:T(8,128)(2,1)S(1)}, bf16[64,768]{1,0:T(8,128)(2,1)S(1)}, u32[]{:S(2)}, u32[]{:S(2)}) %collective-permute-start.5) | collective-permute-done | bytes 98336 | tf_op jit(solution)/shard_map/ppermute | solution.py:17
  17.3 1.3 %collective-permute-done.1.refs_2_ = bf16[144,768]{1,0:T(8,128)(2,1)S(1)} collective-permute-done((bf16[144,768]{1,0:T(8,128)(2,1)S(1)}, bf16[144,768]{1,0:T(8,128)(2,1)S(1)}, u32[]{:S(2)}, u32[]{:S(2)}) %collective-permute-start.1) | collective-permute-done | bytes 221216 | tf_op jit(solution)/shard_map/ppermute | solution.py:17
  18.6 0.1 join_rows.1
  18.8 1.6 %collective-permute-start.6 = (bf16[256,768]{1,0:T(8,128)(2,1)S(1)}, bf16[256,768]{1,0:T(8,128)(2,1)S(1)}, u32[]{:S(2)}, u32[]{:S(2)}) collective-permute-start(bf16[256,768]{1,0:T(8,128)(2,1)S(1)} %get-tuple-element.16.refs_1_.refs_2_), channel_id=1, source_target_pairs={{0,2},{1,3},{2,0},{3,1},{4,6},{5,7},{6,4},{7,5},{8,10},{9,11},{10,... | collective-permute-start | bytes 1179656 | tf_op jit(solution)/shard_map/ppermute | solution.py:17
  20.4 0.7 %collective-permute-start.7 = (bf16[256,768]{1,0:T(8,128)(2,1)S(1)}, bf16[256,768]{1,0:T(8,128)(2,1)S(1)}, u32[]{:S(2)}, u32[]{:S(2)}) collective-permute-start(bf16[256,768]{1,0:T(8,128)(2,1)S(1)} %get-tuple-element.16.refs_1_.refs_2_), channel_id=1, source_target_pairs={{0,4},{1,5},{2,6},{3,7},{4,0},{5,1},{6,2},{7,3},{8,12},{9,13},{10,... | collective-permute-start | bytes 1179656 | tf_op jit(solution)/shard_map/ppermute | solution.py:17
  21.1 0.8 %text_part.2.refs_2_ = f32[256,768]{1,0:T(8,128)S(1)} custom-call(f32[2,128]{1,0:T(2,128)S(1)} %concatenate.6.refs_1_.refs_0_, bf16[256,768]{1,0:T(8,128)(2,1)S(1)} %get-tuple-element.16.refs_1_.refs_2_, bf16[576,768]{1,0:T(8,128)(2,1)S(1)} %get-tuple-element.17.refs_2_), custom_call_target="tpu_custom_call" | custom-call | flops 402653184 | bytes 2065408 | tf_op jit(solution)/shard_map/text_part/pallas_call | solution.py:33
  21.9 0.8 %text_part.3 = (f32[64,768]{1,0:T(8,128)S(1)}, f32[64,768]{1,0:T(8,128)S(1)}, f32[64,768]{1,0:T(8,128)S(1)}, f32[64,768]{1,0:T(8,128)S(1)}) custom-call(f32[2,128]{1,0:T(2,128)S(1)} %concatenate.6.refs_1_.refs_0_, bf16[256,768]{1,0:T(8,128)(2,1)S(1)} %get-tuple-element.16.refs_1_.refs_2_, f32[256,768]{1,0:T(8,128)S(1)} %text_part.2.refs_2_, ...), custom_call_target="tpu_custom_call" | custom-call | flops 402653184 | bytes 2851840 | tf_op jit(solution)/shard_map/text_part/pallas_call | solution.py:33
  22.7 1.6 %collective-permute-start.9 = (f32[64,768]{1,0:T(8,128)S(1)}, f32[64,768]{1,0:T(8,128)S(1)}, u32[]{:S(2)}, u32[]{:S(2)}) collective-permute-start(f32[64,768]{1,0:T(8,128)S(1)} %get-tuple-element.19), channel_id=1, source_target_pairs={{0,8},{8,0},{16,24},{24,16},{1,9},{9,1},{17,25},{25,17},{2,10},{10... | collective-permute-start | bytes 589832 | tf_op jit(solution)/shard_map/ppermute | solution.py:17
  24.4 5.1 %collective-permute-done.9.refs_1_ = f32[64,768]{1,0:T(8,128)S(1)} collective-permute-done((f32[64,768]{1,0:T(8,128)S(1)}, f32[64,768]{1,0:T(8,128)S(1)}, u32[]{:S(2)}, u32[]{:S(2)}) %collective-permute-start.9) | collective-permute-done | bytes 196640 | tf_op jit(solution)/shard_map/ppermute | solution.py:17
  29.5 0.4 collective-permute-start.13
  29.9 1.6 %collective-permute-start.14 = (f32[64,768]{1,0:T(8,128)S(1)}, f32[64,768]{1,0:T(8,128)S(1)}, u32[]{:S(2)}, u32[]{:S(2)}) collective-permute-start(f32[64,768]{1,0:T(8,128)S(1)} %get-tuple-element.24), channel_id=1, source_target_pairs={{0,8},{8,0},{16,24},{24,16},{1,9},{9,1},{17,25},{25,17},{2,10},{10... | collective-permute-start | bytes 589832 | tf_op jit(solution)/shard_map/ppermute | solution.py:17
  31.5 0.1 collective-permute-done.7.refs_4_.refs_0_
  31.6 1.2 %collective-permute-start.10 = (bf16[128,768]{1,0:T(8,128)(2,1)S(1)}, bf16[128,768]{1,0:T(8,128)(2,1)S(1)}, u32[]{:S(2)}, u32[]{:S(2)}) collective-permute-start(bf16[128,768]{1,0:T(8,128)(2,1)S(1)} %get-tuple-element.22), channel_id=1, source_target_pairs={{0,2},{1,3},{2,0},{3,1},{4,6},{5,7},{6,4},{7,5},{8,10},{9,11},{10,... | collective-permute-start | bytes 589832 | tf_op jit(solution)/shard_map/ppermute | solution.py:17
  32.8 0.8 %collective-permute-start.11 = (bf16[128,768]{1,0:T(8,128)(2,1)S(1)}, bf16[128,768]{1,0:T(8,128)(2,1)S(1)}, u32[]{:S(2)}, u32[]{:S(2)}) collective-permute-start(bf16[128,768]{1,0:T(8,128)(2,1)S(1)} %get-tuple-element.23), channel_id=1, source_target_pairs={{0,4},{1,5},{2,6},{3,7},{4,0},{5,1},{6,2},{7,3},{8,12},{9,13},{10,... | collective-permute-start | bytes 589832 | tf_op jit(solution)/shard_map/ppermute | solution.py:17
  33.6 1.0 %speech_part.4.refs_2_ = f32[128,768]{1,0:T(8,128)S(1)} custom-call(f32[2,128]{1,0:T(2,128)S(1)} %concatenate.6.refs_1_.refs_0_, bf16[144,768]{1,0:T(8,128)(2,1)S(1)} %get-tuple-element.14.refs_0_.refs_1_, bf16[256,768]{1,0:T(8,128)(2,1)S(1)} %get-tuple-element.16.refs_1_.refs_2_, bf16[256,768]{1,0:T(8,128)(2,1)S(1)} %collective-permute-done.6.refs_3_.refs_1_, ...), custom_call_target="tpu_custom_call" | custom-call | flops 3019898880 | bytes 1795072 | tf_op jit(solution)/shard_map/speech_part/pallas_call | solution.py:33
  34.7 1.0 %speech_part.6.refs_2_ = f32[128,768]{1,0:T(8,128)S(1)} custom-call(f32[2,128]{1,0:T(2,128)S(1)} %concatenate.6.refs_1_.refs_0_, bf16[144,768]{1,0:T(8,128)(2,1)S(1)} %slice.5.refs_1_, bf16[256,768]{1,0:T(8,128)(2,1)S(1)} %get-tuple-element.16.refs_1_.refs_2_, bf16[256,768]{1,0:T(8,128)(2,1)S(1)} %collective-permute-done.6.refs_3_.refs_1_, ...), custom_call_target="tpu_custom_call" | custom-call | flops 3019898880 | bytes 1795072 | tf_op jit(solution)/shard_map/speech_part/pallas_call | solution.py:33
  35.7 2.1 %collective-permute-done.10.refs_3_ = bf16[128,768]{1,0:T(8,128)(2,1)S(1)} collective-permute-done((bf16[128,768]{1,0:T(8,128)(2,1)S(1)}, bf16[128,768]{1,0:T(8,128)(2,1)S(1)}, u32[]{:S(2)}, u32[]{:S(2)}) %collective-permute-start.10) | collective-permute-done | bytes 196640 | tf_op jit(solution)/shard_map/ppermute | solution.py:17
  37.8 0.7 %collective-permute-done.11.refs_4_ = bf16[128,768]{1,0:T(8,128)(2,1)S(1)} collective-permute-done((bf16[128,768]{1,0:T(8,128)(2,1)S(1)}, bf16[128,768]{1,0:T(8,128)(2,1)S(1)}, u32[]{:S(2)}, u32[]{:S(2)}) %collective-permute-start.11) | collective-permute-done | bytes 196640 | tf_op jit(solution)/shard_map/ppermute | solution.py:17
  38.5 0.5 %speech_part.7 = f32[128,768]{1,0:T(8,128)S(1)} custom-call(f32[2,128]{1,0:T(2,128)S(1)} %concatenate.6.refs_1_.refs_0_, bf16[144,768]{1,0:T(8,128)(2,1)S(1)} %slice.5.refs_1_, f32[128,768]{1,0:T(8,128)S(1)} %speech_part.6.refs_2_, bf16[128,768]{1,0:T(8,128)(2,1)S(1)} %collective-permute-done.10.refs_3_, bf16[128,768]{1,0:T(8,128)(2,1)S(1)} %collective-permute-done.11.refs_4_), custom_call_target="tpu_custom_call" | custom-call | flops 1006632960 | bytes 1401856 | tf_op jit(solution)/shard_map/speech_part/pallas_call | solution.py:33
  39.1 1.5 %collective-permute-done.13.refs_0_ = f32[64,768]{1,0:T(8,128)S(1)} collective-permute-done((f32[64,768]{1,0:T(8,128)S(1)}, f32[64,768]{1,0:T(8,128)S(1)}, u32[]{:S(2)}, u32[]{:S(2)}) %collective-permute-start.13) | collective-permute-done | bytes 196640 | tf_op jit(solution)/shard_map/ppermute | solution.py:17
  40.6 0.5 %speech_part.5.refs_1_ = f32[128,768]{1,0:T(8,128)S(1)} custom-call(f32[2,128]{1,0:T(2,128)S(1)} %concatenate.6.refs_1_.refs_0_, bf16[144,768]{1,0:T(8,128)(2,1)S(1)} %get-tuple-element.14.refs_0_.refs_1_, f32[128,768]{1,0:T(8,128)S(1)} %speech_part.4.refs_2_, bf16[128,768]{1,0:T(8,128)(2,1)S(1)} %collective-permute-done.10.refs_3_, ...), custom_call_target="tpu_custom_call" | custom-call | flops 1006632960 | bytes 1401856 | tf_op jit(solution)/shard_map/speech_part/pallas_call | solution.py:33
  41.1 0.4 copy-done
  41.5 1.0 %finish.1 = (f32[128,768]{1,0:T(8,128)}, f32[64,768]{1,0:T(8,128)}) custom-call(bf16[128,768]{1,0:T(8,128)(2,1)S(1)} %copy-done, f32[128,768]{1,0:T(8,128)S(1)} %speech_part.5.refs_1_, f32[128,768]{1,0:T(8,128)S(1)} %collective-permute-done.12.refs_2_, bf16[64,768]{1,0:T(8,128)(2,1)S(1)} %copy-done.1, f32[64,768]{1,0:T(8,128)S(1)} %text_sum.1.refs_4_), custom_call_target="tpu_custom_call" | custom-call | bytes 1867776 | tf_op jit(solution)/shard_map/finish/pallas_call | solution.py:33
  (18 shorter events, 0.4 us)
Async XLA Ops:
  0.6 11.8 %collective-permute-start.4 = (bf16[64,768]{1,0:T(8,128)(2,1)}, bf16[64,768]{1,0:T(8,128)(2,1)S(1)}, u32[]{:S(2)}, u32[]{:S(2)}) collective-permute-start(bf16[64,768]{1,0:T(8,128)(2,1)} %refs_3_.1), channel_id=1, source_target_pairs={{0,16},{8,24},{16,0},{24,8},{1,17},{9,25},{17,1},{25,9},{2,18},{10... | collective-permute-start | bytes 294920 | tf_op jit(solution)/shard_map/ppermute | solution.py:17
  4.7 4.8 %copy-start.1 = (bf16[64,768]{1,0:T(8,128)(2,1)S(1)}, bf16[64,768]{1,0:T(8,128)(2,1)}, u32[]{:S(2)}) copy-start(bf16[64,768]{1,0:T(8,128)(2,1)} %refs_3_.1) | copy-start | bytes 294916
  6.0 11.3 %collective-permute-start = (bf16[144,768]{1,0:T(8,128)(2,1)S(1)}, bf16[144,768]{1,0:T(8,128)(2,1)S(1)}, u32[]{:S(2)}, u32[]{:S(2)}) collective-permute-start(bf16[144,768]{1,0:T(8,128)(2,1)S(1)} %get-tuple-element.14.refs_0_.refs_1_), channel_id=1, source_target_pairs={{0,6},{1,7},{2,4},{3,5},{4,2},{5,3},{6,0},{7,1},{8,14},{9,15},{10,... | collective-permute-start | bytes 663560 | tf_op jit(solution)/shard_map/ppermute | solution.py:17
  8.5 10.1 %collective-permute-start.1 = (bf16[144,768]{1,0:T(8,128)(2,1)S(1)}, bf16[144,768]{1,0:T(8,128)(2,1)S(1)}, u32[]{:S(2)}, u32[]{:S(2)}) collective-permute-start(bf16[144,768]{1,0:T(8,128)(2,1)S(1)} %get-tuple-element.14.refs_0_.refs_1_), channel_id=1, source_target_pairs={{0,4},{1,5},{2,6},{3,7},{4,0},{5,1},{6,2},{7,3},{8,12},{9,13},{10,... | collective-permute-start | bytes 663560 | tf_op jit(solution)/shard_map/ppermute | solution.py:17
  9.0 9.7 %collective-permute-start.2 = (bf16[144,768]{1,0:T(8,128)(2,1)S(1)}, bf16[144,768]{1,0:T(8,128)(2,1)S(1)}, u32[]{:S(2)}, u32[]{:S(2)}) collective-permute-start(bf16[144,768]{1,0:T(8,128)(2,1)S(1)} %get-tuple-element.14.refs_0_.refs_1_), channel_id=1, source_target_pairs={{0,2},{1,3},{2,0},{3,1},{4,6},{5,7},{6,4},{7,5},{8,10},{9,11},{10,... | collective-permute-start | bytes 663560 | tf_op jit(solution)/shard_map/ppermute | solution.py:17
  9.5 5.1 %collective-permute-start.3 = (bf16[64,768]{1,0:T(8,128)(2,1)S(1)}, bf16[64,768]{1,0:T(8,128)(2,1)S(1)}, u32[]{:S(2)}, u32[]{:S(2)}) collective-permute-start(bf16[64,768]{1,0:T(8,128)(2,1)S(1)} %copy-done.1), channel_id=1, source_target_pairs={{0,8},{8,0},{16,24},{24,16},{1,9},{9,1},{17,25},{25,17},{2,10},{10... | collective-permute-start | bytes 294920 | tf_op jit(solution)/shard_map/ppermute | solution.py:17
  12.6 4.7 %collective-permute-start.5 = (bf16[64,768]{1,0:T(8,128)(2,1)S(1)}, bf16[64,768]{1,0:T(8,128)(2,1)S(1)}, u32[]{:S(2)}, u32[]{:S(2)}) collective-permute-start(bf16[64,768]{1,0:T(8,128)(2,1)S(1)} %unit_far.1.refs_6_), channel_id=1, source_target_pairs={{0,8},{8,0},{16,24},{24,16},{1,9},{9,1},{17,25},{25,17},{2,10},{10... | collective-permute-start | bytes 294920 | tf_op jit(solution)/shard_map/ppermute | solution.py:17
  18.8 3.1 %collective-permute-start.8 = (bf16[576,768]{1,0:T(8,128)(2,1)S(1)}, bf16[576,768]{1,0:T(8,128)(2,1)S(1)}, u32[]{:S(2)}, u32[]{:S(2)}) collective-permute-start(bf16[576,768]{1,0:T(8,128)(2,1)S(1)} %get-tuple-element.17.refs_2_), channel_id=1, source_target_pairs={{0,1},{1,0},{2,3},{3,2},{4,5},{5,4},{6,7},{7,6},{8,9},{9,8},{10,11... | collective-permute-start | bytes 2654216 | tf_op jit(solution)/shard_map/ppermute | solution.py:17
  18.8 12.6 %collective-permute-start.6 = (bf16[256,768]{1,0:T(8,128)(2,1)S(1)}, bf16[256,768]{1,0:T(8,128)(2,1)S(1)}, u32[]{:S(2)}, u32[]{:S(2)}) collective-permute-start(bf16[256,768]{1,0:T(8,128)(2,1)S(1)} %get-tuple-element.16.refs_1_.refs_2_), channel_id=1, source_target_pairs={{0,2},{1,3},{2,0},{3,1},{4,6},{5,7},{6,4},{7,5},{8,10},{9,11},{10,... | collective-permute-start | bytes 1179656 | tf_op jit(solution)/shard_map/ppermute | solution.py:17
  20.4 11.2 %collective-permute-start.7 = (bf16[256,768]{1,0:T(8,128)(2,1)S(1)}, bf16[256,768]{1,0:T(8,128)(2,1)S(1)}, u32[]{:S(2)}, u32[]{:S(2)}) collective-permute-start(bf16[256,768]{1,0:T(8,128)(2,1)S(1)} %get-tuple-element.16.refs_1_.refs_2_), channel_id=1, source_target_pairs={{0,4},{1,5},{2,6},{3,7},{4,0},{5,1},{6,2},{7,3},{8,12},{9,13},{10,... | collective-permute-start | bytes 1179656 | tf_op jit(solution)/shard_map/ppermute | solution.py:17
  22.7 6.8 %collective-permute-start.9 = (f32[64,768]{1,0:T(8,128)S(1)}, f32[64,768]{1,0:T(8,128)S(1)}, u32[]{:S(2)}, u32[]{:S(2)}) collective-permute-start(f32[64,768]{1,0:T(8,128)S(1)} %get-tuple-element.19), channel_id=1, source_target_pairs={{0,8},{8,0},{16,24},{24,16},{1,9},{9,1},{17,25},{25,17},{2,10},{10... | collective-permute-start | bytes 589832 | tf_op jit(solution)/shard_map/ppermute | solution.py:17
  29.5 11.0 %collective-permute-start.13 = (f32[64,768]{1,0:T(8,128)S(1)}, f32[64,768]{1,0:T(8,128)S(1)}, u32[]{:S(2)}, u32[]{:S(2)}) collective-permute-start(f32[64,768]{1,0:T(8,128)S(1)} %get-tuple-element.21.refs_5_.refs_2_), channel_id=1, source_target_pairs={{0,16},{8,24},{16,0},{24,8},{1,17},{9,25},{17,1},{25,9},{2,18},{10... | collective-permute-start | bytes 589832 | tf_op jit(solution)/shard_map/ppermute | solution.py:17
  29.9 10.7 %collective-permute-start.14 = (f32[64,768]{1,0:T(8,128)S(1)}, f32[64,768]{1,0:T(8,128)S(1)}, u32[]{:S(2)}, u32[]{:S(2)}) collective-permute-start(f32[64,768]{1,0:T(8,128)S(1)} %get-tuple-element.24), channel_id=1, source_target_pairs={{0,8},{8,0},{16,24},{24,16},{1,9},{9,1},{17,25},{25,17},{2,10},{10... | collective-permute-start | bytes 589832 | tf_op jit(solution)/shard_map/ppermute | solution.py:17
  31.6 6.2 %collective-permute-start.10 = (bf16[128,768]{1,0:T(8,128)(2,1)S(1)}, bf16[128,768]{1,0:T(8,128)(2,1)S(1)}, u32[]{:S(2)}, u32[]{:S(2)}) collective-permute-start(bf16[128,768]{1,0:T(8,128)(2,1)S(1)} %get-tuple-element.22), channel_id=1, source_target_pairs={{0,2},{1,3},{2,0},{3,1},{4,6},{5,7},{6,4},{7,5},{8,10},{9,11},{10,... | collective-permute-start | bytes 589832 | tf_op jit(solution)/shard_map/ppermute | solution.py:17
  32.8 5.7 %collective-permute-start.11 = (bf16[128,768]{1,0:T(8,128)(2,1)S(1)}, bf16[128,768]{1,0:T(8,128)(2,1)S(1)}, u32[]{:S(2)}, u32[]{:S(2)}) collective-permute-start(bf16[128,768]{1,0:T(8,128)(2,1)S(1)} %get-tuple-element.23), channel_id=1, source_target_pairs={{0,4},{1,5},{2,6},{3,7},{4,0},{5,1},{6,2},{7,3},{8,12},{9,13},{10,... | collective-permute-start | bytes 589832 | tf_op jit(solution)/shard_map/ppermute | solution.py:17
  39.0 2.1 %collective-permute-start.12 = (f32[128,768]{1,0:T(8,128)S(1)}, f32[128,768]{1,0:T(8,128)S(1)}, u32[]{:S(2)}, u32[]{:S(2)}) collective-permute-start(f32[128,768]{1,0:T(8,128)S(1)} %speech_part.7), channel_id=1, source_target_pairs={{0,1},{1,0},{2,3},{3,2},{4,5},{5,4},{6,7},{7,6},{8,9},{9,8},{10,11... | collective-permute-start | bytes 1179656 | tf_op jit(solution)/shard_map/ppermute | solution.py:17
  40.6 0.9 %copy-start = (bf16[128,768]{1,0:T(8,128)(2,1)S(1)}, bf16[128,768]{1,0:T(8,128)(2,1)}, u32[]{:S(2)}) copy-start(bf16[128,768]{1,0:T(8,128)(2,1)} %refs_0_.3) | copy-start | bytes 589828

commit v6 on v5

--- a/solution.py
+++ b/solution.py
@@ -69,23 +69,17 @@
     ).astype(jnp.bfloat16)
 
 
-def unit_body(values, out):
-    out[...] = direction(values[...])[0].astype(jnp.bfloat16)
-
-
-def join_body(chips, raw, *refs):
-    speech, text = refs[-2:]
-    rows = refs[0].shape[0]
-    for k in range(chips):
-        speech[k * rows : (k + 1) * rows, :] = refs[k][...]
-    rows = refs[chips].shape[0]
-    for k, is_raw in enumerate(raw):
-        block = refs[chips + k]
-        target = text.at[k * rows : (k + 1) * rows, :]
-        if is_raw:
-            unit_body(block, target)
-        else:
-            target[...] = block[...]
+def join_body(*refs):
+    out = refs[-1]
+    at = 0
+    for ref in refs[:-1]:
+        out[at : at + ref.shape[0], :] = ref[...]
+        at += ref.shape[0]
+
+
+def join_both_body(count, *refs):
+    join_body(*refs[:count], refs[-2])
+    join_body(*refs[count:-2], refs[-1])
 
 
 def halves_body(upper, lower, upper_out, lower_out):
@@ -108,9 +102,11 @@
     return lax.dot_general(left, right, (((1,), (1,)), ((), ())), preferred_element_type=jnp.float32)
 
 
-def text_part_body(rows, own_text, has_start, speeches, *refs):
-    sharp, shift, text = refs[0][0:1, 0:1], refs[0][1:2, 0:1], refs[1][...]
-    total = refs[2][...] if has_start else None
+def text_part_body(rows, own_text, ks, has_start, speeches, *refs):
+    sharp, shift = refs[0][0:1, 0:1], refs[0][1:2, 0:1]
+    some_text = slice(ks[0] * own_text, (ks[-1] + 1) * own_text)
+    text = refs[1][some_text, :]
+    total = refs[2][some_text, :] if has_start else None
     at = 3 if has_start else 2
     blocks = refs[at : at + speeches]
     outs = refs[at + speeches :]
@@ -128,7 +124,7 @@
             chunk = jnp.concatenate(chunk, axis=0)
             marks = jnp.concatenate(marks, axis=1)
             iota = lax.broadcasted_iota(jnp.int32, (own_text, marks.shape[1]), 0)
-            ids = [((group ^ k) * members + member) * own_text + iota for k in range(groups)]
+            ids = [((group ^ k) * members + member) * own_text + iota for k in ks]
             match = jnp.concatenate(ids, axis=0).astype(jnp.float32) == marks
             coef = coefficients(dot_rows(text, chunk), match, sharp, shift)
             part = jnp.dot(coef, chunk, preferred_element_type=jnp.float32)
@@ -216,16 +212,14 @@
         compiler_params=pltpu.CompilerParams(vmem_limit_bytes=8 << 20),
         name="unit_rows",
     )(*[pltpu.with_memory_space_constraint(v, pltpu.HBM) for v in arguments])
+    def passed_on(block):
+        return call(join_body, bf16(own_text, width), [block], (scalars,), 1 << 29, name="pass_on")
+
     text_blocks = [text_own] + [None] * (groups - 1)
-    raw = [False] * groups
     for k in [1 << i for i in reversed(range(groups.bit_length() - 1))]:
         for j in range(0, groups, 2 * k):
-            came = exchanged(text_blocks[j] if j else sentence_vectors, "group", k)
-            raw[j + k] = not j
-            if not j and k > 1:
-                came = call(unit_body, bf16(own_text, width), [came], (scalars,), EARLY, name="unit_far")
-                raw[j + k] = False
-            text_blocks[j + k] = came
+            came = exchanged(text_blocks[j], "group", k)
+            text_blocks[j + k] = passed_on(came) if k > 1 else came
     square = chips == 4
     masks = [1, 2] if square else list(range(1, chips))
 
@@ -238,10 +232,10 @@
 
     speech_blocks = [exchanged(speech_own, "member", 2 * k) for k in reversed(range(1, chips))]
     column = groups * own_text
-    speech, text = call(
-        functools.partial(join_body, chips, raw),
-        [bf16(chips * (rows + MARK_ROWS), width), bf16(column, width)],
-        [speech_own, *speech_blocks, *text_blocks],
+    text, speech = call(
+        functools.partial(join_both_body, groups),
+        [bf16(column, width), bf16(chips * (rows + MARK_ROWS), width)],
+        [*text_blocks, speech_own, *speech_blocks[::-1]],
         name="join_rows",
     )
     other = exchanged(speech, "member", 1)
@@ -249,15 +243,20 @@
 
     temporary = 4 * column * (6 * CHUNK + 3 * width)
 
-    def text_part(outs, blocks, start):
+    def text_part(outs, blocks, start, ks=range(groups)):
         count = sum(v.shape[0] for v in blocks) // (rows + MARK_ROWS)
-        body = functools.partial(text_part_body, rows, own_text, bool(start), len(blocks))
+        body = functools.partial(text_part_body, rows, own_text, list(ks), bool(start), len(blocks))
         operands = [scalars, text, *start, *blocks]
-        work = 4 * column * count * rows * width
+        work = 4 * len(ks) * own_text * count * rows * width
         return call(body, outs, operands, (), work, temporary, "text_part")
 
     half = text_part([f32(column, width)], [speech], [])
-    parts = list(text_part([f32(own_text, width)] * groups, [other], half))
+    parts = [None] * groups
+    first = [groups - 1]
+    parts[groups - 1] = text_part([f32(own_text, width)], [other], half, first)[0]
+    rest = list(range(groups - 1))
+    for k, part in zip(rest, text_part([f32(own_text, width)] * len(rest), [other], half, rest)):
+        parts[k] = part
 
     text_back = [parts[0]]
     for bit in [1 << i for i in range(groups.bit_length() - 1)]:
@@ -287,7 +286,7 @@
         away = speech_part(other[0 : rows + MARK_ROWS], [away], [3], text_far)
         home = speech_part(speech_own, [home], [3], text_far)
     back = exchanged(away, "member", 1)
-    text_back = call(sum_body, f32(own_text, width), text_back[::-1], (), EARLY, name="text_sum")
+    text_back = call(sum_body, f32(own_text, width), text_back[::-1], (home,), EARLY, name="text_sum")
     speech_grad, text_grad = call(
         finish_body,
         [f32(rows, width), f32(own_text, width)],

time: 42.7 us -> 43.6 us (1.021)
  local copies, waits for them, and re-layouts: 0.49 us -> 1.03 us
    unnamed x4, local copies, waits for them, and re-layouts: 0.4 us -> 0.94 us
    pallas_call x12 -> x13, Pallas kernels: 5.99 us -> 6.43 us  [call(): pl.pallas_call(whole, out_shape=out_shape, in_specs=specs, out_specs=jax....]
  transfers between devices with their start and end apart: 15 -> 15, of which waited for: 9 -> 9; matrix products, arithmetic and copies ran while one was open for 0% -> 0% of each run, Pallas kernels for 14% -> 12%
where the time goes in v6:
time: 43.6 us; the launch traced here: 43.5 us
  starting transfers between devices  18 us (41%)
  waiting for transfers between devices  14.7 us (34%)
  Pallas kernels  7.61 us (17%)
  between operations  2.07 us (5%)
  local copies, waits for them, and re-layouts  1.03 us (2%)
    ppermute x15, starting transfers between devices, exchanged(): return lax.ppermute(value, axis, [(i, i ^ mask) for i in range(size)])  18 us
    ppermute x15, waiting for transfers between devices, exchanged(): return lax.ppermute(value, axis, [(i, i ^ mask) for i in range(size)])  14.7 us
    pallas_call x13, Pallas kernels, call(): pl.pallas_call(whole, out_shape=out_shape, in_specs=specs, out_specs=jax....  6.43 us
    pallas_call x1, Pallas kernels, shards(): pl.pallas_call(prepare_body, out_shape=[bf16(rows + MARK_ROWS, width), bf...  1.18 us
    unnamed x4, local copies, waits for them, and re-layouts  0.94 us
  transfers between devices with their start and end apart: 15, of which 9 were waited for; matrix products, arithmetic and copies ran while one was open for 0% of the time, Pallas kernels for 12%

profile of v6, /device:TPU:0, one launch (start us, length us, event | category | flops | bytes accessed | tf_op | source)
XLA Modules:
  0.0 43.5 jit_solution(393634877438301859)
XLA Ops:
  0.6 1.2 %unit_rows.1 = (bf16[144,768]{1,0:T(8,128)(2,1)S(1)}, bf16[64,768]{1,0:T(8,128)(2,1)S(1)}) custom-call(bf16[128,768]{1,0:T(8,128)(2,1)} %refs_0_.3, bf16[64,768]{1,0:T(8,128)(2,1)} %refs_3_.1, s32[1,128]{1,0:T(1,128)} %bitcast.3), custom_call_target="tpu_custom_call" | custom-call | tf_op jit(solution)/shard_map/unit_rows/pallas_call | solution.py:203
  1.8 4.1 %collective-permute-start.1 = (bf16[64,768]{1,0:T(8,128)(2,1)S(1)}, bf16[64,768]{1,0:T(8,128)(2,1)S(1)}, u32[]{:S(2)}, u32[]{:S(2)}) collective-permute-start(bf16[64,768]{1,0:T(8,128)(2,1)S(1)} %get-tuple-element.14.refs_0_), channel_id=1, source_target_pairs={{0,16},{8,24},{16,0},{24,8},{1,17},{9,25},{17,1},{25,9},{2,18},{10... | collective-permute-start | bytes 294920 | tf_op jit(solution)/shard_map/ppermute | solution.py:17
  5.9 2.4 %collective-permute-start.5 = (bf16[144,768]{1,0:T(8,128)(2,1)S(1)}, bf16[144,768]{1,0:T(8,128)(2,1)S(1)}, u32[]{:S(2)}, u32[]{:S(2)}) collective-permute-start(bf16[144,768]{1,0:T(8,128)(2,1)S(1)} %get-tuple-element.13.refs_4_.refs_1_), channel_id=1, source_target_pairs={{0,6},{1,7},{2,4},{3,5},{4,2},{5,3},{6,0},{7,1},{8,14},{9,15},{10,... | collective-permute-start | bytes 663560 | tf_op jit(solution)/shard_map/ppermute | solution.py:17
  8.4 0.5 %collective-permute-start.4 = (bf16[144,768]{1,0:T(8,128)(2,1)S(1)}, bf16[144,768]{1,0:T(8,128)(2,1)S(1)}, u32[]{:S(2)}, u32[]{:S(2)}) collective-permute-start(bf16[144,768]{1,0:T(8,128)(2,1)S(1)} %get-tuple-element.13.refs_4_.refs_1_), channel_id=1, source_target_pairs={{0,4},{1,5},{2,6},{3,7},{4,0},{5,1},{6,2},{7,3},{8,12},{9,13},{10,... | collective-permute-start | bytes 663560 | tf_op jit(solution)/shard_map/ppermute | solution.py:17
  8.9 0.5 %collective-permute-start.3 = (bf16[144,768]{1,0:T(8,128)(2,1)S(1)}, bf16[144,768]{1,0:T(8,128)(2,1)S(1)}, u32[]{:S(2)}, u32[]{:S(2)}) collective-permute-start(bf16[144,768]{1,0:T(8,128)(2,1)S(1)} %get-tuple-element.13.refs_4_.refs_1_), channel_id=1, source_target_pairs={{0,2},{1,3},{2,0},{3,1},{4,6},{5,7},{6,4},{7,5},{8,10},{9,11},{10,... | collective-permute-start | bytes 663560 | tf_op jit(solution)/shard_map/ppermute | solution.py:17
  9.4 1.6 %collective-permute-start = (bf16[64,768]{1,0:T(8,128)(2,1)S(1)}, bf16[64,768]{1,0:T(8,128)(2,1)S(1)}, u32[]{:S(2)}, u32[]{:S(2)}) collective-permute-start(bf16[64,768]{1,0:T(8,128)(2,1)S(1)} %get-tuple-element.14.refs_0_), channel_id=1, source_target_pairs={{0,8},{8,0},{16,24},{24,16},{1,9},{9,1},{17,25},{25,17},{2,10},{10... | collective-permute-start | bytes 294920 | tf_op jit(solution)/shard_map/ppermute | solution.py:17
  12.4 0.5 %collective-permute-start.2 = (bf16[64,768]{1,0:T(8,128)(2,1)S(1)}, bf16[64,768]{1,0:T(8,128)(2,1)S(1)}, u32[]{:S(2)}, u32[]{:S(2)}) collective-permute-start(bf16[64,768]{1,0:T(8,128)(2,1)S(1)} %pass_on.1.refs_2_), channel_id=1, source_target_pairs={{0,8},{8,0},{16,24},{24,16},{1,9},{9,1},{17,25},{25,17},{2,10},{10... | collective-permute-start | bytes 294920 | tf_op jit(solution)/shard_map/ppermute | solution.py:17
  12.9 1.8 %collective-permute-done.refs_1_ = bf16[64,768]{1,0:T(8,128)(2,1)S(1)} collective-permute-done((bf16[64,768]{1,0:T(8,128)(2,1)S(1)}, bf16[64,768]{1,0:T(8,128)(2,1)S(1)}, u32[]{:S(2)}, u32[]{:S(2)}) %collective-permute-start) | collective-permute-done | bytes 98336 | tf_op jit(solution)/shard_map/ppermute | solution.py:17
  14.7 2.4 %collective-permute-done.2.refs_3_ = bf16[64,768]{1,0:T(8,128)(2,1)S(1)} collective-permute-done((bf16[64,768]{1,0:T(8,128)(2,1)S(1)}, bf16[64,768]{1,0:T(8,128)(2,1)S(1)}, u32[]{:S(2)}, u32[]{:S(2)}) %collective-permute-start.2) | collective-permute-done | bytes 98336 | tf_op jit(solution)/shard_map/ppermute | solution.py:17
  17.1 1.4 %collective-permute-done.4.refs_6_ = bf16[144,768]{1,0:T(8,128)(2,1)S(1)} collective-permute-done((bf16[144,768]{1,0:T(8,128)(2,1)S(1)}, bf16[144,768]{1,0:T(8,128)(2,1)S(1)}, u32[]{:S(2)}, u32[]{:S(2)}) %collective-permute-start.4) | collective-permute-done | bytes 221216 | tf_op jit(solution)/shard_map/ppermute | solution.py:17
  18.4 0.1 collective-permute-done.3.refs_5_
  18.6 0.1 join_rows.1
  18.7 1.5 %collective-permute-start.7 = (bf16[256,768]{1,0:T(8,128)(2,1)S(1)}, bf16[256,768]{1,0:T(8,128)(2,1)S(1)}, u32[]{:S(2)}, u32[]{:S(2)}) collective-permute-start(bf16[256,768]{1,0:T(8,128)(2,1)S(1)} %get-tuple-element.15.refs_1_.refs_2_), channel_id=1, source_target_pairs={{0,4},{1,5},{2,6},{3,7},{4,0},{5,1},{6,2},{7,3},{8,12},{9,13},{10,... | collective-permute-start | bytes 1179656 | tf_op jit(solution)/shard_map/ppermute | solution.py:17
  20.2 0.8 %collective-permute-start.6 = (bf16[256,768]{1,0:T(8,128)(2,1)S(1)}, bf16[256,768]{1,0:T(8,128)(2,1)S(1)}, u32[]{:S(2)}, u32[]{:S(2)}) collective-permute-start(bf16[256,768]{1,0:T(8,128)(2,1)S(1)} %get-tuple-element.15.refs_1_.refs_2_), channel_id=1, source_target_pairs={{0,2},{1,3},{2,0},{3,1},{4,6},{5,7},{6,4},{7,5},{8,10},{9,11},{10,... | collective-permute-start | bytes 1179656 | tf_op jit(solution)/shard_map/ppermute | solution.py:17
  21.0 0.8 %text_part.3.refs_2_ = f32[256,768]{1,0:T(8,128)S(1)} custom-call(f32[2,128]{1,0:T(2,128)S(1)} %concatenate.6.refs_1_.refs_0_, bf16[256,768]{1,0:T(8,128)(2,1)S(1)} %get-tuple-element.15.refs_1_.refs_2_, bf16[576,768]{1,0:T(8,128)(2,1)S(1)} %get-tuple-element.16.refs_2_), custom_call_target="tpu_custom_call" | custom-call | flops 402653184 | bytes 2065408 | tf_op jit(solution)/shard_map/text_part/pallas_call | solution.py:33
  21.8 0.6 %text_part.5 = f32[64,768]{1,0:T(8,128)S(1)} custom-call(f32[2,128]{1,0:T(2,128)S(1)} %concatenate.6.refs_1_.refs_0_, bf16[256,768]{1,0:T(8,128)(2,1)S(1)} %get-tuple-element.15.refs_1_.refs_2_, f32[256,768]{1,0:T(8,128)S(1)} %text_part.3.refs_2_, bf16[576,768]{1,0:T(8,128)(2,1)S(1)} %collective-permute-done.8.refs_3_), custom_call_target="tpu_custom_call" | custom-call | flops 100663296 | bytes 2262016 | tf_op jit(solution)/shard_map/text_part/pallas_call | solution.py:33
  22.4 1.6 %collective-permute-start.9 = (f32[64,768]{1,0:T(8,128)S(1)}, f32[64,768]{1,0:T(8,128)S(1)}, u32[]{:S(2)}, u32[]{:S(2)}) collective-permute-start(f32[64,768]{1,0:T(8,128)S(1)} %text_part.5), channel_id=1, source_target_pairs={{0,8},{8,0},{16,24},{24,16},{1,9},{9,1},{17,25},{25,17},{2,10},{10... | collective-permute-start | bytes 589832 | tf_op jit(solution)/shard_map/ppermute | solution.py:17
  24.1 0.7 %text_part.4 = (f32[64,768]{1,0:T(8,128)S(1)}, f32[64,768]{1,0:T(8,128)S(1)}, f32[64,768]{1,0:T(8,128)S(1)}) custom-call(f32[2,128]{1,0:T(2,128)S(1)} %concatenate.6.refs_1_.refs_0_, bf16[256,768]{1,0:T(8,128)(2,1)S(1)} %get-tuple-element.15.refs_1_.refs_2_, f32[256,768]{1,0:T(8,128)S(1)} %text_part.3.refs_2_, ...), custom_call_target="tpu_custom_call" | custom-call | flops 301989888 | bytes 2655232 | tf_op jit(solution)/shard_map/text_part/pallas_call | solution.py:33
  24.8 4.3 %collective-permute-done.9.refs_1_ = f32[64,768]{1,0:T(8,128)S(1)} collective-permute-done((f32[64,768]{1,0:T(8,128)S(1)}, f32[64,768]{1,0:T(8,128)S(1)}, u32[]{:S(2)}, u32[]{:S(2)}) %collective-permute-start.9) | collective-permute-done | bytes 196640 | tf_op jit(solution)/shard_map/ppermute | solution.py:17
  29.2 1.6 %collective-permute-start.14 = (f32[64,768]{1,0:T(8,128)S(1)}, f32[64,768]{1,0:T(8,128)S(1)}, u32[]{:S(2)}, u32[]{:S(2)}) collective-permute-start(f32[64,768]{1,0:T(8,128)S(1)} %get-tuple-element.22), channel_id=1, source_target_pairs={{0,8},{8,0},{16,24},{24,16},{1,9},{9,1},{17,25},{25,17},{2,10},{10... | collective-permute-start | bytes 589832 | tf_op jit(solution)/shard_map/ppermute | solution.py:17
  30.8 0.5 %collective-permute-start.13 = (f32[64,768]{1,0:T(8,128)S(1)}, f32[64,768]{1,0:T(8,128)S(1)}, u32[]{:S(2)}, u32[]{:S(2)}) collective-permute-start(f32[64,768]{1,0:T(8,128)S(1)} %get-tuple-element.19.refs_5_.refs_2_), channel_id=1, source_target_pairs={{0,16},{8,24},{16,0},{24,8},{1,17},{9,25},{17,1},{25,9},{2,18},{10... | collective-permute-start | bytes 589832 | tf_op jit(solution)/shard_map/ppermute | solution.py:17
  31.4 1.1 %collective-permute-start.10 = (bf16[128,768]{1,0:T(8,128)(2,1)S(1)}, bf16[128,768]{1,0:T(8,128)(2,1)S(1)}, u32[]{:S(2)}, u32[]{:S(2)}) collective-permute-start(bf16[128,768]{1,0:T(8,128)(2,1)S(1)} %get-tuple-element.20), channel_id=1, source_target_pairs={{0,2},{1,3},{2,0},{3,1},{4,6},{5,7},{6,4},{7,5},{8,10},{9,11},{10,... | collective-permute-start | bytes 589832 | tf_op jit(solution)/shard_map/ppermute | solution.py:17
  32.5 1.1 %collective-permute-start.11 = (bf16[128,768]{1,0:T(8,128)(2,1)S(1)}, bf16[128,768]{1,0:T(8,128)(2,1)S(1)}, u32[]{:S(2)}, u32[]{:S(2)}) collective-permute-start(bf16[128,768]{1,0:T(8,128)(2,1)S(1)} %get-tuple-element.21), channel_id=1, source_target_pairs={{0,4},{1,5},{2,6},{3,7},{4,0},{5,1},{6,2},{7,3},{8,12},{9,13},{10,... | collective-permute-start | bytes 589832 | tf_op jit(solution)/shard_map/ppermute | solution.py:17
  33.6 1.0 %speech_part.4.refs_2_ = f32[128,768]{1,0:T(8,128)S(1)} custom-call(f32[2,128]{1,0:T(2,128)S(1)} %concatenate.6.refs_1_.refs_0_, bf16[144,768]{1,0:T(8,128)(2,1)S(1)} %get-tuple-element.13.refs_4_.refs_1_, bf16[256,768]{1,0:T(8,128)(2,1)S(1)} %get-tuple-element.15.refs_1_.refs_2_, bf16[256,768]{1,0:T(8,128)(2,1)S(1)} %collective-permute-done.6.refs_3_.refs_1_, ...), custom_call_target="tpu_custom_call" | custom-call | flops 3019898880 | bytes 1795072 | tf_op jit(solution)/shard_map/speech_part/pallas_call | solution.py:33
  34.6 1.0 %speech_part.6.refs_2_ = f32[128,768]{1,0:T(8,128)S(1)} custom-call(f32[2,128]{1,0:T(2,128)S(1)} %concatenate.6.refs_1_.refs_0_, bf16[144,768]{1,0:T(8,128)(2,1)S(1)} %slice.5.refs_1_, bf16[256,768]{1,0:T(8,128)(2,1)S(1)} %get-tuple-element.15.refs_1_.refs_2_, bf16[256,768]{1,0:T(8,128)(2,1)S(1)} %collective-permute-done.6.refs_3_.refs_1_, ...), custom_call_target="tpu_custom_call" | custom-call | flops 3019898880 | bytes 1795072 | tf_op jit(solution)/shard_map/speech_part/pallas_call | solution.py:33
  35.6 2.0 %collective-permute-done.10.refs_3_ = bf16[128,768]{1,0:T(8,128)(2,1)S(1)} collective-permute-done((bf16[128,768]{1,0:T(8,128)(2,1)S(1)}, bf16[128,768]{1,0:T(8,128)(2,1)S(1)}, u32[]{:S(2)}, u32[]{:S(2)}) %collective-permute-start.10) | collective-permute-done | bytes 196640 | tf_op jit(solution)/shard_map/ppermute | solution.py:17
  37.6 0.6 %collective-permute-done.11.refs_4_ = bf16[128,768]{1,0:T(8,128)(2,1)S(1)} collective-permute-done((bf16[128,768]{1,0:T(8,128)(2,1)S(1)}, bf16[128,768]{1,0:T(8,128)(2,1)S(1)}, u32[]{:S(2)}, u32[]{:S(2)}) %collective-permute-start.11) | collective-permute-done | bytes 196640 | tf_op jit(solution)/shard_map/ppermute | solution.py:17
  38.2 0.5 %speech_part.7 = f32[128,768]{1,0:T(8,128)S(1)} custom-call(f32[2,128]{1,0:T(2,128)S(1)} %concatenate.6.refs_1_.refs_0_, bf16[144,768]{1,0:T(8,128)(2,1)S(1)} %slice.5.refs_1_, f32[128,768]{1,0:T(8,128)S(1)} %speech_part.6.refs_2_, bf16[128,768]{1,0:T(8,128)(2,1)S(1)} %collective-permute-done.10.refs_3_, bf16[128,768]{1,0:T(8,128)(2,1)S(1)} %collective-permute-done.11.refs_4_), custom_call_target="tpu_custom_call" | custom-call | flops 1006632960 | bytes 1401856 | tf_op jit(solution)/shard_map/speech_part/pallas_call | solution.py:33
  38.8 0.5 %speech_part.5.refs_3_.refs_1_ = f32[128,768]{1,0:T(8,128)S(1)} custom-call(f32[2,128]{1,0:T(2,128)S(1)} %concatenate.6.refs_1_.refs_0_, bf16[144,768]{1,0:T(8,128)(2,1)S(1)} %get-tuple-element.13.refs_4_.refs_1_, f32[128,768]{1,0:T(8,128)S(1)} %speech_part.4.refs_2_, bf16[128,768]{1,0:T(8,128)(2,1)S(1)} %collective-permute-done.10.refs_3_, ...), custom_call_target="tpu_custom_call" | custom-call | flops 1006632960 | bytes 1401856 | tf_op jit(solution)/shard_map/speech_part/pallas_call | solution.py:33
  39.3 2.1 %collective-permute-done.13.refs_0_ = f32[64,768]{1,0:T(8,128)S(1)} collective-permute-done((f32[64,768]{1,0:T(8,128)S(1)}, f32[64,768]{1,0:T(8,128)S(1)}, u32[]{:S(2)}, u32[]{:S(2)}) %collective-permute-start.13) | collective-permute-done | bytes 196640 | tf_op jit(solution)/shard_map/ppermute | solution.py:17
  41.5 0.9 %copy-done = bf16[128,768]{1,0:T(8,128)(2,1)S(1)} copy-done((bf16[128,768]{1,0:T(8,128)(2,1)S(1)}, bf16[128,768]{1,0:T(8,128)(2,1)}, u32[]{:S(2)}) %copy-start) | copy-done | bytes 196632
  42.4 1.0 %finish.1 = (f32[128,768]{1,0:T(8,128)}, f32[64,768]{1,0:T(8,128)}) custom-call(bf16[128,768]{1,0:T(8,128)(2,1)S(1)} %copy-done, f32[128,768]{1,0:T(8,128)S(1)} %speech_part.5.refs_3_.refs_1_, f32[128,768]{1,0:T(8,128)S(1)} %collective-permute-done.12.refs_2_, bf16[64,768]{1,0:T(8,128)(2,1)S(1)} %copy-done.1, f32[64,768]{1,0:T(8,128)S(1)} %text_sum.1.refs_4_), custom_call_target="tpu_custom_call" | custom-call | bytes 1867776 | tf_op jit(solution)/shard_map/finish/pallas_call | solution.py:33
  (19 shorter events, 0.5 us)
Async XLA Ops:
  1.8 10.5 %collective-permute-start.1 = (bf16[64,768]{1,0:T(8,128)(2,1)S(1)}, bf16[64,768]{1,0:T(8,128)(2,1)S(1)}, u32[]{:S(2)}, u32[]{:S(2)}) collective-permute-start(bf16[64,768]{1,0:T(8,128)(2,1)S(1)} %get-tuple-element.14.refs_0_), channel_id=1, source_target_pairs={{0,16},{8,24},{16,0},{24,8},{1,17},{9,25},{17,1},{25,9},{2,18},{10... | collective-permute-start | bytes 294920 | tf_op jit(solution)/shard_map/ppermute | solution.py:17
  5.9 11.1 %collective-permute-start.5 = (bf16[144,768]{1,0:T(8,128)(2,1)S(1)}, bf16[144,768]{1,0:T(8,128)(2,1)S(1)}, u32[]{:S(2)}, u32[]{:S(2)}) collective-permute-start(bf16[144,768]{1,0:T(8,128)(2,1)S(1)} %get-tuple-element.13.refs_4_.refs_1_), channel_id=1, source_target_pairs={{0,6},{1,7},{2,4},{3,5},{4,2},{5,3},{6,0},{7,1},{8,14},{9,15},{10,... | collective-permute-start | bytes 663560 | tf_op jit(solution)/shard_map/ppermute | solution.py:17
  8.4 10.1 %collective-permute-start.4 = (bf16[144,768]{1,0:T(8,128)(2,1)S(1)}, bf16[144,768]{1,0:T(8,128)(2,1)S(1)}, u32[]{:S(2)}, u32[]{:S(2)}) collective-permute-start(bf16[144,768]{1,0:T(8,128)(2,1)S(1)} %get-tuple-element.13.refs_4_.refs_1_), channel_id=1, source_target_pairs={{0,4},{1,5},{2,6},{3,7},{4,0},{5,1},{6,2},{7,3},{8,12},{9,13},{10,... | collective-permute-start | bytes 663560 | tf_op jit(solution)/shard_map/ppermute | solution.py:17
  8.9 9.7 %collective-permute-start.3 = (bf16[144,768]{1,0:T(8,128)(2,1)S(1)}, bf16[144,768]{1,0:T(8,128)(2,1)S(1)}, u32[]{:S(2)}, u32[]{:S(2)}) collective-permute-start(bf16[144,768]{1,0:T(8,128)(2,1)S(1)} %get-tuple-element.13.refs_4_.refs_1_), channel_id=1, source_target_pairs={{0,2},{1,3},{2,0},{3,1},{4,6},{5,7},{6,4},{7,5},{8,10},{9,11},{10,... | collective-permute-start | bytes 663560 | tf_op jit(solution)/shard_map/ppermute | solution.py:17
  9.4 5.3 %collective-permute-start = (bf16[64,768]{1,0:T(8,128)(2,1)S(1)}, bf16[64,768]{1,0:T(8,128)(2,1)S(1)}, u32[]{:S(2)}, u32[]{:S(2)}) collective-permute-start(bf16[64,768]{1,0:T(8,128)(2,1)S(1)} %get-tuple-element.14.refs_0_), channel_id=1, source_target_pairs={{0,8},{8,0},{16,24},{24,16},{1,9},{9,1},{17,25},{25,17},{2,10},{10... | collective-permute-start | bytes 294920 | tf_op jit(solution)/shard_map/ppermute | solution.py:17
  12.4 4.7 %collective-permute-start.2 = (bf16[64,768]{1,0:T(8,128)(2,1)S(1)}, bf16[64,768]{1,0:T(8,128)(2,1)S(1)}, u32[]{:S(2)}, u32[]{:S(2)}) collective-permute-start(bf16[64,768]{1,0:T(8,128)(2,1)S(1)} %pass_on.1.refs_2_), channel_id=1, source_target_pairs={{0,8},{8,0},{16,24},{24,16},{1,9},{9,1},{17,25},{25,17},{2,10},{10... | collective-permute-start | bytes 294920 | tf_op jit(solution)/shard_map/ppermute | solution.py:17
  18.6 3.1 %collective-permute-start.8 = (bf16[576,768]{1,0:T(8,128)(2,1)S(1)}, bf16[576,768]{1,0:T(8,128)(2,1)S(1)}, u32[]{:S(2)}, u32[]{:S(2)}) collective-permute-start(bf16[576,768]{1,0:T(8,128)(2,1)S(1)} %get-tuple-element.16.refs_2_), channel_id=1, source_target_pairs={{0,1},{1,0},{2,3},{3,2},{4,5},{5,4},{6,7},{7,6},{8,9},{9,8},{10,11... | collective-permute-start | bytes 2654216 | tf_op jit(solution)/shard_map/ppermute | solution.py:17
  18.7 12.6 %collective-permute-start.7 = (bf16[256,768]{1,0:T(8,128)(2,1)S(1)}, bf16[256,768]{1,0:T(8,128)(2,1)S(1)}, u32[]{:S(2)}, u32[]{:S(2)}) collective-permute-start(bf16[256,768]{1,0:T(8,128)(2,1)S(1)} %get-tuple-element.15.refs_1_.refs_2_), channel_id=1, source_target_pairs={{0,4},{1,5},{2,6},{3,7},{4,0},{5,1},{6,2},{7,3},{8,12},{9,13},{10,... | collective-permute-start | bytes 1179656 | tf_op jit(solution)/shard_map/ppermute | solution.py:17
  20.2 11.2 %collective-permute-start.6 = (bf16[256,768]{1,0:T(8,128)(2,1)S(1)}, bf16[256,768]{1,0:T(8,128)(2,1)S(1)}, u32[]{:S(2)}, u32[]{:S(2)}) collective-permute-start(bf16[256,768]{1,0:T(8,128)(2,1)S(1)} %get-tuple-element.15.refs_1_.refs_2_), channel_id=1, source_target_pairs={{0,2},{1,3},{2,0},{3,1},{4,6},{5,7},{6,4},{7,5},{8,10},{9,11},{10,... | collective-permute-start | bytes 1179656 | tf_op jit(solution)/shard_map/ppermute | solution.py:17
  22.4 6.8 %collective-permute-start.9 = (f32[64,768]{1,0:T(8,128)S(1)}, f32[64,768]{1,0:T(8,128)S(1)}, u32[]{:S(2)}, u32[]{:S(2)}) collective-permute-start(f32[64,768]{1,0:T(8,128)S(1)} %text_part.5), channel_id=1, source_target_pairs={{0,8},{8,0},{16,24},{24,16},{1,9},{9,1},{17,25},{25,17},{2,10},{10... | collective-permute-start | bytes 589832 | tf_op jit(solution)/shard_map/ppermute | solution.py:17
  29.2 10.1 %collective-permute-start.14 = (f32[64,768]{1,0:T(8,128)S(1)}, f32[64,768]{1,0:T(8,128)S(1)}, u32[]{:S(2)}, u32[]{:S(2)}) collective-permute-start(f32[64,768]{1,0:T(8,128)S(1)} %get-tuple-element.22), channel_id=1, source_target_pairs={{0,8},{8,0},{16,24},{24,16},{1,9},{9,1},{17,25},{25,17},{2,10},{10... | collective-permute-start | bytes 589832 | tf_op jit(solution)/shard_map/ppermute | solution.py:17
  30.8 10.6 %collective-permute-start.13 = (f32[64,768]{1,0:T(8,128)S(1)}, f32[64,768]{1,0:T(8,128)S(1)}, u32[]{:S(2)}, u32[]{:S(2)}) collective-permute-start(f32[64,768]{1,0:T(8,128)S(1)} %get-tuple-element.19.refs_5_.refs_2_), channel_id=1, source_target_pairs={{0,16},{8,24},{16,0},{24,8},{1,17},{9,25},{17,1},{25,9},{2,18},{10... | collective-permute-start | bytes 589832 | tf_op jit(solution)/shard_map/ppermute | solution.py:17
  31.4 6.2 %collective-permute-start.10 = (bf16[128,768]{1,0:T(8,128)(2,1)S(1)}, bf16[128,768]{1,0:T(8,128)(2,1)S(1)}, u32[]{:S(2)}, u32[]{:S(2)}) collective-permute-start(bf16[128,768]{1,0:T(8,128)(2,1)S(1)} %get-tuple-element.20), channel_id=1, source_target_pairs={{0,2},{1,3},{2,0},{3,1},{4,6},{5,7},{6,4},{7,5},{8,10},{9,11},{10,... | collective-permute-start | bytes 589832 | tf_op jit(solution)/shard_map/ppermute | solution.py:17
  32.5 5.7 %collective-permute-start.11 = (bf16[128,768]{1,0:T(8,128)(2,1)S(1)}, bf16[128,768]{1,0:T(8,128)(2,1)S(1)}, u32[]{:S(2)}, u32[]{:S(2)}) collective-permute-start(bf16[128,768]{1,0:T(8,128)(2,1)S(1)} %get-tuple-element.21), channel_id=1, source_target_pairs={{0,4},{1,5},{2,6},{3,7},{4,0},{5,1},{6,2},{7,3},{8,12},{9,13},{10,... | collective-permute-start | bytes 589832 | tf_op jit(solution)/shard_map/ppermute | solution.py:17
  38.7 2.8 %collective-permute-start.12 = (f32[128,768]{1,0:T(8,128)S(1)}, f32[128,768]{1,0:T(8,128)S(1)}, u32[]{:S(2)}, u32[]{:S(2)}) collective-permute-start(f32[128,768]{1,0:T(8,128)S(1)} %speech_part.7), channel_id=1, source_target_pairs={{0,1},{1,0},{2,3},{3,2},{4,5},{5,4},{6,7},{7,6},{8,9},{9,8},{10,11... | collective-permute-start | bytes 1179656 | tf_op jit(solution)/shard_map/ppermute | solution.py:17
  41.4 0.9 %copy-start = (bf16[128,768]{1,0:T(8,128)(2,1)S(1)}, bf16[128,768]{1,0:T(8,128)(2,1)}, u32[]{:S(2)}) copy-start(bf16[128,768]{1,0:T(8,128)(2,1)} %refs_0_.3) | copy-start | bytes 589828
  41.4 1.0 %copy-start.1 = (bf16[64,768]{1,0:T(8,128)(2,1)S(1)}, bf16[64,768]{1,0:T(8,128)(2,1)}, u32[]{:S(2)}) copy-start(bf16[64,768]{1,0:T(8,128)(2,1)} %refs_3_.1) | copy-start | bytes 294916

commit v7 on v6

--- a/solution.py
+++ b/solution.py
@@ -200,18 +200,21 @@
         return jax.ShapeDtypeStruct(shape, jnp.float32)
 
     arguments = [audio_vectors, sentence_vectors, label]
-    speech_own, text_own = pl.pallas_call(
+    speech_own, text_own, audio, sentence = pl.pallas_call(
         prepare_body,
-        out_shape=[bf16(rows + MARK_ROWS, width), bf16(own_text, width)],
+        out_shape=[
+            bf16(rows + MARK_ROWS, width),
+            bf16(own_text, width),
+            bf16(rows, width),
+            bf16(own_text, width),
+        ],
         in_specs=[pl.BlockSpec(memory_space=pltpu.HBM)] * 3,
-        out_specs=[pl.BlockSpec(memory_space=pltpu.VMEM)] * 2,
-        scratch_shapes=[
-            *[pltpu.VMEM(v.shape, v.dtype) for v in arguments],
-            pltpu.SemaphoreType.DMA((3,)),
-        ],
+        out_specs=[pl.BlockSpec(memory_space=pltpu.VMEM)] * 4,
+        scratch_shapes=[pltpu.VMEM((1, rows), jnp.int32), pltpu.SemaphoreType.DMA((3,))],
         compiler_params=pltpu.CompilerParams(vmem_limit_bytes=8 << 20),
         name="unit_rows",
     )(*[pltpu.with_memory_space_constraint(v, pltpu.HBM) for v in arguments])
+
     def passed_on(block):
         return call(join_body, bf16(own_text, width), [block], (scalars,), 1 << 29, name="pass_on")
 
@@ -251,12 +254,7 @@
         return call(body, outs, operands, (), work, temporary, "text_part")
 
     half = text_part([f32(column, width)], [speech], [])
-    parts = [None] * groups
-    first = [groups - 1]
-    parts[groups - 1] = text_part([f32(own_text, width)], [other], half, first)[0]
-    rest = list(range(groups - 1))
-    for k, part in zip(rest, text_part([f32(own_text, width)] * len(rest), [other], half, rest)):
-        parts[k] = part
+    parts = list(text_part([f32(own_text, width)] * groups, [other], half))
 
     text_back = [parts[0]]
     for bit in [1 << i for i in range(groups.bit_length() - 1)]:
@@ -286,11 +284,11 @@
         away = speech_part(other[0 : rows + MARK_ROWS], [away], [3], text_far)
         home = speech_part(speech_own, [home], [3], text_far)
     back = exchanged(away, "member", 1)
-    text_back = call(sum_body, f32(own_text, width), text_back[::-1], (home,), EARLY, name="text_sum")
+    text_back = call(sum_body, f32(own_text, width), text_back[::-1], (), EARLY, name="text_sum")
     speech_grad, text_grad = call(
         finish_body,
         [f32(rows, width), f32(own_text, width)],
-        [audio_vectors, home, back, sentence_vectors, text_back],
+        [audio, home, back, sentence, text_back],
         name="finish",
     )
     return (speech_grad, text_grad)

time: 43.6 us -> 42.3 us (0.970)
  local copies, waits for them, and re-layouts: 1.03 us -> 0.09 us
  Pallas kernels: 7.61 us -> 7.04 us
    unnamed x4 -> x0, local copies, waits for them, and re-layouts: 0.94 us -> none
    pallas_call x13 -> x12, Pallas kernels: 6.43 us -> 5.86 us  [call(): pl.pallas_call(whole, out_shape=out_shape, in_specs=specs, out_specs=jax....]
  transfers between devices with their start and end apart: 15 -> 15, of which waited for: 9 -> 7; matrix products, arithmetic and copies ran while one was open for 0% -> 0% of each run, Pallas kernels for 12% -> 11%
where the time goes in v7:
time: 42.3 us; the launch traced here: 42.1 us
  starting transfers between devices  17.9 us (42%)
  waiting for transfers between devices  15 us (35%)
  Pallas kernels  7.04 us (17%)
  between operations  2.06 us (5%)
    ppermute x15, starting transfers between devices, exchanged(): return lax.ppermute(value, axis, [(i, i ^ mask) for i in range(size)])  17.9 us
    ppermute x15, waiting for transfers between devices, exchanged(): return lax.ppermute(value, axis, [(i, i ^ mask) for i in range(size)])  15 us
    pallas_call x12, Pallas kernels, call(): pl.pallas_call(whole, out_shape=out_shape, in_specs=specs, out_specs=jax....  5.86 us
    pallas_call x1, Pallas kernels, shards(): pl.pallas_call(prepare_body, out_shape=[bf16(rows + MARK_ROWS, width), bf...  1.18 us
  transfers between devices with their start and end apart: 15, of which 7 were waited for; matrix products, arithmetic and copies ran while one was open for 0% of the time, Pallas kernels for 11%

profile of v7, /device:TPU:0, one launch (start us, length us, event | category | flops | bytes accessed | tf_op | source)
XLA Modules:
  0.0 42.1 jit_solution(384716430335845609)
XLA Ops:
  0.6 1.2 %unit_rows.1 = (bf16[144,768]{1,0:T(8,128)(2,1)S(1)}, bf16[64,768]{1,0:T(8,128)(2,1)S(1)}, bf16[128,768]{1,0:T(8,128)(2,1)S(1)}, bf16[64,768]{1,0:T(8,128)(2,1)S(1)}) custom-call(bf16[128,768]{1,0:T(8,128)(2,1)} %refs_0_.1, bf16[64,768]{1,0:T(8,128)(2,1)} %refs_1_.1, s32[1,128]{1,0:T(1,128)} %bitcast.3), custom_call_target="tpu_custom_call" | custom-call | tf_op jit(solution)/shard_map/unit_rows/pallas_call | solution.py:203
  1.8 4.1 %collective-permute-start.1 = (bf16[64,768]{1,0:T(8,128)(2,1)S(1)}, bf16[64,768]{1,0:T(8,128)(2,1)S(1)}, u32[]{:S(2)}, u32[]{:S(2)}) collective-permute-start(bf16[64,768]{1,0:T(8,128)(2,1)S(1)} %get-tuple-element.18.refs_0_), channel_id=1, source_target_pairs={{0,16},{8,24},{16,0},{24,8},{1,17},{9,25},{17,1},{25,9},{2,18},{10... | collective-permute-start | bytes 294920 | tf_op jit(solution)/shard_map/ppermute | solution.py:17
  5.9 1.5 %collective-permute-start.3 = (bf16[144,768]{1,0:T(8,128)(2,1)S(1)}, bf16[144,768]{1,0:T(8,128)(2,1)S(1)}, u32[]{:S(2)}, u32[]{:S(2)}) collective-permute-start(bf16[144,768]{1,0:T(8,128)(2,1)S(1)} %get-tuple-element.17.refs_4_.refs_1_), channel_id=1, source_target_pairs={{0,2},{1,3},{2,0},{3,1},{4,6},{5,7},{6,4},{7,5},{8,10},{9,11},{10,... | collective-permute-start | bytes 663560 | tf_op jit(solution)/shard_map/ppermute | solution.py:17
  7.4 1.5 %collective-permute-start.4 = (bf16[144,768]{1,0:T(8,128)(2,1)S(1)}, bf16[144,768]{1,0:T(8,128)(2,1)S(1)}, u32[]{:S(2)}, u32[]{:S(2)}) collective-permute-start(bf16[144,768]{1,0:T(8,128)(2,1)S(1)} %get-tuple-element.17.refs_4_.refs_1_), channel_id=1, source_target_pairs={{0,4},{1,5},{2,6},{3,7},{4,0},{5,1},{6,2},{7,3},{8,12},{9,13},{10,... | collective-permute-start | bytes 663560 | tf_op jit(solution)/shard_map/ppermute | solution.py:17
  8.9 0.5 %collective-permute-start.5 = (bf16[144,768]{1,0:T(8,128)(2,1)S(1)}, bf16[144,768]{1,0:T(8,128)(2,1)S(1)}, u32[]{:S(2)}, u32[]{:S(2)}) collective-permute-start(bf16[144,768]{1,0:T(8,128)(2,1)S(1)} %get-tuple-element.17.refs_4_.refs_1_), channel_id=1, source_target_pairs={{0,6},{1,7},{2,4},{3,5},{4,2},{5,3},{6,0},{7,1},{8,14},{9,15},{10,... | collective-permute-start | bytes 663560 | tf_op jit(solution)/shard_map/ppermute | solution.py:17
  9.4 1.6 %collective-permute-start = (bf16[64,768]{1,0:T(8,128)(2,1)S(1)}, bf16[64,768]{1,0:T(8,128)(2,1)S(1)}, u32[]{:S(2)}, u32[]{:S(2)}) collective-permute-start(bf16[64,768]{1,0:T(8,128)(2,1)S(1)} %get-tuple-element.18.refs_0_), channel_id=1, source_target_pairs={{0,8},{8,0},{16,24},{24,16},{1,9},{9,1},{17,25},{25,17},{2,10},{10... | collective-permute-start | bytes 294920 | tf_op jit(solution)/shard_map/ppermute | solution.py:17
  12.3 0.1 concatenate.6.refs_1_.refs_0_
  12.4 0.5 %collective-permute-start.2 = (bf16[64,768]{1,0:T(8,128)(2,1)S(1)}, bf16[64,768]{1,0:T(8,128)(2,1)S(1)}, u32[]{:S(2)}, u32[]{:S(2)}) collective-permute-start(bf16[64,768]{1,0:T(8,128)(2,1)S(1)} %pass_on.1.refs_2_), channel_id=1, source_target_pairs={{0,8},{8,0},{16,24},{24,16},{1,9},{9,1},{17,25},{25,17},{2,10},{10... | collective-permute-start | bytes 294920 | tf_op jit(solution)/shard_map/ppermute | solution.py:17
  12.9 1.8 %collective-permute-done.refs_1_ = bf16[64,768]{1,0:T(8,128)(2,1)S(1)} collective-permute-done((bf16[64,768]{1,0:T(8,128)(2,1)S(1)}, bf16[64,768]{1,0:T(8,128)(2,1)S(1)}, u32[]{:S(2)}, u32[]{:S(2)}) %collective-permute-start) | collective-permute-done | bytes 98336 | tf_op jit(solution)/shard_map/ppermute | solution.py:17
  14.7 2.4 %collective-permute-done.2.refs_3_ = bf16[64,768]{1,0:T(8,128)(2,1)S(1)} collective-permute-done((bf16[64,768]{1,0:T(8,128)(2,1)S(1)}, bf16[64,768]{1,0:T(8,128)(2,1)S(1)}, u32[]{:S(2)}, u32[]{:S(2)}) %collective-permute-start.2) | collective-permute-done | bytes 98336 | tf_op jit(solution)/shard_map/ppermute | solution.py:17
  17.1 1.7 %collective-permute-done.4.refs_6_ = bf16[144,768]{1,0:T(8,128)(2,1)S(1)} collective-permute-done((bf16[144,768]{1,0:T(8,128)(2,1)S(1)}, bf16[144,768]{1,0:T(8,128)(2,1)S(1)}, u32[]{:S(2)}, u32[]{:S(2)}) %collective-permute-start.4) | collective-permute-done | bytes 221216 | tf_op jit(solution)/shard_map/ppermute | solution.py:17
  18.8 0.1 join_rows.1
  18.9 0.1 collective-permute-start.8
  18.9 1.3 %collective-permute-start.6 = (bf16[256,768]{1,0:T(8,128)(2,1)S(1)}, bf16[256,768]{1,0:T(8,128)(2,1)S(1)}, u32[]{:S(2)}, u32[]{:S(2)}) collective-permute-start(bf16[256,768]{1,0:T(8,128)(2,1)S(1)} %get-tuple-element.19.refs_1_.refs_2_), channel_id=1, source_target_pairs={{0,2},{1,3},{2,0},{3,1},{4,6},{5,7},{6,4},{7,5},{8,10},{9,11},{10,... | collective-permute-start | bytes 1179656 | tf_op jit(solution)/shard_map/ppermute | solution.py:17
  20.2 0.8 %collective-permute-start.7 = (bf16[256,768]{1,0:T(8,128)(2,1)S(1)}, bf16[256,768]{1,0:T(8,128)(2,1)S(1)}, u32[]{:S(2)}, u32[]{:S(2)}) collective-permute-start(bf16[256,768]{1,0:T(8,128)(2,1)S(1)} %get-tuple-element.19.refs_1_.refs_2_), channel_id=1, source_target_pairs={{0,4},{1,5},{2,6},{3,7},{4,0},{5,1},{6,2},{7,3},{8,12},{9,13},{10,... | collective-permute-start | bytes 1179656 | tf_op jit(solution)/shard_map/ppermute | solution.py:17
  21.1 0.8 %text_part.2.refs_2_ = f32[256,768]{1,0:T(8,128)S(1)} custom-call(f32[2,128]{1,0:T(2,128)S(1)} %concatenate.6.refs_1_.refs_0_, bf16[256,768]{1,0:T(8,128)(2,1)S(1)} %get-tuple-element.19.refs_1_.refs_2_, bf16[576,768]{1,0:T(8,128)(2,1)S(1)} %get-tuple-element.20.refs_2_), custom_call_target="tpu_custom_call" | custom-call | flops 402653184 | bytes 2065408 | tf_op jit(solution)/shard_map/text_part/pallas_call | solution.py:33
  21.8 0.8 %text_part.3 = (f32[64,768]{1,0:T(8,128)S(1)}, f32[64,768]{1,0:T(8,128)S(1)}, f32[64,768]{1,0:T(8,128)S(1)}, f32[64,768]{1,0:T(8,128)S(1)}) custom-call(f32[2,128]{1,0:T(2,128)S(1)} %concatenate.6.refs_1_.refs_0_, bf16[256,768]{1,0:T(8,128)(2,1)S(1)} %get-tuple-element.19.refs_1_.refs_2_, f32[256,768]{1,0:T(8,128)S(1)} %text_part.2.refs_2_, ...), custom_call_target="tpu_custom_call" | custom-call | flops 402653184 | bytes 2851840 | tf_op jit(solution)/shard_map/text_part/pallas_call | solution.py:33
  22.6 1.6 %collective-permute-start.9 = (f32[64,768]{1,0:T(8,128)S(1)}, f32[64,768]{1,0:T(8,128)S(1)}, u32[]{:S(2)}, u32[]{:S(2)}) collective-permute-start(f32[64,768]{1,0:T(8,128)S(1)} %get-tuple-element.22), channel_id=1, source_target_pairs={{0,8},{8,0},{16,24},{24,16},{1,9},{9,1},{17,25},{25,17},{2,10},{10... | collective-permute-start | bytes 589832 | tf_op jit(solution)/shard_map/ppermute | solution.py:17
  24.3 5.1 %collective-permute-done.9.refs_1_ = f32[64,768]{1,0:T(8,128)S(1)} collective-permute-done((f32[64,768]{1,0:T(8,128)S(1)}, f32[64,768]{1,0:T(8,128)S(1)}, u32[]{:S(2)}, u32[]{:S(2)}) %collective-permute-start.9) | collective-permute-done | bytes 196640 | tf_op jit(solution)/shard_map/ppermute | solution.py:17
  29.4 0.4 %collective-permute-start.13 = (f32[64,768]{1,0:T(8,128)S(1)}, f32[64,768]{1,0:T(8,128)S(1)}, u32[]{:S(2)}, u32[]{:S(2)}) collective-permute-start(f32[64,768]{1,0:T(8,128)S(1)} %get-tuple-element.24.refs_5_.refs_2_), channel_id=1, source_target_pairs={{0,16},{8,24},{16,0},{24,8},{1,17},{9,25},{17,1},{25,9},{2,18},{10... | collective-permute-start | bytes 589832 | tf_op jit(solution)/shard_map/ppermute | solution.py:17
  29.9 1.7 %collective-permute-start.14 = (f32[64,768]{1,0:T(8,128)S(1)}, f32[64,768]{1,0:T(8,128)S(1)}, u32[]{:S(2)}, u32[]{:S(2)}) collective-permute-start(f32[64,768]{1,0:T(8,128)S(1)} %get-tuple-element.28), channel_id=1, source_target_pairs={{0,8},{8,0},{16,24},{24,16},{1,9},{9,1},{17,25},{25,17},{2,10},{10... | collective-permute-start | bytes 589832 | tf_op jit(solution)/shard_map/ppermute | solution.py:17
  31.6 1.5 %collective-permute-start.10 = (bf16[128,768]{1,0:T(8,128)(2,1)S(1)}, bf16[128,768]{1,0:T(8,128)(2,1)S(1)}, u32[]{:S(2)}, u32[]{:S(2)}) collective-permute-start(bf16[128,768]{1,0:T(8,128)(2,1)S(1)} %get-tuple-element.25), channel_id=1, source_target_pairs={{0,2},{1,3},{2,0},{3,1},{4,6},{5,7},{6,4},{7,5},{8,10},{9,11},{10,... | collective-permute-start | bytes 589832 | tf_op jit(solution)/shard_map/ppermute | solution.py:17
  33.0 0.8 %collective-permute-start.11 = (bf16[128,768]{1,0:T(8,128)(2,1)S(1)}, bf16[128,768]{1,0:T(8,128)(2,1)S(1)}, u32[]{:S(2)}, u32[]{:S(2)}) collective-permute-start(bf16[128,768]{1,0:T(8,128)(2,1)S(1)} %get-tuple-element.26), channel_id=1, source_target_pairs={{0,4},{1,5},{2,6},{3,7},{4,0},{5,1},{6,2},{7,3},{8,12},{9,13},{10,... | collective-permute-start | bytes 589832 | tf_op jit(solution)/shard_map/ppermute | solution.py:17
  33.8 1.0 %speech_part.4.refs_2_ = f32[128,768]{1,0:T(8,128)S(1)} custom-call(f32[2,128]{1,0:T(2,128)S(1)} %concatenate.6.refs_1_.refs_0_, bf16[144,768]{1,0:T(8,128)(2,1)S(1)} %get-tuple-element.17.refs_4_.refs_1_, bf16[256,768]{1,0:T(8,128)(2,1)S(1)} %get-tuple-element.19.refs_1_.refs_2_, bf16[256,768]{1,0:T(8,128)(2,1)S(1)} %collective-permute-done.6.refs_3_.refs_1_, ...), custom_call_target="tpu_custom_call" | custom-call | flops 3019898880 | bytes 1795072 | tf_op jit(solution)/shard_map/speech_part/pallas_call | solution.py:33
  34.9 1.0 %speech_part.6.refs_2_ = f32[128,768]{1,0:T(8,128)S(1)} custom-call(f32[2,128]{1,0:T(2,128)S(1)} %concatenate.6.refs_1_.refs_0_, bf16[144,768]{1,0:T(8,128)(2,1)S(1)} %slice.5.refs_1_, bf16[256,768]{1,0:T(8,128)(2,1)S(1)} %get-tuple-element.19.refs_1_.refs_2_, bf16[256,768]{1,0:T(8,128)(2,1)S(1)} %collective-permute-done.6.refs_3_.refs_1_, ...), custom_call_target="tpu_custom_call" | custom-call | flops 3019898880 | bytes 1795072 | tf_op jit(solution)/shard_map/speech_part/pallas_call | solution.py:33
  35.9 1.8 %collective-permute-done.10.refs_3_ = bf16[128,768]{1,0:T(8,128)(2,1)S(1)} collective-permute-done((bf16[128,768]{1,0:T(8,128)(2,1)S(1)}, bf16[128,768]{1,0:T(8,128)(2,1)S(1)}, u32[]{:S(2)}, u32[]{:S(2)}) %collective-permute-start.10) | collective-permute-done | bytes 196640 | tf_op jit(solution)/shard_map/ppermute | solution.py:17
  37.7 1.0 %collective-permute-done.11.refs_4_ = bf16[128,768]{1,0:T(8,128)(2,1)S(1)} collective-permute-done((bf16[128,768]{1,0:T(8,128)(2,1)S(1)}, bf16[128,768]{1,0:T(8,128)(2,1)S(1)}, u32[]{:S(2)}, u32[]{:S(2)}) %collective-permute-start.11) | collective-permute-done | bytes 196640 | tf_op jit(solution)/shard_map/ppermute | solution.py:17
  38.7 0.5 %speech_part.7 = f32[128,768]{1,0:T(8,128)S(1)} custom-call(f32[2,128]{1,0:T(2,128)S(1)} %concatenate.6.refs_1_.refs_0_, bf16[144,768]{1,0:T(8,128)(2,1)S(1)} %slice.5.refs_1_, f32[128,768]{1,0:T(8,128)S(1)} %speech_part.6.refs_2_, bf16[128,768]{1,0:T(8,128)(2,1)S(1)} %collective-permute-done.10.refs_3_, bf16[128,768]{1,0:T(8,128)(2,1)S(1)} %collective-permute-done.11.refs_4_), custom_call_target="tpu_custom_call" | custom-call | flops 1006632960 | bytes 1401856 | tf_op jit(solution)/shard_map/speech_part/pallas_call | solution.py:33
  39.2 0.1 collective-permute-start.12
  39.3 1.2 %collective-permute-done.13.refs_0_ = f32[64,768]{1,0:T(8,128)S(1)} collective-permute-done((f32[64,768]{1,0:T(8,128)S(1)}, f32[64,768]{1,0:T(8,128)S(1)}, u32[]{:S(2)}, u32[]{:S(2)}) %collective-permute-start.13) | collective-permute-done | bytes 196640 | tf_op jit(solution)/shard_map/ppermute | solution.py:17
  40.5 0.5 %speech_part.5.refs_1_ = f32[128,768]{1,0:T(8,128)S(1)} custom-call(f32[2,128]{1,0:T(2,128)S(1)} %concatenate.6.refs_1_.refs_0_, bf16[144,768]{1,0:T(8,128)(2,1)S(1)} %get-tuple-element.17.refs_4_.refs_1_, f32[128,768]{1,0:T(8,128)S(1)} %speech_part.4.refs_2_, bf16[128,768]{1,0:T(8,128)(2,1)S(1)} %collective-permute-done.10.refs_3_, ...), custom_call_target="tpu_custom_call" | custom-call | flops 1006632960 | bytes 1401856 | tf_op jit(solution)/shard_map/speech_part/pallas_call | solution.py:33
  41.0 1.0 %finish.1 = (f32[128,768]{1,0:T(8,128)}, f32[64,768]{1,0:T(8,128)}) custom-call(bf16[128,768]{1,0:T(8,128)(2,1)S(1)} %get-tuple-element.16.refs_0_, f32[128,768]{1,0:T(8,128)S(1)} %speech_part.5.refs_1_, f32[128,768]{1,0:T(8,128)S(1)} %collective-permute-done.12.refs_2_, bf16[64,768]{1,0:T(8,128)(2,1)S(1)} %get-tuple-element.27.refs_3_, ...), custom_call_target="tpu_custom_call" | custom-call | bytes 1867776 | tf_op jit(solution)/shard_map/finish/pallas_call | solution.py:33
  (14 shorter events, 0.1 us)
Async XLA Ops:
  1.8 10.5 %collective-permute-start.1 = (bf16[64,768]{1,0:T(8,128)(2,1)S(1)}, bf16[64,768]{1,0:T(8,128)(2,1)S(1)}, u32[]{:S(2)}, u32[]{:S(2)}) collective-permute-start(bf16[64,768]{1,0:T(8,128)(2,1)S(1)} %get-tuple-element.18.refs_0_), channel_id=1, source_target_pairs={{0,16},{8,24},{16,0},{24,8},{1,17},{9,25},{17,1},{25,9},{2,18},{10... | collective-permute-start | bytes 294920 | tf_op jit(solution)/shard_map/ppermute | solution.py:17
  5.9 11.1 %collective-permute-start.3 = (bf16[144,768]{1,0:T(8,128)(2,1)S(1)}, bf16[144,768]{1,0:T(8,128)(2,1)S(1)}, u32[]{:S(2)}, u32[]{:S(2)}) collective-permute-start(bf16[144,768]{1,0:T(8,128)(2,1)S(1)} %get-tuple-element.17.refs_4_.refs_1_), channel_id=1, source_target_pairs={{0,2},{1,3},{2,0},{3,1},{4,6},{5,7},{6,4},{7,5},{8,10},{9,11},{10,... | collective-permute-start | bytes 663560 | tf_op jit(solution)/shard_map/ppermute | solution.py:17
  7.4 11.3 %collective-permute-start.4 = (bf16[144,768]{1,0:T(8,128)(2,1)S(1)}, bf16[144,768]{1,0:T(8,128)(2,1)S(1)}, u32[]{:S(2)}, u32[]{:S(2)}) collective-permute-start(bf16[144,768]{1,0:T(8,128)(2,1)S(1)} %get-tuple-element.17.refs_4_.refs_1_), channel_id=1, source_target_pairs={{0,4},{1,5},{2,6},{3,7},{4,0},{5,1},{6,2},{7,3},{8,12},{9,13},{10,... | collective-permute-start | bytes 663560 | tf_op jit(solution)/shard_map/ppermute | solution.py:17
  8.9 9.8 %collective-permute-start.5 = (bf16[144,768]{1,0:T(8,128)(2,1)S(1)}, bf16[144,768]{1,0:T(8,128)(2,1)S(1)}, u32[]{:S(2)}, u32[]{:S(2)}) collective-permute-start(bf16[144,768]{1,0:T(8,128)(2,1)S(1)} %get-tuple-element.17.refs_4_.refs_1_), channel_id=1, source_target_pairs={{0,6},{1,7},{2,4},{3,5},{4,2},{5,3},{6,0},{7,1},{8,14},{9,15},{10,... | collective-permute-start | bytes 663560 | tf_op jit(solution)/shard_map/ppermute | solution.py:17
  9.4 5.3 %collective-permute-start = (bf16[64,768]{1,0:T(8,128)(2,1)S(1)}, bf16[64,768]{1,0:T(8,128)(2,1)S(1)}, u32[]{:S(2)}, u32[]{:S(2)}) collective-permute-start(bf16[64,768]{1,0:T(8,128)(2,1)S(1)} %get-tuple-element.18.refs_0_), channel_id=1, source_target_pairs={{0,8},{8,0},{16,24},{24,16},{1,9},{9,1},{17,25},{25,17},{2,10},{10... | collective-permute-start | bytes 294920 | tf_op jit(solution)/shard_map/ppermute | solution.py:17
  12.4 4.7 %collective-permute-start.2 = (bf16[64,768]{1,0:T(8,128)(2,1)S(1)}, bf16[64,768]{1,0:T(8,128)(2,1)S(1)}, u32[]{:S(2)}, u32[]{:S(2)}) collective-permute-start(bf16[64,768]{1,0:T(8,128)(2,1)S(1)} %pass_on.1.refs_2_), channel_id=1, source_target_pairs={{0,8},{8,0},{16,24},{24,16},{1,9},{9,1},{17,25},{25,17},{2,10},{10... | collective-permute-start | bytes 294920 | tf_op jit(solution)/shard_map/ppermute | solution.py:17
  18.9 3.0 %collective-permute-start.8 = (bf16[576,768]{1,0:T(8,128)(2,1)S(1)}, bf16[576,768]{1,0:T(8,128)(2,1)S(1)}, u32[]{:S(2)}, u32[]{:S(2)}) collective-permute-start(bf16[576,768]{1,0:T(8,128)(2,1)S(1)} %get-tuple-element.20.refs_2_), channel_id=1, source_target_pairs={{0,1},{1,0},{2,3},{3,2},{4,5},{5,4},{6,7},{7,6},{8,9},{9,8},{10,11... | collective-permute-start | bytes 2654216 | tf_op jit(solution)/shard_map/ppermute | solution.py:17
  18.9 12.6 %collective-permute-start.6 = (bf16[256,768]{1,0:T(8,128)(2,1)S(1)}, bf16[256,768]{1,0:T(8,128)(2,1)S(1)}, u32[]{:S(2)}, u32[]{:S(2)}) collective-permute-start(bf16[256,768]{1,0:T(8,128)(2,1)S(1)} %get-tuple-element.19.refs_1_.refs_2_), channel_id=1, source_target_pairs={{0,2},{1,3},{2,0},{3,1},{4,6},{5,7},{6,4},{7,5},{8,10},{9,11},{10,... | collective-permute-start | bytes 1179656 | tf_op jit(solution)/shard_map/ppermute | solution.py:17
  20.2 11.3 %collective-permute-start.7 = (bf16[256,768]{1,0:T(8,128)(2,1)S(1)}, bf16[256,768]{1,0:T(8,128)(2,1)S(1)}, u32[]{:S(2)}, u32[]{:S(2)}) collective-permute-start(bf16[256,768]{1,0:T(8,128)(2,1)S(1)} %get-tuple-element.19.refs_1_.refs_2_), channel_id=1, source_target_pairs={{0,4},{1,5},{2,6},{3,7},{4,0},{5,1},{6,2},{7,3},{8,12},{9,13},{10,... | collective-permute-start | bytes 1179656 | tf_op jit(solution)/shard_map/ppermute | solution.py:17
  22.6 6.8 %collective-permute-start.9 = (f32[64,768]{1,0:T(8,128)S(1)}, f32[64,768]{1,0:T(8,128)S(1)}, u32[]{:S(2)}, u32[]{:S(2)}) collective-permute-start(f32[64,768]{1,0:T(8,128)S(1)} %get-tuple-element.22), channel_id=1, source_target_pairs={{0,8},{8,0},{16,24},{24,16},{1,9},{9,1},{17,25},{25,17},{2,10},{10... | collective-permute-start | bytes 589832 | tf_op jit(solution)/shard_map/ppermute | solution.py:17
  29.4 11.0 %collective-permute-start.13 = (f32[64,768]{1,0:T(8,128)S(1)}, f32[64,768]{1,0:T(8,128)S(1)}, u32[]{:S(2)}, u32[]{:S(2)}) collective-permute-start(f32[64,768]{1,0:T(8,128)S(1)} %get-tuple-element.24.refs_5_.refs_2_), channel_id=1, source_target_pairs={{0,16},{8,24},{16,0},{24,8},{1,17},{9,25},{17,1},{25,9},{2,18},{10... | collective-permute-start | bytes 589832 | tf_op jit(solution)/shard_map/ppermute | solution.py:17
  29.9 10.6 %collective-permute-start.14 = (f32[64,768]{1,0:T(8,128)S(1)}, f32[64,768]{1,0:T(8,128)S(1)}, u32[]{:S(2)}, u32[]{:S(2)}) collective-permute-start(f32[64,768]{1,0:T(8,128)S(1)} %get-tuple-element.28), channel_id=1, source_target_pairs={{0,8},{8,0},{16,24},{24,16},{1,9},{9,1},{17,25},{25,17},{2,10},{10... | collective-permute-start | bytes 589832 | tf_op jit(solution)/shard_map/ppermute | solution.py:17
  31.6 6.1 %collective-permute-start.10 = (bf16[128,768]{1,0:T(8,128)(2,1)S(1)}, bf16[128,768]{1,0:T(8,128)(2,1)S(1)}, u32[]{:S(2)}, u32[]{:S(2)}) collective-permute-start(bf16[128,768]{1,0:T(8,128)(2,1)S(1)} %get-tuple-element.25), channel_id=1, source_target_pairs={{0,2},{1,3},{2,0},{3,1},{4,6},{5,7},{6,4},{7,5},{8,10},{9,11},{10,... | collective-permute-start | bytes 589832 | tf_op jit(solution)/shard_map/ppermute | solution.py:17
  33.0 5.7 %collective-permute-start.11 = (bf16[128,768]{1,0:T(8,128)(2,1)S(1)}, bf16[128,768]{1,0:T(8,128)(2,1)S(1)}, u32[]{:S(2)}, u32[]{:S(2)}) collective-permute-start(bf16[128,768]{1,0:T(8,128)(2,1)S(1)} %get-tuple-element.26), channel_id=1, source_target_pairs={{0,4},{1,5},{2,6},{3,7},{4,0},{5,1},{6,2},{7,3},{8,12},{9,13},{10,... | collective-permute-start | bytes 589832 | tf_op jit(solution)/shard_map/ppermute | solution.py:17
  39.2 1.8 %collective-permute-start.12 = (f32[128,768]{1,0:T(8,128)S(1)}, f32[128,768]{1,0:T(8,128)S(1)}, u32[]{:S(2)}, u32[]{:S(2)}) collective-permute-start(f32[128,768]{1,0:T(8,128)S(1)} %speech_part.7), channel_id=1, source_target_pairs={{0,1},{1,0},{2,3},{3,2},{4,5},{5,4},{6,7},{7,6},{8,9},{9,8},{10,11... | collective-permute-start | bytes 1179656 | tf_op jit(solution)/shard_map/ppermute | solution.py:17

commit v8 on v7

--- a/solution.py
+++ b/solution.py
@@ -216,7 +216,7 @@
     )(*[pltpu.with_memory_space_constraint(v, pltpu.HBM) for v in arguments])
 
     def passed_on(block):
-        return call(join_body, bf16(own_text, width), [block], (scalars,), 1 << 29, name="pass_on")
+        return call(join_body, bf16(own_text, width), [block], (scalars,), 1 << 20, name="pass_on")
 
     text_blocks = [text_own] + [None] * (groups - 1)
     for k in [1 << i for i in reversed(range(groups.bit_length() - 1))]:

time: 42.3 us -> 43.8 us (1.035)
  starting transfers between devices: 17.9 us -> 22.7 us
  waiting for transfers between devices: 15 us -> 11.8 us
    ppermute x15, starting transfers between devices: 17.9 us -> 22.7 us  [exchanged(): return lax.ppermute(value, axis, [(i, i ^ mask) for i in range(size)])]
    ppermute x15, waiting for transfers between devices: 15 us -> 11.8 us  [exchanged(): return lax.ppermute(value, axis, [(i, i ^ mask) for i in range(size)])]
  transfers between devices with their start and end apart: 15 -> 15, of which waited for: 7 -> 9; matrix products, arithmetic and copies ran while one was open for 0% -> 0% of each run, Pallas kernels for 11% -> 11%
where the time goes in v8:
time: 43.8 us; the launch traced here: 43.7 us
  starting transfers between devices  22.7 us (52%)
  waiting for transfers between devices  11.8 us (27%)
  Pallas kernels  7.04 us (16%)
  between operations  2.05 us (5%)
    ppermute x15, starting transfers between devices, exchanged(): return lax.ppermute(value, axis, [(i, i ^ mask) for i in range(size)])  22.7 us
    ppermute x15, waiting for transfers between devices, exchanged(): return lax.ppermute(value, axis, [(i, i ^ mask) for i in range(size)])  11.8 us
    pallas_call x12, Pallas kernels, call(): pl.pallas_call(whole, out_shape=out_shape, in_specs=specs, out_specs=jax....  5.86 us
    pallas_call x1, Pallas kernels, shards(): pl.pallas_call(prepare_body, out_shape=[bf16(rows + MARK_ROWS, width), bf...  1.18 us
  transfers between devices with their start and end apart: 15, of which 9 were waited for; matrix products, arithmetic and copies ran while one was open for 0% of the time, Pallas kernels for 11%

profile of v8, /device:TPU:0, one launch (start us, length us, event | category | flops | bytes accessed | tf_op | source)
XLA Modules:
  0.0 43.7 jit_solution(10799041052627573679)
XLA Ops:
  0.6 1.2 %unit_rows.1 = (bf16[144,768]{1,0:T(8,128)(2,1)S(1)}, bf16[64,768]{1,0:T(8,128)(2,1)S(1)}, bf16[128,768]{1,0:T(8,128)(2,1)S(1)}, bf16[64,768]{1,0:T(8,128)(2,1)S(1)}) custom-call(bf16[128,768]{1,0:T(8,128)(2,1)} %refs_0_.1, bf16[64,768]{1,0:T(8,128)(2,1)} %refs_1_.1, s32[1,128]{1,0:T(1,128)} %bitcast.3), custom_call_target="tpu_custom_call" | custom-call | tf_op jit(solution)/shard_map/unit_rows/pallas_call | solution.py:203
  1.8 3.0 %collective-permute-start.3 = (bf16[144,768]{1,0:T(8,128)(2,1)S(1)}, bf16[144,768]{1,0:T(8,128)(2,1)S(1)}, u32[]{:S(2)}, u32[]{:S(2)}) collective-permute-start(bf16[144,768]{1,0:T(8,128)(2,1)S(1)} %get-tuple-element.17.refs_4_.refs_1_), channel_id=1, source_target_pairs={{0,2},{1,3},{2,0},{3,1},{4,6},{5,7},{6,4},{7,5},{8,10},{9,11},{10,... | collective-permute-start | bytes 663560 | tf_op jit(solution)/shard_map/ppermute | solution.py:17
  4.8 1.5 %collective-permute-start.4 = (bf16[144,768]{1,0:T(8,128)(2,1)S(1)}, bf16[144,768]{1,0:T(8,128)(2,1)S(1)}, u32[]{:S(2)}, u32[]{:S(2)}) collective-permute-start(bf16[144,768]{1,0:T(8,128)(2,1)S(1)} %get-tuple-element.17.refs_4_.refs_1_), channel_id=1, source_target_pairs={{0,4},{1,5},{2,6},{3,7},{4,0},{5,1},{6,2},{7,3},{8,12},{9,13},{10,... | collective-permute-start | bytes 663560 | tf_op jit(solution)/shard_map/ppermute | solution.py:17
  6.4 3.0 %collective-permute-start.1 = (bf16[64,768]{1,0:T(8,128)(2,1)S(1)}, bf16[64,768]{1,0:T(8,128)(2,1)S(1)}, u32[]{:S(2)}, u32[]{:S(2)}) collective-permute-start(bf16[64,768]{1,0:T(8,128)(2,1)S(1)} %get-tuple-element.18.refs_0_), channel_id=1, source_target_pairs={{0,16},{8,24},{16,0},{24,8},{1,17},{9,25},{17,1},{25,9},{2,18},{10... | collective-permute-start | bytes 294920 | tf_op jit(solution)/shard_map/ppermute | solution.py:17
  9.4 1.6 %collective-permute-start = (bf16[64,768]{1,0:T(8,128)(2,1)S(1)}, bf16[64,768]{1,0:T(8,128)(2,1)S(1)}, u32[]{:S(2)}, u32[]{:S(2)}) collective-permute-start(bf16[64,768]{1,0:T(8,128)(2,1)S(1)} %get-tuple-element.18.refs_0_), channel_id=1, source_target_pairs={{0,8},{8,0},{16,24},{24,16},{1,9},{9,1},{17,25},{25,17},{2,10},{10... | collective-permute-start | bytes 294920 | tf_op jit(solution)/shard_map/ppermute | solution.py:17
  12.3 0.2 collective-permute-done.1.refs_0_
  12.5 0.1 concatenate.6.refs_1_.refs_0_
  12.6 1.7 %collective-permute-start.2 = (bf16[64,768]{1,0:T(8,128)(2,1)S(1)}, bf16[64,768]{1,0:T(8,128)(2,1)S(1)}, u32[]{:S(2)}, u32[]{:S(2)}) collective-permute-start(bf16[64,768]{1,0:T(8,128)(2,1)S(1)} %pass_on.1.refs_2_), channel_id=1, source_target_pairs={{0,8},{8,0},{16,24},{24,16},{1,9},{9,1},{17,25},{25,17},{2,10},{10... | collective-permute-start | bytes 294920 | tf_op jit(solution)/shard_map/ppermute | solution.py:17
  14.3 0.3 collective-permute-done.refs_1_
  14.7 2.6 %collective-permute-done.2.refs_3_ = bf16[64,768]{1,0:T(8,128)(2,1)S(1)} collective-permute-done((bf16[64,768]{1,0:T(8,128)(2,1)S(1)}, bf16[64,768]{1,0:T(8,128)(2,1)S(1)}, u32[]{:S(2)}, u32[]{:S(2)}) %collective-permute-start.2) | collective-permute-done | bytes 98336 | tf_op jit(solution)/shard_map/ppermute | solution.py:17
  17.3 0.1 join_rows.1
  17.4 0.1 collective-permute-start.8
  17.5 1.6 %collective-permute-start.6 = (bf16[256,768]{1,0:T(8,128)(2,1)S(1)}, bf16[256,768]{1,0:T(8,128)(2,1)S(1)}, u32[]{:S(2)}, u32[]{:S(2)}) collective-permute-start(bf16[256,768]{1,0:T(8,128)(2,1)S(1)} %get-tuple-element.19.refs_1_.refs_2_), channel_id=1, source_target_pairs={{0,2},{1,3},{2,0},{3,1},{4,6},{5,7},{6,4},{7,5},{8,10},{9,11},{10,... | collective-permute-start | bytes 1179656 | tf_op jit(solution)/shard_map/ppermute | solution.py:17
  19.1 1.5 %collective-permute-start.7 = (bf16[256,768]{1,0:T(8,128)(2,1)S(1)}, bf16[256,768]{1,0:T(8,128)(2,1)S(1)}, u32[]{:S(2)}, u32[]{:S(2)}) collective-permute-start(bf16[256,768]{1,0:T(8,128)(2,1)S(1)} %get-tuple-element.19.refs_1_.refs_2_), channel_id=1, source_target_pairs={{0,4},{1,5},{2,6},{3,7},{4,0},{5,1},{6,2},{7,3},{8,12},{9,13},{10,... | collective-permute-start | bytes 1179656 | tf_op jit(solution)/shard_map/ppermute | solution.py:17
  20.6 0.8 %text_part.2.refs_2_ = f32[256,768]{1,0:T(8,128)S(1)} custom-call(f32[2,128]{1,0:T(2,128)S(1)} %concatenate.6.refs_1_.refs_0_, bf16[256,768]{1,0:T(8,128)(2,1)S(1)} %get-tuple-element.19.refs_1_.refs_2_, bf16[576,768]{1,0:T(8,128)(2,1)S(1)} %get-tuple-element.20.refs_2_), custom_call_target="tpu_custom_call" | custom-call | flops 402653184 | bytes 2065408 | tf_op jit(solution)/shard_map/text_part/pallas_call | solution.py:33
  21.4 0.8 %text_part.3 = (f32[64,768]{1,0:T(8,128)S(1)}, f32[64,768]{1,0:T(8,128)S(1)}, f32[64,768]{1,0:T(8,128)S(1)}, f32[64,768]{1,0:T(8,128)S(1)}) custom-call(f32[2,128]{1,0:T(2,128)S(1)} %concatenate.6.refs_1_.refs_0_, bf16[256,768]{1,0:T(8,128)(2,1)S(1)} %get-tuple-element.19.refs_1_.refs_2_, f32[256,768]{1,0:T(8,128)S(1)} %text_part.2.refs_2_, ...), custom_call_target="tpu_custom_call" | custom-call | flops 402653184 | bytes 2851840 | tf_op jit(solution)/shard_map/text_part/pallas_call | solution.py:33
  22.2 1.7 %collective-permute-start.9 = (f32[64,768]{1,0:T(8,128)S(1)}, f32[64,768]{1,0:T(8,128)S(1)}, u32[]{:S(2)}, u32[]{:S(2)}) collective-permute-start(f32[64,768]{1,0:T(8,128)S(1)} %get-tuple-element.22), channel_id=1, source_target_pairs={{0,8},{8,0},{16,24},{24,16},{1,9},{9,1},{17,25},{25,17},{2,10},{10... | collective-permute-start | bytes 589832 | tf_op jit(solution)/shard_map/ppermute | solution.py:17
  23.9 5.1 %collective-permute-done.9.refs_1_ = f32[64,768]{1,0:T(8,128)S(1)} collective-permute-done((f32[64,768]{1,0:T(8,128)S(1)}, f32[64,768]{1,0:T(8,128)S(1)}, u32[]{:S(2)}, u32[]{:S(2)}) %collective-permute-start.9) | collective-permute-done | bytes 196640 | tf_op jit(solution)/shard_map/ppermute | solution.py:17
  29.0 3.3 %collective-permute-start.13 = (f32[64,768]{1,0:T(8,128)S(1)}, f32[64,768]{1,0:T(8,128)S(1)}, u32[]{:S(2)}, u32[]{:S(2)}) collective-permute-start(f32[64,768]{1,0:T(8,128)S(1)} %get-tuple-element.24.refs_5_.refs_2_), channel_id=1, source_target_pairs={{0,16},{8,24},{16,0},{24,8},{1,17},{9,25},{17,1},{25,9},{2,18},{10... | collective-permute-start | bytes 589832 | tf_op jit(solution)/shard_map/ppermute | solution.py:17
  32.3 1.7 %collective-permute-start.14 = (f32[64,768]{1,0:T(8,128)S(1)}, f32[64,768]{1,0:T(8,128)S(1)}, u32[]{:S(2)}, u32[]{:S(2)}) collective-permute-start(f32[64,768]{1,0:T(8,128)S(1)} %get-tuple-element.28), channel_id=1, source_target_pairs={{0,8},{8,0},{16,24},{24,16},{1,9},{9,1},{17,25},{25,17},{2,10},{10... | collective-permute-start | bytes 589832 | tf_op jit(solution)/shard_map/ppermute | solution.py:17
  34.1 0.6 %collective-permute-start.10 = (bf16[128,768]{1,0:T(8,128)(2,1)S(1)}, bf16[128,768]{1,0:T(8,128)(2,1)S(1)}, u32[]{:S(2)}, u32[]{:S(2)}) collective-permute-start(bf16[128,768]{1,0:T(8,128)(2,1)S(1)} %get-tuple-element.25), channel_id=1, source_target_pairs={{0,2},{1,3},{2,0},{3,1},{4,6},{5,7},{6,4},{7,5},{8,10},{9,11},{10,... | collective-permute-start | bytes 589832 | tf_op jit(solution)/shard_map/ppermute | solution.py:17
  34.7 1.3 %collective-permute-start.11 = (bf16[128,768]{1,0:T(8,128)(2,1)S(1)}, bf16[128,768]{1,0:T(8,128)(2,1)S(1)}, u32[]{:S(2)}, u32[]{:S(2)}) collective-permute-start(bf16[128,768]{1,0:T(8,128)(2,1)S(1)} %get-tuple-element.26), channel_id=1, source_target_pairs={{0,4},{1,5},{2,6},{3,7},{4,0},{5,1},{6,2},{7,3},{8,12},{9,13},{10,... | collective-permute-start | bytes 589832 | tf_op jit(solution)/shard_map/ppermute | solution.py:17
  35.9 1.0 %speech_part.4.refs_2_ = f32[128,768]{1,0:T(8,128)S(1)} custom-call(f32[2,128]{1,0:T(2,128)S(1)} %concatenate.6.refs_1_.refs_0_, bf16[144,768]{1,0:T(8,128)(2,1)S(1)} %get-tuple-element.17.refs_4_.refs_1_, bf16[256,768]{1,0:T(8,128)(2,1)S(1)} %get-tuple-element.19.refs_1_.refs_2_, bf16[256,768]{1,0:T(8,128)(2,1)S(1)} %collective-permute-done.6.refs_3_.refs_1_, ...), custom_call_target="tpu_custom_call" | custom-call | flops 3019898880 | bytes 1795072 | tf_op jit(solution)/shard_map/speech_part/pallas_call | solution.py:33
  37.0 1.0 %speech_part.6.refs_2_ = f32[128,768]{1,0:T(8,128)S(1)} custom-call(f32[2,128]{1,0:T(2,128)S(1)} %concatenate.6.refs_1_.refs_0_, bf16[144,768]{1,0:T(8,128)(2,1)S(1)} %slice.5.refs_1_, bf16[256,768]{1,0:T(8,128)(2,1)S(1)} %get-tuple-element.19.refs_1_.refs_2_, bf16[256,768]{1,0:T(8,128)(2,1)S(1)} %collective-permute-done.6.refs_3_.refs_1_, ...), custom_call_target="tpu_custom_call" | custom-call | flops 3019898880 | bytes 1795072 | tf_op jit(solution)/shard_map/speech_part/pallas_call | solution.py:33
  38.0 1.8 %collective-permute-done.10.refs_3_ = bf16[128,768]{1,0:T(8,128)(2,1)S(1)} collective-permute-done((bf16[128,768]{1,0:T(8,128)(2,1)S(1)}, bf16[128,768]{1,0:T(8,128)(2,1)S(1)}, u32[]{:S(2)}, u32[]{:S(2)}) %collective-permute-start.10) | collective-permute-done | bytes 196640 | tf_op jit(solution)/shard_map/ppermute | solution.py:17
  39.8 0.5 %collective-permute-done.11.refs_4_ = bf16[128,768]{1,0:T(8,128)(2,1)S(1)} collective-permute-done((bf16[128,768]{1,0:T(8,128)(2,1)S(1)}, bf16[128,768]{1,0:T(8,128)(2,1)S(1)}, u32[]{:S(2)}, u32[]{:S(2)}) %collective-permute-start.11) | collective-permute-done | bytes 196640 | tf_op jit(solution)/shard_map/ppermute | solution.py:17
  40.3 0.5 %speech_part.7 = f32[128,768]{1,0:T(8,128)S(1)} custom-call(f32[2,128]{1,0:T(2,128)S(1)} %concatenate.6.refs_1_.refs_0_, bf16[144,768]{1,0:T(8,128)(2,1)S(1)} %slice.5.refs_1_, f32[128,768]{1,0:T(8,128)S(1)} %speech_part.6.refs_2_, bf16[128,768]{1,0:T(8,128)(2,1)S(1)} %collective-permute-done.10.refs_3_, bf16[128,768]{1,0:T(8,128)(2,1)S(1)} %collective-permute-done.11.refs_4_), custom_call_target="tpu_custom_call" | custom-call | flops 1006632960 | bytes 1401856 | tf_op jit(solution)/shard_map/speech_part/pallas_call | solution.py:33
  40.8 0.1 collective-permute-start.12
  41.0 0.4 collective-permute-done.14.refs_1_
  41.4 0.5 %speech_part.5.refs_1_ = f32[128,768]{1,0:T(8,128)S(1)} custom-call(f32[2,128]{1,0:T(2,128)S(1)} %concatenate.6.refs_1_.refs_0_, bf16[144,768]{1,0:T(8,128)(2,1)S(1)} %get-tuple-element.17.refs_4_.refs_1_, f32[128,768]{1,0:T(8,128)S(1)} %speech_part.4.refs_2_, bf16[128,768]{1,0:T(8,128)(2,1)S(1)} %collective-permute-done.10.refs_3_, ...), custom_call_target="tpu_custom_call" | custom-call | flops 1006632960 | bytes 1401856 | tf_op jit(solution)/shard_map/speech_part/pallas_call | solution.py:33
  41.9 0.7 %collective-permute-done.12.refs_2_ = f32[128,768]{1,0:T(8,128)S(1)} collective-permute-done((f32[128,768]{1,0:T(8,128)S(1)}, f32[128,768]{1,0:T(8,128)S(1)}, u32[]{:S(2)}, u32[]{:S(2)}) %collective-permute-start.12) | collective-permute-done | bytes 393248 | tf_op jit(solution)/shard_map/ppermute | solution.py:17
  42.6 1.0 %finish.1 = (f32[128,768]{1,0:T(8,128)}, f32[64,768]{1,0:T(8,128)}) custom-call(bf16[128,768]{1,0:T(8,128)(2,1)S(1)} %get-tuple-element.16.refs_0_, f32[128,768]{1,0:T(8,128)S(1)} %speech_part.5.refs_1_, f32[128,768]{1,0:T(8,128)S(1)} %collective-permute-done.12.refs_2_, bf16[64,768]{1,0:T(8,128)(2,1)S(1)} %get-tuple-element.27.refs_3_, ...), custom_call_target="tpu_custom_call" | custom-call | bytes 1867776 | tf_op jit(solution)/shard_map/finish/pallas_call | solution.py:33
  (14 shorter events, 0.2 us)
Async XLA Ops:
  1.8 15.5 %collective-permute-start.3 = (bf16[144,768]{1,0:T(8,128)(2,1)S(1)}, bf16[144,768]{1,0:T(8,128)(2,1)S(1)}, u32[]{:S(2)}, u32[]{:S(2)}) collective-permute-start(bf16[144,768]{1,0:T(8,128)(2,1)S(1)} %get-tuple-element.17.refs_4_.refs_1_), channel_id=1, source_target_pairs={{0,2},{1,3},{2,0},{3,1},{4,6},{5,7},{6,4},{7,5},{8,10},{9,11},{10,... | collective-permute-start | bytes 663560 | tf_op jit(solution)/shard_map/ppermute | solution.py:17
  4.8 12.5 %collective-permute-start.4 = (bf16[144,768]{1,0:T(8,128)(2,1)S(1)}, bf16[144,768]{1,0:T(8,128)(2,1)S(1)}, u32[]{:S(2)}, u32[]{:S(2)}) collective-permute-start(bf16[144,768]{1,0:T(8,128)(2,1)S(1)} %get-tuple-element.17.refs_4_.refs_1_), channel_id=1, source_target_pairs={{0,4},{1,5},{2,6},{3,7},{4,0},{5,1},{6,2},{7,3},{8,12},{9,13},{10,... | collective-permute-start | bytes 663560 | tf_op jit(solution)/shard_map/ppermute | solution.py:17
  6.3 10.9 %collective-permute-start.5 = (bf16[144,768]{1,0:T(8,128)(2,1)S(1)}, bf16[144,768]{1,0:T(8,128)(2,1)S(1)}, u32[]{:S(2)}, u32[]{:S(2)}) collective-permute-start(bf16[144,768]{1,0:T(8,128)(2,1)S(1)} %get-tuple-element.17.refs_4_.refs_1_), channel_id=1, source_target_pairs={{0,6},{1,7},{2,4},{3,5},{4,2},{5,3},{6,0},{7,1},{8,14},{9,15},{10,... | collective-permute-start | bytes 663560 | tf_op jit(solution)/shard_map/ppermute | solution.py:17
  6.4 6.2 %collective-permute-start.1 = (bf16[64,768]{1,0:T(8,128)(2,1)S(1)}, bf16[64,768]{1,0:T(8,128)(2,1)S(1)}, u32[]{:S(2)}, u32[]{:S(2)}) collective-permute-start(bf16[64,768]{1,0:T(8,128)(2,1)S(1)} %get-tuple-element.18.refs_0_), channel_id=1, source_target_pairs={{0,16},{8,24},{16,0},{24,8},{1,17},{9,25},{17,1},{25,9},{2,18},{10... | collective-permute-start | bytes 294920 | tf_op jit(solution)/shard_map/ppermute | solution.py:17
  9.4 5.3 %collective-permute-start = (bf16[64,768]{1,0:T(8,128)(2,1)S(1)}, bf16[64,768]{1,0:T(8,128)(2,1)S(1)}, u32[]{:S(2)}, u32[]{:S(2)}) collective-permute-start(bf16[64,768]{1,0:T(8,128)(2,1)S(1)} %get-tuple-element.18.refs_0_), channel_id=1, source_target_pairs={{0,8},{8,0},{16,24},{24,16},{1,9},{9,1},{17,25},{25,17},{2,10},{10... | collective-permute-start | bytes 294920 | tf_op jit(solution)/shard_map/ppermute | solution.py:17
  12.6 4.7 %collective-permute-start.2 = (bf16[64,768]{1,0:T(8,128)(2,1)S(1)}, bf16[64,768]{1,0:T(8,128)(2,1)S(1)}, u32[]{:S(2)}, u32[]{:S(2)}) collective-permute-start(bf16[64,768]{1,0:T(8,128)(2,1)S(1)} %pass_on.1.refs_2_), channel_id=1, source_target_pairs={{0,8},{8,0},{16,24},{24,16},{1,9},{9,1},{17,25},{25,17},{2,10},{10... | collective-permute-start | bytes 294920 | tf_op jit(solution)/shard_map/ppermute | solution.py:17
  17.4 4.0 %collective-permute-start.8 = (bf16[576,768]{1,0:T(8,128)(2,1)S(1)}, bf16[576,768]{1,0:T(8,128)(2,1)S(1)}, u32[]{:S(2)}, u32[]{:S(2)}) collective-permute-start(bf16[576,768]{1,0:T(8,128)(2,1)S(1)} %get-tuple-element.20.refs_2_), channel_id=1, source_target_pairs={{0,1},{1,0},{2,3},{3,2},{4,5},{5,4},{6,7},{7,6},{8,9},{9,8},{10,11... | collective-permute-start | bytes 2654216 | tf_op jit(solution)/shard_map/ppermute | solution.py:17
  17.5 16.6 %collective-permute-start.6 = (bf16[256,768]{1,0:T(8,128)(2,1)S(1)}, bf16[256,768]{1,0:T(8,128)(2,1)S(1)}, u32[]{:S(2)}, u32[]{:S(2)}) collective-permute-start(bf16[256,768]{1,0:T(8,128)(2,1)S(1)} %get-tuple-element.19.refs_1_.refs_2_), channel_id=1, source_target_pairs={{0,2},{1,3},{2,0},{3,1},{4,6},{5,7},{6,4},{7,5},{8,10},{9,11},{10,... | collective-permute-start | bytes 1179656 | tf_op jit(solution)/shard_map/ppermute | solution.py:17
  19.1 15.0 %collective-permute-start.7 = (bf16[256,768]{1,0:T(8,128)(2,1)S(1)}, bf16[256,768]{1,0:T(8,128)(2,1)S(1)}, u32[]{:S(2)}, u32[]{:S(2)}) collective-permute-start(bf16[256,768]{1,0:T(8,128)(2,1)S(1)} %get-tuple-element.19.refs_1_.refs_2_), channel_id=1, source_target_pairs={{0,4},{1,5},{2,6},{3,7},{4,0},{5,1},{6,2},{7,3},{8,12},{9,13},{10,... | collective-permute-start | bytes 1179656 | tf_op jit(solution)/shard_map/ppermute | solution.py:17
  22.2 6.8 %collective-permute-start.9 = (f32[64,768]{1,0:T(8,128)S(1)}, f32[64,768]{1,0:T(8,128)S(1)}, u32[]{:S(2)}, u32[]{:S(2)}) collective-permute-start(f32[64,768]{1,0:T(8,128)S(1)} %get-tuple-element.22), channel_id=1, source_target_pairs={{0,8},{8,0},{16,24},{24,16},{1,9},{9,1},{17,25},{25,17},{2,10},{10... | collective-permute-start | bytes 589832 | tf_op jit(solution)/shard_map/ppermute | solution.py:17
  29.0 12.0 %collective-permute-start.13 = (f32[64,768]{1,0:T(8,128)S(1)}, f32[64,768]{1,0:T(8,128)S(1)}, u32[]{:S(2)}, u32[]{:S(2)}) collective-permute-start(f32[64,768]{1,0:T(8,128)S(1)} %get-tuple-element.24.refs_5_.refs_2_), channel_id=1, source_target_pairs={{0,16},{8,24},{16,0},{24,8},{1,17},{9,25},{17,1},{25,9},{2,18},{10... | collective-permute-start | bytes 589832 | tf_op jit(solution)/shard_map/ppermute | solution.py:17
  32.3 9.1 %collective-permute-start.14 = (f32[64,768]{1,0:T(8,128)S(1)}, f32[64,768]{1,0:T(8,128)S(1)}, u32[]{:S(2)}, u32[]{:S(2)}) collective-permute-start(f32[64,768]{1,0:T(8,128)S(1)} %get-tuple-element.28), channel_id=1, source_target_pairs={{0,8},{8,0},{16,24},{24,16},{1,9},{9,1},{17,25},{25,17},{2,10},{10... | collective-permute-start | bytes 589832 | tf_op jit(solution)/shard_map/ppermute | solution.py:17
  34.1 5.7 %collective-permute-start.10 = (bf16[128,768]{1,0:T(8,128)(2,1)S(1)}, bf16[128,768]{1,0:T(8,128)(2,1)S(1)}, u32[]{:S(2)}, u32[]{:S(2)}) collective-permute-start(bf16[128,768]{1,0:T(8,128)(2,1)S(1)} %get-tuple-element.25), channel_id=1, source_target_pairs={{0,2},{1,3},{2,0},{3,1},{4,6},{5,7},{6,4},{7,5},{8,10},{9,11},{10,... | collective-permute-start | bytes 589832 | tf_op jit(solution)/shard_map/ppermute | solution.py:17
  34.7 5.7 %collective-permute-start.11 = (bf16[128,768]{1,0:T(8,128)(2,1)S(1)}, bf16[128,768]{1,0:T(8,128)(2,1)S(1)}, u32[]{:S(2)}, u32[]{:S(2)}) collective-permute-start(bf16[128,768]{1,0:T(8,128)(2,1)S(1)} %get-tuple-element.26), channel_id=1, source_target_pairs={{0,4},{1,5},{2,6},{3,7},{4,0},{5,1},{6,2},{7,3},{8,12},{9,13},{10,... | collective-permute-start | bytes 589832 | tf_op jit(solution)/shard_map/ppermute | solution.py:17
  40.8 1.8 %collective-permute-start.12 = (f32[128,768]{1,0:T(8,128)S(1)}, f32[128,768]{1,0:T(8,128)S(1)}, u32[]{:S(2)}, u32[]{:S(2)}) collective-permute-start(f32[128,768]{1,0:T(8,128)S(1)} %speech_part.7), channel_id=1, source_target_pairs={{0,1},{1,0},{2,3},{3,2},{4,5},{5,4},{6,7},{7,6},{8,9},{9,8},{10,11... | collective-permute-start | bytes 1179656 | tf_op jit(solution)/shard_map/ppermute | solution.py:17

commit v9 on v8

--- a/solution.py
+++ b/solution.py
@@ -67,6 +67,14 @@
     speech[rows : rows + MARK_ROWS, :] = jnp.broadcast_to(
         wide, (MARK_ROWS, speech.shape[1])
     ).astype(jnp.bfloat16)
+
+
+def unit_body(values, out):
+    out[...] = direction(values[...])[0].astype(jnp.bfloat16)
+
+
+def unit_sum_body(rows, values, out):
+    out[...] = rows[...] + direction(values[...])[0].astype(jnp.bfloat16)
 
 
 def join_body(*refs):
@@ -215,14 +223,16 @@
         name="unit_rows",
     )(*[pltpu.with_memory_space_constraint(v, pltpu.HBM) for v in arguments])
 
-    def passed_on(block):
-        return call(join_body, bf16(own_text, width), [block], (scalars,), 1 << 20, name="pass_on")
-
     text_blocks = [text_own] + [None] * (groups - 1)
-    for k in [1 << i for i in reversed(range(groups.bit_length() - 1))]:
+    far = groups // 2
+    up = lax.ppermute(sentence_vectors, "group", [(i, i - far) for i in range(far, groups)])
+    down = lax.ppermute(sentence_vectors, "group", [(i, i + far) for i in range(far)])
+    shape = bf16(own_text, width)
+    up = call(unit_body, shape, [up], (), EARLY, name="unit_far")
+    text_blocks[far] = call(unit_sum_body, shape, [up, down], (scalars,), 1 << 20, name="pass_on")
+    for k in [1 << i for i in reversed(range(groups.bit_length() - 2))]:
         for j in range(0, groups, 2 * k):
-            came = exchanged(text_blocks[j], "group", k)
-            text_blocks[j + k] = passed_on(came) if k > 1 else came
+            text_blocks[j + k] = exchanged(text_blocks[j], "group", k)
     square = chips == 4
     masks = [1, 2] if square else list(range(1, chips))
 

time: 43.8 us -> 48.1 us (1.098)
  starting transfers between devices: 22.7 us -> 26.4 us
    ppermute x0 -> x2, starting transfers between devices: none -> 6.73 us  [the longest x1 5.44 us: shards(): lax.ppermute(sentence_vectors, 'group', [(i, i + far) for i in range(far)])]
    ppermute x15 -> x14, starting transfers between devices: 22.7 us -> 19.6 us  [exchanged(): return lax.ppermute(value, axis, [(i, i ^ mask) for i in range(size)])]
    ppermute x15 -> x14, waiting for transfers between devices: 11.8 us -> 12 us  [exchanged(): return lax.ppermute(value, axis, [(i, i ^ mask) for i in range(size)])]
    pallas_call x12 -> x13, Pallas kernels: 5.86 us -> 6.09 us  [call(): pl.pallas_call(whole, out_shape=out_shape, in_specs=specs, out_specs=jax....]
  transfers between devices with their start and end apart: 15 -> 16, of which waited for: 9 -> 7; matrix products, arithmetic and copies ran while one was open for 0% -> 0% of each run, Pallas kernels for 11% -> 13%
where the time goes in v9:
time: 48.1 us; the launch traced here: 47.9 us
  starting transfers between devices  26.4 us (55%)
  waiting for transfers between devices  12 us (25%)
  Pallas kernels  7.3 us (15%)
  between operations  2.1 us (4%)
    ppermute x14, starting transfers between devices, exchanged(): return lax.ppermute(value, axis, [(i, i ^ mask) for i in range(size)])  19.6 us
    ppermute x14, waiting for transfers between devices, exchanged(): return lax.ppermute(value, axis, [(i, i ^ mask) for i in range(size)])  12 us
    pallas_call x13, Pallas kernels, call(): pl.pallas_call(whole, out_shape=out_shape, in_specs=specs, out_specs=jax....  6.09 us
    ppermute x1, starting transfers between devices, shards(): lax.ppermute(sentence_vectors, 'group', [(i, i + far) for i in range(far)])  5.44 us
    ppermute x1, starting transfers between devices, shards(): lax.ppermute(sentence_vectors, 'group', [(i, i - far) for i in range(far,...  1.29 us
    pallas_call x1, Pallas kernels, shards(): pl.pallas_call(prepare_body, out_shape=[bf16(rows + MARK_ROWS, width), bf...  1.21 us
  transfers between devices with their start and end apart: 16, of which 7 were waited for; matrix products, arithmetic and copies ran while one was open for 0% of the time, Pallas kernels for 13%

profile of v9, /device:TPU:0, one launch (start us, length us, event | category | flops | bytes accessed | tf_op | source)
XLA Modules:
  0.0 47.9 jit_solution(13792805692911602832)
XLA Ops:
  0.6 1.3 %collective-permute-start.1 = (bf16[64,768]{1,0:T(8,128)(2,1)}, bf16[64,768]{1,0:T(8,128)(2,1)S(1)}, u32[]{:S(2)}, u32[]{:S(2)}) collective-permute-start(bf16[64,768]{1,0:T(8,128)(2,1)} %refs_1_.1), channel_id=1, source_target_pairs={{16,0},{24,8},{17,1},{25,9},{18,2},{26,10},{19,3},{27,11},{20,4},{... | collective-permute-start | bytes 294920 | tf_op jit(solution)/shard_map/ppermute | solution.py:228
  1.9 1.2 %unit_rows.1 = (bf16[144,768]{1,0:T(8,128)(2,1)S(1)}, bf16[64,768]{1,0:T(8,128)(2,1)S(1)}, bf16[128,768]{1,0:T(8,128)(2,1)S(1)}, bf16[64,768]{1,0:T(8,128)(2,1)S(1)}) custom-call(bf16[128,768]{1,0:T(8,128)(2,1)} %refs_0_.1, bf16[64,768]{1,0:T(8,128)(2,1)} %refs_1_.1, s32[1,128]{1,0:T(1,128)} %bitcast.3), custom_call_target="tpu_custom_call" | custom-call | tf_op jit(solution)/shard_map/unit_rows/pallas_call | solution.py:211
  3.2 3.0 %collective-permute-start.4 = (bf16[144,768]{1,0:T(8,128)(2,1)S(1)}, bf16[144,768]{1,0:T(8,128)(2,1)S(1)}, u32[]{:S(2)}, u32[]{:S(2)}) collective-permute-start(bf16[144,768]{1,0:T(8,128)(2,1)S(1)} %get-tuple-element.17.refs_4_.refs_1_), channel_id=1, source_target_pairs={{0,2},{1,3},{2,0},{3,1},{4,6},{5,7},{6,4},{7,5},{8,10},{9,11},{10,... | collective-permute-start | bytes 663560 | tf_op jit(solution)/shard_map/ppermute | solution.py:17
  6.2 1.5 %collective-permute-start.5 = (bf16[144,768]{1,0:T(8,128)(2,1)S(1)}, bf16[144,768]{1,0:T(8,128)(2,1)S(1)}, u32[]{:S(2)}, u32[]{:S(2)}) collective-permute-start(bf16[144,768]{1,0:T(8,128)(2,1)S(1)} %get-tuple-element.17.refs_4_.refs_1_), channel_id=1, source_target_pairs={{0,4},{1,5},{2,6},{3,7},{4,0},{5,1},{6,2},{7,3},{8,12},{9,13},{10,... | collective-permute-start | bytes 663560 | tf_op jit(solution)/shard_map/ppermute | solution.py:17
  7.7 5.4 %collective-permute-start.2 = (bf16[64,768]{1,0:T(8,128)(2,1)S(1)}, bf16[64,768]{1,0:T(8,128)(2,1)S(1)}, u32[]{:S(2)}, u32[]{:S(2)}) collective-permute-start(bf16[64,768]{1,0:T(8,128)(2,1)S(1)} %copy-done), channel_id=1, source_target_pairs={{0,16},{8,24},{1,17},{9,25},{2,18},{10,26},{3,19},{11,27},{4,20},{... | collective-permute-start | bytes 294920 | tf_op jit(solution)/shard_map/ppermute | solution.py:229
  14.5 2.1 %collective-permute-start = (bf16[64,768]{1,0:T(8,128)(2,1)S(1)}, bf16[64,768]{1,0:T(8,128)(2,1)S(1)}, u32[]{:S(2)}, u32[]{:S(2)}) collective-permute-start(bf16[64,768]{1,0:T(8,128)(2,1)S(1)} %get-tuple-element.18.refs_0_), channel_id=1, source_target_pairs={{0,8},{8,0},{16,24},{24,16},{1,9},{9,1},{17,25},{25,17},{2,10},{10... | collective-permute-start | bytes 294920 | tf_op jit(solution)/shard_map/ppermute | solution.py:17
  16.6 0.1 unit_far.1.refs_0_
  16.8 0.1 pass_on.1.refs_2_
  16.9 1.3 %collective-permute-start.3 = (bf16[64,768]{1,0:T(8,128)(2,1)S(1)}, bf16[64,768]{1,0:T(8,128)(2,1)S(1)}, u32[]{:S(2)}, u32[]{:S(2)}) collective-permute-start(bf16[64,768]{1,0:T(8,128)(2,1)S(1)} %pass_on.1.refs_2_), channel_id=1, source_target_pairs={{0,8},{8,0},{16,24},{24,16},{1,9},{9,1},{17,25},{25,17},{2,10},{10... | collective-permute-start | bytes 294920 | tf_op jit(solution)/shard_map/ppermute | solution.py:17
  18.2 1.6 %collective-permute-done.refs_1_ = bf16[64,768]{1,0:T(8,128)(2,1)S(1)} collective-permute-done((bf16[64,768]{1,0:T(8,128)(2,1)S(1)}, bf16[64,768]{1,0:T(8,128)(2,1)S(1)}, u32[]{:S(2)}, u32[]{:S(2)}) %collective-permute-start) | collective-permute-done | bytes 98336 | tf_op jit(solution)/shard_map/ppermute | solution.py:17
  19.8 1.8 %collective-permute-done.3.refs_3_ = bf16[64,768]{1,0:T(8,128)(2,1)S(1)} collective-permute-done((bf16[64,768]{1,0:T(8,128)(2,1)S(1)}, bf16[64,768]{1,0:T(8,128)(2,1)S(1)}, u32[]{:S(2)}, u32[]{:S(2)}) %collective-permute-start.3) | collective-permute-done | bytes 98336 | tf_op jit(solution)/shard_map/ppermute | solution.py:17
  21.6 0.1 join_rows.1
  21.7 0.1 collective-permute-start.9
  21.8 1.6 %collective-permute-start.7 = (bf16[256,768]{1,0:T(8,128)(2,1)S(1)}, bf16[256,768]{1,0:T(8,128)(2,1)S(1)}, u32[]{:S(2)}, u32[]{:S(2)}) collective-permute-start(bf16[256,768]{1,0:T(8,128)(2,1)S(1)} %get-tuple-element.19.refs_1_.refs_2_), channel_id=1, source_target_pairs={{0,2},{1,3},{2,0},{3,1},{4,6},{5,7},{6,4},{7,5},{8,10},{9,11},{10,... | collective-permute-start | bytes 1179656 | tf_op jit(solution)/shard_map/ppermute | solution.py:17
  23.3 1.5 %collective-permute-start.8 = (bf16[256,768]{1,0:T(8,128)(2,1)S(1)}, bf16[256,768]{1,0:T(8,128)(2,1)S(1)}, u32[]{:S(2)}, u32[]{:S(2)}) collective-permute-start(bf16[256,768]{1,0:T(8,128)(2,1)S(1)} %get-tuple-element.19.refs_1_.refs_2_), channel_id=1, source_target_pairs={{0,4},{1,5},{2,6},{3,7},{4,0},{5,1},{6,2},{7,3},{8,12},{9,13},{10,... | collective-permute-start | bytes 1179656 | tf_op jit(solution)/shard_map/ppermute | solution.py:17
  24.8 0.8 %text_part.2.refs_2_ = f32[256,768]{1,0:T(8,128)S(1)} custom-call(f32[2,128]{1,0:T(2,128)S(1)} %concatenate.6.refs_2_.refs_0_, bf16[256,768]{1,0:T(8,128)(2,1)S(1)} %get-tuple-element.19.refs_1_.refs_2_, bf16[576,768]{1,0:T(8,128)(2,1)S(1)} %get-tuple-element.20.refs_2_), custom_call_target="tpu_custom_call" | custom-call | flops 402653184 | bytes 2065408 | tf_op jit(solution)/shard_map/text_part/pallas_call | solution.py:33
  25.6 0.8 %text_part.3 = (f32[64,768]{1,0:T(8,128)S(1)}, f32[64,768]{1,0:T(8,128)S(1)}, f32[64,768]{1,0:T(8,128)S(1)}, f32[64,768]{1,0:T(8,128)S(1)}) custom-call(f32[2,128]{1,0:T(2,128)S(1)} %concatenate.6.refs_2_.refs_0_, bf16[256,768]{1,0:T(8,128)(2,1)S(1)} %get-tuple-element.19.refs_1_.refs_2_, f32[256,768]{1,0:T(8,128)S(1)} %text_part.2.refs_2_, ...), custom_call_target="tpu_custom_call" | custom-call | flops 402653184 | bytes 2851840 | tf_op jit(solution)/shard_map/text_part/pallas_call | solution.py:33
  26.4 1.6 %collective-permute-start.10 = (f32[64,768]{1,0:T(8,128)S(1)}, f32[64,768]{1,0:T(8,128)S(1)}, u32[]{:S(2)}, u32[]{:S(2)}) collective-permute-start(f32[64,768]{1,0:T(8,128)S(1)} %get-tuple-element.22), channel_id=1, source_target_pairs={{0,8},{8,0},{16,24},{24,16},{1,9},{9,1},{17,25},{25,17},{2,10},{10... | collective-permute-start | bytes 589832 | tf_op jit(solution)/shard_map/ppermute | solution.py:17
  28.1 5.1 %collective-permute-done.10.refs_1_ = f32[64,768]{1,0:T(8,128)S(1)} collective-permute-done((f32[64,768]{1,0:T(8,128)S(1)}, f32[64,768]{1,0:T(8,128)S(1)}, u32[]{:S(2)}, u32[]{:S(2)}) %collective-permute-start.10) | collective-permute-done | bytes 196640 | tf_op jit(solution)/shard_map/ppermute | solution.py:17
  33.2 3.2 %collective-permute-start.14 = (f32[64,768]{1,0:T(8,128)S(1)}, f32[64,768]{1,0:T(8,128)S(1)}, u32[]{:S(2)}, u32[]{:S(2)}) collective-permute-start(f32[64,768]{1,0:T(8,128)S(1)} %get-tuple-element.24.refs_5_.refs_2_), channel_id=1, source_target_pairs={{0,16},{8,24},{16,0},{24,8},{1,17},{9,25},{17,1},{25,9},{2,18},{10... | collective-permute-start | bytes 589832 | tf_op jit(solution)/shard_map/ppermute | solution.py:17
  36.5 1.7 %collective-permute-start.15 = (f32[64,768]{1,0:T(8,128)S(1)}, f32[64,768]{1,0:T(8,128)S(1)}, u32[]{:S(2)}, u32[]{:S(2)}) collective-permute-start(f32[64,768]{1,0:T(8,128)S(1)} %get-tuple-element.28), channel_id=1, source_target_pairs={{0,8},{8,0},{16,24},{24,16},{1,9},{9,1},{17,25},{25,17},{2,10},{10... | collective-permute-start | bytes 589832 | tf_op jit(solution)/shard_map/ppermute | solution.py:17
  38.2 0.6 %collective-permute-start.11 = (bf16[128,768]{1,0:T(8,128)(2,1)S(1)}, bf16[128,768]{1,0:T(8,128)(2,1)S(1)}, u32[]{:S(2)}, u32[]{:S(2)}) collective-permute-start(bf16[128,768]{1,0:T(8,128)(2,1)S(1)} %get-tuple-element.25), channel_id=1, source_target_pairs={{0,2},{1,3},{2,0},{3,1},{4,6},{5,7},{6,4},{7,5},{8,10},{9,11},{10,... | collective-permute-start | bytes 589832 | tf_op jit(solution)/shard_map/ppermute | solution.py:17
  38.8 1.3 %collective-permute-start.12 = (bf16[128,768]{1,0:T(8,128)(2,1)S(1)}, bf16[128,768]{1,0:T(8,128)(2,1)S(1)}, u32[]{:S(2)}, u32[]{:S(2)}) collective-permute-start(bf16[128,768]{1,0:T(8,128)(2,1)S(1)} %get-tuple-element.26), channel_id=1, source_target_pairs={{0,4},{1,5},{2,6},{3,7},{4,0},{5,1},{6,2},{7,3},{8,12},{9,13},{10,... | collective-permute-start | bytes 589832 | tf_op jit(solution)/shard_map/ppermute | solution.py:17
  40.1 1.0 %speech_part.4.refs_2_ = f32[128,768]{1,0:T(8,128)S(1)} custom-call(f32[2,128]{1,0:T(2,128)S(1)} %concatenate.6.refs_2_.refs_0_, bf16[144,768]{1,0:T(8,128)(2,1)S(1)} %get-tuple-element.17.refs_4_.refs_1_, bf16[256,768]{1,0:T(8,128)(2,1)S(1)} %get-tuple-element.19.refs_1_.refs_2_, bf16[256,768]{1,0:T(8,128)(2,1)S(1)} %collective-permute-done.7.refs_3_.refs_1_, ...), custom_call_target="tpu_custom_call" | custom-call | flops 3019898880 | bytes 1795072 | tf_op jit(solution)/shard_map/speech_part/pallas_call | solution.py:33
  41.1 1.0 %speech_part.6.refs_2_ = f32[128,768]{1,0:T(8,128)S(1)} custom-call(f32[2,128]{1,0:T(2,128)S(1)} %concatenate.6.refs_2_.refs_0_, bf16[144,768]{1,0:T(8,128)(2,1)S(1)} %slice.5.refs_1_, bf16[256,768]{1,0:T(8,128)(2,1)S(1)} %get-tuple-element.19.refs_1_.refs_2_, bf16[256,768]{1,0:T(8,128)(2,1)S(1)} %collective-permute-done.7.refs_3_.refs_1_, ...), custom_call_target="tpu_custom_call" | custom-call | flops 3019898880 | bytes 1795072 | tf_op jit(solution)/shard_map/speech_part/pallas_call | solution.py:33
  42.2 1.8 %collective-permute-done.11.refs_3_ = bf16[128,768]{1,0:T(8,128)(2,1)S(1)} collective-permute-done((bf16[128,768]{1,0:T(8,128)(2,1)S(1)}, bf16[128,768]{1,0:T(8,128)(2,1)S(1)}, u32[]{:S(2)}, u32[]{:S(2)}) %collective-permute-start.11) | collective-permute-done | bytes 196640 | tf_op jit(solution)/shard_map/ppermute | solution.py:17
  44.0 0.5 %collective-permute-done.12.refs_4_ = bf16[128,768]{1,0:T(8,128)(2,1)S(1)} collective-permute-done((bf16[128,768]{1,0:T(8,128)(2,1)S(1)}, bf16[128,768]{1,0:T(8,128)(2,1)S(1)}, u32[]{:S(2)}, u32[]{:S(2)}) %collective-permute-start.12) | collective-permute-done | bytes 196640 | tf_op jit(solution)/shard_map/ppermute | solution.py:17
  44.5 0.5 %speech_part.7 = f32[128,768]{1,0:T(8,128)S(1)} custom-call(f32[2,128]{1,0:T(2,128)S(1)} %concatenate.6.refs_2_.refs_0_, bf16[144,768]{1,0:T(8,128)(2,1)S(1)} %slice.5.refs_1_, f32[128,768]{1,0:T(8,128)S(1)} %speech_part.6.refs_2_, bf16[128,768]{1,0:T(8,128)(2,1)S(1)} %collective-permute-done.11.refs_3_, bf16[128,768]{1,0:T(8,128)(2,1)S(1)} %collective-permute-done.12.refs_4_), custom_call_target="tpu_custom_call" | custom-call | flops 1006632960 | bytes 1401856 | tf_op jit(solution)/shard_map/speech_part/pallas_call | solution.py:33
  45.0 0.1 collective-permute-start.13
  45.2 0.5 %speech_part.5.refs_1_ = f32[128,768]{1,0:T(8,128)S(1)} custom-call(f32[2,128]{1,0:T(2,128)S(1)} %concatenate.6.refs_2_.refs_0_, bf16[144,768]{1,0:T(8,128)(2,1)S(1)} %get-tuple-element.17.refs_4_.refs_1_, f32[128,768]{1,0:T(8,128)S(1)} %speech_part.4.refs_2_, bf16[128,768]{1,0:T(8,128)(2,1)S(1)} %collective-permute-done.11.refs_3_, ...), custom_call_target="tpu_custom_call" | custom-call | flops 1006632960 | bytes 1401856 | tf_op jit(solution)/shard_map/speech_part/pallas_call | solution.py:33
  45.7 1.1 %collective-permute-done.13.refs_2_ = f32[128,768]{1,0:T(8,128)S(1)} collective-permute-done((f32[128,768]{1,0:T(8,128)S(1)}, f32[128,768]{1,0:T(8,128)S(1)}, u32[]{:S(2)}, u32[]{:S(2)}) %collective-permute-start.13) | collective-permute-done | bytes 393248 | tf_op jit(solution)/shard_map/ppermute | solution.py:17
  46.8 1.0 %finish.1 = (f32[128,768]{1,0:T(8,128)}, f32[64,768]{1,0:T(8,128)}) custom-call(bf16[128,768]{1,0:T(8,128)(2,1)S(1)} %get-tuple-element.16.refs_0_, f32[128,768]{1,0:T(8,128)S(1)} %speech_part.5.refs_1_, f32[128,768]{1,0:T(8,128)S(1)} %collective-permute-done.13.refs_2_, bf16[64,768]{1,0:T(8,128)(2,1)S(1)} %get-tuple-element.27.refs_3_, ...), custom_call_target="tpu_custom_call" | custom-call | bytes 1867776 | tf_op jit(solution)/shard_map/finish/pallas_call | solution.py:33
  (19 shorter events, 0.3 us)
Async XLA Ops:
  0.6 13.8 %collective-permute-start.1 = (bf16[64,768]{1,0:T(8,128)(2,1)}, bf16[64,768]{1,0:T(8,128)(2,1)S(1)}, u32[]{:S(2)}, u32[]{:S(2)}) collective-permute-start(bf16[64,768]{1,0:T(8,128)(2,1)} %refs_1_.1), channel_id=1, source_target_pairs={{16,0},{24,8},{17,1},{25,9},{18,2},{26,10},{19,3},{27,11},{20,4},{... | collective-permute-start | bytes 294920 | tf_op jit(solution)/shard_map/ppermute | solution.py:228
  1.9 5.8 %copy-start = (bf16[64,768]{1,0:T(8,128)(2,1)S(1)}, bf16[64,768]{1,0:T(8,128)(2,1)}, u32[]{:S(2)}) copy-start(bf16[64,768]{1,0:T(8,128)(2,1)} %refs_1_.1) | copy-start | bytes 294916
  3.2 18.4 %collective-permute-start.4 = (bf16[144,768]{1,0:T(8,128)(2,1)S(1)}, bf16[144,768]{1,0:T(8,128)(2,1)S(1)}, u32[]{:S(2)}, u32[]{:S(2)}) collective-permute-start(bf16[144,768]{1,0:T(8,128)(2,1)S(1)} %get-tuple-element.17.refs_4_.refs_1_), channel_id=1, source_target_pairs={{0,2},{1,3},{2,0},{3,1},{4,6},{5,7},{6,4},{7,5},{8,10},{9,11},{10,... | collective-permute-start | bytes 663560 | tf_op jit(solution)/shard_map/ppermute | solution.py:17
  6.2 15.4 %collective-permute-start.5 = (bf16[144,768]{1,0:T(8,128)(2,1)S(1)}, bf16[144,768]{1,0:T(8,128)(2,1)S(1)}, u32[]{:S(2)}, u32[]{:S(2)}) collective-permute-start(bf16[144,768]{1,0:T(8,128)(2,1)S(1)} %get-tuple-element.17.refs_4_.refs_1_), channel_id=1, source_target_pairs={{0,4},{1,5},{2,6},{3,7},{4,0},{5,1},{6,2},{7,3},{8,12},{9,13},{10,... | collective-permute-start | bytes 663560 | tf_op jit(solution)/shard_map/ppermute | solution.py:17
  7.7 13.9 %collective-permute-start.6 = (bf16[144,768]{1,0:T(8,128)(2,1)S(1)}, bf16[144,768]{1,0:T(8,128)(2,1)S(1)}, u32[]{:S(2)}, u32[]{:S(2)}) collective-permute-start(bf16[144,768]{1,0:T(8,128)(2,1)S(1)} %get-tuple-element.17.refs_4_.refs_1_), channel_id=1, source_target_pairs={{0,6},{1,7},{2,4},{3,5},{4,2},{5,3},{6,0},{7,1},{8,14},{9,15},{10,... | collective-permute-start | bytes 663560 | tf_op jit(solution)/shard_map/ppermute | solution.py:17
  7.7 9.0 %collective-permute-start.2 = (bf16[64,768]{1,0:T(8,128)(2,1)S(1)}, bf16[64,768]{1,0:T(8,128)(2,1)S(1)}, u32[]{:S(2)}, u32[]{:S(2)}) collective-permute-start(bf16[64,768]{1,0:T(8,128)(2,1)S(1)} %copy-done), channel_id=1, source_target_pairs={{0,16},{8,24},{1,17},{9,25},{2,18},{10,26},{3,19},{11,27},{4,20},{... | collective-permute-start | bytes 294920 | tf_op jit(solution)/shard_map/ppermute | solution.py:229
  14.5 5.3 %collective-permute-start = (bf16[64,768]{1,0:T(8,128)(2,1)S(1)}, bf16[64,768]{1,0:T(8,128)(2,1)S(1)}, u32[]{:S(2)}, u32[]{:S(2)}) collective-permute-start(bf16[64,768]{1,0:T(8,128)(2,1)S(1)} %get-tuple-element.18.refs_0_), channel_id=1, source_target_pairs={{0,8},{8,0},{16,24},{24,16},{1,9},{9,1},{17,25},{25,17},{2,10},{10... | collective-permute-start | bytes 294920 | tf_op jit(solution)/shard_map/ppermute | solution.py:17
  16.9 4.7 %collective-permute-start.3 = (bf16[64,768]{1,0:T(8,128)(2,1)S(1)}, bf16[64,768]{1,0:T(8,128)(2,1)S(1)}, u32[]{:S(2)}, u32[]{:S(2)}) collective-permute-start(bf16[64,768]{1,0:T(8,128)(2,1)S(1)} %pass_on.1.refs_2_), channel_id=1, source_target_pairs={{0,8},{8,0},{16,24},{24,16},{1,9},{9,1},{17,25},{25,17},{2,10},{10... | collective-permute-start | bytes 294920 | tf_op jit(solution)/shard_map/ppermute | solution.py:17
  21.7 3.9 %collective-permute-start.9 = (bf16[576,768]{1,0:T(8,128)(2,1)S(1)}, bf16[576,768]{1,0:T(8,128)(2,1)S(1)}, u32[]{:S(2)}, u32[]{:S(2)}) collective-permute-start(bf16[576,768]{1,0:T(8,128)(2,1)S(1)} %get-tuple-element.20.refs_2_), channel_id=1, source_target_pairs={{0,1},{1,0},{2,3},{3,2},{4,5},{5,4},{6,7},{7,6},{8,9},{9,8},{10,11... | collective-permute-start | bytes 2654216 | tf_op jit(solution)/shard_map/ppermute | solution.py:17
  21.8 16.4 %collective-permute-start.7 = (bf16[256,768]{1,0:T(8,128)(2,1)S(1)}, bf16[256,768]{1,0:T(8,128)(2,1)S(1)}, u32[]{:S(2)}, u32[]{:S(2)}) collective-permute-start(bf16[256,768]{1,0:T(8,128)(2,1)S(1)} %get-tuple-element.19.refs_1_.refs_2_), channel_id=1, source_target_pairs={{0,2},{1,3},{2,0},{3,1},{4,6},{5,7},{6,4},{7,5},{8,10},{9,11},{10,... | collective-permute-start | bytes 1179656 | tf_op jit(solution)/shard_map/ppermute | solution.py:17
  23.3 14.9 %collective-permute-start.8 = (bf16[256,768]{1,0:T(8,128)(2,1)S(1)}, bf16[256,768]{1,0:T(8,128)(2,1)S(1)}, u32[]{:S(2)}, u32[]{:S(2)}) collective-permute-start(bf16[256,768]{1,0:T(8,128)(2,1)S(1)} %get-tuple-element.19.refs_1_.refs_2_), channel_id=1, source_target_pairs={{0,4},{1,5},{2,6},{3,7},{4,0},{5,1},{6,2},{7,3},{8,12},{9,13},{10,... | collective-permute-start | bytes 1179656 | tf_op jit(solution)/shard_map/ppermute | solution.py:17
  26.4 6.8 %collective-permute-start.10 = (f32[64,768]{1,0:T(8,128)S(1)}, f32[64,768]{1,0:T(8,128)S(1)}, u32[]{:S(2)}, u32[]{:S(2)}) collective-permute-start(f32[64,768]{1,0:T(8,128)S(1)} %get-tuple-element.22), channel_id=1, source_target_pairs={{0,8},{8,0},{16,24},{24,16},{1,9},{9,1},{17,25},{25,17},{2,10},{10... | collective-permute-start | bytes 589832 | tf_op jit(solution)/shard_map/ppermute | solution.py:17
  33.2 11.9 %collective-permute-start.14 = (f32[64,768]{1,0:T(8,128)S(1)}, f32[64,768]{1,0:T(8,128)S(1)}, u32[]{:S(2)}, u32[]{:S(2)}) collective-permute-start(f32[64,768]{1,0:T(8,128)S(1)} %get-tuple-element.24.refs_5_.refs_2_), channel_id=1, source_target_pairs={{0,16},{8,24},{16,0},{24,8},{1,17},{9,25},{17,1},{25,9},{2,18},{10... | collective-permute-start | bytes 589832 | tf_op jit(solution)/shard_map/ppermute | solution.py:17
  36.5 8.7 %collective-permute-start.15 = (f32[64,768]{1,0:T(8,128)S(1)}, f32[64,768]{1,0:T(8,128)S(1)}, u32[]{:S(2)}, u32[]{:S(2)}) collective-permute-start(f32[64,768]{1,0:T(8,128)S(1)} %get-tuple-element.28), channel_id=1, source_target_pairs={{0,8},{8,0},{16,24},{24,16},{1,9},{9,1},{17,25},{25,17},{2,10},{10... | collective-permute-start | bytes 589832 | tf_op jit(solution)/shard_map/ppermute | solution.py:17
  38.2 5.7 %collective-permute-start.11 = (bf16[128,768]{1,0:T(8,128)(2,1)S(1)}, bf16[128,768]{1,0:T(8,128)(2,1)S(1)}, u32[]{:S(2)}, u32[]{:S(2)}) collective-permute-start(bf16[128,768]{1,0:T(8,128)(2,1)S(1)} %get-tuple-element.25), channel_id=1, source_target_pairs={{0,2},{1,3},{2,0},{3,1},{4,6},{5,7},{6,4},{7,5},{8,10},{9,11},{10,... | collective-permute-start | bytes 589832 | tf_op jit(solution)/shard_map/ppermute | solution.py:17
  38.8 5.7 %collective-permute-start.12 = (bf16[128,768]{1,0:T(8,128)(2,1)S(1)}, bf16[128,768]{1,0:T(8,128)(2,1)S(1)}, u32[]{:S(2)}, u32[]{:S(2)}) collective-permute-start(bf16[128,768]{1,0:T(8,128)(2,1)S(1)} %get-tuple-element.26), channel_id=1, source_target_pairs={{0,4},{1,5},{2,6},{3,7},{4,0},{5,1},{6,2},{7,3},{8,12},{9,13},{10,... | collective-permute-start | bytes 589832 | tf_op jit(solution)/shard_map/ppermute | solution.py:17
  45.0 1.8 %collective-permute-start.13 = (f32[128,768]{1,0:T(8,128)S(1)}, f32[128,768]{1,0:T(8,128)S(1)}, u32[]{:S(2)}, u32[]{:S(2)}) collective-permute-start(f32[128,768]{1,0:T(8,128)S(1)} %speech_part.7), channel_id=1, source_target_pairs={{0,1},{1,0},{2,3},{3,2},{4,5},{5,4},{6,7},{7,6},{8,9},{9,8},{10,11... | collective-permute-start | bytes 1179656 | tf_op jit(solution)/shard_map/ppermute | solution.py:17

commit v10 on v8

--- a/solution.py
+++ b/solution.py
@@ -77,14 +77,15 @@
         at += ref.shape[0]
 
 
-def join_both_body(count, *refs):
-    join_body(*refs[:count], refs[-2])
-    join_body(*refs[count:-2], refs[-1])
-
-
-def halves_body(upper, lower, upper_out, lower_out):
+def joined(blocks, after=(), name="join"):
+    shape = (sum(v.shape[0] for v in blocks), blocks[0].shape[1])
+    return call(join_body, jax.ShapeDtypeStruct(shape, blocks[0].dtype), blocks, after, name=name)
+
+
+def halves_body(upper, lower, kept, upper_out, lower_out, kept_out):
     upper_out[...] = upper[: upper_out.shape[0], :]
     lower_out[...] = lower[upper_out.shape[0] :, :]
+    kept_out[...] = kept[...]
 
 
 def marks_of(block, rows):
@@ -129,9 +130,12 @@
             coef = coefficients(dot_rows(text, chunk), match, sharp, shift)
             part = jnp.dot(coef, chunk, preferred_element_type=jnp.float32)
             total = part if total is None else total + part
-    size = outs[0].shape[0]
-    for k, out in enumerate(outs):
-        out[...] = total[k * size : (k + 1) * size, :]
+    row, at = 0, 0
+    for out in outs:
+        out[...] = total[row : row + out.shape[0], at : at + out.shape[1]]
+        at += out.shape[1]
+        if at == total.shape[1]:
+            row, at = row + out.shape[0], 0
 
 
 def speech_part_body(rows, own_text, has_start, masks, *refs):
@@ -159,9 +163,13 @@
     out[...] = total
 
 
-def sum_near_body(mine, came, kept, total, kept_out):
-    total[...] = mine[...] + came[...]
-    kept_out[...] = kept[...]
+def add_sides_body(mine, *refs):
+    out = refs[-1]
+    at = 0
+    for side in refs[:-1]:
+        columns = slice(at, at + side.shape[1])
+        out[:, columns] = mine[:, columns] + side[...]
+        at += side.shape[1]
 
 
 def sum_body(*refs):
@@ -177,8 +185,12 @@
     out[...] = (back - heading * along) / norms
 
 
-def finish_body(audio, home, back, sentence, text_back, speech_grad, text_grad):
-    project(sentence[...], text_back[...], text_grad)
+def finish_body(audio, home, back, sentence, *refs):
+    parts, (speech_grad, text_grad) = refs[:-2], refs[-2:]
+    text_back = parts[0][...]
+    for part in parts[1:]:
+        text_back = text_back + part[...]
+    project(sentence[...], text_back, text_grad)
     project(audio[...], home[...] + back[...], speech_grad)
 
 
@@ -216,7 +228,7 @@
     )(*[pltpu.with_memory_space_constraint(v, pltpu.HBM) for v in arguments])
 
     def passed_on(block):
-        return call(join_body, bf16(own_text, width), [block], (scalars,), 1 << 20, name="pass_on")
+        return call(join_body, bf16(own_text, width), [block], (scalars,), 1 << 31, name="pass_on")
 
     text_blocks = [text_own] + [None] * (groups - 1)
     for k in [1 << i for i in reversed(range(groups.bit_length() - 1))]:
@@ -226,22 +238,14 @@
     square = chips == 4
     masks = [1, 2] if square else list(range(1, chips))
 
-    def far_halves(near, middle, after=()):
-        sizes = [middle, near[0].shape[0] - middle]
-        halves = call(
-            halves_body, [bf16(size, width) for size in sizes], near[::-1], after, name="halves"
-        )
-        return [exchanged(half, "member", 2 * k) for half, k in zip(halves, masks)]
-
     speech_blocks = [exchanged(speech_own, "member", 2 * k) for k in reversed(range(1, chips))]
     column = groups * own_text
-    text, speech = call(
-        functools.partial(join_both_body, groups),
-        [bf16(column, width), bf16(chips * (rows + MARK_ROWS), width)],
-        [*text_blocks, speech_own, *speech_blocks[::-1]],
-        name="join_rows",
-    )
-    other = exchanged(speech, "member", 1)
+    if square:
+        speech = [speech_own, *speech_blocks]
+    else:
+        speech = [joined([speech_own, *speech_blocks], name="join_speech")]
+    other = [exchanged(block, "member", 1) for block in speech]
+    text = joined(text_blocks, tuple(other[:1]) if square else (), name="join_text")
     text_near = [exchanged(text, "member", 2 * k) for k in masks]
 
     temporary = 4 * column * (6 * CHUNK + 3 * width)
@@ -253,42 +257,51 @@
         work = 4 * len(ks) * own_text * count * rows * width
         return call(body, outs, operands, (), work, temporary, "text_part")
 
-    half = text_part([f32(column, width)], [speech], [])
-    parts = list(text_part([f32(own_text, width)] * groups, [other], half))
-
-    text_back = [parts[0]]
-    for bit in [1 << i for i in range(groups.bit_length() - 1)]:
-        for k in reversed(range(bit, groups, 2 * bit)):
-            came = exchanged(parts[k], "group", bit)
-            if k == bit:
-                text_back.append(came)
-            else:
-                parts[k - bit], parts[bit] = call(
-                    sum_near_body,
-                    [f32(own_text, width)] * 2,
-                    [parts[k - bit], came, parts[bit]],
-                    name="sum_near",
-                )
-
+    half = text_part([f32(column, width)], speech, [])
+    sides = 2
+    side = f32(own_text, width // sides)
+    outs = [f32(own_text, width)] * (groups // 2) + [side] * (groups // 2 * sides)
+    parts = list(text_part(outs, other, half))
+    far = [parts[groups // 2 + i * sides :][:sides] for i in range(groups // 2)]
+
+    bit = 1
+    while bit < groups // 2:
+        for k in reversed(range(bit, groups // 2, 2 * bit)):
+            came = [exchanged(v, "group", bit) for v in far[k]]
+            far[k - bit] = [
+                call(sum_body, side, [mine, v], name="sum_near") for mine, v in zip(far[k - bit], came)
+            ]
+        bit *= 2
+    from_far = [exchanged(v, "group", groups // 2) for v in far[0]]
     def speech_part(block, start, columns, texts, after=()):
         body = functools.partial(speech_part_body, rows, own_text, bool(start), columns)
         operands = [scalars, block, *start, *texts]
         work = 40 * rows * column * len(columns) * width
         return call(body, f32(rows, width), operands, after, work, temporary, "speech_part")
 
-    near = [[0, *masks], [text, *text_near], (parts[groups // 2],)]
-    away = speech_part(other[0 : rows + MARK_ROWS], [], *near)
+    near = [[0, *masks], [text, *text_near], tuple(far[0])]
+    away = speech_part(other[0][0 : rows + MARK_ROWS], [], *near)
     home = speech_part(speech_own, [], *near)
     if square:
-        text_far = far_halves(text_near, column // 2, (parts[groups // 2],))
-        away = speech_part(other[0 : rows + MARK_ROWS], [away], [3], text_far)
+        *sent, parts[1] = call(
+            halves_body,
+            [bf16(column // 2, width)] * 2 + [f32(own_text, width)],
+            [*text_near[::-1], parts[1]],
+            tuple(far[0]),
+            name="halves",
+        )
+        text_far = [exchanged(half, "member", 2 * k) for half, k in zip(sent, masks)]
+        away = speech_part(other[0][0 : rows + MARK_ROWS], [away], [3], text_far)
         home = speech_part(speech_own, [home], [3], text_far)
     back = exchanged(away, "member", 1)
-    text_back = call(sum_body, f32(own_text, width), text_back[::-1], (), EARLY, name="text_sum")
+    from_near = [exchanged(parts[k], "group", k) for k in range(1, groups // 2)]
+    text_back = call(
+        add_sides_body, f32(own_text, width), [parts[0], *from_far], (), EARLY, name="text_sum"
+    )
     speech_grad, text_grad = call(
         finish_body,
         [f32(rows, width), f32(own_text, width)],
-        [audio, home, back, sentence, text_back],
+        [audio, home, back, sentence, text_back, *from_near],
         name="finish",
     )
     return (speech_grad, text_grad)

time: 43.8 us -> 44.1 us (level)
  starting transfers between devices: 22.7 us -> 20.2 us
  waiting for transfers between devices: 11.8 us -> 13.2 us
  Pallas kernels: 7.04 us -> 8.39 us
    ppermute x15 -> x20, starting transfers between devices: 22.7 us -> 20.2 us  [exchanged(): return lax.ppermute(value, axis, [(i, i ^ mask) for i in range(size)])]
    ppermute x15 -> x20, waiting for transfers between devices: 11.8 us -> 13.2 us  [exchanged(): return lax.ppermute(value, axis, [(i, i ^ mask) for i in range(size)])]
    pallas_call x12 -> x13, Pallas kernels: 5.86 us -> 7.21 us  [call(): pl.pallas_call(whole, out_shape=out_shape, in_specs=specs, out_specs=jax....]
  transfers between devices with their start and end apart: 15 -> 20, of which waited for: 9 -> 7; matrix products, arithmetic and copies ran while one was open for 0% -> 0% of each run, Pallas kernels for 11% -> 14%
where the time goes in v10:
time: 44.1 us; the launch traced here: 43.9 us
  starting transfers between devices  20.2 us (46%)
  waiting for transfers between devices  13.2 us (30%)
  Pallas kernels  8.39 us (19%)
  between operations  2.08 us (5%)
    ppermute x20, starting transfers between devices, exchanged(): return lax.ppermute(value, axis, [(i, i ^ mask) for i in range(size)])  20.2 us
    ppermute x20, waiting for transfers between devices, exchanged(): return lax.ppermute(value, axis, [(i, i ^ mask) for i in range(size)])  13.2 us
    pallas_call x13, Pallas kernels, call(): pl.pallas_call(whole, out_shape=out_shape, in_specs=specs, out_specs=jax....  7.21 us
    pallas_call x1, Pallas kernels, shards(): pl.pallas_call(prepare_body, out_shape=[bf16(rows + MARK_ROWS, width), bf...  1.18 us
  transfers between devices with their start and end apart: 20, of which 7 were waited for; matrix products, arithmetic and copies ran while one was open for 0% of the time, Pallas kernels for 14%

profile of v10, /device:TPU:0, one launch (start us, length us, event | category | flops | bytes accessed | tf_op | source)
XLA Modules:
  0.0 43.9 jit_solution(2432795657368261467)
XLA Ops:
  0.6 1.2 %unit_rows.1 = (bf16[144,768]{1,0:T(8,128)(2,1)S(1)}, bf16[64,768]{1,0:T(8,128)(2,1)S(1)}, bf16[128,768]{1,0:T(8,128)(2,1)S(1)}, bf16[64,768]{1,0:T(8,128)(2,1)S(1)}) custom-call(bf16[128,768]{1,0:T(8,128)(2,1)} %refs_0_.1, bf16[64,768]{1,0:T(8,128)(2,1)} %refs_1_.1, s32[1,128]{1,0:T(1,128)} %bitcast.3), custom_call_target="tpu_custom_call" | custom-call | tf_op jit(solution)/shard_map/unit_rows/pallas_call | solution.py:215
  1.8 4.1 %collective-permute-start.1 = (bf16[64,768]{1,0:T(8,128)(2,1)S(1)}, bf16[64,768]{1,0:T(8,128)(2,1)S(1)}, u32[]{:S(2)}, u32[]{:S(2)}) collective-permute-start(bf16[64,768]{1,0:T(8,128)(2,1)S(1)} %get-tuple-element.17.refs_0_), channel_id=1, source_target_pairs={{0,16},{8,24},{16,0},{24,8},{1,17},{9,25},{17,1},{25,9},{2,18},{10... | collective-permute-start | bytes 294920 | tf_op jit(solution)/shard_map/ppermute | solution.py:17
  5.9 1.6 %collective-permute-start = (bf16[64,768]{1,0:T(8,128)(2,1)S(1)}, bf16[64,768]{1,0:T(8,128)(2,1)S(1)}, u32[]{:S(2)}, u32[]{:S(2)}) collective-permute-start(bf16[64,768]{1,0:T(8,128)(2,1)S(1)} %get-tuple-element.17.refs_0_), channel_id=1, source_target_pairs={{0,8},{8,0},{16,24},{24,16},{1,9},{9,1},{17,25},{25,17},{2,10},{10... | collective-permute-start | bytes 294920 | tf_op jit(solution)/shard_map/ppermute | solution.py:17
  7.5 1.5 %collective-permute-start.8 = (bf16[144,768]{1,0:T(8,128)(2,1)S(1)}, bf16[144,768]{1,0:T(8,128)(2,1)S(1)}, u32[]{:S(2)}, u32[]{:S(2)}) collective-permute-start(bf16[144,768]{1,0:T(8,128)(2,1)S(1)} %get-tuple-element.16.refs_2_.refs_1_), channel_id=1, source_target_pairs={{0,2},{1,3},{2,0},{3,1},{4,6},{5,7},{6,4},{7,5},{8,10},{9,11},{10,... | collective-permute-start | bytes 663560 | tf_op jit(solution)/shard_map/ppermute | solution.py:17
  9.0 1.5 %collective-permute-start.7 = (bf16[144,768]{1,0:T(8,128)(2,1)S(1)}, bf16[144,768]{1,0:T(8,128)(2,1)S(1)}, u32[]{:S(2)}, u32[]{:S(2)}) collective-permute-start(bf16[144,768]{1,0:T(8,128)(2,1)S(1)} %get-tuple-element.16.refs_2_.refs_1_), channel_id=1, source_target_pairs={{0,4},{1,5},{2,6},{3,7},{4,0},{5,1},{6,2},{7,3},{8,12},{9,13},{10,... | collective-permute-start | bytes 663560 | tf_op jit(solution)/shard_map/ppermute | solution.py:17
  10.5 0.5 %collective-permute-start.6 = (bf16[144,768]{1,0:T(8,128)(2,1)S(1)}, bf16[144,768]{1,0:T(8,128)(2,1)S(1)}, u32[]{:S(2)}, u32[]{:S(2)}) collective-permute-start(bf16[144,768]{1,0:T(8,128)(2,1)S(1)} %get-tuple-element.16.refs_2_.refs_1_), channel_id=1, source_target_pairs={{0,6},{1,7},{2,4},{3,5},{4,2},{5,3},{6,0},{7,1},{8,14},{9,15},{10,... | collective-permute-start | bytes 663560 | tf_op jit(solution)/shard_map/ppermute | solution.py:17
  12.3 0.1 collective-permute-start.3
  12.5 0.5 %collective-permute-start.2 = (bf16[64,768]{1,0:T(8,128)(2,1)S(1)}, bf16[64,768]{1,0:T(8,128)(2,1)S(1)}, u32[]{:S(2)}, u32[]{:S(2)}) collective-permute-start(bf16[64,768]{1,0:T(8,128)(2,1)S(1)} %pass_on.1.refs_2_), channel_id=1, source_target_pairs={{0,8},{8,0},{16,24},{24,16},{1,9},{9,1},{17,25},{25,17},{2,10},{10... | collective-permute-start | bytes 294920 | tf_op jit(solution)/shard_map/ppermute | solution.py:17
  13.0 4.7 %collective-permute-done.2.refs_3_ = bf16[64,768]{1,0:T(8,128)(2,1)S(1)} collective-permute-done((bf16[64,768]{1,0:T(8,128)(2,1)S(1)}, bf16[64,768]{1,0:T(8,128)(2,1)S(1)}, u32[]{:S(2)}, u32[]{:S(2)}) %collective-permute-start.2) | collective-permute-done | bytes 98336 | tf_op jit(solution)/shard_map/ppermute | solution.py:17
  17.8 1.6 %collective-permute-start.5 = (bf16[256,768]{1,0:T(8,128)(2,1)S(1)}, bf16[256,768]{1,0:T(8,128)(2,1)S(1)}, u32[]{:S(2)}, u32[]{:S(2)}) collective-permute-start(bf16[256,768]{1,0:T(8,128)(2,1)S(1)} %join_text.1.refs_1_.refs_2_), channel_id=1, source_target_pairs={{0,4},{1,5},{2,6},{3,7},{4,0},{5,1},{6,2},{7,3},{8,12},{9,13},{10,... | collective-permute-start | bytes 1179656 | tf_op jit(solution)/shard_map/ppermute | solution.py:17
  19.4 1.5 %collective-permute-start.4 = (bf16[256,768]{1,0:T(8,128)(2,1)S(1)}, bf16[256,768]{1,0:T(8,128)(2,1)S(1)}, u32[]{:S(2)}, u32[]{:S(2)}) collective-permute-start(bf16[256,768]{1,0:T(8,128)(2,1)S(1)} %join_text.1.refs_1_.refs_2_), channel_id=1, source_target_pairs={{0,2},{1,3},{2,0},{3,1},{4,6},{5,7},{6,4},{7,5},{8,10},{9,11},{10,... | collective-permute-start | bytes 1179656 | tf_op jit(solution)/shard_map/ppermute | solution.py:17
  20.9 0.5 %collective-permute-start.10 = (bf16[144,768]{1,0:T(8,128)(2,1)S(1)}, bf16[144,768]{1,0:T(8,128)(2,1)S(1)}, u32[]{:S(2)}, u32[]{:S(2)}) collective-permute-start(bf16[144,768]{1,0:T(8,128)(2,1)S(1)} %collective-permute-done.7.refs_4_), channel_id=1, source_target_pairs={{0,1},{1,0},{2,3},{3,2},{4,5},{5,4},{6,7},{7,6},{8,9},{9,8},{10,11... | collective-permute-start | bytes 663560 | tf_op jit(solution)/shard_map/ppermute | solution.py:17
  21.4 1.6 %text_part.2.refs_2_ = f32[256,768]{1,0:T(8,128)S(1)} custom-call(f32[2,128]{1,0:T(2,128)S(1)} %concatenate.6.refs_1_.refs_0_, bf16[256,768]{1,0:T(8,128)(2,1)S(1)} %join_text.1.refs_1_.refs_2_, bf16[144,768]{1,0:T(8,128)(2,1)S(1)} %get-tuple-element.16.refs_2_.refs_1_, bf16[144,768]{1,0:T(8,128)(2,1)S(1)} %collective-permute-done.6.refs_3_, ...), custom_call_target="tpu_custom_call" | custom-call | flops 402653184 | bytes 2065408 | tf_op jit(solution)/shard_map/text_part/pallas_call | solution.py:33
  23.1 1.4 %text_part.3 = (f32[64,768]{1,0:T(8,128)S(1)}, f32[64,768]{1,0:T(8,128)S(1)}, f32[64,384]{1,0:T(8,128)S(1)}, f32[64,384]{1,0:T(8,128)S(1)}, f32[64,384]{1,0:T(8,128)S(1)}, /*index=5*/f32[64,384]{1,0:T(8,128)S(1)}) custom-call(f32[2,128]{1,0:T(2,128)S(1)} %concatenate.6.refs_1_.refs_0_, bf16[256,768]{1,0:T(8,128)(2,1)S(1)} %join_text.1.refs_1_.refs_2_, ...), custom_call_target="tpu_custom_call" | custom-call | flops 402653184 | bytes 2851840 | tf_op jit(solution)/shard_map/text_part/pallas_call | solution.py:33
  24.4 0.5 %collective-permute-start.12 = (f32[64,384]{1,0:T(8,128)S(1)}, f32[64,384]{1,0:T(8,128)S(1)}, u32[]{:S(2)}, u32[]{:S(2)}) collective-permute-start(f32[64,384]{1,0:T(8,128)S(1)} %get-tuple-element.19), channel_id=1, source_target_pairs={{0,8},{8,0},{16,24},{24,16},{1,9},{9,1},{17,25},{25,17},{2,10},{10... | collective-permute-start | bytes 294920 | tf_op jit(solution)/shard_map/ppermute | solution.py:17
  25.0 1.6 %collective-permute-start.13 = (f32[64,384]{1,0:T(8,128)S(1)}, f32[64,384]{1,0:T(8,128)S(1)}, u32[]{:S(2)}, u32[]{:S(2)}) collective-permute-start(f32[64,384]{1,0:T(8,128)S(1)} %get-tuple-element.21), channel_id=1, source_target_pairs={{0,8},{8,0},{16,24},{24,16},{1,9},{9,1},{17,25},{25,17},{2,10},{10... | collective-permute-start | bytes 294920 | tf_op jit(solution)/shard_map/ppermute | solution.py:17
  26.5 3.6 %collective-permute-done.12.refs_1_ = f32[64,384]{1,0:T(8,128)S(1)} collective-permute-done((f32[64,384]{1,0:T(8,128)S(1)}, f32[64,384]{1,0:T(8,128)S(1)}, u32[]{:S(2)}, u32[]{:S(2)}) %collective-permute-start.12) | collective-permute-done | bytes 98336 | tf_op jit(solution)/shard_map/ppermute | solution.py:17
  30.1 0.9 %collective-permute-start.17 = (f32[64,384]{1,0:T(8,128)S(1)}, f32[64,384]{1,0:T(8,128)S(1)}, u32[]{:S(2)}, u32[]{:S(2)}) collective-permute-start(f32[64,384]{1,0:T(8,128)S(1)} %sum_near.2.refs_5_.refs_3_), channel_id=1, source_target_pairs={{0,16},{8,24},{16,0},{24,8},{1,17},{9,25},{17,1},{25,9},{2,18},{10... | collective-permute-start | bytes 294920 | tf_op jit(solution)/shard_map/ppermute | solution.py:17
  31.0 0.8 %collective-permute-done.13.refs_1_ = f32[64,384]{1,0:T(8,128)S(1)} collective-permute-done((f32[64,384]{1,0:T(8,128)S(1)}, f32[64,384]{1,0:T(8,128)S(1)}, u32[]{:S(2)}, u32[]{:S(2)}) %collective-permute-start.13) | collective-permute-done | bytes 98336 | tf_op jit(solution)/shard_map/ppermute | solution.py:17
  31.8 1.4 %collective-permute-start.18 = (f32[64,384]{1,0:T(8,128)S(1)}, f32[64,384]{1,0:T(8,128)S(1)}, u32[]{:S(2)}, u32[]{:S(2)}) collective-permute-start(f32[64,384]{1,0:T(8,128)S(1)} %sum_near.3.refs_6_.refs_4_), channel_id=1, source_target_pairs={{0,16},{8,24},{16,0},{24,8},{1,17},{9,25},{17,1},{25,9},{2,18},{10... | collective-permute-start | bytes 294920 | tf_op jit(solution)/shard_map/ppermute | solution.py:17
  33.2 0.6 %collective-permute-start.14 = (bf16[128,768]{1,0:T(8,128)(2,1)S(1)}, bf16[128,768]{1,0:T(8,128)(2,1)S(1)}, u32[]{:S(2)}, u32[]{:S(2)}) collective-permute-start(bf16[128,768]{1,0:T(8,128)(2,1)S(1)} %get-tuple-element.23), channel_id=1, source_target_pairs={{0,2},{1,3},{2,0},{3,1},{4,6},{5,7},{6,4},{7,5},{8,10},{9,11},{10,... | collective-permute-start | bytes 589832 | tf_op jit(solution)/shard_map/ppermute | solution.py:17
  33.8 0.7 %collective-permute-start.15 = (bf16[128,768]{1,0:T(8,128)(2,1)S(1)}, bf16[128,768]{1,0:T(8,128)(2,1)S(1)}, u32[]{:S(2)}, u32[]{:S(2)}) collective-permute-start(bf16[128,768]{1,0:T(8,128)(2,1)S(1)} %get-tuple-element.24), channel_id=1, source_target_pairs={{0,4},{1,5},{2,6},{3,7},{4,0},{5,1},{6,2},{7,3},{8,12},{9,13},{10,... | collective-permute-start | bytes 589832 | tf_op jit(solution)/shard_map/ppermute | solution.py:17
  34.5 1.0 %collective-permute-start.19 = (f32[64,768]{1,0:T(8,128)S(1)}, f32[64,768]{1,0:T(8,128)S(1)}, u32[]{:S(2)}, u32[]{:S(2)}) collective-permute-start(f32[64,768]{1,0:T(8,128)S(1)} %get-tuple-element.27), channel_id=1, source_target_pairs={{0,8},{8,0},{16,24},{24,16},{1,9},{9,1},{17,25},{25,17},{2,10},{10... | collective-permute-start | bytes 589832 | tf_op jit(solution)/shard_map/ppermute | solution.py:17
  35.6 1.0 %speech_part.6.refs_2_ = f32[128,768]{1,0:T(8,128)S(1)} custom-call(f32[2,128]{1,0:T(2,128)S(1)} %concatenate.6.refs_1_.refs_0_, bf16[144,768]{1,0:T(8,128)(2,1)S(1)} %collective-permute-done.3.refs_4_.refs_3_.refs_1_, bf16[256,768]{1,0:T(8,128)(2,1)S(1)} %join_text.1.refs_1_.refs_2_, bf16[256,768]{1,0:T(8,128)(2,1)S(1)} %collective-permute-done.4.refs_3_.refs_1_, ...), custom_call_target="tpu_custom_call" | custom-call | flops 3019898880 | bytes 1795072 | tf_op jit(solution)/shard_map/speech_part/pallas_call | solution.py:33
  36.6 1.0 %speech_part.4.refs_2_ = f32[128,768]{1,0:T(8,128)S(1)} custom-call(f32[2,128]{1,0:T(2,128)S(1)} %concatenate.6.refs_1_.refs_0_, bf16[144,768]{1,0:T(8,128)(2,1)S(1)} %get-tuple-element.16.refs_2_.refs_1_, bf16[256,768]{1,0:T(8,128)(2,1)S(1)} %join_text.1.refs_1_.refs_2_, bf16[256,768]{1,0:T(8,128)(2,1)S(1)} %collective-permute-done.4.refs_3_.refs_1_, ...), custom_call_target="tpu_custom_call" | custom-call | flops 3019898880 | bytes 1795072 | tf_op jit(solution)/shard_map/speech_part/pallas_call | solution.py:33
  37.6 1.4 %collective-permute-done.14.refs_3_ = bf16[128,768]{1,0:T(8,128)(2,1)S(1)} collective-permute-done((bf16[128,768]{1,0:T(8,128)(2,1)S(1)}, bf16[128,768]{1,0:T(8,128)(2,1)S(1)}, u32[]{:S(2)}, u32[]{:S(2)}) %collective-permute-start.14) | collective-permute-done | bytes 196640 | tf_op jit(solution)/shard_map/ppermute | solution.py:17
  39.0 0.5 %collective-permute-done.15.refs_4_ = bf16[128,768]{1,0:T(8,128)(2,1)S(1)} collective-permute-done((bf16[128,768]{1,0:T(8,128)(2,1)S(1)}, bf16[128,768]{1,0:T(8,128)(2,1)S(1)}, u32[]{:S(2)}, u32[]{:S(2)}) %collective-permute-start.15) | collective-permute-done | bytes 196640 | tf_op jit(solution)/shard_map/ppermute | solution.py:17
  39.5 0.5 %speech_part.7 = f32[128,768]{1,0:T(8,128)S(1)} custom-call(f32[2,128]{1,0:T(2,128)S(1)} %concatenate.6.refs_1_.refs_0_, bf16[144,768]{1,0:T(8,128)(2,1)S(1)} %collective-permute-done.3.refs_4_.refs_3_.refs_1_, f32[128,768]{1,0:T(8,128)S(1)} %speech_part.6.refs_2_, bf16[128,768]{1,0:T(8,128)(2,1)S(1)} %collective-permute-done.14.refs_3_, ...), custom_call_target="tpu_custom_call" | custom-call | flops 1006632960 | bytes 1401856 | tf_op jit(solution)/shard_map/speech_part/pallas_call | solution.py:33
  40.1 1.1 %collective-permute-done.18.refs_2_ = f32[64,384]{1,0:T(8,128)S(1)} collective-permute-done((f32[64,384]{1,0:T(8,128)S(1)}, f32[64,384]{1,0:T(8,128)S(1)}, u32[]{:S(2)}, u32[]{:S(2)}) %collective-permute-start.18) | collective-permute-done | bytes 98336 | tf_op jit(solution)/shard_map/ppermute | solution.py:17
  41.3 0.5 %speech_part.5.refs_1_ = f32[128,768]{1,0:T(8,128)S(1)} custom-call(f32[2,128]{1,0:T(2,128)S(1)} %concatenate.6.refs_1_.refs_0_, bf16[144,768]{1,0:T(8,128)(2,1)S(1)} %get-tuple-element.16.refs_2_.refs_1_, f32[128,768]{1,0:T(8,128)S(1)} %speech_part.4.refs_2_, bf16[128,768]{1,0:T(8,128)(2,1)S(1)} %collective-permute-done.14.refs_3_, ...), custom_call_target="tpu_custom_call" | custom-call | flops 1006632960 | bytes 1401856 | tf_op jit(solution)/shard_map/speech_part/pallas_call | solution.py:33
  41.8 1.1 %collective-permute-done.19.refs_5_ = f32[64,768]{1,0:T(8,128)S(1)} collective-permute-done((f32[64,768]{1,0:T(8,128)S(1)}, f32[64,768]{1,0:T(8,128)S(1)}, u32[]{:S(2)}, u32[]{:S(2)}) %collective-permute-start.19) | collective-permute-done | bytes 196640 | tf_op jit(solution)/shard_map/ppermute | solution.py:17
  42.9 1.1 %finish.1 = (f32[128,768]{1,0:T(8,128)}, f32[64,768]{1,0:T(8,128)}) custom-call(bf16[128,768]{1,0:T(8,128)(2,1)S(1)} %get-tuple-element.15.refs_0_, f32[128,768]{1,0:T(8,128)S(1)} %speech_part.5.refs_1_, f32[128,768]{1,0:T(8,128)S(1)} %collective-permute-done.16.refs_2_, bf16[64,768]{1,0:T(8,128)(2,1)S(1)} %get-tuple-element.25.refs_3_, ...), custom_call_target="tpu_custom_call" | custom-call | bytes 2064384 | tf_op jit(solution)/shard_map/finish/pallas_call | solution.py:33
  (24 shorter events, 0.4 us)
Async XLA Ops:
  1.8 10.5 %collective-permute-start.1 = (bf16[64,768]{1,0:T(8,128)(2,1)S(1)}, bf16[64,768]{1,0:T(8,128)(2,1)S(1)}, u32[]{:S(2)}, u32[]{:S(2)}) collective-permute-start(bf16[64,768]{1,0:T(8,128)(2,1)S(1)} %get-tuple-element.17.refs_0_), channel_id=1, source_target_pairs={{0,16},{8,24},{16,0},{24,8},{1,17},{9,25},{17,1},{25,9},{2,18},{10... | collective-permute-start | bytes 294920 | tf_op jit(solution)/shard_map/ppermute | solution.py:17
  5.9 6.5 %collective-permute-start = (bf16[64,768]{1,0:T(8,128)(2,1)S(1)}, bf16[64,768]{1,0:T(8,128)(2,1)S(1)}, u32[]{:S(2)}, u32[]{:S(2)}) collective-permute-start(bf16[64,768]{1,0:T(8,128)(2,1)S(1)} %get-tuple-element.17.refs_0_), channel_id=1, source_target_pairs={{0,8},{8,0},{16,24},{24,16},{1,9},{9,1},{17,25},{25,17},{2,10},{10... | collective-permute-start | bytes 294920 | tf_op jit(solution)/shard_map/ppermute | solution.py:17
  7.5 13.3 %collective-permute-start.8 = (bf16[144,768]{1,0:T(8,128)(2,1)S(1)}, bf16[144,768]{1,0:T(8,128)(2,1)S(1)}, u32[]{:S(2)}, u32[]{:S(2)}) collective-permute-start(bf16[144,768]{1,0:T(8,128)(2,1)S(1)} %get-tuple-element.16.refs_2_.refs_1_), channel_id=1, source_target_pairs={{0,2},{1,3},{2,0},{3,1},{4,6},{5,7},{6,4},{7,5},{8,10},{9,11},{10,... | collective-permute-start | bytes 663560 | tf_op jit(solution)/shard_map/ppermute | solution.py:17
  9.0 11.9 %collective-permute-start.7 = (bf16[144,768]{1,0:T(8,128)(2,1)S(1)}, bf16[144,768]{1,0:T(8,128)(2,1)S(1)}, u32[]{:S(2)}, u32[]{:S(2)}) collective-permute-start(bf16[144,768]{1,0:T(8,128)(2,1)S(1)} %get-tuple-element.16.refs_2_.refs_1_), channel_id=1, source_target_pairs={{0,4},{1,5},{2,6},{3,7},{4,0},{5,1},{6,2},{7,3},{8,12},{9,13},{10,... | collective-permute-start | bytes 663560 | tf_op jit(solution)/shard_map/ppermute | solution.py:17
  10.5 10.9 %collective-permute-start.6 = (bf16[144,768]{1,0:T(8,128)(2,1)S(1)}, bf16[144,768]{1,0:T(8,128)(2,1)S(1)}, u32[]{:S(2)}, u32[]{:S(2)}) collective-permute-start(bf16[144,768]{1,0:T(8,128)(2,1)S(1)} %get-tuple-element.16.refs_2_.refs_1_), channel_id=1, source_target_pairs={{0,6},{1,7},{2,4},{3,5},{4,2},{5,3},{6,0},{7,1},{8,14},{9,15},{10,... | collective-permute-start | bytes 663560 | tf_op jit(solution)/shard_map/ppermute | solution.py:17
  12.3 5.4 %collective-permute-start.3 = (bf16[144,768]{1,0:T(8,128)(2,1)S(1)}, bf16[144,768]{1,0:T(8,128)(2,1)S(1)}, u32[]{:S(2)}, u32[]{:S(2)}) collective-permute-start(bf16[144,768]{1,0:T(8,128)(2,1)S(1)} %get-tuple-element.16.refs_2_.refs_1_), channel_id=1, source_target_pairs={{0,1},{1,0},{2,3},{3,2},{4,5},{5,4},{6,7},{7,6},{8,9},{9,8},{10,11... | collective-permute-start | bytes 663560 | tf_op jit(solution)/shard_map/ppermute | solution.py:17
  12.5 5.3 %collective-permute-start.2 = (bf16[64,768]{1,0:T(8,128)(2,1)S(1)}, bf16[64,768]{1,0:T(8,128)(2,1)S(1)}, u32[]{:S(2)}, u32[]{:S(2)}) collective-permute-start(bf16[64,768]{1,0:T(8,128)(2,1)S(1)} %pass_on.1.refs_2_), channel_id=1, source_target_pairs={{0,8},{8,0},{16,24},{24,16},{1,9},{9,1},{17,25},{25,17},{2,10},{10... | collective-permute-start | bytes 294920 | tf_op jit(solution)/shard_map/ppermute | solution.py:17
  17.8 15.4 %collective-permute-start.5 = (bf16[256,768]{1,0:T(8,128)(2,1)S(1)}, bf16[256,768]{1,0:T(8,128)(2,1)S(1)}, u32[]{:S(2)}, u32[]{:S(2)}) collective-permute-start(bf16[256,768]{1,0:T(8,128)(2,1)S(1)} %join_text.1.refs_1_.refs_2_), channel_id=1, source_target_pairs={{0,4},{1,5},{2,6},{3,7},{4,0},{5,1},{6,2},{7,3},{8,12},{9,13},{10,... | collective-permute-start | bytes 1179656 | tf_op jit(solution)/shard_map/ppermute | solution.py:17
  19.4 13.8 %collective-permute-start.4 = (bf16[256,768]{1,0:T(8,128)(2,1)S(1)}, bf16[256,768]{1,0:T(8,128)(2,1)S(1)}, u32[]{:S(2)}, u32[]{:S(2)}) collective-permute-start(bf16[256,768]{1,0:T(8,128)(2,1)S(1)} %join_text.1.refs_1_.refs_2_), channel_id=1, source_target_pairs={{0,2},{1,3},{2,0},{3,1},{4,6},{5,7},{6,4},{7,5},{8,10},{9,11},{10,... | collective-permute-start | bytes 1179656 | tf_op jit(solution)/shard_map/ppermute | solution.py:17
  20.8 2.2 %collective-permute-start.11 = (bf16[144,768]{1,0:T(8,128)(2,1)S(1)}, bf16[144,768]{1,0:T(8,128)(2,1)S(1)}, u32[]{:S(2)}, u32[]{:S(2)}) collective-permute-start(bf16[144,768]{1,0:T(8,128)(2,1)S(1)} %collective-permute-done.8.refs_5_), channel_id=1, source_target_pairs={{0,1},{1,0},{2,3},{3,2},{4,5},{5,4},{6,7},{7,6},{8,9},{9,8},{10,11... | collective-permute-start | bytes 663560 | tf_op jit(solution)/shard_map/ppermute | solution.py:17
  20.9 2.2 %collective-permute-start.10 = (bf16[144,768]{1,0:T(8,128)(2,1)S(1)}, bf16[144,768]{1,0:T(8,128)(2,1)S(1)}, u32[]{:S(2)}, u32[]{:S(2)}) collective-permute-start(bf16[144,768]{1,0:T(8,128)(2,1)S(1)} %collective-permute-done.7.refs_4_), channel_id=1, source_target_pairs={{0,1},{1,0},{2,3},{3,2},{4,5},{5,4},{6,7},{7,6},{8,9},{9,8},{10,11... | collective-permute-start | bytes 663560 | tf_op jit(solution)/shard_map/ppermute | solution.py:17
  21.4 1.7 %collective-permute-start.9 = (bf16[144,768]{1,0:T(8,128)(2,1)S(1)}, bf16[144,768]{1,0:T(8,128)(2,1)S(1)}, u32[]{:S(2)}, u32[]{:S(2)}) collective-permute-start(bf16[144,768]{1,0:T(8,128)(2,1)S(1)} %collective-permute-done.6.refs_3_), channel_id=1, source_target_pairs={{0,1},{1,0},{2,3},{3,2},{4,5},{5,4},{6,7},{7,6},{8,9},{9,8},{10,11... | collective-permute-start | bytes 663560 | tf_op jit(solution)/shard_map/ppermute | solution.py:17
  24.4 5.7 %collective-permute-start.12 = (f32[64,384]{1,0:T(8,128)S(1)}, f32[64,384]{1,0:T(8,128)S(1)}, u32[]{:S(2)}, u32[]{:S(2)}) collective-permute-start(f32[64,384]{1,0:T(8,128)S(1)} %get-tuple-element.19), channel_id=1, source_target_pairs={{0,8},{8,0},{16,24},{24,16},{1,9},{9,1},{17,25},{25,17},{2,10},{10... | collective-permute-start | bytes 294920 | tf_op jit(solution)/shard_map/ppermute | solution.py:17
  25.0 6.8 %collective-permute-start.13 = (f32[64,384]{1,0:T(8,128)S(1)}, f32[64,384]{1,0:T(8,128)S(1)}, u32[]{:S(2)}, u32[]{:S(2)}) collective-permute-start(f32[64,384]{1,0:T(8,128)S(1)} %get-tuple-element.21), channel_id=1, source_target_pairs={{0,8},{8,0},{16,24},{24,16},{1,9},{9,1},{17,25},{25,17},{2,10},{10... | collective-permute-start | bytes 294920 | tf_op jit(solution)/shard_map/ppermute | solution.py:17
  30.1 10.0 %collective-permute-start.17 = (f32[64,384]{1,0:T(8,128)S(1)}, f32[64,384]{1,0:T(8,128)S(1)}, u32[]{:S(2)}, u32[]{:S(2)}) collective-permute-start(f32[64,384]{1,0:T(8,128)S(1)} %sum_near.2.refs_5_.refs_3_), channel_id=1, source_target_pairs={{0,16},{8,24},{16,0},{24,8},{1,17},{9,25},{17,1},{25,9},{2,18},{10... | collective-permute-start | bytes 294920 | tf_op jit(solution)/shard_map/ppermute | solution.py:17
  31.8 9.5 %collective-permute-start.18 = (f32[64,384]{1,0:T(8,128)S(1)}, f32[64,384]{1,0:T(8,128)S(1)}, u32[]{:S(2)}, u32[]{:S(2)}) collective-permute-start(f32[64,384]{1,0:T(8,128)S(1)} %sum_near.3.refs_6_.refs_4_), channel_id=1, source_target_pairs={{0,16},{8,24},{16,0},{24,8},{1,17},{9,25},{17,1},{25,9},{2,18},{10... | collective-permute-start | bytes 294920 | tf_op jit(solution)/shard_map/ppermute | solution.py:17
  33.2 5.7 %collective-permute-start.14 = (bf16[128,768]{1,0:T(8,128)(2,1)S(1)}, bf16[128,768]{1,0:T(8,128)(2,1)S(1)}, u32[]{:S(2)}, u32[]{:S(2)}) collective-permute-start(bf16[128,768]{1,0:T(8,128)(2,1)S(1)} %get-tuple-element.23), channel_id=1, source_target_pairs={{0,2},{1,3},{2,0},{3,1},{4,6},{5,7},{6,4},{7,5},{8,10},{9,11},{10,... | collective-permute-start | bytes 589832 | tf_op jit(solution)/shard_map/ppermute | solution.py:17
  33.8 5.7 %collective-permute-start.15 = (bf16[128,768]{1,0:T(8,128)(2,1)S(1)}, bf16[128,768]{1,0:T(8,128)(2,1)S(1)}, u32[]{:S(2)}, u32[]{:S(2)}) collective-permute-start(bf16[128,768]{1,0:T(8,128)(2,1)S(1)} %get-tuple-element.24), channel_id=1, source_target_pairs={{0,4},{1,5},{2,6},{3,7},{4,0},{5,1},{6,2},{7,3},{8,12},{9,13},{10,... | collective-permute-start | bytes 589832 | tf_op jit(solution)/shard_map/ppermute | solution.py:17
  34.5 8.4 %collective-permute-start.19 = (f32[64,768]{1,0:T(8,128)S(1)}, f32[64,768]{1,0:T(8,128)S(1)}, u32[]{:S(2)}, u32[]{:S(2)}) collective-permute-start(f32[64,768]{1,0:T(8,128)S(1)} %get-tuple-element.27), channel_id=1, source_target_pairs={{0,8},{8,0},{16,24},{24,16},{1,9},{9,1},{17,25},{25,17},{2,10},{10... | collective-permute-start | bytes 589832 | tf_op jit(solution)/shard_map/ppermute | solution.py:17
  40.0 2.8 %collective-permute-start.16 = (f32[128,768]{1,0:T(8,128)S(1)}, f32[128,768]{1,0:T(8,128)S(1)}, u32[]{:S(2)}, u32[]{:S(2)}) collective-permute-start(f32[128,768]{1,0:T(8,128)S(1)} %speech_part.7), channel_id=1, source_target_pairs={{0,1},{1,0},{2,3},{3,2},{4,5},{5,4},{6,7},{7,6},{8,9},{9,8},{10,11... | collective-permute-start | bytes 1179656 | tf_op jit(solution)/shard_map/ppermute | solution.py:17

commit v11 on v7

--- a/solution.py
+++ b/solution.py
@@ -129,9 +129,12 @@
             coef = coefficients(dot_rows(text, chunk), match, sharp, shift)
             part = jnp.dot(coef, chunk, preferred_element_type=jnp.float32)
             total = part if total is None else total + part
-    size = outs[0].shape[0]
-    for k, out in enumerate(outs):
-        out[...] = total[k * size : (k + 1) * size, :]
+    row, at = 0, 0
+    for out in outs:
+        out[...] = total[row : row + out.shape[0], at : at + out.shape[1]]
+        at += out.shape[1]
+        if at == total.shape[1]:
+            row, at = row + out.shape[0], 0
 
 
 def speech_part_body(rows, own_text, has_start, masks, *refs):
@@ -159,9 +162,23 @@
     out[...] = total
 
 
-def sum_near_body(mine, came, kept, total, kept_out):
+def sum_keep_body(mine, came, kept, total, kept_out):
     total[...] = mine[...] + came[...]
     kept_out[...] = kept[...]
+
+
+def add_sides_body(*refs):
+    out = refs[-1]
+    sides = [ref for ref in refs[:-1] if ref.shape != out.shape]
+    whole = [ref for ref in refs[:-1] if ref.shape == out.shape]
+    at = 0
+    for ref in sides:
+        columns = slice(at, at + ref.shape[1])
+        total = ref[...]
+        for other in whole:
+            total = total + other[:, columns]
+        out[:, columns] = total
+        at += ref.shape[1]
 
 
 def sum_body(*refs):
@@ -254,21 +271,28 @@
         return call(body, outs, operands, (), work, temporary, "text_part")
 
     half = text_part([f32(column, width)], [speech], [])
-    parts = list(text_part([f32(own_text, width)] * groups, [other], half))
-
-    text_back = [parts[0]]
-    for bit in [1 << i for i in range(groups.bit_length() - 1)]:
-        for k in reversed(range(bit, groups, 2 * bit)):
-            came = exchanged(parts[k], "group", bit)
-            if k == bit:
-                text_back.append(came)
-            else:
-                parts[k - bit], parts[bit] = call(
-                    sum_near_body,
-                    [f32(own_text, width)] * 2,
-                    [parts[k - bit], came, parts[bit]],
-                    name="sum_near",
-                )
+    sides = 2
+    side = f32(own_text, width // sides)
+    outs = [f32(own_text, width)] * (groups // 2) + [side] * (groups // 2 * sides)
+    parts = list(text_part(outs, [other], half))
+    far = [parts[groups // 2 + i * sides :][:sides] for i in range(groups // 2)]
+
+    bit = 1
+    while bit < groups // 2:
+        for k in reversed(range(bit, groups // 2, 2 * bit)):
+            came = [exchanged(v, "group", bit) for v in far[k]]
+            mine = far[k - bit]
+            first, parts[bit] = call(
+                sum_keep_body,
+                [side, f32(own_text, width)],
+                [mine[0], came[0], parts[bit]],
+                name="sum_near",
+            )
+            last = call(sum_body, side, [mine[1], came[1]], name="sum_near")
+            far[k - bit] = [first, last]
+        bit *= 2
+    from_far = [exchanged(v, "group", groups // 2) for v in far[0]]
+    from_near = [exchanged(parts[k], "group", k) for k in range(1, groups // 2)]
 
     def speech_part(block, start, columns, texts, after=()):
         body = functools.partial(speech_part_body, rows, own_text, bool(start), columns)
@@ -276,15 +300,22 @@
         work = 40 * rows * column * len(columns) * width
         return call(body, f32(rows, width), operands, after, work, temporary, "speech_part")
 
-    near = [[0, *masks], [text, *text_near], (parts[groups // 2],)]
+    near = [[0, *masks], [text, *text_near], tuple(far[0])]
     away = speech_part(other[0 : rows + MARK_ROWS], [], *near)
     home = speech_part(speech_own, [], *near)
     if square:
-        text_far = far_halves(text_near, column // 2, (parts[groups // 2],))
+        text_far = far_halves(text_near, column // 2, tuple(far[0]))
         away = speech_part(other[0 : rows + MARK_ROWS], [away], [3], text_far)
         home = speech_part(speech_own, [home], [3], text_far)
     back = exchanged(away, "member", 1)
-    text_back = call(sum_body, f32(own_text, width), text_back[::-1], (), EARLY, name="text_sum")
+    text_back = call(
+        add_sides_body,
+        f32(own_text, width),
+        [*from_far, *from_near, parts[0]],
+        (),
+        EARLY,
+        name="text_sum",
+    )
     speech_grad, text_grad = call(
         finish_body,
         [f32(rows, width), f32(own_text, width)],

time: 42.3 us -> 43.8 us (1.035)
  starting transfers between devices: 17.9 us -> 19.9 us
    ppermute x15 -> x17, starting transfers between devices: 17.9 us -> 19.9 us  [exchanged(): return lax.ppermute(value, axis, [(i, i ^ mask) for i in range(size)])]
    ppermute x15 -> x17, waiting for transfers between devices: 15 us -> 14.6 us  [exchanged(): return lax.ppermute(value, axis, [(i, i ^ mask) for i in range(size)])]
    pallas_call x12 -> x13, Pallas kernels: 5.86 us -> 5.86 us  [call(): pl.pallas_call(whole, out_shape=out_shape, in_specs=specs, out_specs=jax....]
  transfers between devices with their start and end apart: 15 -> 17, of which waited for: 7 -> 8; matrix products, arithmetic and copies ran while one was open for 0% -> 0% of each run, Pallas kernels for 11% -> 11%
where the time goes in v11:
time: 43.8 us; the launch traced here: 43.7 us
  starting transfers between devices  19.9 us (45%)
  waiting for transfers between devices  14.6 us (33%)
  Pallas kernels  7.04 us (16%)
  between operations  2.08 us (5%)
    ppermute x17, starting transfers between devices, exchanged(): return lax.ppermute(value, axis, [(i, i ^ mask) for i in range(size)])  19.9 us
    ppermute x17, waiting for transfers between devices, exchanged(): return lax.ppermute(value, axis, [(i, i ^ mask) for i in range(size)])  14.6 us
    pallas_call x13, Pallas kernels, call(): pl.pallas_call(whole, out_shape=out_shape, in_specs=specs, out_specs=jax....  5.86 us
    pallas_call x1, Pallas kernels, shards(): pl.pallas_call(prepare_body, out_shape=[bf16(rows + MARK_ROWS, width), bf...  1.18 us
  transfers between devices with their start and end apart: 17, of which 8 were waited for; matrix products, arithmetic and copies ran while one was open for 0% of the time, Pallas kernels for 11%

profile of v11, /device:TPU:0, one launch (start us, length us, event | category | flops | bytes accessed | tf_op | source)
XLA Modules:
  0.0 43.7 jit_solution(10007277224855780532)
XLA Ops:
  0.6 1.2 %unit_rows.1 = (bf16[144,768]{1,0:T(8,128)(2,1)S(1)}, bf16[64,768]{1,0:T(8,128)(2,1)S(1)}, bf16[128,768]{1,0:T(8,128)(2,1)S(1)}, bf16[64,768]{1,0:T(8,128)(2,1)S(1)}) custom-call(bf16[128,768]{1,0:T(8,128)(2,1)} %refs_0_.1, bf16[64,768]{1,0:T(8,128)(2,1)} %refs_1_.1, s32[1,128]{1,0:T(1,128)} %bitcast.3), custom_call_target="tpu_custom_call" | custom-call | tf_op jit(solution)/shard_map/unit_rows/pallas_call | solution.py:220
  1.8 4.1 %collective-permute-start.1 = (bf16[64,768]{1,0:T(8,128)(2,1)S(1)}, bf16[64,768]{1,0:T(8,128)(2,1)S(1)}, u32[]{:S(2)}, u32[]{:S(2)}) collective-permute-start(bf16[64,768]{1,0:T(8,128)(2,1)S(1)} %get-tuple-element.20.refs_0_), channel_id=1, source_target_pairs={{0,16},{8,24},{16,0},{24,8},{1,17},{9,25},{17,1},{25,9},{2,18},{10... | collective-permute-start | bytes 294920 | tf_op jit(solution)/shard_map/ppermute | solution.py:17
  5.9 1.5 %collective-permute-start.3 = (bf16[144,768]{1,0:T(8,128)(2,1)S(1)}, bf16[144,768]{1,0:T(8,128)(2,1)S(1)}, u32[]{:S(2)}, u32[]{:S(2)}) collective-permute-start(bf16[144,768]{1,0:T(8,128)(2,1)S(1)} %get-tuple-element.19.refs_4_.refs_1_), channel_id=1, source_target_pairs={{0,2},{1,3},{2,0},{3,1},{4,6},{5,7},{6,4},{7,5},{8,10},{9,11},{10,... | collective-permute-start | bytes 663560 | tf_op jit(solution)/shard_map/ppermute | solution.py:17
  7.4 1.5 %collective-permute-start.4 = (bf16[144,768]{1,0:T(8,128)(2,1)S(1)}, bf16[144,768]{1,0:T(8,128)(2,1)S(1)}, u32[]{:S(2)}, u32[]{:S(2)}) collective-permute-start(bf16[144,768]{1,0:T(8,128)(2,1)S(1)} %get-tuple-element.19.refs_4_.refs_1_), channel_id=1, source_target_pairs={{0,4},{1,5},{2,6},{3,7},{4,0},{5,1},{6,2},{7,3},{8,12},{9,13},{10,... | collective-permute-start | bytes 663560 | tf_op jit(solution)/shard_map/ppermute | solution.py:17
  8.9 0.5 %collective-permute-start.5 = (bf16[144,768]{1,0:T(8,128)(2,1)S(1)}, bf16[144,768]{1,0:T(8,128)(2,1)S(1)}, u32[]{:S(2)}, u32[]{:S(2)}) collective-permute-start(bf16[144,768]{1,0:T(8,128)(2,1)S(1)} %get-tuple-element.19.refs_4_.refs_1_), channel_id=1, source_target_pairs={{0,6},{1,7},{2,4},{3,5},{4,2},{5,3},{6,0},{7,1},{8,14},{9,15},{10,... | collective-permute-start | bytes 663560 | tf_op jit(solution)/shard_map/ppermute | solution.py:17
  9.4 1.6 %collective-permute-start = (bf16[64,768]{1,0:T(8,128)(2,1)S(1)}, bf16[64,768]{1,0:T(8,128)(2,1)S(1)}, u32[]{:S(2)}, u32[]{:S(2)}) collective-permute-start(bf16[64,768]{1,0:T(8,128)(2,1)S(1)} %get-tuple-element.20.refs_0_), channel_id=1, source_target_pairs={{0,8},{8,0},{16,24},{24,16},{1,9},{9,1},{17,25},{25,17},{2,10},{10... | collective-permute-start | bytes 294920 | tf_op jit(solution)/shard_map/ppermute | solution.py:17
  12.4 0.5 %collective-permute-start.2 = (bf16[64,768]{1,0:T(8,128)(2,1)S(1)}, bf16[64,768]{1,0:T(8,128)(2,1)S(1)}, u32[]{:S(2)}, u32[]{:S(2)}) collective-permute-start(bf16[64,768]{1,0:T(8,128)(2,1)S(1)} %pass_on.1.refs_2_), channel_id=1, source_target_pairs={{0,8},{8,0},{16,24},{24,16},{1,9},{9,1},{17,25},{25,17},{2,10},{10... | collective-permute-start | bytes 294920 | tf_op jit(solution)/shard_map/ppermute | solution.py:17
  12.9 1.8 %collective-permute-done.refs_1_ = bf16[64,768]{1,0:T(8,128)(2,1)S(1)} collective-permute-done((bf16[64,768]{1,0:T(8,128)(2,1)S(1)}, bf16[64,768]{1,0:T(8,128)(2,1)S(1)}, u32[]{:S(2)}, u32[]{:S(2)}) %collective-permute-start) | collective-permute-done | bytes 98336 | tf_op jit(solution)/shard_map/ppermute | solution.py:17
  14.7 2.4 %collective-permute-done.2.refs_3_ = bf16[64,768]{1,0:T(8,128)(2,1)S(1)} collective-permute-done((bf16[64,768]{1,0:T(8,128)(2,1)S(1)}, bf16[64,768]{1,0:T(8,128)(2,1)S(1)}, u32[]{:S(2)}, u32[]{:S(2)}) %collective-permute-start.2) | collective-permute-done | bytes 98336 | tf_op jit(solution)/shard_map/ppermute | solution.py:17
  17.1 1.7 %collective-permute-done.4.refs_6_ = bf16[144,768]{1,0:T(8,128)(2,1)S(1)} collective-permute-done((bf16[144,768]{1,0:T(8,128)(2,1)S(1)}, bf16[144,768]{1,0:T(8,128)(2,1)S(1)}, u32[]{:S(2)}, u32[]{:S(2)}) %collective-permute-start.4) | collective-permute-done | bytes 221216 | tf_op jit(solution)/shard_map/ppermute | solution.py:17
  18.8 0.1 join_rows.1
  18.9 1.3 %collective-permute-start.6 = (bf16[256,768]{1,0:T(8,128)(2,1)S(1)}, bf16[256,768]{1,0:T(8,128)(2,1)S(1)}, u32[]{:S(2)}, u32[]{:S(2)}) collective-permute-start(bf16[256,768]{1,0:T(8,128)(2,1)S(1)} %get-tuple-element.21.refs_1_.refs_2_), channel_id=1, source_target_pairs={{0,2},{1,3},{2,0},{3,1},{4,6},{5,7},{6,4},{7,5},{8,10},{9,11},{10,... | collective-permute-start | bytes 1179656 | tf_op jit(solution)/shard_map/ppermute | solution.py:17
  20.2 0.8 %collective-permute-start.7 = (bf16[256,768]{1,0:T(8,128)(2,1)S(1)}, bf16[256,768]{1,0:T(8,128)(2,1)S(1)}, u32[]{:S(2)}, u32[]{:S(2)}) collective-permute-start(bf16[256,768]{1,0:T(8,128)(2,1)S(1)} %get-tuple-element.21.refs_1_.refs_2_), channel_id=1, source_target_pairs={{0,4},{1,5},{2,6},{3,7},{4,0},{5,1},{6,2},{7,3},{8,12},{9,13},{10,... | collective-permute-start | bytes 1179656 | tf_op jit(solution)/shard_map/ppermute | solution.py:17
  21.1 0.8 %text_part.2.refs_2_ = f32[256,768]{1,0:T(8,128)S(1)} custom-call(f32[2,128]{1,0:T(2,128)S(1)} %concatenate.6.refs_1_.refs_0_, bf16[256,768]{1,0:T(8,128)(2,1)S(1)} %get-tuple-element.21.refs_1_.refs_2_, bf16[576,768]{1,0:T(8,128)(2,1)S(1)} %get-tuple-element.22.refs_2_), custom_call_target="tpu_custom_call" | custom-call | flops 402653184 | bytes 2065408 | tf_op jit(solution)/shard_map/text_part/pallas_call | solution.py:33
  21.8 0.8 %text_part.3 = (f32[64,768]{1,0:T(8,128)S(1)}, f32[64,768]{1,0:T(8,128)S(1)}, f32[64,384]{1,0:T(8,128)S(1)}, f32[64,384]{1,0:T(8,128)S(1)}, f32[64,384]{1,0:T(8,128)S(1)}, /*index=5*/f32[64,384]{1,0:T(8,128)S(1)}) custom-call(f32[2,128]{1,0:T(2,128)S(1)} %concatenate.6.refs_1_.refs_0_, bf16[256,768]{1,0:T(8,128)(2,1)S(1)} %get-tuple-element.21.refs_1_.refs_2_, ...), custom_call_target="tpu_custom_call" | custom-call | flops 402653184 | bytes 2851840 | tf_op jit(solution)/shard_map/text_part/pallas_call | solution.py:33
  22.6 1.6 %collective-permute-start.10 = (f32[64,384]{1,0:T(8,128)S(1)}, f32[64,384]{1,0:T(8,128)S(1)}, u32[]{:S(2)}, u32[]{:S(2)}) collective-permute-start(f32[64,384]{1,0:T(8,128)S(1)} %get-tuple-element.28), channel_id=1, source_target_pairs={{0,8},{8,0},{16,24},{24,16},{1,9},{9,1},{17,25},{25,17},{2,10},{10... | collective-permute-start | bytes 294920 | tf_op jit(solution)/shard_map/ppermute | solution.py:17
  24.3 0.4 %collective-permute-start.9 = (f32[64,384]{1,0:T(8,128)S(1)}, f32[64,384]{1,0:T(8,128)S(1)}, u32[]{:S(2)}, u32[]{:S(2)}) collective-permute-start(f32[64,384]{1,0:T(8,128)S(1)} %get-tuple-element.24), channel_id=1, source_target_pairs={{0,8},{8,0},{16,24},{24,16},{1,9},{9,1},{17,25},{25,17},{2,10},{10... | collective-permute-start | bytes 294920 | tf_op jit(solution)/shard_map/ppermute | solution.py:17
  24.7 3.4 %collective-permute-done.10.refs_1_ = f32[64,384]{1,0:T(8,128)S(1)} collective-permute-done((f32[64,384]{1,0:T(8,128)S(1)}, f32[64,384]{1,0:T(8,128)S(1)}, u32[]{:S(2)}, u32[]{:S(2)}) %collective-permute-start.10) | collective-permute-done | bytes 98336 | tf_op jit(solution)/shard_map/ppermute | solution.py:17
  28.2 0.3 collective-permute-start.15
  28.5 1.1 %collective-permute-done.9.refs_1_ = f32[64,384]{1,0:T(8,128)S(1)} collective-permute-done((f32[64,384]{1,0:T(8,128)S(1)}, f32[64,384]{1,0:T(8,128)S(1)}, u32[]{:S(2)}, u32[]{:S(2)}) %collective-permute-start.9) | collective-permute-done | bytes 98336 | tf_op jit(solution)/shard_map/ppermute | solution.py:17
  29.6 2.5 %collective-permute-start.16 = (f32[64,768]{1,0:T(8,128)S(1)}, f32[64,768]{1,0:T(8,128)S(1)}, u32[]{:S(2)}, u32[]{:S(2)}) collective-permute-start(f32[64,768]{1,0:T(8,128)S(1)} %get-tuple-element.32), channel_id=1, source_target_pairs={{0,8},{8,0},{16,24},{24,16},{1,9},{9,1},{17,25},{25,17},{2,10},{10... | collective-permute-start | bytes 589832 | tf_op jit(solution)/shard_map/ppermute | solution.py:17
  32.1 0.9 %collective-permute-start.14 = (f32[64,384]{1,0:T(8,128)S(1)}, f32[64,384]{1,0:T(8,128)S(1)}, u32[]{:S(2)}, u32[]{:S(2)}) collective-permute-start(f32[64,384]{1,0:T(8,128)S(1)} %get-tuple-element.26.refs_5_.refs_2_), channel_id=1, source_target_pairs={{0,16},{8,24},{16,0},{24,8},{1,17},{9,25},{17,1},{25,9},{2,18},{10... | collective-permute-start | bytes 294920 | tf_op jit(solution)/shard_map/ppermute | solution.py:17
  33.1 1.6 %collective-permute-start.11 = (bf16[128,768]{1,0:T(8,128)(2,1)S(1)}, bf16[128,768]{1,0:T(8,128)(2,1)S(1)}, u32[]{:S(2)}, u32[]{:S(2)}) collective-permute-start(bf16[128,768]{1,0:T(8,128)(2,1)S(1)} %get-tuple-element.29), channel_id=1, source_target_pairs={{0,2},{1,3},{2,0},{3,1},{4,6},{5,7},{6,4},{7,5},{8,10},{9,11},{10,... | collective-permute-start | bytes 589832 | tf_op jit(solution)/shard_map/ppermute | solution.py:17
  34.6 0.5 %collective-permute-start.12 = (bf16[128,768]{1,0:T(8,128)(2,1)S(1)}, bf16[128,768]{1,0:T(8,128)(2,1)S(1)}, u32[]{:S(2)}, u32[]{:S(2)}) collective-permute-start(bf16[128,768]{1,0:T(8,128)(2,1)S(1)} %get-tuple-element.30), channel_id=1, source_target_pairs={{0,4},{1,5},{2,6},{3,7},{4,0},{5,1},{6,2},{7,3},{8,12},{9,13},{10,... | collective-permute-start | bytes 589832 | tf_op jit(solution)/shard_map/ppermute | solution.py:17
  35.2 1.0 %speech_part.4.refs_2_ = f32[128,768]{1,0:T(8,128)S(1)} custom-call(f32[2,128]{1,0:T(2,128)S(1)} %concatenate.6.refs_1_.refs_0_, bf16[144,768]{1,0:T(8,128)(2,1)S(1)} %get-tuple-element.19.refs_4_.refs_1_, bf16[256,768]{1,0:T(8,128)(2,1)S(1)} %get-tuple-element.21.refs_1_.refs_2_, bf16[256,768]{1,0:T(8,128)(2,1)S(1)} %collective-permute-done.6.refs_3_.refs_1_, ...), custom_call_target="tpu_custom_call" | custom-call | flops 3019898880 | bytes 1795072 | tf_op jit(solution)/shard_map/speech_part/pallas_call | solution.py:33
  36.2 1.0 %speech_part.6.refs_2_ = f32[128,768]{1,0:T(8,128)S(1)} custom-call(f32[2,128]{1,0:T(2,128)S(1)} %concatenate.6.refs_1_.refs_0_, bf16[144,768]{1,0:T(8,128)(2,1)S(1)} %slice.5.refs_1_, bf16[256,768]{1,0:T(8,128)(2,1)S(1)} %get-tuple-element.21.refs_1_.refs_2_, bf16[256,768]{1,0:T(8,128)(2,1)S(1)} %collective-permute-done.6.refs_3_.refs_1_, ...), custom_call_target="tpu_custom_call" | custom-call | flops 3019898880 | bytes 1795072 | tf_op jit(solution)/shard_map/speech_part/pallas_call | solution.py:33
  37.2 1.6 %collective-permute-done.11.refs_3_ = bf16[128,768]{1,0:T(8,128)(2,1)S(1)} collective-permute-done((bf16[128,768]{1,0:T(8,128)(2,1)S(1)}, bf16[128,768]{1,0:T(8,128)(2,1)S(1)}, u32[]{:S(2)}, u32[]{:S(2)}) %collective-permute-start.11) | collective-permute-done | bytes 196640 | tf_op jit(solution)/shard_map/ppermute | solution.py:17
  38.8 1.5 %collective-permute-done.12.refs_4_ = bf16[128,768]{1,0:T(8,128)(2,1)S(1)} collective-permute-done((bf16[128,768]{1,0:T(8,128)(2,1)S(1)}, bf16[128,768]{1,0:T(8,128)(2,1)S(1)}, u32[]{:S(2)}, u32[]{:S(2)}) %collective-permute-start.12) | collective-permute-done | bytes 196640 | tf_op jit(solution)/shard_map/ppermute | solution.py:17
  40.3 0.5 %speech_part.7 = f32[128,768]{1,0:T(8,128)S(1)} custom-call(f32[2,128]{1,0:T(2,128)S(1)} %concatenate.6.refs_1_.refs_0_, bf16[144,768]{1,0:T(8,128)(2,1)S(1)} %slice.5.refs_1_, f32[128,768]{1,0:T(8,128)S(1)} %speech_part.6.refs_2_, bf16[128,768]{1,0:T(8,128)(2,1)S(1)} %collective-permute-done.11.refs_3_, bf16[128,768]{1,0:T(8,128)(2,1)S(1)} %collective-permute-done.12.refs_4_), custom_call_target="tpu_custom_call" | custom-call | flops 1006632960 | bytes 1401856 | tf_op jit(solution)/shard_map/speech_part/pallas_call | solution.py:33
  41.0 0.5 %speech_part.5.refs_1_ = f32[128,768]{1,0:T(8,128)S(1)} custom-call(f32[2,128]{1,0:T(2,128)S(1)} %concatenate.6.refs_1_.refs_0_, bf16[144,768]{1,0:T(8,128)(2,1)S(1)} %get-tuple-element.19.refs_4_.refs_1_, f32[128,768]{1,0:T(8,128)S(1)} %speech_part.4.refs_2_, bf16[128,768]{1,0:T(8,128)(2,1)S(1)} %collective-permute-done.11.refs_3_, ...), custom_call_target="tpu_custom_call" | custom-call | flops 1006632960 | bytes 1401856 | tf_op jit(solution)/shard_map/speech_part/pallas_call | solution.py:33
  41.5 1.1 %collective-permute-done.13.refs_2_ = f32[128,768]{1,0:T(8,128)S(1)} collective-permute-done((f32[128,768]{1,0:T(8,128)S(1)}, f32[128,768]{1,0:T(8,128)S(1)}, u32[]{:S(2)}, u32[]{:S(2)}) %collective-permute-start.13) | collective-permute-done | bytes 393248 | tf_op jit(solution)/shard_map/ppermute | solution.py:17
  42.6 1.0 %finish.1 = (f32[128,768]{1,0:T(8,128)}, f32[64,768]{1,0:T(8,128)}) custom-call(bf16[128,768]{1,0:T(8,128)(2,1)S(1)} %get-tuple-element.18.refs_0_, f32[128,768]{1,0:T(8,128)S(1)} %speech_part.5.refs_1_, f32[128,768]{1,0:T(8,128)S(1)} %collective-permute-done.13.refs_2_, bf16[64,768]{1,0:T(8,128)(2,1)S(1)} %get-tuple-element.31.refs_3_, ...), custom_call_target="tpu_custom_call" | custom-call | bytes 1867776 | tf_op jit(solution)/shard_map/finish/pallas_call | solution.py:33
  (19 shorter events, 0.4 us)
Async XLA Ops:
  1.8 10.5 %collective-permute-start.1 = (bf16[64,768]{1,0:T(8,128)(2,1)S(1)}, bf16[64,768]{1,0:T(8,128)(2,1)S(1)}, u32[]{:S(2)}, u32[]{:S(2)}) collective-permute-start(bf16[64,768]{1,0:T(8,128)(2,1)S(1)} %get-tuple-element.20.refs_0_), channel_id=1, source_target_pairs={{0,16},{8,24},{16,0},{24,8},{1,17},{9,25},{17,1},{25,9},{2,18},{10... | collective-permute-start | bytes 294920 | tf_op jit(solution)/shard_map/ppermute | solution.py:17
  5.9 11.1 %collective-permute-start.3 = (bf16[144,768]{1,0:T(8,128)(2,1)S(1)}, bf16[144,768]{1,0:T(8,128)(2,1)S(1)}, u32[]{:S(2)}, u32[]{:S(2)}) collective-permute-start(bf16[144,768]{1,0:T(8,128)(2,1)S(1)} %get-tuple-element.19.refs_4_.refs_1_), channel_id=1, source_target_pairs={{0,2},{1,3},{2,0},{3,1},{4,6},{5,7},{6,4},{7,5},{8,10},{9,11},{10,... | collective-permute-start | bytes 663560 | tf_op jit(solution)/shard_map/ppermute | solution.py:17
  7.4 11.3 %collective-permute-start.4 = (bf16[144,768]{1,0:T(8,128)(2,1)S(1)}, bf16[144,768]{1,0:T(8,128)(2,1)S(1)}, u32[]{:S(2)}, u32[]{:S(2)}) collective-permute-start(bf16[144,768]{1,0:T(8,128)(2,1)S(1)} %get-tuple-element.19.refs_4_.refs_1_), channel_id=1, source_target_pairs={{0,4},{1,5},{2,6},{3,7},{4,0},{5,1},{6,2},{7,3},{8,12},{9,13},{10,... | collective-permute-start | bytes 663560 | tf_op jit(solution)/shard_map/ppermute | solution.py:17
  8.9 9.8 %collective-permute-start.5 = (bf16[144,768]{1,0:T(8,128)(2,1)S(1)}, bf16[144,768]{1,0:T(8,128)(2,1)S(1)}, u32[]{:S(2)}, u32[]{:S(2)}) collective-permute-start(bf16[144,768]{1,0:T(8,128)(2,1)S(1)} %get-tuple-element.19.refs_4_.refs_1_), channel_id=1, source_target_pairs={{0,6},{1,7},{2,4},{3,5},{4,2},{5,3},{6,0},{7,1},{8,14},{9,15},{10,... | collective-permute-start | bytes 663560 | tf_op jit(solution)/shard_map/ppermute | solution.py:17
  9.4 5.3 %collective-permute-start = (bf16[64,768]{1,0:T(8,128)(2,1)S(1)}, bf16[64,768]{1,0:T(8,128)(2,1)S(1)}, u32[]{:S(2)}, u32[]{:S(2)}) collective-permute-start(bf16[64,768]{1,0:T(8,128)(2,1)S(1)} %get-tuple-element.20.refs_0_), channel_id=1, source_target_pairs={{0,8},{8,0},{16,24},{24,16},{1,9},{9,1},{17,25},{25,17},{2,10},{10... | collective-permute-start | bytes 294920 | tf_op jit(solution)/shard_map/ppermute | solution.py:17
  12.4 4.7 %collective-permute-start.2 = (bf16[64,768]{1,0:T(8,128)(2,1)S(1)}, bf16[64,768]{1,0:T(8,128)(2,1)S(1)}, u32[]{:S(2)}, u32[]{:S(2)}) collective-permute-start(bf16[64,768]{1,0:T(8,128)(2,1)S(1)} %pass_on.1.refs_2_), channel_id=1, source_target_pairs={{0,8},{8,0},{16,24},{24,16},{1,9},{9,1},{17,25},{25,17},{2,10},{10... | collective-permute-start | bytes 294920 | tf_op jit(solution)/shard_map/ppermute | solution.py:17
  18.9 3.0 %collective-permute-start.8 = (bf16[576,768]{1,0:T(8,128)(2,1)S(1)}, bf16[576,768]{1,0:T(8,128)(2,1)S(1)}, u32[]{:S(2)}, u32[]{:S(2)}) collective-permute-start(bf16[576,768]{1,0:T(8,128)(2,1)S(1)} %get-tuple-element.22.refs_2_), channel_id=1, source_target_pairs={{0,1},{1,0},{2,3},{3,2},{4,5},{5,4},{6,7},{7,6},{8,9},{9,8},{10,11... | collective-permute-start | bytes 2654216 | tf_op jit(solution)/shard_map/ppermute | solution.py:17
  18.9 14.1 %collective-permute-start.6 = (bf16[256,768]{1,0:T(8,128)(2,1)S(1)}, bf16[256,768]{1,0:T(8,128)(2,1)S(1)}, u32[]{:S(2)}, u32[]{:S(2)}) collective-permute-start(bf16[256,768]{1,0:T(8,128)(2,1)S(1)} %get-tuple-element.21.refs_1_.refs_2_), channel_id=1, source_target_pairs={{0,2},{1,3},{2,0},{3,1},{4,6},{5,7},{6,4},{7,5},{8,10},{9,11},{10,... | collective-permute-start | bytes 1179656 | tf_op jit(solution)/shard_map/ppermute | solution.py:17
  20.2 12.8 %collective-permute-start.7 = (bf16[256,768]{1,0:T(8,128)(2,1)S(1)}, bf16[256,768]{1,0:T(8,128)(2,1)S(1)}, u32[]{:S(2)}, u32[]{:S(2)}) collective-permute-start(bf16[256,768]{1,0:T(8,128)(2,1)S(1)} %get-tuple-element.21.refs_1_.refs_2_), channel_id=1, source_target_pairs={{0,4},{1,5},{2,6},{3,7},{4,0},{5,1},{6,2},{7,3},{8,12},{9,13},{10,... | collective-permute-start | bytes 1179656 | tf_op jit(solution)/shard_map/ppermute | solution.py:17
  22.6 5.5 %collective-permute-start.10 = (f32[64,384]{1,0:T(8,128)S(1)}, f32[64,384]{1,0:T(8,128)S(1)}, u32[]{:S(2)}, u32[]{:S(2)}) collective-permute-start(f32[64,384]{1,0:T(8,128)S(1)} %get-tuple-element.28), channel_id=1, source_target_pairs={{0,8},{8,0},{16,24},{24,16},{1,9},{9,1},{17,25},{25,17},{2,10},{10... | collective-permute-start | bytes 294920 | tf_op jit(solution)/shard_map/ppermute | solution.py:17
  24.3 5.3 %collective-permute-start.9 = (f32[64,384]{1,0:T(8,128)S(1)}, f32[64,384]{1,0:T(8,128)S(1)}, u32[]{:S(2)}, u32[]{:S(2)}) collective-permute-start(f32[64,384]{1,0:T(8,128)S(1)} %get-tuple-element.24), channel_id=1, source_target_pairs={{0,8},{8,0},{16,24},{24,16},{1,9},{9,1},{17,25},{25,17},{2,10},{10... | collective-permute-start | bytes 294920 | tf_op jit(solution)/shard_map/ppermute | solution.py:17
  28.2 12.7 %collective-permute-start.15 = (f32[64,384]{1,0:T(8,128)S(1)}, f32[64,384]{1,0:T(8,128)S(1)}, u32[]{:S(2)}, u32[]{:S(2)}) collective-permute-start(f32[64,384]{1,0:T(8,128)S(1)} %sum_near.3.refs_6_.refs_3_), channel_id=1, source_target_pairs={{0,16},{8,24},{16,0},{24,8},{1,17},{9,25},{17,1},{25,9},{2,18},{10... | collective-permute-start | bytes 294920 | tf_op jit(solution)/shard_map/ppermute | solution.py:17
  29.6 11.3 %collective-permute-start.16 = (f32[64,768]{1,0:T(8,128)S(1)}, f32[64,768]{1,0:T(8,128)S(1)}, u32[]{:S(2)}, u32[]{:S(2)}) collective-permute-start(f32[64,768]{1,0:T(8,128)S(1)} %get-tuple-element.32), channel_id=1, source_target_pairs={{0,8},{8,0},{16,24},{24,16},{1,9},{9,1},{17,25},{25,17},{2,10},{10... | collective-permute-start | bytes 589832 | tf_op jit(solution)/shard_map/ppermute | solution.py:17
  32.1 8.8 %collective-permute-start.14 = (f32[64,384]{1,0:T(8,128)S(1)}, f32[64,384]{1,0:T(8,128)S(1)}, u32[]{:S(2)}, u32[]{:S(2)}) collective-permute-start(f32[64,384]{1,0:T(8,128)S(1)} %get-tuple-element.26.refs_5_.refs_2_), channel_id=1, source_target_pairs={{0,16},{8,24},{16,0},{24,8},{1,17},{9,25},{17,1},{25,9},{2,18},{10... | collective-permute-start | bytes 294920 | tf_op jit(solution)/shard_map/ppermute | solution.py:17
  33.1 5.7 %collective-permute-start.11 = (bf16[128,768]{1,0:T(8,128)(2,1)S(1)}, bf16[128,768]{1,0:T(8,128)(2,1)S(1)}, u32[]{:S(2)}, u32[]{:S(2)}) collective-permute-start(bf16[128,768]{1,0:T(8,128)(2,1)S(1)} %get-tuple-element.29), channel_id=1, source_target_pairs={{0,2},{1,3},{2,0},{3,1},{4,6},{5,7},{6,4},{7,5},{8,10},{9,11},{10,... | collective-permute-start | bytes 589832 | tf_op jit(solution)/shard_map/ppermute | solution.py:17
  34.6 5.7 %collective-permute-start.12 = (bf16[128,768]{1,0:T(8,128)(2,1)S(1)}, bf16[128,768]{1,0:T(8,128)(2,1)S(1)}, u32[]{:S(2)}, u32[]{:S(2)}) collective-permute-start(bf16[128,768]{1,0:T(8,128)(2,1)S(1)} %get-tuple-element.30), channel_id=1, source_target_pairs={{0,4},{1,5},{2,6},{3,7},{4,0},{5,1},{6,2},{7,3},{8,12},{9,13},{10,... | collective-permute-start | bytes 589832 | tf_op jit(solution)/shard_map/ppermute | solution.py:17
  40.8 1.8 %collective-permute-start.13 = (f32[128,768]{1,0:T(8,128)S(1)}, f32[128,768]{1,0:T(8,128)S(1)}, u32[]{:S(2)}, u32[]{:S(2)}) collective-permute-start(f32[128,768]{1,0:T(8,128)S(1)} %speech_part.7), channel_id=1, source_target_pairs={{0,1},{1,0},{2,3},{3,2},{4,5},{5,4},{6,7},{7,6},{8,9},{9,8},{10,11... | collective-permute-start | bytes 1179656 | tf_op jit(solution)/shard_map/ppermute | solution.py:17

commit v12 on v11

--- a/solution.py
+++ b/solution.py
@@ -162,11 +162,6 @@
     out[...] = total
 
 
-def sum_keep_body(mine, came, kept, total, kept_out):
-    total[...] = mine[...] + came[...]
-    kept_out[...] = kept[...]
-
-
 def add_sides_body(*refs):
     out = refs[-1]
     sides = [ref for ref in refs[:-1] if ref.shape != out.shape]
@@ -281,15 +276,9 @@
     while bit < groups // 2:
         for k in reversed(range(bit, groups // 2, 2 * bit)):
             came = [exchanged(v, "group", bit) for v in far[k]]
-            mine = far[k - bit]
-            first, parts[bit] = call(
-                sum_keep_body,
-                [side, f32(own_text, width)],
-                [mine[0], came[0], parts[bit]],
-                name="sum_near",
-            )
-            last = call(sum_body, side, [mine[1], came[1]], name="sum_near")
-            far[k - bit] = [first, last]
+            far[k - bit] = [
+                call(sum_body, side, [mine, v], name="sum_near") for mine, v in zip(far[k - bit], came)
+            ]
         bit *= 2
     from_far = [exchanged(v, "group", groups // 2) for v in far[0]]
     from_near = [exchanged(parts[k], "group", k) for k in range(1, groups // 2)]

time: 43.8 us -> 42.2 us (0.963)
  starting transfers between devices: 19.9 us -> 18.4 us
    ppermute x17, starting transfers between devices: 19.9 us -> 18.4 us  [exchanged(): return lax.ppermute(value, axis, [(i, i ^ mask) for i in range(size)])]
  transfers between devices with their start and end apart: 17 -> 17, of which waited for: 8 -> 9; matrix products, arithmetic and copies ran while one was open for 0% -> 0% of each run, Pallas kernels for 11% -> 11%
where the time goes in v12:
time: 42.2 us; the launch traced here: 42 us
  starting transfers between devices  18.4 us (44%)
  waiting for transfers between devices  14.5 us (34%)
  Pallas kernels  7.03 us (17%)
  between operations  2.1 us (5%)
    ppermute x17, starting transfers between devices, exchanged(): return lax.ppermute(value, axis, [(i, i ^ mask) for i in range(size)])  18.4 us
    ppermute x17, waiting for transfers between devices, exchanged(): return lax.ppermute(value, axis, [(i, i ^ mask) for i in range(size)])  14.5 us
    pallas_call x13, Pallas kernels, call(): pl.pallas_call(whole, out_shape=out_shape, in_specs=specs, out_specs=jax....  5.85 us
    pallas_call x1, Pallas kernels, shards(): pl.pallas_call(prepare_body, out_shape=[bf16(rows + MARK_ROWS, width), bf...  1.18 us
  transfers between devices with their start and end apart: 17, of which 9 were waited for; matrix products, arithmetic and copies ran while one was open for 0% of the time, Pallas kernels for 11%

profile of v12, /device:TPU:0, one launch (start us, length us, event | category | flops | bytes accessed | tf_op | source)
XLA Modules:
  0.0 42.0 jit_solution(5756091490262811745)
XLA Ops:
  0.6 1.2 %unit_rows.1 = (bf16[144,768]{1,0:T(8,128)(2,1)S(1)}, bf16[64,768]{1,0:T(8,128)(2,1)S(1)}, bf16[128,768]{1,0:T(8,128)(2,1)S(1)}, bf16[64,768]{1,0:T(8,128)(2,1)S(1)}) custom-call(bf16[128,768]{1,0:T(8,128)(2,1)} %refs_0_.1, bf16[64,768]{1,0:T(8,128)(2,1)} %refs_1_.1, s32[1,128]{1,0:T(1,128)} %bitcast.3), custom_call_target="tpu_custom_call" | custom-call | tf_op jit(solution)/shard_map/unit_rows/pallas_call | solution.py:215
  1.8 4.1 %collective-permute-start.1 = (bf16[64,768]{1,0:T(8,128)(2,1)S(1)}, bf16[64,768]{1,0:T(8,128)(2,1)S(1)}, u32[]{:S(2)}, u32[]{:S(2)}) collective-permute-start(bf16[64,768]{1,0:T(8,128)(2,1)S(1)} %get-tuple-element.18.refs_0_), channel_id=1, source_target_pairs={{0,16},{8,24},{16,0},{24,8},{1,17},{9,25},{17,1},{25,9},{2,18},{10... | collective-permute-start | bytes 294920 | tf_op jit(solution)/shard_map/ppermute | solution.py:17
  5.9 1.5 %collective-permute-start.3 = (bf16[144,768]{1,0:T(8,128)(2,1)S(1)}, bf16[144,768]{1,0:T(8,128)(2,1)S(1)}, u32[]{:S(2)}, u32[]{:S(2)}) collective-permute-start(bf16[144,768]{1,0:T(8,128)(2,1)S(1)} %get-tuple-element.17.refs_4_.refs_1_), channel_id=1, source_target_pairs={{0,2},{1,3},{2,0},{3,1},{4,6},{5,7},{6,4},{7,5},{8,10},{9,11},{10,... | collective-permute-start | bytes 663560 | tf_op jit(solution)/shard_map/ppermute | solution.py:17
  7.4 1.5 %collective-permute-start.4 = (bf16[144,768]{1,0:T(8,128)(2,1)S(1)}, bf16[144,768]{1,0:T(8,128)(2,1)S(1)}, u32[]{:S(2)}, u32[]{:S(2)}) collective-permute-start(bf16[144,768]{1,0:T(8,128)(2,1)S(1)} %get-tuple-element.17.refs_4_.refs_1_), channel_id=1, source_target_pairs={{0,4},{1,5},{2,6},{3,7},{4,0},{5,1},{6,2},{7,3},{8,12},{9,13},{10,... | collective-permute-start | bytes 663560 | tf_op jit(solution)/shard_map/ppermute | solution.py:17
  8.9 0.5 %collective-permute-start.5 = (bf16[144,768]{1,0:T(8,128)(2,1)S(1)}, bf16[144,768]{1,0:T(8,128)(2,1)S(1)}, u32[]{:S(2)}, u32[]{:S(2)}) collective-permute-start(bf16[144,768]{1,0:T(8,128)(2,1)S(1)} %get-tuple-element.17.refs_4_.refs_1_), channel_id=1, source_target_pairs={{0,6},{1,7},{2,4},{3,5},{4,2},{5,3},{6,0},{7,1},{8,14},{9,15},{10,... | collective-permute-start | bytes 663560 | tf_op jit(solution)/shard_map/ppermute | solution.py:17
  9.4 1.6 %collective-permute-start = (bf16[64,768]{1,0:T(8,128)(2,1)S(1)}, bf16[64,768]{1,0:T(8,128)(2,1)S(1)}, u32[]{:S(2)}, u32[]{:S(2)}) collective-permute-start(bf16[64,768]{1,0:T(8,128)(2,1)S(1)} %get-tuple-element.18.refs_0_), channel_id=1, source_target_pairs={{0,8},{8,0},{16,24},{24,16},{1,9},{9,1},{17,25},{25,17},{2,10},{10... | collective-permute-start | bytes 294920 | tf_op jit(solution)/shard_map/ppermute | solution.py:17
  12.4 0.5 %collective-permute-start.2 = (bf16[64,768]{1,0:T(8,128)(2,1)S(1)}, bf16[64,768]{1,0:T(8,128)(2,1)S(1)}, u32[]{:S(2)}, u32[]{:S(2)}) collective-permute-start(bf16[64,768]{1,0:T(8,128)(2,1)S(1)} %pass_on.1.refs_2_), channel_id=1, source_target_pairs={{0,8},{8,0},{16,24},{24,16},{1,9},{9,1},{17,25},{25,17},{2,10},{10... | collective-permute-start | bytes 294920 | tf_op jit(solution)/shard_map/ppermute | solution.py:17
  12.9 1.8 %collective-permute-done.refs_1_ = bf16[64,768]{1,0:T(8,128)(2,1)S(1)} collective-permute-done((bf16[64,768]{1,0:T(8,128)(2,1)S(1)}, bf16[64,768]{1,0:T(8,128)(2,1)S(1)}, u32[]{:S(2)}, u32[]{:S(2)}) %collective-permute-start) | collective-permute-done | bytes 98336 | tf_op jit(solution)/shard_map/ppermute | solution.py:17
  14.7 2.4 %collective-permute-done.2.refs_3_ = bf16[64,768]{1,0:T(8,128)(2,1)S(1)} collective-permute-done((bf16[64,768]{1,0:T(8,128)(2,1)S(1)}, bf16[64,768]{1,0:T(8,128)(2,1)S(1)}, u32[]{:S(2)}, u32[]{:S(2)}) %collective-permute-start.2) | collective-permute-done | bytes 98336 | tf_op jit(solution)/shard_map/ppermute | solution.py:17
  17.1 1.7 %collective-permute-done.4.refs_6_ = bf16[144,768]{1,0:T(8,128)(2,1)S(1)} collective-permute-done((bf16[144,768]{1,0:T(8,128)(2,1)S(1)}, bf16[144,768]{1,0:T(8,128)(2,1)S(1)}, u32[]{:S(2)}, u32[]{:S(2)}) %collective-permute-start.4) | collective-permute-done | bytes 221216 | tf_op jit(solution)/shard_map/ppermute | solution.py:17
  18.8 0.1 join_rows.1
  18.9 1.3 %collective-permute-start.6 = (bf16[256,768]{1,0:T(8,128)(2,1)S(1)}, bf16[256,768]{1,0:T(8,128)(2,1)S(1)}, u32[]{:S(2)}, u32[]{:S(2)}) collective-permute-start(bf16[256,768]{1,0:T(8,128)(2,1)S(1)} %get-tuple-element.19.refs_1_.refs_2_), channel_id=1, source_target_pairs={{0,2},{1,3},{2,0},{3,1},{4,6},{5,7},{6,4},{7,5},{8,10},{9,11},{10,... | collective-permute-start | bytes 1179656 | tf_op jit(solution)/shard_map/ppermute | solution.py:17
  20.2 0.8 %collective-permute-start.7 = (bf16[256,768]{1,0:T(8,128)(2,1)S(1)}, bf16[256,768]{1,0:T(8,128)(2,1)S(1)}, u32[]{:S(2)}, u32[]{:S(2)}) collective-permute-start(bf16[256,768]{1,0:T(8,128)(2,1)S(1)} %get-tuple-element.19.refs_1_.refs_2_), channel_id=1, source_target_pairs={{0,4},{1,5},{2,6},{3,7},{4,0},{5,1},{6,2},{7,3},{8,12},{9,13},{10,... | collective-permute-start | bytes 1179656 | tf_op jit(solution)/shard_map/ppermute | solution.py:17
  21.1 0.8 %text_part.2.refs_2_ = f32[256,768]{1,0:T(8,128)S(1)} custom-call(f32[2,128]{1,0:T(2,128)S(1)} %concatenate.6.refs_1_.refs_0_, bf16[256,768]{1,0:T(8,128)(2,1)S(1)} %get-tuple-element.19.refs_1_.refs_2_, bf16[576,768]{1,0:T(8,128)(2,1)S(1)} %get-tuple-element.20.refs_2_), custom_call_target="tpu_custom_call" | custom-call | flops 402653184 | bytes 2065408 | tf_op jit(solution)/shard_map/text_part/pallas_call | solution.py:33
  21.8 0.8 %text_part.3 = (f32[64,768]{1,0:T(8,128)S(1)}, f32[64,768]{1,0:T(8,128)S(1)}, f32[64,384]{1,0:T(8,128)S(1)}, f32[64,384]{1,0:T(8,128)S(1)}, f32[64,384]{1,0:T(8,128)S(1)}, /*index=5*/f32[64,384]{1,0:T(8,128)S(1)}) custom-call(f32[2,128]{1,0:T(2,128)S(1)} %concatenate.6.refs_1_.refs_0_, bf16[256,768]{1,0:T(8,128)(2,1)S(1)} %get-tuple-element.19.refs_1_.refs_2_, ...), custom_call_target="tpu_custom_call" | custom-call | flops 402653184 | bytes 2851840 | tf_op jit(solution)/shard_map/text_part/pallas_call | solution.py:33
  22.6 1.6 %collective-permute-start.10 = (f32[64,384]{1,0:T(8,128)S(1)}, f32[64,384]{1,0:T(8,128)S(1)}, u32[]{:S(2)}, u32[]{:S(2)}) collective-permute-start(f32[64,384]{1,0:T(8,128)S(1)} %get-tuple-element.24), channel_id=1, source_target_pairs={{0,8},{8,0},{16,24},{24,16},{1,9},{9,1},{17,25},{25,17},{2,10},{10... | collective-permute-start | bytes 294920 | tf_op jit(solution)/shard_map/ppermute | solution.py:17
  24.3 0.4 %collective-permute-start.9 = (f32[64,384]{1,0:T(8,128)S(1)}, f32[64,384]{1,0:T(8,128)S(1)}, u32[]{:S(2)}, u32[]{:S(2)}) collective-permute-start(f32[64,384]{1,0:T(8,128)S(1)} %get-tuple-element.22), channel_id=1, source_target_pairs={{0,8},{8,0},{16,24},{24,16},{1,9},{9,1},{17,25},{25,17},{2,10},{10... | collective-permute-start | bytes 294920 | tf_op jit(solution)/shard_map/ppermute | solution.py:17
  24.7 1.6 %collective-permute-start.16 = (f32[64,768]{1,0:T(8,128)S(1)}, f32[64,768]{1,0:T(8,128)S(1)}, u32[]{:S(2)}, u32[]{:S(2)}) collective-permute-start(f32[64,768]{1,0:T(8,128)S(1)} %get-tuple-element.28), channel_id=1, source_target_pairs={{0,8},{8,0},{16,24},{24,16},{1,9},{9,1},{17,25},{25,17},{2,10},{10... | collective-permute-start | bytes 589832 | tf_op jit(solution)/shard_map/ppermute | solution.py:17
  26.3 1.8 %collective-permute-done.10.refs_1_ = f32[64,384]{1,0:T(8,128)S(1)} collective-permute-done((f32[64,384]{1,0:T(8,128)S(1)}, f32[64,384]{1,0:T(8,128)S(1)}, u32[]{:S(2)}, u32[]{:S(2)}) %collective-permute-start.10) | collective-permute-done | bytes 98336 | tf_op jit(solution)/shard_map/ppermute | solution.py:17
  28.2 0.3 collective-permute-start.15
  28.5 2.8 %collective-permute-done.9.refs_1_ = f32[64,384]{1,0:T(8,128)S(1)} collective-permute-done((f32[64,384]{1,0:T(8,128)S(1)}, f32[64,384]{1,0:T(8,128)S(1)}, u32[]{:S(2)}, u32[]{:S(2)}) %collective-permute-start.9) | collective-permute-done | bytes 98336 | tf_op jit(solution)/shard_map/ppermute | solution.py:17
  31.5 1.6 %collective-permute-start.11 = (bf16[128,768]{1,0:T(8,128)(2,1)S(1)}, bf16[128,768]{1,0:T(8,128)(2,1)S(1)}, u32[]{:S(2)}, u32[]{:S(2)}) collective-permute-start(bf16[128,768]{1,0:T(8,128)(2,1)S(1)} %get-tuple-element.25), channel_id=1, source_target_pairs={{0,2},{1,3},{2,0},{3,1},{4,6},{5,7},{6,4},{7,5},{8,10},{9,11},{10,... | collective-permute-start | bytes 589832 | tf_op jit(solution)/shard_map/ppermute | solution.py:17
  33.0 0.8 %collective-permute-start.12 = (bf16[128,768]{1,0:T(8,128)(2,1)S(1)}, bf16[128,768]{1,0:T(8,128)(2,1)S(1)}, u32[]{:S(2)}, u32[]{:S(2)}) collective-permute-start(bf16[128,768]{1,0:T(8,128)(2,1)S(1)} %get-tuple-element.26), channel_id=1, source_target_pairs={{0,4},{1,5},{2,6},{3,7},{4,0},{5,1},{6,2},{7,3},{8,12},{9,13},{10,... | collective-permute-start | bytes 589832 | tf_op jit(solution)/shard_map/ppermute | solution.py:17
  33.8 1.0 %speech_part.4.refs_2_ = f32[128,768]{1,0:T(8,128)S(1)} custom-call(f32[2,128]{1,0:T(2,128)S(1)} %concatenate.6.refs_1_.refs_0_, bf16[144,768]{1,0:T(8,128)(2,1)S(1)} %get-tuple-element.17.refs_4_.refs_1_, bf16[256,768]{1,0:T(8,128)(2,1)S(1)} %get-tuple-element.19.refs_1_.refs_2_, bf16[256,768]{1,0:T(8,128)(2,1)S(1)} %collective-permute-done.6.refs_3_.refs_1_, ...), custom_call_target="tpu_custom_call" | custom-call | flops 3019898880 | bytes 1795072 | tf_op jit(solution)/shard_map/speech_part/pallas_call | solution.py:33
  34.9 1.0 %speech_part.6.refs_2_ = f32[128,768]{1,0:T(8,128)S(1)} custom-call(f32[2,128]{1,0:T(2,128)S(1)} %concatenate.6.refs_1_.refs_0_, bf16[144,768]{1,0:T(8,128)(2,1)S(1)} %slice.5.refs_1_, bf16[256,768]{1,0:T(8,128)(2,1)S(1)} %get-tuple-element.19.refs_1_.refs_2_, bf16[256,768]{1,0:T(8,128)(2,1)S(1)} %collective-permute-done.6.refs_3_.refs_1_, ...), custom_call_target="tpu_custom_call" | custom-call | flops 3019898880 | bytes 1795072 | tf_op jit(solution)/shard_map/speech_part/pallas_call | solution.py:33
  35.9 1.8 %collective-permute-done.11.refs_3_ = bf16[128,768]{1,0:T(8,128)(2,1)S(1)} collective-permute-done((bf16[128,768]{1,0:T(8,128)(2,1)S(1)}, bf16[128,768]{1,0:T(8,128)(2,1)S(1)}, u32[]{:S(2)}, u32[]{:S(2)}) %collective-permute-start.11) | collective-permute-done | bytes 196640 | tf_op jit(solution)/shard_map/ppermute | solution.py:17
  37.7 1.0 %collective-permute-done.12.refs_4_ = bf16[128,768]{1,0:T(8,128)(2,1)S(1)} collective-permute-done((bf16[128,768]{1,0:T(8,128)(2,1)S(1)}, bf16[128,768]{1,0:T(8,128)(2,1)S(1)}, u32[]{:S(2)}, u32[]{:S(2)}) %collective-permute-start.12) | collective-permute-done | bytes 196640 | tf_op jit(solution)/shard_map/ppermute | solution.py:17
  38.7 0.5 %speech_part.7 = f32[128,768]{1,0:T(8,128)S(1)} custom-call(f32[2,128]{1,0:T(2,128)S(1)} %concatenate.6.refs_1_.refs_0_, bf16[144,768]{1,0:T(8,128)(2,1)S(1)} %slice.5.refs_1_, f32[128,768]{1,0:T(8,128)S(1)} %speech_part.6.refs_2_, bf16[128,768]{1,0:T(8,128)(2,1)S(1)} %collective-permute-done.11.refs_3_, bf16[128,768]{1,0:T(8,128)(2,1)S(1)} %collective-permute-done.12.refs_4_), custom_call_target="tpu_custom_call" | custom-call | flops 1006632960 | bytes 1401856 | tf_op jit(solution)/shard_map/speech_part/pallas_call | solution.py:33
  39.3 0.3 collective-permute-done.14.refs_0_
  39.7 0.5 %speech_part.5.refs_1_ = f32[128,768]{1,0:T(8,128)S(1)} custom-call(f32[2,128]{1,0:T(2,128)S(1)} %concatenate.6.refs_1_.refs_0_, bf16[144,768]{1,0:T(8,128)(2,1)S(1)} %get-tuple-element.17.refs_4_.refs_1_, f32[128,768]{1,0:T(8,128)S(1)} %speech_part.4.refs_2_, bf16[128,768]{1,0:T(8,128)(2,1)S(1)} %collective-permute-done.11.refs_3_, ...), custom_call_target="tpu_custom_call" | custom-call | flops 1006632960 | bytes 1401856 | tf_op jit(solution)/shard_map/speech_part/pallas_call | solution.py:33
  40.2 0.8 %collective-permute-done.13.refs_2_ = f32[128,768]{1,0:T(8,128)S(1)} collective-permute-done((f32[128,768]{1,0:T(8,128)S(1)}, f32[128,768]{1,0:T(8,128)S(1)}, u32[]{:S(2)}, u32[]{:S(2)}) %collective-permute-start.13) | collective-permute-done | bytes 393248 | tf_op jit(solution)/shard_map/ppermute | solution.py:17
  41.0 1.0 %finish.1 = (f32[128,768]{1,0:T(8,128)}, f32[64,768]{1,0:T(8,128)}) custom-call(bf16[128,768]{1,0:T(8,128)(2,1)S(1)} %get-tuple-element.16.refs_0_, f32[128,768]{1,0:T(8,128)S(1)} %speech_part.5.refs_1_, f32[128,768]{1,0:T(8,128)S(1)} %collective-permute-done.13.refs_2_, bf16[64,768]{1,0:T(8,128)(2,1)S(1)} %get-tuple-element.27.refs_3_, ...), custom_call_target="tpu_custom_call" | custom-call | bytes 1867776 | tf_op jit(solution)/shard_map/finish/pallas_call | solution.py:33
  (19 shorter events, 0.4 us)
Async XLA Ops:
  1.8 10.5 %collective-permute-start.1 = (bf16[64,768]{1,0:T(8,128)(2,1)S(1)}, bf16[64,768]{1,0:T(8,128)(2,1)S(1)}, u32[]{:S(2)}, u32[]{:S(2)}) collective-permute-start(bf16[64,768]{1,0:T(8,128)(2,1)S(1)} %get-tuple-element.18.refs_0_), channel_id=1, source_target_pairs={{0,16},{8,24},{16,0},{24,8},{1,17},{9,25},{17,1},{25,9},{2,18},{10... | collective-permute-start | bytes 294920 | tf_op jit(solution)/shard_map/ppermute | solution.py:17
  5.9 11.1 %collective-permute-start.3 = (bf16[144,768]{1,0:T(8,128)(2,1)S(1)}, bf16[144,768]{1,0:T(8,128)(2,1)S(1)}, u32[]{:S(2)}, u32[]{:S(2)}) collective-permute-start(bf16[144,768]{1,0:T(8,128)(2,1)S(1)} %get-tuple-element.17.refs_4_.refs_1_), channel_id=1, source_target_pairs={{0,2},{1,3},{2,0},{3,1},{4,6},{5,7},{6,4},{7,5},{8,10},{9,11},{10,... | collective-permute-start | bytes 663560 | tf_op jit(solution)/shard_map/ppermute | solution.py:17
  7.4 11.3 %collective-permute-start.4 = (bf16[144,768]{1,0:T(8,128)(2,1)S(1)}, bf16[144,768]{1,0:T(8,128)(2,1)S(1)}, u32[]{:S(2)}, u32[]{:S(2)}) collective-permute-start(bf16[144,768]{1,0:T(8,128)(2,1)S(1)} %get-tuple-element.17.refs_4_.refs_1_), channel_id=1, source_target_pairs={{0,4},{1,5},{2,6},{3,7},{4,0},{5,1},{6,2},{7,3},{8,12},{9,13},{10,... | collective-permute-start | bytes 663560 | tf_op jit(solution)/shard_map/ppermute | solution.py:17
  8.9 9.8 %collective-permute-start.5 = (bf16[144,768]{1,0:T(8,128)(2,1)S(1)}, bf16[144,768]{1,0:T(8,128)(2,1)S(1)}, u32[]{:S(2)}, u32[]{:S(2)}) collective-permute-start(bf16[144,768]{1,0:T(8,128)(2,1)S(1)} %get-tuple-element.17.refs_4_.refs_1_), channel_id=1, source_target_pairs={{0,6},{1,7},{2,4},{3,5},{4,2},{5,3},{6,0},{7,1},{8,14},{9,15},{10,... | collective-permute-start | bytes 663560 | tf_op jit(solution)/shard_map/ppermute | solution.py:17
  9.4 5.3 %collective-permute-start = (bf16[64,768]{1,0:T(8,128)(2,1)S(1)}, bf16[64,768]{1,0:T(8,128)(2,1)S(1)}, u32[]{:S(2)}, u32[]{:S(2)}) collective-permute-start(bf16[64,768]{1,0:T(8,128)(2,1)S(1)} %get-tuple-element.18.refs_0_), channel_id=1, source_target_pairs={{0,8},{8,0},{16,24},{24,16},{1,9},{9,1},{17,25},{25,17},{2,10},{10... | collective-permute-start | bytes 294920 | tf_op jit(solution)/shard_map/ppermute | solution.py:17
  12.4 4.7 %collective-permute-start.2 = (bf16[64,768]{1,0:T(8,128)(2,1)S(1)}, bf16[64,768]{1,0:T(8,128)(2,1)S(1)}, u32[]{:S(2)}, u32[]{:S(2)}) collective-permute-start(bf16[64,768]{1,0:T(8,128)(2,1)S(1)} %pass_on.1.refs_2_), channel_id=1, source_target_pairs={{0,8},{8,0},{16,24},{24,16},{1,9},{9,1},{17,25},{25,17},{2,10},{10... | collective-permute-start | bytes 294920 | tf_op jit(solution)/shard_map/ppermute | solution.py:17
  18.9 3.0 %collective-permute-start.8 = (bf16[576,768]{1,0:T(8,128)(2,1)S(1)}, bf16[576,768]{1,0:T(8,128)(2,1)S(1)}, u32[]{:S(2)}, u32[]{:S(2)}) collective-permute-start(bf16[576,768]{1,0:T(8,128)(2,1)S(1)} %get-tuple-element.20.refs_2_), channel_id=1, source_target_pairs={{0,1},{1,0},{2,3},{3,2},{4,5},{5,4},{6,7},{7,6},{8,9},{9,8},{10,11... | collective-permute-start | bytes 2654216 | tf_op jit(solution)/shard_map/ppermute | solution.py:17
  18.9 12.5 %collective-permute-start.6 = (bf16[256,768]{1,0:T(8,128)(2,1)S(1)}, bf16[256,768]{1,0:T(8,128)(2,1)S(1)}, u32[]{:S(2)}, u32[]{:S(2)}) collective-permute-start(bf16[256,768]{1,0:T(8,128)(2,1)S(1)} %get-tuple-element.19.refs_1_.refs_2_), channel_id=1, source_target_pairs={{0,2},{1,3},{2,0},{3,1},{4,6},{5,7},{6,4},{7,5},{8,10},{9,11},{10,... | collective-permute-start | bytes 1179656 | tf_op jit(solution)/shard_map/ppermute | solution.py:17
  20.2 11.2 %collective-permute-start.7 = (bf16[256,768]{1,0:T(8,128)(2,1)S(1)}, bf16[256,768]{1,0:T(8,128)(2,1)S(1)}, u32[]{:S(2)}, u32[]{:S(2)}) collective-permute-start(bf16[256,768]{1,0:T(8,128)(2,1)S(1)} %get-tuple-element.19.refs_1_.refs_2_), channel_id=1, source_target_pairs={{0,4},{1,5},{2,6},{3,7},{4,0},{5,1},{6,2},{7,3},{8,12},{9,13},{10,... | collective-permute-start | bytes 1179656 | tf_op jit(solution)/shard_map/ppermute | solution.py:17
  22.6 5.5 %collective-permute-start.10 = (f32[64,384]{1,0:T(8,128)S(1)}, f32[64,384]{1,0:T(8,128)S(1)}, u32[]{:S(2)}, u32[]{:S(2)}) collective-permute-start(f32[64,384]{1,0:T(8,128)S(1)} %get-tuple-element.24), channel_id=1, source_target_pairs={{0,8},{8,0},{16,24},{24,16},{1,9},{9,1},{17,25},{25,17},{2,10},{10... | collective-permute-start | bytes 294920 | tf_op jit(solution)/shard_map/ppermute | solution.py:17
  24.3 7.0 %collective-permute-start.9 = (f32[64,384]{1,0:T(8,128)S(1)}, f32[64,384]{1,0:T(8,128)S(1)}, u32[]{:S(2)}, u32[]{:S(2)}) collective-permute-start(f32[64,384]{1,0:T(8,128)S(1)} %get-tuple-element.22), channel_id=1, source_target_pairs={{0,8},{8,0},{16,24},{24,16},{1,9},{9,1},{17,25},{25,17},{2,10},{10... | collective-permute-start | bytes 294920 | tf_op jit(solution)/shard_map/ppermute | solution.py:17
  24.7 14.6 %collective-permute-start.16 = (f32[64,768]{1,0:T(8,128)S(1)}, f32[64,768]{1,0:T(8,128)S(1)}, u32[]{:S(2)}, u32[]{:S(2)}) collective-permute-start(f32[64,768]{1,0:T(8,128)S(1)} %get-tuple-element.28), channel_id=1, source_target_pairs={{0,8},{8,0},{16,24},{24,16},{1,9},{9,1},{17,25},{25,17},{2,10},{10... | collective-permute-start | bytes 589832 | tf_op jit(solution)/shard_map/ppermute | solution.py:17
  28.2 11.1 %collective-permute-start.15 = (f32[64,384]{1,0:T(8,128)S(1)}, f32[64,384]{1,0:T(8,128)S(1)}, u32[]{:S(2)}, u32[]{:S(2)}) collective-permute-start(f32[64,384]{1,0:T(8,128)S(1)} %sum_near.3.refs_6_.refs_3_), channel_id=1, source_target_pairs={{0,16},{8,24},{16,0},{24,8},{1,17},{9,25},{17,1},{25,9},{2,18},{10... | collective-permute-start | bytes 294920 | tf_op jit(solution)/shard_map/ppermute | solution.py:17
  31.3 8.3 %collective-permute-start.14 = (f32[64,384]{1,0:T(8,128)S(1)}, f32[64,384]{1,0:T(8,128)S(1)}, u32[]{:S(2)}, u32[]{:S(2)}) collective-permute-start(f32[64,384]{1,0:T(8,128)S(1)} %sum_near.2.refs_5_.refs_2_), channel_id=1, source_target_pairs={{0,16},{8,24},{16,0},{24,8},{1,17},{9,25},{17,1},{25,9},{2,18},{10... | collective-permute-start | bytes 294920 | tf_op jit(solution)/shard_map/ppermute | solution.py:17
  31.5 6.2 %collective-permute-start.11 = (bf16[128,768]{1,0:T(8,128)(2,1)S(1)}, bf16[128,768]{1,0:T(8,128)(2,1)S(1)}, u32[]{:S(2)}, u32[]{:S(2)}) collective-permute-start(bf16[128,768]{1,0:T(8,128)(2,1)S(1)} %get-tuple-element.25), channel_id=1, source_target_pairs={{0,2},{1,3},{2,0},{3,1},{4,6},{5,7},{6,4},{7,5},{8,10},{9,11},{10,... | collective-permute-start | bytes 589832 | tf_op jit(solution)/shard_map/ppermute | solution.py:17
  33.0 5.7 %collective-permute-start.12 = (bf16[128,768]{1,0:T(8,128)(2,1)S(1)}, bf16[128,768]{1,0:T(8,128)(2,1)S(1)}, u32[]{:S(2)}, u32[]{:S(2)}) collective-permute-start(bf16[128,768]{1,0:T(8,128)(2,1)S(1)} %get-tuple-element.26), channel_id=1, source_target_pairs={{0,4},{1,5},{2,6},{3,7},{4,0},{5,1},{6,2},{7,3},{8,12},{9,13},{10,... | collective-permute-start | bytes 589832 | tf_op jit(solution)/shard_map/ppermute | solution.py:17
  39.2 1.8 %collective-permute-start.13 = (f32[128,768]{1,0:T(8,128)S(1)}, f32[128,768]{1,0:T(8,128)S(1)}, u32[]{:S(2)}, u32[]{:S(2)}) collective-permute-start(f32[128,768]{1,0:T(8,128)S(1)} %speech_part.7), channel_id=1, source_target_pairs={{0,1},{1,0},{2,3},{3,2},{4,5},{5,4},{6,7},{7,6},{8,9},{9,8},{10,11... | collective-permute-start | bytes 1179656 | tf_op jit(solution)/shard_map/ppermute | solution.py:17

commit v13 on v12

--- a/solution.py
+++ b/solution.py
@@ -228,7 +228,7 @@
     )(*[pltpu.with_memory_space_constraint(v, pltpu.HBM) for v in arguments])
 
     def passed_on(block):
-        return call(join_body, bf16(own_text, width), [block], (scalars,), 1 << 29, name="pass_on")
+        return call(join_body, bf16(own_text, width), [block], (), 1 << 20, name="pass_on")
 
     text_blocks = [text_own] + [None] * (groups - 1)
     for k in [1 << i for i in reversed(range(groups.bit_length() - 1))]:
@@ -243,7 +243,7 @@
         halves = call(
             halves_body, [bf16(size, width) for size in sizes], near[::-1], after, name="halves"
         )
-        return [exchanged(half, "member", 2 * k) for half, k in zip(halves, masks)]
+        return [(half, exchanged(half, "member", 2 * k)) for half, k in zip(halves, masks)]
 
     speech_blocks = [exchanged(speech_own, "member", 2 * k) for k in reversed(range(1, chips))]
     column = groups * own_text
@@ -251,6 +251,7 @@
         functools.partial(join_both_body, groups),
         [bf16(column, width), bf16(chips * (rows + MARK_ROWS), width)],
         [*text_blocks, speech_own, *speech_blocks[::-1]],
+        (scalars,),
         name="join_rows",
     )
     other = exchanged(speech, "member", 1)
@@ -272,14 +273,23 @@
     parts = list(text_part(outs, [other], half))
     far = [parts[groups // 2 + i * sides :][:sides] for i in range(groups // 2)]
 
+    text_far = []
     bit = 1
     while bit < groups // 2:
         for k in reversed(range(bit, groups // 2, 2 * bit)):
             came = [exchanged(v, "group", bit) for v in far[k]]
-            far[k - bit] = [
-                call(sum_body, side, [mine, v], name="sum_near") for mine, v in zip(far[k - bit], came)
-            ]
+            sums = []
+            for mine, v in zip(far[k - bit], came):
+                if sums and square and not text_far:
+                    text_far = far_halves(text_near, column // 2, tuple(sums))
+                    gate = (text_far[0][0],)
+                else:
+                    gate = ()
+                sums.append(call(sum_body, side, [mine, v], gate, name="sum_near"))
+            far[k - bit] = sums
         bit *= 2
+    if square:
+        text_far = [came for _, came in text_far]
     from_far = [exchanged(v, "group", groups // 2) for v in far[0]]
     from_near = [exchanged(parts[k], "group", k) for k in range(1, groups // 2)]
 
@@ -293,7 +303,6 @@
     away = speech_part(other[0 : rows + MARK_ROWS], [], *near)
     home = speech_part(speech_own, [], *near)
     if square:
-        text_far = far_halves(text_near, column // 2, tuple(far[0]))
         away = speech_part(other[0 : rows + MARK_ROWS], [away], [3], text_far)
         home = speech_part(speech_own, [home], [3], text_far)
     back = exchanged(away, "member", 1)

time: 42.2 us -> 43.1 us (1.021)
  starting transfers between devices: 18.4 us -> 25.5 us
  waiting for transfers between devices: 14.5 us -> 8.27 us
    ppermute x17, starting transfers between devices: 18.4 us -> 25.5 us  [exchanged(): return lax.ppermute(value, axis, [(i, i ^ mask) for i in range(size)])]
    ppermute x17, waiting for transfers between devices: 14.5 us -> 8.27 us  [exchanged(): return lax.ppermute(value, axis, [(i, i ^ mask) for i in range(size)])]
  transfers between devices with their start and end apart: 17 -> 17, of which waited for: 9 -> 6; matrix products, arithmetic and copies ran while one was open for 0% -> 0% of each run, Pallas kernels for 11% -> 11%
where the time goes in v13:
time: 43.1 us; the launch traced here: 43 us
  starting transfers between devices  25.5 us (59%)
  waiting for transfers between devices  8.27 us (19%)
  Pallas kernels  7.03 us (16%)
  between operations  2.08 us (5%)
    ppermute x17, starting transfers between devices, exchanged(): return lax.ppermute(value, axis, [(i, i ^ mask) for i in range(size)])  25.5 us
    ppermute x17, waiting for transfers between devices, exchanged(): return lax.ppermute(value, axis, [(i, i ^ mask) for i in range(size)])  8.27 us
    pallas_call x13, Pallas kernels, call(): pl.pallas_call(whole, out_shape=out_shape, in_specs=specs, out_specs=jax....  5.85 us
    pallas_call x1, Pallas kernels, shards(): pl.pallas_call(prepare_body, out_shape=[bf16(rows + MARK_ROWS, width), bf...  1.18 us
  transfers between devices with their start and end apart: 17, of which 6 were waited for; matrix products, arithmetic and copies ran while one was open for 0% of the time, Pallas kernels for 11%

profile of v13, /device:TPU:0, one launch (start us, length us, event | category | flops | bytes accessed | tf_op | source)
XLA Modules:
  0.0 43.0 jit_solution(9256485413947119950)
XLA Ops:
  0.6 1.2 %unit_rows.1 = (bf16[144,768]{1,0:T(8,128)(2,1)S(1)}, bf16[64,768]{1,0:T(8,128)(2,1)S(1)}, bf16[128,768]{1,0:T(8,128)(2,1)S(1)}, bf16[64,768]{1,0:T(8,128)(2,1)S(1)}) custom-call(bf16[128,768]{1,0:T(8,128)(2,1)} %refs_0_.1, bf16[64,768]{1,0:T(8,128)(2,1)} %refs_1_.1, s32[1,128]{1,0:T(1,128)} %bitcast.3), custom_call_target="tpu_custom_call" | custom-call | tf_op jit(solution)/shard_map/unit_rows/pallas_call | solution.py:215
  1.8 3.0 %collective-permute-start.3 = (bf16[144,768]{1,0:T(8,128)(2,1)S(1)}, bf16[144,768]{1,0:T(8,128)(2,1)S(1)}, u32[]{:S(2)}, u32[]{:S(2)}) collective-permute-start(bf16[144,768]{1,0:T(8,128)(2,1)S(1)} %get-tuple-element.17.refs_4_.refs_1_), channel_id=1, source_target_pairs={{0,2},{1,3},{2,0},{3,1},{4,6},{5,7},{6,4},{7,5},{8,10},{9,11},{10,... | collective-permute-start | bytes 663560 | tf_op jit(solution)/shard_map/ppermute | solution.py:17
  4.8 1.5 %collective-permute-start.4 = (bf16[144,768]{1,0:T(8,128)(2,1)S(1)}, bf16[144,768]{1,0:T(8,128)(2,1)S(1)}, u32[]{:S(2)}, u32[]{:S(2)}) collective-permute-start(bf16[144,768]{1,0:T(8,128)(2,1)S(1)} %get-tuple-element.17.refs_4_.refs_1_), channel_id=1, source_target_pairs={{0,4},{1,5},{2,6},{3,7},{4,0},{5,1},{6,2},{7,3},{8,12},{9,13},{10,... | collective-permute-start | bytes 663560 | tf_op jit(solution)/shard_map/ppermute | solution.py:17
  6.4 3.0 %collective-permute-start.1 = (bf16[64,768]{1,0:T(8,128)(2,1)S(1)}, bf16[64,768]{1,0:T(8,128)(2,1)S(1)}, u32[]{:S(2)}, u32[]{:S(2)}) collective-permute-start(bf16[64,768]{1,0:T(8,128)(2,1)S(1)} %get-tuple-element.18.refs_0_), channel_id=1, source_target_pairs={{0,16},{8,24},{16,0},{24,8},{1,17},{9,25},{17,1},{25,9},{2,18},{10... | collective-permute-start | bytes 294920 | tf_op jit(solution)/shard_map/ppermute | solution.py:17
  9.4 1.6 %collective-permute-start = (bf16[64,768]{1,0:T(8,128)(2,1)S(1)}, bf16[64,768]{1,0:T(8,128)(2,1)S(1)}, u32[]{:S(2)}, u32[]{:S(2)}) collective-permute-start(bf16[64,768]{1,0:T(8,128)(2,1)S(1)} %get-tuple-element.18.refs_0_), channel_id=1, source_target_pairs={{0,8},{8,0},{16,24},{24,16},{1,9},{9,1},{17,25},{25,17},{2,10},{10... | collective-permute-start | bytes 294920 | tf_op jit(solution)/shard_map/ppermute | solution.py:17
  11.0 1.5 %collective-permute-done.1.refs_0_ = bf16[64,768]{1,0:T(8,128)(2,1)S(1)} collective-permute-done((bf16[64,768]{1,0:T(8,128)(2,1)S(1)}, bf16[64,768]{1,0:T(8,128)(2,1)S(1)}, u32[]{:S(2)}, u32[]{:S(2)}) %collective-permute-start.1) | collective-permute-done | bytes 98336 | tf_op jit(solution)/shard_map/ppermute | solution.py:17
  12.5 1.7 %collective-permute-start.2 = (bf16[64,768]{1,0:T(8,128)(2,1)S(1)}, bf16[64,768]{1,0:T(8,128)(2,1)S(1)}, u32[]{:S(2)}, u32[]{:S(2)}) collective-permute-start(bf16[64,768]{1,0:T(8,128)(2,1)S(1)} %pass_on.1.refs_2_), channel_id=1, source_target_pairs={{0,8},{8,0},{16,24},{24,16},{1,9},{9,1},{17,25},{25,17},{2,10},{10... | collective-permute-start | bytes 294920 | tf_op jit(solution)/shard_map/ppermute | solution.py:17
  15.5 1.7 %collective-permute-done.2.refs_3_ = bf16[64,768]{1,0:T(8,128)(2,1)S(1)} collective-permute-done((bf16[64,768]{1,0:T(8,128)(2,1)S(1)}, bf16[64,768]{1,0:T(8,128)(2,1)S(1)}, u32[]{:S(2)}, u32[]{:S(2)}) %collective-permute-start.2) | collective-permute-done | bytes 98336 | tf_op jit(solution)/shard_map/ppermute | solution.py:17
  17.2 0.1 concatenate.6.refs_8_.refs_0_
  17.3 0.1 join_rows.1
  17.4 0.1 collective-permute-start.8
  17.5 1.6 %collective-permute-start.6 = (bf16[256,768]{1,0:T(8,128)(2,1)S(1)}, bf16[256,768]{1,0:T(8,128)(2,1)S(1)}, u32[]{:S(2)}, u32[]{:S(2)}) collective-permute-start(bf16[256,768]{1,0:T(8,128)(2,1)S(1)} %get-tuple-element.19.refs_1_.refs_2_), channel_id=1, source_target_pairs={{0,2},{1,3},{2,0},{3,1},{4,6},{5,7},{6,4},{7,5},{8,10},{9,11},{10,... | collective-permute-start | bytes 1179656 | tf_op jit(solution)/shard_map/ppermute | solution.py:17
  19.1 1.5 %collective-permute-start.7 = (bf16[256,768]{1,0:T(8,128)(2,1)S(1)}, bf16[256,768]{1,0:T(8,128)(2,1)S(1)}, u32[]{:S(2)}, u32[]{:S(2)}) collective-permute-start(bf16[256,768]{1,0:T(8,128)(2,1)S(1)} %get-tuple-element.19.refs_1_.refs_2_), channel_id=1, source_target_pairs={{0,4},{1,5},{2,6},{3,7},{4,0},{5,1},{6,2},{7,3},{8,12},{9,13},{10,... | collective-permute-start | bytes 1179656 | tf_op jit(solution)/shard_map/ppermute | solution.py:17
  20.6 0.8 %text_part.2.refs_2_ = f32[256,768]{1,0:T(8,128)S(1)} custom-call(f32[2,128]{1,0:T(2,128)S(1)} %concatenate.6.refs_8_.refs_0_, bf16[256,768]{1,0:T(8,128)(2,1)S(1)} %get-tuple-element.19.refs_1_.refs_2_, bf16[576,768]{1,0:T(8,128)(2,1)S(1)} %get-tuple-element.20.refs_2_), custom_call_target="tpu_custom_call" | custom-call | flops 402653184 | bytes 2065408 | tf_op jit(solution)/shard_map/text_part/pallas_call | solution.py:33
  21.4 0.8 %text_part.3 = (f32[64,768]{1,0:T(8,128)S(1)}, f32[64,768]{1,0:T(8,128)S(1)}, f32[64,384]{1,0:T(8,128)S(1)}, f32[64,384]{1,0:T(8,128)S(1)}, f32[64,384]{1,0:T(8,128)S(1)}, /*index=5*/f32[64,384]{1,0:T(8,128)S(1)}) custom-call(f32[2,128]{1,0:T(2,128)S(1)} %concatenate.6.refs_8_.refs_0_, bf16[256,768]{1,0:T(8,128)(2,1)S(1)} %get-tuple-element.19.refs_1_.refs_2_, ...), custom_call_target="tpu_custom_call" | custom-call | flops 402653184 | bytes 2851840 | tf_op jit(solution)/shard_map/text_part/pallas_call | solution.py:33
  22.2 1.7 %collective-permute-start.9 = (f32[64,384]{1,0:T(8,128)S(1)}, f32[64,384]{1,0:T(8,128)S(1)}, u32[]{:S(2)}, u32[]{:S(2)}) collective-permute-start(f32[64,384]{1,0:T(8,128)S(1)} %get-tuple-element.22), channel_id=1, source_target_pairs={{0,8},{8,0},{16,24},{24,16},{1,9},{9,1},{17,25},{25,17},{2,10},{10... | collective-permute-start | bytes 294920 | tf_op jit(solution)/shard_map/ppermute | solution.py:17
  23.8 0.4 %collective-permute-start.10 = (f32[64,384]{1,0:T(8,128)S(1)}, f32[64,384]{1,0:T(8,128)S(1)}, u32[]{:S(2)}, u32[]{:S(2)}) collective-permute-start(f32[64,384]{1,0:T(8,128)S(1)} %get-tuple-element.24), channel_id=1, source_target_pairs={{0,8},{8,0},{16,24},{24,16},{1,9},{9,1},{17,25},{25,17},{2,10},{10... | collective-permute-start | bytes 294920 | tf_op jit(solution)/shard_map/ppermute | solution.py:17
  24.3 1.6 %collective-permute-start.16 = (f32[64,768]{1,0:T(8,128)S(1)}, f32[64,768]{1,0:T(8,128)S(1)}, u32[]{:S(2)}, u32[]{:S(2)}) collective-permute-start(f32[64,768]{1,0:T(8,128)S(1)} %get-tuple-element.28), channel_id=1, source_target_pairs={{0,8},{8,0},{16,24},{24,16},{1,9},{9,1},{17,25},{25,17},{2,10},{10... | collective-permute-start | bytes 589832 | tf_op jit(solution)/shard_map/ppermute | solution.py:17
  25.9 1.8 %collective-permute-done.9.refs_1_ = f32[64,384]{1,0:T(8,128)S(1)} collective-permute-done((f32[64,384]{1,0:T(8,128)S(1)}, f32[64,384]{1,0:T(8,128)S(1)}, u32[]{:S(2)}, u32[]{:S(2)}) %collective-permute-start.9) | collective-permute-done | bytes 98336 | tf_op jit(solution)/shard_map/ppermute | solution.py:17
  27.7 3.2 %collective-permute-start.14 = (f32[64,384]{1,0:T(8,128)S(1)}, f32[64,384]{1,0:T(8,128)S(1)}, u32[]{:S(2)}, u32[]{:S(2)}) collective-permute-start(f32[64,384]{1,0:T(8,128)S(1)} %sum_near.2.refs_2_.refs_5_), channel_id=1, source_target_pairs={{0,16},{8,24},{16,0},{24,8},{1,17},{9,25},{17,1},{25,9},{2,18},{10... | collective-permute-start | bytes 294920 | tf_op jit(solution)/shard_map/ppermute | solution.py:17
  30.9 0.6 %collective-permute-start.11 = (bf16[128,768]{1,0:T(8,128)(2,1)S(1)}, bf16[128,768]{1,0:T(8,128)(2,1)S(1)}, u32[]{:S(2)}, u32[]{:S(2)}) collective-permute-start(bf16[128,768]{1,0:T(8,128)(2,1)S(1)} %get-tuple-element.25.refs_2_), channel_id=1, source_target_pairs={{0,2},{1,3},{2,0},{3,1},{4,6},{5,7},{6,4},{7,5},{8,10},{9,11},{10,... | collective-permute-start | bytes 589832 | tf_op jit(solution)/shard_map/ppermute | solution.py:17
  31.5 2.4 %collective-permute-start.15 = (f32[64,384]{1,0:T(8,128)S(1)}, f32[64,384]{1,0:T(8,128)S(1)}, u32[]{:S(2)}, u32[]{:S(2)}) collective-permute-start(f32[64,384]{1,0:T(8,128)S(1)} %sum_near.3.refs_6_), channel_id=1, source_target_pairs={{0,16},{8,24},{16,0},{24,8},{1,17},{9,25},{17,1},{25,9},{2,18},{10... | collective-permute-start | bytes 294920 | tf_op jit(solution)/shard_map/ppermute | solution.py:17
  34.0 1.5 %collective-permute-start.12 = (bf16[128,768]{1,0:T(8,128)(2,1)S(1)}, bf16[128,768]{1,0:T(8,128)(2,1)S(1)}, u32[]{:S(2)}, u32[]{:S(2)}) collective-permute-start(bf16[128,768]{1,0:T(8,128)(2,1)S(1)} %get-tuple-element.26), channel_id=1, source_target_pairs={{0,4},{1,5},{2,6},{3,7},{4,0},{5,1},{6,2},{7,3},{8,12},{9,13},{10,... | collective-permute-start | bytes 589832 | tf_op jit(solution)/shard_map/ppermute | solution.py:17
  35.5 1.0 %speech_part.4.refs_2_ = f32[128,768]{1,0:T(8,128)S(1)} custom-call(f32[2,128]{1,0:T(2,128)S(1)} %concatenate.6.refs_8_.refs_0_, bf16[144,768]{1,0:T(8,128)(2,1)S(1)} %get-tuple-element.17.refs_4_.refs_1_, bf16[256,768]{1,0:T(8,128)(2,1)S(1)} %get-tuple-element.19.refs_1_.refs_2_, bf16[256,768]{1,0:T(8,128)(2,1)S(1)} %collective-permute-done.6.refs_1_.refs_3_, ...), custom_call_target="tpu_custom_call" | custom-call | flops 3019898880 | bytes 1795072 | tf_op jit(solution)/shard_map/speech_part/pallas_call | solution.py:33
  36.5 1.0 %speech_part.6.refs_2_ = f32[128,768]{1,0:T(8,128)S(1)} custom-call(f32[2,128]{1,0:T(2,128)S(1)} %concatenate.6.refs_8_.refs_0_, bf16[144,768]{1,0:T(8,128)(2,1)S(1)} %slice.5.refs_1_, bf16[256,768]{1,0:T(8,128)(2,1)S(1)} %get-tuple-element.19.refs_1_.refs_2_, bf16[256,768]{1,0:T(8,128)(2,1)S(1)} %collective-permute-done.6.refs_1_.refs_3_, ...), custom_call_target="tpu_custom_call" | custom-call | flops 3019898880 | bytes 1795072 | tf_op jit(solution)/shard_map/speech_part/pallas_call | solution.py:33
  37.5 2.1 %collective-permute-done.12.refs_4_ = bf16[128,768]{1,0:T(8,128)(2,1)S(1)} collective-permute-done((bf16[128,768]{1,0:T(8,128)(2,1)S(1)}, bf16[128,768]{1,0:T(8,128)(2,1)S(1)}, u32[]{:S(2)}, u32[]{:S(2)}) %collective-permute-start.12) | collective-permute-done | bytes 196640 | tf_op jit(solution)/shard_map/ppermute | solution.py:17
  39.6 0.5 %speech_part.7 = f32[128,768]{1,0:T(8,128)S(1)} custom-call(f32[2,128]{1,0:T(2,128)S(1)} %concatenate.6.refs_8_.refs_0_, bf16[144,768]{1,0:T(8,128)(2,1)S(1)} %slice.5.refs_1_, f32[128,768]{1,0:T(8,128)S(1)} %speech_part.6.refs_2_, bf16[128,768]{1,0:T(8,128)(2,1)S(1)} %collective-permute-done.11.refs_3_, bf16[128,768]{1,0:T(8,128)(2,1)S(1)} %collective-permute-done.12.refs_4_), custom_call_target="tpu_custom_call" | custom-call | flops 1006632960 | bytes 1401856 | tf_op jit(solution)/shard_map/speech_part/pallas_call | solution.py:33
  40.1 0.1 collective-permute-start.13
  40.2 0.6 %collective-permute-done.15.refs_1_ = f32[64,384]{1,0:T(8,128)S(1)} collective-permute-done((f32[64,384]{1,0:T(8,128)S(1)}, f32[64,384]{1,0:T(8,128)S(1)}, u32[]{:S(2)}, u32[]{:S(2)}) %collective-permute-start.15) | collective-permute-done | bytes 98336 | tf_op jit(solution)/shard_map/ppermute | solution.py:17
  40.9 0.5 %speech_part.5.refs_1_ = f32[128,768]{1,0:T(8,128)S(1)} custom-call(f32[2,128]{1,0:T(2,128)S(1)} %concatenate.6.refs_8_.refs_0_, bf16[144,768]{1,0:T(8,128)(2,1)S(1)} %get-tuple-element.17.refs_4_.refs_1_, f32[128,768]{1,0:T(8,128)S(1)} %speech_part.4.refs_2_, bf16[128,768]{1,0:T(8,128)(2,1)S(1)} %collective-permute-done.11.refs_3_, ...), custom_call_target="tpu_custom_call" | custom-call | flops 1006632960 | bytes 1401856 | tf_op jit(solution)/shard_map/speech_part/pallas_call | solution.py:33
  41.4 0.5 %collective-permute-done.13.refs_2_ = f32[128,768]{1,0:T(8,128)S(1)} collective-permute-done((f32[128,768]{1,0:T(8,128)S(1)}, f32[128,768]{1,0:T(8,128)S(1)}, u32[]{:S(2)}, u32[]{:S(2)}) %collective-permute-start.13) | collective-permute-done | bytes 393248 | tf_op jit(solution)/shard_map/ppermute | solution.py:17
  41.9 1.0 %finish.1 = (f32[128,768]{1,0:T(8,128)}, f32[64,768]{1,0:T(8,128)}) custom-call(bf16[128,768]{1,0:T(8,128)(2,1)S(1)} %get-tuple-element.16.refs_0_, f32[128,768]{1,0:T(8,128)S(1)} %speech_part.5.refs_1_, f32[128,768]{1,0:T(8,128)S(1)} %collective-permute-done.13.refs_2_, bf16[64,768]{1,0:T(8,128)(2,1)S(1)} %get-tuple-element.27.refs_3_, ...), custom_call_target="tpu_custom_call" | custom-call | bytes 1867776 | tf_op jit(solution)/shard_map/finish/pallas_call | solution.py:33
  (19 shorter events, 0.2 us)
Async XLA Ops:
  1.8 15.4 %collective-permute-start.3 = (bf16[144,768]{1,0:T(8,128)(2,1)S(1)}, bf16[144,768]{1,0:T(8,128)(2,1)S(1)}, u32[]{:S(2)}, u32[]{:S(2)}) collective-permute-start(bf16[144,768]{1,0:T(8,128)(2,1)S(1)} %get-tuple-element.17.refs_4_.refs_1_), channel_id=1, source_target_pairs={{0,2},{1,3},{2,0},{3,1},{4,6},{5,7},{6,4},{7,5},{8,10},{9,11},{10,... | collective-permute-start | bytes 663560 | tf_op jit(solution)/shard_map/ppermute | solution.py:17
  4.8 12.4 %collective-permute-start.4 = (bf16[144,768]{1,0:T(8,128)(2,1)S(1)}, bf16[144,768]{1,0:T(8,128)(2,1)S(1)}, u32[]{:S(2)}, u32[]{:S(2)}) collective-permute-start(bf16[144,768]{1,0:T(8,128)(2,1)S(1)} %get-tuple-element.17.refs_4_.refs_1_), channel_id=1, source_target_pairs={{0,4},{1,5},{2,6},{3,7},{4,0},{5,1},{6,2},{7,3},{8,12},{9,13},{10,... | collective-permute-start | bytes 663560 | tf_op jit(solution)/shard_map/ppermute | solution.py:17
  6.3 10.9 %collective-permute-start.5 = (bf16[144,768]{1,0:T(8,128)(2,1)S(1)}, bf16[144,768]{1,0:T(8,128)(2,1)S(1)}, u32[]{:S(2)}, u32[]{:S(2)}) collective-permute-start(bf16[144,768]{1,0:T(8,128)(2,1)S(1)} %get-tuple-element.17.refs_4_.refs_1_), channel_id=1, source_target_pairs={{0,6},{1,7},{2,4},{3,5},{4,2},{5,3},{6,0},{7,1},{8,14},{9,15},{10,... | collective-permute-start | bytes 663560 | tf_op jit(solution)/shard_map/ppermute | solution.py:17
  6.4 6.2 %collective-permute-start.1 = (bf16[64,768]{1,0:T(8,128)(2,1)S(1)}, bf16[64,768]{1,0:T(8,128)(2,1)S(1)}, u32[]{:S(2)}, u32[]{:S(2)}) collective-permute-start(bf16[64,768]{1,0:T(8,128)(2,1)S(1)} %get-tuple-element.18.refs_0_), channel_id=1, source_target_pairs={{0,16},{8,24},{16,0},{24,8},{1,17},{9,25},{17,1},{25,9},{2,18},{10... | collective-permute-start | bytes 294920 | tf_op jit(solution)/shard_map/ppermute | solution.py:17
  9.4 6.1 %collective-permute-start = (bf16[64,768]{1,0:T(8,128)(2,1)S(1)}, bf16[64,768]{1,0:T(8,128)(2,1)S(1)}, u32[]{:S(2)}, u32[]{:S(2)}) collective-permute-start(bf16[64,768]{1,0:T(8,128)(2,1)S(1)} %get-tuple-element.18.refs_0_), channel_id=1, source_target_pairs={{0,8},{8,0},{16,24},{24,16},{1,9},{9,1},{17,25},{25,17},{2,10},{10... | collective-permute-start | bytes 294920 | tf_op jit(solution)/shard_map/ppermute | solution.py:17
  12.5 4.7 %collective-permute-start.2 = (bf16[64,768]{1,0:T(8,128)(2,1)S(1)}, bf16[64,768]{1,0:T(8,128)(2,1)S(1)}, u32[]{:S(2)}, u32[]{:S(2)}) collective-permute-start(bf16[64,768]{1,0:T(8,128)(2,1)S(1)} %pass_on.1.refs_2_), channel_id=1, source_target_pairs={{0,8},{8,0},{16,24},{24,16},{1,9},{9,1},{17,25},{25,17},{2,10},{10... | collective-permute-start | bytes 294920 | tf_op jit(solution)/shard_map/ppermute | solution.py:17
  17.4 4.0 %collective-permute-start.8 = (bf16[576,768]{1,0:T(8,128)(2,1)S(1)}, bf16[576,768]{1,0:T(8,128)(2,1)S(1)}, u32[]{:S(2)}, u32[]{:S(2)}) collective-permute-start(bf16[576,768]{1,0:T(8,128)(2,1)S(1)} %get-tuple-element.20.refs_2_), channel_id=1, source_target_pairs={{0,1},{1,0},{2,3},{3,2},{4,5},{5,4},{6,7},{7,6},{8,9},{9,8},{10,11... | collective-permute-start | bytes 2654216 | tf_op jit(solution)/shard_map/ppermute | solution.py:17
  17.5 13.4 %collective-permute-start.6 = (bf16[256,768]{1,0:T(8,128)(2,1)S(1)}, bf16[256,768]{1,0:T(8,128)(2,1)S(1)}, u32[]{:S(2)}, u32[]{:S(2)}) collective-permute-start(bf16[256,768]{1,0:T(8,128)(2,1)S(1)} %get-tuple-element.19.refs_1_.refs_2_), channel_id=1, source_target_pairs={{0,2},{1,3},{2,0},{3,1},{4,6},{5,7},{6,4},{7,5},{8,10},{9,11},{10,... | collective-permute-start | bytes 1179656 | tf_op jit(solution)/shard_map/ppermute | solution.py:17
  19.1 11.8 %collective-permute-start.7 = (bf16[256,768]{1,0:T(8,128)(2,1)S(1)}, bf16[256,768]{1,0:T(8,128)(2,1)S(1)}, u32[]{:S(2)}, u32[]{:S(2)}) collective-permute-start(bf16[256,768]{1,0:T(8,128)(2,1)S(1)} %get-tuple-element.19.refs_1_.refs_2_), channel_id=1, source_target_pairs={{0,4},{1,5},{2,6},{3,7},{4,0},{5,1},{6,2},{7,3},{8,12},{9,13},{10,... | collective-permute-start | bytes 1179656 | tf_op jit(solution)/shard_map/ppermute | solution.py:17
  22.2 5.5 %collective-permute-start.9 = (f32[64,384]{1,0:T(8,128)S(1)}, f32[64,384]{1,0:T(8,128)S(1)}, u32[]{:S(2)}, u32[]{:S(2)}) collective-permute-start(f32[64,384]{1,0:T(8,128)S(1)} %get-tuple-element.22), channel_id=1, source_target_pairs={{0,8},{8,0},{16,24},{24,16},{1,9},{9,1},{17,25},{25,17},{2,10},{10... | collective-permute-start | bytes 294920 | tf_op jit(solution)/shard_map/ppermute | solution.py:17
  23.8 7.7 %collective-permute-start.10 = (f32[64,384]{1,0:T(8,128)S(1)}, f32[64,384]{1,0:T(8,128)S(1)}, u32[]{:S(2)}, u32[]{:S(2)}) collective-permute-start(f32[64,384]{1,0:T(8,128)S(1)} %get-tuple-element.24), channel_id=1, source_target_pairs={{0,8},{8,0},{16,24},{24,16},{1,9},{9,1},{17,25},{25,17},{2,10},{10... | collective-permute-start | bytes 294920 | tf_op jit(solution)/shard_map/ppermute | solution.py:17
  24.3 16.0 %collective-permute-start.16 = (f32[64,768]{1,0:T(8,128)S(1)}, f32[64,768]{1,0:T(8,128)S(1)}, u32[]{:S(2)}, u32[]{:S(2)}) collective-permute-start(f32[64,768]{1,0:T(8,128)S(1)} %get-tuple-element.28), channel_id=1, source_target_pairs={{0,8},{8,0},{16,24},{24,16},{1,9},{9,1},{17,25},{25,17},{2,10},{10... | collective-permute-start | bytes 589832 | tf_op jit(solution)/shard_map/ppermute | solution.py:17
  27.7 13.1 %collective-permute-start.14 = (f32[64,384]{1,0:T(8,128)S(1)}, f32[64,384]{1,0:T(8,128)S(1)}, u32[]{:S(2)}, u32[]{:S(2)}) collective-permute-start(f32[64,384]{1,0:T(8,128)S(1)} %sum_near.2.refs_2_.refs_5_), channel_id=1, source_target_pairs={{0,16},{8,24},{16,0},{24,8},{1,17},{9,25},{17,1},{25,9},{2,18},{10... | collective-permute-start | bytes 294920 | tf_op jit(solution)/shard_map/ppermute | solution.py:17
  30.9 6.6 %collective-permute-start.11 = (bf16[128,768]{1,0:T(8,128)(2,1)S(1)}, bf16[128,768]{1,0:T(8,128)(2,1)S(1)}, u32[]{:S(2)}, u32[]{:S(2)}) collective-permute-start(bf16[128,768]{1,0:T(8,128)(2,1)S(1)} %get-tuple-element.25.refs_2_), channel_id=1, source_target_pairs={{0,2},{1,3},{2,0},{3,1},{4,6},{5,7},{6,4},{7,5},{8,10},{9,11},{10,... | collective-permute-start | bytes 589832 | tf_op jit(solution)/shard_map/ppermute | solution.py:17
  31.5 9.3 %collective-permute-start.15 = (f32[64,384]{1,0:T(8,128)S(1)}, f32[64,384]{1,0:T(8,128)S(1)}, u32[]{:S(2)}, u32[]{:S(2)}) collective-permute-start(f32[64,384]{1,0:T(8,128)S(1)} %sum_near.3.refs_6_), channel_id=1, source_target_pairs={{0,16},{8,24},{16,0},{24,8},{1,17},{9,25},{17,1},{25,9},{2,18},{10... | collective-permute-start | bytes 294920 | tf_op jit(solution)/shard_map/ppermute | solution.py:17
  34.0 5.7 %collective-permute-start.12 = (bf16[128,768]{1,0:T(8,128)(2,1)S(1)}, bf16[128,768]{1,0:T(8,128)(2,1)S(1)}, u32[]{:S(2)}, u32[]{:S(2)}) collective-permute-start(bf16[128,768]{1,0:T(8,128)(2,1)S(1)} %get-tuple-element.26), channel_id=1, source_target_pairs={{0,4},{1,5},{2,6},{3,7},{4,0},{5,1},{6,2},{7,3},{8,12},{9,13},{10,... | collective-permute-start | bytes 589832 | tf_op jit(solution)/shard_map/ppermute | solution.py:17
  40.1 1.8 %collective-permute-start.13 = (f32[128,768]{1,0:T(8,128)S(1)}, f32[128,768]{1,0:T(8,128)S(1)}, u32[]{:S(2)}, u32[]{:S(2)}) collective-permute-start(f32[128,768]{1,0:T(8,128)S(1)} %speech_part.7), channel_id=1, source_target_pairs={{0,1},{1,0},{2,3},{3,2},{4,5},{5,4},{6,7},{7,6},{8,9},{9,8},{10,11... | collective-permute-start | bytes 1179656 | tf_op jit(solution)/shard_map/ppermute | solution.py:17

commit v14 on v13

--- a/solution.py
+++ b/solution.py
@@ -228,7 +228,7 @@
     )(*[pltpu.with_memory_space_constraint(v, pltpu.HBM) for v in arguments])
 
     def passed_on(block):
-        return call(join_body, bf16(own_text, width), [block], (), 1 << 20, name="pass_on")
+        return call(join_body, bf16(own_text, width), [block], (), 1 << 29, name="pass_on")
 
     text_blocks = [text_own] + [None] * (groups - 1)
     for k in [1 << i for i in reversed(range(groups.bit_length() - 1))]:

time: 43.1 us -> 42.1 us (0.977)
  starting transfers between devices: 25.5 us -> 18.9 us
  waiting for transfers between devices: 8.27 us -> 13.8 us
    ppermute x17, starting transfers between devices: 25.5 us -> 18.9 us  [exchanged(): return lax.ppermute(value, axis, [(i, i ^ mask) for i in range(size)])]
    ppermute x17, waiting for transfers between devices: 8.27 us -> 13.8 us  [exchanged(): return lax.ppermute(value, axis, [(i, i ^ mask) for i in range(size)])]
  transfers between devices with their start and end apart: 17 -> 17, of which waited for: 6 -> 10; matrix products, arithmetic and copies ran while one was open for 0% -> 0% of each run, Pallas kernels for 11% -> 11%
where the time goes in v14:
time: 42.1 us; the launch traced here: 41.9 us
  starting transfers between devices  18.9 us (45%)
  waiting for transfers between devices  13.8 us (33%)
  Pallas kernels  7.03 us (17%)
  between operations  2.06 us (5%)
    ppermute x17, starting transfers between devices, exchanged(): return lax.ppermute(value, axis, [(i, i ^ mask) for i in range(size)])  18.9 us
    ppermute x17, waiting for transfers between devices, exchanged(): return lax.ppermute(value, axis, [(i, i ^ mask) for i in range(size)])  13.8 us
    pallas_call x13, Pallas kernels, call(): pl.pallas_call(whole, out_shape=out_shape, in_specs=specs, out_specs=jax....  5.85 us
    pallas_call x1, Pallas kernels, shards(): pl.pallas_call(prepare_body, out_shape=[bf16(rows + MARK_ROWS, width), bf...  1.18 us
  transfers between devices with their start and end apart: 17, of which 10 were waited for; matrix products, arithmetic and copies ran while one was open for 0% of the time, Pallas kernels for 11%

profile of v14, /device:TPU:0, one launch (start us, length us, event | category | flops | bytes accessed | tf_op | source)
XLA Modules:
  0.0 41.9 jit_solution(7497506051215385453)
XLA Ops:
  0.6 1.2 %unit_rows.1 = (bf16[144,768]{1,0:T(8,128)(2,1)S(1)}, bf16[64,768]{1,0:T(8,128)(2,1)S(1)}, bf16[128,768]{1,0:T(8,128)(2,1)S(1)}, bf16[64,768]{1,0:T(8,128)(2,1)S(1)}) custom-call(bf16[128,768]{1,0:T(8,128)(2,1)} %refs_0_.1, bf16[64,768]{1,0:T(8,128)(2,1)} %refs_1_.1, s32[1,128]{1,0:T(1,128)} %bitcast.3), custom_call_target="tpu_custom_call" | custom-call | tf_op jit(solution)/shard_map/unit_rows/pallas_call | solution.py:215
  1.8 4.1 %collective-permute-start.1 = (bf16[64,768]{1,0:T(8,128)(2,1)S(1)}, bf16[64,768]{1,0:T(8,128)(2,1)S(1)}, u32[]{:S(2)}, u32[]{:S(2)}) collective-permute-start(bf16[64,768]{1,0:T(8,128)(2,1)S(1)} %get-tuple-element.18.refs_0_), channel_id=1, source_target_pairs={{0,16},{8,24},{16,0},{24,8},{1,17},{9,25},{17,1},{25,9},{2,18},{10... | collective-permute-start | bytes 294920 | tf_op jit(solution)/shard_map/ppermute | solution.py:17
  5.9 1.5 %collective-permute-start.3 = (bf16[144,768]{1,0:T(8,128)(2,1)S(1)}, bf16[144,768]{1,0:T(8,128)(2,1)S(1)}, u32[]{:S(2)}, u32[]{:S(2)}) collective-permute-start(bf16[144,768]{1,0:T(8,128)(2,1)S(1)} %get-tuple-element.17.refs_4_.refs_1_), channel_id=1, source_target_pairs={{0,2},{1,3},{2,0},{3,1},{4,6},{5,7},{6,4},{7,5},{8,10},{9,11},{10,... | collective-permute-start | bytes 663560 | tf_op jit(solution)/shard_map/ppermute | solution.py:17
  7.4 1.5 %collective-permute-start.4 = (bf16[144,768]{1,0:T(8,128)(2,1)S(1)}, bf16[144,768]{1,0:T(8,128)(2,1)S(1)}, u32[]{:S(2)}, u32[]{:S(2)}) collective-permute-start(bf16[144,768]{1,0:T(8,128)(2,1)S(1)} %get-tuple-element.17.refs_4_.refs_1_), channel_id=1, source_target_pairs={{0,4},{1,5},{2,6},{3,7},{4,0},{5,1},{6,2},{7,3},{8,12},{9,13},{10,... | collective-permute-start | bytes 663560 | tf_op jit(solution)/shard_map/ppermute | solution.py:17
  8.9 0.5 %collective-permute-start.5 = (bf16[144,768]{1,0:T(8,128)(2,1)S(1)}, bf16[144,768]{1,0:T(8,128)(2,1)S(1)}, u32[]{:S(2)}, u32[]{:S(2)}) collective-permute-start(bf16[144,768]{1,0:T(8,128)(2,1)S(1)} %get-tuple-element.17.refs_4_.refs_1_), channel_id=1, source_target_pairs={{0,6},{1,7},{2,4},{3,5},{4,2},{5,3},{6,0},{7,1},{8,14},{9,15},{10,... | collective-permute-start | bytes 663560 | tf_op jit(solution)/shard_map/ppermute | solution.py:17
  9.4 1.6 %collective-permute-start = (bf16[64,768]{1,0:T(8,128)(2,1)S(1)}, bf16[64,768]{1,0:T(8,128)(2,1)S(1)}, u32[]{:S(2)}, u32[]{:S(2)}) collective-permute-start(bf16[64,768]{1,0:T(8,128)(2,1)S(1)} %get-tuple-element.18.refs_0_), channel_id=1, source_target_pairs={{0,8},{8,0},{16,24},{24,16},{1,9},{9,1},{17,25},{25,17},{2,10},{10... | collective-permute-start | bytes 294920 | tf_op jit(solution)/shard_map/ppermute | solution.py:17
  11.0 0.6 %collective-permute-start.2 = (bf16[64,768]{1,0:T(8,128)(2,1)S(1)}, bf16[64,768]{1,0:T(8,128)(2,1)S(1)}, u32[]{:S(2)}, u32[]{:S(2)}) collective-permute-start(bf16[64,768]{1,0:T(8,128)(2,1)S(1)} %pass_on.1.refs_2_), channel_id=1, source_target_pairs={{0,8},{8,0},{16,24},{24,16},{1,9},{9,1},{17,25},{25,17},{2,10},{10... | collective-permute-start | bytes 294920 | tf_op jit(solution)/shard_map/ppermute | solution.py:17
  12.9 1.9 %collective-permute-done.refs_1_ = bf16[64,768]{1,0:T(8,128)(2,1)S(1)} collective-permute-done((bf16[64,768]{1,0:T(8,128)(2,1)S(1)}, bf16[64,768]{1,0:T(8,128)(2,1)S(1)}, u32[]{:S(2)}, u32[]{:S(2)}) %collective-permute-start) | collective-permute-done | bytes 98336 | tf_op jit(solution)/shard_map/ppermute | solution.py:17
  14.9 1.1 %collective-permute-done.2.refs_3_ = bf16[64,768]{1,0:T(8,128)(2,1)S(1)} collective-permute-done((bf16[64,768]{1,0:T(8,128)(2,1)S(1)}, bf16[64,768]{1,0:T(8,128)(2,1)S(1)}, u32[]{:S(2)}, u32[]{:S(2)}) %collective-permute-start.2) | collective-permute-done | bytes 98336 | tf_op jit(solution)/shard_map/ppermute | solution.py:17
  15.9 2.8 %collective-permute-done.4.refs_6_ = bf16[144,768]{1,0:T(8,128)(2,1)S(1)} collective-permute-done((bf16[144,768]{1,0:T(8,128)(2,1)S(1)}, bf16[144,768]{1,0:T(8,128)(2,1)S(1)}, u32[]{:S(2)}, u32[]{:S(2)}) %collective-permute-start.4) | collective-permute-done | bytes 221216 | tf_op jit(solution)/shard_map/ppermute | solution.py:17
  19.0 1.3 %collective-permute-start.6 = (bf16[256,768]{1,0:T(8,128)(2,1)S(1)}, bf16[256,768]{1,0:T(8,128)(2,1)S(1)}, u32[]{:S(2)}, u32[]{:S(2)}) collective-permute-start(bf16[256,768]{1,0:T(8,128)(2,1)S(1)} %get-tuple-element.19.refs_1_.refs_2_), channel_id=1, source_target_pairs={{0,2},{1,3},{2,0},{3,1},{4,6},{5,7},{6,4},{7,5},{8,10},{9,11},{10,... | collective-permute-start | bytes 1179656 | tf_op jit(solution)/shard_map/ppermute | solution.py:17
  20.3 0.8 %collective-permute-start.7 = (bf16[256,768]{1,0:T(8,128)(2,1)S(1)}, bf16[256,768]{1,0:T(8,128)(2,1)S(1)}, u32[]{:S(2)}, u32[]{:S(2)}) collective-permute-start(bf16[256,768]{1,0:T(8,128)(2,1)S(1)} %get-tuple-element.19.refs_1_.refs_2_), channel_id=1, source_target_pairs={{0,4},{1,5},{2,6},{3,7},{4,0},{5,1},{6,2},{7,3},{8,12},{9,13},{10,... | collective-permute-start | bytes 1179656 | tf_op jit(solution)/shard_map/ppermute | solution.py:17
  21.1 0.8 %text_part.2.refs_2_ = f32[256,768]{1,0:T(8,128)S(1)} custom-call(f32[2,128]{1,0:T(2,128)S(1)} %concatenate.6.refs_8_.refs_0_, bf16[256,768]{1,0:T(8,128)(2,1)S(1)} %get-tuple-element.19.refs_1_.refs_2_, bf16[576,768]{1,0:T(8,128)(2,1)S(1)} %get-tuple-element.20.refs_2_), custom_call_target="tpu_custom_call" | custom-call | flops 402653184 | bytes 2065408 | tf_op jit(solution)/shard_map/text_part/pallas_call | solution.py:33
  21.9 0.8 %text_part.3 = (f32[64,768]{1,0:T(8,128)S(1)}, f32[64,768]{1,0:T(8,128)S(1)}, f32[64,384]{1,0:T(8,128)S(1)}, f32[64,384]{1,0:T(8,128)S(1)}, f32[64,384]{1,0:T(8,128)S(1)}, /*index=5*/f32[64,384]{1,0:T(8,128)S(1)}) custom-call(f32[2,128]{1,0:T(2,128)S(1)} %concatenate.6.refs_8_.refs_0_, bf16[256,768]{1,0:T(8,128)(2,1)S(1)} %get-tuple-element.19.refs_1_.refs_2_, ...), custom_call_target="tpu_custom_call" | custom-call | flops 402653184 | bytes 2851840 | tf_op jit(solution)/shard_map/text_part/pallas_call | solution.py:33
  22.7 1.6 %collective-permute-start.9 = (f32[64,384]{1,0:T(8,128)S(1)}, f32[64,384]{1,0:T(8,128)S(1)}, u32[]{:S(2)}, u32[]{:S(2)}) collective-permute-start(f32[64,384]{1,0:T(8,128)S(1)} %get-tuple-element.22), channel_id=1, source_target_pairs={{0,8},{8,0},{16,24},{24,16},{1,9},{9,1},{17,25},{25,17},{2,10},{10... | collective-permute-start | bytes 294920 | tf_op jit(solution)/shard_map/ppermute | solution.py:17
  24.3 0.4 %collective-permute-start.10 = (f32[64,384]{1,0:T(8,128)S(1)}, f32[64,384]{1,0:T(8,128)S(1)}, u32[]{:S(2)}, u32[]{:S(2)}) collective-permute-start(f32[64,384]{1,0:T(8,128)S(1)} %get-tuple-element.24), channel_id=1, source_target_pairs={{0,8},{8,0},{16,24},{24,16},{1,9},{9,1},{17,25},{25,17},{2,10},{10... | collective-permute-start | bytes 294920 | tf_op jit(solution)/shard_map/ppermute | solution.py:17
  24.8 1.6 %collective-permute-start.16 = (f32[64,768]{1,0:T(8,128)S(1)}, f32[64,768]{1,0:T(8,128)S(1)}, u32[]{:S(2)}, u32[]{:S(2)}) collective-permute-start(f32[64,768]{1,0:T(8,128)S(1)} %get-tuple-element.28), channel_id=1, source_target_pairs={{0,8},{8,0},{16,24},{24,16},{1,9},{9,1},{17,25},{25,17},{2,10},{10... | collective-permute-start | bytes 589832 | tf_op jit(solution)/shard_map/ppermute | solution.py:17
  26.4 1.8 %collective-permute-done.9.refs_1_ = f32[64,384]{1,0:T(8,128)S(1)} collective-permute-done((f32[64,384]{1,0:T(8,128)S(1)}, f32[64,384]{1,0:T(8,128)S(1)}, u32[]{:S(2)}, u32[]{:S(2)}) %collective-permute-start.9) | collective-permute-done | bytes 98336 | tf_op jit(solution)/shard_map/ppermute | solution.py:17
  28.2 0.4 collective-permute-start.14
  28.6 1.9 %collective-permute-done.6.refs_1_.refs_3_ = bf16[256,768]{1,0:T(8,128)(2,1)S(1)} collective-permute-done((bf16[256,768]{1,0:T(8,128)(2,1)S(1)}, bf16[256,768]{1,0:T(8,128)(2,1)S(1)}, u32[]{:S(2)}, u32[]{:S(2)}) %collective-permute-start.6) | collective-permute-done | bytes 393248 | tf_op jit(solution)/shard_map/ppermute | solution.py:17
  30.5 1.0 %collective-permute-done.7.refs_0_.refs_4_ = bf16[256,768]{1,0:T(8,128)(2,1)S(1)} collective-permute-done((bf16[256,768]{1,0:T(8,128)(2,1)S(1)}, bf16[256,768]{1,0:T(8,128)(2,1)S(1)}, u32[]{:S(2)}, u32[]{:S(2)}) %collective-permute-start.7) | collective-permute-done | bytes 393248 | tf_op jit(solution)/shard_map/ppermute | solution.py:17
  31.5 0.9 %collective-permute-start.11 = (bf16[128,768]{1,0:T(8,128)(2,1)S(1)}, bf16[128,768]{1,0:T(8,128)(2,1)S(1)}, u32[]{:S(2)}, u32[]{:S(2)}) collective-permute-start(bf16[128,768]{1,0:T(8,128)(2,1)S(1)} %get-tuple-element.25.refs_2_), channel_id=1, source_target_pairs={{0,2},{1,3},{2,0},{3,1},{4,6},{5,7},{6,4},{7,5},{8,10},{9,11},{10,... | collective-permute-start | bytes 589832 | tf_op jit(solution)/shard_map/ppermute | solution.py:17
  32.4 0.5 %collective-permute-start.15 = (f32[64,384]{1,0:T(8,128)S(1)}, f32[64,384]{1,0:T(8,128)S(1)}, u32[]{:S(2)}, u32[]{:S(2)}) collective-permute-start(f32[64,384]{1,0:T(8,128)S(1)} %sum_near.3.refs_6_), channel_id=1, source_target_pairs={{0,16},{8,24},{16,0},{24,8},{1,17},{9,25},{17,1},{25,9},{2,18},{10... | collective-permute-start | bytes 294920 | tf_op jit(solution)/shard_map/ppermute | solution.py:17
  32.9 1.4 %collective-permute-start.12 = (bf16[128,768]{1,0:T(8,128)(2,1)S(1)}, bf16[128,768]{1,0:T(8,128)(2,1)S(1)}, u32[]{:S(2)}, u32[]{:S(2)}) collective-permute-start(bf16[128,768]{1,0:T(8,128)(2,1)S(1)} %get-tuple-element.26), channel_id=1, source_target_pairs={{0,4},{1,5},{2,6},{3,7},{4,0},{5,1},{6,2},{7,3},{8,12},{9,13},{10,... | collective-permute-start | bytes 589832 | tf_op jit(solution)/shard_map/ppermute | solution.py:17
  34.3 1.0 %speech_part.4.refs_2_ = f32[128,768]{1,0:T(8,128)S(1)} custom-call(f32[2,128]{1,0:T(2,128)S(1)} %concatenate.6.refs_8_.refs_0_, bf16[144,768]{1,0:T(8,128)(2,1)S(1)} %get-tuple-element.17.refs_4_.refs_1_, bf16[256,768]{1,0:T(8,128)(2,1)S(1)} %get-tuple-element.19.refs_1_.refs_2_, bf16[256,768]{1,0:T(8,128)(2,1)S(1)} %collective-permute-done.6.refs_1_.refs_3_, ...), custom_call_target="tpu_custom_call" | custom-call | flops 3019898880 | bytes 1795072 | tf_op jit(solution)/shard_map/speech_part/pallas_call | solution.py:33
  35.4 1.0 %speech_part.6.refs_2_ = f32[128,768]{1,0:T(8,128)S(1)} custom-call(f32[2,128]{1,0:T(2,128)S(1)} %concatenate.6.refs_8_.refs_0_, bf16[144,768]{1,0:T(8,128)(2,1)S(1)} %slice.5.refs_1_, bf16[256,768]{1,0:T(8,128)(2,1)S(1)} %get-tuple-element.19.refs_1_.refs_2_, bf16[256,768]{1,0:T(8,128)(2,1)S(1)} %collective-permute-done.6.refs_1_.refs_3_, ...), custom_call_target="tpu_custom_call" | custom-call | flops 3019898880 | bytes 1795072 | tf_op jit(solution)/shard_map/speech_part/pallas_call | solution.py:33
  36.4 1.3 %collective-permute-done.11.refs_3_ = bf16[128,768]{1,0:T(8,128)(2,1)S(1)} collective-permute-done((bf16[128,768]{1,0:T(8,128)(2,1)S(1)}, bf16[128,768]{1,0:T(8,128)(2,1)S(1)}, u32[]{:S(2)}, u32[]{:S(2)}) %collective-permute-start.11) | collective-permute-done | bytes 196640 | tf_op jit(solution)/shard_map/ppermute | solution.py:17
  37.7 0.9 %collective-permute-done.12.refs_4_ = bf16[128,768]{1,0:T(8,128)(2,1)S(1)} collective-permute-done((bf16[128,768]{1,0:T(8,128)(2,1)S(1)}, bf16[128,768]{1,0:T(8,128)(2,1)S(1)}, u32[]{:S(2)}, u32[]{:S(2)}) %collective-permute-start.12) | collective-permute-done | bytes 196640 | tf_op jit(solution)/shard_map/ppermute | solution.py:17
  38.6 0.5 %speech_part.7 = f32[128,768]{1,0:T(8,128)S(1)} custom-call(f32[2,128]{1,0:T(2,128)S(1)} %concatenate.6.refs_8_.refs_0_, bf16[144,768]{1,0:T(8,128)(2,1)S(1)} %slice.5.refs_1_, f32[128,768]{1,0:T(8,128)S(1)} %speech_part.6.refs_2_, bf16[128,768]{1,0:T(8,128)(2,1)S(1)} %collective-permute-done.11.refs_3_, bf16[128,768]{1,0:T(8,128)(2,1)S(1)} %collective-permute-done.12.refs_4_), custom_call_target="tpu_custom_call" | custom-call | flops 1006632960 | bytes 1401856 | tf_op jit(solution)/shard_map/speech_part/pallas_call | solution.py:33
  39.2 0.9 %collective-permute-done.15.refs_1_ = f32[64,384]{1,0:T(8,128)S(1)} collective-permute-done((f32[64,384]{1,0:T(8,128)S(1)}, f32[64,384]{1,0:T(8,128)S(1)}, u32[]{:S(2)}, u32[]{:S(2)}) %collective-permute-start.15) | collective-permute-done | bytes 98336 | tf_op jit(solution)/shard_map/ppermute | solution.py:17
  40.1 0.5 %speech_part.5.refs_1_ = f32[128,768]{1,0:T(8,128)S(1)} custom-call(f32[2,128]{1,0:T(2,128)S(1)} %concatenate.6.refs_8_.refs_0_, bf16[144,768]{1,0:T(8,128)(2,1)S(1)} %get-tuple-element.17.refs_4_.refs_1_, f32[128,768]{1,0:T(8,128)S(1)} %speech_part.4.refs_2_, bf16[128,768]{1,0:T(8,128)(2,1)S(1)} %collective-permute-done.11.refs_3_, ...), custom_call_target="tpu_custom_call" | custom-call | flops 1006632960 | bytes 1401856 | tf_op jit(solution)/shard_map/speech_part/pallas_call | solution.py:33
  40.9 1.0 %finish.1 = (f32[128,768]{1,0:T(8,128)}, f32[64,768]{1,0:T(8,128)}) custom-call(bf16[128,768]{1,0:T(8,128)(2,1)S(1)} %get-tuple-element.16.refs_0_, f32[128,768]{1,0:T(8,128)S(1)} %speech_part.5.refs_1_, f32[128,768]{1,0:T(8,128)S(1)} %collective-permute-done.13.refs_2_, bf16[64,768]{1,0:T(8,128)(2,1)S(1)} %get-tuple-element.27.refs_3_, ...), custom_call_target="tpu_custom_call" | custom-call | bytes 1867776 | tf_op jit(solution)/shard_map/finish/pallas_call | solution.py:33
  (19 shorter events, 0.7 us)
Async XLA Ops:
  1.8 9.2 %collective-permute-start.1 = (bf16[64,768]{1,0:T(8,128)(2,1)S(1)}, bf16[64,768]{1,0:T(8,128)(2,1)S(1)}, u32[]{:S(2)}, u32[]{:S(2)}) collective-permute-start(bf16[64,768]{1,0:T(8,128)(2,1)S(1)} %get-tuple-element.18.refs_0_), channel_id=1, source_target_pairs={{0,16},{8,24},{16,0},{24,8},{1,17},{9,25},{17,1},{25,9},{2,18},{10... | collective-permute-start | bytes 294920 | tf_op jit(solution)/shard_map/ppermute | solution.py:17
  5.9 10.0 %collective-permute-start.3 = (bf16[144,768]{1,0:T(8,128)(2,1)S(1)}, bf16[144,768]{1,0:T(8,128)(2,1)S(1)}, u32[]{:S(2)}, u32[]{:S(2)}) collective-permute-start(bf16[144,768]{1,0:T(8,128)(2,1)S(1)} %get-tuple-element.17.refs_4_.refs_1_), channel_id=1, source_target_pairs={{0,2},{1,3},{2,0},{3,1},{4,6},{5,7},{6,4},{7,5},{8,10},{9,11},{10,... | collective-permute-start | bytes 663560 | tf_op jit(solution)/shard_map/ppermute | solution.py:17
  7.4 11.3 %collective-permute-start.4 = (bf16[144,768]{1,0:T(8,128)(2,1)S(1)}, bf16[144,768]{1,0:T(8,128)(2,1)S(1)}, u32[]{:S(2)}, u32[]{:S(2)}) collective-permute-start(bf16[144,768]{1,0:T(8,128)(2,1)S(1)} %get-tuple-element.17.refs_4_.refs_1_), channel_id=1, source_target_pairs={{0,4},{1,5},{2,6},{3,7},{4,0},{5,1},{6,2},{7,3},{8,12},{9,13},{10,... | collective-permute-start | bytes 663560 | tf_op jit(solution)/shard_map/ppermute | solution.py:17
  8.9 9.8 %collective-permute-start.5 = (bf16[144,768]{1,0:T(8,128)(2,1)S(1)}, bf16[144,768]{1,0:T(8,128)(2,1)S(1)}, u32[]{:S(2)}, u32[]{:S(2)}) collective-permute-start(bf16[144,768]{1,0:T(8,128)(2,1)S(1)} %get-tuple-element.17.refs_4_.refs_1_), channel_id=1, source_target_pairs={{0,6},{1,7},{2,4},{3,5},{4,2},{5,3},{6,0},{7,1},{8,14},{9,15},{10,... | collective-permute-start | bytes 663560 | tf_op jit(solution)/shard_map/ppermute | solution.py:17
  9.4 5.5 %collective-permute-start = (bf16[64,768]{1,0:T(8,128)(2,1)S(1)}, bf16[64,768]{1,0:T(8,128)(2,1)S(1)}, u32[]{:S(2)}, u32[]{:S(2)}) collective-permute-start(bf16[64,768]{1,0:T(8,128)(2,1)S(1)} %get-tuple-element.18.refs_0_), channel_id=1, source_target_pairs={{0,8},{8,0},{16,24},{24,16},{1,9},{9,1},{17,25},{25,17},{2,10},{10... | collective-permute-start | bytes 294920 | tf_op jit(solution)/shard_map/ppermute | solution.py:17
  11.0 4.9 %collective-permute-start.2 = (bf16[64,768]{1,0:T(8,128)(2,1)S(1)}, bf16[64,768]{1,0:T(8,128)(2,1)S(1)}, u32[]{:S(2)}, u32[]{:S(2)}) collective-permute-start(bf16[64,768]{1,0:T(8,128)(2,1)S(1)} %pass_on.1.refs_2_), channel_id=1, source_target_pairs={{0,8},{8,0},{16,24},{24,16},{1,9},{9,1},{17,25},{25,17},{2,10},{10... | collective-permute-start | bytes 294920 | tf_op jit(solution)/shard_map/ppermute | solution.py:17
  18.9 3.0 %collective-permute-start.8 = (bf16[576,768]{1,0:T(8,128)(2,1)S(1)}, bf16[576,768]{1,0:T(8,128)(2,1)S(1)}, u32[]{:S(2)}, u32[]{:S(2)}) collective-permute-start(bf16[576,768]{1,0:T(8,128)(2,1)S(1)} %get-tuple-element.20.refs_2_), channel_id=1, source_target_pairs={{0,1},{1,0},{2,3},{3,2},{4,5},{5,4},{6,7},{7,6},{8,9},{9,8},{10,11... | collective-permute-start | bytes 2654216 | tf_op jit(solution)/shard_map/ppermute | solution.py:17
  19.0 11.5 %collective-permute-start.6 = (bf16[256,768]{1,0:T(8,128)(2,1)S(1)}, bf16[256,768]{1,0:T(8,128)(2,1)S(1)}, u32[]{:S(2)}, u32[]{:S(2)}) collective-permute-start(bf16[256,768]{1,0:T(8,128)(2,1)S(1)} %get-tuple-element.19.refs_1_.refs_2_), channel_id=1, source_target_pairs={{0,2},{1,3},{2,0},{3,1},{4,6},{5,7},{6,4},{7,5},{8,10},{9,11},{10,... | collective-permute-start | bytes 1179656 | tf_op jit(solution)/shard_map/ppermute | solution.py:17
  20.3 11.2 %collective-permute-start.7 = (bf16[256,768]{1,0:T(8,128)(2,1)S(1)}, bf16[256,768]{1,0:T(8,128)(2,1)S(1)}, u32[]{:S(2)}, u32[]{:S(2)}) collective-permute-start(bf16[256,768]{1,0:T(8,128)(2,1)S(1)} %get-tuple-element.19.refs_1_.refs_2_), channel_id=1, source_target_pairs={{0,4},{1,5},{2,6},{3,7},{4,0},{5,1},{6,2},{7,3},{8,12},{9,13},{10,... | collective-permute-start | bytes 1179656 | tf_op jit(solution)/shard_map/ppermute | solution.py:17
  22.7 5.5 %collective-permute-start.9 = (f32[64,384]{1,0:T(8,128)S(1)}, f32[64,384]{1,0:T(8,128)S(1)}, u32[]{:S(2)}, u32[]{:S(2)}) collective-permute-start(f32[64,384]{1,0:T(8,128)S(1)} %get-tuple-element.22), channel_id=1, source_target_pairs={{0,8},{8,0},{16,24},{24,16},{1,9},{9,1},{17,25},{25,17},{2,10},{10... | collective-permute-start | bytes 294920 | tf_op jit(solution)/shard_map/ppermute | solution.py:17
  24.3 8.0 %collective-permute-start.10 = (f32[64,384]{1,0:T(8,128)S(1)}, f32[64,384]{1,0:T(8,128)S(1)}, u32[]{:S(2)}, u32[]{:S(2)}) collective-permute-start(f32[64,384]{1,0:T(8,128)S(1)} %get-tuple-element.24), channel_id=1, source_target_pairs={{0,8},{8,0},{16,24},{24,16},{1,9},{9,1},{17,25},{25,17},{2,10},{10... | collective-permute-start | bytes 294920 | tf_op jit(solution)/shard_map/ppermute | solution.py:17
  24.8 14.4 %collective-permute-start.16 = (f32[64,768]{1,0:T(8,128)S(1)}, f32[64,768]{1,0:T(8,128)S(1)}, u32[]{:S(2)}, u32[]{:S(2)}) collective-permute-start(f32[64,768]{1,0:T(8,128)S(1)} %get-tuple-element.28), channel_id=1, source_target_pairs={{0,8},{8,0},{16,24},{24,16},{1,9},{9,1},{17,25},{25,17},{2,10},{10... | collective-permute-start | bytes 589832 | tf_op jit(solution)/shard_map/ppermute | solution.py:17
  28.2 11.9 %collective-permute-start.14 = (f32[64,384]{1,0:T(8,128)S(1)}, f32[64,384]{1,0:T(8,128)S(1)}, u32[]{:S(2)}, u32[]{:S(2)}) collective-permute-start(f32[64,384]{1,0:T(8,128)S(1)} %sum_near.2.refs_2_.refs_5_), channel_id=1, source_target_pairs={{0,16},{8,24},{16,0},{24,8},{1,17},{9,25},{17,1},{25,9},{2,18},{10... | collective-permute-start | bytes 294920 | tf_op jit(solution)/shard_map/ppermute | solution.py:17
  31.5 6.2 %collective-permute-start.11 = (bf16[128,768]{1,0:T(8,128)(2,1)S(1)}, bf16[128,768]{1,0:T(8,128)(2,1)S(1)}, u32[]{:S(2)}, u32[]{:S(2)}) collective-permute-start(bf16[128,768]{1,0:T(8,128)(2,1)S(1)} %get-tuple-element.25.refs_2_), channel_id=1, source_target_pairs={{0,2},{1,3},{2,0},{3,1},{4,6},{5,7},{6,4},{7,5},{8,10},{9,11},{10,... | collective-permute-start | bytes 589832 | tf_op jit(solution)/shard_map/ppermute | solution.py:17
  32.4 7.7 %collective-permute-start.15 = (f32[64,384]{1,0:T(8,128)S(1)}, f32[64,384]{1,0:T(8,128)S(1)}, u32[]{:S(2)}, u32[]{:S(2)}) collective-permute-start(f32[64,384]{1,0:T(8,128)S(1)} %sum_near.3.refs_6_), channel_id=1, source_target_pairs={{0,16},{8,24},{16,0},{24,8},{1,17},{9,25},{17,1},{25,9},{2,18},{10... | collective-permute-start | bytes 294920 | tf_op jit(solution)/shard_map/ppermute | solution.py:17
  32.9 5.7 %collective-permute-start.12 = (bf16[128,768]{1,0:T(8,128)(2,1)S(1)}, bf16[128,768]{1,0:T(8,128)(2,1)S(1)}, u32[]{:S(2)}, u32[]{:S(2)}) collective-permute-start(bf16[128,768]{1,0:T(8,128)(2,1)S(1)} %get-tuple-element.26), channel_id=1, source_target_pairs={{0,4},{1,5},{2,6},{3,7},{4,0},{5,1},{6,2},{7,3},{8,12},{9,13},{10,... | collective-permute-start | bytes 589832 | tf_op jit(solution)/shard_map/ppermute | solution.py:17
  39.1 1.8 %collective-permute-start.13 = (f32[128,768]{1,0:T(8,128)S(1)}, f32[128,768]{1,0:T(8,128)S(1)}, u32[]{:S(2)}, u32[]{:S(2)}) collective-permute-start(f32[128,768]{1,0:T(8,128)S(1)} %speech_part.7), channel_id=1, source_target_pairs={{0,1},{1,0},{2,3},{3,2},{4,5},{5,4},{6,7},{7,6},{8,9},{9,8},{10,11... | collective-permute-start | bytes 1179656 | tf_op jit(solution)/shard_map/ppermute | solution.py:17

commit v15 on v14

--- a/solution.py
+++ b/solution.py
@@ -6,7 +6,8 @@
 from jax.experimental.pallas import tpu as pltpu
 from jax.sharding import PartitionSpec as P
 
-MARK_ROWS = 16
+MARK_ROWS = 8
+TILE_ROWS = 16
 RADIX = 256
 CHUNK = 512
 EARLY = 1 << 33
@@ -77,9 +78,36 @@
         at += ref.shape[0]
 
 
+def digits_of(rows, block):
+    digits = block[rows : rows + MARK_ROWS, 0 : 2 * rows].astype(jnp.float32)
+    return digits[0:1, 0:rows], digits[0:1, rows : 2 * rows]
+
+
+def mark_rows_of(chips, rows):
+    chunks = -(-chips // (CHUNK // rows))
+    return -(-2 * chunks // TILE_ROWS) * TILE_ROWS
+
+
 def join_both_body(count, *refs):
-    join_body(*refs[:count], refs[-2])
-    join_body(*refs[count:-2], refs[-1])
+    text, speech = refs[-2:]
+    join_body(*refs[:count], text)
+    blocks = refs[count:-2]
+    rows = blocks[0].shape[0] - MARK_ROWS
+    width = speech.shape[1]
+    for k, ref in enumerate(blocks):
+        speech[k * rows : (k + 1) * rows, :] = ref[0:rows, :]
+    per = CHUNK // rows
+    height = mark_rows_of(len(blocks), rows)
+    place = lax.broadcasted_iota(jnp.int32, (height, width), 0)
+    table = jnp.zeros((height, width), jnp.float32)
+    for chunk in range(0, len(blocks), per):
+        both = [digits_of(rows, ref) for ref in blocks[chunk : chunk + per]]
+        for i in range(2):
+            parts = [digits[i] for digits in both]
+            rest = width - rows * len(parts)
+            line = jnp.concatenate([*parts, jnp.zeros((1, rest), jnp.float32)], axis=1)
+            table = jnp.where(place == 2 * (chunk // per) + i, line, table)
+    speech[len(blocks) * rows :, :] = table.astype(jnp.bfloat16)
 
 
 def halves_body(upper, lower, upper_out, lower_out):
@@ -87,9 +115,9 @@
     lower_out[...] = lower[upper_out.shape[0] :, :]
 
 
-def marks_of(block, rows):
-    digits = block[rows : rows + MARK_ROWS, 0 : 2 * rows][0:1, :].astype(jnp.float32)
-    return digits[:, 0:rows] + RADIX * digits[:, rows : 2 * rows]
+def marks_of(table, chunk, count):
+    digits = table[2 * chunk : 2 * chunk + 2, 0:count]
+    return digits[0:1, :] + RADIX * digits[1:2, :]
 
 
 def coefficients(dots, match, sharp, shift):
@@ -102,33 +130,25 @@
     return lax.dot_general(left, right, (((1,), (1,)), ((), ())), preferred_element_type=jnp.float32)
 
 
-def text_part_body(rows, own_text, ks, has_start, speeches, *refs):
+def text_part_body(rows, own_text, has_start, chips, *refs):
     sharp, shift = refs[0][0:1, 0:1], refs[0][1:2, 0:1]
-    some_text = slice(ks[0] * own_text, (ks[-1] + 1) * own_text)
-    text = refs[1][some_text, :]
-    total = refs[2][some_text, :] if has_start else None
-    at = 3 if has_start else 2
-    blocks = refs[at : at + speeches]
-    outs = refs[at + speeches :]
+    text, speech = refs[1][...], refs[2]
+    total = refs[3][...] if has_start else None
+    outs = refs[4 if has_start else 3 :]
     groups = lax.axis_size("group")
     members = lax.axis_size("member")
     group = lax.axis_index("group")
     member = lax.axis_index("member")
-    stride = rows + MARK_ROWS
-    for speech in blocks:
-        count = speech.shape[0] // stride
-        for first in range(0, count, CHUNK // rows):
-            some = range(first, min(count, first + CHUNK // rows))
-            chunk = [speech[k * stride : k * stride + rows, :] for k in some]
-            marks = [marks_of(speech.at[k * stride : (k + 1) * stride, :], rows) for k in some]
-            chunk = jnp.concatenate(chunk, axis=0)
-            marks = jnp.concatenate(marks, axis=1)
-            iota = lax.broadcasted_iota(jnp.int32, (own_text, marks.shape[1]), 0)
-            ids = [((group ^ k) * members + member) * own_text + iota for k in ks]
-            match = jnp.concatenate(ids, axis=0).astype(jnp.float32) == marks
-            coef = coefficients(dot_rows(text, chunk), match, sharp, shift)
-            part = jnp.dot(coef, chunk, preferred_element_type=jnp.float32)
-            total = part if total is None else total + part
+    table = speech[chips * rows :, :].astype(jnp.float32)
+    for first in range(0, chips * rows, CHUNK):
+        chunk = speech[first : min(first + CHUNK, chips * rows), :]
+        marks = marks_of(table, first // CHUNK, chunk.shape[0])
+        iota = lax.broadcasted_iota(jnp.int32, (own_text, chunk.shape[0]), 0)
+        ids = [((group ^ k) * members + member) * own_text + iota for k in range(groups)]
+        match = jnp.concatenate(ids, axis=0).astype(jnp.float32) == marks
+        coef = coefficients(dot_rows(text, chunk), match, sharp, shift)
+        part = jnp.dot(coef, chunk, preferred_element_type=jnp.float32)
+        total = part if total is None else total + part
     row, at = 0, 0
     for out in outs:
         out[...] = total[row : row + out.shape[0], at : at + out.shape[1]]
@@ -137,15 +157,16 @@
             row, at = row + out.shape[0], 0
 
 
-def speech_part_body(rows, own_text, has_start, masks, *refs):
+def speech_part_body(rows, own_text, has_start, chips, masks, outputs, *refs):
     sharp, shift, speech = refs[0][0:1, 0:1], refs[0][1:2, 0:1], refs[1]
     total = refs[2][...] if has_start else None
-    texts, out = list(refs[3 if has_start else 2 : -1]), refs[-1]
+    texts, outs = list(refs[3 if has_start else 2 : -outputs]), refs[-outputs:]
     groups = lax.axis_size("group")
     members = lax.axis_size("member")
     group = lax.axis_index("group")
     member = lax.axis_index("member")
-    marks = jnp.broadcast_to(marks_of(speech, rows), (rows, rows)).T[:, 0:1]
+    table = speech[chips * rows :, :].astype(jnp.float32)
+    marks = jnp.broadcast_to(marks_of(table, 0, rows), (rows, rows)).T[:, 0:1]
     block = speech[0:rows, :]
     column = groups * own_text
     lane = lax.broadcasted_iota(jnp.int32, (1, column), 1)
@@ -159,7 +180,8 @@
         coef = coefficients(dot_rows(block, text), marks == ids, sharp, shift)
         part = jnp.dot(coef, text, preferred_element_type=jnp.float32)
         total = part if total is None else total + part
-    out[...] = total
+    for k, out in enumerate(outs):
+        out[...] = total[k * out.shape[0] : (k + 1) * out.shape[0], :]
 
 
 def add_sides_body(*refs):
@@ -183,15 +205,29 @@
     refs[-1][...] = total
 
 
-def project(values, back, out):
+def project(values, back):
     heading, norms = direction(values)
     along = jnp.sum(heading * back, axis=-1, keepdims=True)
-    out[...] = (back - heading * along) / norms
-
-
-def finish_body(audio, home, back, sentence, text_back, speech_grad, text_grad):
-    project(sentence[...], text_back[...], text_grad)
-    project(audio[...], home[...] + back[...], speech_grad)
+    return (back - heading * along) / norms
+
+
+def finish_body(pieces, audio, home, *refs):
+    backs, (sentence, text_back) = refs[:pieces], refs[pieces : pieces + 2]
+    speech_grad, text_grad, speech_held, text_held, done = refs[pieces + 2 :]
+    text_held[...] = project(sentence[...], text_back[...])
+    copies = [pltpu.make_async_copy(text_held, text_grad, done.at[0])]
+    copies[0].start()
+    for i, back in enumerate(backs):
+        size = back.shape[0]
+        some = slice(i * size, (i + 1) * size)
+        speech_held[some, :] = project(audio[some, :], home[some, :] + back[...])
+        copy = pltpu.make_async_copy(
+            speech_held.at[some, :], speech_grad.at[some, :], done.at[i + 1]
+        )
+        copy.start()
+        copies.append(copy)
+    for copy in copies:
+        copy.wait()
 
 
 def shards(audio_vectors, sentence_vectors, matching_indices, sharpness_array, offset_term):
@@ -249,7 +285,7 @@
     column = groups * own_text
     text, speech = call(
         functools.partial(join_both_body, groups),
-        [bf16(column, width), bf16(chips * (rows + MARK_ROWS), width)],
+        [bf16(column, width), bf16(chips * rows + mark_rows_of(chips, rows), width)],
         [*text_blocks, speech_own, *speech_blocks[::-1]],
         (scalars,),
         name="join_rows",
@@ -259,18 +295,16 @@
 
     temporary = 4 * column * (6 * CHUNK + 3 * width)
 
-    def text_part(outs, blocks, start, ks=range(groups)):
-        count = sum(v.shape[0] for v in blocks) // (rows + MARK_ROWS)
-        body = functools.partial(text_part_body, rows, own_text, list(ks), bool(start), len(blocks))
-        operands = [scalars, text, *start, *blocks]
-        work = 4 * len(ks) * own_text * count * rows * width
-        return call(body, outs, operands, (), work, temporary, "text_part")
-
-    half = text_part([f32(column, width)], [speech], [])
+    def text_part(outs, speech, start):
+        body = functools.partial(text_part_body, rows, own_text, bool(start), chips)
+        work = 4 * column * chips * rows * width
+        return call(body, outs, [scalars, text, speech, *start], (), work, temporary, "text_part")
+
+    half = text_part([f32(column, width)], speech, [])
     sides = 2
     side = f32(own_text, width // sides)
     outs = [f32(own_text, width)] * (groups // 2) + [side] * (groups // 2 * sides)
-    parts = list(text_part(outs, [other], half))
+    parts = list(text_part(outs, other, half))
     far = [parts[groups // 2 + i * sides :][:sides] for i in range(groups // 2)]
 
     text_far = []
@@ -293,19 +327,25 @@
     from_far = [exchanged(v, "group", groups // 2) for v in far[0]]
     from_near = [exchanged(parts[k], "group", k) for k in range(1, groups // 2)]
 
-    def speech_part(block, start, columns, texts, after=()):
-        body = functools.partial(speech_part_body, rows, own_text, bool(start), columns)
-        operands = [scalars, block, *start, *texts]
+    def speech_part(speech, start, columns, texts, after=(), pieces=1):
+        body = functools.partial(
+            speech_part_body, rows, own_text, bool(start), chips, columns, pieces
+        )
         work = 40 * rows * column * len(columns) * width
-        return call(body, f32(rows, width), operands, after, work, temporary, "speech_part")
+        outs = [f32(rows // pieces, width)] * pieces
+        operands = [scalars, speech, *start, *texts]
+        return call(body, outs, operands, after, work, temporary, "speech_part")
 
     near = [[0, *masks], [text, *text_near], tuple(far[0])]
-    away = speech_part(other[0 : rows + MARK_ROWS], [], *near)
-    home = speech_part(speech_own, [], *near)
     if square:
-        away = speech_part(other[0 : rows + MARK_ROWS], [away], [3], text_far)
-        home = speech_part(speech_own, [home], [3], text_far)
-    back = exchanged(away, "member", 1)
+        away = speech_part(other, [], *near)
+        home = speech_part(speech, [], *near)
+        away = speech_part(other, away, [3], text_far, pieces=2)
+        home = speech_part(speech, home, [3], text_far)
+    else:
+        away = speech_part(other, [], *near, pieces=2)
+        home = speech_part(speech, [], *near)
+    back = [exchanged(piece, "member", 1) for piece in away]
     text_back = call(
         add_sides_body,
         f32(own_text, width),
@@ -314,12 +354,19 @@
         EARLY,
         name="text_sum",
     )
-    speech_grad, text_grad = call(
-        finish_body,
-        [f32(rows, width), f32(own_text, width)],
-        [audio, home, back, sentence, text_back],
+    results = [f32(rows, width), f32(own_text, width)]
+    speech_grad, text_grad = pl.pallas_call(
+        functools.partial(finish_body, len(back)),
+        out_shape=results,
+        in_specs=[pl.BlockSpec(memory_space=pltpu.VMEM)] * (4 + len(back)),
+        out_specs=[pl.BlockSpec(memory_space=pltpu.HBM)] * 2,
+        scratch_shapes=[
+            *[pltpu.VMEM(v.shape, v.dtype) for v in results],
+            pltpu.SemaphoreType.DMA((1 + len(back),)),
+        ],
+        compiler_params=pltpu.CompilerParams(vmem_limit_bytes=8 << 20),
         name="finish",
-    )
+    )(audio, *home, *back, sentence, text_back)
     return (speech_grad, text_grad)
 
 

time: 42.1 us -> 41.9 us (level)
  waiting for transfers between devices: 13.8 us -> 12.9 us
  starting transfers between devices: 18.9 us -> 19.7 us
    pallas_call x0 -> x1, Pallas kernels: none -> 1.07 us  [shards(): pl.pallas_call(functools.partial(finish_body, len(back)), out_shape=resul...]
    pallas_call x13 -> x12, Pallas kernels: 5.85 us -> 4.79 us  [call(): pl.pallas_call(whole, out_shape=out_shape, in_specs=specs, out_specs=jax....]
    ppermute x17 -> x18, waiting for transfers between devices: 13.8 us -> 12.9 us  [exchanged(): return lax.ppermute(value, axis, [(i, i ^ mask) for i in range(size)])]
    ppermute x17 -> x18, starting transfers between devices: 18.9 us -> 19.7 us  [exchanged(): return lax.ppermute(value, axis, [(i, i ^ mask) for i in range(size)])]
  transfers between devices with their start and end apart: 17 -> 18, of which waited for: 10 -> 11; matrix products, arithmetic and copies ran while one was open for 0% -> 0% of each run, Pallas kernels for 11% -> 11%
where the time goes in v15:
time: 41.9 us; the launch traced here: 41.8 us
  starting transfers between devices  19.7 us (47%)
  waiting for transfers between devices  12.9 us (31%)
  Pallas kernels  7.03 us (17%)
  between operations  2.05 us (5%)
    ppermute x18, starting transfers between devices, exchanged(): return lax.ppermute(value, axis, [(i, i ^ mask) for i in range(size)])  19.7 us
    ppermute x18, waiting for transfers between devices, exchanged(): return lax.ppermute(value, axis, [(i, i ^ mask) for i in range(size)])  12.9 us
    pallas_call x12, Pallas kernels, call(): pl.pallas_call(whole, out_shape=out_shape, in_specs=specs, out_specs=jax....  4.79 us
    pallas_call x1, Pallas kernels, shards(): pl.pallas_call(prepare_body, out_shape=[bf16(rows + MARK_ROWS, width), bf...  1.18 us
    pallas_call x1, Pallas kernels, shards(): pl.pallas_call(functools.partial(finish_body, len(back)), out_shape=resul...  1.07 us
  transfers between devices with their start and end apart: 18, of which 11 were waited for; matrix products, arithmetic and copies ran while one was open for 0% of the time, Pallas kernels for 11%

profile of v15, /device:TPU:0, one launch (start us, length us, event | category | flops | bytes accessed | tf_op | source)
XLA Modules:
  0.0 41.8 jit_solution(12345060587321316836)
XLA Ops:
  0.6 1.2 %unit_rows.1 = (bf16[136,768]{1,0:T(8,128)(2,1)S(1)}, bf16[64,768]{1,0:T(8,128)(2,1)S(1)}, bf16[128,768]{1,0:T(8,128)(2,1)S(1)}, bf16[64,768]{1,0:T(8,128)(2,1)S(1)}) custom-call(bf16[128,768]{1,0:T(8,128)(2,1)} %refs_0_.1, bf16[64,768]{1,0:T(8,128)(2,1)} %refs_1_.1, s32[1,128]{1,0:T(1,128)} %bitcast.3), custom_call_target="tpu_custom_call" | custom-call | tf_op jit(solution)/shard_map/unit_rows/pallas_call | solution.py:251
  1.8 4.1 %collective-permute-start.1 = (bf16[64,768]{1,0:T(8,128)(2,1)S(1)}, bf16[64,768]{1,0:T(8,128)(2,1)S(1)}, u32[]{:S(2)}, u32[]{:S(2)}) collective-permute-start(bf16[64,768]{1,0:T(8,128)(2,1)S(1)} %get-tuple-element.19.refs_0_), channel_id=1, source_target_pairs={{0,16},{8,24},{16,0},{24,8},{1,17},{9,25},{17,1},{25,9},{2,18},{10... | collective-permute-start | bytes 294920 | tf_op jit(solution)/shard_map/ppermute | solution.py:18
  5.9 2.4 %collective-permute-start.5 = (bf16[136,768]{1,0:T(8,128)(2,1)S(1)}, bf16[136,768]{1,0:T(8,128)(2,1)S(1)}, u32[]{:S(2)}, u32[]{:S(2)}) collective-permute-start(bf16[136,768]{1,0:T(8,128)(2,1)S(1)} %get-tuple-element.20.refs_4_), channel_id=1, source_target_pairs={{0,6},{1,7},{2,4},{3,5},{4,2},{5,3},{6,0},{7,1},{8,14},{9,15},{10,... | collective-permute-start | bytes 626696 | tf_op jit(solution)/shard_map/ppermute | solution.py:18
  8.4 0.5 %collective-permute-start.4 = (bf16[136,768]{1,0:T(8,128)(2,1)S(1)}, bf16[136,768]{1,0:T(8,128)(2,1)S(1)}, u32[]{:S(2)}, u32[]{:S(2)}) collective-permute-start(bf16[136,768]{1,0:T(8,128)(2,1)S(1)} %get-tuple-element.20.refs_4_), channel_id=1, source_target_pairs={{0,4},{1,5},{2,6},{3,7},{4,0},{5,1},{6,2},{7,3},{8,12},{9,13},{10,... | collective-permute-start | bytes 626696 | tf_op jit(solution)/shard_map/ppermute | solution.py:18
  8.9 0.5 %collective-permute-start.3 = (bf16[136,768]{1,0:T(8,128)(2,1)S(1)}, bf16[136,768]{1,0:T(8,128)(2,1)S(1)}, u32[]{:S(2)}, u32[]{:S(2)}) collective-permute-start(bf16[136,768]{1,0:T(8,128)(2,1)S(1)} %get-tuple-element.20.refs_4_), channel_id=1, source_target_pairs={{0,2},{1,3},{2,0},{3,1},{4,6},{5,7},{6,4},{7,5},{8,10},{9,11},{10,... | collective-permute-start | bytes 626696 | tf_op jit(solution)/shard_map/ppermute | solution.py:18
  9.4 1.6 %collective-permute-start = (bf16[64,768]{1,0:T(8,128)(2,1)S(1)}, bf16[64,768]{1,0:T(8,128)(2,1)S(1)}, u32[]{:S(2)}, u32[]{:S(2)}) collective-permute-start(bf16[64,768]{1,0:T(8,128)(2,1)S(1)} %get-tuple-element.19.refs_0_), channel_id=1, source_target_pairs={{0,8},{8,0},{16,24},{24,16},{1,9},{9,1},{17,25},{25,17},{2,10},{10... | collective-permute-start | bytes 294920 | tf_op jit(solution)/shard_map/ppermute | solution.py:18
  11.0 0.6 %collective-permute-start.2 = (bf16[64,768]{1,0:T(8,128)(2,1)S(1)}, bf16[64,768]{1,0:T(8,128)(2,1)S(1)}, u32[]{:S(2)}, u32[]{:S(2)}) collective-permute-start(bf16[64,768]{1,0:T(8,128)(2,1)S(1)} %pass_on.1.refs_2_), channel_id=1, source_target_pairs={{0,8},{8,0},{16,24},{24,16},{1,9},{9,1},{17,25},{25,17},{2,10},{10... | collective-permute-start | bytes 294920 | tf_op jit(solution)/shard_map/ppermute | solution.py:18
  12.9 1.9 %collective-permute-done.refs_1_ = bf16[64,768]{1,0:T(8,128)(2,1)S(1)} collective-permute-done((bf16[64,768]{1,0:T(8,128)(2,1)S(1)}, bf16[64,768]{1,0:T(8,128)(2,1)S(1)}, u32[]{:S(2)}, u32[]{:S(2)}) %collective-permute-start) | collective-permute-done | bytes 98336 | tf_op jit(solution)/shard_map/ppermute | solution.py:18
  14.9 1.1 %collective-permute-done.2.refs_3_ = bf16[64,768]{1,0:T(8,128)(2,1)S(1)} collective-permute-done((bf16[64,768]{1,0:T(8,128)(2,1)S(1)}, bf16[64,768]{1,0:T(8,128)(2,1)S(1)}, u32[]{:S(2)}, u32[]{:S(2)}) %collective-permute-start.2) | collective-permute-done | bytes 98336 | tf_op jit(solution)/shard_map/ppermute | solution.py:18
  15.9 2.0 %collective-permute-done.4.refs_6_ = bf16[136,768]{1,0:T(8,128)(2,1)S(1)} collective-permute-done((bf16[136,768]{1,0:T(8,128)(2,1)S(1)}, bf16[136,768]{1,0:T(8,128)(2,1)S(1)}, u32[]{:S(2)}, u32[]{:S(2)}) %collective-permute-start.4) | collective-permute-done | bytes 208928 | tf_op jit(solution)/shard_map/ppermute | solution.py:18
  18.3 1.5 %collective-permute-start.7 = (bf16[256,768]{1,0:T(8,128)(2,1)S(1)}, bf16[256,768]{1,0:T(8,128)(2,1)S(1)}, u32[]{:S(2)}, u32[]{:S(2)}) collective-permute-start(bf16[256,768]{1,0:T(8,128)(2,1)S(1)} %get-tuple-element.22.refs_1_.refs_2_), channel_id=1, source_target_pairs={{0,4},{1,5},{2,6},{3,7},{4,0},{5,1},{6,2},{7,3},{8,12},{9,13},{10,... | collective-permute-start | bytes 1179656 | tf_op jit(solution)/shard_map/ppermute | solution.py:18
  19.7 0.8 %collective-permute-start.6 = (bf16[256,768]{1,0:T(8,128)(2,1)S(1)}, bf16[256,768]{1,0:T(8,128)(2,1)S(1)}, u32[]{:S(2)}, u32[]{:S(2)}) collective-permute-start(bf16[256,768]{1,0:T(8,128)(2,1)S(1)} %get-tuple-element.22.refs_1_.refs_2_), channel_id=1, source_target_pairs={{0,2},{1,3},{2,0},{3,1},{4,6},{5,7},{6,4},{7,5},{8,10},{9,11},{10,... | collective-permute-start | bytes 1179656 | tf_op jit(solution)/shard_map/ppermute | solution.py:18
  20.5 0.8 %text_part.2.refs_3_ = f32[256,768]{1,0:T(8,128)S(1)} custom-call(f32[2,128]{1,0:T(2,128)S(1)} %concatenate.6.refs_8_.refs_0_, bf16[256,768]{1,0:T(8,128)(2,1)S(1)} %get-tuple-element.22.refs_1_.refs_2_, bf16[528,768]{1,0:T(8,128)(2,1)S(1)} %get-tuple-element.21.refs_2_.refs_1_), custom_call_target="tpu_custom_call" | custom-call | flops 402653184 | bytes 1991680 | tf_op jit(solution)/shard_map/text_part/pallas_call | solution.py:34
  21.3 0.8 %text_part.3 = (f32[64,768]{1,0:T(8,128)S(1)}, f32[64,768]{1,0:T(8,128)S(1)}, f32[64,384]{1,0:T(8,128)S(1)}, f32[64,384]{1,0:T(8,128)S(1)}, f32[64,384]{1,0:T(8,128)S(1)}, /*index=5*/f32[64,384]{1,0:T(8,128)S(1)}) custom-call(f32[2,128]{1,0:T(2,128)S(1)} %concatenate.6.refs_8_.refs_0_, bf16[256,768]{1,0:T(8,128)(2,1)S(1)} %get-tuple-element.22.refs_1_.refs_2_, ...), custom_call_target="tpu_custom_call" | custom-call | flops 402653184 | bytes 2778112 | tf_op jit(solution)/shard_map/text_part/pallas_call | solution.py:34
  22.1 1.6 %collective-permute-start.9 = (f32[64,384]{1,0:T(8,128)S(1)}, f32[64,384]{1,0:T(8,128)S(1)}, u32[]{:S(2)}, u32[]{:S(2)}) collective-permute-start(f32[64,384]{1,0:T(8,128)S(1)} %get-tuple-element.24), channel_id=1, source_target_pairs={{0,8},{8,0},{16,24},{24,16},{1,9},{9,1},{17,25},{25,17},{2,10},{10... | collective-permute-start | bytes 294920 | tf_op jit(solution)/shard_map/ppermute | solution.py:18
  23.7 0.4 %collective-permute-start.10 = (f32[64,384]{1,0:T(8,128)S(1)}, f32[64,384]{1,0:T(8,128)S(1)}, u32[]{:S(2)}, u32[]{:S(2)}) collective-permute-start(f32[64,384]{1,0:T(8,128)S(1)} %get-tuple-element.26), channel_id=1, source_target_pairs={{0,8},{8,0},{16,24},{24,16},{1,9},{9,1},{17,25},{25,17},{2,10},{10... | collective-permute-start | bytes 294920 | tf_op jit(solution)/shard_map/ppermute | solution.py:18
  24.2 1.6 %collective-permute-start.17 = (f32[64,768]{1,0:T(8,128)S(1)}, f32[64,768]{1,0:T(8,128)S(1)}, u32[]{:S(2)}, u32[]{:S(2)}) collective-permute-start(f32[64,768]{1,0:T(8,128)S(1)} %get-tuple-element.32), channel_id=1, source_target_pairs={{0,8},{8,0},{16,24},{24,16},{1,9},{9,1},{17,25},{25,17},{2,10},{10... | collective-permute-start | bytes 589832 | tf_op jit(solution)/shard_map/ppermute | solution.py:18
  25.8 1.8 %collective-permute-done.9.refs_1_ = f32[64,384]{1,0:T(8,128)S(1)} collective-permute-done((f32[64,384]{1,0:T(8,128)S(1)}, f32[64,384]{1,0:T(8,128)S(1)}, u32[]{:S(2)}, u32[]{:S(2)}) %collective-permute-start.9) | collective-permute-done | bytes 98336 | tf_op jit(solution)/shard_map/ppermute | solution.py:18
  27.6 0.8 %collective-permute-start.15 = (f32[64,384]{1,0:T(8,128)S(1)}, f32[64,384]{1,0:T(8,128)S(1)}, u32[]{:S(2)}, u32[]{:S(2)}) collective-permute-start(f32[64,384]{1,0:T(8,128)S(1)} %sum_near.2.refs_2_.refs_5_), channel_id=1, source_target_pairs={{0,16},{8,24},{16,0},{24,8},{1,17},{9,25},{17,1},{25,9},{2,18},{10... | collective-permute-start | bytes 294920 | tf_op jit(solution)/shard_map/ppermute | solution.py:18
  28.4 1.4 %collective-permute-done.7.refs_0_.refs_4_ = bf16[256,768]{1,0:T(8,128)(2,1)S(1)} collective-permute-done((bf16[256,768]{1,0:T(8,128)(2,1)S(1)}, bf16[256,768]{1,0:T(8,128)(2,1)S(1)}, u32[]{:S(2)}, u32[]{:S(2)}) %collective-permute-start.7) | collective-permute-done | bytes 393248 | tf_op jit(solution)/shard_map/ppermute | solution.py:18
  29.8 1.1 %collective-permute-done.6.refs_1_.refs_3_ = bf16[256,768]{1,0:T(8,128)(2,1)S(1)} collective-permute-done((bf16[256,768]{1,0:T(8,128)(2,1)S(1)}, bf16[256,768]{1,0:T(8,128)(2,1)S(1)}, u32[]{:S(2)}, u32[]{:S(2)}) %collective-permute-start.6) | collective-permute-done | bytes 393248 | tf_op jit(solution)/shard_map/ppermute | solution.py:18
  31.0 0.9 %collective-permute-start.11 = (bf16[128,768]{1,0:T(8,128)(2,1)S(1)}, bf16[128,768]{1,0:T(8,128)(2,1)S(1)}, u32[]{:S(2)}, u32[]{:S(2)}) collective-permute-start(bf16[128,768]{1,0:T(8,128)(2,1)S(1)} %get-tuple-element.27.refs_2_), channel_id=1, source_target_pairs={{0,2},{1,3},{2,0},{3,1},{4,6},{5,7},{6,4},{7,5},{8,10},{9,11},{10,... | collective-permute-start | bytes 589832 | tf_op jit(solution)/shard_map/ppermute | solution.py:18
  31.8 0.9 %collective-permute-start.16 = (f32[64,384]{1,0:T(8,128)S(1)}, f32[64,384]{1,0:T(8,128)S(1)}, u32[]{:S(2)}, u32[]{:S(2)}) collective-permute-start(f32[64,384]{1,0:T(8,128)S(1)} %sum_near.3.refs_6_), channel_id=1, source_target_pairs={{0,16},{8,24},{16,0},{24,8},{1,17},{9,25},{17,1},{25,9},{2,18},{10... | collective-permute-start | bytes 294920 | tf_op jit(solution)/shard_map/ppermute | solution.py:18
  32.7 0.9 %collective-permute-start.12 = (bf16[128,768]{1,0:T(8,128)(2,1)S(1)}, bf16[128,768]{1,0:T(8,128)(2,1)S(1)}, u32[]{:S(2)}, u32[]{:S(2)}) collective-permute-start(bf16[128,768]{1,0:T(8,128)(2,1)S(1)} %get-tuple-element.28), channel_id=1, source_target_pairs={{0,4},{1,5},{2,6},{3,7},{4,0},{5,1},{6,2},{7,3},{8,12},{9,13},{10,... | collective-permute-start | bytes 589832 | tf_op jit(solution)/shard_map/ppermute | solution.py:18
  33.6 1.0 %speech_part.6.refs_2_ = f32[128,768]{1,0:T(8,128)S(1)} custom-call(f32[2,128]{1,0:T(2,128)S(1)} %concatenate.6.refs_8_.refs_0_, bf16[528,768]{1,0:T(8,128)(2,1)S(1)} %collective-permute-done.8.refs_2_.refs_1_, bf16[256,768]{1,0:T(8,128)(2,1)S(1)} %get-tuple-element.22.refs_1_.refs_2_, bf16[256,768]{1,0:T(8,128)(2,1)S(1)} %collective-permute-done.6.refs_1_.refs_3_, ...), custom_call_target="tpu_custom_call" | custom-call | flops 3019898880 | bytes 2384896 | tf_op jit(solution)/shard_map/speech_part/pallas_call | solution.py:34
  34.6 1.0 %speech_part.4.refs_2_ = f32[128,768]{1,0:T(8,128)S(1)} custom-call(f32[2,128]{1,0:T(2,128)S(1)} %concatenate.6.refs_8_.refs_0_, bf16[528,768]{1,0:T(8,128)(2,1)S(1)} %get-tuple-element.21.refs_2_.refs_1_, bf16[256,768]{1,0:T(8,128)(2,1)S(1)} %get-tuple-element.22.refs_1_.refs_2_, bf16[256,768]{1,0:T(8,128)(2,1)S(1)} %collective-permute-done.6.refs_1_.refs_3_, ...), custom_call_target="tpu_custom_call" | custom-call | flops 3019898880 | bytes 2384896 | tf_op jit(solution)/shard_map/speech_part/pallas_call | solution.py:34
  35.6 2.8 %collective-permute-done.12.refs_4_ = bf16[128,768]{1,0:T(8,128)(2,1)S(1)} collective-permute-done((bf16[128,768]{1,0:T(8,128)(2,1)S(1)}, bf16[128,768]{1,0:T(8,128)(2,1)S(1)}, u32[]{:S(2)}, u32[]{:S(2)}) %collective-permute-start.12) | collective-permute-done | bytes 196640 | tf_op jit(solution)/shard_map/ppermute | solution.py:18
  38.4 0.5 %speech_part.7 = (f32[64,768]{1,0:T(8,128)S(1)}, f32[64,768]{1,0:T(8,128)S(1)}) custom-call(f32[2,128]{1,0:T(2,128)S(1)} %concatenate.6.refs_8_.refs_0_, bf16[528,768]{1,0:T(8,128)(2,1)S(1)} %collective-permute-done.8.refs_2_.refs_1_, f32[128,768]{1,0:T(8,128)S(1)} %speech_part.6.refs_2_, bf16[128,768]{1,0:T(8,128)(2,1)S(1)} %collective-permute-done.11.refs_3_, ...), custom_call_target="tpu_custom_call" | custom-call | flops 1006632960 | bytes 1991680 | tf_op jit(solution)/shard_map/speech_part/pallas_call | solution.py:34
  39.0 0.5 %collective-permute-start.14 = (f32[64,768]{1,0:T(8,128)S(1)}, f32[64,768]{1,0:T(8,128)S(1)}, u32[]{:S(2)}, u32[]{:S(2)}) collective-permute-start(f32[64,768]{1,0:T(8,128)S(1)} %get-tuple-element.30), channel_id=1, source_target_pairs={{0,1},{1,0},{2,3},{3,2},{4,5},{5,4},{6,7},{7,6},{8,9},{9,8},{10,11... | collective-permute-start | bytes 589832 | tf_op jit(solution)/shard_map/ppermute | solution.py:18
  39.7 0.5 %speech_part.5.home = f32[128,768]{1,0:T(8,128)S(1)} custom-call(f32[2,128]{1,0:T(2,128)S(1)} %concatenate.6.refs_8_.refs_0_, bf16[528,768]{1,0:T(8,128)(2,1)S(1)} %get-tuple-element.21.refs_2_.refs_1_, f32[128,768]{1,0:T(8,128)S(1)} %speech_part.4.refs_2_, bf16[128,768]{1,0:T(8,128)(2,1)S(1)} %collective-permute-done.11.refs_3_, ...), custom_call_target="tpu_custom_call" | custom-call | flops 1006632960 | bytes 1991680 | tf_op jit(solution)/shard_map/speech_part/pallas_call | solution.py:34
  40.4 0.3 collective-permute-done.14.refs_1_
  40.7 1.1 %finish.1 = (f32[128,768]{1,0:T(8,128)}, f32[64,768]{1,0:T(8,128)}) custom-call(bf16[128,768]{1,0:T(8,128)(2,1)S(1)} %get-tuple-element.18.audio, f32[128,768]{1,0:T(8,128)S(1)} %speech_part.5.home, f32[64,768]{1,0:T(8,128)S(1)} %collective-permute-done.13.refs_0_, f32[64,768]{1,0:T(8,128)S(1)} %collective-permute-done.14.refs_1_, ...), custom_call_target="tpu_custom_call" | custom-call | tf_op jit(solution)/shard_map/finish/pallas_call | solution.py:358
  (20 shorter events, 0.9 us)
Async XLA Ops:
  1.8 9.2 %collective-permute-start.1 = (bf16[64,768]{1,0:T(8,128)(2,1)S(1)}, bf16[64,768]{1,0:T(8,128)(2,1)S(1)}, u32[]{:S(2)}, u32[]{:S(2)}) collective-permute-start(bf16[64,768]{1,0:T(8,128)(2,1)S(1)} %get-tuple-element.19.refs_0_), channel_id=1, source_target_pairs={{0,16},{8,24},{16,0},{24,8},{1,17},{9,25},{17,1},{25,9},{2,18},{10... | collective-permute-start | bytes 294920 | tf_op jit(solution)/shard_map/ppermute | solution.py:18
  5.9 10.0 %collective-permute-start.5 = (bf16[136,768]{1,0:T(8,128)(2,1)S(1)}, bf16[136,768]{1,0:T(8,128)(2,1)S(1)}, u32[]{:S(2)}, u32[]{:S(2)}) collective-permute-start(bf16[136,768]{1,0:T(8,128)(2,1)S(1)} %get-tuple-element.20.refs_4_), channel_id=1, source_target_pairs={{0,6},{1,7},{2,4},{3,5},{4,2},{5,3},{6,0},{7,1},{8,14},{9,15},{10,... | collective-permute-start | bytes 626696 | tf_op jit(solution)/shard_map/ppermute | solution.py:18
  8.4 9.6 %collective-permute-start.4 = (bf16[136,768]{1,0:T(8,128)(2,1)S(1)}, bf16[136,768]{1,0:T(8,128)(2,1)S(1)}, u32[]{:S(2)}, u32[]{:S(2)}) collective-permute-start(bf16[136,768]{1,0:T(8,128)(2,1)S(1)} %get-tuple-element.20.refs_4_), channel_id=1, source_target_pairs={{0,4},{1,5},{2,6},{3,7},{4,0},{5,1},{6,2},{7,3},{8,12},{9,13},{10,... | collective-permute-start | bytes 626696 | tf_op jit(solution)/shard_map/ppermute | solution.py:18
  8.9 9.1 %collective-permute-start.3 = (bf16[136,768]{1,0:T(8,128)(2,1)S(1)}, bf16[136,768]{1,0:T(8,128)(2,1)S(1)}, u32[]{:S(2)}, u32[]{:S(2)}) collective-permute-start(bf16[136,768]{1,0:T(8,128)(2,1)S(1)} %get-tuple-element.20.refs_4_), channel_id=1, source_target_pairs={{0,2},{1,3},{2,0},{3,1},{4,6},{5,7},{6,4},{7,5},{8,10},{9,11},{10,... | collective-permute-start | bytes 626696 | tf_op jit(solution)/shard_map/ppermute | solution.py:18
  9.4 5.5 %collective-permute-start = (bf16[64,768]{1,0:T(8,128)(2,1)S(1)}, bf16[64,768]{1,0:T(8,128)(2,1)S(1)}, u32[]{:S(2)}, u32[]{:S(2)}) collective-permute-start(bf16[64,768]{1,0:T(8,128)(2,1)S(1)} %get-tuple-element.19.refs_0_), channel_id=1, source_target_pairs={{0,8},{8,0},{16,24},{24,16},{1,9},{9,1},{17,25},{25,17},{2,10},{10... | collective-permute-start | bytes 294920 | tf_op jit(solution)/shard_map/ppermute | solution.py:18
  11.0 4.9 %collective-permute-start.2 = (bf16[64,768]{1,0:T(8,128)(2,1)S(1)}, bf16[64,768]{1,0:T(8,128)(2,1)S(1)}, u32[]{:S(2)}, u32[]{:S(2)}) collective-permute-start(bf16[64,768]{1,0:T(8,128)(2,1)S(1)} %pass_on.1.refs_2_), channel_id=1, source_target_pairs={{0,8},{8,0},{16,24},{24,16},{1,9},{9,1},{17,25},{25,17},{2,10},{10... | collective-permute-start | bytes 294920 | tf_op jit(solution)/shard_map/ppermute | solution.py:18
  18.2 3.1 %collective-permute-start.8 = (bf16[528,768]{1,0:T(8,128)(2,1)S(1)}, bf16[528,768]{1,0:T(8,128)(2,1)S(1)}, u32[]{:S(2)}, u32[]{:S(2)}) collective-permute-start(bf16[528,768]{1,0:T(8,128)(2,1)S(1)} %get-tuple-element.21.refs_2_.refs_1_), channel_id=1, source_target_pairs={{0,1},{1,0},{2,3},{3,2},{4,5},{5,4},{6,7},{7,6},{8,9},{9,8},{10,11... | collective-permute-start | bytes 2433032 | tf_op jit(solution)/shard_map/ppermute | solution.py:18
  18.3 11.5 %collective-permute-start.7 = (bf16[256,768]{1,0:T(8,128)(2,1)S(1)}, bf16[256,768]{1,0:T(8,128)(2,1)S(1)}, u32[]{:S(2)}, u32[]{:S(2)}) collective-permute-start(bf16[256,768]{1,0:T(8,128)(2,1)S(1)} %get-tuple-element.22.refs_1_.refs_2_), channel_id=1, source_target_pairs={{0,4},{1,5},{2,6},{3,7},{4,0},{5,1},{6,2},{7,3},{8,12},{9,13},{10,... | collective-permute-start | bytes 1179656 | tf_op jit(solution)/shard_map/ppermute | solution.py:18
  19.7 11.2 %collective-permute-start.6 = (bf16[256,768]{1,0:T(8,128)(2,1)S(1)}, bf16[256,768]{1,0:T(8,128)(2,1)S(1)}, u32[]{:S(2)}, u32[]{:S(2)}) collective-permute-start(bf16[256,768]{1,0:T(8,128)(2,1)S(1)} %get-tuple-element.22.refs_1_.refs_2_), channel_id=1, source_target_pairs={{0,2},{1,3},{2,0},{3,1},{4,6},{5,7},{6,4},{7,5},{8,10},{9,11},{10,... | collective-permute-start | bytes 1179656 | tf_op jit(solution)/shard_map/ppermute | solution.py:18
  22.1 5.5 %collective-permute-start.9 = (f32[64,384]{1,0:T(8,128)S(1)}, f32[64,384]{1,0:T(8,128)S(1)}, u32[]{:S(2)}, u32[]{:S(2)}) collective-permute-start(f32[64,384]{1,0:T(8,128)S(1)} %get-tuple-element.24), channel_id=1, source_target_pairs={{0,8},{8,0},{16,24},{24,16},{1,9},{9,1},{17,25},{25,17},{2,10},{10... | collective-permute-start | bytes 294920 | tf_op jit(solution)/shard_map/ppermute | solution.py:18
  23.7 8.1 %collective-permute-start.10 = (f32[64,384]{1,0:T(8,128)S(1)}, f32[64,384]{1,0:T(8,128)S(1)}, u32[]{:S(2)}, u32[]{:S(2)}) collective-permute-start(f32[64,384]{1,0:T(8,128)S(1)} %get-tuple-element.26), channel_id=1, source_target_pairs={{0,8},{8,0},{16,24},{24,16},{1,9},{9,1},{17,25},{25,17},{2,10},{10... | collective-permute-start | bytes 294920 | tf_op jit(solution)/shard_map/ppermute | solution.py:18
  24.2 15.3 %collective-permute-start.17 = (f32[64,768]{1,0:T(8,128)S(1)}, f32[64,768]{1,0:T(8,128)S(1)}, u32[]{:S(2)}, u32[]{:S(2)}) collective-permute-start(f32[64,768]{1,0:T(8,128)S(1)} %get-tuple-element.32), channel_id=1, source_target_pairs={{0,8},{8,0},{16,24},{24,16},{1,9},{9,1},{17,25},{25,17},{2,10},{10... | collective-permute-start | bytes 589832 | tf_op jit(solution)/shard_map/ppermute | solution.py:18
  27.6 11.8 %collective-permute-start.15 = (f32[64,384]{1,0:T(8,128)S(1)}, f32[64,384]{1,0:T(8,128)S(1)}, u32[]{:S(2)}, u32[]{:S(2)}) collective-permute-start(f32[64,384]{1,0:T(8,128)S(1)} %sum_near.2.refs_2_.refs_5_), channel_id=1, source_target_pairs={{0,16},{8,24},{16,0},{24,8},{1,17},{9,25},{17,1},{25,9},{2,18},{10... | collective-permute-start | bytes 294920 | tf_op jit(solution)/shard_map/ppermute | solution.py:18
  31.0 7.4 %collective-permute-start.11 = (bf16[128,768]{1,0:T(8,128)(2,1)S(1)}, bf16[128,768]{1,0:T(8,128)(2,1)S(1)}, u32[]{:S(2)}, u32[]{:S(2)}) collective-permute-start(bf16[128,768]{1,0:T(8,128)(2,1)S(1)} %get-tuple-element.27.refs_2_), channel_id=1, source_target_pairs={{0,2},{1,3},{2,0},{3,1},{4,6},{5,7},{6,4},{7,5},{8,10},{9,11},{10,... | collective-permute-start | bytes 589832 | tf_op jit(solution)/shard_map/ppermute | solution.py:18
  31.8 7.8 %collective-permute-start.16 = (f32[64,384]{1,0:T(8,128)S(1)}, f32[64,384]{1,0:T(8,128)S(1)}, u32[]{:S(2)}, u32[]{:S(2)}) collective-permute-start(f32[64,384]{1,0:T(8,128)S(1)} %sum_near.3.refs_6_), channel_id=1, source_target_pairs={{0,16},{8,24},{16,0},{24,8},{1,17},{9,25},{17,1},{25,9},{2,18},{10... | collective-permute-start | bytes 294920 | tf_op jit(solution)/shard_map/ppermute | solution.py:18
  32.7 5.7 %collective-permute-start.12 = (bf16[128,768]{1,0:T(8,128)(2,1)S(1)}, bf16[128,768]{1,0:T(8,128)(2,1)S(1)}, u32[]{:S(2)}, u32[]{:S(2)}) collective-permute-start(bf16[128,768]{1,0:T(8,128)(2,1)S(1)} %get-tuple-element.28), channel_id=1, source_target_pairs={{0,4},{1,5},{2,6},{3,7},{4,0},{5,1},{6,2},{7,3},{8,12},{9,13},{10,... | collective-permute-start | bytes 589832 | tf_op jit(solution)/shard_map/ppermute | solution.py:18
  38.9 1.5 %collective-permute-start.13 = (f32[64,768]{1,0:T(8,128)S(1)}, f32[64,768]{1,0:T(8,128)S(1)}, u32[]{:S(2)}, u32[]{:S(2)}) collective-permute-start(f32[64,768]{1,0:T(8,128)S(1)} %get-tuple-element.29), channel_id=1, source_target_pairs={{0,1},{1,0},{2,3},{3,2},{4,5},{5,4},{6,7},{7,6},{8,9},{9,8},{10,11... | collective-permute-start | bytes 589832 | tf_op jit(solution)/shard_map/ppermute | solution.py:18
  39.0 1.7 %collective-permute-start.14 = (f32[64,768]{1,0:T(8,128)S(1)}, f32[64,768]{1,0:T(8,128)S(1)}, u32[]{:S(2)}, u32[]{:S(2)}) collective-permute-start(f32[64,768]{1,0:T(8,128)S(1)} %get-tuple-element.30), channel_id=1, source_target_pairs={{0,1},{1,0},{2,3},{3,2},{4,5},{5,4},{6,7},{7,6},{8,9},{9,8},{10,11... | collective-permute-start | bytes 589832 | tf_op jit(solution)/shard_map/ppermute | solution.py:18

commit v16 on v15

--- a/solution.py
+++ b/solution.py
@@ -110,9 +110,8 @@
     speech[len(blocks) * rows :, :] = table.astype(jnp.bfloat16)
 
 
-def halves_body(upper, lower, upper_out, lower_out):
-    upper_out[...] = upper[: upper_out.shape[0], :]
-    lower_out[...] = lower[upper_out.shape[0] :, :]
+def cut_body(first, source, out):
+    out[...] = source[first : first + out.shape[0], :]
 
 
 def marks_of(table, chunk, count):
@@ -275,11 +274,13 @@
     masks = [1, 2] if square else list(range(1, chips))
 
     def far_halves(near, middle, after=()):
-        sizes = [middle, near[0].shape[0] - middle]
-        halves = call(
-            halves_body, [bf16(size, width) for size in sizes], near[::-1], after, name="halves"
-        )
-        return [(half, exchanged(half, "member", 2 * k)) for half, k in zip(halves, masks)]
+        pairs = []
+        for i, (source, k) in enumerate(zip(near[::-1], masks)):
+            half = call(
+                functools.partial(cut_body, i * middle), bf16(middle, width), [source], after, name="cut"
+            )
+            pairs.append((half, exchanged(half, "member", 2 * k)))
+        return pairs
 
     speech_blocks = [exchanged(speech_own, "member", 2 * k) for k in reversed(range(1, chips))]
     column = groups * own_text
@@ -316,7 +317,7 @@
             for mine, v in zip(far[k - bit], came):
                 if sums and square and not text_far:
                     text_far = far_halves(text_near, column // 2, tuple(sums))
-                    gate = (text_far[0][0],)
+                    gate = tuple(half for half, _ in text_far)
                 else:
                     gate = ()
                 sums.append(call(sum_body, side, [mine, v], gate, name="sum_near"))
@@ -350,7 +351,7 @@
         add_sides_body,
         f32(own_text, width),
         [*from_far, *from_near, parts[0]],
-        (),
+        tuple(home),
         EARLY,
         name="text_sum",
     )

time: 41.9 us -> 41.4 us (0.988)
  waiting for transfers between devices: 12.9 us -> 12.1 us
    ppermute x18, waiting for transfers between devices: 12.9 us -> 12.1 us  [exchanged(): return lax.ppermute(value, axis, [(i, i ^ mask) for i in range(size)])]
    pallas_call x12 -> x13, Pallas kernels: 4.79 us -> 4.79 us  [call(): pl.pallas_call(whole, out_shape=out_shape, in_specs=specs, out_specs=jax....]
  transfers between devices with their start and end apart: 18 -> 18, of which waited for: 11 -> 10; matrix products, arithmetic and copies ran while one was open for 0% -> 0% of each run, Pallas kernels for 11% -> 11%
where the time goes in v16:
time: 41.4 us; the launch traced here: 41.3 us
  starting transfers between devices  20 us (48%)
  waiting for transfers between devices  12.1 us (29%)
  Pallas kernels  7.03 us (17%)
  between operations  2.06 us (5%)
    ppermute x18, starting transfers between devices, exchanged(): return lax.ppermute(value, axis, [(i, i ^ mask) for i in range(size)])  20 us
    ppermute x18, waiting for transfers between devices, exchanged(): return lax.ppermute(value, axis, [(i, i ^ mask) for i in range(size)])  12.1 us
    pallas_call x13, Pallas kernels, call(): pl.pallas_call(whole, out_shape=out_shape, in_specs=specs, out_specs=jax....  4.79 us
    pallas_call x1, Pallas kernels, shards(): pl.pallas_call(prepare_body, out_shape=[bf16(rows + MARK_ROWS, width), bf...  1.18 us
    pallas_call x1, Pallas kernels, shards(): pl.pallas_call(functools.partial(finish_body, len(back)), out_shape=resul...  1.07 us
  transfers between devices with their start and end apart: 18, of which 10 were waited for; matrix products, arithmetic and copies ran while one was open for 0% of the time, Pallas kernels for 11%

profile of v16, /device:TPU:0, one launch (start us, length us, event | category | flops | bytes accessed | tf_op | source)
XLA Modules:
  0.0 41.3 jit_solution(11655661983050897418)
XLA Ops:
  0.6 1.2 %unit_rows.1 = (bf16[136,768]{1,0:T(8,128)(2,1)S(1)}, bf16[64,768]{1,0:T(8,128)(2,1)S(1)}, bf16[128,768]{1,0:T(8,128)(2,1)S(1)}, bf16[64,768]{1,0:T(8,128)(2,1)S(1)}) custom-call(bf16[128,768]{1,0:T(8,128)(2,1)} %refs_0_.1, bf16[64,768]{1,0:T(8,128)(2,1)} %refs_1_.1, s32[1,128]{1,0:T(1,128)} %bitcast.3), custom_call_target="tpu_custom_call" | custom-call | tf_op jit(solution)/shard_map/unit_rows/pallas_call | solution.py:250
  1.8 4.1 %collective-permute-start.1 = (bf16[64,768]{1,0:T(8,128)(2,1)S(1)}, bf16[64,768]{1,0:T(8,128)(2,1)S(1)}, u32[]{:S(2)}, u32[]{:S(2)}) collective-permute-start(bf16[64,768]{1,0:T(8,128)(2,1)S(1)} %get-tuple-element.17.refs_0_), channel_id=1, source_target_pairs={{0,16},{8,24},{16,0},{24,8},{1,17},{9,25},{17,1},{25,9},{2,18},{10... | collective-permute-start | bytes 294920 | tf_op jit(solution)/shard_map/ppermute | solution.py:18
  5.9 1.5 %collective-permute-start.3 = (bf16[136,768]{1,0:T(8,128)(2,1)S(1)}, bf16[136,768]{1,0:T(8,128)(2,1)S(1)}, u32[]{:S(2)}, u32[]{:S(2)}) collective-permute-start(bf16[136,768]{1,0:T(8,128)(2,1)S(1)} %get-tuple-element.18.refs_4_), channel_id=1, source_target_pairs={{0,2},{1,3},{2,0},{3,1},{4,6},{5,7},{6,4},{7,5},{8,10},{9,11},{10,... | collective-permute-start | bytes 626696 | tf_op jit(solution)/shard_map/ppermute | solution.py:18
  7.4 1.5 %collective-permute-start.4 = (bf16[136,768]{1,0:T(8,128)(2,1)S(1)}, bf16[136,768]{1,0:T(8,128)(2,1)S(1)}, u32[]{:S(2)}, u32[]{:S(2)}) collective-permute-start(bf16[136,768]{1,0:T(8,128)(2,1)S(1)} %get-tuple-element.18.refs_4_), channel_id=1, source_target_pairs={{0,4},{1,5},{2,6},{3,7},{4,0},{5,1},{6,2},{7,3},{8,12},{9,13},{10,... | collective-permute-start | bytes 626696 | tf_op jit(solution)/shard_map/ppermute | solution.py:18
  8.9 0.5 %collective-permute-start.5 = (bf16[136,768]{1,0:T(8,128)(2,1)S(1)}, bf16[136,768]{1,0:T(8,128)(2,1)S(1)}, u32[]{:S(2)}, u32[]{:S(2)}) collective-permute-start(bf16[136,768]{1,0:T(8,128)(2,1)S(1)} %get-tuple-element.18.refs_4_), channel_id=1, source_target_pairs={{0,6},{1,7},{2,4},{3,5},{4,2},{5,3},{6,0},{7,1},{8,14},{9,15},{10,... | collective-permute-start | bytes 626696 | tf_op jit(solution)/shard_map/ppermute | solution.py:18
  9.4 1.6 %collective-permute-start = (bf16[64,768]{1,0:T(8,128)(2,1)S(1)}, bf16[64,768]{1,0:T(8,128)(2,1)S(1)}, u32[]{:S(2)}, u32[]{:S(2)}) collective-permute-start(bf16[64,768]{1,0:T(8,128)(2,1)S(1)} %get-tuple-element.17.refs_0_), channel_id=1, source_target_pairs={{0,8},{8,0},{16,24},{24,16},{1,9},{9,1},{17,25},{25,17},{2,10},{10... | collective-permute-start | bytes 294920 | tf_op jit(solution)/shard_map/ppermute | solution.py:18
  11.0 0.6 %collective-permute-start.2 = (bf16[64,768]{1,0:T(8,128)(2,1)S(1)}, bf16[64,768]{1,0:T(8,128)(2,1)S(1)}, u32[]{:S(2)}, u32[]{:S(2)}) collective-permute-start(bf16[64,768]{1,0:T(8,128)(2,1)S(1)} %pass_on.1.refs_2_), channel_id=1, source_target_pairs={{0,8},{8,0},{16,24},{24,16},{1,9},{9,1},{17,25},{25,17},{2,10},{10... | collective-permute-start | bytes 294920 | tf_op jit(solution)/shard_map/ppermute | solution.py:18
  12.9 1.9 %collective-permute-done.refs_1_ = bf16[64,768]{1,0:T(8,128)(2,1)S(1)} collective-permute-done((bf16[64,768]{1,0:T(8,128)(2,1)S(1)}, bf16[64,768]{1,0:T(8,128)(2,1)S(1)}, u32[]{:S(2)}, u32[]{:S(2)}) %collective-permute-start) | collective-permute-done | bytes 98336 | tf_op jit(solution)/shard_map/ppermute | solution.py:18
  14.9 1.1 %collective-permute-done.2.refs_3_ = bf16[64,768]{1,0:T(8,128)(2,1)S(1)} collective-permute-done((bf16[64,768]{1,0:T(8,128)(2,1)S(1)}, bf16[64,768]{1,0:T(8,128)(2,1)S(1)}, u32[]{:S(2)}, u32[]{:S(2)}) %collective-permute-start.2) | collective-permute-done | bytes 98336 | tf_op jit(solution)/shard_map/ppermute | solution.py:18
  15.9 2.3 %collective-permute-done.4.refs_6_ = bf16[136,768]{1,0:T(8,128)(2,1)S(1)} collective-permute-done((bf16[136,768]{1,0:T(8,128)(2,1)S(1)}, bf16[136,768]{1,0:T(8,128)(2,1)S(1)}, u32[]{:S(2)}, u32[]{:S(2)}) %collective-permute-start.4) | collective-permute-done | bytes 208928 | tf_op jit(solution)/shard_map/ppermute | solution.py:18
  18.5 1.3 %collective-permute-start.6 = (bf16[256,768]{1,0:T(8,128)(2,1)S(1)}, bf16[256,768]{1,0:T(8,128)(2,1)S(1)}, u32[]{:S(2)}, u32[]{:S(2)}) collective-permute-start(bf16[256,768]{1,0:T(8,128)(2,1)S(1)} %get-tuple-element.20.refs_1_.refs_2_), channel_id=1, source_target_pairs={{0,2},{1,3},{2,0},{3,1},{4,6},{5,7},{6,4},{7,5},{8,10},{9,11},{10,... | collective-permute-start | bytes 1179656 | tf_op jit(solution)/shard_map/ppermute | solution.py:18
  19.8 0.8 %collective-permute-start.7 = (bf16[256,768]{1,0:T(8,128)(2,1)S(1)}, bf16[256,768]{1,0:T(8,128)(2,1)S(1)}, u32[]{:S(2)}, u32[]{:S(2)}) collective-permute-start(bf16[256,768]{1,0:T(8,128)(2,1)S(1)} %get-tuple-element.20.refs_1_.refs_2_), channel_id=1, source_target_pairs={{0,4},{1,5},{2,6},{3,7},{4,0},{5,1},{6,2},{7,3},{8,12},{9,13},{10,... | collective-permute-start | bytes 1179656 | tf_op jit(solution)/shard_map/ppermute | solution.py:18
  20.6 0.8 %text_part.2.refs_3_ = f32[256,768]{1,0:T(8,128)S(1)} custom-call(f32[2,128]{1,0:T(2,128)S(1)} %concatenate.6.refs_8_.refs_0_, bf16[256,768]{1,0:T(8,128)(2,1)S(1)} %get-tuple-element.20.refs_1_.refs_2_, bf16[528,768]{1,0:T(8,128)(2,1)S(1)} %get-tuple-element.19.refs_2_.refs_1_), custom_call_target="tpu_custom_call" | custom-call | flops 402653184 | bytes 1991680 | tf_op jit(solution)/shard_map/text_part/pallas_call | solution.py:34
  21.4 0.8 %text_part.3 = (f32[64,768]{1,0:T(8,128)S(1)}, f32[64,768]{1,0:T(8,128)S(1)}, f32[64,384]{1,0:T(8,128)S(1)}, f32[64,384]{1,0:T(8,128)S(1)}, f32[64,384]{1,0:T(8,128)S(1)}, /*index=5*/f32[64,384]{1,0:T(8,128)S(1)}) custom-call(f32[2,128]{1,0:T(2,128)S(1)} %concatenate.6.refs_8_.refs_0_, bf16[256,768]{1,0:T(8,128)(2,1)S(1)} %get-tuple-element.20.refs_1_.refs_2_, ...), custom_call_target="tpu_custom_call" | custom-call | flops 402653184 | bytes 2778112 | tf_op jit(solution)/shard_map/text_part/pallas_call | solution.py:34
  22.2 1.6 %collective-permute-start.9 = (f32[64,384]{1,0:T(8,128)S(1)}, f32[64,384]{1,0:T(8,128)S(1)}, u32[]{:S(2)}, u32[]{:S(2)}) collective-permute-start(f32[64,384]{1,0:T(8,128)S(1)} %get-tuple-element.22), channel_id=1, source_target_pairs={{0,8},{8,0},{16,24},{24,16},{1,9},{9,1},{17,25},{25,17},{2,10},{10... | collective-permute-start | bytes 294920 | tf_op jit(solution)/shard_map/ppermute | solution.py:18
  23.8 0.4 %collective-permute-start.10 = (f32[64,384]{1,0:T(8,128)S(1)}, f32[64,384]{1,0:T(8,128)S(1)}, u32[]{:S(2)}, u32[]{:S(2)}) collective-permute-start(f32[64,384]{1,0:T(8,128)S(1)} %get-tuple-element.24), channel_id=1, source_target_pairs={{0,8},{8,0},{16,24},{24,16},{1,9},{9,1},{17,25},{25,17},{2,10},{10... | collective-permute-start | bytes 294920 | tf_op jit(solution)/shard_map/ppermute | solution.py:18
  24.3 1.6 %collective-permute-start.17 = (f32[64,768]{1,0:T(8,128)S(1)}, f32[64,768]{1,0:T(8,128)S(1)}, u32[]{:S(2)}, u32[]{:S(2)}) collective-permute-start(f32[64,768]{1,0:T(8,128)S(1)} %get-tuple-element.28), channel_id=1, source_target_pairs={{0,8},{8,0},{16,24},{24,16},{1,9},{9,1},{17,25},{25,17},{2,10},{10... | collective-permute-start | bytes 589832 | tf_op jit(solution)/shard_map/ppermute | solution.py:18
  25.8 1.9 %collective-permute-done.9.refs_1_ = f32[64,384]{1,0:T(8,128)S(1)} collective-permute-done((f32[64,384]{1,0:T(8,128)S(1)}, f32[64,384]{1,0:T(8,128)S(1)}, u32[]{:S(2)}, u32[]{:S(2)}) %collective-permute-start.9) | collective-permute-done | bytes 98336 | tf_op jit(solution)/shard_map/ppermute | solution.py:18
  27.7 0.7 %collective-permute-start.15 = (f32[64,384]{1,0:T(8,128)S(1)}, f32[64,384]{1,0:T(8,128)S(1)}, u32[]{:S(2)}, u32[]{:S(2)}) collective-permute-start(f32[64,384]{1,0:T(8,128)S(1)} %sum_near.2.refs_1_.refs_5_), channel_id=1, source_target_pairs={{0,16},{8,24},{16,0},{24,8},{1,17},{9,25},{17,1},{25,9},{2,18},{10... | collective-permute-start | bytes 294920 | tf_op jit(solution)/shard_map/ppermute | solution.py:18
  28.4 1.6 %collective-permute-done.6.refs_0_.refs_3_ = bf16[256,768]{1,0:T(8,128)(2,1)S(1)} collective-permute-done((bf16[256,768]{1,0:T(8,128)(2,1)S(1)}, bf16[256,768]{1,0:T(8,128)(2,1)S(1)}, u32[]{:S(2)}, u32[]{:S(2)}) %collective-permute-start.6) | collective-permute-done | bytes 393248 | tf_op jit(solution)/shard_map/ppermute | solution.py:18
  30.0 1.6 %collective-permute-start.12 = (bf16[128,768]{1,0:T(8,128)(2,1)S(1)}, bf16[128,768]{1,0:T(8,128)(2,1)S(1)}, u32[]{:S(2)}, u32[]{:S(2)}) collective-permute-start(bf16[128,768]{1,0:T(8,128)(2,1)S(1)} %cut.3.refs_3_), channel_id=1, source_target_pairs={{0,4},{1,5},{2,6},{3,7},{4,0},{5,1},{6,2},{7,3},{8,12},{9,13},{10,... | collective-permute-start | bytes 589832 | tf_op jit(solution)/shard_map/ppermute | solution.py:18
  31.6 0.6 %collective-permute-start.11 = (bf16[128,768]{1,0:T(8,128)(2,1)S(1)}, bf16[128,768]{1,0:T(8,128)(2,1)S(1)}, u32[]{:S(2)}, u32[]{:S(2)}) collective-permute-start(bf16[128,768]{1,0:T(8,128)(2,1)S(1)} %cut.2.refs_2_), channel_id=1, source_target_pairs={{0,2},{1,3},{2,0},{3,1},{4,6},{5,7},{6,4},{7,5},{8,10},{9,11},{10,... | collective-permute-start | bytes 589832 | tf_op jit(solution)/shard_map/ppermute | solution.py:18
  32.3 0.8 %collective-permute-start.16 = (f32[64,384]{1,0:T(8,128)S(1)}, f32[64,384]{1,0:T(8,128)S(1)}, u32[]{:S(2)}, u32[]{:S(2)}) collective-permute-start(f32[64,384]{1,0:T(8,128)S(1)} %sum_near.3.refs_6_), channel_id=1, source_target_pairs={{0,16},{8,24},{16,0},{24,8},{1,17},{9,25},{17,1},{25,9},{2,18},{10... | collective-permute-start | bytes 294920 | tf_op jit(solution)/shard_map/ppermute | solution.py:18
  33.1 1.0 %speech_part.4.refs_2_ = f32[128,768]{1,0:T(8,128)S(1)} custom-call(f32[2,128]{1,0:T(2,128)S(1)} %concatenate.6.refs_8_.refs_0_, bf16[528,768]{1,0:T(8,128)(2,1)S(1)} %get-tuple-element.19.refs_2_.refs_1_, bf16[256,768]{1,0:T(8,128)(2,1)S(1)} %get-tuple-element.20.refs_1_.refs_2_, bf16[256,768]{1,0:T(8,128)(2,1)S(1)} %collective-permute-done.6.refs_0_.refs_3_, ...), custom_call_target="tpu_custom_call" | custom-call | flops 3019898880 | bytes 2384896 | tf_op jit(solution)/shard_map/speech_part/pallas_call | solution.py:34
  34.1 1.0 %speech_part.6.refs_2_ = f32[128,768]{1,0:T(8,128)S(1)} custom-call(f32[2,128]{1,0:T(2,128)S(1)} %concatenate.6.refs_8_.refs_0_, bf16[528,768]{1,0:T(8,128)(2,1)S(1)} %collective-permute-done.8.refs_2_.refs_1_, bf16[256,768]{1,0:T(8,128)(2,1)S(1)} %get-tuple-element.20.refs_1_.refs_2_, bf16[256,768]{1,0:T(8,128)(2,1)S(1)} %collective-permute-done.6.refs_0_.refs_3_, ...), custom_call_target="tpu_custom_call" | custom-call | flops 3019898880 | bytes 2384896 | tf_op jit(solution)/shard_map/speech_part/pallas_call | solution.py:34
  35.1 1.4 %collective-permute-done.12.refs_4_ = bf16[128,768]{1,0:T(8,128)(2,1)S(1)} collective-permute-done((bf16[128,768]{1,0:T(8,128)(2,1)S(1)}, bf16[128,768]{1,0:T(8,128)(2,1)S(1)}, u32[]{:S(2)}, u32[]{:S(2)}) %collective-permute-start.12) | collective-permute-done | bytes 196640 | tf_op jit(solution)/shard_map/ppermute | solution.py:18
  36.6 1.3 %collective-permute-done.11.refs_3_ = bf16[128,768]{1,0:T(8,128)(2,1)S(1)} collective-permute-done((bf16[128,768]{1,0:T(8,128)(2,1)S(1)}, bf16[128,768]{1,0:T(8,128)(2,1)S(1)}, u32[]{:S(2)}, u32[]{:S(2)}) %collective-permute-start.11) | collective-permute-done | bytes 196640 | tf_op jit(solution)/shard_map/ppermute | solution.py:18
  37.9 0.5 %speech_part.7 = (f32[64,768]{1,0:T(8,128)S(1)}, f32[64,768]{1,0:T(8,128)S(1)}) custom-call(f32[2,128]{1,0:T(2,128)S(1)} %concatenate.6.refs_8_.refs_0_, bf16[528,768]{1,0:T(8,128)(2,1)S(1)} %collective-permute-done.8.refs_2_.refs_1_, f32[128,768]{1,0:T(8,128)S(1)} %speech_part.6.refs_2_, bf16[128,768]{1,0:T(8,128)(2,1)S(1)} %collective-permute-done.11.refs_3_, ...), custom_call_target="tpu_custom_call" | custom-call | flops 1006632960 | bytes 1991680 | tf_op jit(solution)/shard_map/speech_part/pallas_call | solution.py:34
  38.5 0.5 %collective-permute-start.14 = (f32[64,768]{1,0:T(8,128)S(1)}, f32[64,768]{1,0:T(8,128)S(1)}, u32[]{:S(2)}, u32[]{:S(2)}) collective-permute-start(f32[64,768]{1,0:T(8,128)S(1)} %get-tuple-element.26), channel_id=1, source_target_pairs={{0,1},{1,0},{2,3},{3,2},{4,5},{5,4},{6,7},{7,6},{8,9},{9,8},{10,11... | collective-permute-start | bytes 589832 | tf_op jit(solution)/shard_map/ppermute | solution.py:18
  39.0 0.5 %speech_part.5.refs_4_.home = f32[128,768]{1,0:T(8,128)S(1)} custom-call(f32[2,128]{1,0:T(2,128)S(1)} %concatenate.6.refs_8_.refs_0_, bf16[528,768]{1,0:T(8,128)(2,1)S(1)} %get-tuple-element.19.refs_2_.refs_1_, f32[128,768]{1,0:T(8,128)S(1)} %speech_part.4.refs_2_, bf16[128,768]{1,0:T(8,128)(2,1)S(1)} %collective-permute-done.11.refs_3_, ...), custom_call_target="tpu_custom_call" | custom-call | flops 1006632960 | bytes 1991680 | tf_op jit(solution)/shard_map/speech_part/pallas_call | solution.py:34
  39.9 0.3 collective-permute-done.14.refs_1_
  40.2 1.1 %finish.1 = (f32[128,768]{1,0:T(8,128)}, f32[64,768]{1,0:T(8,128)}) custom-call(bf16[128,768]{1,0:T(8,128)(2,1)S(1)} %get-tuple-element.16.audio, f32[128,768]{1,0:T(8,128)S(1)} %speech_part.5.refs_4_.home, f32[64,768]{1,0:T(8,128)S(1)} %collective-permute-done.13.refs_0_, f32[64,768]{1,0:T(8,128)S(1)} %collective-permute-done.14.refs_1_, ...), custom_call_target="tpu_custom_call" | custom-call | tf_op jit(solution)/shard_map/finish/pallas_call | solution.py:359
  (21 shorter events, 0.8 us)
Async XLA Ops:
  1.8 9.2 %collective-permute-start.1 = (bf16[64,768]{1,0:T(8,128)(2,1)S(1)}, bf16[64,768]{1,0:T(8,128)(2,1)S(1)}, u32[]{:S(2)}, u32[]{:S(2)}) collective-permute-start(bf16[64,768]{1,0:T(8,128)(2,1)S(1)} %get-tuple-element.17.refs_0_), channel_id=1, source_target_pairs={{0,16},{8,24},{16,0},{24,8},{1,17},{9,25},{17,1},{25,9},{2,18},{10... | collective-permute-start | bytes 294920 | tf_op jit(solution)/shard_map/ppermute | solution.py:18
  5.9 10.0 %collective-permute-start.3 = (bf16[136,768]{1,0:T(8,128)(2,1)S(1)}, bf16[136,768]{1,0:T(8,128)(2,1)S(1)}, u32[]{:S(2)}, u32[]{:S(2)}) collective-permute-start(bf16[136,768]{1,0:T(8,128)(2,1)S(1)} %get-tuple-element.18.refs_4_), channel_id=1, source_target_pairs={{0,2},{1,3},{2,0},{3,1},{4,6},{5,7},{6,4},{7,5},{8,10},{9,11},{10,... | collective-permute-start | bytes 626696 | tf_op jit(solution)/shard_map/ppermute | solution.py:18
  7.4 10.8 %collective-permute-start.4 = (bf16[136,768]{1,0:T(8,128)(2,1)S(1)}, bf16[136,768]{1,0:T(8,128)(2,1)S(1)}, u32[]{:S(2)}, u32[]{:S(2)}) collective-permute-start(bf16[136,768]{1,0:T(8,128)(2,1)S(1)} %get-tuple-element.18.refs_4_), channel_id=1, source_target_pairs={{0,4},{1,5},{2,6},{3,7},{4,0},{5,1},{6,2},{7,3},{8,12},{9,13},{10,... | collective-permute-start | bytes 626696 | tf_op jit(solution)/shard_map/ppermute | solution.py:18
  8.9 9.3 %collective-permute-start.5 = (bf16[136,768]{1,0:T(8,128)(2,1)S(1)}, bf16[136,768]{1,0:T(8,128)(2,1)S(1)}, u32[]{:S(2)}, u32[]{:S(2)}) collective-permute-start(bf16[136,768]{1,0:T(8,128)(2,1)S(1)} %get-tuple-element.18.refs_4_), channel_id=1, source_target_pairs={{0,6},{1,7},{2,4},{3,5},{4,2},{5,3},{6,0},{7,1},{8,14},{9,15},{10,... | collective-permute-start | bytes 626696 | tf_op jit(solution)/shard_map/ppermute | solution.py:18
  9.4 5.5 %collective-permute-start = (bf16[64,768]{1,0:T(8,128)(2,1)S(1)}, bf16[64,768]{1,0:T(8,128)(2,1)S(1)}, u32[]{:S(2)}, u32[]{:S(2)}) collective-permute-start(bf16[64,768]{1,0:T(8,128)(2,1)S(1)} %get-tuple-element.17.refs_0_), channel_id=1, source_target_pairs={{0,8},{8,0},{16,24},{24,16},{1,9},{9,1},{17,25},{25,17},{2,10},{10... | collective-permute-start | bytes 294920 | tf_op jit(solution)/shard_map/ppermute | solution.py:18
  11.0 4.9 %collective-permute-start.2 = (bf16[64,768]{1,0:T(8,128)(2,1)S(1)}, bf16[64,768]{1,0:T(8,128)(2,1)S(1)}, u32[]{:S(2)}, u32[]{:S(2)}) collective-permute-start(bf16[64,768]{1,0:T(8,128)(2,1)S(1)} %pass_on.1.refs_2_), channel_id=1, source_target_pairs={{0,8},{8,0},{16,24},{24,16},{1,9},{9,1},{17,25},{25,17},{2,10},{10... | collective-permute-start | bytes 294920 | tf_op jit(solution)/shard_map/ppermute | solution.py:18
  18.4 3.0 %collective-permute-start.8 = (bf16[528,768]{1,0:T(8,128)(2,1)S(1)}, bf16[528,768]{1,0:T(8,128)(2,1)S(1)}, u32[]{:S(2)}, u32[]{:S(2)}) collective-permute-start(bf16[528,768]{1,0:T(8,128)(2,1)S(1)} %get-tuple-element.19.refs_2_.refs_1_), channel_id=1, source_target_pairs={{0,1},{1,0},{2,3},{3,2},{4,5},{5,4},{6,7},{7,6},{8,9},{9,8},{10,11... | collective-permute-start | bytes 2433032 | tf_op jit(solution)/shard_map/ppermute | solution.py:18
  18.5 11.5 %collective-permute-start.6 = (bf16[256,768]{1,0:T(8,128)(2,1)S(1)}, bf16[256,768]{1,0:T(8,128)(2,1)S(1)}, u32[]{:S(2)}, u32[]{:S(2)}) collective-permute-start(bf16[256,768]{1,0:T(8,128)(2,1)S(1)} %get-tuple-element.20.refs_1_.refs_2_), channel_id=1, source_target_pairs={{0,2},{1,3},{2,0},{3,1},{4,6},{5,7},{6,4},{7,5},{8,10},{9,11},{10,... | collective-permute-start | bytes 1179656 | tf_op jit(solution)/shard_map/ppermute | solution.py:18
  19.8 11.8 %collective-permute-start.7 = (bf16[256,768]{1,0:T(8,128)(2,1)S(1)}, bf16[256,768]{1,0:T(8,128)(2,1)S(1)}, u32[]{:S(2)}, u32[]{:S(2)}) collective-permute-start(bf16[256,768]{1,0:T(8,128)(2,1)S(1)} %get-tuple-element.20.refs_1_.refs_2_), channel_id=1, source_target_pairs={{0,4},{1,5},{2,6},{3,7},{4,0},{5,1},{6,2},{7,3},{8,12},{9,13},{10,... | collective-permute-start | bytes 1179656 | tf_op jit(solution)/shard_map/ppermute | solution.py:18
  22.2 5.5 %collective-permute-start.9 = (f32[64,384]{1,0:T(8,128)S(1)}, f32[64,384]{1,0:T(8,128)S(1)}, u32[]{:S(2)}, u32[]{:S(2)}) collective-permute-start(f32[64,384]{1,0:T(8,128)S(1)} %get-tuple-element.22), channel_id=1, source_target_pairs={{0,8},{8,0},{16,24},{24,16},{1,9},{9,1},{17,25},{25,17},{2,10},{10... | collective-permute-start | bytes 294920 | tf_op jit(solution)/shard_map/ppermute | solution.py:18
  23.8 8.4 %collective-permute-start.10 = (f32[64,384]{1,0:T(8,128)S(1)}, f32[64,384]{1,0:T(8,128)S(1)}, u32[]{:S(2)}, u32[]{:S(2)}) collective-permute-start(f32[64,384]{1,0:T(8,128)S(1)} %get-tuple-element.24), channel_id=1, source_target_pairs={{0,8},{8,0},{16,24},{24,16},{1,9},{9,1},{17,25},{25,17},{2,10},{10... | collective-permute-start | bytes 294920 | tf_op jit(solution)/shard_map/ppermute | solution.py:18
  24.3 15.2 %collective-permute-start.17 = (f32[64,768]{1,0:T(8,128)S(1)}, f32[64,768]{1,0:T(8,128)S(1)}, u32[]{:S(2)}, u32[]{:S(2)}) collective-permute-start(f32[64,768]{1,0:T(8,128)S(1)} %get-tuple-element.28), channel_id=1, source_target_pairs={{0,8},{8,0},{16,24},{24,16},{1,9},{9,1},{17,25},{25,17},{2,10},{10... | collective-permute-start | bytes 589832 | tf_op jit(solution)/shard_map/ppermute | solution.py:18
  27.7 12.0 %collective-permute-start.15 = (f32[64,384]{1,0:T(8,128)S(1)}, f32[64,384]{1,0:T(8,128)S(1)}, u32[]{:S(2)}, u32[]{:S(2)}) collective-permute-start(f32[64,384]{1,0:T(8,128)S(1)} %sum_near.2.refs_1_.refs_5_), channel_id=1, source_target_pairs={{0,16},{8,24},{16,0},{24,8},{1,17},{9,25},{17,1},{25,9},{2,18},{10... | collective-permute-start | bytes 294920 | tf_op jit(solution)/shard_map/ppermute | solution.py:18
  30.0 6.5 %collective-permute-start.12 = (bf16[128,768]{1,0:T(8,128)(2,1)S(1)}, bf16[128,768]{1,0:T(8,128)(2,1)S(1)}, u32[]{:S(2)}, u32[]{:S(2)}) collective-permute-start(bf16[128,768]{1,0:T(8,128)(2,1)S(1)} %cut.3.refs_3_), channel_id=1, source_target_pairs={{0,4},{1,5},{2,6},{3,7},{4,0},{5,1},{6,2},{7,3},{8,12},{9,13},{10,... | collective-permute-start | bytes 589832 | tf_op jit(solution)/shard_map/ppermute | solution.py:18
  31.6 6.3 %collective-permute-start.11 = (bf16[128,768]{1,0:T(8,128)(2,1)S(1)}, bf16[128,768]{1,0:T(8,128)(2,1)S(1)}, u32[]{:S(2)}, u32[]{:S(2)}) collective-permute-start(bf16[128,768]{1,0:T(8,128)(2,1)S(1)} %cut.2.refs_2_), channel_id=1, source_target_pairs={{0,2},{1,3},{2,0},{3,1},{4,6},{5,7},{6,4},{7,5},{8,10},{9,11},{10,... | collective-permute-start | bytes 589832 | tf_op jit(solution)/shard_map/ppermute | solution.py:18
  32.3 7.4 %collective-permute-start.16 = (f32[64,384]{1,0:T(8,128)S(1)}, f32[64,384]{1,0:T(8,128)S(1)}, u32[]{:S(2)}, u32[]{:S(2)}) collective-permute-start(f32[64,384]{1,0:T(8,128)S(1)} %sum_near.3.refs_6_), channel_id=1, source_target_pairs={{0,16},{8,24},{16,0},{24,8},{1,17},{9,25},{17,1},{25,9},{2,18},{10... | collective-permute-start | bytes 294920 | tf_op jit(solution)/shard_map/ppermute | solution.py:18
  38.4 1.5 %collective-permute-start.13 = (f32[64,768]{1,0:T(8,128)S(1)}, f32[64,768]{1,0:T(8,128)S(1)}, u32[]{:S(2)}, u32[]{:S(2)}) collective-permute-start(f32[64,768]{1,0:T(8,128)S(1)} %get-tuple-element.25), channel_id=1, source_target_pairs={{0,1},{1,0},{2,3},{3,2},{4,5},{5,4},{6,7},{7,6},{8,9},{9,8},{10,11... | collective-permute-start | bytes 589832 | tf_op jit(solution)/shard_map/ppermute | solution.py:18
  38.5 1.7 %collective-permute-start.14 = (f32[64,768]{1,0:T(8,128)S(1)}, f32[64,768]{1,0:T(8,128)S(1)}, u32[]{:S(2)}, u32[]{:S(2)}) collective-permute-start(f32[64,768]{1,0:T(8,128)S(1)} %get-tuple-element.26), channel_id=1, source_target_pairs={{0,1},{1,0},{2,3},{3,2},{4,5},{5,4},{6,7},{7,6},{8,9},{9,8},{10,11... | collective-permute-start | bytes 589832 | tf_op jit(solution)/shard_map/ppermute | solution.py:18

commit v17 on v16

--- a/solution.py
+++ b/solution.py
@@ -45,7 +45,8 @@
 def direction(values):
     floats = values.astype(jnp.float32)
     norms = jnp.sqrt(jnp.sum(floats * floats, axis=-1, keepdims=True) + 1e-06)
-    return floats / norms, norms
+    inverse = 1.0 / norms
+    return floats * inverse, inverse
 
 
 def prepare_body(*refs):
@@ -120,9 +121,10 @@
 
 
 def coefficients(dots, match, sharp, shift):
-    logits = sharp * dots + shift
-    probs = 1.0 / (1.0 + jnp.exp(-logits))
-    return (sharp * (probs - jnp.where(match, 1.0, 0.0))).astype(jnp.bfloat16)
+    below = 1.0 + jnp.exp((-sharp) * dots - shift)
+    probs = pl.reciprocal(below, approx=True)
+    probs = probs * (2.0 - below * probs)
+    return (sharp * jnp.where(match, probs - 1.0, probs)).astype(jnp.bfloat16)
 
 
 def dot_rows(left, right):
@@ -142,7 +144,7 @@
     for first in range(0, chips * rows, CHUNK):
         chunk = speech[first : min(first + CHUNK, chips * rows), :]
         marks = marks_of(table, first // CHUNK, chunk.shape[0])
-        iota = lax.broadcasted_iota(jnp.int32, (own_text, chunk.shape[0]), 0)
+        iota = lax.broadcasted_iota(jnp.int32, (own_text, 1), 0)
         ids = [((group ^ k) * members + member) * own_text + iota for k in range(groups)]
         match = jnp.concatenate(ids, axis=0).astype(jnp.float32) == marks
         coef = coefficients(dot_rows(text, chunk), match, sharp, shift)
@@ -156,10 +158,10 @@
             row, at = row + out.shape[0], 0
 
 
-def speech_part_body(rows, own_text, has_start, chips, masks, outputs, *refs):
+def speech_part_body(rows, own_text, has_start, chips, masks, *refs):
     sharp, shift, speech = refs[0][0:1, 0:1], refs[0][1:2, 0:1], refs[1]
     total = refs[2][...] if has_start else None
-    texts, outs = list(refs[3 if has_start else 2 : -outputs]), refs[-outputs:]
+    texts, out = list(refs[3 if has_start else 2 : -1]), refs[-1]
     groups = lax.axis_size("group")
     members = lax.axis_size("member")
     group = lax.axis_index("group")
@@ -179,8 +181,7 @@
         coef = coefficients(dot_rows(block, text), marks == ids, sharp, shift)
         part = jnp.dot(coef, text, preferred_element_type=jnp.float32)
         total = part if total is None else total + part
-    for k, out in enumerate(outs):
-        out[...] = total[k * out.shape[0] : (k + 1) * out.shape[0], :]
+    out[...] = total
 
 
 def add_sides_body(*refs):
@@ -205,21 +206,21 @@
 
 
 def project(values, back):
-    heading, norms = direction(values)
+    heading, inverse = direction(values)
     along = jnp.sum(heading * back, axis=-1, keepdims=True)
-    return (back - heading * along) / norms
-
-
-def finish_body(pieces, audio, home, *refs):
-    backs, (sentence, text_back) = refs[:pieces], refs[pieces : pieces + 2]
-    speech_grad, text_grad, speech_held, text_held, done = refs[pieces + 2 :]
+    return (back - heading * along) * inverse
+
+
+def finish_body(
+    audio, home, back, sentence, text_back, speech_grad, text_grad, speech_held, text_held, done
+):
     text_held[...] = project(sentence[...], text_back[...])
     copies = [pltpu.make_async_copy(text_held, text_grad, done.at[0])]
     copies[0].start()
-    for i, back in enumerate(backs):
-        size = back.shape[0]
+    size = audio.shape[0] // 2
+    for i in range(2):
         some = slice(i * size, (i + 1) * size)
-        speech_held[some, :] = project(audio[some, :], home[some, :] + back[...])
+        speech_held[some, :] = project(audio[some, :], home[some, :] + back[some, :])
         copy = pltpu.make_async_copy(
             speech_held.at[some, :], speech_grad.at[some, :], done.at[i + 1]
         )
@@ -328,25 +329,22 @@
     from_far = [exchanged(v, "group", groups // 2) for v in far[0]]
     from_near = [exchanged(parts[k], "group", k) for k in range(1, groups // 2)]
 
-    def speech_part(speech, start, columns, texts, after=(), pieces=1):
-        body = functools.partial(
-            speech_part_body, rows, own_text, bool(start), chips, columns, pieces
-        )
+    def speech_part(speech, start, columns, texts, after=()):
+        body = functools.partial(speech_part_body, rows, own_text, bool(start), chips, columns)
         work = 40 * rows * column * len(columns) * width
-        outs = [f32(rows // pieces, width)] * pieces
         operands = [scalars, speech, *start, *texts]
-        return call(body, outs, operands, after, work, temporary, "speech_part")
+        return call(body, [f32(rows, width)], operands, after, work, temporary, "speech_part")
 
     near = [[0, *masks], [text, *text_near], tuple(far[0])]
     if square:
         away = speech_part(other, [], *near)
         home = speech_part(speech, [], *near)
-        away = speech_part(other, away, [3], text_far, pieces=2)
+        away = speech_part(other, away, [3], text_far)
         home = speech_part(speech, home, [3], text_far)
     else:
-        away = speech_part(other, [], *near, pieces=2)
+        away = speech_part(other, [], *near)
         home = speech_part(speech, [], *near)
-    back = [exchanged(piece, "member", 1) for piece in away]
+    back = exchanged(away[0], "member", 1)
     text_back = call(
         add_sides_body,
         f32(own_text, width),
@@ -357,17 +355,17 @@
     )
     results = [f32(rows, width), f32(own_text, width)]
     speech_grad, text_grad = pl.pallas_call(
-        functools.partial(finish_body, len(back)),
+        finish_body,
         out_shape=results,
-        in_specs=[pl.BlockSpec(memory_space=pltpu.VMEM)] * (4 + len(back)),
+        in_specs=[pl.BlockSpec(memory_space=pltpu.VMEM)] * 5,
         out_specs=[pl.BlockSpec(memory_space=pltpu.HBM)] * 2,
         scratch_shapes=[
             *[pltpu.VMEM(v.shape, v.dtype) for v in results],
-            pltpu.SemaphoreType.DMA((1 + len(back),)),
+            pltpu.SemaphoreType.DMA((3,)),
         ],
         compiler_params=pltpu.CompilerParams(vmem_limit_bytes=8 << 20),
         name="finish",
-    )(audio, *home, *back, sentence, text_back)
+    )(audio, *home, back, sentence, text_back)
     return (speech_grad, text_grad)
 
 

time: 41.4 us -> 41.4 us (level)
  starting transfers between devices: 20 us -> 19.5 us
    ppermute x18 -> x17, starting transfers between devices: 20 us -> 19.5 us  [exchanged(): return lax.ppermute(value, axis, [(i, i ^ mask) for i in range(size)])]
    ppermute x18 -> x17, waiting for transfers between devices: 12.1 us -> 12.5 us  [exchanged(): return lax.ppermute(value, axis, [(i, i ^ mask) for i in range(size)])]
  transfers between devices with their start and end apart: 18 -> 17, of which waited for: 10 -> 9; matrix products, arithmetic and copies ran while one was open for 0% -> 0% of each run, Pallas kernels for 11% -> 12%
where the time goes in v17:
time: 41.4 us; the launch traced here: 41.3 us
  starting transfers between devices  19.5 us (47%)
  waiting for transfers between devices  12.5 us (30%)
  Pallas kernels  7.18 us (17%)
  between operations  2.06 us (5%)
    ppermute x17, starting transfers between devices, exchanged(): return lax.ppermute(value, axis, [(i, i ^ mask) for i in range(size)])  19.5 us
    ppermute x17, waiting for transfers between devices, exchanged(): return lax.ppermute(value, axis, [(i, i ^ mask) for i in range(size)])  12.5 us
    pallas_call x13, Pallas kernels, call(): pl.pallas_call(whole, out_shape=out_shape, in_specs=specs, out_specs=jax....  4.93 us
    pallas_call x1, Pallas kernels, shards(): pl.pallas_call(prepare_body, out_shape=[bf16(rows + MARK_ROWS, width), bf...  1.18 us
    pallas_call x1, Pallas kernels, shards(): pl.pallas_call(finish_body, out_shape=results, in_specs=[pl.BlockSpec(mem...  1.07 us
  transfers between devices with their start and end apart: 17, of which 9 were waited for; matrix products, arithmetic and copies ran while one was open for 0% of the time, Pallas kernels for 12%

profile of v17, /device:TPU:0, one launch (start us, length us, event | category | flops | bytes accessed | tf_op | source)
XLA Modules:
  0.0 41.3 jit_solution(1858304316018076675)
XLA Ops:
  0.6 1.2 %unit_rows.1 = (bf16[136,768]{1,0:T(8,128)(2,1)S(1)}, bf16[64,768]{1,0:T(8,128)(2,1)S(1)}, bf16[128,768]{1,0:T(8,128)(2,1)S(1)}, bf16[64,768]{1,0:T(8,128)(2,1)S(1)}) custom-call(bf16[128,768]{1,0:T(8,128)(2,1)} %refs_0_.1, bf16[64,768]{1,0:T(8,128)(2,1)} %refs_1_.1, s32[1,128]{1,0:T(1,128)} %bitcast.3), custom_call_target="tpu_custom_call" | custom-call | tf_op jit(solution)/shard_map/unit_rows/pallas_call | solution.py:251
  1.8 4.1 %collective-permute-start.1 = (bf16[64,768]{1,0:T(8,128)(2,1)S(1)}, bf16[64,768]{1,0:T(8,128)(2,1)S(1)}, u32[]{:S(2)}, u32[]{:S(2)}) collective-permute-start(bf16[64,768]{1,0:T(8,128)(2,1)S(1)} %get-tuple-element.15.refs_0_), channel_id=1, source_target_pairs={{0,16},{8,24},{16,0},{24,8},{1,17},{9,25},{17,1},{25,9},{2,18},{10... | collective-permute-start | bytes 294920 | tf_op jit(solution)/shard_map/ppermute | solution.py:18
  5.9 1.5 %collective-permute-start.3 = (bf16[136,768]{1,0:T(8,128)(2,1)S(1)}, bf16[136,768]{1,0:T(8,128)(2,1)S(1)}, u32[]{:S(2)}, u32[]{:S(2)}) collective-permute-start(bf16[136,768]{1,0:T(8,128)(2,1)S(1)} %get-tuple-element.16.refs_4_), channel_id=1, source_target_pairs={{0,2},{1,3},{2,0},{3,1},{4,6},{5,7},{6,4},{7,5},{8,10},{9,11},{10,... | collective-permute-start | bytes 626696 | tf_op jit(solution)/shard_map/ppermute | solution.py:18
  7.4 1.5 %collective-permute-start.4 = (bf16[136,768]{1,0:T(8,128)(2,1)S(1)}, bf16[136,768]{1,0:T(8,128)(2,1)S(1)}, u32[]{:S(2)}, u32[]{:S(2)}) collective-permute-start(bf16[136,768]{1,0:T(8,128)(2,1)S(1)} %get-tuple-element.16.refs_4_), channel_id=1, source_target_pairs={{0,4},{1,5},{2,6},{3,7},{4,0},{5,1},{6,2},{7,3},{8,12},{9,13},{10,... | collective-permute-start | bytes 626696 | tf_op jit(solution)/shard_map/ppermute | solution.py:18
  8.9 0.5 %collective-permute-start.5 = (bf16[136,768]{1,0:T(8,128)(2,1)S(1)}, bf16[136,768]{1,0:T(8,128)(2,1)S(1)}, u32[]{:S(2)}, u32[]{:S(2)}) collective-permute-start(bf16[136,768]{1,0:T(8,128)(2,1)S(1)} %get-tuple-element.16.refs_4_), channel_id=1, source_target_pairs={{0,6},{1,7},{2,4},{3,5},{4,2},{5,3},{6,0},{7,1},{8,14},{9,15},{10,... | collective-permute-start | bytes 626696 | tf_op jit(solution)/shard_map/ppermute | solution.py:18
  9.4 1.6 %collective-permute-start = (bf16[64,768]{1,0:T(8,128)(2,1)S(1)}, bf16[64,768]{1,0:T(8,128)(2,1)S(1)}, u32[]{:S(2)}, u32[]{:S(2)}) collective-permute-start(bf16[64,768]{1,0:T(8,128)(2,1)S(1)} %get-tuple-element.15.refs_0_), channel_id=1, source_target_pairs={{0,8},{8,0},{16,24},{24,16},{1,9},{9,1},{17,25},{25,17},{2,10},{10... | collective-permute-start | bytes 294920 | tf_op jit(solution)/shard_map/ppermute | solution.py:18
  11.0 0.6 %collective-permute-start.2 = (bf16[64,768]{1,0:T(8,128)(2,1)S(1)}, bf16[64,768]{1,0:T(8,128)(2,1)S(1)}, u32[]{:S(2)}, u32[]{:S(2)}) collective-permute-start(bf16[64,768]{1,0:T(8,128)(2,1)S(1)} %pass_on.1.refs_2_), channel_id=1, source_target_pairs={{0,8},{8,0},{16,24},{24,16},{1,9},{9,1},{17,25},{25,17},{2,10},{10... | collective-permute-start | bytes 294920 | tf_op jit(solution)/shard_map/ppermute | solution.py:18
  12.9 1.9 %collective-permute-done.refs_1_ = bf16[64,768]{1,0:T(8,128)(2,1)S(1)} collective-permute-done((bf16[64,768]{1,0:T(8,128)(2,1)S(1)}, bf16[64,768]{1,0:T(8,128)(2,1)S(1)}, u32[]{:S(2)}, u32[]{:S(2)}) %collective-permute-start) | collective-permute-done | bytes 98336 | tf_op jit(solution)/shard_map/ppermute | solution.py:18
  14.9 1.1 %collective-permute-done.2.refs_3_ = bf16[64,768]{1,0:T(8,128)(2,1)S(1)} collective-permute-done((bf16[64,768]{1,0:T(8,128)(2,1)S(1)}, bf16[64,768]{1,0:T(8,128)(2,1)S(1)}, u32[]{:S(2)}, u32[]{:S(2)}) %collective-permute-start.2) | collective-permute-done | bytes 98336 | tf_op jit(solution)/shard_map/ppermute | solution.py:18
  15.9 2.3 %collective-permute-done.4.refs_6_ = bf16[136,768]{1,0:T(8,128)(2,1)S(1)} collective-permute-done((bf16[136,768]{1,0:T(8,128)(2,1)S(1)}, bf16[136,768]{1,0:T(8,128)(2,1)S(1)}, u32[]{:S(2)}, u32[]{:S(2)}) %collective-permute-start.4) | collective-permute-done | bytes 208928 | tf_op jit(solution)/shard_map/ppermute | solution.py:18
  18.5 1.3 %collective-permute-start.6 = (bf16[256,768]{1,0:T(8,128)(2,1)S(1)}, bf16[256,768]{1,0:T(8,128)(2,1)S(1)}, u32[]{:S(2)}, u32[]{:S(2)}) collective-permute-start(bf16[256,768]{1,0:T(8,128)(2,1)S(1)} %get-tuple-element.18.refs_1_.refs_2_), channel_id=1, source_target_pairs={{0,2},{1,3},{2,0},{3,1},{4,6},{5,7},{6,4},{7,5},{8,10},{9,11},{10,... | collective-permute-start | bytes 1179656 | tf_op jit(solution)/shard_map/ppermute | solution.py:18
  19.8 0.8 %collective-permute-start.7 = (bf16[256,768]{1,0:T(8,128)(2,1)S(1)}, bf16[256,768]{1,0:T(8,128)(2,1)S(1)}, u32[]{:S(2)}, u32[]{:S(2)}) collective-permute-start(bf16[256,768]{1,0:T(8,128)(2,1)S(1)} %get-tuple-element.18.refs_1_.refs_2_), channel_id=1, source_target_pairs={{0,4},{1,5},{2,6},{3,7},{4,0},{5,1},{6,2},{7,3},{8,12},{9,13},{10,... | collective-permute-start | bytes 1179656 | tf_op jit(solution)/shard_map/ppermute | solution.py:18
  20.6 0.8 %text_part.2.refs_3_ = f32[256,768]{1,0:T(8,128)S(1)} custom-call(f32[2,128]{1,0:T(2,128)S(1)} %concatenate.6.refs_8_.refs_0_, bf16[256,768]{1,0:T(8,128)(2,1)S(1)} %get-tuple-element.18.refs_1_.refs_2_, bf16[528,768]{1,0:T(8,128)(2,1)S(1)} %get-tuple-element.17.refs_2_.refs_1_), custom_call_target="tpu_custom_call" | custom-call | flops 402653184 | bytes 1991680 | tf_op jit(solution)/shard_map/text_part/pallas_call | solution.py:34
  21.4 0.8 %text_part.3 = (f32[64,768]{1,0:T(8,128)S(1)}, f32[64,768]{1,0:T(8,128)S(1)}, f32[64,384]{1,0:T(8,128)S(1)}, f32[64,384]{1,0:T(8,128)S(1)}, f32[64,384]{1,0:T(8,128)S(1)}, /*index=5*/f32[64,384]{1,0:T(8,128)S(1)}) custom-call(f32[2,128]{1,0:T(2,128)S(1)} %concatenate.6.refs_8_.refs_0_, bf16[256,768]{1,0:T(8,128)(2,1)S(1)} %get-tuple-element.18.refs_1_.refs_2_, ...), custom_call_target="tpu_custom_call" | custom-call | flops 402653184 | bytes 2778112 | tf_op jit(solution)/shard_map/text_part/pallas_call | solution.py:34
  22.2 1.6 %collective-permute-start.9 = (f32[64,384]{1,0:T(8,128)S(1)}, f32[64,384]{1,0:T(8,128)S(1)}, u32[]{:S(2)}, u32[]{:S(2)}) collective-permute-start(f32[64,384]{1,0:T(8,128)S(1)} %get-tuple-element.20), channel_id=1, source_target_pairs={{0,8},{8,0},{16,24},{24,16},{1,9},{9,1},{17,25},{25,17},{2,10},{10... | collective-permute-start | bytes 294920 | tf_op jit(solution)/shard_map/ppermute | solution.py:18
  23.9 0.5 %collective-permute-start.10 = (f32[64,384]{1,0:T(8,128)S(1)}, f32[64,384]{1,0:T(8,128)S(1)}, u32[]{:S(2)}, u32[]{:S(2)}) collective-permute-start(f32[64,384]{1,0:T(8,128)S(1)} %get-tuple-element.22), channel_id=1, source_target_pairs={{0,8},{8,0},{16,24},{24,16},{1,9},{9,1},{17,25},{25,17},{2,10},{10... | collective-permute-start | bytes 294920 | tf_op jit(solution)/shard_map/ppermute | solution.py:18
  24.3 1.6 %collective-permute-start.16 = (f32[64,768]{1,0:T(8,128)S(1)}, f32[64,768]{1,0:T(8,128)S(1)}, u32[]{:S(2)}, u32[]{:S(2)}) collective-permute-start(f32[64,768]{1,0:T(8,128)S(1)} %get-tuple-element.24), channel_id=1, source_target_pairs={{0,8},{8,0},{16,24},{24,16},{1,9},{9,1},{17,25},{25,17},{2,10},{10... | collective-permute-start | bytes 589832 | tf_op jit(solution)/shard_map/ppermute | solution.py:18
  25.9 1.9 %collective-permute-done.9.refs_1_ = f32[64,384]{1,0:T(8,128)S(1)} collective-permute-done((f32[64,384]{1,0:T(8,128)S(1)}, f32[64,384]{1,0:T(8,128)S(1)}, u32[]{:S(2)}, u32[]{:S(2)}) %collective-permute-start.9) | collective-permute-done | bytes 98336 | tf_op jit(solution)/shard_map/ppermute | solution.py:18
  27.8 0.7 %collective-permute-start.14 = (f32[64,384]{1,0:T(8,128)S(1)}, f32[64,384]{1,0:T(8,128)S(1)}, u32[]{:S(2)}, u32[]{:S(2)}) collective-permute-start(f32[64,384]{1,0:T(8,128)S(1)} %sum_near.2.refs_1_.refs_5_), channel_id=1, source_target_pairs={{0,16},{8,24},{16,0},{24,8},{1,17},{9,25},{17,1},{25,9},{2,18},{10... | collective-permute-start | bytes 294920 | tf_op jit(solution)/shard_map/ppermute | solution.py:18
  28.5 1.5 %collective-permute-done.6.refs_0_.refs_3_ = bf16[256,768]{1,0:T(8,128)(2,1)S(1)} collective-permute-done((bf16[256,768]{1,0:T(8,128)(2,1)S(1)}, bf16[256,768]{1,0:T(8,128)(2,1)S(1)}, u32[]{:S(2)}, u32[]{:S(2)}) %collective-permute-start.6) | collective-permute-done | bytes 393248 | tf_op jit(solution)/shard_map/ppermute | solution.py:18
  30.0 1.6 %collective-permute-start.12 = (bf16[128,768]{1,0:T(8,128)(2,1)S(1)}, bf16[128,768]{1,0:T(8,128)(2,1)S(1)}, u32[]{:S(2)}, u32[]{:S(2)}) collective-permute-start(bf16[128,768]{1,0:T(8,128)(2,1)S(1)} %cut.3.refs_3_), channel_id=1, source_target_pairs={{0,4},{1,5},{2,6},{3,7},{4,0},{5,1},{6,2},{7,3},{8,12},{9,13},{10,... | collective-permute-start | bytes 589832 | tf_op jit(solution)/shard_map/ppermute | solution.py:18
  31.6 0.6 %collective-permute-start.11 = (bf16[128,768]{1,0:T(8,128)(2,1)S(1)}, bf16[128,768]{1,0:T(8,128)(2,1)S(1)}, u32[]{:S(2)}, u32[]{:S(2)}) collective-permute-start(bf16[128,768]{1,0:T(8,128)(2,1)S(1)} %cut.2.refs_2_), channel_id=1, source_target_pairs={{0,2},{1,3},{2,0},{3,1},{4,6},{5,7},{6,4},{7,5},{8,10},{9,11},{10,... | collective-permute-start | bytes 589832 | tf_op jit(solution)/shard_map/ppermute | solution.py:18
  32.3 0.8 %collective-permute-start.15 = (f32[64,384]{1,0:T(8,128)S(1)}, f32[64,384]{1,0:T(8,128)S(1)}, u32[]{:S(2)}, u32[]{:S(2)}) collective-permute-start(f32[64,384]{1,0:T(8,128)S(1)} %sum_near.3.refs_6_), channel_id=1, source_target_pairs={{0,16},{8,24},{16,0},{24,8},{1,17},{9,25},{17,1},{25,9},{2,18},{10... | collective-permute-start | bytes 294920 | tf_op jit(solution)/shard_map/ppermute | solution.py:18
  33.1 1.0 %speech_part.4.refs_2_ = f32[128,768]{1,0:T(8,128)S(1)} custom-call(f32[2,128]{1,0:T(2,128)S(1)} %concatenate.6.refs_8_.refs_0_, bf16[528,768]{1,0:T(8,128)(2,1)S(1)} %get-tuple-element.17.refs_2_.refs_1_, bf16[256,768]{1,0:T(8,128)(2,1)S(1)} %get-tuple-element.18.refs_1_.refs_2_, bf16[256,768]{1,0:T(8,128)(2,1)S(1)} %collective-permute-done.6.refs_0_.refs_3_, ...), custom_call_target="tpu_custom_call" | custom-call | flops 3019898880 | bytes 2384896 | tf_op jit(solution)/shard_map/speech_part/pallas_call | solution.py:34
  34.1 1.1 %speech_part.6.refs_2_ = f32[128,768]{1,0:T(8,128)S(1)} custom-call(f32[2,128]{1,0:T(2,128)S(1)} %concatenate.6.refs_8_.refs_0_, bf16[528,768]{1,0:T(8,128)(2,1)S(1)} %collective-permute-done.8.refs_2_.refs_1_, bf16[256,768]{1,0:T(8,128)(2,1)S(1)} %get-tuple-element.18.refs_1_.refs_2_, bf16[256,768]{1,0:T(8,128)(2,1)S(1)} %collective-permute-done.6.refs_0_.refs_3_, ...), custom_call_target="tpu_custom_call" | custom-call | flops 3019898880 | bytes 2384896 | tf_op jit(solution)/shard_map/speech_part/pallas_call | solution.py:34
  35.2 1.4 %collective-permute-done.12.refs_4_ = bf16[128,768]{1,0:T(8,128)(2,1)S(1)} collective-permute-done((bf16[128,768]{1,0:T(8,128)(2,1)S(1)}, bf16[128,768]{1,0:T(8,128)(2,1)S(1)}, u32[]{:S(2)}, u32[]{:S(2)}) %collective-permute-start.12) | collective-permute-done | bytes 196640 | tf_op jit(solution)/shard_map/ppermute | solution.py:18
  36.6 1.3 %collective-permute-done.11.refs_3_ = bf16[128,768]{1,0:T(8,128)(2,1)S(1)} collective-permute-done((bf16[128,768]{1,0:T(8,128)(2,1)S(1)}, bf16[128,768]{1,0:T(8,128)(2,1)S(1)}, u32[]{:S(2)}, u32[]{:S(2)}) %collective-permute-start.11) | collective-permute-done | bytes 196640 | tf_op jit(solution)/shard_map/ppermute | solution.py:18
  37.9 0.5 %speech_part.7 = f32[128,768]{1,0:T(8,128)S(1)} custom-call(f32[2,128]{1,0:T(2,128)S(1)} %concatenate.6.refs_8_.refs_0_, bf16[528,768]{1,0:T(8,128)(2,1)S(1)} %collective-permute-done.8.refs_2_.refs_1_, f32[128,768]{1,0:T(8,128)S(1)} %speech_part.6.refs_2_, bf16[128,768]{1,0:T(8,128)(2,1)S(1)} %collective-permute-done.11.refs_3_, ...), custom_call_target="tpu_custom_call" | custom-call | flops 1006632960 | bytes 1991680 | tf_op jit(solution)/shard_map/speech_part/pallas_call | solution.py:34
  38.5 0.5 %speech_part.5.refs_4_.home = f32[128,768]{1,0:T(8,128)S(1)} custom-call(f32[2,128]{1,0:T(2,128)S(1)} %concatenate.6.refs_8_.refs_0_, bf16[528,768]{1,0:T(8,128)(2,1)S(1)} %get-tuple-element.17.refs_2_.refs_1_, f32[128,768]{1,0:T(8,128)S(1)} %speech_part.4.refs_2_, bf16[128,768]{1,0:T(8,128)(2,1)S(1)} %collective-permute-done.11.refs_3_, ...), custom_call_target="tpu_custom_call" | custom-call | flops 1006632960 | bytes 1991680 | tf_op jit(solution)/shard_map/speech_part/pallas_call | solution.py:34
  39.0 0.7 %collective-permute-done.15.refs_1_ = f32[64,384]{1,0:T(8,128)S(1)} collective-permute-done((f32[64,384]{1,0:T(8,128)S(1)}, f32[64,384]{1,0:T(8,128)S(1)}, u32[]{:S(2)}, u32[]{:S(2)}) %collective-permute-start.15) | collective-permute-done | bytes 98336 | tf_op jit(solution)/shard_map/ppermute | solution.py:18
  39.8 0.4 collective-permute-done.13.back
  40.2 1.1 %finish.1 = (f32[128,768]{1,0:T(8,128)}, f32[64,768]{1,0:T(8,128)}) custom-call(bf16[128,768]{1,0:T(8,128)(2,1)S(1)} %get-tuple-element.14.audio, f32[128,768]{1,0:T(8,128)S(1)} %speech_part.5.refs_4_.home, f32[128,768]{1,0:T(8,128)S(1)} %collective-permute-done.13.back, bf16[64,768]{1,0:T(8,128)(2,1)S(1)} %get-tuple-element.23.sentence, ...), custom_call_target="tpu_custom_call" | custom-call | tf_op jit(solution)/shard_map/finish/pallas_call | solution.py:357
  (19 shorter events, 0.4 us)
Async XLA Ops:
  1.8 9.2 %collective-permute-start.1 = (bf16[64,768]{1,0:T(8,128)(2,1)S(1)}, bf16[64,768]{1,0:T(8,128)(2,1)S(1)}, u32[]{:S(2)}, u32[]{:S(2)}) collective-permute-start(bf16[64,768]{1,0:T(8,128)(2,1)S(1)} %get-tuple-element.15.refs_0_), channel_id=1, source_target_pairs={{0,16},{8,24},{16,0},{24,8},{1,17},{9,25},{17,1},{25,9},{2,18},{10... | collective-permute-start | bytes 294920 | tf_op jit(solution)/shard_map/ppermute | solution.py:18
  5.9 10.0 %collective-permute-start.3 = (bf16[136,768]{1,0:T(8,128)(2,1)S(1)}, bf16[136,768]{1,0:T(8,128)(2,1)S(1)}, u32[]{:S(2)}, u32[]{:S(2)}) collective-permute-start(bf16[136,768]{1,0:T(8,128)(2,1)S(1)} %get-tuple-element.16.refs_4_), channel_id=1, source_target_pairs={{0,2},{1,3},{2,0},{3,1},{4,6},{5,7},{6,4},{7,5},{8,10},{9,11},{10,... | collective-permute-start | bytes 626696 | tf_op jit(solution)/shard_map/ppermute | solution.py:18
  7.4 10.8 %collective-permute-start.4 = (bf16[136,768]{1,0:T(8,128)(2,1)S(1)}, bf16[136,768]{1,0:T(8,128)(2,1)S(1)}, u32[]{:S(2)}, u32[]{:S(2)}) collective-permute-start(bf16[136,768]{1,0:T(8,128)(2,1)S(1)} %get-tuple-element.16.refs_4_), channel_id=1, source_target_pairs={{0,4},{1,5},{2,6},{3,7},{4,0},{5,1},{6,2},{7,3},{8,12},{9,13},{10,... | collective-permute-start | bytes 626696 | tf_op jit(solution)/shard_map/ppermute | solution.py:18
  8.9 9.3 %collective-permute-start.5 = (bf16[136,768]{1,0:T(8,128)(2,1)S(1)}, bf16[136,768]{1,0:T(8,128)(2,1)S(1)}, u32[]{:S(2)}, u32[]{:S(2)}) collective-permute-start(bf16[136,768]{1,0:T(8,128)(2,1)S(1)} %get-tuple-element.16.refs_4_), channel_id=1, source_target_pairs={{0,6},{1,7},{2,4},{3,5},{4,2},{5,3},{6,0},{7,1},{8,14},{9,15},{10,... | collective-permute-start | bytes 626696 | tf_op jit(solution)/shard_map/ppermute | solution.py:18
  9.4 5.5 %collective-permute-start = (bf16[64,768]{1,0:T(8,128)(2,1)S(1)}, bf16[64,768]{1,0:T(8,128)(2,1)S(1)}, u32[]{:S(2)}, u32[]{:S(2)}) collective-permute-start(bf16[64,768]{1,0:T(8,128)(2,1)S(1)} %get-tuple-element.15.refs_0_), channel_id=1, source_target_pairs={{0,8},{8,0},{16,24},{24,16},{1,9},{9,1},{17,25},{25,17},{2,10},{10... | collective-permute-start | bytes 294920 | tf_op jit(solution)/shard_map/ppermute | solution.py:18
  11.0 4.9 %collective-permute-start.2 = (bf16[64,768]{1,0:T(8,128)(2,1)S(1)}, bf16[64,768]{1,0:T(8,128)(2,1)S(1)}, u32[]{:S(2)}, u32[]{:S(2)}) collective-permute-start(bf16[64,768]{1,0:T(8,128)(2,1)S(1)} %pass_on.1.refs_2_), channel_id=1, source_target_pairs={{0,8},{8,0},{16,24},{24,16},{1,9},{9,1},{17,25},{25,17},{2,10},{10... | collective-permute-start | bytes 294920 | tf_op jit(solution)/shard_map/ppermute | solution.py:18
  18.4 3.0 %collective-permute-start.8 = (bf16[528,768]{1,0:T(8,128)(2,1)S(1)}, bf16[528,768]{1,0:T(8,128)(2,1)S(1)}, u32[]{:S(2)}, u32[]{:S(2)}) collective-permute-start(bf16[528,768]{1,0:T(8,128)(2,1)S(1)} %get-tuple-element.17.refs_2_.refs_1_), channel_id=1, source_target_pairs={{0,1},{1,0},{2,3},{3,2},{4,5},{5,4},{6,7},{7,6},{8,9},{9,8},{10,11... | collective-permute-start | bytes 2433032 | tf_op jit(solution)/shard_map/ppermute | solution.py:18
  18.5 11.5 %collective-permute-start.6 = (bf16[256,768]{1,0:T(8,128)(2,1)S(1)}, bf16[256,768]{1,0:T(8,128)(2,1)S(1)}, u32[]{:S(2)}, u32[]{:S(2)}) collective-permute-start(bf16[256,768]{1,0:T(8,128)(2,1)S(1)} %get-tuple-element.18.refs_1_.refs_2_), channel_id=1, source_target_pairs={{0,2},{1,3},{2,0},{3,1},{4,6},{5,7},{6,4},{7,5},{8,10},{9,11},{10,... | collective-permute-start | bytes 1179656 | tf_op jit(solution)/shard_map/ppermute | solution.py:18
  19.8 11.8 %collective-permute-start.7 = (bf16[256,768]{1,0:T(8,128)(2,1)S(1)}, bf16[256,768]{1,0:T(8,128)(2,1)S(1)}, u32[]{:S(2)}, u32[]{:S(2)}) collective-permute-start(bf16[256,768]{1,0:T(8,128)(2,1)S(1)} %get-tuple-element.18.refs_1_.refs_2_), channel_id=1, source_target_pairs={{0,4},{1,5},{2,6},{3,7},{4,0},{5,1},{6,2},{7,3},{8,12},{9,13},{10,... | collective-permute-start | bytes 1179656 | tf_op jit(solution)/shard_map/ppermute | solution.py:18
  22.2 5.5 %collective-permute-start.9 = (f32[64,384]{1,0:T(8,128)S(1)}, f32[64,384]{1,0:T(8,128)S(1)}, u32[]{:S(2)}, u32[]{:S(2)}) collective-permute-start(f32[64,384]{1,0:T(8,128)S(1)} %get-tuple-element.20), channel_id=1, source_target_pairs={{0,8},{8,0},{16,24},{24,16},{1,9},{9,1},{17,25},{25,17},{2,10},{10... | collective-permute-start | bytes 294920 | tf_op jit(solution)/shard_map/ppermute | solution.py:18
  23.9 8.4 %collective-permute-start.10 = (f32[64,384]{1,0:T(8,128)S(1)}, f32[64,384]{1,0:T(8,128)S(1)}, u32[]{:S(2)}, u32[]{:S(2)}) collective-permute-start(f32[64,384]{1,0:T(8,128)S(1)} %get-tuple-element.22), channel_id=1, source_target_pairs={{0,8},{8,0},{16,24},{24,16},{1,9},{9,1},{17,25},{25,17},{2,10},{10... | collective-permute-start | bytes 294920 | tf_op jit(solution)/shard_map/ppermute | solution.py:18
  24.3 14.7 %collective-permute-start.16 = (f32[64,768]{1,0:T(8,128)S(1)}, f32[64,768]{1,0:T(8,128)S(1)}, u32[]{:S(2)}, u32[]{:S(2)}) collective-permute-start(f32[64,768]{1,0:T(8,128)S(1)} %get-tuple-element.24), channel_id=1, source_target_pairs={{0,8},{8,0},{16,24},{24,16},{1,9},{9,1},{17,25},{25,17},{2,10},{10... | collective-permute-start | bytes 589832 | tf_op jit(solution)/shard_map/ppermute | solution.py:18
  27.8 12.0 %collective-permute-start.14 = (f32[64,384]{1,0:T(8,128)S(1)}, f32[64,384]{1,0:T(8,128)S(1)}, u32[]{:S(2)}, u32[]{:S(2)}) collective-permute-start(f32[64,384]{1,0:T(8,128)S(1)} %sum_near.2.refs_1_.refs_5_), channel_id=1, source_target_pairs={{0,16},{8,24},{16,0},{24,8},{1,17},{9,25},{17,1},{25,9},{2,18},{10... | collective-permute-start | bytes 294920 | tf_op jit(solution)/shard_map/ppermute | solution.py:18
  30.0 6.5 %collective-permute-start.12 = (bf16[128,768]{1,0:T(8,128)(2,1)S(1)}, bf16[128,768]{1,0:T(8,128)(2,1)S(1)}, u32[]{:S(2)}, u32[]{:S(2)}) collective-permute-start(bf16[128,768]{1,0:T(8,128)(2,1)S(1)} %cut.3.refs_3_), channel_id=1, source_target_pairs={{0,4},{1,5},{2,6},{3,7},{4,0},{5,1},{6,2},{7,3},{8,12},{9,13},{10,... | collective-permute-start | bytes 589832 | tf_op jit(solution)/shard_map/ppermute | solution.py:18
  31.6 6.3 %collective-permute-start.11 = (bf16[128,768]{1,0:T(8,128)(2,1)S(1)}, bf16[128,768]{1,0:T(8,128)(2,1)S(1)}, u32[]{:S(2)}, u32[]{:S(2)}) collective-permute-start(bf16[128,768]{1,0:T(8,128)(2,1)S(1)} %cut.2.refs_2_), channel_id=1, source_target_pairs={{0,2},{1,3},{2,0},{3,1},{4,6},{5,7},{6,4},{7,5},{8,10},{9,11},{10,... | collective-permute-start | bytes 589832 | tf_op jit(solution)/shard_map/ppermute | solution.py:18
  32.3 7.5 %collective-permute-start.15 = (f32[64,384]{1,0:T(8,128)S(1)}, f32[64,384]{1,0:T(8,128)S(1)}, u32[]{:S(2)}, u32[]{:S(2)}) collective-permute-start(f32[64,384]{1,0:T(8,128)S(1)} %sum_near.3.refs_6_), channel_id=1, source_target_pairs={{0,16},{8,24},{16,0},{24,8},{1,17},{9,25},{17,1},{25,9},{2,18},{10... | collective-permute-start | bytes 294920 | tf_op jit(solution)/shard_map/ppermute | solution.py:18
  38.4 1.8 %collective-permute-start.13 = (f32[128,768]{1,0:T(8,128)S(1)}, f32[128,768]{1,0:T(8,128)S(1)}, u32[]{:S(2)}, u32[]{:S(2)}) collective-permute-start(f32[128,768]{1,0:T(8,128)S(1)} %speech_part.7), channel_id=1, source_target_pairs={{0,1},{1,0},{2,3},{3,2},{4,5},{5,4},{6,7},{7,6},{8,9},{9,8},{10,11... | collective-permute-start | bytes 1179656 | tf_op jit(solution)/shard_map/ppermute | solution.py:18

commit v18 on v16

--- a/solution.py
+++ b/solution.py
@@ -8,6 +8,7 @@
 
 MARK_ROWS = 8
 TILE_ROWS = 16
+PIECE_ROWS = 32
 RADIX = 256
 CHUNK = 512
 EARLY = 1 << 33
@@ -51,16 +52,25 @@
 def prepare_body(*refs):
     sources, (speech, text) = refs[:3], refs[3:5]
     held, done = refs[5:8], refs[8]
-    copies = [pltpu.make_async_copy(sources[i], held[i], done.at[i]) for i in range(3)]
-    for copy in copies:
-        copy.start()
-    for copy in copies:
-        copy.wait()
-    audio, sentence, label = held
-    rows = audio.shape[0]
-    speech[0:rows, :] = direction(audio[...])[0].astype(jnp.bfloat16)
-    text[...] = direction(sentence[...])[0].astype(jnp.bfloat16)
-    number = label[...]
+    pieces = []
+    for source, target, out in zip(sources, held, (speech, text, None)):
+        size = source.shape[0] if out is None else PIECE_ROWS
+        for first in range(0, source.shape[0], size):
+            pieces.append((source, target, out, slice(first, first + size)))
+    copies = [
+        pltpu.make_async_copy(source.at[some, :], target.at[some, :], done.at[i])
+        for i, (source, target, _, some) in enumerate(pieces)
+    ]
+    order = sorted(range(len(pieces)), key=lambda i: (pieces[i][2] is speech, i))
+    for i in order:
+        copies[i].start()
+    for i in order:
+        copies[i].wait()
+        _, target, out, some = pieces[i]
+        if out is not None:
+            out[some, :] = direction(target[some, :])[0].astype(jnp.bfloat16)
+    rows = held[0].shape[0]
+    number = held[2][...]
     digits = jnp.concatenate([number % RADIX, number // RADIX], axis=1).astype(jnp.float32)
     wide = jnp.concatenate(
         [digits, jnp.zeros((1, speech.shape[1] - 2 * rows), jnp.float32)], axis=1
@@ -257,7 +267,10 @@
         ],
         in_specs=[pl.BlockSpec(memory_space=pltpu.HBM)] * 3,
         out_specs=[pl.BlockSpec(memory_space=pltpu.VMEM)] * 4,
-        scratch_shapes=[pltpu.VMEM((1, rows), jnp.int32), pltpu.SemaphoreType.DMA((3,))],
+        scratch_shapes=[
+            pltpu.VMEM((1, rows), jnp.int32),
+            pltpu.SemaphoreType.DMA(((rows + own_text) // PIECE_ROWS + 1,)),
+        ],
         compiler_params=pltpu.CompilerParams(vmem_limit_bytes=8 << 20),
         name="unit_rows",
     )(*[pltpu.with_memory_space_constraint(v, pltpu.HBM) for v in arguments])
@@ -287,7 +300,7 @@
     text, speech = call(
         functools.partial(join_both_body, groups),
         [bf16(column, width), bf16(chips * rows + mark_rows_of(chips, rows), width)],
-        [*text_blocks, speech_own, *speech_blocks[::-1]],
+        [*text_blocks, speech_own, *speech_blocks],
         (scalars,),
         name="join_rows",
     )

time: 41.4 us -> 41.5 us (level)
  waiting for transfers between devices: 12.1 us -> 11.4 us
    ppermute x18, waiting for transfers between devices: 12.1 us -> 11.4 us  [exchanged(): return lax.ppermute(value, axis, [(i, i ^ mask) for i in range(size)])]
    ppermute x18, starting transfers between devices: 20 us -> 20.4 us  [exchanged(): return lax.ppermute(value, axis, [(i, i ^ mask) for i in range(size)])]
where the time goes in v18:
time: 41.5 us; the launch traced here: 41.3 us
  starting transfers between devices  20.4 us (49%)
  waiting for transfers between devices  11.4 us (27%)
  Pallas kernels  7.37 us (18%)
  between operations  2.07 us (5%)
    ppermute x18, starting transfers between devices, exchanged(): return lax.ppermute(value, axis, [(i, i ^ mask) for i in range(size)])  20.4 us
    ppermute x18, waiting for transfers between devices, exchanged(): return lax.ppermute(value, axis, [(i, i ^ mask) for i in range(size)])  11.4 us
    pallas_call x13, Pallas kernels, call(): pl.pallas_call(whole, out_shape=out_shape, in_specs=specs, out_specs=jax....  4.79 us
    pallas_call x1, Pallas kernels, shards(): pl.pallas_call(prepare_body, out_shape=[bf16(rows + MARK_ROWS, width), bf...  1.51 us
    pallas_call x1, Pallas kernels, shards(): pl.pallas_call(functools.partial(finish_body, len(back)), out_shape=resul...  1.07 us
  transfers between devices with their start and end apart: 18, of which 10 were waited for; matrix products, arithmetic and copies ran while one was open for 0% of the time, Pallas kernels for 11%

profile of v18, /device:TPU:0, one launch (start us, length us, event | category | flops | bytes accessed | tf_op | source)
XLA Modules:
  0.0 41.3 jit_solution(15507849238194982450)
XLA Ops:
  0.6 1.5 %unit_rows.1 = (bf16[136,768]{1,0:T(8,128)(2,1)S(1)}, bf16[64,768]{1,0:T(8,128)(2,1)S(1)}, bf16[128,768]{1,0:T(8,128)(2,1)S(1)}, bf16[64,768]{1,0:T(8,128)(2,1)S(1)}) custom-call(bf16[128,768]{1,0:T(8,128)(2,1)} %refs_0_.1, bf16[64,768]{1,0:T(8,128)(2,1)} %refs_1_.1, s32[1,128]{1,0:T(1,128)} %bitcast.3), custom_call_target="tpu_custom_call" | custom-call | tf_op jit(solution)/shard_map/unit_rows/pallas_call | solution.py:260
  2.2 4.1 %collective-permute-start.1 = (bf16[64,768]{1,0:T(8,128)(2,1)S(1)}, bf16[64,768]{1,0:T(8,128)(2,1)S(1)}, u32[]{:S(2)}, u32[]{:S(2)}) collective-permute-start(bf16[64,768]{1,0:T(8,128)(2,1)S(1)} %get-tuple-element.17.refs_0_), channel_id=1, source_target_pairs={{0,16},{8,24},{16,0},{24,8},{1,17},{9,25},{17,1},{25,9},{2,18},{10... | collective-permute-start | bytes 294920 | tf_op jit(solution)/shard_map/ppermute | solution.py:19
  6.3 2.4 %collective-permute-start.3 = (bf16[136,768]{1,0:T(8,128)(2,1)S(1)}, bf16[136,768]{1,0:T(8,128)(2,1)S(1)}, u32[]{:S(2)}, u32[]{:S(2)}) collective-permute-start(bf16[136,768]{1,0:T(8,128)(2,1)S(1)} %get-tuple-element.18.refs_4_), channel_id=1, source_target_pairs={{0,6},{1,7},{2,4},{3,5},{4,2},{5,3},{6,0},{7,1},{8,14},{9,15},{10,... | collective-permute-start | bytes 626696 | tf_op jit(solution)/shard_map/ppermute | solution.py:19
  8.7 0.5 %collective-permute-start.4 = (bf16[136,768]{1,0:T(8,128)(2,1)S(1)}, bf16[136,768]{1,0:T(8,128)(2,1)S(1)}, u32[]{:S(2)}, u32[]{:S(2)}) collective-permute-start(bf16[136,768]{1,0:T(8,128)(2,1)S(1)} %get-tuple-element.18.refs_4_), channel_id=1, source_target_pairs={{0,4},{1,5},{2,6},{3,7},{4,0},{5,1},{6,2},{7,3},{8,12},{9,13},{10,... | collective-permute-start | bytes 626696 | tf_op jit(solution)/shard_map/ppermute | solution.py:19
  9.2 0.5 %collective-permute-start.5 = (bf16[136,768]{1,0:T(8,128)(2,1)S(1)}, bf16[136,768]{1,0:T(8,128)(2,1)S(1)}, u32[]{:S(2)}, u32[]{:S(2)}) collective-permute-start(bf16[136,768]{1,0:T(8,128)(2,1)S(1)} %get-tuple-element.18.refs_4_), channel_id=1, source_target_pairs={{0,2},{1,3},{2,0},{3,1},{4,6},{5,7},{6,4},{7,5},{8,10},{9,11},{10,... | collective-permute-start | bytes 626696 | tf_op jit(solution)/shard_map/ppermute | solution.py:19
  9.7 1.6 %collective-permute-start = (bf16[64,768]{1,0:T(8,128)(2,1)S(1)}, bf16[64,768]{1,0:T(8,128)(2,1)S(1)}, u32[]{:S(2)}, u32[]{:S(2)}) collective-permute-start(bf16[64,768]{1,0:T(8,128)(2,1)S(1)} %get-tuple-element.17.refs_0_), channel_id=1, source_target_pairs={{0,8},{8,0},{16,24},{24,16},{1,9},{9,1},{17,25},{25,17},{2,10},{10... | collective-permute-start | bytes 294920 | tf_op jit(solution)/shard_map/ppermute | solution.py:19
  11.3 0.6 %collective-permute-start.2 = (bf16[64,768]{1,0:T(8,128)(2,1)S(1)}, bf16[64,768]{1,0:T(8,128)(2,1)S(1)}, u32[]{:S(2)}, u32[]{:S(2)}) collective-permute-start(bf16[64,768]{1,0:T(8,128)(2,1)S(1)} %pass_on.1.refs_2_), channel_id=1, source_target_pairs={{0,8},{8,0},{16,24},{24,16},{1,9},{9,1},{17,25},{25,17},{2,10},{10... | collective-permute-start | bytes 294920 | tf_op jit(solution)/shard_map/ppermute | solution.py:19
  13.3 1.9 %collective-permute-done.refs_1_ = bf16[64,768]{1,0:T(8,128)(2,1)S(1)} collective-permute-done((bf16[64,768]{1,0:T(8,128)(2,1)S(1)}, bf16[64,768]{1,0:T(8,128)(2,1)S(1)}, u32[]{:S(2)}, u32[]{:S(2)}) %collective-permute-start) | collective-permute-done | bytes 98336 | tf_op jit(solution)/shard_map/ppermute | solution.py:19
  15.2 1.1 %collective-permute-done.2.refs_3_ = bf16[64,768]{1,0:T(8,128)(2,1)S(1)} collective-permute-done((bf16[64,768]{1,0:T(8,128)(2,1)S(1)}, bf16[64,768]{1,0:T(8,128)(2,1)S(1)}, u32[]{:S(2)}, u32[]{:S(2)}) %collective-permute-start.2) | collective-permute-done | bytes 98336 | tf_op jit(solution)/shard_map/ppermute | solution.py:19
  16.3 2.0 %collective-permute-done.4.refs_6_ = bf16[136,768]{1,0:T(8,128)(2,1)S(1)} collective-permute-done((bf16[136,768]{1,0:T(8,128)(2,1)S(1)}, bf16[136,768]{1,0:T(8,128)(2,1)S(1)}, u32[]{:S(2)}, u32[]{:S(2)}) %collective-permute-start.4) | collective-permute-done | bytes 208928 | tf_op jit(solution)/shard_map/ppermute | solution.py:19
  18.6 1.6 %collective-permute-start.6 = (bf16[256,768]{1,0:T(8,128)(2,1)S(1)}, bf16[256,768]{1,0:T(8,128)(2,1)S(1)}, u32[]{:S(2)}, u32[]{:S(2)}) collective-permute-start(bf16[256,768]{1,0:T(8,128)(2,1)S(1)} %get-tuple-element.20.refs_1_.refs_2_), channel_id=1, source_target_pairs={{0,2},{1,3},{2,0},{3,1},{4,6},{5,7},{6,4},{7,5},{8,10},{9,11},{10,... | collective-permute-start | bytes 1179656 | tf_op jit(solution)/shard_map/ppermute | solution.py:19
  20.1 0.7 %collective-permute-start.7 = (bf16[256,768]{1,0:T(8,128)(2,1)S(1)}, bf16[256,768]{1,0:T(8,128)(2,1)S(1)}, u32[]{:S(2)}, u32[]{:S(2)}) collective-permute-start(bf16[256,768]{1,0:T(8,128)(2,1)S(1)} %get-tuple-element.20.refs_1_.refs_2_), channel_id=1, source_target_pairs={{0,4},{1,5},{2,6},{3,7},{4,0},{5,1},{6,2},{7,3},{8,12},{9,13},{10,... | collective-permute-start | bytes 1179656 | tf_op jit(solution)/shard_map/ppermute | solution.py:19
  20.9 0.8 %text_part.2.refs_3_ = f32[256,768]{1,0:T(8,128)S(1)} custom-call(f32[2,128]{1,0:T(2,128)S(1)} %concatenate.6.refs_8_.refs_0_, bf16[256,768]{1,0:T(8,128)(2,1)S(1)} %get-tuple-element.20.refs_1_.refs_2_, bf16[528,768]{1,0:T(8,128)(2,1)S(1)} %get-tuple-element.19.refs_2_.refs_1_), custom_call_target="tpu_custom_call" | custom-call | flops 402653184 | bytes 1991680 | tf_op jit(solution)/shard_map/text_part/pallas_call | solution.py:35
  21.7 0.8 %text_part.3 = (f32[64,768]{1,0:T(8,128)S(1)}, f32[64,768]{1,0:T(8,128)S(1)}, f32[64,384]{1,0:T(8,128)S(1)}, f32[64,384]{1,0:T(8,128)S(1)}, f32[64,384]{1,0:T(8,128)S(1)}, /*index=5*/f32[64,384]{1,0:T(8,128)S(1)}) custom-call(f32[2,128]{1,0:T(2,128)S(1)} %concatenate.6.refs_8_.refs_0_, bf16[256,768]{1,0:T(8,128)(2,1)S(1)} %get-tuple-element.20.refs_1_.refs_2_, ...), custom_call_target="tpu_custom_call" | custom-call | flops 402653184 | bytes 2778112 | tf_op jit(solution)/shard_map/text_part/pallas_call | solution.py:35
  22.4 1.6 %collective-permute-start.9 = (f32[64,384]{1,0:T(8,128)S(1)}, f32[64,384]{1,0:T(8,128)S(1)}, u32[]{:S(2)}, u32[]{:S(2)}) collective-permute-start(f32[64,384]{1,0:T(8,128)S(1)} %get-tuple-element.22), channel_id=1, source_target_pairs={{0,8},{8,0},{16,24},{24,16},{1,9},{9,1},{17,25},{25,17},{2,10},{10... | collective-permute-start | bytes 294920 | tf_op jit(solution)/shard_map/ppermute | solution.py:19
  24.1 0.4 %collective-permute-start.10 = (f32[64,384]{1,0:T(8,128)S(1)}, f32[64,384]{1,0:T(8,128)S(1)}, u32[]{:S(2)}, u32[]{:S(2)}) collective-permute-start(f32[64,384]{1,0:T(8,128)S(1)} %get-tuple-element.24), channel_id=1, source_target_pairs={{0,8},{8,0},{16,24},{24,16},{1,9},{9,1},{17,25},{25,17},{2,10},{10... | collective-permute-start | bytes 294920 | tf_op jit(solution)/shard_map/ppermute | solution.py:19
  24.5 1.6 %collective-permute-start.17 = (f32[64,768]{1,0:T(8,128)S(1)}, f32[64,768]{1,0:T(8,128)S(1)}, u32[]{:S(2)}, u32[]{:S(2)}) collective-permute-start(f32[64,768]{1,0:T(8,128)S(1)} %get-tuple-element.28), channel_id=1, source_target_pairs={{0,8},{8,0},{16,24},{24,16},{1,9},{9,1},{17,25},{25,17},{2,10},{10... | collective-permute-start | bytes 589832 | tf_op jit(solution)/shard_map/ppermute | solution.py:19
  26.1 1.9 %collective-permute-done.9.refs_1_ = f32[64,384]{1,0:T(8,128)S(1)} collective-permute-done((f32[64,384]{1,0:T(8,128)S(1)}, f32[64,384]{1,0:T(8,128)S(1)}, u32[]{:S(2)}, u32[]{:S(2)}) %collective-permute-start.9) | collective-permute-done | bytes 98336 | tf_op jit(solution)/shard_map/ppermute | solution.py:19
  28.0 0.8 %collective-permute-start.15 = (f32[64,384]{1,0:T(8,128)S(1)}, f32[64,384]{1,0:T(8,128)S(1)}, u32[]{:S(2)}, u32[]{:S(2)}) collective-permute-start(f32[64,384]{1,0:T(8,128)S(1)} %sum_near.2.refs_1_.refs_5_), channel_id=1, source_target_pairs={{0,16},{8,24},{16,0},{24,8},{1,17},{9,25},{17,1},{25,9},{2,18},{10... | collective-permute-start | bytes 294920 | tf_op jit(solution)/shard_map/ppermute | solution.py:19
  28.8 1.4 %collective-permute-done.6.refs_0_.refs_3_ = bf16[256,768]{1,0:T(8,128)(2,1)S(1)} collective-permute-done((bf16[256,768]{1,0:T(8,128)(2,1)S(1)}, bf16[256,768]{1,0:T(8,128)(2,1)S(1)}, u32[]{:S(2)}, u32[]{:S(2)}) %collective-permute-start.6) | collective-permute-done | bytes 393248 | tf_op jit(solution)/shard_map/ppermute | solution.py:19
  30.1 1.5 %collective-permute-start.12 = (bf16[128,768]{1,0:T(8,128)(2,1)S(1)}, bf16[128,768]{1,0:T(8,128)(2,1)S(1)}, u32[]{:S(2)}, u32[]{:S(2)}) collective-permute-start(bf16[128,768]{1,0:T(8,128)(2,1)S(1)} %cut.3.refs_3_), channel_id=1, source_target_pairs={{0,4},{1,5},{2,6},{3,7},{4,0},{5,1},{6,2},{7,3},{8,12},{9,13},{10,... | collective-permute-start | bytes 589832 | tf_op jit(solution)/shard_map/ppermute | solution.py:19
  31.7 0.9 %collective-permute-start.11 = (bf16[128,768]{1,0:T(8,128)(2,1)S(1)}, bf16[128,768]{1,0:T(8,128)(2,1)S(1)}, u32[]{:S(2)}, u32[]{:S(2)}) collective-permute-start(bf16[128,768]{1,0:T(8,128)(2,1)S(1)} %cut.2.refs_2_), channel_id=1, source_target_pairs={{0,2},{1,3},{2,0},{3,1},{4,6},{5,7},{6,4},{7,5},{8,10},{9,11},{10,... | collective-permute-start | bytes 589832 | tf_op jit(solution)/shard_map/ppermute | solution.py:19
  32.5 0.9 %collective-permute-start.16 = (f32[64,384]{1,0:T(8,128)S(1)}, f32[64,384]{1,0:T(8,128)S(1)}, u32[]{:S(2)}, u32[]{:S(2)}) collective-permute-start(f32[64,384]{1,0:T(8,128)S(1)} %sum_near.3.refs_6_), channel_id=1, source_target_pairs={{0,16},{8,24},{16,0},{24,8},{1,17},{9,25},{17,1},{25,9},{2,18},{10... | collective-permute-start | bytes 294920 | tf_op jit(solution)/shard_map/ppermute | solution.py:19
  33.4 1.0 %speech_part.4.refs_2_ = f32[128,768]{1,0:T(8,128)S(1)} custom-call(f32[2,128]{1,0:T(2,128)S(1)} %concatenate.6.refs_8_.refs_0_, bf16[528,768]{1,0:T(8,128)(2,1)S(1)} %get-tuple-element.19.refs_2_.refs_1_, bf16[256,768]{1,0:T(8,128)(2,1)S(1)} %get-tuple-element.20.refs_1_.refs_2_, bf16[256,768]{1,0:T(8,128)(2,1)S(1)} %collective-permute-done.6.refs_0_.refs_3_, ...), custom_call_target="tpu_custom_call" | custom-call | flops 3019898880 | bytes 2384896 | tf_op jit(solution)/shard_map/speech_part/pallas_call | solution.py:35
  34.4 1.0 %speech_part.6.refs_2_ = f32[128,768]{1,0:T(8,128)S(1)} custom-call(f32[2,128]{1,0:T(2,128)S(1)} %concatenate.6.refs_8_.refs_0_, bf16[528,768]{1,0:T(8,128)(2,1)S(1)} %collective-permute-done.8.refs_2_.refs_1_, bf16[256,768]{1,0:T(8,128)(2,1)S(1)} %get-tuple-element.20.refs_1_.refs_2_, bf16[256,768]{1,0:T(8,128)(2,1)S(1)} %collective-permute-done.6.refs_0_.refs_3_, ...), custom_call_target="tpu_custom_call" | custom-call | flops 3019898880 | bytes 2384896 | tf_op jit(solution)/shard_map/speech_part/pallas_call | solution.py:35
  35.5 1.2 %collective-permute-done.12.refs_4_ = bf16[128,768]{1,0:T(8,128)(2,1)S(1)} collective-permute-done((bf16[128,768]{1,0:T(8,128)(2,1)S(1)}, bf16[128,768]{1,0:T(8,128)(2,1)S(1)}, u32[]{:S(2)}, u32[]{:S(2)}) %collective-permute-start.12) | collective-permute-done | bytes 196640 | tf_op jit(solution)/shard_map/ppermute | solution.py:19
  36.7 1.2 %collective-permute-done.11.refs_3_ = bf16[128,768]{1,0:T(8,128)(2,1)S(1)} collective-permute-done((bf16[128,768]{1,0:T(8,128)(2,1)S(1)}, bf16[128,768]{1,0:T(8,128)(2,1)S(1)}, u32[]{:S(2)}, u32[]{:S(2)}) %collective-permute-start.11) | collective-permute-done | bytes 196640 | tf_op jit(solution)/shard_map/ppermute | solution.py:19
  37.9 0.5 %speech_part.7 = (f32[64,768]{1,0:T(8,128)S(1)}, f32[64,768]{1,0:T(8,128)S(1)}) custom-call(f32[2,128]{1,0:T(2,128)S(1)} %concatenate.6.refs_8_.refs_0_, bf16[528,768]{1,0:T(8,128)(2,1)S(1)} %collective-permute-done.8.refs_2_.refs_1_, f32[128,768]{1,0:T(8,128)S(1)} %speech_part.6.refs_2_, bf16[128,768]{1,0:T(8,128)(2,1)S(1)} %collective-permute-done.11.refs_3_, ...), custom_call_target="tpu_custom_call" | custom-call | flops 1006632960 | bytes 1991680 | tf_op jit(solution)/shard_map/speech_part/pallas_call | solution.py:35
  38.5 0.5 %collective-permute-start.14 = (f32[64,768]{1,0:T(8,128)S(1)}, f32[64,768]{1,0:T(8,128)S(1)}, u32[]{:S(2)}, u32[]{:S(2)}) collective-permute-start(f32[64,768]{1,0:T(8,128)S(1)} %get-tuple-element.26), channel_id=1, source_target_pairs={{0,1},{1,0},{2,3},{3,2},{4,5},{5,4},{6,7},{7,6},{8,9},{9,8},{10,11... | collective-permute-start | bytes 589832 | tf_op jit(solution)/shard_map/ppermute | solution.py:19
  39.0 0.5 %speech_part.5.refs_4_.home = f32[128,768]{1,0:T(8,128)S(1)} custom-call(f32[2,128]{1,0:T(2,128)S(1)} %concatenate.6.refs_8_.refs_0_, bf16[528,768]{1,0:T(8,128)(2,1)S(1)} %get-tuple-element.19.refs_2_.refs_1_, f32[128,768]{1,0:T(8,128)S(1)} %speech_part.4.refs_2_, bf16[128,768]{1,0:T(8,128)(2,1)S(1)} %collective-permute-done.11.refs_3_, ...), custom_call_target="tpu_custom_call" | custom-call | flops 1006632960 | bytes 1991680 | tf_op jit(solution)/shard_map/speech_part/pallas_call | solution.py:35
  39.5 0.5 %collective-permute-done.16.refs_1_ = f32[64,384]{1,0:T(8,128)S(1)} collective-permute-done((f32[64,384]{1,0:T(8,128)S(1)}, f32[64,384]{1,0:T(8,128)S(1)}, u32[]{:S(2)}, u32[]{:S(2)}) %collective-permute-start.16) | collective-permute-done | bytes 98336 | tf_op jit(solution)/shard_map/ppermute | solution.py:19
  40.2 1.1 %finish.1 = (f32[128,768]{1,0:T(8,128)}, f32[64,768]{1,0:T(8,128)}) custom-call(bf16[128,768]{1,0:T(8,128)(2,1)S(1)} %get-tuple-element.16.audio, f32[128,768]{1,0:T(8,128)S(1)} %speech_part.5.refs_4_.home, f32[64,768]{1,0:T(8,128)S(1)} %collective-permute-done.13.refs_0_, f32[64,768]{1,0:T(8,128)S(1)} %collective-permute-done.14.refs_1_, ...), custom_call_target="tpu_custom_call" | custom-call | tf_op jit(solution)/shard_map/finish/pallas_call | solution.py:372
  (21 shorter events, 0.7 us)
Async XLA Ops:
  2.2 9.2 %collective-permute-start.1 = (bf16[64,768]{1,0:T(8,128)(2,1)S(1)}, bf16[64,768]{1,0:T(8,128)(2,1)S(1)}, u32[]{:S(2)}, u32[]{:S(2)}) collective-permute-start(bf16[64,768]{1,0:T(8,128)(2,1)S(1)} %get-tuple-element.17.refs_0_), channel_id=1, source_target_pairs={{0,16},{8,24},{16,0},{24,8},{1,17},{9,25},{17,1},{25,9},{2,18},{10... | collective-permute-start | bytes 294920 | tf_op jit(solution)/shard_map/ppermute | solution.py:19
  6.3 10.0 %collective-permute-start.3 = (bf16[136,768]{1,0:T(8,128)(2,1)S(1)}, bf16[136,768]{1,0:T(8,128)(2,1)S(1)}, u32[]{:S(2)}, u32[]{:S(2)}) collective-permute-start(bf16[136,768]{1,0:T(8,128)(2,1)S(1)} %get-tuple-element.18.refs_4_), channel_id=1, source_target_pairs={{0,6},{1,7},{2,4},{3,5},{4,2},{5,3},{6,0},{7,1},{8,14},{9,15},{10,... | collective-permute-start | bytes 626696 | tf_op jit(solution)/shard_map/ppermute | solution.py:19
  8.7 9.6 %collective-permute-start.4 = (bf16[136,768]{1,0:T(8,128)(2,1)S(1)}, bf16[136,768]{1,0:T(8,128)(2,1)S(1)}, u32[]{:S(2)}, u32[]{:S(2)}) collective-permute-start(bf16[136,768]{1,0:T(8,128)(2,1)S(1)} %get-tuple-element.18.refs_4_), channel_id=1, source_target_pairs={{0,4},{1,5},{2,6},{3,7},{4,0},{5,1},{6,2},{7,3},{8,12},{9,13},{10,... | collective-permute-start | bytes 626696 | tf_op jit(solution)/shard_map/ppermute | solution.py:19
  9.2 9.1 %collective-permute-start.5 = (bf16[136,768]{1,0:T(8,128)(2,1)S(1)}, bf16[136,768]{1,0:T(8,128)(2,1)S(1)}, u32[]{:S(2)}, u32[]{:S(2)}) collective-permute-start(bf16[136,768]{1,0:T(8,128)(2,1)S(1)} %get-tuple-element.18.refs_4_), channel_id=1, source_target_pairs={{0,2},{1,3},{2,0},{3,1},{4,6},{5,7},{6,4},{7,5},{8,10},{9,11},{10,... | collective-permute-start | bytes 626696 | tf_op jit(solution)/shard_map/ppermute | solution.py:19
  9.7 5.5 %collective-permute-start = (bf16[64,768]{1,0:T(8,128)(2,1)S(1)}, bf16[64,768]{1,0:T(8,128)(2,1)S(1)}, u32[]{:S(2)}, u32[]{:S(2)}) collective-permute-start(bf16[64,768]{1,0:T(8,128)(2,1)S(1)} %get-tuple-element.17.refs_0_), channel_id=1, source_target_pairs={{0,8},{8,0},{16,24},{24,16},{1,9},{9,1},{17,25},{25,17},{2,10},{10... | collective-permute-start | bytes 294920 | tf_op jit(solution)/shard_map/ppermute | solution.py:19
  11.3 4.9 %collective-permute-start.2 = (bf16[64,768]{1,0:T(8,128)(2,1)S(1)}, bf16[64,768]{1,0:T(8,128)(2,1)S(1)}, u32[]{:S(2)}, u32[]{:S(2)}) collective-permute-start(bf16[64,768]{1,0:T(8,128)(2,1)S(1)} %pass_on.1.refs_2_), channel_id=1, source_target_pairs={{0,8},{8,0},{16,24},{24,16},{1,9},{9,1},{17,25},{25,17},{2,10},{10... | collective-permute-start | bytes 294920 | tf_op jit(solution)/shard_map/ppermute | solution.py:19
  18.5 3.1 %collective-permute-start.8 = (bf16[528,768]{1,0:T(8,128)(2,1)S(1)}, bf16[528,768]{1,0:T(8,128)(2,1)S(1)}, u32[]{:S(2)}, u32[]{:S(2)}) collective-permute-start(bf16[528,768]{1,0:T(8,128)(2,1)S(1)} %get-tuple-element.19.refs_2_.refs_1_), channel_id=1, source_target_pairs={{0,1},{1,0},{2,3},{3,2},{4,5},{5,4},{6,7},{7,6},{8,9},{9,8},{10,11... | collective-permute-start | bytes 2433032 | tf_op jit(solution)/shard_map/ppermute | solution.py:19
  18.6 11.5 %collective-permute-start.6 = (bf16[256,768]{1,0:T(8,128)(2,1)S(1)}, bf16[256,768]{1,0:T(8,128)(2,1)S(1)}, u32[]{:S(2)}, u32[]{:S(2)}) collective-permute-start(bf16[256,768]{1,0:T(8,128)(2,1)S(1)} %get-tuple-element.20.refs_1_.refs_2_), channel_id=1, source_target_pairs={{0,2},{1,3},{2,0},{3,1},{4,6},{5,7},{6,4},{7,5},{8,10},{9,11},{10,... | collective-permute-start | bytes 1179656 | tf_op jit(solution)/shard_map/ppermute | solution.py:19
  20.1 11.5 %collective-permute-start.7 = (bf16[256,768]{1,0:T(8,128)(2,1)S(1)}, bf16[256,768]{1,0:T(8,128)(2,1)S(1)}, u32[]{:S(2)}, u32[]{:S(2)}) collective-permute-start(bf16[256,768]{1,0:T(8,128)(2,1)S(1)} %get-tuple-element.20.refs_1_.refs_2_), channel_id=1, source_target_pairs={{0,4},{1,5},{2,6},{3,7},{4,0},{5,1},{6,2},{7,3},{8,12},{9,13},{10,... | collective-permute-start | bytes 1179656 | tf_op jit(solution)/shard_map/ppermute | solution.py:19
  22.4 5.5 %collective-permute-start.9 = (f32[64,384]{1,0:T(8,128)S(1)}, f32[64,384]{1,0:T(8,128)S(1)}, u32[]{:S(2)}, u32[]{:S(2)}) collective-permute-start(f32[64,384]{1,0:T(8,128)S(1)} %get-tuple-element.22), channel_id=1, source_target_pairs={{0,8},{8,0},{16,24},{24,16},{1,9},{9,1},{17,25},{25,17},{2,10},{10... | collective-permute-start | bytes 294920 | tf_op jit(solution)/shard_map/ppermute | solution.py:19
  24.1 8.4 %collective-permute-start.10 = (f32[64,384]{1,0:T(8,128)S(1)}, f32[64,384]{1,0:T(8,128)S(1)}, u32[]{:S(2)}, u32[]{:S(2)}) collective-permute-start(f32[64,384]{1,0:T(8,128)S(1)} %get-tuple-element.24), channel_id=1, source_target_pairs={{0,8},{8,0},{16,24},{24,16},{1,9},{9,1},{17,25},{25,17},{2,10},{10... | collective-permute-start | bytes 294920 | tf_op jit(solution)/shard_map/ppermute | solution.py:19
  24.5 15.0 %collective-permute-start.17 = (f32[64,768]{1,0:T(8,128)S(1)}, f32[64,768]{1,0:T(8,128)S(1)}, u32[]{:S(2)}, u32[]{:S(2)}) collective-permute-start(f32[64,768]{1,0:T(8,128)S(1)} %get-tuple-element.28), channel_id=1, source_target_pairs={{0,8},{8,0},{16,24},{24,16},{1,9},{9,1},{17,25},{25,17},{2,10},{10... | collective-permute-start | bytes 589832 | tf_op jit(solution)/shard_map/ppermute | solution.py:19
  28.0 12.0 %collective-permute-start.15 = (f32[64,384]{1,0:T(8,128)S(1)}, f32[64,384]{1,0:T(8,128)S(1)}, u32[]{:S(2)}, u32[]{:S(2)}) collective-permute-start(f32[64,384]{1,0:T(8,128)S(1)} %sum_near.2.refs_1_.refs_5_), channel_id=1, source_target_pairs={{0,16},{8,24},{16,0},{24,8},{1,17},{9,25},{17,1},{25,9},{2,18},{10... | collective-permute-start | bytes 294920 | tf_op jit(solution)/shard_map/ppermute | solution.py:19
  30.1 6.5 %collective-permute-start.12 = (bf16[128,768]{1,0:T(8,128)(2,1)S(1)}, bf16[128,768]{1,0:T(8,128)(2,1)S(1)}, u32[]{:S(2)}, u32[]{:S(2)}) collective-permute-start(bf16[128,768]{1,0:T(8,128)(2,1)S(1)} %cut.3.refs_3_), channel_id=1, source_target_pairs={{0,4},{1,5},{2,6},{3,7},{4,0},{5,1},{6,2},{7,3},{8,12},{9,13},{10,... | collective-permute-start | bytes 589832 | tf_op jit(solution)/shard_map/ppermute | solution.py:19
  31.7 6.3 %collective-permute-start.11 = (bf16[128,768]{1,0:T(8,128)(2,1)S(1)}, bf16[128,768]{1,0:T(8,128)(2,1)S(1)}, u32[]{:S(2)}, u32[]{:S(2)}) collective-permute-start(bf16[128,768]{1,0:T(8,128)(2,1)S(1)} %cut.2.refs_2_), channel_id=1, source_target_pairs={{0,2},{1,3},{2,0},{3,1},{4,6},{5,7},{6,4},{7,5},{8,10},{9,11},{10,... | collective-permute-start | bytes 589832 | tf_op jit(solution)/shard_map/ppermute | solution.py:19
  32.5 7.5 %collective-permute-start.16 = (f32[64,384]{1,0:T(8,128)S(1)}, f32[64,384]{1,0:T(8,128)S(1)}, u32[]{:S(2)}, u32[]{:S(2)}) collective-permute-start(f32[64,384]{1,0:T(8,128)S(1)} %sum_near.3.refs_6_), channel_id=1, source_target_pairs={{0,16},{8,24},{16,0},{24,8},{1,17},{9,25},{17,1},{25,9},{2,18},{10... | collective-permute-start | bytes 294920 | tf_op jit(solution)/shard_map/ppermute | solution.py:19
  38.4 1.6 %collective-permute-start.13 = (f32[64,768]{1,0:T(8,128)S(1)}, f32[64,768]{1,0:T(8,128)S(1)}, u32[]{:S(2)}, u32[]{:S(2)}) collective-permute-start(f32[64,768]{1,0:T(8,128)S(1)} %get-tuple-element.25), channel_id=1, source_target_pairs={{0,1},{1,0},{2,3},{3,2},{4,5},{5,4},{6,7},{7,6},{8,9},{9,8},{10,11... | collective-permute-start | bytes 589832 | tf_op jit(solution)/shard_map/ppermute | solution.py:19
  38.5 1.7 %collective-permute-start.14 = (f32[64,768]{1,0:T(8,128)S(1)}, f32[64,768]{1,0:T(8,128)S(1)}, u32[]{:S(2)}, u32[]{:S(2)}) collective-permute-start(f32[64,768]{1,0:T(8,128)S(1)} %get-tuple-element.26), channel_id=1, source_target_pairs={{0,1},{1,0},{2,3},{3,2},{4,5},{5,4},{6,7},{7,6},{8,9},{9,8},{10,11... | collective-permute-start | bytes 589832 | tf_op jit(solution)/shard_map/ppermute | solution.py:19

commit v19 on v16

--- a/solution.py
+++ b/solution.py
@@ -287,7 +287,7 @@
     text, speech = call(
         functools.partial(join_both_body, groups),
         [bf16(column, width), bf16(chips * rows + mark_rows_of(chips, rows), width)],
-        [*text_blocks, speech_own, *speech_blocks[::-1]],
+        [*text_blocks, speech_own, *speech_blocks],
         (scalars,),
         name="join_rows",
     )

time: 41.4 us -> 41.1 us (level)
  waiting for transfers between devices: 12.1 us -> 11.4 us
    ppermute x18, waiting for transfers between devices: 12.1 us -> 11.4 us  [exchanged(): return lax.ppermute(value, axis, [(i, i ^ mask) for i in range(size)])]
    ppermute x18, starting transfers between devices: 20 us -> 20.4 us  [exchanged(): return lax.ppermute(value, axis, [(i, i ^ mask) for i in range(size)])]
where the time goes in v19:
time: 41.1 us; the launch traced here: 40.9 us
  starting transfers between devices  20.4 us (50%)
  waiting for transfers between devices  11.4 us (28%)
  Pallas kernels  7.03 us (17%)
  between operations  2.07 us (5%)
    ppermute x18, starting transfers between devices, exchanged(): return lax.ppermute(value, axis, [(i, i ^ mask) for i in range(size)])  20.4 us
    ppermute x18, waiting for transfers between devices, exchanged(): return lax.ppermute(value, axis, [(i, i ^ mask) for i in range(size)])  11.4 us
    pallas_call x13, Pallas kernels, call(): pl.pallas_call(whole, out_shape=out_shape, in_specs=specs, out_specs=jax....  4.79 us
    pallas_call x1, Pallas kernels, shards(): pl.pallas_call(prepare_body, out_shape=[bf16(rows + MARK_ROWS, width), bf...  1.18 us
    pallas_call x1, Pallas kernels, shards(): pl.pallas_call(functools.partial(finish_body, len(back)), out_shape=resul...  1.07 us
  transfers between devices with their start and end apart: 18, of which 10 were waited for; matrix products, arithmetic and copies ran while one was open for 0% of the time, Pallas kernels for 11%

profile of v19, /device:TPU:0, one launch (start us, length us, event | category | flops | bytes accessed | tf_op | source)
XLA Modules:
  0.0 40.9 jit_solution(3347205317992747106)
XLA Ops:
  0.6 1.2 %unit_rows.1 = (bf16[136,768]{1,0:T(8,128)(2,1)S(1)}, bf16[64,768]{1,0:T(8,128)(2,1)S(1)}, bf16[128,768]{1,0:T(8,128)(2,1)S(1)}, bf16[64,768]{1,0:T(8,128)(2,1)S(1)}) custom-call(bf16[128,768]{1,0:T(8,128)(2,1)} %refs_0_.1, bf16[64,768]{1,0:T(8,128)(2,1)} %refs_1_.1, s32[1,128]{1,0:T(1,128)} %bitcast.3), custom_call_target="tpu_custom_call" | custom-call | tf_op jit(solution)/shard_map/unit_rows/pallas_call | solution.py:250
  1.8 4.1 %collective-permute-start.1 = (bf16[64,768]{1,0:T(8,128)(2,1)S(1)}, bf16[64,768]{1,0:T(8,128)(2,1)S(1)}, u32[]{:S(2)}, u32[]{:S(2)}) collective-permute-start(bf16[64,768]{1,0:T(8,128)(2,1)S(1)} %get-tuple-element.17.refs_0_), channel_id=1, source_target_pairs={{0,16},{8,24},{16,0},{24,8},{1,17},{9,25},{17,1},{25,9},{2,18},{10... | collective-permute-start | bytes 294920 | tf_op jit(solution)/shard_map/ppermute | solution.py:18
  5.9 2.4 %collective-permute-start.3 = (bf16[136,768]{1,0:T(8,128)(2,1)S(1)}, bf16[136,768]{1,0:T(8,128)(2,1)S(1)}, u32[]{:S(2)}, u32[]{:S(2)}) collective-permute-start(bf16[136,768]{1,0:T(8,128)(2,1)S(1)} %get-tuple-element.18.refs_4_), channel_id=1, source_target_pairs={{0,6},{1,7},{2,4},{3,5},{4,2},{5,3},{6,0},{7,1},{8,14},{9,15},{10,... | collective-permute-start | bytes 626696 | tf_op jit(solution)/shard_map/ppermute | solution.py:18
  8.4 0.5 %collective-permute-start.4 = (bf16[136,768]{1,0:T(8,128)(2,1)S(1)}, bf16[136,768]{1,0:T(8,128)(2,1)S(1)}, u32[]{:S(2)}, u32[]{:S(2)}) collective-permute-start(bf16[136,768]{1,0:T(8,128)(2,1)S(1)} %get-tuple-element.18.refs_4_), channel_id=1, source_target_pairs={{0,4},{1,5},{2,6},{3,7},{4,0},{5,1},{6,2},{7,3},{8,12},{9,13},{10,... | collective-permute-start | bytes 626696 | tf_op jit(solution)/shard_map/ppermute | solution.py:18
  8.9 0.5 %collective-permute-start.5 = (bf16[136,768]{1,0:T(8,128)(2,1)S(1)}, bf16[136,768]{1,0:T(8,128)(2,1)S(1)}, u32[]{:S(2)}, u32[]{:S(2)}) collective-permute-start(bf16[136,768]{1,0:T(8,128)(2,1)S(1)} %get-tuple-element.18.refs_4_), channel_id=1, source_target_pairs={{0,2},{1,3},{2,0},{3,1},{4,6},{5,7},{6,4},{7,5},{8,10},{9,11},{10,... | collective-permute-start | bytes 626696 | tf_op jit(solution)/shard_map/ppermute | solution.py:18
  9.4 1.6 %collective-permute-start = (bf16[64,768]{1,0:T(8,128)(2,1)S(1)}, bf16[64,768]{1,0:T(8,128)(2,1)S(1)}, u32[]{:S(2)}, u32[]{:S(2)}) collective-permute-start(bf16[64,768]{1,0:T(8,128)(2,1)S(1)} %get-tuple-element.17.refs_0_), channel_id=1, source_target_pairs={{0,8},{8,0},{16,24},{24,16},{1,9},{9,1},{17,25},{25,17},{2,10},{10... | collective-permute-start | bytes 294920 | tf_op jit(solution)/shard_map/ppermute | solution.py:18
  11.0 0.6 %collective-permute-start.2 = (bf16[64,768]{1,0:T(8,128)(2,1)S(1)}, bf16[64,768]{1,0:T(8,128)(2,1)S(1)}, u32[]{:S(2)}, u32[]{:S(2)}) collective-permute-start(bf16[64,768]{1,0:T(8,128)(2,1)S(1)} %pass_on.1.refs_2_), channel_id=1, source_target_pairs={{0,8},{8,0},{16,24},{24,16},{1,9},{9,1},{17,25},{25,17},{2,10},{10... | collective-permute-start | bytes 294920 | tf_op jit(solution)/shard_map/ppermute | solution.py:18
  12.9 1.9 %collective-permute-done.refs_1_ = bf16[64,768]{1,0:T(8,128)(2,1)S(1)} collective-permute-done((bf16[64,768]{1,0:T(8,128)(2,1)S(1)}, bf16[64,768]{1,0:T(8,128)(2,1)S(1)}, u32[]{:S(2)}, u32[]{:S(2)}) %collective-permute-start) | collective-permute-done | bytes 98336 | tf_op jit(solution)/shard_map/ppermute | solution.py:18
  14.9 1.1 %collective-permute-done.2.refs_3_ = bf16[64,768]{1,0:T(8,128)(2,1)S(1)} collective-permute-done((bf16[64,768]{1,0:T(8,128)(2,1)S(1)}, bf16[64,768]{1,0:T(8,128)(2,1)S(1)}, u32[]{:S(2)}, u32[]{:S(2)}) %collective-permute-start.2) | collective-permute-done | bytes 98336 | tf_op jit(solution)/shard_map/ppermute | solution.py:18
  15.9 2.0 %collective-permute-done.4.refs_6_ = bf16[136,768]{1,0:T(8,128)(2,1)S(1)} collective-permute-done((bf16[136,768]{1,0:T(8,128)(2,1)S(1)}, bf16[136,768]{1,0:T(8,128)(2,1)S(1)}, u32[]{:S(2)}, u32[]{:S(2)}) %collective-permute-start.4) | collective-permute-done | bytes 208928 | tf_op jit(solution)/shard_map/ppermute | solution.py:18
  18.3 1.6 %collective-permute-start.6 = (bf16[256,768]{1,0:T(8,128)(2,1)S(1)}, bf16[256,768]{1,0:T(8,128)(2,1)S(1)}, u32[]{:S(2)}, u32[]{:S(2)}) collective-permute-start(bf16[256,768]{1,0:T(8,128)(2,1)S(1)} %get-tuple-element.20.refs_1_.refs_2_), channel_id=1, source_target_pairs={{0,2},{1,3},{2,0},{3,1},{4,6},{5,7},{6,4},{7,5},{8,10},{9,11},{10,... | collective-permute-start | bytes 1179656 | tf_op jit(solution)/shard_map/ppermute | solution.py:18
  19.8 0.7 %collective-permute-start.7 = (bf16[256,768]{1,0:T(8,128)(2,1)S(1)}, bf16[256,768]{1,0:T(8,128)(2,1)S(1)}, u32[]{:S(2)}, u32[]{:S(2)}) collective-permute-start(bf16[256,768]{1,0:T(8,128)(2,1)S(1)} %get-tuple-element.20.refs_1_.refs_2_), channel_id=1, source_target_pairs={{0,4},{1,5},{2,6},{3,7},{4,0},{5,1},{6,2},{7,3},{8,12},{9,13},{10,... | collective-permute-start | bytes 1179656 | tf_op jit(solution)/shard_map/ppermute | solution.py:18
  20.5 0.8 %text_part.2.refs_3_ = f32[256,768]{1,0:T(8,128)S(1)} custom-call(f32[2,128]{1,0:T(2,128)S(1)} %concatenate.6.refs_8_.refs_0_, bf16[256,768]{1,0:T(8,128)(2,1)S(1)} %get-tuple-element.20.refs_1_.refs_2_, bf16[528,768]{1,0:T(8,128)(2,1)S(1)} %get-tuple-element.19.refs_2_.refs_1_), custom_call_target="tpu_custom_call" | custom-call | flops 402653184 | bytes 1991680 | tf_op jit(solution)/shard_map/text_part/pallas_call | solution.py:34
  21.3 0.8 %text_part.3 = (f32[64,768]{1,0:T(8,128)S(1)}, f32[64,768]{1,0:T(8,128)S(1)}, f32[64,384]{1,0:T(8,128)S(1)}, f32[64,384]{1,0:T(8,128)S(1)}, f32[64,384]{1,0:T(8,128)S(1)}, /*index=5*/f32[64,384]{1,0:T(8,128)S(1)}) custom-call(f32[2,128]{1,0:T(2,128)S(1)} %concatenate.6.refs_8_.refs_0_, bf16[256,768]{1,0:T(8,128)(2,1)S(1)} %get-tuple-element.20.refs_1_.refs_2_, ...), custom_call_target="tpu_custom_call" | custom-call | flops 402653184 | bytes 2778112 | tf_op jit(solution)/shard_map/text_part/pallas_call | solution.py:34
  22.1 1.6 %collective-permute-start.9 = (f32[64,384]{1,0:T(8,128)S(1)}, f32[64,384]{1,0:T(8,128)S(1)}, u32[]{:S(2)}, u32[]{:S(2)}) collective-permute-start(f32[64,384]{1,0:T(8,128)S(1)} %get-tuple-element.22), channel_id=1, source_target_pairs={{0,8},{8,0},{16,24},{24,16},{1,9},{9,1},{17,25},{25,17},{2,10},{10... | collective-permute-start | bytes 294920 | tf_op jit(solution)/shard_map/ppermute | solution.py:18
  23.7 0.4 %collective-permute-start.10 = (f32[64,384]{1,0:T(8,128)S(1)}, f32[64,384]{1,0:T(8,128)S(1)}, u32[]{:S(2)}, u32[]{:S(2)}) collective-permute-start(f32[64,384]{1,0:T(8,128)S(1)} %get-tuple-element.24), channel_id=1, source_target_pairs={{0,8},{8,0},{16,24},{24,16},{1,9},{9,1},{17,25},{25,17},{2,10},{10... | collective-permute-start | bytes 294920 | tf_op jit(solution)/shard_map/ppermute | solution.py:18
  24.2 1.6 %collective-permute-start.17 = (f32[64,768]{1,0:T(8,128)S(1)}, f32[64,768]{1,0:T(8,128)S(1)}, u32[]{:S(2)}, u32[]{:S(2)}) collective-permute-start(f32[64,768]{1,0:T(8,128)S(1)} %get-tuple-element.28), channel_id=1, source_target_pairs={{0,8},{8,0},{16,24},{24,16},{1,9},{9,1},{17,25},{25,17},{2,10},{10... | collective-permute-start | bytes 589832 | tf_op jit(solution)/shard_map/ppermute | solution.py:18
  25.8 1.8 %collective-permute-done.9.refs_1_ = f32[64,384]{1,0:T(8,128)S(1)} collective-permute-done((f32[64,384]{1,0:T(8,128)S(1)}, f32[64,384]{1,0:T(8,128)S(1)}, u32[]{:S(2)}, u32[]{:S(2)}) %collective-permute-start.9) | collective-permute-done | bytes 98336 | tf_op jit(solution)/shard_map/ppermute | solution.py:18
  27.6 0.8 %collective-permute-start.15 = (f32[64,384]{1,0:T(8,128)S(1)}, f32[64,384]{1,0:T(8,128)S(1)}, u32[]{:S(2)}, u32[]{:S(2)}) collective-permute-start(f32[64,384]{1,0:T(8,128)S(1)} %sum_near.2.refs_1_.refs_5_), channel_id=1, source_target_pairs={{0,16},{8,24},{16,0},{24,8},{1,17},{9,25},{17,1},{25,9},{2,18},{10... | collective-permute-start | bytes 294920 | tf_op jit(solution)/shard_map/ppermute | solution.py:18
  28.4 1.3 %collective-permute-done.6.refs_0_.refs_3_ = bf16[256,768]{1,0:T(8,128)(2,1)S(1)} collective-permute-done((bf16[256,768]{1,0:T(8,128)(2,1)S(1)}, bf16[256,768]{1,0:T(8,128)(2,1)S(1)}, u32[]{:S(2)}, u32[]{:S(2)}) %collective-permute-start.6) | collective-permute-done | bytes 393248 | tf_op jit(solution)/shard_map/ppermute | solution.py:18
  29.8 1.5 %collective-permute-start.12 = (bf16[128,768]{1,0:T(8,128)(2,1)S(1)}, bf16[128,768]{1,0:T(8,128)(2,1)S(1)}, u32[]{:S(2)}, u32[]{:S(2)}) collective-permute-start(bf16[128,768]{1,0:T(8,128)(2,1)S(1)} %cut.3.refs_3_), channel_id=1, source_target_pairs={{0,4},{1,5},{2,6},{3,7},{4,0},{5,1},{6,2},{7,3},{8,12},{9,13},{10,... | collective-permute-start | bytes 589832 | tf_op jit(solution)/shard_map/ppermute | solution.py:18
  31.3 0.9 %collective-permute-start.11 = (bf16[128,768]{1,0:T(8,128)(2,1)S(1)}, bf16[128,768]{1,0:T(8,128)(2,1)S(1)}, u32[]{:S(2)}, u32[]{:S(2)}) collective-permute-start(bf16[128,768]{1,0:T(8,128)(2,1)S(1)} %cut.2.refs_2_), channel_id=1, source_target_pairs={{0,2},{1,3},{2,0},{3,1},{4,6},{5,7},{6,4},{7,5},{8,10},{9,11},{10,... | collective-permute-start | bytes 589832 | tf_op jit(solution)/shard_map/ppermute | solution.py:18
  32.2 0.9 %collective-permute-start.16 = (f32[64,384]{1,0:T(8,128)S(1)}, f32[64,384]{1,0:T(8,128)S(1)}, u32[]{:S(2)}, u32[]{:S(2)}) collective-permute-start(f32[64,384]{1,0:T(8,128)S(1)} %sum_near.3.refs_6_), channel_id=1, source_target_pairs={{0,16},{8,24},{16,0},{24,8},{1,17},{9,25},{17,1},{25,9},{2,18},{10... | collective-permute-start | bytes 294920 | tf_op jit(solution)/shard_map/ppermute | solution.py:18
  33.1 1.0 %speech_part.4.refs_2_ = f32[128,768]{1,0:T(8,128)S(1)} custom-call(f32[2,128]{1,0:T(2,128)S(1)} %concatenate.6.refs_8_.refs_0_, bf16[528,768]{1,0:T(8,128)(2,1)S(1)} %get-tuple-element.19.refs_2_.refs_1_, bf16[256,768]{1,0:T(8,128)(2,1)S(1)} %get-tuple-element.20.refs_1_.refs_2_, bf16[256,768]{1,0:T(8,128)(2,1)S(1)} %collective-permute-done.6.refs_0_.refs_3_, ...), custom_call_target="tpu_custom_call" | custom-call | flops 3019898880 | bytes 2384896 | tf_op jit(solution)/shard_map/speech_part/pallas_call | solution.py:34
  34.1 1.0 %speech_part.6.refs_2_ = f32[128,768]{1,0:T(8,128)S(1)} custom-call(f32[2,128]{1,0:T(2,128)S(1)} %concatenate.6.refs_8_.refs_0_, bf16[528,768]{1,0:T(8,128)(2,1)S(1)} %collective-permute-done.8.refs_2_.refs_1_, bf16[256,768]{1,0:T(8,128)(2,1)S(1)} %get-tuple-element.20.refs_1_.refs_2_, bf16[256,768]{1,0:T(8,128)(2,1)S(1)} %collective-permute-done.6.refs_0_.refs_3_, ...), custom_call_target="tpu_custom_call" | custom-call | flops 3019898880 | bytes 2384896 | tf_op jit(solution)/shard_map/speech_part/pallas_call | solution.py:34
  35.1 1.2 %collective-permute-done.12.refs_4_ = bf16[128,768]{1,0:T(8,128)(2,1)S(1)} collective-permute-done((bf16[128,768]{1,0:T(8,128)(2,1)S(1)}, bf16[128,768]{1,0:T(8,128)(2,1)S(1)}, u32[]{:S(2)}, u32[]{:S(2)}) %collective-permute-start.12) | collective-permute-done | bytes 196640 | tf_op jit(solution)/shard_map/ppermute | solution.py:18
  36.3 1.2 %collective-permute-done.11.refs_3_ = bf16[128,768]{1,0:T(8,128)(2,1)S(1)} collective-permute-done((bf16[128,768]{1,0:T(8,128)(2,1)S(1)}, bf16[128,768]{1,0:T(8,128)(2,1)S(1)}, u32[]{:S(2)}, u32[]{:S(2)}) %collective-permute-start.11) | collective-permute-done | bytes 196640 | tf_op jit(solution)/shard_map/ppermute | solution.py:18
  37.6 0.5 %speech_part.7 = (f32[64,768]{1,0:T(8,128)S(1)}, f32[64,768]{1,0:T(8,128)S(1)}) custom-call(f32[2,128]{1,0:T(2,128)S(1)} %concatenate.6.refs_8_.refs_0_, bf16[528,768]{1,0:T(8,128)(2,1)S(1)} %collective-permute-done.8.refs_2_.refs_1_, f32[128,768]{1,0:T(8,128)S(1)} %speech_part.6.refs_2_, bf16[128,768]{1,0:T(8,128)(2,1)S(1)} %collective-permute-done.11.refs_3_, ...), custom_call_target="tpu_custom_call" | custom-call | flops 1006632960 | bytes 1991680 | tf_op jit(solution)/shard_map/speech_part/pallas_call | solution.py:34
  38.2 0.5 %collective-permute-start.14 = (f32[64,768]{1,0:T(8,128)S(1)}, f32[64,768]{1,0:T(8,128)S(1)}, u32[]{:S(2)}, u32[]{:S(2)}) collective-permute-start(f32[64,768]{1,0:T(8,128)S(1)} %get-tuple-element.26), channel_id=1, source_target_pairs={{0,1},{1,0},{2,3},{3,2},{4,5},{5,4},{6,7},{7,6},{8,9},{9,8},{10,11... | collective-permute-start | bytes 589832 | tf_op jit(solution)/shard_map/ppermute | solution.py:18
  38.7 0.5 %speech_part.5.refs_4_.home = f32[128,768]{1,0:T(8,128)S(1)} custom-call(f32[2,128]{1,0:T(2,128)S(1)} %concatenate.6.refs_8_.refs_0_, bf16[528,768]{1,0:T(8,128)(2,1)S(1)} %get-tuple-element.19.refs_2_.refs_1_, f32[128,768]{1,0:T(8,128)S(1)} %speech_part.4.refs_2_, bf16[128,768]{1,0:T(8,128)(2,1)S(1)} %collective-permute-done.11.refs_3_, ...), custom_call_target="tpu_custom_call" | custom-call | flops 1006632960 | bytes 1991680 | tf_op jit(solution)/shard_map/speech_part/pallas_call | solution.py:34
  39.2 0.5 %collective-permute-done.16.refs_1_ = f32[64,384]{1,0:T(8,128)S(1)} collective-permute-done((f32[64,384]{1,0:T(8,128)S(1)}, f32[64,384]{1,0:T(8,128)S(1)}, u32[]{:S(2)}, u32[]{:S(2)}) %collective-permute-start.16) | collective-permute-done | bytes 98336 | tf_op jit(solution)/shard_map/ppermute | solution.py:18
  39.9 1.1 %finish.1 = (f32[128,768]{1,0:T(8,128)}, f32[64,768]{1,0:T(8,128)}) custom-call(bf16[128,768]{1,0:T(8,128)(2,1)S(1)} %get-tuple-element.16.audio, f32[128,768]{1,0:T(8,128)S(1)} %speech_part.5.refs_4_.home, f32[64,768]{1,0:T(8,128)S(1)} %collective-permute-done.13.refs_0_, f32[64,768]{1,0:T(8,128)S(1)} %collective-permute-done.14.refs_1_, ...), custom_call_target="tpu_custom_call" | custom-call | tf_op jit(solution)/shard_map/finish/pallas_call | solution.py:359
  (21 shorter events, 0.7 us)
Async XLA Ops:
  1.8 9.2 %collective-permute-start.1 = (bf16[64,768]{1,0:T(8,128)(2,1)S(1)}, bf16[64,768]{1,0:T(8,128)(2,1)S(1)}, u32[]{:S(2)}, u32[]{:S(2)}) collective-permute-start(bf16[64,768]{1,0:T(8,128)(2,1)S(1)} %get-tuple-element.17.refs_0_), channel_id=1, source_target_pairs={{0,16},{8,24},{16,0},{24,8},{1,17},{9,25},{17,1},{25,9},{2,18},{10... | collective-permute-start | bytes 294920 | tf_op jit(solution)/shard_map/ppermute | solution.py:18
  5.9 10.0 %collective-permute-start.3 = (bf16[136,768]{1,0:T(8,128)(2,1)S(1)}, bf16[136,768]{1,0:T(8,128)(2,1)S(1)}, u32[]{:S(2)}, u32[]{:S(2)}) collective-permute-start(bf16[136,768]{1,0:T(8,128)(2,1)S(1)} %get-tuple-element.18.refs_4_), channel_id=1, source_target_pairs={{0,6},{1,7},{2,4},{3,5},{4,2},{5,3},{6,0},{7,1},{8,14},{9,15},{10,... | collective-permute-start | bytes 626696 | tf_op jit(solution)/shard_map/ppermute | solution.py:18
  8.4 9.6 %collective-permute-start.4 = (bf16[136,768]{1,0:T(8,128)(2,1)S(1)}, bf16[136,768]{1,0:T(8,128)(2,1)S(1)}, u32[]{:S(2)}, u32[]{:S(2)}) collective-permute-start(bf16[136,768]{1,0:T(8,128)(2,1)S(1)} %get-tuple-element.18.refs_4_), channel_id=1, source_target_pairs={{0,4},{1,5},{2,6},{3,7},{4,0},{5,1},{6,2},{7,3},{8,12},{9,13},{10,... | collective-permute-start | bytes 626696 | tf_op jit(solution)/shard_map/ppermute | solution.py:18
  8.9 9.1 %collective-permute-start.5 = (bf16[136,768]{1,0:T(8,128)(2,1)S(1)}, bf16[136,768]{1,0:T(8,128)(2,1)S(1)}, u32[]{:S(2)}, u32[]{:S(2)}) collective-permute-start(bf16[136,768]{1,0:T(8,128)(2,1)S(1)} %get-tuple-element.18.refs_4_), channel_id=1, source_target_pairs={{0,2},{1,3},{2,0},{3,1},{4,6},{5,7},{6,4},{7,5},{8,10},{9,11},{10,... | collective-permute-start | bytes 626696 | tf_op jit(solution)/shard_map/ppermute | solution.py:18
  9.4 5.5 %collective-permute-start = (bf16[64,768]{1,0:T(8,128)(2,1)S(1)}, bf16[64,768]{1,0:T(8,128)(2,1)S(1)}, u32[]{:S(2)}, u32[]{:S(2)}) collective-permute-start(bf16[64,768]{1,0:T(8,128)(2,1)S(1)} %get-tuple-element.17.refs_0_), channel_id=1, source_target_pairs={{0,8},{8,0},{16,24},{24,16},{1,9},{9,1},{17,25},{25,17},{2,10},{10... | collective-permute-start | bytes 294920 | tf_op jit(solution)/shard_map/ppermute | solution.py:18
  11.0 4.9 %collective-permute-start.2 = (bf16[64,768]{1,0:T(8,128)(2,1)S(1)}, bf16[64,768]{1,0:T(8,128)(2,1)S(1)}, u32[]{:S(2)}, u32[]{:S(2)}) collective-permute-start(bf16[64,768]{1,0:T(8,128)(2,1)S(1)} %pass_on.1.refs_2_), channel_id=1, source_target_pairs={{0,8},{8,0},{16,24},{24,16},{1,9},{9,1},{17,25},{25,17},{2,10},{10... | collective-permute-start | bytes 294920 | tf_op jit(solution)/shard_map/ppermute | solution.py:18
  18.2 3.1 %collective-permute-start.8 = (bf16[528,768]{1,0:T(8,128)(2,1)S(1)}, bf16[528,768]{1,0:T(8,128)(2,1)S(1)}, u32[]{:S(2)}, u32[]{:S(2)}) collective-permute-start(bf16[528,768]{1,0:T(8,128)(2,1)S(1)} %get-tuple-element.19.refs_2_.refs_1_), channel_id=1, source_target_pairs={{0,1},{1,0},{2,3},{3,2},{4,5},{5,4},{6,7},{7,6},{8,9},{9,8},{10,11... | collective-permute-start | bytes 2433032 | tf_op jit(solution)/shard_map/ppermute | solution.py:18
  18.3 11.5 %collective-permute-start.6 = (bf16[256,768]{1,0:T(8,128)(2,1)S(1)}, bf16[256,768]{1,0:T(8,128)(2,1)S(1)}, u32[]{:S(2)}, u32[]{:S(2)}) collective-permute-start(bf16[256,768]{1,0:T(8,128)(2,1)S(1)} %get-tuple-element.20.refs_1_.refs_2_), channel_id=1, source_target_pairs={{0,2},{1,3},{2,0},{3,1},{4,6},{5,7},{6,4},{7,5},{8,10},{9,11},{10,... | collective-permute-start | bytes 1179656 | tf_op jit(solution)/shard_map/ppermute | solution.py:18
  19.8 11.5 %collective-permute-start.7 = (bf16[256,768]{1,0:T(8,128)(2,1)S(1)}, bf16[256,768]{1,0:T(8,128)(2,1)S(1)}, u32[]{:S(2)}, u32[]{:S(2)}) collective-permute-start(bf16[256,768]{1,0:T(8,128)(2,1)S(1)} %get-tuple-element.20.refs_1_.refs_2_), channel_id=1, source_target_pairs={{0,4},{1,5},{2,6},{3,7},{4,0},{5,1},{6,2},{7,3},{8,12},{9,13},{10,... | collective-permute-start | bytes 1179656 | tf_op jit(solution)/shard_map/ppermute | solution.py:18
  22.1 5.5 %collective-permute-start.9 = (f32[64,384]{1,0:T(8,128)S(1)}, f32[64,384]{1,0:T(8,128)S(1)}, u32[]{:S(2)}, u32[]{:S(2)}) collective-permute-start(f32[64,384]{1,0:T(8,128)S(1)} %get-tuple-element.22), channel_id=1, source_target_pairs={{0,8},{8,0},{16,24},{24,16},{1,9},{9,1},{17,25},{25,17},{2,10},{10... | collective-permute-start | bytes 294920 | tf_op jit(solution)/shard_map/ppermute | solution.py:18
  23.7 8.4 %collective-permute-start.10 = (f32[64,384]{1,0:T(8,128)S(1)}, f32[64,384]{1,0:T(8,128)S(1)}, u32[]{:S(2)}, u32[]{:S(2)}) collective-permute-start(f32[64,384]{1,0:T(8,128)S(1)} %get-tuple-element.24), channel_id=1, source_target_pairs={{0,8},{8,0},{16,24},{24,16},{1,9},{9,1},{17,25},{25,17},{2,10},{10... | collective-permute-start | bytes 294920 | tf_op jit(solution)/shard_map/ppermute | solution.py:18
  24.2 15.0 %collective-permute-start.17 = (f32[64,768]{1,0:T(8,128)S(1)}, f32[64,768]{1,0:T(8,128)S(1)}, u32[]{:S(2)}, u32[]{:S(2)}) collective-permute-start(f32[64,768]{1,0:T(8,128)S(1)} %get-tuple-element.28), channel_id=1, source_target_pairs={{0,8},{8,0},{16,24},{24,16},{1,9},{9,1},{17,25},{25,17},{2,10},{10... | collective-permute-start | bytes 589832 | tf_op jit(solution)/shard_map/ppermute | solution.py:18
  27.6 12.0 %collective-permute-start.15 = (f32[64,384]{1,0:T(8,128)S(1)}, f32[64,384]{1,0:T(8,128)S(1)}, u32[]{:S(2)}, u32[]{:S(2)}) collective-permute-start(f32[64,384]{1,0:T(8,128)S(1)} %sum_near.2.refs_1_.refs_5_), channel_id=1, source_target_pairs={{0,16},{8,24},{16,0},{24,8},{1,17},{9,25},{17,1},{25,9},{2,18},{10... | collective-permute-start | bytes 294920 | tf_op jit(solution)/shard_map/ppermute | solution.py:18
  29.8 6.5 %collective-permute-start.12 = (bf16[128,768]{1,0:T(8,128)(2,1)S(1)}, bf16[128,768]{1,0:T(8,128)(2,1)S(1)}, u32[]{:S(2)}, u32[]{:S(2)}) collective-permute-start(bf16[128,768]{1,0:T(8,128)(2,1)S(1)} %cut.3.refs_3_), channel_id=1, source_target_pairs={{0,4},{1,5},{2,6},{3,7},{4,0},{5,1},{6,2},{7,3},{8,12},{9,13},{10,... | collective-permute-start | bytes 589832 | tf_op jit(solution)/shard_map/ppermute | solution.py:18
  31.3 6.3 %collective-permute-start.11 = (bf16[128,768]{1,0:T(8,128)(2,1)S(1)}, bf16[128,768]{1,0:T(8,128)(2,1)S(1)}, u32[]{:S(2)}, u32[]{:S(2)}) collective-permute-start(bf16[128,768]{1,0:T(8,128)(2,1)S(1)} %cut.2.refs_2_), channel_id=1, source_target_pairs={{0,2},{1,3},{2,0},{3,1},{4,6},{5,7},{6,4},{7,5},{8,10},{9,11},{10,... | collective-permute-start | bytes 589832 | tf_op jit(solution)/shard_map/ppermute | solution.py:18
  32.2 7.5 %collective-permute-start.16 = (f32[64,384]{1,0:T(8,128)S(1)}, f32[64,384]{1,0:T(8,128)S(1)}, u32[]{:S(2)}, u32[]{:S(2)}) collective-permute-start(f32[64,384]{1,0:T(8,128)S(1)} %sum_near.3.refs_6_), channel_id=1, source_target_pairs={{0,16},{8,24},{16,0},{24,8},{1,17},{9,25},{17,1},{25,9},{2,18},{10... | collective-permute-start | bytes 294920 | tf_op jit(solution)/shard_map/ppermute | solution.py:18
  38.1 1.6 %collective-permute-start.13 = (f32[64,768]{1,0:T(8,128)S(1)}, f32[64,768]{1,0:T(8,128)S(1)}, u32[]{:S(2)}, u32[]{:S(2)}) collective-permute-start(f32[64,768]{1,0:T(8,128)S(1)} %get-tuple-element.25), channel_id=1, source_target_pairs={{0,1},{1,0},{2,3},{3,2},{4,5},{5,4},{6,7},{7,6},{8,9},{9,8},{10,11... | collective-permute-start | bytes 589832 | tf_op jit(solution)/shard_map/ppermute | solution.py:18
  38.2 1.7 %collective-permute-start.14 = (f32[64,768]{1,0:T(8,128)S(1)}, f32[64,768]{1,0:T(8,128)S(1)}, u32[]{:S(2)}, u32[]{:S(2)}) collective-permute-start(f32[64,768]{1,0:T(8,128)S(1)} %get-tuple-element.26), channel_id=1, source_target_pairs={{0,1},{1,0},{2,3},{3,2},{4,5},{5,4},{6,7},{7,6},{8,9},{9,8},{10,11... | collective-permute-start | bytes 589832 | tf_op jit(solution)/shard_map/ppermute | solution.py:18

commit v20 on v19

--- a/solution.py
+++ b/solution.py
@@ -129,25 +129,25 @@
     return lax.dot_general(left, right, (((1,), (1,)), ((), ())), preferred_element_type=jnp.float32)
 
 
-def text_part_body(rows, own_text, has_start, chips, *refs):
+def text_part_body(rows, own_text, chips, *refs):
     sharp, shift = refs[0][0:1, 0:1], refs[0][1:2, 0:1]
-    text, speech = refs[1][...], refs[2]
-    total = refs[3][...] if has_start else None
-    outs = refs[4 if has_start else 3 :]
+    text, speeches, outs = refs[1][...], refs[2:4], refs[4:]
     groups = lax.axis_size("group")
     members = lax.axis_size("member")
     group = lax.axis_index("group")
     member = lax.axis_index("member")
-    table = speech[chips * rows :, :].astype(jnp.float32)
-    for first in range(0, chips * rows, CHUNK):
-        chunk = speech[first : min(first + CHUNK, chips * rows), :]
-        marks = marks_of(table, first // CHUNK, chunk.shape[0])
-        iota = lax.broadcasted_iota(jnp.int32, (own_text, chunk.shape[0]), 0)
-        ids = [((group ^ k) * members + member) * own_text + iota for k in range(groups)]
-        match = jnp.concatenate(ids, axis=0).astype(jnp.float32) == marks
-        coef = coefficients(dot_rows(text, chunk), match, sharp, shift)
-        part = jnp.dot(coef, chunk, preferred_element_type=jnp.float32)
-        total = part if total is None else total + part
+    total = None
+    for speech in speeches:
+        table = speech[chips * rows :, :].astype(jnp.float32)
+        for first in range(0, chips * rows, CHUNK):
+            chunk = speech[first : min(first + CHUNK, chips * rows), :]
+            marks = marks_of(table, first // CHUNK, chunk.shape[0])
+            iota = lax.broadcasted_iota(jnp.int32, (own_text, chunk.shape[0]), 0)
+            ids = [((group ^ k) * members + member) * own_text + iota for k in range(groups)]
+            match = jnp.concatenate(ids, axis=0).astype(jnp.float32) == marks
+            coef = coefficients(dot_rows(text, chunk), match, sharp, shift)
+            part = jnp.dot(coef, chunk, preferred_element_type=jnp.float32)
+            total = part if total is None else total + part
     row, at = 0, 0
     for out in outs:
         out[...] = total[row : row + out.shape[0], at : at + out.shape[1]]
@@ -205,9 +205,10 @@
 
 
 def project(values, back):
-    heading, norms = direction(values)
-    along = jnp.sum(heading * back, axis=-1, keepdims=True)
-    return (back - heading * along) / norms
+    floats = values.astype(jnp.float32)
+    along = jnp.sum(floats * back, axis=-1, keepdims=True)
+    square = jnp.sum(floats * floats, axis=-1, keepdims=True) + 1e-06
+    return (back - floats * (along / square)) * (1.0 / jnp.sqrt(square))
 
 
 def finish_body(pieces, audio, home, *refs):
@@ -296,16 +297,13 @@
 
     temporary = 4 * column * (6 * CHUNK + 3 * width)
 
-    def text_part(outs, speech, start):
-        body = functools.partial(text_part_body, rows, own_text, bool(start), chips)
-        work = 4 * column * chips * rows * width
-        return call(body, outs, [scalars, text, speech, *start], (), work, temporary, "text_part")
-
-    half = text_part([f32(column, width)], speech, [])
     sides = 2
     side = f32(own_text, width // sides)
     outs = [f32(own_text, width)] * (groups // 2) + [side] * (groups // 2 * sides)
-    parts = list(text_part(outs, other, half))
+    body = functools.partial(text_part_body, rows, own_text, chips)
+    work = 8 * column * chips * rows * width
+    operands = [scalars, text, speech, other]
+    parts = list(call(body, outs, operands, (), work, temporary, "text_part"))
     far = [parts[groups // 2 + i * sides :][:sides] for i in range(groups // 2)]
 
     text_far = []

time: 41.1 us -> 41.1 us (level)
    ppermute x18, waiting for transfers between devices: 11.4 us -> 11.8 us  [exchanged(): return lax.ppermute(value, axis, [(i, i ^ mask) for i in range(size)])]
    pallas_call x13 -> x12, Pallas kernels: 4.79 us -> 4.59 us  [call(): pl.pallas_call(whole, out_shape=out_shape, in_specs=specs, out_specs=jax....]
where the time goes in v20:
time: 41.1 us; the launch traced here: 40.9 us
  starting transfers between devices  20.2 us (49%)
  waiting for transfers between devices  11.8 us (29%)
  Pallas kernels  6.79 us (17%)
  between operations  2.05 us (5%)
    ppermute x18, starting transfers between devices, exchanged(): return lax.ppermute(value, axis, [(i, i ^ mask) for i in range(size)])  20.2 us
    ppermute x18, waiting for transfers between devices, exchanged(): return lax.ppermute(value, axis, [(i, i ^ mask) for i in range(size)])  11.8 us
    pallas_call x12, Pallas kernels, call(): pl.pallas_call(whole, out_shape=out_shape, in_specs=specs, out_specs=jax....  4.59 us
    pallas_call x1, Pallas kernels, shards(): pl.pallas_call(prepare_body, out_shape=[bf16(rows + MARK_ROWS, width), bf...  1.18 us
    pallas_call x1, Pallas kernels, shards(): pl.pallas_call(functools.partial(finish_body, len(back)), out_shape=resul...  1.02 us
  transfers between devices with their start and end apart: 18, of which 10 were waited for; matrix products, arithmetic and copies ran while one was open for 0% of the time, Pallas kernels for 11%

profile of v20, /device:TPU:0, one launch (start us, length us, event | category | flops | bytes accessed | tf_op | source)
XLA Modules:
  0.0 40.9 jit_solution(3936441170995907275)
XLA Ops:
  0.6 1.2 %unit_rows.1 = (bf16[136,768]{1,0:T(8,128)(2,1)S(1)}, bf16[64,768]{1,0:T(8,128)(2,1)S(1)}, bf16[128,768]{1,0:T(8,128)(2,1)S(1)}, bf16[64,768]{1,0:T(8,128)(2,1)S(1)}) custom-call(bf16[128,768]{1,0:T(8,128)(2,1)} %refs_0_.1, bf16[64,768]{1,0:T(8,128)(2,1)} %refs_1_.1, s32[1,128]{1,0:T(1,128)} %bitcast.3), custom_call_target="tpu_custom_call" | custom-call | tf_op jit(solution)/shard_map/unit_rows/pallas_call | solution.py:251
  1.8 4.1 %collective-permute-start.1 = (bf16[64,768]{1,0:T(8,128)(2,1)S(1)}, bf16[64,768]{1,0:T(8,128)(2,1)S(1)}, u32[]{:S(2)}, u32[]{:S(2)}) collective-permute-start(bf16[64,768]{1,0:T(8,128)(2,1)S(1)} %get-tuple-element.17.refs_0_), channel_id=1, source_target_pairs={{0,16},{8,24},{16,0},{24,8},{1,17},{9,25},{17,1},{25,9},{2,18},{10... | collective-permute-start | bytes 294920 | tf_op jit(solution)/shard_map/ppermute | solution.py:18
  5.9 2.4 %collective-permute-start.3 = (bf16[136,768]{1,0:T(8,128)(2,1)S(1)}, bf16[136,768]{1,0:T(8,128)(2,1)S(1)}, u32[]{:S(2)}, u32[]{:S(2)}) collective-permute-start(bf16[136,768]{1,0:T(8,128)(2,1)S(1)} %get-tuple-element.18.refs_4_), channel_id=1, source_target_pairs={{0,6},{1,7},{2,4},{3,5},{4,2},{5,3},{6,0},{7,1},{8,14},{9,15},{10,... | collective-permute-start | bytes 626696 | tf_op jit(solution)/shard_map/ppermute | solution.py:18
  8.4 0.5 %collective-permute-start.4 = (bf16[136,768]{1,0:T(8,128)(2,1)S(1)}, bf16[136,768]{1,0:T(8,128)(2,1)S(1)}, u32[]{:S(2)}, u32[]{:S(2)}) collective-permute-start(bf16[136,768]{1,0:T(8,128)(2,1)S(1)} %get-tuple-element.18.refs_4_), channel_id=1, source_target_pairs={{0,4},{1,5},{2,6},{3,7},{4,0},{5,1},{6,2},{7,3},{8,12},{9,13},{10,... | collective-permute-start | bytes 626696 | tf_op jit(solution)/shard_map/ppermute | solution.py:18
  8.9 0.5 %collective-permute-start.5 = (bf16[136,768]{1,0:T(8,128)(2,1)S(1)}, bf16[136,768]{1,0:T(8,128)(2,1)S(1)}, u32[]{:S(2)}, u32[]{:S(2)}) collective-permute-start(bf16[136,768]{1,0:T(8,128)(2,1)S(1)} %get-tuple-element.18.refs_4_), channel_id=1, source_target_pairs={{0,2},{1,3},{2,0},{3,1},{4,6},{5,7},{6,4},{7,5},{8,10},{9,11},{10,... | collective-permute-start | bytes 626696 | tf_op jit(solution)/shard_map/ppermute | solution.py:18
  9.4 1.6 %collective-permute-start = (bf16[64,768]{1,0:T(8,128)(2,1)S(1)}, bf16[64,768]{1,0:T(8,128)(2,1)S(1)}, u32[]{:S(2)}, u32[]{:S(2)}) collective-permute-start(bf16[64,768]{1,0:T(8,128)(2,1)S(1)} %get-tuple-element.17.refs_0_), channel_id=1, source_target_pairs={{0,8},{8,0},{16,24},{24,16},{1,9},{9,1},{17,25},{25,17},{2,10},{10... | collective-permute-start | bytes 294920 | tf_op jit(solution)/shard_map/ppermute | solution.py:18
  11.0 0.6 %collective-permute-start.2 = (bf16[64,768]{1,0:T(8,128)(2,1)S(1)}, bf16[64,768]{1,0:T(8,128)(2,1)S(1)}, u32[]{:S(2)}, u32[]{:S(2)}) collective-permute-start(bf16[64,768]{1,0:T(8,128)(2,1)S(1)} %pass_on.1.refs_2_), channel_id=1, source_target_pairs={{0,8},{8,0},{16,24},{24,16},{1,9},{9,1},{17,25},{25,17},{2,10},{10... | collective-permute-start | bytes 294920 | tf_op jit(solution)/shard_map/ppermute | solution.py:18
  12.9 1.9 %collective-permute-done.refs_1_ = bf16[64,768]{1,0:T(8,128)(2,1)S(1)} collective-permute-done((bf16[64,768]{1,0:T(8,128)(2,1)S(1)}, bf16[64,768]{1,0:T(8,128)(2,1)S(1)}, u32[]{:S(2)}, u32[]{:S(2)}) %collective-permute-start) | collective-permute-done | bytes 98336 | tf_op jit(solution)/shard_map/ppermute | solution.py:18
  14.9 1.1 %collective-permute-done.2.refs_3_ = bf16[64,768]{1,0:T(8,128)(2,1)S(1)} collective-permute-done((bf16[64,768]{1,0:T(8,128)(2,1)S(1)}, bf16[64,768]{1,0:T(8,128)(2,1)S(1)}, u32[]{:S(2)}, u32[]{:S(2)}) %collective-permute-start.2) | collective-permute-done | bytes 98336 | tf_op jit(solution)/shard_map/ppermute | solution.py:18
  15.9 2.0 %collective-permute-done.4.refs_6_ = bf16[136,768]{1,0:T(8,128)(2,1)S(1)} collective-permute-done((bf16[136,768]{1,0:T(8,128)(2,1)S(1)}, bf16[136,768]{1,0:T(8,128)(2,1)S(1)}, u32[]{:S(2)}, u32[]{:S(2)}) %collective-permute-start.4) | collective-permute-done | bytes 208928 | tf_op jit(solution)/shard_map/ppermute | solution.py:18
  18.3 1.6 %collective-permute-start.6 = (bf16[256,768]{1,0:T(8,128)(2,1)S(1)}, bf16[256,768]{1,0:T(8,128)(2,1)S(1)}, u32[]{:S(2)}, u32[]{:S(2)}) collective-permute-start(bf16[256,768]{1,0:T(8,128)(2,1)S(1)} %get-tuple-element.20.refs_1_.refs_2_), channel_id=1, source_target_pairs={{0,2},{1,3},{2,0},{3,1},{4,6},{5,7},{6,4},{7,5},{8,10},{9,11},{10,... | collective-permute-start | bytes 1179656 | tf_op jit(solution)/shard_map/ppermute | solution.py:18
  19.8 0.7 %collective-permute-start.7 = (bf16[256,768]{1,0:T(8,128)(2,1)S(1)}, bf16[256,768]{1,0:T(8,128)(2,1)S(1)}, u32[]{:S(2)}, u32[]{:S(2)}) collective-permute-start(bf16[256,768]{1,0:T(8,128)(2,1)S(1)} %get-tuple-element.20.refs_1_.refs_2_), channel_id=1, source_target_pairs={{0,4},{1,5},{2,6},{3,7},{4,0},{5,1},{6,2},{7,3},{8,12},{9,13},{10,... | collective-permute-start | bytes 1179656 | tf_op jit(solution)/shard_map/ppermute | solution.py:18
  20.6 1.3 %text_part.1 = (f32[64,768]{1,0:T(8,128)S(1)}, f32[64,768]{1,0:T(8,128)S(1)}, f32[64,384]{1,0:T(8,128)S(1)}, f32[64,384]{1,0:T(8,128)S(1)}, f32[64,384]{1,0:T(8,128)S(1)}, /*index=5*/f32[64,384]{1,0:T(8,128)S(1)}) custom-call(f32[2,128]{1,0:T(2,128)S(1)} %concatenate.6.refs_8_.refs_0_, bf16[256,768]{1,0:T(8,128)(2,1)S(1)} %get-tuple-element.20.refs_1_.refs_2_, ...), custom_call_target="tpu_custom_call" | custom-call | flops 805306368 | bytes 2802688 | tf_op jit(solution)/shard_map/text_part/pallas_call | solution.py:34
  21.9 1.6 %collective-permute-start.9 = (f32[64,384]{1,0:T(8,128)S(1)}, f32[64,384]{1,0:T(8,128)S(1)}, u32[]{:S(2)}, u32[]{:S(2)}) collective-permute-start(f32[64,384]{1,0:T(8,128)S(1)} %get-tuple-element.22), channel_id=1, source_target_pairs={{0,8},{8,0},{16,24},{24,16},{1,9},{9,1},{17,25},{25,17},{2,10},{10... | collective-permute-start | bytes 294920 | tf_op jit(solution)/shard_map/ppermute | solution.py:18
  23.6 0.4 %collective-permute-start.10 = (f32[64,384]{1,0:T(8,128)S(1)}, f32[64,384]{1,0:T(8,128)S(1)}, u32[]{:S(2)}, u32[]{:S(2)}) collective-permute-start(f32[64,384]{1,0:T(8,128)S(1)} %get-tuple-element.24), channel_id=1, source_target_pairs={{0,8},{8,0},{16,24},{24,16},{1,9},{9,1},{17,25},{25,17},{2,10},{10... | collective-permute-start | bytes 294920 | tf_op jit(solution)/shard_map/ppermute | solution.py:18
  24.0 1.6 %collective-permute-start.17 = (f32[64,768]{1,0:T(8,128)S(1)}, f32[64,768]{1,0:T(8,128)S(1)}, u32[]{:S(2)}, u32[]{:S(2)}) collective-permute-start(f32[64,768]{1,0:T(8,128)S(1)} %get-tuple-element.28), channel_id=1, source_target_pairs={{0,8},{8,0},{16,24},{24,16},{1,9},{9,1},{17,25},{25,17},{2,10},{10... | collective-permute-start | bytes 589832 | tf_op jit(solution)/shard_map/ppermute | solution.py:18
  25.6 2.0 %collective-permute-done.9.refs_1_ = f32[64,384]{1,0:T(8,128)S(1)} collective-permute-done((f32[64,384]{1,0:T(8,128)S(1)}, f32[64,384]{1,0:T(8,128)S(1)}, u32[]{:S(2)}, u32[]{:S(2)}) %collective-permute-start.9) | collective-permute-done | bytes 98336 | tf_op jit(solution)/shard_map/ppermute | solution.py:18
  27.6 0.6 %collective-permute-start.15 = (f32[64,384]{1,0:T(8,128)S(1)}, f32[64,384]{1,0:T(8,128)S(1)}, u32[]{:S(2)}, u32[]{:S(2)}) collective-permute-start(f32[64,384]{1,0:T(8,128)S(1)} %sum_near.2.refs_1_.refs_5_), channel_id=1, source_target_pairs={{0,16},{8,24},{16,0},{24,8},{1,17},{9,25},{17,1},{25,9},{2,18},{10... | collective-permute-start | bytes 294920 | tf_op jit(solution)/shard_map/ppermute | solution.py:18
  28.2 1.6 %collective-permute-done.6.refs_0_.refs_3_ = bf16[256,768]{1,0:T(8,128)(2,1)S(1)} collective-permute-done((bf16[256,768]{1,0:T(8,128)(2,1)S(1)}, bf16[256,768]{1,0:T(8,128)(2,1)S(1)}, u32[]{:S(2)}, u32[]{:S(2)}) %collective-permute-start.6) | collective-permute-done | bytes 393248 | tf_op jit(solution)/shard_map/ppermute | solution.py:18
  29.8 1.5 %collective-permute-start.12 = (bf16[128,768]{1,0:T(8,128)(2,1)S(1)}, bf16[128,768]{1,0:T(8,128)(2,1)S(1)}, u32[]{:S(2)}, u32[]{:S(2)}) collective-permute-start(bf16[128,768]{1,0:T(8,128)(2,1)S(1)} %cut.3.refs_3_), channel_id=1, source_target_pairs={{0,4},{1,5},{2,6},{3,7},{4,0},{5,1},{6,2},{7,3},{8,12},{9,13},{10,... | collective-permute-start | bytes 589832 | tf_op jit(solution)/shard_map/ppermute | solution.py:18
  31.3 0.9 %collective-permute-start.11 = (bf16[128,768]{1,0:T(8,128)(2,1)S(1)}, bf16[128,768]{1,0:T(8,128)(2,1)S(1)}, u32[]{:S(2)}, u32[]{:S(2)}) collective-permute-start(bf16[128,768]{1,0:T(8,128)(2,1)S(1)} %cut.2.refs_2_), channel_id=1, source_target_pairs={{0,2},{1,3},{2,0},{3,1},{4,6},{5,7},{6,4},{7,5},{8,10},{9,11},{10,... | collective-permute-start | bytes 589832 | tf_op jit(solution)/shard_map/ppermute | solution.py:18
  32.2 0.9 %collective-permute-start.16 = (f32[64,384]{1,0:T(8,128)S(1)}, f32[64,384]{1,0:T(8,128)S(1)}, u32[]{:S(2)}, u32[]{:S(2)}) collective-permute-start(f32[64,384]{1,0:T(8,128)S(1)} %sum_near.3.refs_6_), channel_id=1, source_target_pairs={{0,16},{8,24},{16,0},{24,8},{1,17},{9,25},{17,1},{25,9},{2,18},{10... | collective-permute-start | bytes 294920 | tf_op jit(solution)/shard_map/ppermute | solution.py:18
  33.1 1.0 %speech_part.4.refs_2_ = f32[128,768]{1,0:T(8,128)S(1)} custom-call(f32[2,128]{1,0:T(2,128)S(1)} %concatenate.6.refs_8_.refs_0_, bf16[528,768]{1,0:T(8,128)(2,1)S(1)} %get-tuple-element.19.refs_2_.refs_1_, bf16[256,768]{1,0:T(8,128)(2,1)S(1)} %get-tuple-element.20.refs_1_.refs_2_, bf16[256,768]{1,0:T(8,128)(2,1)S(1)} %collective-permute-done.6.refs_0_.refs_3_, ...), custom_call_target="tpu_custom_call" | custom-call | flops 3019898880 | bytes 2384896 | tf_op jit(solution)/shard_map/speech_part/pallas_call | solution.py:34
  34.1 1.0 %speech_part.6.refs_2_ = f32[128,768]{1,0:T(8,128)S(1)} custom-call(f32[2,128]{1,0:T(2,128)S(1)} %concatenate.6.refs_8_.refs_0_, bf16[528,768]{1,0:T(8,128)(2,1)S(1)} %collective-permute-done.8.refs_3_.refs_1_, bf16[256,768]{1,0:T(8,128)(2,1)S(1)} %get-tuple-element.20.refs_1_.refs_2_, bf16[256,768]{1,0:T(8,128)(2,1)S(1)} %collective-permute-done.6.refs_0_.refs_3_, ...), custom_call_target="tpu_custom_call" | custom-call | flops 3019898880 | bytes 2384896 | tf_op jit(solution)/shard_map/speech_part/pallas_call | solution.py:34
  35.2 1.2 %collective-permute-done.12.refs_4_ = bf16[128,768]{1,0:T(8,128)(2,1)S(1)} collective-permute-done((bf16[128,768]{1,0:T(8,128)(2,1)S(1)}, bf16[128,768]{1,0:T(8,128)(2,1)S(1)}, u32[]{:S(2)}, u32[]{:S(2)}) %collective-permute-start.12) | collective-permute-done | bytes 196640 | tf_op jit(solution)/shard_map/ppermute | solution.py:18
  36.3 1.2 %collective-permute-done.11.refs_3_ = bf16[128,768]{1,0:T(8,128)(2,1)S(1)} collective-permute-done((bf16[128,768]{1,0:T(8,128)(2,1)S(1)}, bf16[128,768]{1,0:T(8,128)(2,1)S(1)}, u32[]{:S(2)}, u32[]{:S(2)}) %collective-permute-start.11) | collective-permute-done | bytes 196640 | tf_op jit(solution)/shard_map/ppermute | solution.py:18
  37.6 0.5 %speech_part.7 = (f32[64,768]{1,0:T(8,128)S(1)}, f32[64,768]{1,0:T(8,128)S(1)}) custom-call(f32[2,128]{1,0:T(2,128)S(1)} %concatenate.6.refs_8_.refs_0_, bf16[528,768]{1,0:T(8,128)(2,1)S(1)} %collective-permute-done.8.refs_3_.refs_1_, f32[128,768]{1,0:T(8,128)S(1)} %speech_part.6.refs_2_, bf16[128,768]{1,0:T(8,128)(2,1)S(1)} %collective-permute-done.11.refs_3_, ...), custom_call_target="tpu_custom_call" | custom-call | flops 1006632960 | bytes 1991680 | tf_op jit(solution)/shard_map/speech_part/pallas_call | solution.py:34
  38.2 0.5 %collective-permute-start.14 = (f32[64,768]{1,0:T(8,128)S(1)}, f32[64,768]{1,0:T(8,128)S(1)}, u32[]{:S(2)}, u32[]{:S(2)}) collective-permute-start(f32[64,768]{1,0:T(8,128)S(1)} %get-tuple-element.26), channel_id=1, source_target_pairs={{0,1},{1,0},{2,3},{3,2},{4,5},{5,4},{6,7},{7,6},{8,9},{9,8},{10,11... | collective-permute-start | bytes 589832 | tf_op jit(solution)/shard_map/ppermute | solution.py:18
  38.7 0.5 %speech_part.5.refs_4_.home = f32[128,768]{1,0:T(8,128)S(1)} custom-call(f32[2,128]{1,0:T(2,128)S(1)} %concatenate.6.refs_8_.refs_0_, bf16[528,768]{1,0:T(8,128)(2,1)S(1)} %get-tuple-element.19.refs_2_.refs_1_, f32[128,768]{1,0:T(8,128)S(1)} %speech_part.4.refs_2_, bf16[128,768]{1,0:T(8,128)(2,1)S(1)} %collective-permute-done.11.refs_3_, ...), custom_call_target="tpu_custom_call" | custom-call | flops 1006632960 | bytes 1991680 | tf_op jit(solution)/shard_map/speech_part/pallas_call | solution.py:34
  39.2 0.3 collective-permute-done.16.refs_1_
  39.6 0.3 collective-permute-done.14.refs_1_
  39.9 1.0 %finish.1 = (f32[128,768]{1,0:T(8,128)}, f32[64,768]{1,0:T(8,128)}) custom-call(bf16[128,768]{1,0:T(8,128)(2,1)S(1)} %get-tuple-element.16.audio, f32[128,768]{1,0:T(8,128)S(1)} %speech_part.5.refs_4_.home, f32[64,768]{1,0:T(8,128)S(1)} %collective-permute-done.13.refs_0_, f32[64,768]{1,0:T(8,128)S(1)} %collective-permute-done.14.refs_1_, ...), custom_call_target="tpu_custom_call" | custom-call | tf_op jit(solution)/shard_map/finish/pallas_call | solution.py:357
  (20 shorter events, 0.6 us)
Async XLA Ops:
  1.8 9.2 %collective-permute-start.1 = (bf16[64,768]{1,0:T(8,128)(2,1)S(1)}, bf16[64,768]{1,0:T(8,128)(2,1)S(1)}, u32[]{:S(2)}, u32[]{:S(2)}) collective-permute-start(bf16[64,768]{1,0:T(8,128)(2,1)S(1)} %get-tuple-element.17.refs_0_), channel_id=1, source_target_pairs={{0,16},{8,24},{16,0},{24,8},{1,17},{9,25},{17,1},{25,9},{2,18},{10... | collective-permute-start | bytes 294920 | tf_op jit(solution)/shard_map/ppermute | solution.py:18
  5.9 10.0 %collective-permute-start.3 = (bf16[136,768]{1,0:T(8,128)(2,1)S(1)}, bf16[136,768]{1,0:T(8,128)(2,1)S(1)}, u32[]{:S(2)}, u32[]{:S(2)}) collective-permute-start(bf16[136,768]{1,0:T(8,128)(2,1)S(1)} %get-tuple-element.18.refs_4_), channel_id=1, source_target_pairs={{0,6},{1,7},{2,4},{3,5},{4,2},{5,3},{6,0},{7,1},{8,14},{9,15},{10,... | collective-permute-start | bytes 626696 | tf_op jit(solution)/shard_map/ppermute | solution.py:18
  8.4 9.6 %collective-permute-start.4 = (bf16[136,768]{1,0:T(8,128)(2,1)S(1)}, bf16[136,768]{1,0:T(8,128)(2,1)S(1)}, u32[]{:S(2)}, u32[]{:S(2)}) collective-permute-start(bf16[136,768]{1,0:T(8,128)(2,1)S(1)} %get-tuple-element.18.refs_4_), channel_id=1, source_target_pairs={{0,4},{1,5},{2,6},{3,7},{4,0},{5,1},{6,2},{7,3},{8,12},{9,13},{10,... | collective-permute-start | bytes 626696 | tf_op jit(solution)/shard_map/ppermute | solution.py:18
  8.9 9.1 %collective-permute-start.5 = (bf16[136,768]{1,0:T(8,128)(2,1)S(1)}, bf16[136,768]{1,0:T(8,128)(2,1)S(1)}, u32[]{:S(2)}, u32[]{:S(2)}) collective-permute-start(bf16[136,768]{1,0:T(8,128)(2,1)S(1)} %get-tuple-element.18.refs_4_), channel_id=1, source_target_pairs={{0,2},{1,3},{2,0},{3,1},{4,6},{5,7},{6,4},{7,5},{8,10},{9,11},{10,... | collective-permute-start | bytes 626696 | tf_op jit(solution)/shard_map/ppermute | solution.py:18
  9.4 5.5 %collective-permute-start = (bf16[64,768]{1,0:T(8,128)(2,1)S(1)}, bf16[64,768]{1,0:T(8,128)(2,1)S(1)}, u32[]{:S(2)}, u32[]{:S(2)}) collective-permute-start(bf16[64,768]{1,0:T(8,128)(2,1)S(1)} %get-tuple-element.17.refs_0_), channel_id=1, source_target_pairs={{0,8},{8,0},{16,24},{24,16},{1,9},{9,1},{17,25},{25,17},{2,10},{10... | collective-permute-start | bytes 294920 | tf_op jit(solution)/shard_map/ppermute | solution.py:18
  11.0 4.9 %collective-permute-start.2 = (bf16[64,768]{1,0:T(8,128)(2,1)S(1)}, bf16[64,768]{1,0:T(8,128)(2,1)S(1)}, u32[]{:S(2)}, u32[]{:S(2)}) collective-permute-start(bf16[64,768]{1,0:T(8,128)(2,1)S(1)} %pass_on.1.refs_2_), channel_id=1, source_target_pairs={{0,8},{8,0},{16,24},{24,16},{1,9},{9,1},{17,25},{25,17},{2,10},{10... | collective-permute-start | bytes 294920 | tf_op jit(solution)/shard_map/ppermute | solution.py:18
  18.2 2.4 %collective-permute-start.8 = (bf16[528,768]{1,0:T(8,128)(2,1)S(1)}, bf16[528,768]{1,0:T(8,128)(2,1)S(1)}, u32[]{:S(2)}, u32[]{:S(2)}) collective-permute-start(bf16[528,768]{1,0:T(8,128)(2,1)S(1)} %get-tuple-element.19.refs_2_.refs_1_), channel_id=1, source_target_pairs={{0,1},{1,0},{2,3},{3,2},{4,5},{5,4},{6,7},{7,6},{8,9},{9,8},{10,11... | collective-permute-start | bytes 2433032 | tf_op jit(solution)/shard_map/ppermute | solution.py:18
  18.3 11.5 %collective-permute-start.6 = (bf16[256,768]{1,0:T(8,128)(2,1)S(1)}, bf16[256,768]{1,0:T(8,128)(2,1)S(1)}, u32[]{:S(2)}, u32[]{:S(2)}) collective-permute-start(bf16[256,768]{1,0:T(8,128)(2,1)S(1)} %get-tuple-element.20.refs_1_.refs_2_), channel_id=1, source_target_pairs={{0,2},{1,3},{2,0},{3,1},{4,6},{5,7},{6,4},{7,5},{8,10},{9,11},{10,... | collective-permute-start | bytes 1179656 | tf_op jit(solution)/shard_map/ppermute | solution.py:18
  19.8 11.5 %collective-permute-start.7 = (bf16[256,768]{1,0:T(8,128)(2,1)S(1)}, bf16[256,768]{1,0:T(8,128)(2,1)S(1)}, u32[]{:S(2)}, u32[]{:S(2)}) collective-permute-start(bf16[256,768]{1,0:T(8,128)(2,1)S(1)} %get-tuple-element.20.refs_1_.refs_2_), channel_id=1, source_target_pairs={{0,4},{1,5},{2,6},{3,7},{4,0},{5,1},{6,2},{7,3},{8,12},{9,13},{10,... | collective-permute-start | bytes 1179656 | tf_op jit(solution)/shard_map/ppermute | solution.py:18
  21.9 5.7 %collective-permute-start.9 = (f32[64,384]{1,0:T(8,128)S(1)}, f32[64,384]{1,0:T(8,128)S(1)}, u32[]{:S(2)}, u32[]{:S(2)}) collective-permute-start(f32[64,384]{1,0:T(8,128)S(1)} %get-tuple-element.22), channel_id=1, source_target_pairs={{0,8},{8,0},{16,24},{24,16},{1,9},{9,1},{17,25},{25,17},{2,10},{10... | collective-permute-start | bytes 294920 | tf_op jit(solution)/shard_map/ppermute | solution.py:18
  23.6 8.6 %collective-permute-start.10 = (f32[64,384]{1,0:T(8,128)S(1)}, f32[64,384]{1,0:T(8,128)S(1)}, u32[]{:S(2)}, u32[]{:S(2)}) collective-permute-start(f32[64,384]{1,0:T(8,128)S(1)} %get-tuple-element.24), channel_id=1, source_target_pairs={{0,8},{8,0},{16,24},{24,16},{1,9},{9,1},{17,25},{25,17},{2,10},{10... | collective-permute-start | bytes 294920 | tf_op jit(solution)/shard_map/ppermute | solution.py:18
  24.0 15.2 %collective-permute-start.17 = (f32[64,768]{1,0:T(8,128)S(1)}, f32[64,768]{1,0:T(8,128)S(1)}, u32[]{:S(2)}, u32[]{:S(2)}) collective-permute-start(f32[64,768]{1,0:T(8,128)S(1)} %get-tuple-element.28), channel_id=1, source_target_pairs={{0,8},{8,0},{16,24},{24,16},{1,9},{9,1},{17,25},{25,17},{2,10},{10... | collective-permute-start | bytes 589832 | tf_op jit(solution)/shard_map/ppermute | solution.py:18
  27.6 11.9 %collective-permute-start.15 = (f32[64,384]{1,0:T(8,128)S(1)}, f32[64,384]{1,0:T(8,128)S(1)}, u32[]{:S(2)}, u32[]{:S(2)}) collective-permute-start(f32[64,384]{1,0:T(8,128)S(1)} %sum_near.2.refs_1_.refs_5_), channel_id=1, source_target_pairs={{0,16},{8,24},{16,0},{24,8},{1,17},{9,25},{17,1},{25,9},{2,18},{10... | collective-permute-start | bytes 294920 | tf_op jit(solution)/shard_map/ppermute | solution.py:18
  29.8 6.5 %collective-permute-start.12 = (bf16[128,768]{1,0:T(8,128)(2,1)S(1)}, bf16[128,768]{1,0:T(8,128)(2,1)S(1)}, u32[]{:S(2)}, u32[]{:S(2)}) collective-permute-start(bf16[128,768]{1,0:T(8,128)(2,1)S(1)} %cut.3.refs_3_), channel_id=1, source_target_pairs={{0,4},{1,5},{2,6},{3,7},{4,0},{5,1},{6,2},{7,3},{8,12},{9,13},{10,... | collective-permute-start | bytes 589832 | tf_op jit(solution)/shard_map/ppermute | solution.py:18
  31.3 6.3 %collective-permute-start.11 = (bf16[128,768]{1,0:T(8,128)(2,1)S(1)}, bf16[128,768]{1,0:T(8,128)(2,1)S(1)}, u32[]{:S(2)}, u32[]{:S(2)}) collective-permute-start(bf16[128,768]{1,0:T(8,128)(2,1)S(1)} %cut.2.refs_2_), channel_id=1, source_target_pairs={{0,2},{1,3},{2,0},{3,1},{4,6},{5,7},{6,4},{7,5},{8,10},{9,11},{10,... | collective-permute-start | bytes 589832 | tf_op jit(solution)/shard_map/ppermute | solution.py:18
  32.2 7.3 %collective-permute-start.16 = (f32[64,384]{1,0:T(8,128)S(1)}, f32[64,384]{1,0:T(8,128)S(1)}, u32[]{:S(2)}, u32[]{:S(2)}) collective-permute-start(f32[64,384]{1,0:T(8,128)S(1)} %sum_near.3.refs_6_), channel_id=1, source_target_pairs={{0,16},{8,24},{16,0},{24,8},{1,17},{9,25},{17,1},{25,9},{2,18},{10... | collective-permute-start | bytes 294920 | tf_op jit(solution)/shard_map/ppermute | solution.py:18
  38.1 1.5 %collective-permute-start.13 = (f32[64,768]{1,0:T(8,128)S(1)}, f32[64,768]{1,0:T(8,128)S(1)}, u32[]{:S(2)}, u32[]{:S(2)}) collective-permute-start(f32[64,768]{1,0:T(8,128)S(1)} %get-tuple-element.25), channel_id=1, source_target_pairs={{0,1},{1,0},{2,3},{3,2},{4,5},{5,4},{6,7},{7,6},{8,9},{9,8},{10,11... | collective-permute-start | bytes 589832 | tf_op jit(solution)/shard_map/ppermute | solution.py:18
  38.2 1.7 %collective-permute-start.14 = (f32[64,768]{1,0:T(8,128)S(1)}, f32[64,768]{1,0:T(8,128)S(1)}, u32[]{:S(2)}, u32[]{:S(2)}) collective-permute-start(f32[64,768]{1,0:T(8,128)S(1)} %get-tuple-element.26), channel_id=1, source_target_pairs={{0,1},{1,0},{2,3},{3,2},{4,5},{5,4},{6,7},{7,6},{8,9},{9,8},{10,11... | collective-permute-start | bytes 589832 | tf_op jit(solution)/shard_map/ppermute | solution.py:18

commit v21 on v20

--- a/solution.py
+++ b/solution.py
@@ -238,7 +238,7 @@
     own_text = sentence_vectors.shape[0]
     label = matching_indices.reshape(1, rows)
     scalars = jnp.concatenate(
-        [jnp.broadcast_to(v[:, None], (1, 128)) for v in (sharpness_array, offset_term)], axis=0
+        [v[:, None] for v in (sharpness_array, offset_term)], axis=0
     )
 
     def bf16(*shape):

time: 41.1 us -> 41 us (level)
  no operation moved by 1% of the time
where the time goes in v21:
time: 41 us; the launch traced here: 40.8 us
  starting transfers between devices  20.1 us (49%)
  waiting for transfers between devices  11.9 us (29%)
  Pallas kernels  6.79 us (17%)
  between operations  2.05 us (5%)
    ppermute x18, starting transfers between devices, exchanged(): return lax.ppermute(value, axis, [(i, i ^ mask) for i in range(size)])  20.1 us
    ppermute x18, waiting for transfers between devices, exchanged(): return lax.ppermute(value, axis, [(i, i ^ mask) for i in range(size)])  11.9 us
    pallas_call x12, Pallas kernels, call(): pl.pallas_call(whole, out_shape=out_shape, in_specs=specs, out_specs=jax....  4.59 us
    pallas_call x1, Pallas kernels, shards(): pl.pallas_call(prepare_body, out_shape=[bf16(rows + MARK_ROWS, width), bf...  1.18 us
    pallas_call x1, Pallas kernels, shards(): pl.pallas_call(functools.partial(finish_body, len(back)), out_shape=resul...  1.02 us
  transfers between devices with their start and end apart: 18, of which 10 were waited for; matrix products, arithmetic and copies ran while one was open for 0% of the time, Pallas kernels for 11%

profile of v21, /device:TPU:0, one launch (start us, length us, event | category | flops | bytes accessed | tf_op | source)
XLA Modules:
  0.0 40.8 jit_solution(1578168678710028058)
XLA Ops:
  0.6 1.2 %unit_rows.1 = (bf16[136,768]{1,0:T(8,128)(2,1)S(1)}, bf16[64,768]{1,0:T(8,128)(2,1)S(1)}, bf16[128,768]{1,0:T(8,128)(2,1)S(1)}, bf16[64,768]{1,0:T(8,128)(2,1)S(1)}) custom-call(bf16[128,768]{1,0:T(8,128)(2,1)} %refs_0_.1, bf16[64,768]{1,0:T(8,128)(2,1)} %refs_1_.1, s32[1,128]{1,0:T(1,128)} %bitcast.5), custom_call_target="tpu_custom_call" | custom-call | tf_op jit(solution)/shard_map/unit_rows/pallas_call | solution.py:251
  1.8 4.1 %collective-permute-start.1 = (bf16[64,768]{1,0:T(8,128)(2,1)S(1)}, bf16[64,768]{1,0:T(8,128)(2,1)S(1)}, u32[]{:S(2)}, u32[]{:S(2)}) collective-permute-start(bf16[64,768]{1,0:T(8,128)(2,1)S(1)} %get-tuple-element.17.refs_0_), channel_id=1, source_target_pairs={{0,16},{8,24},{16,0},{24,8},{1,17},{9,25},{17,1},{25,9},{2,18},{10... | collective-permute-start | bytes 294920 | tf_op jit(solution)/shard_map/ppermute | solution.py:18
  5.9 2.4 %collective-permute-start.3 = (bf16[136,768]{1,0:T(8,128)(2,1)S(1)}, bf16[136,768]{1,0:T(8,128)(2,1)S(1)}, u32[]{:S(2)}, u32[]{:S(2)}) collective-permute-start(bf16[136,768]{1,0:T(8,128)(2,1)S(1)} %get-tuple-element.18.refs_4_), channel_id=1, source_target_pairs={{0,6},{1,7},{2,4},{3,5},{4,2},{5,3},{6,0},{7,1},{8,14},{9,15},{10,... | collective-permute-start | bytes 626696 | tf_op jit(solution)/shard_map/ppermute | solution.py:18
  8.4 0.5 %collective-permute-start.4 = (bf16[136,768]{1,0:T(8,128)(2,1)S(1)}, bf16[136,768]{1,0:T(8,128)(2,1)S(1)}, u32[]{:S(2)}, u32[]{:S(2)}) collective-permute-start(bf16[136,768]{1,0:T(8,128)(2,1)S(1)} %get-tuple-element.18.refs_4_), channel_id=1, source_target_pairs={{0,4},{1,5},{2,6},{3,7},{4,0},{5,1},{6,2},{7,3},{8,12},{9,13},{10,... | collective-permute-start | bytes 626696 | tf_op jit(solution)/shard_map/ppermute | solution.py:18
  8.9 0.5 %collective-permute-start.5 = (bf16[136,768]{1,0:T(8,128)(2,1)S(1)}, bf16[136,768]{1,0:T(8,128)(2,1)S(1)}, u32[]{:S(2)}, u32[]{:S(2)}) collective-permute-start(bf16[136,768]{1,0:T(8,128)(2,1)S(1)} %get-tuple-element.18.refs_4_), channel_id=1, source_target_pairs={{0,2},{1,3},{2,0},{3,1},{4,6},{5,7},{6,4},{7,5},{8,10},{9,11},{10,... | collective-permute-start | bytes 626696 | tf_op jit(solution)/shard_map/ppermute | solution.py:18
  9.4 1.6 %collective-permute-start = (bf16[64,768]{1,0:T(8,128)(2,1)S(1)}, bf16[64,768]{1,0:T(8,128)(2,1)S(1)}, u32[]{:S(2)}, u32[]{:S(2)}) collective-permute-start(bf16[64,768]{1,0:T(8,128)(2,1)S(1)} %get-tuple-element.17.refs_0_), channel_id=1, source_target_pairs={{0,8},{8,0},{16,24},{24,16},{1,9},{9,1},{17,25},{25,17},{2,10},{10... | collective-permute-start | bytes 294920 | tf_op jit(solution)/shard_map/ppermute | solution.py:18
  12.3 0.5 %collective-permute-start.2 = (bf16[64,768]{1,0:T(8,128)(2,1)S(1)}, bf16[64,768]{1,0:T(8,128)(2,1)S(1)}, u32[]{:S(2)}, u32[]{:S(2)}) collective-permute-start(bf16[64,768]{1,0:T(8,128)(2,1)S(1)} %pass_on.1.refs_2_), channel_id=1, source_target_pairs={{0,8},{8,0},{16,24},{24,16},{1,9},{9,1},{17,25},{25,17},{2,10},{10... | collective-permute-start | bytes 294920 | tf_op jit(solution)/shard_map/ppermute | solution.py:18
  12.8 1.9 %collective-permute-done.refs_1_ = bf16[64,768]{1,0:T(8,128)(2,1)S(1)} collective-permute-done((bf16[64,768]{1,0:T(8,128)(2,1)S(1)}, bf16[64,768]{1,0:T(8,128)(2,1)S(1)}, u32[]{:S(2)}, u32[]{:S(2)}) %collective-permute-start) | collective-permute-done | bytes 98336 | tf_op jit(solution)/shard_map/ppermute | solution.py:18
  14.7 2.3 %collective-permute-done.2.refs_3_ = bf16[64,768]{1,0:T(8,128)(2,1)S(1)} collective-permute-done((bf16[64,768]{1,0:T(8,128)(2,1)S(1)}, bf16[64,768]{1,0:T(8,128)(2,1)S(1)}, u32[]{:S(2)}, u32[]{:S(2)}) %collective-permute-start.2) | collective-permute-done | bytes 98336 | tf_op jit(solution)/shard_map/ppermute | solution.py:18
  17.0 0.9 %collective-permute-done.4.refs_6_ = bf16[136,768]{1,0:T(8,128)(2,1)S(1)} collective-permute-done((bf16[136,768]{1,0:T(8,128)(2,1)S(1)}, bf16[136,768]{1,0:T(8,128)(2,1)S(1)}, u32[]{:S(2)}, u32[]{:S(2)}) %collective-permute-start.4) | collective-permute-done | bytes 208928 | tf_op jit(solution)/shard_map/ppermute | solution.py:18
  18.2 1.6 %collective-permute-start.6 = (bf16[256,768]{1,0:T(8,128)(2,1)S(1)}, bf16[256,768]{1,0:T(8,128)(2,1)S(1)}, u32[]{:S(2)}, u32[]{:S(2)}) collective-permute-start(bf16[256,768]{1,0:T(8,128)(2,1)S(1)} %get-tuple-element.20.refs_1_.refs_2_), channel_id=1, source_target_pairs={{0,2},{1,3},{2,0},{3,1},{4,6},{5,7},{6,4},{7,5},{8,10},{9,11},{10,... | collective-permute-start | bytes 1179656 | tf_op jit(solution)/shard_map/ppermute | solution.py:18
  19.7 0.7 %collective-permute-start.7 = (bf16[256,768]{1,0:T(8,128)(2,1)S(1)}, bf16[256,768]{1,0:T(8,128)(2,1)S(1)}, u32[]{:S(2)}, u32[]{:S(2)}) collective-permute-start(bf16[256,768]{1,0:T(8,128)(2,1)S(1)} %get-tuple-element.20.refs_1_.refs_2_), channel_id=1, source_target_pairs={{0,4},{1,5},{2,6},{3,7},{4,0},{5,1},{6,2},{7,3},{8,12},{9,13},{10,... | collective-permute-start | bytes 1179656 | tf_op jit(solution)/shard_map/ppermute | solution.py:18
  20.5 1.3 %text_part.1 = (f32[64,768]{1,0:T(8,128)S(1)}, f32[64,768]{1,0:T(8,128)S(1)}, f32[64,384]{1,0:T(8,128)S(1)}, f32[64,384]{1,0:T(8,128)S(1)}, f32[64,384]{1,0:T(8,128)S(1)}, /*index=5*/f32[64,384]{1,0:T(8,128)S(1)}) custom-call(f32[2,1]{1,0:T(2,128)S(1)} %pad_maximum_fusion.refs_8_.refs_0_, bf16[256,768]{1,0:T(8,128)(2,1)S(1)} %get-tuple-element.20.refs_1_.refs_2_, ...), custom_call_target="tpu_custom_call" | custom-call | flops 805306368 | bytes 2801672 | tf_op jit(solution)/shard_map/text_part/pallas_call | solution.py:34
  21.8 1.6 %collective-permute-start.9 = (f32[64,384]{1,0:T(8,128)S(1)}, f32[64,384]{1,0:T(8,128)S(1)}, u32[]{:S(2)}, u32[]{:S(2)}) collective-permute-start(f32[64,384]{1,0:T(8,128)S(1)} %get-tuple-element.22), channel_id=1, source_target_pairs={{0,8},{8,0},{16,24},{24,16},{1,9},{9,1},{17,25},{25,17},{2,10},{10... | collective-permute-start | bytes 294920 | tf_op jit(solution)/shard_map/ppermute | solution.py:18
  23.5 0.4 %collective-permute-start.10 = (f32[64,384]{1,0:T(8,128)S(1)}, f32[64,384]{1,0:T(8,128)S(1)}, u32[]{:S(2)}, u32[]{:S(2)}) collective-permute-start(f32[64,384]{1,0:T(8,128)S(1)} %get-tuple-element.24), channel_id=1, source_target_pairs={{0,8},{8,0},{16,24},{24,16},{1,9},{9,1},{17,25},{25,17},{2,10},{10... | collective-permute-start | bytes 294920 | tf_op jit(solution)/shard_map/ppermute | solution.py:18
  23.9 1.6 %collective-permute-start.17 = (f32[64,768]{1,0:T(8,128)S(1)}, f32[64,768]{1,0:T(8,128)S(1)}, u32[]{:S(2)}, u32[]{:S(2)}) collective-permute-start(f32[64,768]{1,0:T(8,128)S(1)} %get-tuple-element.28), channel_id=1, source_target_pairs={{0,8},{8,0},{16,24},{24,16},{1,9},{9,1},{17,25},{25,17},{2,10},{10... | collective-permute-start | bytes 589832 | tf_op jit(solution)/shard_map/ppermute | solution.py:18
  25.5 2.0 %collective-permute-done.9.refs_1_ = f32[64,384]{1,0:T(8,128)S(1)} collective-permute-done((f32[64,384]{1,0:T(8,128)S(1)}, f32[64,384]{1,0:T(8,128)S(1)}, u32[]{:S(2)}, u32[]{:S(2)}) %collective-permute-start.9) | collective-permute-done | bytes 98336 | tf_op jit(solution)/shard_map/ppermute | solution.py:18
  27.6 0.6 %collective-permute-start.15 = (f32[64,384]{1,0:T(8,128)S(1)}, f32[64,384]{1,0:T(8,128)S(1)}, u32[]{:S(2)}, u32[]{:S(2)}) collective-permute-start(f32[64,384]{1,0:T(8,128)S(1)} %sum_near.2.refs_1_.refs_5_), channel_id=1, source_target_pairs={{0,16},{8,24},{16,0},{24,8},{1,17},{9,25},{17,1},{25,9},{2,18},{10... | collective-permute-start | bytes 294920 | tf_op jit(solution)/shard_map/ppermute | solution.py:18
  28.2 1.6 %collective-permute-done.6.refs_0_.refs_3_ = bf16[256,768]{1,0:T(8,128)(2,1)S(1)} collective-permute-done((bf16[256,768]{1,0:T(8,128)(2,1)S(1)}, bf16[256,768]{1,0:T(8,128)(2,1)S(1)}, u32[]{:S(2)}, u32[]{:S(2)}) %collective-permute-start.6) | collective-permute-done | bytes 393248 | tf_op jit(solution)/shard_map/ppermute | solution.py:18
  29.7 1.5 %collective-permute-start.12 = (bf16[128,768]{1,0:T(8,128)(2,1)S(1)}, bf16[128,768]{1,0:T(8,128)(2,1)S(1)}, u32[]{:S(2)}, u32[]{:S(2)}) collective-permute-start(bf16[128,768]{1,0:T(8,128)(2,1)S(1)} %cut.3.refs_3_), channel_id=1, source_target_pairs={{0,4},{1,5},{2,6},{3,7},{4,0},{5,1},{6,2},{7,3},{8,12},{9,13},{10,... | collective-permute-start | bytes 589832 | tf_op jit(solution)/shard_map/ppermute | solution.py:18
  31.2 0.9 %collective-permute-start.11 = (bf16[128,768]{1,0:T(8,128)(2,1)S(1)}, bf16[128,768]{1,0:T(8,128)(2,1)S(1)}, u32[]{:S(2)}, u32[]{:S(2)}) collective-permute-start(bf16[128,768]{1,0:T(8,128)(2,1)S(1)} %cut.2.refs_2_), channel_id=1, source_target_pairs={{0,2},{1,3},{2,0},{3,1},{4,6},{5,7},{6,4},{7,5},{8,10},{9,11},{10,... | collective-permute-start | bytes 589832 | tf_op jit(solution)/shard_map/ppermute | solution.py:18
  32.1 0.9 %collective-permute-start.16 = (f32[64,384]{1,0:T(8,128)S(1)}, f32[64,384]{1,0:T(8,128)S(1)}, u32[]{:S(2)}, u32[]{:S(2)}) collective-permute-start(f32[64,384]{1,0:T(8,128)S(1)} %sum_near.3.refs_6_), channel_id=1, source_target_pairs={{0,16},{8,24},{16,0},{24,8},{1,17},{9,25},{17,1},{25,9},{2,18},{10... | collective-permute-start | bytes 294920 | tf_op jit(solution)/shard_map/ppermute | solution.py:18
  33.0 1.0 %speech_part.4.refs_2_ = f32[128,768]{1,0:T(8,128)S(1)} custom-call(f32[2,1]{1,0:T(2,128)S(1)} %pad_maximum_fusion.refs_8_.refs_0_, bf16[528,768]{1,0:T(8,128)(2,1)S(1)} %get-tuple-element.19.refs_2_.refs_1_, bf16[256,768]{1,0:T(8,128)(2,1)S(1)} %get-tuple-element.20.refs_1_.refs_2_, bf16[256,768]{1,0:T(8,128)(2,1)S(1)} %collective-permute-done.6.refs_0_.refs_3_, ...), custom_call_target="tpu_custom_call" | custom-call | flops 3019898880 | bytes 2383880 | tf_op jit(solution)/shard_map/speech_part/pallas_call | solution.py:34
  34.1 1.0 %speech_part.6.refs_2_ = f32[128,768]{1,0:T(8,128)S(1)} custom-call(f32[2,1]{1,0:T(2,128)S(1)} %pad_maximum_fusion.refs_8_.refs_0_, bf16[528,768]{1,0:T(8,128)(2,1)S(1)} %collective-permute-done.8.refs_3_.refs_1_, bf16[256,768]{1,0:T(8,128)(2,1)S(1)} %get-tuple-element.20.refs_1_.refs_2_, bf16[256,768]{1,0:T(8,128)(2,1)S(1)} %collective-permute-done.6.refs_0_.refs_3_, ...), custom_call_target="tpu_custom_call" | custom-call | flops 3019898880 | bytes 2383880 | tf_op jit(solution)/shard_map/speech_part/pallas_call | solution.py:34
  35.1 1.2 %collective-permute-done.12.refs_4_ = bf16[128,768]{1,0:T(8,128)(2,1)S(1)} collective-permute-done((bf16[128,768]{1,0:T(8,128)(2,1)S(1)}, bf16[128,768]{1,0:T(8,128)(2,1)S(1)}, u32[]{:S(2)}, u32[]{:S(2)}) %collective-permute-start.12) | collective-permute-done | bytes 196640 | tf_op jit(solution)/shard_map/ppermute | solution.py:18
  36.3 1.2 %collective-permute-done.11.refs_3_ = bf16[128,768]{1,0:T(8,128)(2,1)S(1)} collective-permute-done((bf16[128,768]{1,0:T(8,128)(2,1)S(1)}, bf16[128,768]{1,0:T(8,128)(2,1)S(1)}, u32[]{:S(2)}, u32[]{:S(2)}) %collective-permute-start.11) | collective-permute-done | bytes 196640 | tf_op jit(solution)/shard_map/ppermute | solution.py:18
  37.5 0.5 %speech_part.7 = (f32[64,768]{1,0:T(8,128)S(1)}, f32[64,768]{1,0:T(8,128)S(1)}) custom-call(f32[2,1]{1,0:T(2,128)S(1)} %pad_maximum_fusion.refs_8_.refs_0_, bf16[528,768]{1,0:T(8,128)(2,1)S(1)} %collective-permute-done.8.refs_3_.refs_1_, f32[128,768]{1,0:T(8,128)S(1)} %speech_part.6.refs_2_, bf16[128,768]{1,0:T(8,128)(2,1)S(1)} %collective-permute-done.11.refs_3_, ...), custom_call_target="tpu_custom_call" | custom-call | flops 1006632960 | bytes 1990664 | tf_op jit(solution)/shard_map/speech_part/pallas_call | solution.py:34
  38.1 0.5 %collective-permute-start.14 = (f32[64,768]{1,0:T(8,128)S(1)}, f32[64,768]{1,0:T(8,128)S(1)}, u32[]{:S(2)}, u32[]{:S(2)}) collective-permute-start(f32[64,768]{1,0:T(8,128)S(1)} %get-tuple-element.26), channel_id=1, source_target_pairs={{0,1},{1,0},{2,3},{3,2},{4,5},{5,4},{6,7},{7,6},{8,9},{9,8},{10,11... | collective-permute-start | bytes 589832 | tf_op jit(solution)/shard_map/ppermute | solution.py:18
  38.6 0.5 %speech_part.5.refs_4_.home = f32[128,768]{1,0:T(8,128)S(1)} custom-call(f32[2,1]{1,0:T(2,128)S(1)} %pad_maximum_fusion.refs_8_.refs_0_, bf16[528,768]{1,0:T(8,128)(2,1)S(1)} %get-tuple-element.19.refs_2_.refs_1_, f32[128,768]{1,0:T(8,128)S(1)} %speech_part.4.refs_2_, bf16[128,768]{1,0:T(8,128)(2,1)S(1)} %collective-permute-done.11.refs_3_, ...), custom_call_target="tpu_custom_call" | custom-call | flops 1006632960 | bytes 1990664 | tf_op jit(solution)/shard_map/speech_part/pallas_call | solution.py:34
  39.1 0.3 collective-permute-done.16.refs_1_
  39.5 0.3 collective-permute-done.14.refs_1_
  39.8 1.0 %finish.1 = (f32[128,768]{1,0:T(8,128)}, f32[64,768]{1,0:T(8,128)}) custom-call(bf16[128,768]{1,0:T(8,128)(2,1)S(1)} %get-tuple-element.16.audio, f32[128,768]{1,0:T(8,128)S(1)} %speech_part.5.refs_4_.home, f32[64,768]{1,0:T(8,128)S(1)} %collective-permute-done.13.refs_0_, f32[64,768]{1,0:T(8,128)S(1)} %collective-permute-done.14.refs_1_, ...), custom_call_target="tpu_custom_call" | custom-call | tf_op jit(solution)/shard_map/finish/pallas_call | solution.py:357
  (19 shorter events, 0.5 us)
Async XLA Ops:
  1.8 10.5 %collective-permute-start.1 = (bf16[64,768]{1,0:T(8,128)(2,1)S(1)}, bf16[64,768]{1,0:T(8,128)(2,1)S(1)}, u32[]{:S(2)}, u32[]{:S(2)}) collective-permute-start(bf16[64,768]{1,0:T(8,128)(2,1)S(1)} %get-tuple-element.17.refs_0_), channel_id=1, source_target_pairs={{0,16},{8,24},{16,0},{24,8},{1,17},{9,25},{17,1},{25,9},{2,18},{10... | collective-permute-start | bytes 294920 | tf_op jit(solution)/shard_map/ppermute | solution.py:18
  5.9 11.1 %collective-permute-start.3 = (bf16[136,768]{1,0:T(8,128)(2,1)S(1)}, bf16[136,768]{1,0:T(8,128)(2,1)S(1)}, u32[]{:S(2)}, u32[]{:S(2)}) collective-permute-start(bf16[136,768]{1,0:T(8,128)(2,1)S(1)} %get-tuple-element.18.refs_4_), channel_id=1, source_target_pairs={{0,6},{1,7},{2,4},{3,5},{4,2},{5,3},{6,0},{7,1},{8,14},{9,15},{10,... | collective-permute-start | bytes 626696 | tf_op jit(solution)/shard_map/ppermute | solution.py:18
  8.4 9.6 %collective-permute-start.4 = (bf16[136,768]{1,0:T(8,128)(2,1)S(1)}, bf16[136,768]{1,0:T(8,128)(2,1)S(1)}, u32[]{:S(2)}, u32[]{:S(2)}) collective-permute-start(bf16[136,768]{1,0:T(8,128)(2,1)S(1)} %get-tuple-element.18.refs_4_), channel_id=1, source_target_pairs={{0,4},{1,5},{2,6},{3,7},{4,0},{5,1},{6,2},{7,3},{8,12},{9,13},{10,... | collective-permute-start | bytes 626696 | tf_op jit(solution)/shard_map/ppermute | solution.py:18
  8.9 9.1 %collective-permute-start.5 = (bf16[136,768]{1,0:T(8,128)(2,1)S(1)}, bf16[136,768]{1,0:T(8,128)(2,1)S(1)}, u32[]{:S(2)}, u32[]{:S(2)}) collective-permute-start(bf16[136,768]{1,0:T(8,128)(2,1)S(1)} %get-tuple-element.18.refs_4_), channel_id=1, source_target_pairs={{0,2},{1,3},{2,0},{3,1},{4,6},{5,7},{6,4},{7,5},{8,10},{9,11},{10,... | collective-permute-start | bytes 626696 | tf_op jit(solution)/shard_map/ppermute | solution.py:18
  9.4 5.3 %collective-permute-start = (bf16[64,768]{1,0:T(8,128)(2,1)S(1)}, bf16[64,768]{1,0:T(8,128)(2,1)S(1)}, u32[]{:S(2)}, u32[]{:S(2)}) collective-permute-start(bf16[64,768]{1,0:T(8,128)(2,1)S(1)} %get-tuple-element.17.refs_0_), channel_id=1, source_target_pairs={{0,8},{8,0},{16,24},{24,16},{1,9},{9,1},{17,25},{25,17},{2,10},{10... | collective-permute-start | bytes 294920 | tf_op jit(solution)/shard_map/ppermute | solution.py:18
  12.3 4.7 %collective-permute-start.2 = (bf16[64,768]{1,0:T(8,128)(2,1)S(1)}, bf16[64,768]{1,0:T(8,128)(2,1)S(1)}, u32[]{:S(2)}, u32[]{:S(2)}) collective-permute-start(bf16[64,768]{1,0:T(8,128)(2,1)S(1)} %pass_on.1.refs_2_), channel_id=1, source_target_pairs={{0,8},{8,0},{16,24},{24,16},{1,9},{9,1},{17,25},{25,17},{2,10},{10... | collective-permute-start | bytes 294920 | tf_op jit(solution)/shard_map/ppermute | solution.py:18
  18.1 2.4 %collective-permute-start.8 = (bf16[528,768]{1,0:T(8,128)(2,1)S(1)}, bf16[528,768]{1,0:T(8,128)(2,1)S(1)}, u32[]{:S(2)}, u32[]{:S(2)}) collective-permute-start(bf16[528,768]{1,0:T(8,128)(2,1)S(1)} %get-tuple-element.19.refs_2_.refs_1_), channel_id=1, source_target_pairs={{0,1},{1,0},{2,3},{3,2},{4,5},{5,4},{6,7},{7,6},{8,9},{9,8},{10,11... | collective-permute-start | bytes 2433032 | tf_op jit(solution)/shard_map/ppermute | solution.py:18
  18.2 11.5 %collective-permute-start.6 = (bf16[256,768]{1,0:T(8,128)(2,1)S(1)}, bf16[256,768]{1,0:T(8,128)(2,1)S(1)}, u32[]{:S(2)}, u32[]{:S(2)}) collective-permute-start(bf16[256,768]{1,0:T(8,128)(2,1)S(1)} %get-tuple-element.20.refs_1_.refs_2_), channel_id=1, source_target_pairs={{0,2},{1,3},{2,0},{3,1},{4,6},{5,7},{6,4},{7,5},{8,10},{9,11},{10,... | collective-permute-start | bytes 1179656 | tf_op jit(solution)/shard_map/ppermute | solution.py:18
  19.7 11.5 %collective-permute-start.7 = (bf16[256,768]{1,0:T(8,128)(2,1)S(1)}, bf16[256,768]{1,0:T(8,128)(2,1)S(1)}, u32[]{:S(2)}, u32[]{:S(2)}) collective-permute-start(bf16[256,768]{1,0:T(8,128)(2,1)S(1)} %get-tuple-element.20.refs_1_.refs_2_), channel_id=1, source_target_pairs={{0,4},{1,5},{2,6},{3,7},{4,0},{5,1},{6,2},{7,3},{8,12},{9,13},{10,... | collective-permute-start | bytes 1179656 | tf_op jit(solution)/shard_map/ppermute | solution.py:18
  21.8 5.7 %collective-permute-start.9 = (f32[64,384]{1,0:T(8,128)S(1)}, f32[64,384]{1,0:T(8,128)S(1)}, u32[]{:S(2)}, u32[]{:S(2)}) collective-permute-start(f32[64,384]{1,0:T(8,128)S(1)} %get-tuple-element.22), channel_id=1, source_target_pairs={{0,8},{8,0},{16,24},{24,16},{1,9},{9,1},{17,25},{25,17},{2,10},{10... | collective-permute-start | bytes 294920 | tf_op jit(solution)/shard_map/ppermute | solution.py:18
  23.5 8.6 %collective-permute-start.10 = (f32[64,384]{1,0:T(8,128)S(1)}, f32[64,384]{1,0:T(8,128)S(1)}, u32[]{:S(2)}, u32[]{:S(2)}) collective-permute-start(f32[64,384]{1,0:T(8,128)S(1)} %get-tuple-element.24), channel_id=1, source_target_pairs={{0,8},{8,0},{16,24},{24,16},{1,9},{9,1},{17,25},{25,17},{2,10},{10... | collective-permute-start | bytes 294920 | tf_op jit(solution)/shard_map/ppermute | solution.py:18
  23.9 15.2 %collective-permute-start.17 = (f32[64,768]{1,0:T(8,128)S(1)}, f32[64,768]{1,0:T(8,128)S(1)}, u32[]{:S(2)}, u32[]{:S(2)}) collective-permute-start(f32[64,768]{1,0:T(8,128)S(1)} %get-tuple-element.28), channel_id=1, source_target_pairs={{0,8},{8,0},{16,24},{24,16},{1,9},{9,1},{17,25},{25,17},{2,10},{10... | collective-permute-start | bytes 589832 | tf_op jit(solution)/shard_map/ppermute | solution.py:18
  27.6 11.9 %collective-permute-start.15 = (f32[64,384]{1,0:T(8,128)S(1)}, f32[64,384]{1,0:T(8,128)S(1)}, u32[]{:S(2)}, u32[]{:S(2)}) collective-permute-start(f32[64,384]{1,0:T(8,128)S(1)} %sum_near.2.refs_1_.refs_5_), channel_id=1, source_target_pairs={{0,16},{8,24},{16,0},{24,8},{1,17},{9,25},{17,1},{25,9},{2,18},{10... | collective-permute-start | bytes 294920 | tf_op jit(solution)/shard_map/ppermute | solution.py:18
  29.7 6.5 %collective-permute-start.12 = (bf16[128,768]{1,0:T(8,128)(2,1)S(1)}, bf16[128,768]{1,0:T(8,128)(2,1)S(1)}, u32[]{:S(2)}, u32[]{:S(2)}) collective-permute-start(bf16[128,768]{1,0:T(8,128)(2,1)S(1)} %cut.3.refs_3_), channel_id=1, source_target_pairs={{0,4},{1,5},{2,6},{3,7},{4,0},{5,1},{6,2},{7,3},{8,12},{9,13},{10,... | collective-permute-start | bytes 589832 | tf_op jit(solution)/shard_map/ppermute | solution.py:18
  31.2 6.3 %collective-permute-start.11 = (bf16[128,768]{1,0:T(8,128)(2,1)S(1)}, bf16[128,768]{1,0:T(8,128)(2,1)S(1)}, u32[]{:S(2)}, u32[]{:S(2)}) collective-permute-start(bf16[128,768]{1,0:T(8,128)(2,1)S(1)} %cut.2.refs_2_), channel_id=1, source_target_pairs={{0,2},{1,3},{2,0},{3,1},{4,6},{5,7},{6,4},{7,5},{8,10},{9,11},{10,... | collective-permute-start | bytes 589832 | tf_op jit(solution)/shard_map/ppermute | solution.py:18
  32.1 7.3 %collective-permute-start.16 = (f32[64,384]{1,0:T(8,128)S(1)}, f32[64,384]{1,0:T(8,128)S(1)}, u32[]{:S(2)}, u32[]{:S(2)}) collective-permute-start(f32[64,384]{1,0:T(8,128)S(1)} %sum_near.3.refs_6_), channel_id=1, source_target_pairs={{0,16},{8,24},{16,0},{24,8},{1,17},{9,25},{17,1},{25,9},{2,18},{10... | collective-permute-start | bytes 294920 | tf_op jit(solution)/shard_map/ppermute | solution.py:18
  38.0 1.5 %collective-permute-start.13 = (f32[64,768]{1,0:T(8,128)S(1)}, f32[64,768]{1,0:T(8,128)S(1)}, u32[]{:S(2)}, u32[]{:S(2)}) collective-permute-start(f32[64,768]{1,0:T(8,128)S(1)} %get-tuple-element.25), channel_id=1, source_target_pairs={{0,1},{1,0},{2,3},{3,2},{4,5},{5,4},{6,7},{7,6},{8,9},{9,8},{10,11... | collective-permute-start | bytes 589832 | tf_op jit(solution)/shard_map/ppermute | solution.py:18
  38.1 1.7 %collective-permute-start.14 = (f32[64,768]{1,0:T(8,128)S(1)}, f32[64,768]{1,0:T(8,128)S(1)}, u32[]{:S(2)}, u32[]{:S(2)}) collective-permute-start(f32[64,768]{1,0:T(8,128)S(1)} %get-tuple-element.26), channel_id=1, source_target_pairs={{0,1},{1,0},{2,3},{3,2},{4,5},{5,4},{6,7},{7,6},{8,9},{9,8},{10,11... | collective-permute-start | bytes 589832 | tf_op jit(solution)/shard_map/ppermute | solution.py:18

commit v22 on v21

--- a/solution.py
+++ b/solution.py
@@ -156,26 +156,21 @@
             row, at = row + out.shape[0], 0
 
 
-def speech_part_body(rows, own_text, has_start, chips, masks, outputs, *refs):
+def speech_part_body(rows, own_text, has_start, chips, places, outputs, *refs):
     sharp, shift, speech = refs[0][0:1, 0:1], refs[0][1:2, 0:1], refs[1]
     total = refs[2][...] if has_start else None
-    texts, outs = list(refs[3 if has_start else 2 : -outputs]), refs[-outputs:]
-    groups = lax.axis_size("group")
+    texts, outs = refs[3 if has_start else 2 : -outputs], refs[-outputs:]
     members = lax.axis_size("member")
     group = lax.axis_index("group")
     member = lax.axis_index("member")
     table = speech[chips * rows :, :].astype(jnp.float32)
     marks = jnp.broadcast_to(marks_of(table, 0, rows), (rows, rows)).T[:, 0:1]
     block = speech[0:rows, :]
-    column = groups * own_text
-    lane = lax.broadcasted_iota(jnp.int32, (1, column), 1)
-    base = (group ^ (lane // own_text)) * members * own_text + lane % own_text
-    for mask in masks:
-        pieces = [texts.pop(0)[...]]
-        while sum(v.shape[0] for v in pieces) < column:
-            pieces.append(texts.pop(0)[...])
-        text = jnp.concatenate(pieces, axis=0)
-        ids = (base + (member ^ (2 * mask)) * own_text).astype(jnp.float32)
+    for (mask, first), ref in zip(places, texts):
+        text = ref[...]
+        lane = lax.broadcasted_iota(jnp.int32, (1, text.shape[0]), 1)
+        owner = (group ^ (first + lane // own_text)) * members + (member ^ (2 * mask))
+        ids = (owner * own_text + lane % own_text).astype(jnp.float32)
         coef = coefficients(dot_rows(block, text), marks == ids, sharp, shift)
         part = jnp.dot(coef, text, preferred_element_type=jnp.float32)
         total = part if total is None else total + part
@@ -326,21 +321,23 @@
     from_far = [exchanged(v, "group", groups // 2) for v in far[0]]
     from_near = [exchanged(parts[k], "group", k) for k in range(1, groups // 2)]
 
-    def speech_part(speech, start, columns, texts, after=(), pieces=1):
+    def speech_part(speech, start, places, texts, after=(), pieces=1):
         body = functools.partial(
-            speech_part_body, rows, own_text, bool(start), chips, columns, pieces
+            speech_part_body, rows, own_text, bool(start), chips, places, pieces
         )
-        work = 40 * rows * column * len(columns) * width
+        work = 40 * rows * sum(v.shape[0] for v in texts) * width
         outs = [f32(rows // pieces, width)] * pieces
         operands = [scalars, speech, *start, *texts]
         return call(body, outs, operands, after, work, temporary, "speech_part")
 
-    near = [[0, *masks], [text, *text_near], tuple(far[0])]
+    near = [[(k, 0) for k in (0, *masks)], [text, *text_near], tuple(far[0])]
     if square:
         away = speech_part(other, [], *near)
         home = speech_part(speech, [], *near)
-        away = speech_part(other, away, [3], text_far, pieces=2)
-        home = speech_part(speech, home, [3], text_far)
+        far_places = [(3, 0), (3, groups // 2)]
+        away = speech_part(other, away, far_places[1:], text_far[1:])
+        away = speech_part(other, away, far_places[:1], text_far[:1], pieces=2)
+        home = speech_part(speech, home, far_places, text_far)
     else:
         away = speech_part(other, [], *near, pieces=2)
         home = speech_part(speech, [], *near)

time: 41 us -> 40.9 us (level)
  waiting for transfers between devices: 11.9 us -> 11.2 us
  Pallas kernels: 6.79 us -> 7.39 us
    ppermute x18, waiting for transfers between devices: 11.9 us -> 11.2 us  [exchanged(): return lax.ppermute(value, axis, [(i, i ^ mask) for i in range(size)])]
    pallas_call x12 -> x13, Pallas kernels: 4.59 us -> 5.19 us  [call(): pl.pallas_call(whole, out_shape=out_shape, in_specs=specs, out_specs=jax....]
  transfers between devices with their start and end apart: 18 -> 18, of which waited for: 10 -> 10; matrix products, arithmetic and copies ran while one was open for 0% -> 0% of each run, Pallas kernels for 11% -> 13%
where the time goes in v22:
time: 40.9 us; the launch traced here: 40.8 us
  starting transfers between devices  20.1 us (49%)
  waiting for transfers between devices  11.2 us (27%)
  Pallas kernels  7.39 us (18%)
  between operations  2.06 us (5%)
    ppermute x18, starting transfers between devices, exchanged(): return lax.ppermute(value, axis, [(i, i ^ mask) for i in range(size)])  20.1 us
    ppermute x18, waiting for transfers between devices, exchanged(): return lax.ppermute(value, axis, [(i, i ^ mask) for i in range(size)])  11.2 us
    pallas_call x13, Pallas kernels, call(): pl.pallas_call(whole, out_shape=out_shape, in_specs=specs, out_specs=jax....  5.19 us
    pallas_call x1, Pallas kernels, shards(): pl.pallas_call(prepare_body, out_shape=[bf16(rows + MARK_ROWS, width), bf...  1.18 us
    pallas_call x1, Pallas kernels, shards(): pl.pallas_call(functools.partial(finish_body, len(back)), out_shape=resul...  1.02 us
  transfers between devices with their start and end apart: 18, of which 10 were waited for; matrix products, arithmetic and copies ran while one was open for 0% of the time, Pallas kernels for 13%

profile of v22, /device:TPU:0, one launch (start us, length us, event | category | flops | bytes accessed | tf_op | source)
XLA Modules:
  0.0 40.8 jit_solution(11487074241373837588)
XLA Ops:
  0.6 1.2 %unit_rows.1 = (bf16[136,768]{1,0:T(8,128)(2,1)S(1)}, bf16[64,768]{1,0:T(8,128)(2,1)S(1)}, bf16[128,768]{1,0:T(8,128)(2,1)S(1)}, bf16[64,768]{1,0:T(8,128)(2,1)S(1)}) custom-call(bf16[128,768]{1,0:T(8,128)(2,1)} %refs_0_.1, bf16[64,768]{1,0:T(8,128)(2,1)} %refs_1_.1, s32[1,128]{1,0:T(1,128)} %bitcast.5), custom_call_target="tpu_custom_call" | custom-call | tf_op jit(solution)/shard_map/unit_rows/pallas_call | solution.py:246
  1.8 4.1 %collective-permute-start.1 = (bf16[64,768]{1,0:T(8,128)(2,1)S(1)}, bf16[64,768]{1,0:T(8,128)(2,1)S(1)}, u32[]{:S(2)}, u32[]{:S(2)}) collective-permute-start(bf16[64,768]{1,0:T(8,128)(2,1)S(1)} %get-tuple-element.17.refs_0_), channel_id=1, source_target_pairs={{0,16},{8,24},{16,0},{24,8},{1,17},{9,25},{17,1},{25,9},{2,18},{10... | collective-permute-start | bytes 294920 | tf_op jit(solution)/shard_map/ppermute | solution.py:18
  5.9 2.4 %collective-permute-start.3 = (bf16[136,768]{1,0:T(8,128)(2,1)S(1)}, bf16[136,768]{1,0:T(8,128)(2,1)S(1)}, u32[]{:S(2)}, u32[]{:S(2)}) collective-permute-start(bf16[136,768]{1,0:T(8,128)(2,1)S(1)} %get-tuple-element.18.refs_4_), channel_id=1, source_target_pairs={{0,6},{1,7},{2,4},{3,5},{4,2},{5,3},{6,0},{7,1},{8,14},{9,15},{10,... | collective-permute-start | bytes 626696 | tf_op jit(solution)/shard_map/ppermute | solution.py:18
  8.4 0.5 %collective-permute-start.4 = (bf16[136,768]{1,0:T(8,128)(2,1)S(1)}, bf16[136,768]{1,0:T(8,128)(2,1)S(1)}, u32[]{:S(2)}, u32[]{:S(2)}) collective-permute-start(bf16[136,768]{1,0:T(8,128)(2,1)S(1)} %get-tuple-element.18.refs_4_), channel_id=1, source_target_pairs={{0,4},{1,5},{2,6},{3,7},{4,0},{5,1},{6,2},{7,3},{8,12},{9,13},{10,... | collective-permute-start | bytes 626696 | tf_op jit(solution)/shard_map/ppermute | solution.py:18
  8.9 0.5 %collective-permute-start.5 = (bf16[136,768]{1,0:T(8,128)(2,1)S(1)}, bf16[136,768]{1,0:T(8,128)(2,1)S(1)}, u32[]{:S(2)}, u32[]{:S(2)}) collective-permute-start(bf16[136,768]{1,0:T(8,128)(2,1)S(1)} %get-tuple-element.18.refs_4_), channel_id=1, source_target_pairs={{0,2},{1,3},{2,0},{3,1},{4,6},{5,7},{6,4},{7,5},{8,10},{9,11},{10,... | collective-permute-start | bytes 626696 | tf_op jit(solution)/shard_map/ppermute | solution.py:18
  9.4 1.6 %collective-permute-start = (bf16[64,768]{1,0:T(8,128)(2,1)S(1)}, bf16[64,768]{1,0:T(8,128)(2,1)S(1)}, u32[]{:S(2)}, u32[]{:S(2)}) collective-permute-start(bf16[64,768]{1,0:T(8,128)(2,1)S(1)} %get-tuple-element.17.refs_0_), channel_id=1, source_target_pairs={{0,8},{8,0},{16,24},{24,16},{1,9},{9,1},{17,25},{25,17},{2,10},{10... | collective-permute-start | bytes 294920 | tf_op jit(solution)/shard_map/ppermute | solution.py:18
  12.3 0.5 %collective-permute-start.2 = (bf16[64,768]{1,0:T(8,128)(2,1)S(1)}, bf16[64,768]{1,0:T(8,128)(2,1)S(1)}, u32[]{:S(2)}, u32[]{:S(2)}) collective-permute-start(bf16[64,768]{1,0:T(8,128)(2,1)S(1)} %pass_on.1.refs_2_), channel_id=1, source_target_pairs={{0,8},{8,0},{16,24},{24,16},{1,9},{9,1},{17,25},{25,17},{2,10},{10... | collective-permute-start | bytes 294920 | tf_op jit(solution)/shard_map/ppermute | solution.py:18
  12.8 1.9 %collective-permute-done.refs_1_ = bf16[64,768]{1,0:T(8,128)(2,1)S(1)} collective-permute-done((bf16[64,768]{1,0:T(8,128)(2,1)S(1)}, bf16[64,768]{1,0:T(8,128)(2,1)S(1)}, u32[]{:S(2)}, u32[]{:S(2)}) %collective-permute-start) | collective-permute-done | bytes 98336 | tf_op jit(solution)/shard_map/ppermute | solution.py:18
  14.7 2.3 %collective-permute-done.2.refs_3_ = bf16[64,768]{1,0:T(8,128)(2,1)S(1)} collective-permute-done((bf16[64,768]{1,0:T(8,128)(2,1)S(1)}, bf16[64,768]{1,0:T(8,128)(2,1)S(1)}, u32[]{:S(2)}, u32[]{:S(2)}) %collective-permute-start.2) | collective-permute-done | bytes 98336 | tf_op jit(solution)/shard_map/ppermute | solution.py:18
  17.0 0.9 %collective-permute-done.4.refs_6_ = bf16[136,768]{1,0:T(8,128)(2,1)S(1)} collective-permute-done((bf16[136,768]{1,0:T(8,128)(2,1)S(1)}, bf16[136,768]{1,0:T(8,128)(2,1)S(1)}, u32[]{:S(2)}, u32[]{:S(2)}) %collective-permute-start.4) | collective-permute-done | bytes 208928 | tf_op jit(solution)/shard_map/ppermute | solution.py:18
  18.2 1.6 %collective-permute-start.6 = (bf16[256,768]{1,0:T(8,128)(2,1)S(1)}, bf16[256,768]{1,0:T(8,128)(2,1)S(1)}, u32[]{:S(2)}, u32[]{:S(2)}) collective-permute-start(bf16[256,768]{1,0:T(8,128)(2,1)S(1)} %get-tuple-element.20.refs_1_.refs_2_), channel_id=1, source_target_pairs={{0,2},{1,3},{2,0},{3,1},{4,6},{5,7},{6,4},{7,5},{8,10},{9,11},{10,... | collective-permute-start | bytes 1179656 | tf_op jit(solution)/shard_map/ppermute | solution.py:18
  19.7 0.7 %collective-permute-start.7 = (bf16[256,768]{1,0:T(8,128)(2,1)S(1)}, bf16[256,768]{1,0:T(8,128)(2,1)S(1)}, u32[]{:S(2)}, u32[]{:S(2)}) collective-permute-start(bf16[256,768]{1,0:T(8,128)(2,1)S(1)} %get-tuple-element.20.refs_1_.refs_2_), channel_id=1, source_target_pairs={{0,4},{1,5},{2,6},{3,7},{4,0},{5,1},{6,2},{7,3},{8,12},{9,13},{10,... | collective-permute-start | bytes 1179656 | tf_op jit(solution)/shard_map/ppermute | solution.py:18
  20.5 1.3 %text_part.1 = (f32[64,768]{1,0:T(8,128)S(1)}, f32[64,768]{1,0:T(8,128)S(1)}, f32[64,384]{1,0:T(8,128)S(1)}, f32[64,384]{1,0:T(8,128)S(1)}, f32[64,384]{1,0:T(8,128)S(1)}, /*index=5*/f32[64,384]{1,0:T(8,128)S(1)}) custom-call(f32[2,1]{1,0:T(2,128)S(1)} %pad_maximum_fusion.refs_8_.refs_0_, bf16[256,768]{1,0:T(8,128)(2,1)S(1)} %get-tuple-element.20.refs_1_.refs_2_, ...), custom_call_target="tpu_custom_call" | custom-call | flops 805306368 | bytes 2801672 | tf_op jit(solution)/shard_map/text_part/pallas_call | solution.py:34
  21.8 1.6 %collective-permute-start.9 = (f32[64,384]{1,0:T(8,128)S(1)}, f32[64,384]{1,0:T(8,128)S(1)}, u32[]{:S(2)}, u32[]{:S(2)}) collective-permute-start(f32[64,384]{1,0:T(8,128)S(1)} %get-tuple-element.22), channel_id=1, source_target_pairs={{0,8},{8,0},{16,24},{24,16},{1,9},{9,1},{17,25},{25,17},{2,10},{10... | collective-permute-start | bytes 294920 | tf_op jit(solution)/shard_map/ppermute | solution.py:18
  23.5 0.4 %collective-permute-start.10 = (f32[64,384]{1,0:T(8,128)S(1)}, f32[64,384]{1,0:T(8,128)S(1)}, u32[]{:S(2)}, u32[]{:S(2)}) collective-permute-start(f32[64,384]{1,0:T(8,128)S(1)} %get-tuple-element.24), channel_id=1, source_target_pairs={{0,8},{8,0},{16,24},{24,16},{1,9},{9,1},{17,25},{25,17},{2,10},{10... | collective-permute-start | bytes 294920 | tf_op jit(solution)/shard_map/ppermute | solution.py:18
  23.9 1.6 %collective-permute-start.17 = (f32[64,768]{1,0:T(8,128)S(1)}, f32[64,768]{1,0:T(8,128)S(1)}, u32[]{:S(2)}, u32[]{:S(2)}) collective-permute-start(f32[64,768]{1,0:T(8,128)S(1)} %get-tuple-element.28), channel_id=1, source_target_pairs={{0,8},{8,0},{16,24},{24,16},{1,9},{9,1},{17,25},{25,17},{2,10},{10... | collective-permute-start | bytes 589832 | tf_op jit(solution)/shard_map/ppermute | solution.py:18
  25.5 2.0 %collective-permute-done.9.refs_1_ = f32[64,384]{1,0:T(8,128)S(1)} collective-permute-done((f32[64,384]{1,0:T(8,128)S(1)}, f32[64,384]{1,0:T(8,128)S(1)}, u32[]{:S(2)}, u32[]{:S(2)}) %collective-permute-start.9) | collective-permute-done | bytes 98336 | tf_op jit(solution)/shard_map/ppermute | solution.py:18
  27.6 0.6 %collective-permute-start.15 = (f32[64,384]{1,0:T(8,128)S(1)}, f32[64,384]{1,0:T(8,128)S(1)}, u32[]{:S(2)}, u32[]{:S(2)}) collective-permute-start(f32[64,384]{1,0:T(8,128)S(1)} %sum_near.2.refs_1_.refs_5_), channel_id=1, source_target_pairs={{0,16},{8,24},{16,0},{24,8},{1,17},{9,25},{17,1},{25,9},{2,18},{10... | collective-permute-start | bytes 294920 | tf_op jit(solution)/shard_map/ppermute | solution.py:18
  28.2 1.6 %collective-permute-done.6.refs_0_.refs_3_ = bf16[256,768]{1,0:T(8,128)(2,1)S(1)} collective-permute-done((bf16[256,768]{1,0:T(8,128)(2,1)S(1)}, bf16[256,768]{1,0:T(8,128)(2,1)S(1)}, u32[]{:S(2)}, u32[]{:S(2)}) %collective-permute-start.6) | collective-permute-done | bytes 393248 | tf_op jit(solution)/shard_map/ppermute | solution.py:18
  29.7 1.5 %collective-permute-start.12 = (bf16[128,768]{1,0:T(8,128)(2,1)S(1)}, bf16[128,768]{1,0:T(8,128)(2,1)S(1)}, u32[]{:S(2)}, u32[]{:S(2)}) collective-permute-start(bf16[128,768]{1,0:T(8,128)(2,1)S(1)} %cut.3.refs_3_), channel_id=1, source_target_pairs={{0,4},{1,5},{2,6},{3,7},{4,0},{5,1},{6,2},{7,3},{8,12},{9,13},{10,... | collective-permute-start | bytes 589832 | tf_op jit(solution)/shard_map/ppermute | solution.py:18
  31.2 0.9 %collective-permute-start.11 = (bf16[128,768]{1,0:T(8,128)(2,1)S(1)}, bf16[128,768]{1,0:T(8,128)(2,1)S(1)}, u32[]{:S(2)}, u32[]{:S(2)}) collective-permute-start(bf16[128,768]{1,0:T(8,128)(2,1)S(1)} %cut.2.refs_2_), channel_id=1, source_target_pairs={{0,2},{1,3},{2,0},{3,1},{4,6},{5,7},{6,4},{7,5},{8,10},{9,11},{10,... | collective-permute-start | bytes 589832 | tf_op jit(solution)/shard_map/ppermute | solution.py:18
  32.1 0.9 %collective-permute-start.16 = (f32[64,384]{1,0:T(8,128)S(1)}, f32[64,384]{1,0:T(8,128)S(1)}, u32[]{:S(2)}, u32[]{:S(2)}) collective-permute-start(f32[64,384]{1,0:T(8,128)S(1)} %sum_near.3.refs_6_), channel_id=1, source_target_pairs={{0,16},{8,24},{16,0},{24,8},{1,17},{9,25},{17,1},{25,9},{2,18},{10... | collective-permute-start | bytes 294920 | tf_op jit(solution)/shard_map/ppermute | solution.py:18
  33.0 1.0 %speech_part.5.refs_2_ = f32[128,768]{1,0:T(8,128)S(1)} custom-call(f32[2,1]{1,0:T(2,128)S(1)} %pad_maximum_fusion.refs_8_.refs_0_, bf16[528,768]{1,0:T(8,128)(2,1)S(1)} %get-tuple-element.19.refs_2_.refs_1_, bf16[256,768]{1,0:T(8,128)(2,1)S(1)} %get-tuple-element.20.refs_1_.refs_2_, bf16[256,768]{1,0:T(8,128)(2,1)S(1)} %collective-permute-done.6.refs_0_.refs_3_, ...), custom_call_target="tpu_custom_call" | custom-call | flops 3019898880 | bytes 2383880 | tf_op jit(solution)/shard_map/speech_part/pallas_call | solution.py:34
  34.1 1.0 %speech_part.7.refs_2_ = f32[128,768]{1,0:T(8,128)S(1)} custom-call(f32[2,1]{1,0:T(2,128)S(1)} %pad_maximum_fusion.refs_8_.refs_0_, bf16[528,768]{1,0:T(8,128)(2,1)S(1)} %collective-permute-done.8.refs_3_.refs_1_, bf16[256,768]{1,0:T(8,128)(2,1)S(1)} %get-tuple-element.20.refs_1_.refs_2_, bf16[256,768]{1,0:T(8,128)(2,1)S(1)} %collective-permute-done.6.refs_0_.refs_3_, ...), custom_call_target="tpu_custom_call" | custom-call | flops 3019898880 | bytes 2383880 | tf_op jit(solution)/shard_map/speech_part/pallas_call | solution.py:34
  35.1 1.2 %collective-permute-done.12.refs_4_.refs_3_ = bf16[128,768]{1,0:T(8,128)(2,1)S(1)} collective-permute-done((bf16[128,768]{1,0:T(8,128)(2,1)S(1)}, bf16[128,768]{1,0:T(8,128)(2,1)S(1)}, u32[]{:S(2)}, u32[]{:S(2)}) %collective-permute-start.12) | collective-permute-done | bytes 196640 | tf_op jit(solution)/shard_map/ppermute | solution.py:18
  36.3 0.5 %speech_part.8.refs_2_ = f32[128,768]{1,0:T(8,128)S(1)} custom-call(f32[2,1]{1,0:T(2,128)S(1)} %pad_maximum_fusion.refs_8_.refs_0_, bf16[528,768]{1,0:T(8,128)(2,1)S(1)} %collective-permute-done.8.refs_3_.refs_1_, f32[128,768]{1,0:T(8,128)S(1)} %speech_part.7.refs_2_, bf16[128,768]{1,0:T(8,128)(2,1)S(1)} %collective-permute-done.12.refs_4_.refs_3_), custom_call_target="tpu_custom_call" | custom-call | flops 503316480 | bytes 1794056 | tf_op jit(solution)/shard_map/speech_part/pallas_call | solution.py:34
  36.7 0.8 %collective-permute-done.11.refs_3_ = bf16[128,768]{1,0:T(8,128)(2,1)S(1)} collective-permute-done((bf16[128,768]{1,0:T(8,128)(2,1)S(1)}, bf16[128,768]{1,0:T(8,128)(2,1)S(1)}, u32[]{:S(2)}, u32[]{:S(2)}) %collective-permute-start.11) | collective-permute-done | bytes 196640 | tf_op jit(solution)/shard_map/ppermute | solution.py:18
  37.5 0.5 %speech_part.9 = (f32[64,768]{1,0:T(8,128)S(1)}, f32[64,768]{1,0:T(8,128)S(1)}) custom-call(f32[2,1]{1,0:T(2,128)S(1)} %pad_maximum_fusion.refs_8_.refs_0_, bf16[528,768]{1,0:T(8,128)(2,1)S(1)} %collective-permute-done.8.refs_3_.refs_1_, f32[128,768]{1,0:T(8,128)S(1)} %speech_part.8.refs_2_, bf16[128,768]{1,0:T(8,128)(2,1)S(1)} %collective-permute-done.11.refs_3_), custom_call_target="tpu_custom_call" | custom-call | flops 503316480 | bytes 1794056 | tf_op jit(solution)/shard_map/speech_part/pallas_call | solution.py:34
  38.0 0.5 %collective-permute-start.14 = (f32[64,768]{1,0:T(8,128)S(1)}, f32[64,768]{1,0:T(8,128)S(1)}, u32[]{:S(2)}, u32[]{:S(2)}) collective-permute-start(f32[64,768]{1,0:T(8,128)S(1)} %get-tuple-element.26), channel_id=1, source_target_pairs={{0,1},{1,0},{2,3},{3,2},{4,5},{5,4},{6,7},{7,6},{8,9},{9,8},{10,11... | collective-permute-start | bytes 589832 | tf_op jit(solution)/shard_map/ppermute | solution.py:18
  38.5 0.7 %speech_part.6.refs_4_.home = f32[128,768]{1,0:T(8,128)S(1)} custom-call(f32[2,1]{1,0:T(2,128)S(1)} %pad_maximum_fusion.refs_8_.refs_0_, bf16[528,768]{1,0:T(8,128)(2,1)S(1)} %get-tuple-element.19.refs_2_.refs_1_, f32[128,768]{1,0:T(8,128)S(1)} %speech_part.5.refs_2_, bf16[128,768]{1,0:T(8,128)(2,1)S(1)} %collective-permute-done.11.refs_3_, ...), custom_call_target="tpu_custom_call" | custom-call | flops 1006632960 | bytes 1990664 | tf_op jit(solution)/shard_map/speech_part/pallas_call | solution.py:34
  39.5 0.2 collective-permute-done.14.refs_1_
  39.8 1.0 %finish.1 = (f32[128,768]{1,0:T(8,128)}, f32[64,768]{1,0:T(8,128)}) custom-call(bf16[128,768]{1,0:T(8,128)(2,1)S(1)} %get-tuple-element.16.audio, f32[128,768]{1,0:T(8,128)S(1)} %speech_part.6.refs_4_.home, f32[64,768]{1,0:T(8,128)S(1)} %collective-permute-done.13.refs_0_, f32[64,768]{1,0:T(8,128)S(1)} %collective-permute-done.14.refs_1_, ...), custom_call_target="tpu_custom_call" | custom-call | tf_op jit(solution)/shard_map/finish/pallas_call | solution.py:354
  (20 shorter events, 0.7 us)
Async XLA Ops:
  1.8 10.5 %collective-permute-start.1 = (bf16[64,768]{1,0:T(8,128)(2,1)S(1)}, bf16[64,768]{1,0:T(8,128)(2,1)S(1)}, u32[]{:S(2)}, u32[]{:S(2)}) collective-permute-start(bf16[64,768]{1,0:T(8,128)(2,1)S(1)} %get-tuple-element.17.refs_0_), channel_id=1, source_target_pairs={{0,16},{8,24},{16,0},{24,8},{1,17},{9,25},{17,1},{25,9},{2,18},{10... | collective-permute-start | bytes 294920 | tf_op jit(solution)/shard_map/ppermute | solution.py:18
  5.9 11.1 %collective-permute-start.3 = (bf16[136,768]{1,0:T(8,128)(2,1)S(1)}, bf16[136,768]{1,0:T(8,128)(2,1)S(1)}, u32[]{:S(2)}, u32[]{:S(2)}) collective-permute-start(bf16[136,768]{1,0:T(8,128)(2,1)S(1)} %get-tuple-element.18.refs_4_), channel_id=1, source_target_pairs={{0,6},{1,7},{2,4},{3,5},{4,2},{5,3},{6,0},{7,1},{8,14},{9,15},{10,... | collective-permute-start | bytes 626696 | tf_op jit(solution)/shard_map/ppermute | solution.py:18
  8.4 9.6 %collective-permute-start.4 = (bf16[136,768]{1,0:T(8,128)(2,1)S(1)}, bf16[136,768]{1,0:T(8,128)(2,1)S(1)}, u32[]{:S(2)}, u32[]{:S(2)}) collective-permute-start(bf16[136,768]{1,0:T(8,128)(2,1)S(1)} %get-tuple-element.18.refs_4_), channel_id=1, source_target_pairs={{0,4},{1,5},{2,6},{3,7},{4,0},{5,1},{6,2},{7,3},{8,12},{9,13},{10,... | collective-permute-start | bytes 626696 | tf_op jit(solution)/shard_map/ppermute | solution.py:18
  8.9 9.1 %collective-permute-start.5 = (bf16[136,768]{1,0:T(8,128)(2,1)S(1)}, bf16[136,768]{1,0:T(8,128)(2,1)S(1)}, u32[]{:S(2)}, u32[]{:S(2)}) collective-permute-start(bf16[136,768]{1,0:T(8,128)(2,1)S(1)} %get-tuple-element.18.refs_4_), channel_id=1, source_target_pairs={{0,2},{1,3},{2,0},{3,1},{4,6},{5,7},{6,4},{7,5},{8,10},{9,11},{10,... | collective-permute-start | bytes 626696 | tf_op jit(solution)/shard_map/ppermute | solution.py:18
  9.4 5.3 %collective-permute-start = (bf16[64,768]{1,0:T(8,128)(2,1)S(1)}, bf16[64,768]{1,0:T(8,128)(2,1)S(1)}, u32[]{:S(2)}, u32[]{:S(2)}) collective-permute-start(bf16[64,768]{1,0:T(8,128)(2,1)S(1)} %get-tuple-element.17.refs_0_), channel_id=1, source_target_pairs={{0,8},{8,0},{16,24},{24,16},{1,9},{9,1},{17,25},{25,17},{2,10},{10... | collective-permute-start | bytes 294920 | tf_op jit(solution)/shard_map/ppermute | solution.py:18
  12.3 4.7 %collective-permute-start.2 = (bf16[64,768]{1,0:T(8,128)(2,1)S(1)}, bf16[64,768]{1,0:T(8,128)(2,1)S(1)}, u32[]{:S(2)}, u32[]{:S(2)}) collective-permute-start(bf16[64,768]{1,0:T(8,128)(2,1)S(1)} %pass_on.1.refs_2_), channel_id=1, source_target_pairs={{0,8},{8,0},{16,24},{24,16},{1,9},{9,1},{17,25},{25,17},{2,10},{10... | collective-permute-start | bytes 294920 | tf_op jit(solution)/shard_map/ppermute | solution.py:18
  18.1 2.4 %collective-permute-start.8 = (bf16[528,768]{1,0:T(8,128)(2,1)S(1)}, bf16[528,768]{1,0:T(8,128)(2,1)S(1)}, u32[]{:S(2)}, u32[]{:S(2)}) collective-permute-start(bf16[528,768]{1,0:T(8,128)(2,1)S(1)} %get-tuple-element.19.refs_2_.refs_1_), channel_id=1, source_target_pairs={{0,1},{1,0},{2,3},{3,2},{4,5},{5,4},{6,7},{7,6},{8,9},{9,8},{10,11... | collective-permute-start | bytes 2433032 | tf_op jit(solution)/shard_map/ppermute | solution.py:18
  18.2 11.5 %collective-permute-start.6 = (bf16[256,768]{1,0:T(8,128)(2,1)S(1)}, bf16[256,768]{1,0:T(8,128)(2,1)S(1)}, u32[]{:S(2)}, u32[]{:S(2)}) collective-permute-start(bf16[256,768]{1,0:T(8,128)(2,1)S(1)} %get-tuple-element.20.refs_1_.refs_2_), channel_id=1, source_target_pairs={{0,2},{1,3},{2,0},{3,1},{4,6},{5,7},{6,4},{7,5},{8,10},{9,11},{10,... | collective-permute-start | bytes 1179656 | tf_op jit(solution)/shard_map/ppermute | solution.py:18
  19.7 11.5 %collective-permute-start.7 = (bf16[256,768]{1,0:T(8,128)(2,1)S(1)}, bf16[256,768]{1,0:T(8,128)(2,1)S(1)}, u32[]{:S(2)}, u32[]{:S(2)}) collective-permute-start(bf16[256,768]{1,0:T(8,128)(2,1)S(1)} %get-tuple-element.20.refs_1_.refs_2_), channel_id=1, source_target_pairs={{0,4},{1,5},{2,6},{3,7},{4,0},{5,1},{6,2},{7,3},{8,12},{9,13},{10,... | collective-permute-start | bytes 1179656 | tf_op jit(solution)/shard_map/ppermute | solution.py:18
  21.8 5.7 %collective-permute-start.9 = (f32[64,384]{1,0:T(8,128)S(1)}, f32[64,384]{1,0:T(8,128)S(1)}, u32[]{:S(2)}, u32[]{:S(2)}) collective-permute-start(f32[64,384]{1,0:T(8,128)S(1)} %get-tuple-element.22), channel_id=1, source_target_pairs={{0,8},{8,0},{16,24},{24,16},{1,9},{9,1},{17,25},{25,17},{2,10},{10... | collective-permute-start | bytes 294920 | tf_op jit(solution)/shard_map/ppermute | solution.py:18
  23.5 8.6 %collective-permute-start.10 = (f32[64,384]{1,0:T(8,128)S(1)}, f32[64,384]{1,0:T(8,128)S(1)}, u32[]{:S(2)}, u32[]{:S(2)}) collective-permute-start(f32[64,384]{1,0:T(8,128)S(1)} %get-tuple-element.24), channel_id=1, source_target_pairs={{0,8},{8,0},{16,24},{24,16},{1,9},{9,1},{17,25},{25,17},{2,10},{10... | collective-permute-start | bytes 294920 | tf_op jit(solution)/shard_map/ppermute | solution.py:18
  23.9 15.3 %collective-permute-start.17 = (f32[64,768]{1,0:T(8,128)S(1)}, f32[64,768]{1,0:T(8,128)S(1)}, u32[]{:S(2)}, u32[]{:S(2)}) collective-permute-start(f32[64,768]{1,0:T(8,128)S(1)} %get-tuple-element.28), channel_id=1, source_target_pairs={{0,8},{8,0},{16,24},{24,16},{1,9},{9,1},{17,25},{25,17},{2,10},{10... | collective-permute-start | bytes 589832 | tf_op jit(solution)/shard_map/ppermute | solution.py:18
  27.6 11.9 %collective-permute-start.15 = (f32[64,384]{1,0:T(8,128)S(1)}, f32[64,384]{1,0:T(8,128)S(1)}, u32[]{:S(2)}, u32[]{:S(2)}) collective-permute-start(f32[64,384]{1,0:T(8,128)S(1)} %sum_near.2.refs_1_.refs_5_), channel_id=1, source_target_pairs={{0,16},{8,24},{16,0},{24,8},{1,17},{9,25},{17,1},{25,9},{2,18},{10... | collective-permute-start | bytes 294920 | tf_op jit(solution)/shard_map/ppermute | solution.py:18
  29.7 6.5 %collective-permute-start.12 = (bf16[128,768]{1,0:T(8,128)(2,1)S(1)}, bf16[128,768]{1,0:T(8,128)(2,1)S(1)}, u32[]{:S(2)}, u32[]{:S(2)}) collective-permute-start(bf16[128,768]{1,0:T(8,128)(2,1)S(1)} %cut.3.refs_3_), channel_id=1, source_target_pairs={{0,4},{1,5},{2,6},{3,7},{4,0},{5,1},{6,2},{7,3},{8,12},{9,13},{10,... | collective-permute-start | bytes 589832 | tf_op jit(solution)/shard_map/ppermute | solution.py:18
  31.2 6.3 %collective-permute-start.11 = (bf16[128,768]{1,0:T(8,128)(2,1)S(1)}, bf16[128,768]{1,0:T(8,128)(2,1)S(1)}, u32[]{:S(2)}, u32[]{:S(2)}) collective-permute-start(bf16[128,768]{1,0:T(8,128)(2,1)S(1)} %cut.2.refs_2_), channel_id=1, source_target_pairs={{0,2},{1,3},{2,0},{3,1},{4,6},{5,7},{6,4},{7,5},{8,10},{9,11},{10,... | collective-permute-start | bytes 589832 | tf_op jit(solution)/shard_map/ppermute | solution.py:18
  32.1 7.3 %collective-permute-start.16 = (f32[64,384]{1,0:T(8,128)S(1)}, f32[64,384]{1,0:T(8,128)S(1)}, u32[]{:S(2)}, u32[]{:S(2)}) collective-permute-start(f32[64,384]{1,0:T(8,128)S(1)} %sum_near.3.refs_6_), channel_id=1, source_target_pairs={{0,16},{8,24},{16,0},{24,8},{1,17},{9,25},{17,1},{25,9},{2,18},{10... | collective-permute-start | bytes 294920 | tf_op jit(solution)/shard_map/ppermute | solution.py:18
  38.0 1.5 %collective-permute-start.13 = (f32[64,768]{1,0:T(8,128)S(1)}, f32[64,768]{1,0:T(8,128)S(1)}, u32[]{:S(2)}, u32[]{:S(2)}) collective-permute-start(f32[64,768]{1,0:T(8,128)S(1)} %get-tuple-element.25), channel_id=1, source_target_pairs={{0,1},{1,0},{2,3},{3,2},{4,5},{5,4},{6,7},{7,6},{8,9},{9,8},{10,11... | collective-permute-start | bytes 589832 | tf_op jit(solution)/shard_map/ppermute | solution.py:18
  38.0 1.7 %collective-permute-start.14 = (f32[64,768]{1,0:T(8,128)S(1)}, f32[64,768]{1,0:T(8,128)S(1)}, u32[]{:S(2)}, u32[]{:S(2)}) collective-permute-start(f32[64,768]{1,0:T(8,128)S(1)} %get-tuple-element.26), channel_id=1, source_target_pairs={{0,1},{1,0},{2,3},{3,2},{4,5},{5,4},{6,7},{7,6},{8,9},{9,8},{10,11... | collective-permute-start | bytes 589832 | tf_op jit(solution)/shard_map/ppermute | solution.py:18

commit v23 on v22

--- a/solution.py
+++ b/solution.py
@@ -158,16 +158,23 @@
 
 def speech_part_body(rows, own_text, has_start, chips, places, outputs, *refs):
     sharp, shift, speech = refs[0][0:1, 0:1], refs[0][1:2, 0:1], refs[1]
-    total = refs[2][...] if has_start else None
-    texts, outs = refs[3 if has_start else 2 : -outputs], refs[-outputs:]
+    texts, outs = list(refs[4 if has_start else 2 : -outputs]), refs[-outputs:]
     members = lax.axis_size("member")
     group = lax.axis_index("group")
     member = lax.axis_index("member")
-    table = speech[chips * rows :, :].astype(jnp.float32)
-    marks = jnp.broadcast_to(marks_of(table, 0, rows), (rows, rows)).T[:, 0:1]
+    if has_start:
+        total = refs[2][...]
+        marks = refs[3][:, 0:1]
+    else:
+        total = None
+        table = speech[chips * rows :, :].astype(jnp.float32)
+        spread = jnp.broadcast_to(marks_of(table, 0, rows), (rows, rows)).T
+        outs, kept = outs[:-1], outs[-1]
+        kept[...] = spread
+        marks = spread[:, 0:1]
     block = speech[0:rows, :]
-    for (mask, first), ref in zip(places, texts):
-        text = ref[...]
+    for mask, first, count in places:
+        text = jnp.concatenate([texts.pop(0)[...] for _ in range(count)], axis=0)
         lane = lax.broadcasted_iota(jnp.int32, (1, text.shape[0]), 1)
         owner = (group ^ (first + lane // own_text)) * members + (member ^ (2 * mask))
         ids = (owner * own_text + lane % own_text).astype(jnp.float32)
@@ -322,25 +329,27 @@
     from_near = [exchanged(parts[k], "group", k) for k in range(1, groups // 2)]
 
     def speech_part(speech, start, places, texts, after=(), pieces=1):
+        outs = [f32(rows // pieces, width)] * pieces
+        if not start:
+            outs.append(f32(rows, rows))
         body = functools.partial(
-            speech_part_body, rows, own_text, bool(start), chips, places, pieces
+            speech_part_body, rows, own_text, bool(start), chips, places, len(outs)
         )
         work = 40 * rows * sum(v.shape[0] for v in texts) * width
-        outs = [f32(rows // pieces, width)] * pieces
         operands = [scalars, speech, *start, *texts]
-        return call(body, outs, operands, after, work, temporary, "speech_part")
-
-    near = [[(k, 0) for k in (0, *masks)], [text, *text_near], tuple(far[0])]
+        return list(call(body, outs, operands, after, work, temporary, "speech_part"))
+
+    near = [[(k, 0, 1) for k in (0, *masks)], [text, *text_near], tuple(far[0])]
     if square:
-        away = speech_part(other, [], *near)
-        home = speech_part(speech, [], *near)
-        far_places = [(3, 0), (3, groups // 2)]
-        away = speech_part(other, away, far_places[1:], text_far[1:])
-        away = speech_part(other, away, far_places[:1], text_far[:1], pieces=2)
-        home = speech_part(speech, home, far_places, text_far)
+        away, away_marks = speech_part(other, [], *near)
+        home, home_marks = speech_part(speech, [], *near)
+        last = [(3, groups // 2, 1)]
+        away = speech_part(other, [away, away_marks], last, text_far[1:])
+        away = speech_part(other, [*away, away_marks], [(3, 0, 1)], text_far[:1], pieces=2)
+        home = speech_part(speech, [home, home_marks], [(3, 0, 2)], text_far)
     else:
-        away = speech_part(other, [], *near, pieces=2)
-        home = speech_part(speech, [], *near)
+        away = speech_part(other, [], *near, pieces=2)[:-1]
+        home = speech_part(speech, [], *near)[:-1]
     back = [exchanged(piece, "member", 1) for piece in away]
     text_back = call(
         add_sides_body,

time: 40.9 us -> 40.9 us (level)
  transfers between devices with their start and end apart: 18 -> 18, of which waited for: 10 -> 10; matrix products, arithmetic and copies ran while one was open for 0% -> 0% of each run, Pallas kernels for 13% -> 12%
where the time goes in v23:
time: 40.9 us; the launch traced here: 40.8 us
  starting transfers between devices  20.1 us (49%)
  waiting for transfers between devices  11.4 us (28%)
  Pallas kernels  7.2 us (18%)
  between operations  2.06 us (5%)
    ppermute x18, starting transfers between devices, exchanged(): return lax.ppermute(value, axis, [(i, i ^ mask) for i in range(size)])  20.1 us
    ppermute x18, waiting for transfers between devices, exchanged(): return lax.ppermute(value, axis, [(i, i ^ mask) for i in range(size)])  11.4 us
    pallas_call x13, Pallas kernels, call(): pl.pallas_call(whole, out_shape=out_shape, in_specs=specs, out_specs=jax....  5 us
    pallas_call x1, Pallas kernels, shards(): pl.pallas_call(prepare_body, out_shape=[bf16(rows + MARK_ROWS, width), bf...  1.18 us
    pallas_call x1, Pallas kernels, shards(): pl.pallas_call(functools.partial(finish_body, len(back)), out_shape=resul...  1.02 us
  transfers between devices with their start and end apart: 18, of which 10 were waited for; matrix products, arithmetic and copies ran while one was open for 0% of the time, Pallas kernels for 12%

profile of v23, /device:TPU:0, one launch (start us, length us, event | category | flops | bytes accessed | tf_op | source)
XLA Modules:
  0.0 40.8 jit_solution(556374384064065018)
XLA Ops:
  0.6 1.2 %unit_rows.1 = (bf16[136,768]{1,0:T(8,128)(2,1)S(1)}, bf16[64,768]{1,0:T(8,128)(2,1)S(1)}, bf16[128,768]{1,0:T(8,128)(2,1)S(1)}, bf16[64,768]{1,0:T(8,128)(2,1)S(1)}) custom-call(bf16[128,768]{1,0:T(8,128)(2,1)} %refs_0_.1, bf16[64,768]{1,0:T(8,128)(2,1)} %refs_1_.1, s32[1,128]{1,0:T(1,128)} %bitcast.5), custom_call_target="tpu_custom_call" | custom-call | tf_op jit(solution)/shard_map/unit_rows/pallas_call | solution.py:253
  1.8 4.1 %collective-permute-start.1 = (bf16[64,768]{1,0:T(8,128)(2,1)S(1)}, bf16[64,768]{1,0:T(8,128)(2,1)S(1)}, u32[]{:S(2)}, u32[]{:S(2)}) collective-permute-start(bf16[64,768]{1,0:T(8,128)(2,1)S(1)} %get-tuple-element.21.refs_0_), channel_id=1, source_target_pairs={{0,16},{8,24},{16,0},{24,8},{1,17},{9,25},{17,1},{25,9},{2,18},{10... | collective-permute-start | bytes 294920 | tf_op jit(solution)/shard_map/ppermute | solution.py:18
  5.9 2.4 %collective-permute-start.3 = (bf16[136,768]{1,0:T(8,128)(2,1)S(1)}, bf16[136,768]{1,0:T(8,128)(2,1)S(1)}, u32[]{:S(2)}, u32[]{:S(2)}) collective-permute-start(bf16[136,768]{1,0:T(8,128)(2,1)S(1)} %get-tuple-element.22.refs_4_), channel_id=1, source_target_pairs={{0,6},{1,7},{2,4},{3,5},{4,2},{5,3},{6,0},{7,1},{8,14},{9,15},{10,... | collective-permute-start | bytes 626696 | tf_op jit(solution)/shard_map/ppermute | solution.py:18
  8.4 0.5 %collective-permute-start.4 = (bf16[136,768]{1,0:T(8,128)(2,1)S(1)}, bf16[136,768]{1,0:T(8,128)(2,1)S(1)}, u32[]{:S(2)}, u32[]{:S(2)}) collective-permute-start(bf16[136,768]{1,0:T(8,128)(2,1)S(1)} %get-tuple-element.22.refs_4_), channel_id=1, source_target_pairs={{0,4},{1,5},{2,6},{3,7},{4,0},{5,1},{6,2},{7,3},{8,12},{9,13},{10,... | collective-permute-start | bytes 626696 | tf_op jit(solution)/shard_map/ppermute | solution.py:18
  8.9 0.5 %collective-permute-start.5 = (bf16[136,768]{1,0:T(8,128)(2,1)S(1)}, bf16[136,768]{1,0:T(8,128)(2,1)S(1)}, u32[]{:S(2)}, u32[]{:S(2)}) collective-permute-start(bf16[136,768]{1,0:T(8,128)(2,1)S(1)} %get-tuple-element.22.refs_4_), channel_id=1, source_target_pairs={{0,2},{1,3},{2,0},{3,1},{4,6},{5,7},{6,4},{7,5},{8,10},{9,11},{10,... | collective-permute-start | bytes 626696 | tf_op jit(solution)/shard_map/ppermute | solution.py:18
  9.4 1.6 %collective-permute-start = (bf16[64,768]{1,0:T(8,128)(2,1)S(1)}, bf16[64,768]{1,0:T(8,128)(2,1)S(1)}, u32[]{:S(2)}, u32[]{:S(2)}) collective-permute-start(bf16[64,768]{1,0:T(8,128)(2,1)S(1)} %get-tuple-element.21.refs_0_), channel_id=1, source_target_pairs={{0,8},{8,0},{16,24},{24,16},{1,9},{9,1},{17,25},{25,17},{2,10},{10... | collective-permute-start | bytes 294920 | tf_op jit(solution)/shard_map/ppermute | solution.py:18
  12.3 0.5 %collective-permute-start.2 = (bf16[64,768]{1,0:T(8,128)(2,1)S(1)}, bf16[64,768]{1,0:T(8,128)(2,1)S(1)}, u32[]{:S(2)}, u32[]{:S(2)}) collective-permute-start(bf16[64,768]{1,0:T(8,128)(2,1)S(1)} %pass_on.1.refs_2_), channel_id=1, source_target_pairs={{0,8},{8,0},{16,24},{24,16},{1,9},{9,1},{17,25},{25,17},{2,10},{10... | collective-permute-start | bytes 294920 | tf_op jit(solution)/shard_map/ppermute | solution.py:18
  12.8 1.9 %collective-permute-done.refs_1_ = bf16[64,768]{1,0:T(8,128)(2,1)S(1)} collective-permute-done((bf16[64,768]{1,0:T(8,128)(2,1)S(1)}, bf16[64,768]{1,0:T(8,128)(2,1)S(1)}, u32[]{:S(2)}, u32[]{:S(2)}) %collective-permute-start) | collective-permute-done | bytes 98336 | tf_op jit(solution)/shard_map/ppermute | solution.py:18
  14.7 2.3 %collective-permute-done.2.refs_3_ = bf16[64,768]{1,0:T(8,128)(2,1)S(1)} collective-permute-done((bf16[64,768]{1,0:T(8,128)(2,1)S(1)}, bf16[64,768]{1,0:T(8,128)(2,1)S(1)}, u32[]{:S(2)}, u32[]{:S(2)}) %collective-permute-start.2) | collective-permute-done | bytes 98336 | tf_op jit(solution)/shard_map/ppermute | solution.py:18
  17.0 0.9 %collective-permute-done.4.refs_6_ = bf16[136,768]{1,0:T(8,128)(2,1)S(1)} collective-permute-done((bf16[136,768]{1,0:T(8,128)(2,1)S(1)}, bf16[136,768]{1,0:T(8,128)(2,1)S(1)}, u32[]{:S(2)}, u32[]{:S(2)}) %collective-permute-start.4) | collective-permute-done | bytes 208928 | tf_op jit(solution)/shard_map/ppermute | solution.py:18
  18.2 1.6 %collective-permute-start.6 = (bf16[256,768]{1,0:T(8,128)(2,1)S(1)}, bf16[256,768]{1,0:T(8,128)(2,1)S(1)}, u32[]{:S(2)}, u32[]{:S(2)}) collective-permute-start(bf16[256,768]{1,0:T(8,128)(2,1)S(1)} %get-tuple-element.24.refs_1_.refs_2_), channel_id=1, source_target_pairs={{0,2},{1,3},{2,0},{3,1},{4,6},{5,7},{6,4},{7,5},{8,10},{9,11},{10,... | collective-permute-start | bytes 1179656 | tf_op jit(solution)/shard_map/ppermute | solution.py:18
  19.7 0.7 %collective-permute-start.7 = (bf16[256,768]{1,0:T(8,128)(2,1)S(1)}, bf16[256,768]{1,0:T(8,128)(2,1)S(1)}, u32[]{:S(2)}, u32[]{:S(2)}) collective-permute-start(bf16[256,768]{1,0:T(8,128)(2,1)S(1)} %get-tuple-element.24.refs_1_.refs_2_), channel_id=1, source_target_pairs={{0,4},{1,5},{2,6},{3,7},{4,0},{5,1},{6,2},{7,3},{8,12},{9,13},{10,... | collective-permute-start | bytes 1179656 | tf_op jit(solution)/shard_map/ppermute | solution.py:18
  20.5 1.3 %text_part.1 = (f32[64,768]{1,0:T(8,128)S(1)}, f32[64,768]{1,0:T(8,128)S(1)}, f32[64,384]{1,0:T(8,128)S(1)}, f32[64,384]{1,0:T(8,128)S(1)}, f32[64,384]{1,0:T(8,128)S(1)}, /*index=5*/f32[64,384]{1,0:T(8,128)S(1)}) custom-call(f32[2,1]{1,0:T(2,128)S(1)} %pad_maximum_fusion.refs_8_.refs_0_, bf16[256,768]{1,0:T(8,128)(2,1)S(1)} %get-tuple-element.24.refs_1_.refs_2_, ...), custom_call_target="tpu_custom_call" | custom-call | flops 805306368 | bytes 2801672 | tf_op jit(solution)/shard_map/text_part/pallas_call | solution.py:34
  21.8 1.6 %collective-permute-start.9 = (f32[64,384]{1,0:T(8,128)S(1)}, f32[64,384]{1,0:T(8,128)S(1)}, u32[]{:S(2)}, u32[]{:S(2)}) collective-permute-start(f32[64,384]{1,0:T(8,128)S(1)} %get-tuple-element.26), channel_id=1, source_target_pairs={{0,8},{8,0},{16,24},{24,16},{1,9},{9,1},{17,25},{25,17},{2,10},{10... | collective-permute-start | bytes 294920 | tf_op jit(solution)/shard_map/ppermute | solution.py:18
  23.5 0.4 %collective-permute-start.10 = (f32[64,384]{1,0:T(8,128)S(1)}, f32[64,384]{1,0:T(8,128)S(1)}, u32[]{:S(2)}, u32[]{:S(2)}) collective-permute-start(f32[64,384]{1,0:T(8,128)S(1)} %get-tuple-element.28), channel_id=1, source_target_pairs={{0,8},{8,0},{16,24},{24,16},{1,9},{9,1},{17,25},{25,17},{2,10},{10... | collective-permute-start | bytes 294920 | tf_op jit(solution)/shard_map/ppermute | solution.py:18
  23.9 1.6 %collective-permute-start.17 = (f32[64,768]{1,0:T(8,128)S(1)}, f32[64,768]{1,0:T(8,128)S(1)}, u32[]{:S(2)}, u32[]{:S(2)}) collective-permute-start(f32[64,768]{1,0:T(8,128)S(1)} %get-tuple-element.36), channel_id=1, source_target_pairs={{0,8},{8,0},{16,24},{24,16},{1,9},{9,1},{17,25},{25,17},{2,10},{10... | collective-permute-start | bytes 589832 | tf_op jit(solution)/shard_map/ppermute | solution.py:18
  25.5 2.0 %collective-permute-done.9.refs_1_ = f32[64,384]{1,0:T(8,128)S(1)} collective-permute-done((f32[64,384]{1,0:T(8,128)S(1)}, f32[64,384]{1,0:T(8,128)S(1)}, u32[]{:S(2)}, u32[]{:S(2)}) %collective-permute-start.9) | collective-permute-done | bytes 98336 | tf_op jit(solution)/shard_map/ppermute | solution.py:18
  27.6 0.6 %collective-permute-start.15 = (f32[64,384]{1,0:T(8,128)S(1)}, f32[64,384]{1,0:T(8,128)S(1)}, u32[]{:S(2)}, u32[]{:S(2)}) collective-permute-start(f32[64,384]{1,0:T(8,128)S(1)} %sum_near.2.refs_1_.refs_5_), channel_id=1, source_target_pairs={{0,16},{8,24},{16,0},{24,8},{1,17},{9,25},{17,1},{25,9},{2,18},{10... | collective-permute-start | bytes 294920 | tf_op jit(solution)/shard_map/ppermute | solution.py:18
  28.2 1.6 %collective-permute-done.6.refs_0_.refs_3_ = bf16[256,768]{1,0:T(8,128)(2,1)S(1)} collective-permute-done((bf16[256,768]{1,0:T(8,128)(2,1)S(1)}, bf16[256,768]{1,0:T(8,128)(2,1)S(1)}, u32[]{:S(2)}, u32[]{:S(2)}) %collective-permute-start.6) | collective-permute-done | bytes 393248 | tf_op jit(solution)/shard_map/ppermute | solution.py:18
  29.7 1.5 %collective-permute-start.12 = (bf16[128,768]{1,0:T(8,128)(2,1)S(1)}, bf16[128,768]{1,0:T(8,128)(2,1)S(1)}, u32[]{:S(2)}, u32[]{:S(2)}) collective-permute-start(bf16[128,768]{1,0:T(8,128)(2,1)S(1)} %cut.3.refs_3_), channel_id=1, source_target_pairs={{0,4},{1,5},{2,6},{3,7},{4,0},{5,1},{6,2},{7,3},{8,12},{9,13},{10,... | collective-permute-start | bytes 589832 | tf_op jit(solution)/shard_map/ppermute | solution.py:18
  31.2 0.9 %collective-permute-start.11 = (bf16[128,768]{1,0:T(8,128)(2,1)S(1)}, bf16[128,768]{1,0:T(8,128)(2,1)S(1)}, u32[]{:S(2)}, u32[]{:S(2)}) collective-permute-start(bf16[128,768]{1,0:T(8,128)(2,1)S(1)} %cut.2.refs_2_), channel_id=1, source_target_pairs={{0,2},{1,3},{2,0},{3,1},{4,6},{5,7},{6,4},{7,5},{8,10},{9,11},{10,... | collective-permute-start | bytes 589832 | tf_op jit(solution)/shard_map/ppermute | solution.py:18
  32.1 0.9 %collective-permute-start.16 = (f32[64,384]{1,0:T(8,128)S(1)}, f32[64,384]{1,0:T(8,128)S(1)}, u32[]{:S(2)}, u32[]{:S(2)}) collective-permute-start(f32[64,384]{1,0:T(8,128)S(1)} %sum_near.3.refs_6_), channel_id=1, source_target_pairs={{0,16},{8,24},{16,0},{24,8},{1,17},{9,25},{17,1},{25,9},{2,18},{10... | collective-permute-start | bytes 294920 | tf_op jit(solution)/shard_map/ppermute | solution.py:18
  33.0 1.0 %speech_part.5 = (f32[128,768]{1,0:T(8,128)S(1)}, f32[128,128]{1,0:T(8,128)S(1)}) custom-call(f32[2,1]{1,0:T(2,128)S(1)} %pad_maximum_fusion.refs_8_.refs_0_, bf16[528,768]{1,0:T(8,128)(2,1)S(1)} %get-tuple-element.23.refs_2_.refs_1_, bf16[256,768]{1,0:T(8,128)(2,1)S(1)} %get-tuple-element.24.refs_1_.refs_2_, ...), custom_call_target="tpu_custom_call" | custom-call | flops 3019898880 | bytes 2449416 | tf_op jit(solution)/shard_map/speech_part/pallas_call | solution.py:34
  34.1 1.0 %speech_part.7 = (f32[128,768]{1,0:T(8,128)S(1)}, f32[128,128]{1,0:T(8,128)S(1)}) custom-call(f32[2,1]{1,0:T(2,128)S(1)} %pad_maximum_fusion.refs_8_.refs_0_, bf16[528,768]{1,0:T(8,128)(2,1)S(1)} %collective-permute-done.8.refs_3_.refs_1_, bf16[256,768]{1,0:T(8,128)(2,1)S(1)} %get-tuple-element.24.refs_1_.refs_2_, ...), custom_call_target="tpu_custom_call" | custom-call | flops 3019898880 | bytes 2449416 | tf_op jit(solution)/shard_map/speech_part/pallas_call | solution.py:34
  35.1 1.2 %collective-permute-done.12.refs_5_.refs_4_ = bf16[128,768]{1,0:T(8,128)(2,1)S(1)} collective-permute-done((bf16[128,768]{1,0:T(8,128)(2,1)S(1)}, bf16[128,768]{1,0:T(8,128)(2,1)S(1)}, u32[]{:S(2)}, u32[]{:S(2)}) %collective-permute-start.12) | collective-permute-done | bytes 196640 | tf_op jit(solution)/shard_map/ppermute | solution.py:18
  36.3 0.5 %speech_part.8.refs_2_ = f32[128,768]{1,0:T(8,128)S(1)} custom-call(f32[2,1]{1,0:T(2,128)S(1)} %pad_maximum_fusion.refs_8_.refs_0_, bf16[528,768]{1,0:T(8,128)(2,1)S(1)} %collective-permute-done.8.refs_3_.refs_1_, f32[128,768]{1,0:T(8,128)S(1)} %get-tuple-element.31.refs_2_, f32[128,128]{1,0:T(8,128)S(1)} %get-tuple-element.32.refs_3_, ...), custom_call_target="tpu_custom_call" | custom-call | flops 503316480 | bytes 1859592 | tf_op jit(solution)/shard_map/speech_part/pallas_call | solution.py:34
  36.7 0.8 %collective-permute-done.11.refs_4_ = bf16[128,768]{1,0:T(8,128)(2,1)S(1)} collective-permute-done((bf16[128,768]{1,0:T(8,128)(2,1)S(1)}, bf16[128,768]{1,0:T(8,128)(2,1)S(1)}, u32[]{:S(2)}, u32[]{:S(2)}) %collective-permute-start.11) | collective-permute-done | bytes 196640 | tf_op jit(solution)/shard_map/ppermute | solution.py:18
  37.5 0.5 %speech_part.9 = (f32[64,768]{1,0:T(8,128)S(1)}, f32[64,768]{1,0:T(8,128)S(1)}) custom-call(f32[2,1]{1,0:T(2,128)S(1)} %pad_maximum_fusion.refs_8_.refs_0_, bf16[528,768]{1,0:T(8,128)(2,1)S(1)} %collective-permute-done.8.refs_3_.refs_1_, f32[128,768]{1,0:T(8,128)S(1)} %speech_part.8.refs_2_, f32[128,128]{1,0:T(8,128)S(1)} %get-tuple-element.32.refs_3_, ...), custom_call_target="tpu_custom_call" | custom-call | flops 503316480 | bytes 1859592 | tf_op jit(solution)/shard_map/speech_part/pallas_call | solution.py:34
  38.0 0.5 %collective-permute-start.14 = (f32[64,768]{1,0:T(8,128)S(1)}, f32[64,768]{1,0:T(8,128)S(1)}, u32[]{:S(2)}, u32[]{:S(2)}) collective-permute-start(f32[64,768]{1,0:T(8,128)S(1)} %get-tuple-element.34), channel_id=1, source_target_pairs={{0,1},{1,0},{2,3},{3,2},{4,5},{5,4},{6,7},{7,6},{8,9},{9,8},{10,11... | collective-permute-start | bytes 589832 | tf_op jit(solution)/shard_map/ppermute | solution.py:18
  38.5 0.5 %speech_part.6.refs_4_.home = f32[128,768]{1,0:T(8,128)S(1)} custom-call(f32[2,1]{1,0:T(2,128)S(1)} %pad_maximum_fusion.refs_8_.refs_0_, bf16[528,768]{1,0:T(8,128)(2,1)S(1)} %get-tuple-element.23.refs_2_.refs_1_, f32[128,768]{1,0:T(8,128)S(1)} %get-tuple-element.29.refs_2_, f32[128,128]{1,0:T(8,128)S(1)} %get-tuple-element.30.refs_3_, ...), custom_call_target="tpu_custom_call" | custom-call | flops 1006632960 | bytes 2056200 | tf_op jit(solution)/shard_map/speech_part/pallas_call | solution.py:34
  39.1 0.4 collective-permute-done.16.refs_1_
  39.8 1.0 %finish.1 = (f32[128,768]{1,0:T(8,128)}, f32[64,768]{1,0:T(8,128)}) custom-call(bf16[128,768]{1,0:T(8,128)(2,1)S(1)} %get-tuple-element.20.audio, f32[128,768]{1,0:T(8,128)S(1)} %speech_part.6.refs_4_.home, f32[64,768]{1,0:T(8,128)S(1)} %collective-permute-done.13.refs_0_, f32[64,768]{1,0:T(8,128)S(1)} %collective-permute-done.14.refs_1_, ...), custom_call_target="tpu_custom_call" | custom-call | tf_op jit(solution)/shard_map/finish/pallas_call | solution.py:363
  (20 shorter events, 0.7 us)
Async XLA Ops:
  1.8 10.5 %collective-permute-start.1 = (bf16[64,768]{1,0:T(8,128)(2,1)S(1)}, bf16[64,768]{1,0:T(8,128)(2,1)S(1)}, u32[]{:S(2)}, u32[]{:S(2)}) collective-permute-start(bf16[64,768]{1,0:T(8,128)(2,1)S(1)} %get-tuple-element.21.refs_0_), channel_id=1, source_target_pairs={{0,16},{8,24},{16,0},{24,8},{1,17},{9,25},{17,1},{25,9},{2,18},{10... | collective-permute-start | bytes 294920 | tf_op jit(solution)/shard_map/ppermute | solution.py:18
  5.9 11.1 %collective-permute-start.3 = (bf16[136,768]{1,0:T(8,128)(2,1)S(1)}, bf16[136,768]{1,0:T(8,128)(2,1)S(1)}, u32[]{:S(2)}, u32[]{:S(2)}) collective-permute-start(bf16[136,768]{1,0:T(8,128)(2,1)S(1)} %get-tuple-element.22.refs_4_), channel_id=1, source_target_pairs={{0,6},{1,7},{2,4},{3,5},{4,2},{5,3},{6,0},{7,1},{8,14},{9,15},{10,... | collective-permute-start | bytes 626696 | tf_op jit(solution)/shard_map/ppermute | solution.py:18
  8.4 9.6 %collective-permute-start.4 = (bf16[136,768]{1,0:T(8,128)(2,1)S(1)}, bf16[136,768]{1,0:T(8,128)(2,1)S(1)}, u32[]{:S(2)}, u32[]{:S(2)}) collective-permute-start(bf16[136,768]{1,0:T(8,128)(2,1)S(1)} %get-tuple-element.22.refs_4_), channel_id=1, source_target_pairs={{0,4},{1,5},{2,6},{3,7},{4,0},{5,1},{6,2},{7,3},{8,12},{9,13},{10,... | collective-permute-start | bytes 626696 | tf_op jit(solution)/shard_map/ppermute | solution.py:18
  8.9 9.1 %collective-permute-start.5 = (bf16[136,768]{1,0:T(8,128)(2,1)S(1)}, bf16[136,768]{1,0:T(8,128)(2,1)S(1)}, u32[]{:S(2)}, u32[]{:S(2)}) collective-permute-start(bf16[136,768]{1,0:T(8,128)(2,1)S(1)} %get-tuple-element.22.refs_4_), channel_id=1, source_target_pairs={{0,2},{1,3},{2,0},{3,1},{4,6},{5,7},{6,4},{7,5},{8,10},{9,11},{10,... | collective-permute-start | bytes 626696 | tf_op jit(solution)/shard_map/ppermute | solution.py:18
  9.4 5.3 %collective-permute-start = (bf16[64,768]{1,0:T(8,128)(2,1)S(1)}, bf16[64,768]{1,0:T(8,128)(2,1)S(1)}, u32[]{:S(2)}, u32[]{:S(2)}) collective-permute-start(bf16[64,768]{1,0:T(8,128)(2,1)S(1)} %get-tuple-element.21.refs_0_), channel_id=1, source_target_pairs={{0,8},{8,0},{16,24},{24,16},{1,9},{9,1},{17,25},{25,17},{2,10},{10... | collective-permute-start | bytes 294920 | tf_op jit(solution)/shard_map/ppermute | solution.py:18
  12.3 4.7 %collective-permute-start.2 = (bf16[64,768]{1,0:T(8,128)(2,1)S(1)}, bf16[64,768]{1,0:T(8,128)(2,1)S(1)}, u32[]{:S(2)}, u32[]{:S(2)}) collective-permute-start(bf16[64,768]{1,0:T(8,128)(2,1)S(1)} %pass_on.1.refs_2_), channel_id=1, source_target_pairs={{0,8},{8,0},{16,24},{24,16},{1,9},{9,1},{17,25},{25,17},{2,10},{10... | collective-permute-start | bytes 294920 | tf_op jit(solution)/shard_map/ppermute | solution.py:18
  18.1 2.4 %collective-permute-start.8 = (bf16[528,768]{1,0:T(8,128)(2,1)S(1)}, bf16[528,768]{1,0:T(8,128)(2,1)S(1)}, u32[]{:S(2)}, u32[]{:S(2)}) collective-permute-start(bf16[528,768]{1,0:T(8,128)(2,1)S(1)} %get-tuple-element.23.refs_2_.refs_1_), channel_id=1, source_target_pairs={{0,1},{1,0},{2,3},{3,2},{4,5},{5,4},{6,7},{7,6},{8,9},{9,8},{10,11... | collective-permute-start | bytes 2433032 | tf_op jit(solution)/shard_map/ppermute | solution.py:18
  18.2 11.5 %collective-permute-start.6 = (bf16[256,768]{1,0:T(8,128)(2,1)S(1)}, bf16[256,768]{1,0:T(8,128)(2,1)S(1)}, u32[]{:S(2)}, u32[]{:S(2)}) collective-permute-start(bf16[256,768]{1,0:T(8,128)(2,1)S(1)} %get-tuple-element.24.refs_1_.refs_2_), channel_id=1, source_target_pairs={{0,2},{1,3},{2,0},{3,1},{4,6},{5,7},{6,4},{7,5},{8,10},{9,11},{10,... | collective-permute-start | bytes 1179656 | tf_op jit(solution)/shard_map/ppermute | solution.py:18
  19.7 11.5 %collective-permute-start.7 = (bf16[256,768]{1,0:T(8,128)(2,1)S(1)}, bf16[256,768]{1,0:T(8,128)(2,1)S(1)}, u32[]{:S(2)}, u32[]{:S(2)}) collective-permute-start(bf16[256,768]{1,0:T(8,128)(2,1)S(1)} %get-tuple-element.24.refs_1_.refs_2_), channel_id=1, source_target_pairs={{0,4},{1,5},{2,6},{3,7},{4,0},{5,1},{6,2},{7,3},{8,12},{9,13},{10,... | collective-permute-start | bytes 1179656 | tf_op jit(solution)/shard_map/ppermute | solution.py:18
  21.8 5.7 %collective-permute-start.9 = (f32[64,384]{1,0:T(8,128)S(1)}, f32[64,384]{1,0:T(8,128)S(1)}, u32[]{:S(2)}, u32[]{:S(2)}) collective-permute-start(f32[64,384]{1,0:T(8,128)S(1)} %get-tuple-element.26), channel_id=1, source_target_pairs={{0,8},{8,0},{16,24},{24,16},{1,9},{9,1},{17,25},{25,17},{2,10},{10... | collective-permute-start | bytes 294920 | tf_op jit(solution)/shard_map/ppermute | solution.py:18
  23.5 8.6 %collective-permute-start.10 = (f32[64,384]{1,0:T(8,128)S(1)}, f32[64,384]{1,0:T(8,128)S(1)}, u32[]{:S(2)}, u32[]{:S(2)}) collective-permute-start(f32[64,384]{1,0:T(8,128)S(1)} %get-tuple-element.28), channel_id=1, source_target_pairs={{0,8},{8,0},{16,24},{24,16},{1,9},{9,1},{17,25},{25,17},{2,10},{10... | collective-permute-start | bytes 294920 | tf_op jit(solution)/shard_map/ppermute | solution.py:18
  23.9 15.1 %collective-permute-start.17 = (f32[64,768]{1,0:T(8,128)S(1)}, f32[64,768]{1,0:T(8,128)S(1)}, u32[]{:S(2)}, u32[]{:S(2)}) collective-permute-start(f32[64,768]{1,0:T(8,128)S(1)} %get-tuple-element.36), channel_id=1, source_target_pairs={{0,8},{8,0},{16,24},{24,16},{1,9},{9,1},{17,25},{25,17},{2,10},{10... | collective-permute-start | bytes 589832 | tf_op jit(solution)/shard_map/ppermute | solution.py:18
  27.6 11.9 %collective-permute-start.15 = (f32[64,384]{1,0:T(8,128)S(1)}, f32[64,384]{1,0:T(8,128)S(1)}, u32[]{:S(2)}, u32[]{:S(2)}) collective-permute-start(f32[64,384]{1,0:T(8,128)S(1)} %sum_near.2.refs_1_.refs_5_), channel_id=1, source_target_pairs={{0,16},{8,24},{16,0},{24,8},{1,17},{9,25},{17,1},{25,9},{2,18},{10... | collective-permute-start | bytes 294920 | tf_op jit(solution)/shard_map/ppermute | solution.py:18
  29.7 6.5 %collective-permute-start.12 = (bf16[128,768]{1,0:T(8,128)(2,1)S(1)}, bf16[128,768]{1,0:T(8,128)(2,1)S(1)}, u32[]{:S(2)}, u32[]{:S(2)}) collective-permute-start(bf16[128,768]{1,0:T(8,128)(2,1)S(1)} %cut.3.refs_3_), channel_id=1, source_target_pairs={{0,4},{1,5},{2,6},{3,7},{4,0},{5,1},{6,2},{7,3},{8,12},{9,13},{10,... | collective-permute-start | bytes 589832 | tf_op jit(solution)/shard_map/ppermute | solution.py:18
  31.2 6.3 %collective-permute-start.11 = (bf16[128,768]{1,0:T(8,128)(2,1)S(1)}, bf16[128,768]{1,0:T(8,128)(2,1)S(1)}, u32[]{:S(2)}, u32[]{:S(2)}) collective-permute-start(bf16[128,768]{1,0:T(8,128)(2,1)S(1)} %cut.2.refs_2_), channel_id=1, source_target_pairs={{0,2},{1,3},{2,0},{3,1},{4,6},{5,7},{6,4},{7,5},{8,10},{9,11},{10,... | collective-permute-start | bytes 589832 | tf_op jit(solution)/shard_map/ppermute | solution.py:18
  32.1 7.3 %collective-permute-start.16 = (f32[64,384]{1,0:T(8,128)S(1)}, f32[64,384]{1,0:T(8,128)S(1)}, u32[]{:S(2)}, u32[]{:S(2)}) collective-permute-start(f32[64,384]{1,0:T(8,128)S(1)} %sum_near.3.refs_6_), channel_id=1, source_target_pairs={{0,16},{8,24},{16,0},{24,8},{1,17},{9,25},{17,1},{25,9},{2,18},{10... | collective-permute-start | bytes 294920 | tf_op jit(solution)/shard_map/ppermute | solution.py:18
  38.0 1.5 %collective-permute-start.13 = (f32[64,768]{1,0:T(8,128)S(1)}, f32[64,768]{1,0:T(8,128)S(1)}, u32[]{:S(2)}, u32[]{:S(2)}) collective-permute-start(f32[64,768]{1,0:T(8,128)S(1)} %get-tuple-element.33), channel_id=1, source_target_pairs={{0,1},{1,0},{2,3},{3,2},{4,5},{5,4},{6,7},{7,6},{8,9},{9,8},{10,11... | collective-permute-start | bytes 589832 | tf_op jit(solution)/shard_map/ppermute | solution.py:18
  38.0 1.7 %collective-permute-start.14 = (f32[64,768]{1,0:T(8,128)S(1)}, f32[64,768]{1,0:T(8,128)S(1)}, u32[]{:S(2)}, u32[]{:S(2)}) collective-permute-start(f32[64,768]{1,0:T(8,128)S(1)} %get-tuple-element.34), channel_id=1, source_target_pairs={{0,1},{1,0},{2,3},{3,2},{4,5},{5,4},{6,7},{7,6},{8,9},{9,8},{10,11... | collective-permute-start | bytes 589832 | tf_op jit(solution)/shard_map/ppermute | solution.py:18

commit v24 on v22

--- a/solution.py
+++ b/solution.py
@@ -68,6 +68,10 @@
     speech[rows : rows + MARK_ROWS, :] = jnp.broadcast_to(
         wide, (MARK_ROWS, speech.shape[1])
     ).astype(jnp.bfloat16)
+
+
+def unit_body(values, out):
+    out[...] = direction(values[...])[0].astype(jnp.bfloat16)
 
 
 def join_body(*refs):
@@ -258,14 +262,16 @@
         name="unit_rows",
     )(*[pltpu.with_memory_space_constraint(v, pltpu.HBM) for v in arguments])
 
-    def passed_on(block):
-        return call(join_body, bf16(own_text, width), [block], (), 1 << 29, name="pass_on")
+    def unit_far(block):
+        return call(unit_body, bf16(own_text, width), [block], (), 1 << 29, name="unit_far")
 
     text_blocks = [text_own] + [None] * (groups - 1)
     for k in [1 << i for i in reversed(range(groups.bit_length() - 1))]:
         for j in range(0, groups, 2 * k):
-            came = exchanged(text_blocks[j], "group", k)
-            text_blocks[j + k] = passed_on(came) if k > 1 else came
+            if k == groups // 2 and k > 1:
+                text_blocks[k] = unit_far(exchanged(sentence_vectors, "group", k))
+            else:
+                text_blocks[j + k] = exchanged(text_blocks[j], "group", k)
     square = chips == 4
     masks = [1, 2] if square else list(range(1, chips))
 

time: 40.9 us -> 41 us (level)
  transfers between devices with their start and end apart: 18 -> 18, of which waited for: 10 -> 10; matrix products, arithmetic and copies ran while one was open for 0% -> 0% of each run, Pallas kernels for 13% -> 16%
where the time goes in v24:
time: 41 us; the launch traced here: 40.8 us
  starting transfers between devices  20 us (49%)
  waiting for transfers between devices  11.3 us (28%)
  Pallas kernels  7.49 us (18%)
  between operations  2.06 us (5%)
    ppermute x18, starting transfers between devices, exchanged(): return lax.ppermute(value, axis, [(i, i ^ mask) for i in range(size)])  20 us
    ppermute x18, waiting for transfers between devices, exchanged(): return lax.ppermute(value, axis, [(i, i ^ mask) for i in range(size)])  11.3 us
    pallas_call x13, Pallas kernels, call(): pl.pallas_call(whole, out_shape=out_shape, in_specs=specs, out_specs=jax....  5.3 us
    pallas_call x1, Pallas kernels, shards(): pl.pallas_call(prepare_body, out_shape=[bf16(rows + MARK_ROWS, width), bf...  1.18 us
    pallas_call x1, Pallas kernels, shards(): pl.pallas_call(functools.partial(finish_body, len(back)), out_shape=resul...  1.02 us
  transfers between devices with their start and end apart: 18, of which 10 were waited for; matrix products, arithmetic and copies ran while one was open for 0% of the time, Pallas kernels for 16%

profile of v24, /device:TPU:0, one launch (start us, length us, event | category | flops | bytes accessed | tf_op | source)
XLA Modules:
  0.0 40.8 jit_solution(3682740745927427607)
XLA Ops:
  0.6 4.1 %collective-permute-start.1 = (bf16[64,768]{1,0:T(8,128)(2,1)}, bf16[64,768]{1,0:T(8,128)(2,1)S(1)}, u32[]{:S(2)}, u32[]{:S(2)}) collective-permute-start(bf16[64,768]{1,0:T(8,128)(2,1)} %refs_1_.1), channel_id=1, source_target_pairs={{0,16},{8,24},{16,0},{24,8},{1,17},{9,25},{17,1},{25,9},{2,18},{10... | collective-permute-start | bytes 294920 | tf_op jit(solution)/shard_map/ppermute | solution.py:18
  4.7 1.2 %unit_rows.1 = (bf16[136,768]{1,0:T(8,128)(2,1)S(1)}, bf16[64,768]{1,0:T(8,128)(2,1)S(1)}, bf16[128,768]{1,0:T(8,128)(2,1)S(1)}, bf16[64,768]{1,0:T(8,128)(2,1)S(1)}) custom-call(bf16[128,768]{1,0:T(8,128)(2,1)} %refs_0_.1, bf16[64,768]{1,0:T(8,128)(2,1)} %refs_1_.1, s32[1,128]{1,0:T(1,128)} %bitcast.5), custom_call_target="tpu_custom_call" | custom-call | tf_op jit(solution)/shard_map/unit_rows/pallas_call | solution.py:250
  5.9 2.5 %collective-permute-start.3 = (bf16[136,768]{1,0:T(8,128)(2,1)S(1)}, bf16[136,768]{1,0:T(8,128)(2,1)S(1)}, u32[]{:S(2)}, u32[]{:S(2)}) collective-permute-start(bf16[136,768]{1,0:T(8,128)(2,1)S(1)} %get-tuple-element.18.refs_4_), channel_id=1, source_target_pairs={{0,6},{1,7},{2,4},{3,5},{4,2},{5,3},{6,0},{7,1},{8,14},{9,15},{10,... | collective-permute-start | bytes 626696 | tf_op jit(solution)/shard_map/ppermute | solution.py:18
  8.4 0.5 %collective-permute-start.4 = (bf16[136,768]{1,0:T(8,128)(2,1)S(1)}, bf16[136,768]{1,0:T(8,128)(2,1)S(1)}, u32[]{:S(2)}, u32[]{:S(2)}) collective-permute-start(bf16[136,768]{1,0:T(8,128)(2,1)S(1)} %get-tuple-element.18.refs_4_), channel_id=1, source_target_pairs={{0,4},{1,5},{2,6},{3,7},{4,0},{5,1},{6,2},{7,3},{8,12},{9,13},{10,... | collective-permute-start | bytes 626696 | tf_op jit(solution)/shard_map/ppermute | solution.py:18
  8.9 0.5 %collective-permute-start.5 = (bf16[136,768]{1,0:T(8,128)(2,1)S(1)}, bf16[136,768]{1,0:T(8,128)(2,1)S(1)}, u32[]{:S(2)}, u32[]{:S(2)}) collective-permute-start(bf16[136,768]{1,0:T(8,128)(2,1)S(1)} %get-tuple-element.18.refs_4_), channel_id=1, source_target_pairs={{0,2},{1,3},{2,0},{3,1},{4,6},{5,7},{6,4},{7,5},{8,10},{9,11},{10,... | collective-permute-start | bytes 626696 | tf_op jit(solution)/shard_map/ppermute | solution.py:18
  9.5 1.6 %collective-permute-start = (bf16[64,768]{1,0:T(8,128)(2,1)S(1)}, bf16[64,768]{1,0:T(8,128)(2,1)S(1)}, u32[]{:S(2)}, u32[]{:S(2)}) collective-permute-start(bf16[64,768]{1,0:T(8,128)(2,1)S(1)} %get-tuple-element.17.refs_0_), channel_id=1, source_target_pairs={{0,8},{8,0},{16,24},{24,16},{1,9},{9,1},{17,25},{25,17},{2,10},{10... | collective-permute-start | bytes 294920 | tf_op jit(solution)/shard_map/ppermute | solution.py:18
  12.5 0.5 %collective-permute-start.2 = (bf16[64,768]{1,0:T(8,128)(2,1)S(1)}, bf16[64,768]{1,0:T(8,128)(2,1)S(1)}, u32[]{:S(2)}, u32[]{:S(2)}) collective-permute-start(bf16[64,768]{1,0:T(8,128)(2,1)S(1)} %unit_far.1.refs_2_), channel_id=1, source_target_pairs={{0,8},{8,0},{16,24},{24,16},{1,9},{9,1},{17,25},{25,17},{2,10},{10... | collective-permute-start | bytes 294920 | tf_op jit(solution)/shard_map/ppermute | solution.py:18
  13.0 1.7 %collective-permute-done.refs_1_ = bf16[64,768]{1,0:T(8,128)(2,1)S(1)} collective-permute-done((bf16[64,768]{1,0:T(8,128)(2,1)S(1)}, bf16[64,768]{1,0:T(8,128)(2,1)S(1)}, u32[]{:S(2)}, u32[]{:S(2)}) %collective-permute-start) | collective-permute-done | bytes 98336 | tf_op jit(solution)/shard_map/ppermute | solution.py:18
  14.7 2.5 %collective-permute-done.2.refs_3_ = bf16[64,768]{1,0:T(8,128)(2,1)S(1)} collective-permute-done((bf16[64,768]{1,0:T(8,128)(2,1)S(1)}, bf16[64,768]{1,0:T(8,128)(2,1)S(1)}, u32[]{:S(2)}, u32[]{:S(2)}) %collective-permute-start.2) | collective-permute-done | bytes 98336 | tf_op jit(solution)/shard_map/ppermute | solution.py:18
  17.2 0.8 %collective-permute-done.4.refs_6_ = bf16[136,768]{1,0:T(8,128)(2,1)S(1)} collective-permute-done((bf16[136,768]{1,0:T(8,128)(2,1)S(1)}, bf16[136,768]{1,0:T(8,128)(2,1)S(1)}, u32[]{:S(2)}, u32[]{:S(2)}) %collective-permute-start.4) | collective-permute-done | bytes 208928 | tf_op jit(solution)/shard_map/ppermute | solution.py:18
  18.3 1.6 %collective-permute-start.6 = (bf16[256,768]{1,0:T(8,128)(2,1)S(1)}, bf16[256,768]{1,0:T(8,128)(2,1)S(1)}, u32[]{:S(2)}, u32[]{:S(2)}) collective-permute-start(bf16[256,768]{1,0:T(8,128)(2,1)S(1)} %get-tuple-element.20.refs_1_.refs_2_), channel_id=1, source_target_pairs={{0,2},{1,3},{2,0},{3,1},{4,6},{5,7},{6,4},{7,5},{8,10},{9,11},{10,... | collective-permute-start | bytes 1179656 | tf_op jit(solution)/shard_map/ppermute | solution.py:18
  19.8 0.7 %collective-permute-start.7 = (bf16[256,768]{1,0:T(8,128)(2,1)S(1)}, bf16[256,768]{1,0:T(8,128)(2,1)S(1)}, u32[]{:S(2)}, u32[]{:S(2)}) collective-permute-start(bf16[256,768]{1,0:T(8,128)(2,1)S(1)} %get-tuple-element.20.refs_1_.refs_2_), channel_id=1, source_target_pairs={{0,4},{1,5},{2,6},{3,7},{4,0},{5,1},{6,2},{7,3},{8,12},{9,13},{10,... | collective-permute-start | bytes 1179656 | tf_op jit(solution)/shard_map/ppermute | solution.py:18
  20.6 1.3 %text_part.1 = (f32[64,768]{1,0:T(8,128)S(1)}, f32[64,768]{1,0:T(8,128)S(1)}, f32[64,384]{1,0:T(8,128)S(1)}, f32[64,384]{1,0:T(8,128)S(1)}, f32[64,384]{1,0:T(8,128)S(1)}, /*index=5*/f32[64,384]{1,0:T(8,128)S(1)}) custom-call(f32[2,1]{1,0:T(2,128)S(1)} %pad_maximum_fusion.refs_8_.refs_0_, bf16[256,768]{1,0:T(8,128)(2,1)S(1)} %get-tuple-element.20.refs_1_.refs_2_, ...), custom_call_target="tpu_custom_call" | custom-call | flops 805306368 | bytes 2801672 | tf_op jit(solution)/shard_map/text_part/pallas_call | solution.py:34
  21.9 1.6 %collective-permute-start.9 = (f32[64,384]{1,0:T(8,128)S(1)}, f32[64,384]{1,0:T(8,128)S(1)}, u32[]{:S(2)}, u32[]{:S(2)}) collective-permute-start(f32[64,384]{1,0:T(8,128)S(1)} %get-tuple-element.22), channel_id=1, source_target_pairs={{0,8},{8,0},{16,24},{24,16},{1,9},{9,1},{17,25},{25,17},{2,10},{10... | collective-permute-start | bytes 294920 | tf_op jit(solution)/shard_map/ppermute | solution.py:18
  23.5 0.5 %collective-permute-start.10 = (f32[64,384]{1,0:T(8,128)S(1)}, f32[64,384]{1,0:T(8,128)S(1)}, u32[]{:S(2)}, u32[]{:S(2)}) collective-permute-start(f32[64,384]{1,0:T(8,128)S(1)} %get-tuple-element.24), channel_id=1, source_target_pairs={{0,8},{8,0},{16,24},{24,16},{1,9},{9,1},{17,25},{25,17},{2,10},{10... | collective-permute-start | bytes 294920 | tf_op jit(solution)/shard_map/ppermute | solution.py:18
  24.0 1.6 %collective-permute-start.17 = (f32[64,768]{1,0:T(8,128)S(1)}, f32[64,768]{1,0:T(8,128)S(1)}, u32[]{:S(2)}, u32[]{:S(2)}) collective-permute-start(f32[64,768]{1,0:T(8,128)S(1)} %get-tuple-element.28), channel_id=1, source_target_pairs={{0,8},{8,0},{16,24},{24,16},{1,9},{9,1},{17,25},{25,17},{2,10},{10... | collective-permute-start | bytes 589832 | tf_op jit(solution)/shard_map/ppermute | solution.py:18
  25.6 2.0 %collective-permute-done.9.refs_1_ = f32[64,384]{1,0:T(8,128)S(1)} collective-permute-done((f32[64,384]{1,0:T(8,128)S(1)}, f32[64,384]{1,0:T(8,128)S(1)}, u32[]{:S(2)}, u32[]{:S(2)}) %collective-permute-start.9) | collective-permute-done | bytes 98336 | tf_op jit(solution)/shard_map/ppermute | solution.py:18
  27.6 0.4 collective-permute-start.15
  28.0 1.8 %collective-permute-done.6.refs_0_.refs_3_ = bf16[256,768]{1,0:T(8,128)(2,1)S(1)} collective-permute-done((bf16[256,768]{1,0:T(8,128)(2,1)S(1)}, bf16[256,768]{1,0:T(8,128)(2,1)S(1)}, u32[]{:S(2)}, u32[]{:S(2)}) %collective-permute-start.6) | collective-permute-done | bytes 393248 | tf_op jit(solution)/shard_map/ppermute | solution.py:18
  29.8 1.5 %collective-permute-start.12 = (bf16[128,768]{1,0:T(8,128)(2,1)S(1)}, bf16[128,768]{1,0:T(8,128)(2,1)S(1)}, u32[]{:S(2)}, u32[]{:S(2)}) collective-permute-start(bf16[128,768]{1,0:T(8,128)(2,1)S(1)} %cut.3.refs_3_), channel_id=1, source_target_pairs={{0,4},{1,5},{2,6},{3,7},{4,0},{5,1},{6,2},{7,3},{8,12},{9,13},{10,... | collective-permute-start | bytes 589832 | tf_op jit(solution)/shard_map/ppermute | solution.py:18
  31.3 0.9 %collective-permute-start.11 = (bf16[128,768]{1,0:T(8,128)(2,1)S(1)}, bf16[128,768]{1,0:T(8,128)(2,1)S(1)}, u32[]{:S(2)}, u32[]{:S(2)}) collective-permute-start(bf16[128,768]{1,0:T(8,128)(2,1)S(1)} %cut.2.refs_2_), channel_id=1, source_target_pairs={{0,2},{1,3},{2,0},{3,1},{4,6},{5,7},{6,4},{7,5},{8,10},{9,11},{10,... | collective-permute-start | bytes 589832 | tf_op jit(solution)/shard_map/ppermute | solution.py:18
  32.2 0.9 %collective-permute-start.16 = (f32[64,384]{1,0:T(8,128)S(1)}, f32[64,384]{1,0:T(8,128)S(1)}, u32[]{:S(2)}, u32[]{:S(2)}) collective-permute-start(f32[64,384]{1,0:T(8,128)S(1)} %sum_near.3.refs_6_), channel_id=1, source_target_pairs={{0,16},{8,24},{16,0},{24,8},{1,17},{9,25},{17,1},{25,9},{2,18},{10... | collective-permute-start | bytes 294920 | tf_op jit(solution)/shard_map/ppermute | solution.py:18
  33.1 1.0 %speech_part.5.refs_2_ = f32[128,768]{1,0:T(8,128)S(1)} custom-call(f32[2,1]{1,0:T(2,128)S(1)} %pad_maximum_fusion.refs_8_.refs_0_, bf16[528,768]{1,0:T(8,128)(2,1)S(1)} %get-tuple-element.19.refs_2_.refs_1_, bf16[256,768]{1,0:T(8,128)(2,1)S(1)} %get-tuple-element.20.refs_1_.refs_2_, bf16[256,768]{1,0:T(8,128)(2,1)S(1)} %collective-permute-done.6.refs_0_.refs_3_, ...), custom_call_target="tpu_custom_call" | custom-call | flops 3019898880 | bytes 2383880 | tf_op jit(solution)/shard_map/speech_part/pallas_call | solution.py:34
  34.1 1.0 %speech_part.7.refs_2_ = f32[128,768]{1,0:T(8,128)S(1)} custom-call(f32[2,1]{1,0:T(2,128)S(1)} %pad_maximum_fusion.refs_8_.refs_0_, bf16[528,768]{1,0:T(8,128)(2,1)S(1)} %collective-permute-done.8.refs_3_.refs_1_, bf16[256,768]{1,0:T(8,128)(2,1)S(1)} %get-tuple-element.20.refs_1_.refs_2_, bf16[256,768]{1,0:T(8,128)(2,1)S(1)} %collective-permute-done.6.refs_0_.refs_3_, ...), custom_call_target="tpu_custom_call" | custom-call | flops 3019898880 | bytes 2383880 | tf_op jit(solution)/shard_map/speech_part/pallas_call | solution.py:34
  35.2 1.2 %collective-permute-done.12.refs_4_.refs_3_ = bf16[128,768]{1,0:T(8,128)(2,1)S(1)} collective-permute-done((bf16[128,768]{1,0:T(8,128)(2,1)S(1)}, bf16[128,768]{1,0:T(8,128)(2,1)S(1)}, u32[]{:S(2)}, u32[]{:S(2)}) %collective-permute-start.12) | collective-permute-done | bytes 196640 | tf_op jit(solution)/shard_map/ppermute | solution.py:18
  36.3 0.5 %speech_part.8.refs_2_ = f32[128,768]{1,0:T(8,128)S(1)} custom-call(f32[2,1]{1,0:T(2,128)S(1)} %pad_maximum_fusion.refs_8_.refs_0_, bf16[528,768]{1,0:T(8,128)(2,1)S(1)} %collective-permute-done.8.refs_3_.refs_1_, f32[128,768]{1,0:T(8,128)S(1)} %speech_part.7.refs_2_, bf16[128,768]{1,0:T(8,128)(2,1)S(1)} %collective-permute-done.12.refs_4_.refs_3_), custom_call_target="tpu_custom_call" | custom-call | flops 503316480 | bytes 1794056 | tf_op jit(solution)/shard_map/speech_part/pallas_call | solution.py:34
  36.8 0.8 %collective-permute-done.11.refs_3_ = bf16[128,768]{1,0:T(8,128)(2,1)S(1)} collective-permute-done((bf16[128,768]{1,0:T(8,128)(2,1)S(1)}, bf16[128,768]{1,0:T(8,128)(2,1)S(1)}, u32[]{:S(2)}, u32[]{:S(2)}) %collective-permute-start.11) | collective-permute-done | bytes 196640 | tf_op jit(solution)/shard_map/ppermute | solution.py:18
  37.6 0.5 %speech_part.9 = (f32[64,768]{1,0:T(8,128)S(1)}, f32[64,768]{1,0:T(8,128)S(1)}) custom-call(f32[2,1]{1,0:T(2,128)S(1)} %pad_maximum_fusion.refs_8_.refs_0_, bf16[528,768]{1,0:T(8,128)(2,1)S(1)} %collective-permute-done.8.refs_3_.refs_1_, f32[128,768]{1,0:T(8,128)S(1)} %speech_part.8.refs_2_, bf16[128,768]{1,0:T(8,128)(2,1)S(1)} %collective-permute-done.11.refs_3_), custom_call_target="tpu_custom_call" | custom-call | flops 503316480 | bytes 1794056 | tf_op jit(solution)/shard_map/speech_part/pallas_call | solution.py:34
  38.1 0.5 %collective-permute-start.14 = (f32[64,768]{1,0:T(8,128)S(1)}, f32[64,768]{1,0:T(8,128)S(1)}, u32[]{:S(2)}, u32[]{:S(2)}) collective-permute-start(f32[64,768]{1,0:T(8,128)S(1)} %get-tuple-element.26), channel_id=1, source_target_pairs={{0,1},{1,0},{2,3},{3,2},{4,5},{5,4},{6,7},{7,6},{8,9},{9,8},{10,11... | collective-permute-start | bytes 589832 | tf_op jit(solution)/shard_map/ppermute | solution.py:18
  38.6 0.7 %speech_part.6.refs_4_.home = f32[128,768]{1,0:T(8,128)S(1)} custom-call(f32[2,1]{1,0:T(2,128)S(1)} %pad_maximum_fusion.refs_8_.refs_0_, bf16[528,768]{1,0:T(8,128)(2,1)S(1)} %get-tuple-element.19.refs_2_.refs_1_, f32[128,768]{1,0:T(8,128)S(1)} %speech_part.5.refs_2_, bf16[128,768]{1,0:T(8,128)(2,1)S(1)} %collective-permute-done.11.refs_3_, ...), custom_call_target="tpu_custom_call" | custom-call | flops 1006632960 | bytes 1990664 | tf_op jit(solution)/shard_map/speech_part/pallas_call | solution.py:34
  39.5 0.3 collective-permute-done.14.refs_1_
  39.8 1.0 %finish.1 = (f32[128,768]{1,0:T(8,128)}, f32[64,768]{1,0:T(8,128)}) custom-call(bf16[128,768]{1,0:T(8,128)(2,1)S(1)} %get-tuple-element.16.audio, f32[128,768]{1,0:T(8,128)S(1)} %speech_part.6.refs_4_.home, f32[64,768]{1,0:T(8,128)S(1)} %collective-permute-done.13.refs_0_, f32[64,768]{1,0:T(8,128)S(1)} %collective-permute-done.14.refs_1_, ...), custom_call_target="tpu_custom_call" | custom-call | tf_op jit(solution)/shard_map/finish/pallas_call | solution.py:360
  (20 shorter events, 0.8 us)
Async XLA Ops:
  0.6 11.7 %collective-permute-start.1 = (bf16[64,768]{1,0:T(8,128)(2,1)}, bf16[64,768]{1,0:T(8,128)(2,1)S(1)}, u32[]{:S(2)}, u32[]{:S(2)}) collective-permute-start(bf16[64,768]{1,0:T(8,128)(2,1)} %refs_1_.1), channel_id=1, source_target_pairs={{0,16},{8,24},{16,0},{24,8},{1,17},{9,25},{17,1},{25,9},{2,18},{10... | collective-permute-start | bytes 294920 | tf_op jit(solution)/shard_map/ppermute | solution.py:18
  5.9 11.3 %collective-permute-start.3 = (bf16[136,768]{1,0:T(8,128)(2,1)S(1)}, bf16[136,768]{1,0:T(8,128)(2,1)S(1)}, u32[]{:S(2)}, u32[]{:S(2)}) collective-permute-start(bf16[136,768]{1,0:T(8,128)(2,1)S(1)} %get-tuple-element.18.refs_4_), channel_id=1, source_target_pairs={{0,6},{1,7},{2,4},{3,5},{4,2},{5,3},{6,0},{7,1},{8,14},{9,15},{10,... | collective-permute-start | bytes 626696 | tf_op jit(solution)/shard_map/ppermute | solution.py:18
  8.4 9.6 %collective-permute-start.4 = (bf16[136,768]{1,0:T(8,128)(2,1)S(1)}, bf16[136,768]{1,0:T(8,128)(2,1)S(1)}, u32[]{:S(2)}, u32[]{:S(2)}) collective-permute-start(bf16[136,768]{1,0:T(8,128)(2,1)S(1)} %get-tuple-element.18.refs_4_), channel_id=1, source_target_pairs={{0,4},{1,5},{2,6},{3,7},{4,0},{5,1},{6,2},{7,3},{8,12},{9,13},{10,... | collective-permute-start | bytes 626696 | tf_op jit(solution)/shard_map/ppermute | solution.py:18
  8.9 9.1 %collective-permute-start.5 = (bf16[136,768]{1,0:T(8,128)(2,1)S(1)}, bf16[136,768]{1,0:T(8,128)(2,1)S(1)}, u32[]{:S(2)}, u32[]{:S(2)}) collective-permute-start(bf16[136,768]{1,0:T(8,128)(2,1)S(1)} %get-tuple-element.18.refs_4_), channel_id=1, source_target_pairs={{0,2},{1,3},{2,0},{3,1},{4,6},{5,7},{6,4},{7,5},{8,10},{9,11},{10,... | collective-permute-start | bytes 626696 | tf_op jit(solution)/shard_map/ppermute | solution.py:18
  9.5 5.2 %collective-permute-start = (bf16[64,768]{1,0:T(8,128)(2,1)S(1)}, bf16[64,768]{1,0:T(8,128)(2,1)S(1)}, u32[]{:S(2)}, u32[]{:S(2)}) collective-permute-start(bf16[64,768]{1,0:T(8,128)(2,1)S(1)} %get-tuple-element.17.refs_0_), channel_id=1, source_target_pairs={{0,8},{8,0},{16,24},{24,16},{1,9},{9,1},{17,25},{25,17},{2,10},{10... | collective-permute-start | bytes 294920 | tf_op jit(solution)/shard_map/ppermute | solution.py:18
  12.5 4.7 %collective-permute-start.2 = (bf16[64,768]{1,0:T(8,128)(2,1)S(1)}, bf16[64,768]{1,0:T(8,128)(2,1)S(1)}, u32[]{:S(2)}, u32[]{:S(2)}) collective-permute-start(bf16[64,768]{1,0:T(8,128)(2,1)S(1)} %unit_far.1.refs_2_), channel_id=1, source_target_pairs={{0,8},{8,0},{16,24},{24,16},{1,9},{9,1},{17,25},{25,17},{2,10},{10... | collective-permute-start | bytes 294920 | tf_op jit(solution)/shard_map/ppermute | solution.py:18
  18.2 2.4 %collective-permute-start.8 = (bf16[528,768]{1,0:T(8,128)(2,1)S(1)}, bf16[528,768]{1,0:T(8,128)(2,1)S(1)}, u32[]{:S(2)}, u32[]{:S(2)}) collective-permute-start(bf16[528,768]{1,0:T(8,128)(2,1)S(1)} %get-tuple-element.19.refs_2_.refs_1_), channel_id=1, source_target_pairs={{0,1},{1,0},{2,3},{3,2},{4,5},{5,4},{6,7},{7,6},{8,9},{9,8},{10,11... | collective-permute-start | bytes 2433032 | tf_op jit(solution)/shard_map/ppermute | solution.py:18
  18.3 11.5 %collective-permute-start.6 = (bf16[256,768]{1,0:T(8,128)(2,1)S(1)}, bf16[256,768]{1,0:T(8,128)(2,1)S(1)}, u32[]{:S(2)}, u32[]{:S(2)}) collective-permute-start(bf16[256,768]{1,0:T(8,128)(2,1)S(1)} %get-tuple-element.20.refs_1_.refs_2_), channel_id=1, source_target_pairs={{0,2},{1,3},{2,0},{3,1},{4,6},{5,7},{6,4},{7,5},{8,10},{9,11},{10,... | collective-permute-start | bytes 1179656 | tf_op jit(solution)/shard_map/ppermute | solution.py:18
  19.8 11.5 %collective-permute-start.7 = (bf16[256,768]{1,0:T(8,128)(2,1)S(1)}, bf16[256,768]{1,0:T(8,128)(2,1)S(1)}, u32[]{:S(2)}, u32[]{:S(2)}) collective-permute-start(bf16[256,768]{1,0:T(8,128)(2,1)S(1)} %get-tuple-element.20.refs_1_.refs_2_), channel_id=1, source_target_pairs={{0,4},{1,5},{2,6},{3,7},{4,0},{5,1},{6,2},{7,3},{8,12},{9,13},{10,... | collective-permute-start | bytes 1179656 | tf_op jit(solution)/shard_map/ppermute | solution.py:18
  21.9 5.7 %collective-permute-start.9 = (f32[64,384]{1,0:T(8,128)S(1)}, f32[64,384]{1,0:T(8,128)S(1)}, u32[]{:S(2)}, u32[]{:S(2)}) collective-permute-start(f32[64,384]{1,0:T(8,128)S(1)} %get-tuple-element.22), channel_id=1, source_target_pairs={{0,8},{8,0},{16,24},{24,16},{1,9},{9,1},{17,25},{25,17},{2,10},{10... | collective-permute-start | bytes 294920 | tf_op jit(solution)/shard_map/ppermute | solution.py:18
  23.5 8.6 %collective-permute-start.10 = (f32[64,384]{1,0:T(8,128)S(1)}, f32[64,384]{1,0:T(8,128)S(1)}, u32[]{:S(2)}, u32[]{:S(2)}) collective-permute-start(f32[64,384]{1,0:T(8,128)S(1)} %get-tuple-element.24), channel_id=1, source_target_pairs={{0,8},{8,0},{16,24},{24,16},{1,9},{9,1},{17,25},{25,17},{2,10},{10... | collective-permute-start | bytes 294920 | tf_op jit(solution)/shard_map/ppermute | solution.py:18
  24.0 15.3 %collective-permute-start.17 = (f32[64,768]{1,0:T(8,128)S(1)}, f32[64,768]{1,0:T(8,128)S(1)}, u32[]{:S(2)}, u32[]{:S(2)}) collective-permute-start(f32[64,768]{1,0:T(8,128)S(1)} %get-tuple-element.28), channel_id=1, source_target_pairs={{0,8},{8,0},{16,24},{24,16},{1,9},{9,1},{17,25},{25,17},{2,10},{10... | collective-permute-start | bytes 589832 | tf_op jit(solution)/shard_map/ppermute | solution.py:18
  27.6 11.9 %collective-permute-start.15 = (f32[64,384]{1,0:T(8,128)S(1)}, f32[64,384]{1,0:T(8,128)S(1)}, u32[]{:S(2)}, u32[]{:S(2)}) collective-permute-start(f32[64,384]{1,0:T(8,128)S(1)} %sum_near.2.refs_1_.refs_5_), channel_id=1, source_target_pairs={{0,16},{8,24},{16,0},{24,8},{1,17},{9,25},{17,1},{25,9},{2,18},{10... | collective-permute-start | bytes 294920 | tf_op jit(solution)/shard_map/ppermute | solution.py:18
  29.8 6.5 %collective-permute-start.12 = (bf16[128,768]{1,0:T(8,128)(2,1)S(1)}, bf16[128,768]{1,0:T(8,128)(2,1)S(1)}, u32[]{:S(2)}, u32[]{:S(2)}) collective-permute-start(bf16[128,768]{1,0:T(8,128)(2,1)S(1)} %cut.3.refs_3_), channel_id=1, source_target_pairs={{0,4},{1,5},{2,6},{3,7},{4,0},{5,1},{6,2},{7,3},{8,12},{9,13},{10,... | collective-permute-start | bytes 589832 | tf_op jit(solution)/shard_map/ppermute | solution.py:18
  31.3 6.3 %collective-permute-start.11 = (bf16[128,768]{1,0:T(8,128)(2,1)S(1)}, bf16[128,768]{1,0:T(8,128)(2,1)S(1)}, u32[]{:S(2)}, u32[]{:S(2)}) collective-permute-start(bf16[128,768]{1,0:T(8,128)(2,1)S(1)} %cut.2.refs_2_), channel_id=1, source_target_pairs={{0,2},{1,3},{2,0},{3,1},{4,6},{5,7},{6,4},{7,5},{8,10},{9,11},{10,... | collective-permute-start | bytes 589832 | tf_op jit(solution)/shard_map/ppermute | solution.py:18
  32.2 7.3 %collective-permute-start.16 = (f32[64,384]{1,0:T(8,128)S(1)}, f32[64,384]{1,0:T(8,128)S(1)}, u32[]{:S(2)}, u32[]{:S(2)}) collective-permute-start(f32[64,384]{1,0:T(8,128)S(1)} %sum_near.3.refs_6_), channel_id=1, source_target_pairs={{0,16},{8,24},{16,0},{24,8},{1,17},{9,25},{17,1},{25,9},{2,18},{10... | collective-permute-start | bytes 294920 | tf_op jit(solution)/shard_map/ppermute | solution.py:18
  38.0 1.5 %collective-permute-start.13 = (f32[64,768]{1,0:T(8,128)S(1)}, f32[64,768]{1,0:T(8,128)S(1)}, u32[]{:S(2)}, u32[]{:S(2)}) collective-permute-start(f32[64,768]{1,0:T(8,128)S(1)} %get-tuple-element.25), channel_id=1, source_target_pairs={{0,1},{1,0},{2,3},{3,2},{4,5},{5,4},{6,7},{7,6},{8,9},{9,8},{10,11... | collective-permute-start | bytes 589832 | tf_op jit(solution)/shard_map/ppermute | solution.py:18
  38.1 1.7 %collective-permute-start.14 = (f32[64,768]{1,0:T(8,128)S(1)}, f32[64,768]{1,0:T(8,128)S(1)}, u32[]{:S(2)}, u32[]{:S(2)}) collective-permute-start(f32[64,768]{1,0:T(8,128)S(1)} %get-tuple-element.26), channel_id=1, source_target_pairs={{0,1},{1,0},{2,3},{3,2},{4,5},{5,4},{6,7},{7,6},{8,9},{9,8},{10,11... | collective-permute-start | bytes 589832 | tf_op jit(solution)/shard_map/ppermute | solution.py:18

commit v25 on v24

--- a/solution.py
+++ b/solution.py
@@ -342,7 +342,7 @@
         home = speech_part(speech, [], *near)
         far_places = [(3, 0), (3, groups // 2)]
         away = speech_part(other, away, far_places[1:], text_far[1:])
-        away = speech_part(other, away, far_places[:1], text_far[:1], pieces=2)
+        away = speech_part(other, away, far_places[:1], text_far[:1])
         home = speech_part(speech, home, far_places, text_far)
     else:
         away = speech_part(other, [], *near, pieces=2)

time: 41 us -> 41 us (level)
  starting transfers between devices: 20 us -> 19.5 us
  waiting for transfers between devices: 11.3 us -> 11.8 us
    ppermute x18 -> x17, waiting for transfers between devices: 11.3 us -> 11.8 us  [exchanged(): return lax.ppermute(value, axis, [(i, i ^ mask) for i in range(size)])]
    ppermute x18 -> x17, starting transfers between devices: 20 us -> 19.5 us  [exchanged(): return lax.ppermute(value, axis, [(i, i ^ mask) for i in range(size)])]
  transfers between devices with their start and end apart: 18 -> 17, of which waited for: 10 -> 10; matrix products, arithmetic and copies ran while one was open for 0% -> 0% of each run, Pallas kernels for 16% -> 16%
where the time goes in v25:
time: 41 us; the launch traced here: 40.8 us
  starting transfers between devices  19.5 us (48%)
  waiting for transfers between devices  11.8 us (29%)
  Pallas kernels  7.49 us (18%)
  between operations  2.05 us (5%)
    ppermute x17, starting transfers between devices, exchanged(): return lax.ppermute(value, axis, [(i, i ^ mask) for i in range(size)])  19.5 us
    ppermute x17, waiting for transfers between devices, exchanged(): return lax.ppermute(value, axis, [(i, i ^ mask) for i in range(size)])  11.8 us
    pallas_call x13, Pallas kernels, call(): pl.pallas_call(whole, out_shape=out_shape, in_specs=specs, out_specs=jax....  5.3 us
    pallas_call x1, Pallas kernels, shards(): pl.pallas_call(prepare_body, out_shape=[bf16(rows + MARK_ROWS, width), bf...  1.18 us
    pallas_call x1, Pallas kernels, shards(): pl.pallas_call(functools.partial(finish_body, len(back)), out_shape=resul...  1.02 us
  transfers between devices with their start and end apart: 17, of which 10 were waited for; matrix products, arithmetic and copies ran while one was open for 0% of the time, Pallas kernels for 16%

profile of v25, /device:TPU:0, one launch (start us, length us, event | category | flops | bytes accessed | tf_op | source)
XLA Modules:
  0.0 40.8 jit_solution(10487653800287754432)
XLA Ops:
  0.6 4.1 %collective-permute-start.1 = (bf16[64,768]{1,0:T(8,128)(2,1)}, bf16[64,768]{1,0:T(8,128)(2,1)S(1)}, u32[]{:S(2)}, u32[]{:S(2)}) collective-permute-start(bf16[64,768]{1,0:T(8,128)(2,1)} %refs_1_.1), channel_id=1, source_target_pairs={{0,16},{8,24},{16,0},{24,8},{1,17},{9,25},{17,1},{25,9},{2,18},{10... | collective-permute-start | bytes 294920 | tf_op jit(solution)/shard_map/ppermute | solution.py:18
  4.7 1.2 %unit_rows.1 = (bf16[136,768]{1,0:T(8,128)(2,1)S(1)}, bf16[64,768]{1,0:T(8,128)(2,1)S(1)}, bf16[128,768]{1,0:T(8,128)(2,1)S(1)}, bf16[64,768]{1,0:T(8,128)(2,1)S(1)}) custom-call(bf16[128,768]{1,0:T(8,128)(2,1)} %refs_0_.1, bf16[64,768]{1,0:T(8,128)(2,1)} %refs_1_.1, s32[1,128]{1,0:T(1,128)} %bitcast.5), custom_call_target="tpu_custom_call" | custom-call | tf_op jit(solution)/shard_map/unit_rows/pallas_call | solution.py:250
  5.9 2.5 %collective-permute-start.3 = (bf16[136,768]{1,0:T(8,128)(2,1)S(1)}, bf16[136,768]{1,0:T(8,128)(2,1)S(1)}, u32[]{:S(2)}, u32[]{:S(2)}) collective-permute-start(bf16[136,768]{1,0:T(8,128)(2,1)S(1)} %get-tuple-element.16.refs_4_), channel_id=1, source_target_pairs={{0,6},{1,7},{2,4},{3,5},{4,2},{5,3},{6,0},{7,1},{8,14},{9,15},{10,... | collective-permute-start | bytes 626696 | tf_op jit(solution)/shard_map/ppermute | solution.py:18
  8.4 0.5 %collective-permute-start.4 = (bf16[136,768]{1,0:T(8,128)(2,1)S(1)}, bf16[136,768]{1,0:T(8,128)(2,1)S(1)}, u32[]{:S(2)}, u32[]{:S(2)}) collective-permute-start(bf16[136,768]{1,0:T(8,128)(2,1)S(1)} %get-tuple-element.16.refs_4_), channel_id=1, source_target_pairs={{0,4},{1,5},{2,6},{3,7},{4,0},{5,1},{6,2},{7,3},{8,12},{9,13},{10,... | collective-permute-start | bytes 626696 | tf_op jit(solution)/shard_map/ppermute | solution.py:18
  8.9 0.5 %collective-permute-start.5 = (bf16[136,768]{1,0:T(8,128)(2,1)S(1)}, bf16[136,768]{1,0:T(8,128)(2,1)S(1)}, u32[]{:S(2)}, u32[]{:S(2)}) collective-permute-start(bf16[136,768]{1,0:T(8,128)(2,1)S(1)} %get-tuple-element.16.refs_4_), channel_id=1, source_target_pairs={{0,2},{1,3},{2,0},{3,1},{4,6},{5,7},{6,4},{7,5},{8,10},{9,11},{10,... | collective-permute-start | bytes 626696 | tf_op jit(solution)/shard_map/ppermute | solution.py:18
  9.5 1.6 %collective-permute-start = (bf16[64,768]{1,0:T(8,128)(2,1)S(1)}, bf16[64,768]{1,0:T(8,128)(2,1)S(1)}, u32[]{:S(2)}, u32[]{:S(2)}) collective-permute-start(bf16[64,768]{1,0:T(8,128)(2,1)S(1)} %get-tuple-element.15.refs_0_), channel_id=1, source_target_pairs={{0,8},{8,0},{16,24},{24,16},{1,9},{9,1},{17,25},{25,17},{2,10},{10... | collective-permute-start | bytes 294920 | tf_op jit(solution)/shard_map/ppermute | solution.py:18
  12.5 0.5 %collective-permute-start.2 = (bf16[64,768]{1,0:T(8,128)(2,1)S(1)}, bf16[64,768]{1,0:T(8,128)(2,1)S(1)}, u32[]{:S(2)}, u32[]{:S(2)}) collective-permute-start(bf16[64,768]{1,0:T(8,128)(2,1)S(1)} %unit_far.1.refs_2_), channel_id=1, source_target_pairs={{0,8},{8,0},{16,24},{24,16},{1,9},{9,1},{17,25},{25,17},{2,10},{10... | collective-permute-start | bytes 294920 | tf_op jit(solution)/shard_map/ppermute | solution.py:18
  13.0 1.7 %collective-permute-done.refs_1_ = bf16[64,768]{1,0:T(8,128)(2,1)S(1)} collective-permute-done((bf16[64,768]{1,0:T(8,128)(2,1)S(1)}, bf16[64,768]{1,0:T(8,128)(2,1)S(1)}, u32[]{:S(2)}, u32[]{:S(2)}) %collective-permute-start) | collective-permute-done | bytes 98336 | tf_op jit(solution)/shard_map/ppermute | solution.py:18
  14.7 2.5 %collective-permute-done.2.refs_3_ = bf16[64,768]{1,0:T(8,128)(2,1)S(1)} collective-permute-done((bf16[64,768]{1,0:T(8,128)(2,1)S(1)}, bf16[64,768]{1,0:T(8,128)(2,1)S(1)}, u32[]{:S(2)}, u32[]{:S(2)}) %collective-permute-start.2) | collective-permute-done | bytes 98336 | tf_op jit(solution)/shard_map/ppermute | solution.py:18
  17.2 0.8 %collective-permute-done.4.refs_6_ = bf16[136,768]{1,0:T(8,128)(2,1)S(1)} collective-permute-done((bf16[136,768]{1,0:T(8,128)(2,1)S(1)}, bf16[136,768]{1,0:T(8,128)(2,1)S(1)}, u32[]{:S(2)}, u32[]{:S(2)}) %collective-permute-start.4) | collective-permute-done | bytes 208928 | tf_op jit(solution)/shard_map/ppermute | solution.py:18
  18.3 1.6 %collective-permute-start.6 = (bf16[256,768]{1,0:T(8,128)(2,1)S(1)}, bf16[256,768]{1,0:T(8,128)(2,1)S(1)}, u32[]{:S(2)}, u32[]{:S(2)}) collective-permute-start(bf16[256,768]{1,0:T(8,128)(2,1)S(1)} %get-tuple-element.18.refs_1_.refs_2_), channel_id=1, source_target_pairs={{0,2},{1,3},{2,0},{3,1},{4,6},{5,7},{6,4},{7,5},{8,10},{9,11},{10,... | collective-permute-start | bytes 1179656 | tf_op jit(solution)/shard_map/ppermute | solution.py:18
  19.8 0.7 %collective-permute-start.7 = (bf16[256,768]{1,0:T(8,128)(2,1)S(1)}, bf16[256,768]{1,0:T(8,128)(2,1)S(1)}, u32[]{:S(2)}, u32[]{:S(2)}) collective-permute-start(bf16[256,768]{1,0:T(8,128)(2,1)S(1)} %get-tuple-element.18.refs_1_.refs_2_), channel_id=1, source_target_pairs={{0,4},{1,5},{2,6},{3,7},{4,0},{5,1},{6,2},{7,3},{8,12},{9,13},{10,... | collective-permute-start | bytes 1179656 | tf_op jit(solution)/shard_map/ppermute | solution.py:18
  20.6 1.3 %text_part.1 = (f32[64,768]{1,0:T(8,128)S(1)}, f32[64,768]{1,0:T(8,128)S(1)}, f32[64,384]{1,0:T(8,128)S(1)}, f32[64,384]{1,0:T(8,128)S(1)}, f32[64,384]{1,0:T(8,128)S(1)}, /*index=5*/f32[64,384]{1,0:T(8,128)S(1)}) custom-call(f32[2,1]{1,0:T(2,128)S(1)} %pad_maximum_fusion.refs_8_.refs_0_, bf16[256,768]{1,0:T(8,128)(2,1)S(1)} %get-tuple-element.18.refs_1_.refs_2_, ...), custom_call_target="tpu_custom_call" | custom-call | flops 805306368 | bytes 2801672 | tf_op jit(solution)/shard_map/text_part/pallas_call | solution.py:34
  21.9 1.6 %collective-permute-start.9 = (f32[64,384]{1,0:T(8,128)S(1)}, f32[64,384]{1,0:T(8,128)S(1)}, u32[]{:S(2)}, u32[]{:S(2)}) collective-permute-start(f32[64,384]{1,0:T(8,128)S(1)} %get-tuple-element.20), channel_id=1, source_target_pairs={{0,8},{8,0},{16,24},{24,16},{1,9},{9,1},{17,25},{25,17},{2,10},{10... | collective-permute-start | bytes 294920 | tf_op jit(solution)/shard_map/ppermute | solution.py:18
  23.5 0.5 %collective-permute-start.10 = (f32[64,384]{1,0:T(8,128)S(1)}, f32[64,384]{1,0:T(8,128)S(1)}, u32[]{:S(2)}, u32[]{:S(2)}) collective-permute-start(f32[64,384]{1,0:T(8,128)S(1)} %get-tuple-element.22), channel_id=1, source_target_pairs={{0,8},{8,0},{16,24},{24,16},{1,9},{9,1},{17,25},{25,17},{2,10},{10... | collective-permute-start | bytes 294920 | tf_op jit(solution)/shard_map/ppermute | solution.py:18
  24.0 1.6 %collective-permute-start.16 = (f32[64,768]{1,0:T(8,128)S(1)}, f32[64,768]{1,0:T(8,128)S(1)}, u32[]{:S(2)}, u32[]{:S(2)}) collective-permute-start(f32[64,768]{1,0:T(8,128)S(1)} %get-tuple-element.24), channel_id=1, source_target_pairs={{0,8},{8,0},{16,24},{24,16},{1,9},{9,1},{17,25},{25,17},{2,10},{10... | collective-permute-start | bytes 589832 | tf_op jit(solution)/shard_map/ppermute | solution.py:18
  25.6 2.0 %collective-permute-done.9.refs_1_ = f32[64,384]{1,0:T(8,128)S(1)} collective-permute-done((f32[64,384]{1,0:T(8,128)S(1)}, f32[64,384]{1,0:T(8,128)S(1)}, u32[]{:S(2)}, u32[]{:S(2)}) %collective-permute-start.9) | collective-permute-done | bytes 98336 | tf_op jit(solution)/shard_map/ppermute | solution.py:18
  27.6 0.4 collective-permute-start.14
  28.0 1.8 %collective-permute-done.6.refs_0_.refs_3_ = bf16[256,768]{1,0:T(8,128)(2,1)S(1)} collective-permute-done((bf16[256,768]{1,0:T(8,128)(2,1)S(1)}, bf16[256,768]{1,0:T(8,128)(2,1)S(1)}, u32[]{:S(2)}, u32[]{:S(2)}) %collective-permute-start.6) | collective-permute-done | bytes 393248 | tf_op jit(solution)/shard_map/ppermute | solution.py:18
  29.8 1.5 %collective-permute-start.12 = (bf16[128,768]{1,0:T(8,128)(2,1)S(1)}, bf16[128,768]{1,0:T(8,128)(2,1)S(1)}, u32[]{:S(2)}, u32[]{:S(2)}) collective-permute-start(bf16[128,768]{1,0:T(8,128)(2,1)S(1)} %cut.3.refs_3_), channel_id=1, source_target_pairs={{0,4},{1,5},{2,6},{3,7},{4,0},{5,1},{6,2},{7,3},{8,12},{9,13},{10,... | collective-permute-start | bytes 589832 | tf_op jit(solution)/shard_map/ppermute | solution.py:18
  31.3 0.9 %collective-permute-start.11 = (bf16[128,768]{1,0:T(8,128)(2,1)S(1)}, bf16[128,768]{1,0:T(8,128)(2,1)S(1)}, u32[]{:S(2)}, u32[]{:S(2)}) collective-permute-start(bf16[128,768]{1,0:T(8,128)(2,1)S(1)} %cut.2.refs_2_), channel_id=1, source_target_pairs={{0,2},{1,3},{2,0},{3,1},{4,6},{5,7},{6,4},{7,5},{8,10},{9,11},{10,... | collective-permute-start | bytes 589832 | tf_op jit(solution)/shard_map/ppermute | solution.py:18
  32.2 0.9 %collective-permute-start.15 = (f32[64,384]{1,0:T(8,128)S(1)}, f32[64,384]{1,0:T(8,128)S(1)}, u32[]{:S(2)}, u32[]{:S(2)}) collective-permute-start(f32[64,384]{1,0:T(8,128)S(1)} %sum_near.3.refs_6_), channel_id=1, source_target_pairs={{0,16},{8,24},{16,0},{24,8},{1,17},{9,25},{17,1},{25,9},{2,18},{10... | collective-permute-start | bytes 294920 | tf_op jit(solution)/shard_map/ppermute | solution.py:18
  33.1 1.0 %speech_part.5.refs_2_ = f32[128,768]{1,0:T(8,128)S(1)} custom-call(f32[2,1]{1,0:T(2,128)S(1)} %pad_maximum_fusion.refs_8_.refs_0_, bf16[528,768]{1,0:T(8,128)(2,1)S(1)} %get-tuple-element.17.refs_2_.refs_1_, bf16[256,768]{1,0:T(8,128)(2,1)S(1)} %get-tuple-element.18.refs_1_.refs_2_, bf16[256,768]{1,0:T(8,128)(2,1)S(1)} %collective-permute-done.6.refs_0_.refs_3_, ...), custom_call_target="tpu_custom_call" | custom-call | flops 3019898880 | bytes 2383880 | tf_op jit(solution)/shard_map/speech_part/pallas_call | solution.py:34
  34.1 1.0 %speech_part.7.refs_2_ = f32[128,768]{1,0:T(8,128)S(1)} custom-call(f32[2,1]{1,0:T(2,128)S(1)} %pad_maximum_fusion.refs_8_.refs_0_, bf16[528,768]{1,0:T(8,128)(2,1)S(1)} %collective-permute-done.8.refs_3_.refs_1_, bf16[256,768]{1,0:T(8,128)(2,1)S(1)} %get-tuple-element.18.refs_1_.refs_2_, bf16[256,768]{1,0:T(8,128)(2,1)S(1)} %collective-permute-done.6.refs_0_.refs_3_, ...), custom_call_target="tpu_custom_call" | custom-call | flops 3019898880 | bytes 2383880 | tf_op jit(solution)/shard_map/speech_part/pallas_call | solution.py:34
  35.2 1.2 %collective-permute-done.12.refs_4_.refs_3_ = bf16[128,768]{1,0:T(8,128)(2,1)S(1)} collective-permute-done((bf16[128,768]{1,0:T(8,128)(2,1)S(1)}, bf16[128,768]{1,0:T(8,128)(2,1)S(1)}, u32[]{:S(2)}, u32[]{:S(2)}) %collective-permute-start.12) | collective-permute-done | bytes 196640 | tf_op jit(solution)/shard_map/ppermute | solution.py:18
  36.3 0.5 %speech_part.8.refs_2_ = f32[128,768]{1,0:T(8,128)S(1)} custom-call(f32[2,1]{1,0:T(2,128)S(1)} %pad_maximum_fusion.refs_8_.refs_0_, bf16[528,768]{1,0:T(8,128)(2,1)S(1)} %collective-permute-done.8.refs_3_.refs_1_, f32[128,768]{1,0:T(8,128)S(1)} %speech_part.7.refs_2_, bf16[128,768]{1,0:T(8,128)(2,1)S(1)} %collective-permute-done.12.refs_4_.refs_3_), custom_call_target="tpu_custom_call" | custom-call | flops 503316480 | bytes 1794056 | tf_op jit(solution)/shard_map/speech_part/pallas_call | solution.py:34
  36.8 0.8 %collective-permute-done.11.refs_3_ = bf16[128,768]{1,0:T(8,128)(2,1)S(1)} collective-permute-done((bf16[128,768]{1,0:T(8,128)(2,1)S(1)}, bf16[128,768]{1,0:T(8,128)(2,1)S(1)}, u32[]{:S(2)}, u32[]{:S(2)}) %collective-permute-start.11) | collective-permute-done | bytes 196640 | tf_op jit(solution)/shard_map/ppermute | solution.py:18
  37.6 0.5 %speech_part.9 = f32[128,768]{1,0:T(8,128)S(1)} custom-call(f32[2,1]{1,0:T(2,128)S(1)} %pad_maximum_fusion.refs_8_.refs_0_, bf16[528,768]{1,0:T(8,128)(2,1)S(1)} %collective-permute-done.8.refs_3_.refs_1_, f32[128,768]{1,0:T(8,128)S(1)} %speech_part.8.refs_2_, bf16[128,768]{1,0:T(8,128)(2,1)S(1)} %collective-permute-done.11.refs_3_), custom_call_target="tpu_custom_call" | custom-call | flops 503316480 | bytes 1794056 | tf_op jit(solution)/shard_map/speech_part/pallas_call | solution.py:34
  38.1 0.7 %speech_part.6.refs_4_.home = f32[128,768]{1,0:T(8,128)S(1)} custom-call(f32[2,1]{1,0:T(2,128)S(1)} %pad_maximum_fusion.refs_8_.refs_0_, bf16[528,768]{1,0:T(8,128)(2,1)S(1)} %get-tuple-element.17.refs_2_.refs_1_, f32[128,768]{1,0:T(8,128)S(1)} %speech_part.5.refs_2_, bf16[128,768]{1,0:T(8,128)(2,1)S(1)} %collective-permute-done.11.refs_3_, ...), custom_call_target="tpu_custom_call" | custom-call | flops 1006632960 | bytes 1990664 | tf_op jit(solution)/shard_map/speech_part/pallas_call | solution.py:34
  38.8 0.7 %collective-permute-done.15.refs_1_ = f32[64,384]{1,0:T(8,128)S(1)} collective-permute-done((f32[64,384]{1,0:T(8,128)S(1)}, f32[64,384]{1,0:T(8,128)S(1)}, u32[]{:S(2)}, u32[]{:S(2)}) %collective-permute-start.15) | collective-permute-done | bytes 98336 | tf_op jit(solution)/shard_map/ppermute | solution.py:18
  39.5 0.3 collective-permute-done.13.refs_0_
  39.8 1.0 %finish.1 = (f32[128,768]{1,0:T(8,128)}, f32[64,768]{1,0:T(8,128)}) custom-call(bf16[128,768]{1,0:T(8,128)(2,1)S(1)} %get-tuple-element.14.audio, f32[128,768]{1,0:T(8,128)S(1)} %speech_part.6.refs_4_.home, f32[128,768]{1,0:T(8,128)S(1)} %collective-permute-done.13.refs_0_, bf16[64,768]{1,0:T(8,128)(2,1)S(1)} %get-tuple-element.23.refs_1_, ...), custom_call_target="tpu_custom_call" | custom-call | tf_op jit(solution)/shard_map/finish/pallas_call | solution.py:360
  (18 shorter events, 0.6 us)
Async XLA Ops:
  0.6 11.7 %collective-permute-start.1 = (bf16[64,768]{1,0:T(8,128)(2,1)}, bf16[64,768]{1,0:T(8,128)(2,1)S(1)}, u32[]{:S(2)}, u32[]{:S(2)}) collective-permute-start(bf16[64,768]{1,0:T(8,128)(2,1)} %refs_1_.1), channel_id=1, source_target_pairs={{0,16},{8,24},{16,0},{24,8},{1,17},{9,25},{17,1},{25,9},{2,18},{10... | collective-permute-start | bytes 294920 | tf_op jit(solution)/shard_map/ppermute | solution.py:18
  5.9 11.3 %collective-permute-start.3 = (bf16[136,768]{1,0:T(8,128)(2,1)S(1)}, bf16[136,768]{1,0:T(8,128)(2,1)S(1)}, u32[]{:S(2)}, u32[]{:S(2)}) collective-permute-start(bf16[136,768]{1,0:T(8,128)(2,1)S(1)} %get-tuple-element.16.refs_4_), channel_id=1, source_target_pairs={{0,6},{1,7},{2,4},{3,5},{4,2},{5,3},{6,0},{7,1},{8,14},{9,15},{10,... | collective-permute-start | bytes 626696 | tf_op jit(solution)/shard_map/ppermute | solution.py:18
  8.4 9.6 %collective-permute-start.4 = (bf16[136,768]{1,0:T(8,128)(2,1)S(1)}, bf16[136,768]{1,0:T(8,128)(2,1)S(1)}, u32[]{:S(2)}, u32[]{:S(2)}) collective-permute-start(bf16[136,768]{1,0:T(8,128)(2,1)S(1)} %get-tuple-element.16.refs_4_), channel_id=1, source_target_pairs={{0,4},{1,5},{2,6},{3,7},{4,0},{5,1},{6,2},{7,3},{8,12},{9,13},{10,... | collective-permute-start | bytes 626696 | tf_op jit(solution)/shard_map/ppermute | solution.py:18
  8.9 9.1 %collective-permute-start.5 = (bf16[136,768]{1,0:T(8,128)(2,1)S(1)}, bf16[136,768]{1,0:T(8,128)(2,1)S(1)}, u32[]{:S(2)}, u32[]{:S(2)}) collective-permute-start(bf16[136,768]{1,0:T(8,128)(2,1)S(1)} %get-tuple-element.16.refs_4_), channel_id=1, source_target_pairs={{0,2},{1,3},{2,0},{3,1},{4,6},{5,7},{6,4},{7,5},{8,10},{9,11},{10,... | collective-permute-start | bytes 626696 | tf_op jit(solution)/shard_map/ppermute | solution.py:18
  9.5 5.2 %collective-permute-start = (bf16[64,768]{1,0:T(8,128)(2,1)S(1)}, bf16[64,768]{1,0:T(8,128)(2,1)S(1)}, u32[]{:S(2)}, u32[]{:S(2)}) collective-permute-start(bf16[64,768]{1,0:T(8,128)(2,1)S(1)} %get-tuple-element.15.refs_0_), channel_id=1, source_target_pairs={{0,8},{8,0},{16,24},{24,16},{1,9},{9,1},{17,25},{25,17},{2,10},{10... | collective-permute-start | bytes 294920 | tf_op jit(solution)/shard_map/ppermute | solution.py:18
  12.5 4.7 %collective-permute-start.2 = (bf16[64,768]{1,0:T(8,128)(2,1)S(1)}, bf16[64,768]{1,0:T(8,128)(2,1)S(1)}, u32[]{:S(2)}, u32[]{:S(2)}) collective-permute-start(bf16[64,768]{1,0:T(8,128)(2,1)S(1)} %unit_far.1.refs_2_), channel_id=1, source_target_pairs={{0,8},{8,0},{16,24},{24,16},{1,9},{9,1},{17,25},{25,17},{2,10},{10... | collective-permute-start | bytes 294920 | tf_op jit(solution)/shard_map/ppermute | solution.py:18
  18.2 2.4 %collective-permute-start.8 = (bf16[528,768]{1,0:T(8,128)(2,1)S(1)}, bf16[528,768]{1,0:T(8,128)(2,1)S(1)}, u32[]{:S(2)}, u32[]{:S(2)}) collective-permute-start(bf16[528,768]{1,0:T(8,128)(2,1)S(1)} %get-tuple-element.17.refs_2_.refs_1_), channel_id=1, source_target_pairs={{0,1},{1,0},{2,3},{3,2},{4,5},{5,4},{6,7},{7,6},{8,9},{9,8},{10,11... | collective-permute-start | bytes 2433032 | tf_op jit(solution)/shard_map/ppermute | solution.py:18
  18.3 11.5 %collective-permute-start.6 = (bf16[256,768]{1,0:T(8,128)(2,1)S(1)}, bf16[256,768]{1,0:T(8,128)(2,1)S(1)}, u32[]{:S(2)}, u32[]{:S(2)}) collective-permute-start(bf16[256,768]{1,0:T(8,128)(2,1)S(1)} %get-tuple-element.18.refs_1_.refs_2_), channel_id=1, source_target_pairs={{0,2},{1,3},{2,0},{3,1},{4,6},{5,7},{6,4},{7,5},{8,10},{9,11},{10,... | collective-permute-start | bytes 1179656 | tf_op jit(solution)/shard_map/ppermute | solution.py:18
  19.8 11.5 %collective-permute-start.7 = (bf16[256,768]{1,0:T(8,128)(2,1)S(1)}, bf16[256,768]{1,0:T(8,128)(2,1)S(1)}, u32[]{:S(2)}, u32[]{:S(2)}) collective-permute-start(bf16[256,768]{1,0:T(8,128)(2,1)S(1)} %get-tuple-element.18.refs_1_.refs_2_), channel_id=1, source_target_pairs={{0,4},{1,5},{2,6},{3,7},{4,0},{5,1},{6,2},{7,3},{8,12},{9,13},{10,... | collective-permute-start | bytes 1179656 | tf_op jit(solution)/shard_map/ppermute | solution.py:18
  21.9 5.7 %collective-permute-start.9 = (f32[64,384]{1,0:T(8,128)S(1)}, f32[64,384]{1,0:T(8,128)S(1)}, u32[]{:S(2)}, u32[]{:S(2)}) collective-permute-start(f32[64,384]{1,0:T(8,128)S(1)} %get-tuple-element.20), channel_id=1, source_target_pairs={{0,8},{8,0},{16,24},{24,16},{1,9},{9,1},{17,25},{25,17},{2,10},{10... | collective-permute-start | bytes 294920 | tf_op jit(solution)/shard_map/ppermute | solution.py:18
  23.5 8.6 %collective-permute-start.10 = (f32[64,384]{1,0:T(8,128)S(1)}, f32[64,384]{1,0:T(8,128)S(1)}, u32[]{:S(2)}, u32[]{:S(2)}) collective-permute-start(f32[64,384]{1,0:T(8,128)S(1)} %get-tuple-element.22), channel_id=1, source_target_pairs={{0,8},{8,0},{16,24},{24,16},{1,9},{9,1},{17,25},{25,17},{2,10},{10... | collective-permute-start | bytes 294920 | tf_op jit(solution)/shard_map/ppermute | solution.py:18
  24.0 14.8 %collective-permute-start.16 = (f32[64,768]{1,0:T(8,128)S(1)}, f32[64,768]{1,0:T(8,128)S(1)}, u32[]{:S(2)}, u32[]{:S(2)}) collective-permute-start(f32[64,768]{1,0:T(8,128)S(1)} %get-tuple-element.24), channel_id=1, source_target_pairs={{0,8},{8,0},{16,24},{24,16},{1,9},{9,1},{17,25},{25,17},{2,10},{10... | collective-permute-start | bytes 589832 | tf_op jit(solution)/shard_map/ppermute | solution.py:18
  27.6 11.9 %collective-permute-start.14 = (f32[64,384]{1,0:T(8,128)S(1)}, f32[64,384]{1,0:T(8,128)S(1)}, u32[]{:S(2)}, u32[]{:S(2)}) collective-permute-start(f32[64,384]{1,0:T(8,128)S(1)} %sum_near.2.refs_1_.refs_5_), channel_id=1, source_target_pairs={{0,16},{8,24},{16,0},{24,8},{1,17},{9,25},{17,1},{25,9},{2,18},{10... | collective-permute-start | bytes 294920 | tf_op jit(solution)/shard_map/ppermute | solution.py:18
  29.8 6.5 %collective-permute-start.12 = (bf16[128,768]{1,0:T(8,128)(2,1)S(1)}, bf16[128,768]{1,0:T(8,128)(2,1)S(1)}, u32[]{:S(2)}, u32[]{:S(2)}) collective-permute-start(bf16[128,768]{1,0:T(8,128)(2,1)S(1)} %cut.3.refs_3_), channel_id=1, source_target_pairs={{0,4},{1,5},{2,6},{3,7},{4,0},{5,1},{6,2},{7,3},{8,12},{9,13},{10,... | collective-permute-start | bytes 589832 | tf_op jit(solution)/shard_map/ppermute | solution.py:18
  31.3 6.3 %collective-permute-start.11 = (bf16[128,768]{1,0:T(8,128)(2,1)S(1)}, bf16[128,768]{1,0:T(8,128)(2,1)S(1)}, u32[]{:S(2)}, u32[]{:S(2)}) collective-permute-start(bf16[128,768]{1,0:T(8,128)(2,1)S(1)} %cut.2.refs_2_), channel_id=1, source_target_pairs={{0,2},{1,3},{2,0},{3,1},{4,6},{5,7},{6,4},{7,5},{8,10},{9,11},{10,... | collective-permute-start | bytes 589832 | tf_op jit(solution)/shard_map/ppermute | solution.py:18
  32.2 7.3 %collective-permute-start.15 = (f32[64,384]{1,0:T(8,128)S(1)}, f32[64,384]{1,0:T(8,128)S(1)}, u32[]{:S(2)}, u32[]{:S(2)}) collective-permute-start(f32[64,384]{1,0:T(8,128)S(1)} %sum_near.3.refs_6_), channel_id=1, source_target_pairs={{0,16},{8,24},{16,0},{24,8},{1,17},{9,25},{17,1},{25,9},{2,18},{10... | collective-permute-start | bytes 294920 | tf_op jit(solution)/shard_map/ppermute | solution.py:18
  38.0 1.8 %collective-permute-start.13 = (f32[128,768]{1,0:T(8,128)S(1)}, f32[128,768]{1,0:T(8,128)S(1)}, u32[]{:S(2)}, u32[]{:S(2)}) collective-permute-start(f32[128,768]{1,0:T(8,128)S(1)} %speech_part.9), channel_id=1, source_target_pairs={{0,1},{1,0},{2,3},{3,2},{4,5},{5,4},{6,7},{7,6},{8,9},{9,8},{10,11... | collective-permute-start | bytes 1179656 | tf_op jit(solution)/shard_map/ppermute | solution.py:18
